TPU v7x, 32 devices: a whole 2x2x4 slice. The times are simulated.
32 devices in a mesh: traj: 4 (over z), tm: 8 (over y, x, core).
Axes of the slice: x: 2, y: 2, z: 4, core: 2. Of those that a mesh axis runs over, the one named last changes fastest.
Arguments:
- query_states: bfloat16 [8192, 768], P(('traj', 'tm')), parts along dimension 0, may hold values from -8 to 8
- key_states: bfloat16 [8192, 768], P(('traj', 'tm')), parts along dimension 0, may hold values from -8 to 8
- value_states: bfloat16 [8192, 768], P(('traj', 'tm')), parts along dimension 0, may hold values from -6 to 6
- grad_out: bfloat16 [8192, 768], P(('traj', 'tm')), parts along dimension 0, may hold values from -6 to 6
- camera_pose: int32 [64], P('traj'), parts along dimension 0, may hold values from 0 to 15
- pose_bias: float32 [6, 16, 16], replicated, may hold values from -2 to 2
- memory_index: int32 [32, 2], P(('traj', 'tm')), parts along dimension 0, may hold values from 0 to 3, all different within a row
- bank_frames: int32 [16], P('traj'), parts along dimension 0, may hold values from 0 to 15, as said below
Outputs:
- attended: bfloat16 [8192, 768], P(('traj', 'tm')), parts along dimension 0
- grad_query: bfloat16 [8192, 768], P(('traj', 'tm')), parts along dimension 0
- grad_key: bfloat16 [8192, 768], P(('traj', 'tm')), parts along dimension 0
- grad_value: bfloat16 [8192, 768], P(('traj', 'tm')), parts along dimension 0
There are 4 independent parts, one for each index of `traj`. A program takes and returns all parts, laid end to end along the dimension named above; an argument that names none is the same for every part. Nothing has to cross between parts.
Inputs may be any that keep to these rules, and one draw needn't show every extreme that they name: `bank_frames`: 4 distinct frames; frame 0 and frame 16 - 1 are always among them. `memory_index`: each group names 2 different slots, and every slot is named by some group.
All inputs are finite; a program needn't handle non-finite values.
Results may differ from a plain program's by a relative error of at most 0.0085.
Values may be sent and summed in bfloat16 or wider, within the bound.
No kernel may reach another device: no remote copies, remote signals or barrier semaphores. Data moves between devices by JAX's collectives and lax.ppermute only.
A program may use at most 64 MiB of HBM per device.

v0:
```python
import math

import jax
import jax.numpy as jnp
from jax import lax
from jax.sharding import PartitionSpec as P

FR_DEV = 2
MEM = 2


BLOCKED_LOGIT = -1e30


def passed_along(shard, axis, by):
    peers = lax.axis_size(axis)
    pairs = [(i, i + by) for i in range(peers) if 0 <= i + by < peers]
    return lax.ppermute(shard, axis, pairs)


def broadcast(block, axis, source):
    block = jnp.where(lax.axis_index(axis) == source, block, jnp.zeros_like(block))
    return lax.psum(block, axis)


def pose_table(pose_bias, query_pose, key_pose):
    pose_count = pose_bias.shape[1]
    pose_range = jnp.arange(pose_count, dtype=jnp.int32)
    left_hot = (query_pose[:, None] == pose_range[None, :]).astype(jnp.float32)
    right_hot = (key_pose[:, None] == pose_range[None, :]).astype(jnp.float32)
    return jnp.einsum(
        "ap,hpr,br->hab", left_hot, pose_bias, right_hot, precision=lax.Precision.HIGHEST
    )


def biased_logits(query_heads, key_heads, bias_rows, factor):
    head_count = bias_rows.shape[0]
    query_count = query_heads.shape[0]
    key_count = key_heads.shape[0]
    logits = (
        jnp.einsum("qhd,khd->hqk", query_heads, key_heads, preferred_element_type=jnp.float32)
        * factor
    )
    logits = logits.reshape(
        head_count,
        bias_rows.shape[1],
        query_count // bias_rows.shape[1],
        bias_rows.shape[2],
        key_count // bias_rows.shape[2],
    )
    return logits + bias_rows[:, :, None, :, None]


def attend(query_rows, key_rows, value_rows, cotangent, bias_rows, blocked):
    head_count = bias_rows.shape[0]
    query_count = query_rows.shape[0]
    key_count = key_rows.shape[0]
    head_depth = query_rows.shape[1] // head_count
    factor = 1.0 / math.sqrt(head_depth)
    query_heads = query_rows.reshape(query_count, head_count, head_depth)
    key_heads = key_rows.reshape(key_count, head_count, head_depth)
    value_heads = value_rows.reshape(key_count, head_count, head_depth)
    cotangent_heads = cotangent.reshape(query_count, head_count, head_depth)
    logits = biased_logits(query_heads, key_heads, bias_rows, factor)
    logits = jnp.where(blocked[None, None, None, :, None], BLOCKED_LOGIT, logits)
    logits = logits.reshape(head_count, query_count, key_count)
    row_peak = jnp.max(logits, axis=-1, keepdims=True)
    shifted_exp = jnp.exp(logits - row_peak)
    row_total = jnp.sum(shifted_exp, axis=-1, keepdims=True)
    probs_all = shifted_exp / row_total
    weights = probs_all.astype(jnp.bfloat16)
    attended = jnp.einsum("hqk,khd->qhd", weights, value_heads, preferred_element_type=jnp.float32)
    attended = attended.reshape(query_count, -1).astype(jnp.bfloat16)
    slope_grad = jnp.einsum(
        "qhd,khd->hqk", cotangent_heads, value_heads, preferred_element_type=jnp.float32
    )
    spread = jnp.sum(probs_all * slope_grad, axis=-1, keepdims=True)
    logit_grad = (probs_all * (slope_grad - spread)).astype(jnp.bfloat16)
    grad_query = (
        jnp.einsum("hqk,khd->qhd", logit_grad, key_heads, preferred_element_type=jnp.float32)
        * factor
    )
    grad_query = grad_query.reshape(query_count, -1).astype(jnp.bfloat16)
    key_grad = (
        jnp.einsum("hqk,qhd->khd", logit_grad, query_heads, preferred_element_type=jnp.float32)
        * factor
    )
    value_grad = jnp.einsum(
        "hqk,qhd->khd", weights, cotangent_heads, preferred_element_type=jnp.float32
    )
    return (
        attended,
        grad_query,
        key_grad.reshape(key_count, -1),
        value_grad.reshape(key_count, -1),
        row_peak[..., 0],
        row_total[..., 0],
        spread[..., 0],
    )


def body(
    query_states,
    key_states,
    value_states,
    grad_out,
    camera_pose,
    pose_bias,
    memory_index,
    bank_frames,
):
    row_count, width = query_states.shape
    frame_len = row_count // FR_DEV
    slot_count = bank_frames.shape[0]
    group_index = lax.axis_index("tm")
    frame_range = jnp.arange(FR_DEV, dtype=jnp.int32)
    slot_range = jnp.arange(slot_count, dtype=jnp.int32)
    own_ids = group_index * FR_DEV + frame_range
    prev_ids = jnp.maximum(own_ids - FR_DEV, 0)
    chosen = memory_index[0]
    mem_ids = jnp.take(bank_frames, chosen)
    owner_hit = bank_frames[:, None] == own_ids[None, :]
    prev_keys, prev_values = passed_along((key_states, value_states), "tm", 1)
    fetched_keys = []
    fetched_values = []
    for slot_index in range(slot_count):
        frame_id = bank_frames[slot_index]
        start_row = frame_id % FR_DEV * frame_len
        piece_keys = lax.dynamic_slice_in_dim(key_states, start_row, frame_len, 0)
        piece_values = lax.dynamic_slice_in_dim(value_states, start_row, frame_len, 0)
        got_keys, got_values = (
            broadcast(piece_keys, "tm", frame_id // FR_DEV),
            broadcast(piece_values, "tm", frame_id // FR_DEV),
        )
        fetched_keys.append(got_keys)
        fetched_values.append(got_values)
    bank_keys = jnp.stack(fetched_keys)
    bank_values = jnp.stack(fetched_values)
    select = chosen[:, None] == slot_range[None, :]
    mem_keys = jnp.sum(jnp.where(select[:, :, None, None], bank_keys[None], 0), axis=1)
    mem_values = jnp.sum(jnp.where(select[:, :, None, None], bank_values[None], 0), axis=1)
    all_keys = jnp.concatenate([prev_keys, key_states, mem_keys.reshape(-1, width)], axis=0)
    all_values = jnp.concatenate([prev_values, value_states, mem_values.reshape(-1, width)], axis=0)
    key_ids = jnp.concatenate([prev_ids, own_ids, mem_ids])
    bias_rows = pose_table(
        pose_bias, jnp.take(camera_pose, own_ids), jnp.take(camera_pose, key_ids)
    )
    key_slots = jnp.arange(key_ids.shape[0], dtype=jnp.int32)
    blocked = (key_slots < FR_DEV) & (group_index == 0)
    attended, grad_query, key_grad, value_grad, row_peak, row_total, spread = attend(
        query_states, all_keys, all_values, grad_out, bias_rows, blocked
    )
    back_keys, back_values = (
        passed_along(key_grad[:row_count].astype(jnp.bfloat16), "tm", -1).astype(jnp.float32),
        passed_along(value_grad[:row_count].astype(jnp.bfloat16), "tm", -1).astype(jnp.float32),
    )
    mem_key_grad = key_grad[2 * row_count :].reshape(MEM, frame_len, width)
    mem_value_grad = value_grad[2 * row_count :].reshape(MEM, frame_len, width)
    part_keys = jnp.sum(jnp.where(select[:, :, None, None], mem_key_grad[:, None], 0.0), axis=0)
    part_values = jnp.sum(jnp.where(select[:, :, None, None], mem_value_grad[:, None], 0.0), axis=0)
    part_keys = lax.optimization_barrier(part_keys.astype(jnp.bfloat16)).astype(jnp.float32)
    part_values = lax.optimization_barrier(part_values.astype(jnp.bfloat16)).astype(jnp.float32)
    bank_key_grad, bank_value_grad = (
        lax.psum(part_keys.astype(jnp.bfloat16), "tm").astype(jnp.float32),
        lax.psum(part_values.astype(jnp.bfloat16), "tm").astype(jnp.float32),
    )
    own_key_add = jnp.sum(
        jnp.where(owner_hit[:, :, None, None], bank_key_grad[:, None], 0.0), axis=0
    ).reshape(row_count, width)
    own_value_add = jnp.sum(
        jnp.where(owner_hit[:, :, None, None], bank_value_grad[:, None], 0.0), axis=0
    ).reshape(row_count, width)
    grad_key = (key_grad[row_count : 2 * row_count] + back_keys + own_key_add).astype(jnp.bfloat16)
    grad_value = (value_grad[row_count : 2 * row_count] + back_values + own_value_add).astype(
        jnp.bfloat16
    )
    return (attended, grad_query, grad_key, grad_value)


def solution(mesh):
    in_specs = (
        P(("traj", "tm"), None),
        P(("traj", "tm"), None),
        P(("traj", "tm"), None),
        P(("traj", "tm"), None),
        P("traj"),
        P(),
        P(("traj", "tm"), None),
        P("traj"),
    )
    out_specs = (
        P(("traj", "tm"), None),
        P(("traj", "tm"), None),
        P(("traj", "tm"), None),
        P(("traj", "tm"), None),
    )
    return jax.shard_map(body, mesh=mesh, in_specs=in_specs, out_specs=out_specs, check_vma=False)
```

profile of v0, /device:TPU:0, one launch (start us, length us, event | category | flops | bytes accessed | tf_op | source)
XLA Modules:
  0.0 202.2 jit_solution(13677840331939638553)
XLA Ops:
  7.2 1.2 copy.62
  8.4 3.1 %collective-permute-start.1 = (bf16[256,768]{0,1:T(8,128)(2,1)S(1)}, bf16[256,768]{0,1:T(8,128)(2,1)}, u32[]{:S(2)}, u32[]{:S(2)}) collective-permute-start(bf16[256,768]{0,1:T(8,128)(2,1)S(1)} %copy.62), channel_id=1, source_target_pairs={{0,1},{1,2},{2,3},{3,4},{4,5},{5,6},{6,7},{8,9},{9,10},{10,11},{11... | collective-permute-start | bytes 1179656 | tf_op jit(solution)/shard_map/ppermute | solution.py:18
  11.6 3.8 %collective-permute-start = (bf16[256,768]{1,0:T(8,128)(2,1)}, bf16[256,768]{1,0:T(8,128)(2,1)S(1)}, u32[]{:S(2)}, u32[]{:S(2)}) collective-permute-start(bf16[256,768]{1,0:T(8,128)(2,1)} %param.10), channel_id=1, source_target_pairs={{0,1},{1,2},{2,3},{3,4},{4,5},{5,6},{6,7},{8,9},{9,10},{10,11},{11... | collective-permute-start | bytes 1179656 | tf_op jit(solution)/shard_map/ppermute | solution.py:18
  15.4 1.4 fusion.31
  27.3 2.2 %select_bitcast_fusion.3 = (bf16[1,128,768]{2,1,0:T(8,128)(2,1)}, bf16[1,128,768]{2,1,0:T(8,128)(2,1)}, bf16[1,128,768]{2,1,0:T(8,128)(2,1)}, bf16[1,128,768]{2,1,0:T(8,128)(2,1)}) fusion(bf16[256,768]{1,0:T(8,128)(2,1)} %param.9, s32[]{:T(128)S(6)} %select_n.220, pred[]{:T(512)S(6)} %eq.90, s32[]{:T(128)S(6)} %select_n.225, pred[]{:T(512)S(6)} %eq.91, ...), kind=kLoop, calls=%fused_computation.41 | loop fusion | flops 393216 | bytes 1572884 | tf_op jit(solution)/shard_map/stack | solution.py:137
  29.4 1.0 select_bitcast_fusion.7
  30.6 0.6 gather_fusion
  31.3 0.6 gather_fusion.1
  32.0 0.6 gather_fusion.2
  32.9 0.9 copy.60
  34.6 0.9 copy.73
  35.5 3.5 %add.220 = f32[6,2,128,6,128]{2,1,4,3,0:T(2,128)} broadcast(f32[6,2,6]{1,2,0:T(8,128)S(1)} %copy.71), dimensions={0,1,3} | broadcast | bytes 4718880 | tf_op jit(solution)/shard_map/add | solution.py:51
  39.0 7.2 %add.221 = f32[6,256,768]{1,2,0:T(8,128)} reshape(f32[6,2,128,6,128]{2,1,4,3,0:T(2,128)} %add.220) | data formatting | bytes 9437184 | tf_op jit(solution)/shard_map/add | solution.py:51
  46.4 1.2 copy.65
  47.7 0.9 copy.59
  48.6 42.8 %all-reduce.7.cloned.1.call-done = (bf16[1,128,768]{2,1,0:T(8,128)(2,1)}, bf16[1,128,768]{2,1,0:T(8,128)(2,1)}, bf16[1,128,768]{2,1,0:T(8,128)(2,1)}, bf16[1,128...) async-done(((bf16[1,128,768]{2,1,0:T(8,128)(2,1)}, ...) | async-done | bytes 1572880 | tf_op jit(solution)/shard_map/psum | solution.py:23
  91.3 1.7 pad_maximum_fusion.2
  93.0 1.5 select_reduce_fusion.4
  94.5 0.5 reshape.355
  95.0 1.4 copy.61
  96.5 1.0 concatenate.61
  97.5 3.3 %fusion.4 = f32[6,256,768]{1,2,0:T(8,128)S(1)} fusion(f32[6,256,768]{1,2,0:T(8,128)} %add.221, pred[768]{0:T(1024)(128)(4,1)S(1)} %broadcast_bitcast_fusion, bf16[256,6,128]{0,2,1:T(8,128)(2,1)S(1)} %bitcast.106, bf16[256,6,128]{2,0,1:T(8,128)(2,1)S(1)} %copy.67, bf16[256,6,128]{2,0,1:T(8,128)(2,1)S(1)} %copy.66, bf16[256,6,128]{2,0,1:T(8,128)(2,1)S(1)} %copy.65), kind=kOutput, calls=%fused_computation.10 | convolution fusion | flops 309067776 | bytes 11010816 | tf_op jit(solution)/shard_map/qhd,khd->hqk/dot_general | solution.py:41
  100.8 3.6 %fusion.32 = (f32[6,256]{1,0:T(8,128)S(1)}, f32[6,256,768]{1,2,0:T(8,128)}) fusion(f32[6,256,768]{1,2,0:T(8,128)S(1)} %fusion.4), kind=kOutput, calls=%fused_computation.85 | output fusion | flops 2360063 | bytes 9443328 | tf_op jit(solution)/shard_map/sub | solution.py:68
  104.4 6.5 %convolution_bitcast_fusion = f32[768,6,128]{0,2,1:T(8,128)} fusion(bf16[256,6,128]{0,2,1:T(8,128)(2,1)S(1)} %bitcast.117, f32[6,256]{1,0:T(8,128)S(1)} %get-tuple-element.48, f32[6,256,768]{1,2,0:T(8,128)} %copy-done.3), kind=kOutput, calls=%fused_computation.18 | convolution fusion | flops 305531136 | bytes 7477248 | tf_op jit(solution)/shard_map/hqk,qhd->khd/dot_general | solution.py:88
  110.9 2.4 %fusion.29 = (f32[256,6,128]{0,2,1:T(8,128)}, f32[256,6,128]{0,2,1:T(8,128)S(1)}) fusion(f32[768,6,128]{0,2,1:T(8,128)} %convolution_bitcast_fusion), kind=kLoop, calls=%fused_computation.82 | loop fusion | bytes 3145728 | tf_op jit(solution)/shard_map/slice | solution.py:174
  113.7 1.2 copy.85
  114.9 3.5 %fusion.1 = (f32[6,256]{1,0:T(8,128)S(1)}, f32[6,768,256]{2,1,0:T(8,128)S(1)}) fusion(f32[6,256,768]{1,2,0:T(8,128)} %get-tuple-element.49, f32[6,256]{1,0:T(8,128)S(1)} %get-tuple-element.48, bf16[256,6,128]{0,2,1:T(8,128)(2,1)S(1)} %bitcast.118, bf16[256,6,128]{0,2,1:T(8,128)(2,1)} %concatenate.61, bf16[256,6,128]{0,2,1:T(8,128)(2,1)S(1)} %bitcast.114, ...), kind=kOutput, calls=%fused_computation.6 | convolution fusion | flops 309066240 | bytes 11022336 | tf_op jit(solution)/shard_map/qhd,khd->hqk/dot_general | solution.py:74
  118.7 0.8 fusion.3
  119.6 0.9 multiply_bitcast_fusion
  120.5 1.4 copy-done.4
  121.9 1.4 fusion.30
  123.4 1.5 broadcast_in_dim.142
  124.9 1.2 copy.81
  126.1 3.6 %select_reduce_fusion.1 = (bf16[4,128,768]{2,1,0:T(8,128)(2,1)}, bf16[4,128,768]{2,1,0:T(8,128)(2,1)}) fusion(f32[2,128,768]{2,1,0:T(8,128)} %copy.85, pred[2,4]{1,0:T(4,128)(4,1)S(1)} %iota_compare_fusion.1, f32[2,128,768]{2,1,0:T(8,128)} %copy.81), kind=kLoop, calls=%fused_computation.13 | loop fusion | flops 2359296 | bytes 3145736 | tf_op jit(solution)/shard_map/reduce_sum | solution.py:160
  129.8 2.0 slice.69
  131.8 1.9 copy.79
  133.7 1.5 collective-permute-start.2
  135.2 2.3 %fusion.5 = bf16[6,128,256]{2,1,0:T(8,128)(2,1)} fusion(bf16[6,256,768]{1,2,0:T(8,128)(2,1)S(1)} %fusion.3, bf16[256,6,128]{2,0,1:T(8,128)(2,1)S(1)} %copy-done.9, bf16[256,6,128]{2,0,1:T(8,128)(2,1)S(1)} %copy-done.11, bf16[256,6,128]{2,0,1:T(8,128)(2,1)} %copy-done.12), kind=kOutput, calls=%fused_computation.22 | convolution fusion | flops 305922048 | bytes 3932160 | tf_op jit(solution)/shard_map/hqk,khd->qhd/dot_general | solution.py:80
  137.6 5.6 %convolution_convert_fusion = bf16[6,128,256]{2,1,0:T(8,128)(2,1)S(1)} fusion(bf16[256,6,128]{0,2,1:T(8,128)(2,1)} %concatenate.61, bf16[256,6,128]{0,2,1:T(8,128)(2,1)} %bitcast.113, bf16[256,6,128]{0,2,1:T(8,128)(2,1)} %bitcast.115, f32[6,256]{1,0:T(8,128)S(1)} %get-tuple-element.48, f32[6,256,768]{1,2,0:T(8,128)} %copy-done.3), kind=kOutput, calls=%fused_computation.23 | convolution fusion | flops 309266688 | bytes 6297600 | tf_op jit(solution)/shard_map/hqk,khd->qhd/dot_general | solution.py:72
  143.2 1.3 slice.68
  144.5 0.9 copy.86
  145.8 1.3 collective-permute-start.3
  147.1 1.9 copy.87
  149.3 41.2 %all-reduce.5.cloned.1.call-done = (bf16[4,128,768]{2,1,0:T(8,128)(2,1)}, bf16[4,128,768]{2,1,0:T(8,128)(2,1)}) async-done(((bf16[4,128,768]{2,1,0:T(8,128)(2,1)}, bf16[4,128,768]{2,1,0:T(8,128)(2,1)}), (bf16[4,128,768]{2,1,0:T(8,128)(2,1)}, bf16[4,128,768]{2,1,0:T(8,128)(2,1)})) %all-reduce.5.cloned.1.call-update) | async-done | bytes 1572880 | tf_op jit(solution)/shard_map/psum | solution.py:165
  190.6 1.3 convert_element_type.85
  192.1 0.5 select_reduce_fusion
  192.6 1.9 fusion.9
  194.5 0.9 fusion.8
  (78 shorter events, 3.2 us)
Async XLA Ops:
  7.2 25.5 %copy-start = (f32[6,16,16]{2,1,0:T(8,128)S(1)}, f32[6,16,16]{2,1,0:T(8,128)}, u32[]{:S(2)}) copy-start(f32[6,16,16]{2,1,0:T(8,128)} %param.13) | copy-start | bytes 18436
  7.2 22.3 %copy-start.5 = (bf16[256,768]{1,0:T(8,128)(2,1)S(1)}, bf16[256,768]{1,0:T(8,128)(2,1)}, u32[]{:S(2)}) copy-start(bf16[256,768]{1,0:T(8,128)(2,1)} %param.10) | copy-start | bytes 1179652
  7.2 84.1 %all-reduce.7.cloned.1.call-start = ((), (), s32[]{:S(2)}) async-start(), calls=%async_computation.1 | async-start | bytes 3145728 | tf_op jit(solution)/shard_map/psum | solution.py:23
  8.4 37.9 %collective-permute-start.1 = (bf16[256,768]{0,1:T(8,128)(2,1)S(1)}, bf16[256,768]{0,1:T(8,128)(2,1)}, u32[]{:S(2)}, u32[]{:S(2)}) collective-permute-start(bf16[256,768]{0,1:T(8,128)(2,1)S(1)} %copy.62), channel_id=1, source_target_pairs={{0,1},{1,2},{2,3},{3,4},{4,5},{5,6},{6,7},{8,9},{9,10},{10,11},{11... | collective-permute-start | bytes 1179656 | tf_op jit(solution)/shard_map/ppermute | solution.py:18
  11.6 36.1 %collective-permute-start = (bf16[256,768]{1,0:T(8,128)(2,1)}, bf16[256,768]{1,0:T(8,128)(2,1)S(1)}, u32[]{:S(2)}, u32[]{:S(2)}) collective-permute-start(bf16[256,768]{1,0:T(8,128)(2,1)} %param.10), channel_id=1, source_target_pairs={{0,1},{1,2},{2,3},{3,4},{4,5},{5,6},{6,7},{8,9},{9,10},{10,11},{11... | collective-permute-start | bytes 1179656 | tf_op jit(solution)/shard_map/ppermute | solution.py:18
  27.2 3.3 %copy-start.19 = (s32[1,2]{1,0:T(1,128)S(1)}, s32[1,2]{1,0:T(1,128)}, u32[]{:S(2)}) copy-start(s32[1,2]{1,0:T(1,128)} %param.14) | copy-start | bytes 28
  27.2 3.4 %copy-start.1 = (s32[16]{0:T(128)S(1)}, s32[16]{0:T(128)}, u32[]{:S(2)}) copy-start(s32[16]{0:T(128)} %param.12) | copy-start | bytes 196
  27.2 4.0 %copy-start.2 = (s32[4]{0:T(128)S(1)}, s32[4]{0:T(128)}, u32[]{:S(2)}) copy-start(s32[4]{0:T(128)} %param.15) | copy-start | bytes 52
  30.4 4.0 %copy-start.14 = (bf16[256,768]{1,0:T(8,128)(2,1)S(1)}, bf16[256,768]{1,0:T(8,128)(2,1)}, u32[]{:S(2)}) copy-start(bf16[256,768]{1,0:T(8,128)(2,1)} %param.8) | copy-start | bytes 1179652
  30.5 4.2 %copy-start.15 = (bf16[256,768]{1,0:T(8,128)(2,1)S(1)}, bf16[256,768]{1,0:T(8,128)(2,1)}, u32[]{:S(2)}) copy-start(bf16[256,768]{1,0:T(8,128)(2,1)} %param.11) | copy-start | bytes 1179652
  30.5 160.1 %all-reduce.5.cloned.1.call-start = ((), (), s32[]{:S(2)}) async-start(), calls=%async_computation | async-start | bytes 3145728 | tf_op jit(solution)/shard_map/psum | solution.py:165
  34.4 63.1 %copy-start.10 = (bf16[256,6,128]{2,0,1:T(8,128)(2,1)}, bf16[256,6,128]{2,0,1:T(8,128)(2,1)S(1)}, u32[]{:S(2)}) copy-start(bf16[256,6,128]{2,0,1:T(8,128)(2,1)S(1)} %copy.66) | copy-start | bytes 1179652
  47.6 49.8 %copy-start.12 = (bf16[256,6,128]{2,0,1:T(8,128)(2,1)}, bf16[256,6,128]{2,0,1:T(8,128)(2,1)S(1)}, u32[]{:S(2)}) copy-start(bf16[256,6,128]{2,0,1:T(8,128)(2,1)S(1)} %copy.65) | copy-start | bytes 1179652
  95.0 5.7 %copy-start.8 = (bf16[256,6,128]{2,0,1:T(8,128)(2,1)}, bf16[256,6,128]{2,0,1:T(8,128)(2,1)S(1)}, u32[]{:S(2)}) copy-start(bf16[256,6,128]{2,0,1:T(8,128)(2,1)S(1)} %copy.67) | copy-start | bytes 1179652
  100.8 3.7 %copy-start.3 = (f32[6,256,768]{1,2,0:T(8,128)}, f32[6,256,768]{1,2,0:T(8,128)S(1)}, u32[]{:S(2)}) copy-start(f32[6,256,768]{1,2,0:T(8,128)S(1)} %fusion.4) | copy-start | bytes 14155780
  100.8 3.6 %copy-start.18 = (bf16[256,768]{0,1:T(8,128)(2,1)S(1)}, bf16[256,768]{0,1:T(8,128)(2,1)}, u32[]{:S(2)}) copy-start(bf16[256,768]{0,1:T(8,128)(2,1)} %copy.73) | copy-start | bytes 1179652
  113.3 1.6 copy-start.16
  113.3 1.6 copy-start.17
  114.9 3.7 %slice-start = ((s8[4718592]{0:T(1024)(128)(4,1)}), s8[4194304]{0:T(1024)(128)(4,1)S(1)}, s32[]{:S(2)}) async-start(s8[4718592]{0:T(1024)(128)(4,1)} %bitcast.104), calls=%async_computation.2 | async-start | bytes 8388608
  114.9 3.8 %slice-start.1 = ((s8[4718592]{0:T(1024)(128)(4,1)}), s8[524288]{0:T(1024)(128)(4,1)S(1)}, s32[]{:S(2)}) async-start(s8[4718592]{0:T(1024)(128)(4,1)} %bitcast.104), calls=%async_computation.3 | async-start | bytes 1048576
  120.5 1.4 copy-start.4
  129.7 5.5 %copy-start.9 = (bf16[256,6,128]{2,0,1:T(8,128)(2,1)S(1)}, bf16[256,6,128]{2,0,1:T(8,128)(2,1)}, u32[]{:S(2)}) copy-start(bf16[256,6,128]{2,0,1:T(8,128)(2,1)} %copy-done.8) | copy-start | bytes 1179652
  129.7 5.5 %copy-start.11 = (bf16[256,6,128]{2,0,1:T(8,128)(2,1)S(1)}, bf16[256,6,128]{2,0,1:T(8,128)(2,1)}, u32[]{:S(2)}) copy-start(bf16[256,6,128]{2,0,1:T(8,128)(2,1)} %copy-done.10) | copy-start | bytes 1179652
  133.7 58.9 %collective-permute-start.2 = (bf16[256,768]{1,0:T(8,128)(2,1)}, bf16[256,768]{1,0:T(8,128)(2,1)}, u32[]{:S(2)}, u32[]{:S(2)}) collective-permute-start(bf16[256,768]{1,0:T(8,128)(2,1)} %copy.79), channel_id=1, source_target_pairs={{1,0},{2,1},{3,2},{4,3},{5,4},{6,5},{7,6},{9,8},{10,9},{11,10},{12... | collective-permute-start | bytes 1179656 | tf_op jit(solution)/shard_map/ppermute | solution.py:18
  137.6 7.8 %copy-start.6 = (f32[256,6,128]{0,2,1:T(8,128)S(1)}, f32[256,6,128]{0,2,1:T(8,128)}, u32[]{:S(2)}) copy-start(f32[256,6,128]{0,2,1:T(8,128)} %get-tuple-element.32) | copy-start | bytes 2359300
  143.2 5.9 %copy-start.7 = (f32[256,6,128]{0,2,1:T(8,128)S(1)}, f32[256,6,128]{0,2,1:T(8,128)}, u32[]{:S(2)}) copy-start(f32[256,6,128]{0,2,1:T(8,128)} %get-tuple-element.34) | copy-start | bytes 2359300
  145.8 48.7 %collective-permute-start.3 = (bf16[256,768]{1,0:T(8,128)(2,1)S(1)}, bf16[256,768]{1,0:T(8,128)(2,1)S(1)}, u32[]{:S(2)}, u32[]{:S(2)}) collective-permute-start(bf16[256,768]{1,0:T(8,128)(2,1)S(1)} %copy.83), channel_id=1, source_target_pairs={{1,0},{2,1},{3,2},{4,3},{5,4},{6,5},{7,6},{9,8},{10,9},{11,10},{12... | collective-permute-start | bytes 1179656 | tf_op jit(solution)/shard_map/ppermute | solution.py:18
  190.6 1.4 copy-start.13
Sparse Core Ops, SparseCore 0:
  30.6 60.7 all-reduce.6
  129.8 60.6 all-reduce.4
where the time goes:
time: 203 us; the launch traced here: 202 us
  waiting for transfers between devices  84 us (41%)
  local copies, waits for them, and re-layouts  41.5 us (20%)
  between operations  24.9 us (12%)
  matrix products  22.5 us (11%)
  other arithmetic  19.5 us (10%)
  starting transfers between devices  9.77 us (5%)
    psum x1, waiting for transfers between devices, broadcast(): return lax.psum(block, axis)  42.8 us
    psum x1, waiting for transfers between devices, body(): lax.psum(part_values.astype(jnp.bfloat16), 'tm').astype(jnp.float32)  41.2 us
    add x2, local copies, waits for them, and re-layouts, biased_logits(): return logits + bias_rows[:, :, None, :, None]  10.7 us
    ppermute x4, starting transfers between devices, passed_along(): return lax.ppermute(shard, axis, pairs)  9.69 us
    unnamed x50, local copies, waits for them, and re-layouts  7.95 us
    dot_general x1, matrix products, attend(): jnp.einsum('hqk,qhd->khd', weights, cotangent_heads, preferred_element_ty...  6.49 us
    dot_general x1, matrix products, attend(): jnp.einsum('hqk,khd->qhd', weights, value_heads, preferred_element_type=j...  5.62 us
  transfers between devices with their start and end apart: 6, of which 2 were waited for; matrix products, arithmetic and copies ran while one was open for 21% of the time, Pallas kernels for 0%

commit v1 on v0

v1 whole, which is shorter than its diff:
```python
import functools
import math

import jax
import jax.numpy as jnp
from jax import lax
from jax.experimental import pallas as pl
from jax.experimental.pallas import tpu as pltpu
from jax.sharding import PartitionSpec as P

FR_DEV = 2
MEM = 2

BLOCKED_LOGIT = -1e30
LOG2E = math.log2(math.e)

SMEM = pl.BlockSpec(memory_space=pltpu.SMEM)
VMEM = pl.BlockSpec(memory_space=pltpu.VMEM)
PARAMS = pltpu.CompilerParams(vmem_limit_bytes=32 * 1024 * 1024)


def swap(block, bit, peers):
    return lax.ppermute(block, "tm", [(i, i ^ bit) for i in range(peers)])


def passed_along(block, by, peers):
    pairs = [(i, i + by) for i in range(peers) if 0 <= i + by < peers]
    return lax.ppermute(block, "tm", pairs)


def dyn_frames(bank_ref, slots, last_frame):
    found = [jnp.int32(0)] * (slots - 2)
    seen = jnp.int32(0)
    for slot in range(slots):
        frame = bank_ref[slot]
        free = jnp.logical_and(frame != 0, frame != last_frame)
        for j in range(slots - 2):
            found[j] = jnp.where(jnp.logical_and(free, seen == j), frame, found[j])
        seen = seen + free.astype(jnp.int32)
    return found


def place_of(frame, dyns, last_frame):
    place = jnp.where(frame == 0, len(dyns), len(dyns) + 1)
    for j, dyn in enumerate(dyns):
        place = jnp.where(frame == dyn, j, place)
    return place


def choose(out, take_first, first, second):
    @pl.when(take_first)
    def _():
        out[...] = first[...]

    @pl.when(jnp.logical_not(take_first))
    def _():
        out[...] = second[...]


def has_end(me, done, peers):
    return jnp.logical_or((me & ~done) == 0, (me | done) == peers - 1)


def has_dyn(me, frame, done):
    return ((me ^ (frame // FR_DEV)) & ~done) == 0


def pack_kernel(peers, bank_ref, key_ref, value_ref, keep_ref, send_ref):
    me = lax.axis_index("tm")
    slots = bank_ref.shape[0]
    frame_len = key_ref.shape[0] // FR_DEV
    last_frame = peers * FR_DEV - 1
    dyns = dyn_frames(bank_ref, slots, last_frame)
    even = (me & 1) == 0
    rows = [(dyn % FR_DEV) for dyn in dyns] + [jnp.where(me == peers - 1, FR_DEV - 1, 0)]
    for j, row in enumerate(rows):
        part = pl.ds(pl.multiple_of(row * frame_len, frame_len), frame_len)
        choose(keep_ref.at[j], even, key_ref.at[part], value_ref.at[part])
        choose(send_ref.at[j], even, value_ref.at[part], key_ref.at[part])


def split_kernel(peers, bank_ref, mine_ref, got_ref, low_ref, high_ref):
    me = lax.axis_index("tm")
    slots = bank_ref.shape[0]
    half = mine_ref.shape[1] // 2
    dyns = dyn_frames(bank_ref, slots, peers * FR_DEV - 1)
    flags = [has_dyn(me, dyn, 0) for dyn in dyns] + [has_end(me, 0, peers)]
    for j, flag in enumerate(flags):
        for out, start in ((low_ref, 0), (high_ref, half)):
            part = pl.ds(start, half)
            choose(out.at[j], flag, mine_ref.at[j, part], got_ref.at[j, part])


def step_kernel(peers, low_done, high_done, bank_ref, low_mine, low_got, high_mine, high_got, low_ref, high_ref):
    me = lax.axis_index("tm")
    slots = bank_ref.shape[0]
    dyns = dyn_frames(bank_ref, slots, peers * FR_DEV - 1)
    for out, mine, got, done in (
        (low_ref, low_mine, low_got, low_done),
        (high_ref, high_mine, high_got, high_done),
    ):
        flags = [has_dyn(me, dyn, done) for dyn in dyns] + [has_end(me, done, peers)]
        for j, flag in enumerate(flags):
            choose(out.at[j], flag, mine.at[j], got.at[j])


def pick_kernel(
    peers,
    low_bit,
    high_bit,
    bank_ref,
    index_ref,
    other_index_ref,
    low_mine,
    low_got,
    high_mine,
    high_got,
    own_ref,
    other_ref,
):
    me = lax.axis_index("tm")
    slots = bank_ref.shape[0]
    half = low_mine.shape[1]
    last_frame = peers * FR_DEV - 1
    dyns = dyn_frames(bank_ref, slots, last_frame)
    for out, chosen in ((own_ref, index_ref), (other_ref, other_index_ref)):
        for m in range(MEM):
            frame = bank_ref[chosen[0, m]]
            place = place_of(frame, dyns, last_frame)
            source = jnp.minimum(place, len(dyns))
            for start, mine, got, bit in (
                (0, low_mine, low_got, low_bit),
                (half, high_mine, high_got, high_bit),
            ):
                upper = (me & bit) != 0
                done = (peers - 1) & ~bit
                local = jnp.where(frame == 0, jnp.logical_not(upper), upper)
                for j, dyn in enumerate(dyns):
                    local = jnp.where(frame == dyn, has_dyn(me, dyn, done), local)
                choose(out.at[m, pl.ds(start, half)], local, mine.at[source], got.at[source])


def attend_kernel(
    peers,
    pose_ref,
    bias_ref,
    index_ref,
    bank_ref,
    query_ref,
    cotangent_ref,
    prev_key_ref,
    prev_value_ref,
    key_ref,
    value_ref,
    mem_mine_ref,
    mem_got_ref,
    attended_ref,
    grad_query_ref,
    back_ref,
    own_ref,
    mem_same_ref,
    mem_other_ref,
):
    me = lax.axis_index("tm")
    row_count, columns = query_ref.shape
    frame_len = row_count // FR_DEV
    depth = 128
    factor = 1.0 / math.sqrt(depth)
    even = (me & 1) == 0
    own_ids = [me * FR_DEV + j for j in range(FR_DEV)]
    prev_ids = [jnp.maximum(own - FR_DEV, 0) for own in own_ids]
    mem_ids = [bank_ref[index_ref[0, m]] for m in range(MEM)]
    query_poses = [pose_ref[f] for f in own_ids]
    lane_frame = lax.broadcasted_iota(jnp.int32, (1, row_count), 1) // frame_len
    blocked = me == 0
    f32 = jnp.float32

    def dot(a, b, contract):
        return lax.dot_general(a, b, ((contract[:1], contract[1:]), ((), ())), preferred_element_type=f32)

    for local in range(columns // depth):
        head = pl.program_id(0) * (columns // depth) + local
        cols = pl.ds(local * depth, depth)
        query = query_ref[:, cols]
        cotangent = cotangent_ref[:, cols]
        mine = mem_mine_ref[:, :, cols].reshape(MEM * frame_len, depth)
        got = mem_got_ref[:, :, cols].reshape(MEM * frame_len, depth)
        keys = [prev_key_ref[:, cols], key_ref[:, cols], jnp.where(even, mine, got)]
        values = [prev_value_ref[:, cols], value_ref[:, cols], jnp.where(even, got, mine)]
        logits = []
        peak = None
        for piece, ids in enumerate((prev_ids, own_ids, mem_ids)):
            raw = dot(keys[piece], query, (1, 1)) * (factor * LOG2E)
            rows = []
            for j, frame in enumerate(ids):
                key_pose = pose_ref[frame]
                bias = jnp.zeros((1, row_count), f32)
                for a, query_pose in enumerate(query_poses):
                    value = bias_ref[head, query_pose, key_pose] * LOG2E
                    if piece == 0:
                        value = jnp.where(blocked, BLOCKED_LOGIT, value)
                    bias = jnp.where(lane_frame == a, value, bias)
                rows.append(raw[j * frame_len : (j + 1) * frame_len] + bias)
            block = jnp.concatenate(rows, axis=0)
            logits.append(block)
            block_peak = jnp.max(block, axis=0, keepdims=True)
            peak = block_peak if peak is None else jnp.maximum(peak, block_peak)
        exps = [jnp.exp2(block - peak) for block in logits]
        total = sum(jnp.sum(block, axis=0, keepdims=True) for block in exps)
        inverse = 1.0 / total
        probs = [block * inverse for block in exps]
        weights = [block.astype(jnp.bfloat16) for block in probs]
        slopes = [dot(value, cotangent, (1, 1)) for value in values]
        spread = sum(jnp.sum(p * s, axis=0, keepdims=True) for p, s in zip(probs, slopes))
        dlogits = [(p * (s - spread)).astype(jnp.bfloat16) for p, s in zip(probs, slopes)]
        attended = sum(dot(value, w, (0, 0)) for value, w in zip(values, weights))
        attended_ref[:, cols] = attended.T.astype(jnp.bfloat16)
        grad_query = sum(dot(key, d, (0, 0)) for key, d in zip(keys, dlogits)) * factor
        grad_query_ref[:, cols] = grad_query.T.astype(jnp.bfloat16)
        key_terms = [dot(d, query, (1, 0)) * factor for d in dlogits]
        value_terms = [dot(w, cotangent, (1, 0)) for w in weights]
        back_ref[0, :, cols] = key_terms[0].astype(jnp.bfloat16)
        back_ref[1, :, cols] = value_terms[0].astype(jnp.bfloat16)
        own_ref[0, :, cols] = key_terms[1]
        own_ref[1, :, cols] = value_terms[1]
        shape = (MEM, frame_len, depth)
        key_part = key_terms[2].astype(jnp.bfloat16).reshape(shape)
        value_part = value_terms[2].astype(jnp.bfloat16).reshape(shape)
        mem_same_ref[:, :, cols] = jnp.where(even, key_part, value_part)
        mem_other_ref[:, :, cols] = jnp.where(even, value_part, key_part)


def sum_kernel(
    peers,
    low_bit,
    high_bit,
    bank_ref,
    index_ref,
    other_index_ref,
    mine_ref,
    got_ref,
    low_keep,
    low_send,
    high_keep,
    high_send,
):
    me = lax.axis_index("tm")
    slots = bank_ref.shape[0]
    half = mine_ref.shape[1] // 2
    last_frame = peers * FR_DEV - 1
    dyns = dyn_frames(bank_ref, slots, last_frame)
    named = [(bank_ref[index_ref[0, m]], mine_ref, m) for m in range(MEM)]
    named += [(bank_ref[other_index_ref[0, m]], got_ref, m) for m in range(MEM)]
    for start, keep, send, bit in ((0, low_keep, low_send, low_bit), (half, high_keep, high_send, high_bit)):
        upper = (me & bit) != 0
        near = jnp.where(upper, last_frame, 0)
        far = jnp.where(upper, 0, last_frame)
        part = pl.ds(start, half)
        terms = [ref[m, part].astype(jnp.float32) for _, ref, m in named]

        def total(frame):
            return sum(jnp.where(name == frame, term, 0.0) for (name, _, _), term in zip(named, terms))

        for j, dyn in enumerate(dyns):
            value = total(dyn)
            keep[j] = value
            send[j] = value.astype(jnp.bfloat16)
        keep[len(dyns)] = total(near)
        send[len(dyns)] = total(far).astype(jnp.bfloat16)


def add_kernel(low_keep, low_got, high_keep, high_got, low_out, low_send, high_out, high_send):
    for keep, got, out, send in ((low_keep, low_got, low_out, low_send), (high_keep, high_got, high_out, high_send)):
        value = keep[...] + got[...].astype(jnp.float32)
        out[...] = value
        send[...] = value.astype(jnp.bfloat16)


def owned_kernel(peers, bank_ref, low_keep, low_got, high_keep, high_got, mine_ref, other_ref):
    me = lax.axis_index("tm")
    slots = bank_ref.shape[0]
    half = low_keep.shape[1]
    last_frame = peers * FR_DEV - 1
    dyns = dyn_frames(bank_ref, slots, last_frame)
    for start, keep, got in ((0, low_keep, low_got), (half, high_keep, high_got)):
        part = pl.ds(start, half)
        for out, group in ((mine_ref, me), (other_ref, me ^ 1)):
            for j in range(FR_DEV):
                frame = group * FR_DEV + j
                named = jnp.logical_or(frame == 0, frame == last_frame)
                place = jnp.int32(len(dyns))
                for d, dyn in enumerate(dyns):
                    named = jnp.logical_or(named, frame == dyn)
                    place = jnp.where(frame == dyn, d, place)

                @pl.when(named)
                def _(out=out, j=j, place=place):
                    value = keep[place] + got[place].astype(jnp.float32)
                    out[j, part] = value.astype(out.dtype)

                @pl.when(jnp.logical_not(named))
                def _(out=out, j=j):
                    out[j, part] = jnp.zeros((half, out.shape[2]), out.dtype)


def final_kernel(own_ref, back_ref, mine_ref, got_ref, grad_key_ref, grad_value_ref):
    even = (lax.axis_index("tm") & 1) == 0
    shape = grad_key_ref.shape
    mine = mine_ref[...].reshape(shape)
    got = got_ref[...].astype(jnp.float32).reshape(shape)
    key_sum = own_ref[0] + back_ref[0].astype(jnp.float32) + jnp.where(even, mine, got)
    value_sum = own_ref[1] + back_ref[1].astype(jnp.float32) + jnp.where(even, got, mine)
    grad_key_ref[...] = key_sum.astype(jnp.bfloat16)
    grad_value_ref[...] = value_sum.astype(jnp.bfloat16)


def body(
    query_states,
    key_states,
    value_states,
    grad_out,
    camera_pose,
    pose_bias,
    memory_index,
    bank_frames,
):
    row_count, width = query_states.shape
    frame_len = row_count // FR_DEV
    half = frame_len // 2
    slots = bank_frames.shape[0]
    peers = lax.axis_size("tm")
    bits = [1 << i for i in range(1, peers.bit_length() - 1)]
    kept = slots - 1
    bf16, f32 = jnp.bfloat16, jnp.float32

    def shape(dtype, *dims):
        return jax.ShapeDtypeStruct(dims, dtype)

    def call(kernel, outs, scalars, arrays):
        return pl.pallas_call(
            kernel,
            out_shape=outs,
            in_specs=[SMEM] * len(scalars) + [VMEM] * len(arrays),
            out_specs=[VMEM] * len(outs),
            compiler_params=PARAMS,
        )(*scalars, *arrays)

    prev_keys = passed_along(key_states, 1, peers)
    prev_values = passed_along(value_states, 1, peers)
    other_index = swap(memory_index, 1, peers)
    frames = shape(bf16, kept, frame_len, width)
    halves = shape(bf16, kept, half, width)
    sums = shape(f32, kept, half, width)
    keep, send = call(functools.partial(pack_kernel, peers), [frames] * 2, [bank_frames], [key_states, value_states])
    got = swap(send, 1, peers)
    low, high = call(functools.partial(split_kernel, peers), [halves] * 2, [bank_frames], [keep, got])
    low_done = high_done = 1
    for step, (low_bit, high_bit) in enumerate(zip(bits, bits[::-1])):
        low_got = swap(low, low_bit, peers)
        high_got = swap(high, high_bit, peers)
        if step + 1 < len(bits):
            low, high = call(
                functools.partial(step_kernel, peers, low_done, high_done),
                [halves] * 2,
                [bank_frames],
                [low, low_got, high, high_got],
            )
        low_done |= low_bit
        high_done |= high_bit
    chosen = shape(bf16, MEM, frame_len, width)
    mem_mine, mem_send = call(
        functools.partial(pick_kernel, peers, bits[-1], bits[0]),
        [chosen] * 2,
        [bank_frames, memory_index, other_index],
        [low, low_got, high, high_got],
    )
    mem_got = swap(mem_send, 1, peers)

    columns = 256
    rows_spec = pl.BlockSpec((row_count, columns), lambda i: (0, i))
    pair_spec = pl.BlockSpec((2, row_count, columns), lambda i: (0, 0, i))
    mem_spec = pl.BlockSpec((MEM, frame_len, columns), lambda i: (0, 0, i))
    attended, grad_query, back, own, mem_same, mem_other = pl.pallas_call(
        functools.partial(attend_kernel, peers),
        grid=(width // columns,),
        out_shape=[
            shape(bf16, row_count, width),
            shape(bf16, row_count, width),
            shape(bf16, 2, row_count, width),
            shape(f32, 2, row_count, width),
            chosen,
            chosen,
        ],
        in_specs=[SMEM] * 4 + [rows_spec] * 6 + [mem_spec] * 2,
        out_specs=[rows_spec] * 2 + [pair_spec] * 2 + [mem_spec] * 2,
        compiler_params=PARAMS,
    )(
        camera_pose,
        pose_bias,
        memory_index,
        bank_frames,
        query_states,
        grad_out,
        prev_keys,
        prev_values,
        key_states,
        value_states,
        mem_mine,
        mem_got,
    )
    same_got = swap(mem_other, 1, peers)
    back_got = passed_along(back, -1, peers)
    low_keep, low_send, high_keep, high_send = call(
        functools.partial(sum_kernel, peers, bits[-1], bits[0]),
        [sums, halves] * 2,
        [bank_frames, memory_index, other_index],
        [mem_same, same_got],
    )
    for step, (low_bit, high_bit) in enumerate(zip(bits[::-1], bits)):
        low_got = swap(low_send, low_bit, peers)
        high_got = swap(high_send, high_bit, peers)
        if step + 1 < len(bits):
            low_keep, low_send, high_keep, high_send = call(
                add_kernel, [sums, halves] * 2, [], [low_keep, low_got, high_keep, high_got]
            )
    owned_mine, owned_send = call(
        functools.partial(owned_kernel, peers),
        [shape(f32, FR_DEV, frame_len, width), shape(bf16, FR_DEV, frame_len, width)],
        [bank_frames],
        [low_keep, low_got, high_keep, high_got],
    )
    owned_got = swap(owned_send, 1, peers)
    grad_key, grad_value = call(
        final_kernel, [shape(bf16, row_count, width)] * 2, [], [own, back_got, owned_mine, owned_got]
    )
    return (attended, grad_query, grad_key, grad_value)


def solution(mesh):
    rows = P(("traj", "tm"), None)
    in_specs = (rows, rows, rows, rows, P("traj"), P(), rows, P("traj"))
    return jax.shard_map(body, mesh=mesh, in_specs=in_specs, out_specs=(rows,) * 4, check_vma=False)
```

time: 203 us -> 76.8 us (0.38)
  waiting for transfers between devices: 84 us -> 38.3 us
  local copies, waits for them, and re-layouts: 41.5 us -> 2.66 us
  between operations: 24.9 us -> 0.81 us
  matrix products: 22.5 us -> 0 us
  other arithmetic: 19.5 us -> 0 us
  Pallas kernels: 0 us -> 14.1 us
  starting transfers between devices: 9.77 us -> 20.7 us
    psum x2 -> x0, waiting for transfers between devices: 84 us -> none  [the longest x1 42.8 us: broadcast(): return lax.psum(block, axis)]
    ppermute x4 -> x16, waiting for transfers between devices: 0.01 us -> 38.3 us  [the longest x13 38.3 us: swap(): return lax.ppermute(block, 'tm', [(i, i ^ bit) for i in range(peers)])]
    dot_general x8 -> x0, matrix products: 22.5 us -> none  [the longest x1 6.49 us: attend(): jnp.einsum('hqk,qhd->khd', weights, cotangent_heads, preferred_element_ty...]
    pallas_call x0 -> x9, Pallas kernels: none -> 14.1 us  [the longest x1 8.44 us: body(): pl.pallas_call(functools.partial(attend_kernel, peers), grid=(width // co...]
    ppermute x4 -> x16, starting transfers between devices: 9.69 us -> 20.7 us  [the longest x13 14 us: swap(): return lax.ppermute(block, 'tm', [(i, i ^ bit) for i in range(peers)])]
    add x2 -> x0, local copies, waits for them, and re-layouts: 10.7 us -> none  [biased_logits(): return logits + bias_rows[:, :, None, :, None]]
    slice x7 -> x0, local copies, waits for them, and re-layouts: 8.95 us -> none  [the longest x2 2.63 us: body(): value_grad[row_count:2 * row_count] + back_values + own_value_add]
    reduce_sum x3 -> x0, other arithmetic: 5.65 us -> none  [the longest x1 3.6 us: body(): jnp.sum(jnp.where(select[:, :, None, None], mem_value_grad[:, None], 0.0)...]
  transfers between devices with their start and end apart: 6 -> 16, of which waited for: 2 -> 11; matrix products, arithmetic and copies ran while one was open for 21% -> 0% of each run, Pallas kernels for 0% -> 2%
where the time goes in v1:
time: 76.8 us; the launch traced here: 76.6 us
  waiting for transfers between devices  38.3 us (50%)
  starting transfers between devices  20.7 us (27%)
  Pallas kernels  14.1 us (18%)
  local copies, waits for them, and re-layouts  2.66 us (3%)
  between operations  0.81 us (1%)
    ppermute x13, waiting for transfers between devices, swap(): return lax.ppermute(block, 'tm', [(i, i ^ bit) for i in range(peers)])  38.3 us
    ppermute x13, starting transfers between devices, swap(): return lax.ppermute(block, 'tm', [(i, i ^ bit) for i in range(peers)])  14 us
    pallas_call x1, Pallas kernels, body(): pl.pallas_call(functools.partial(attend_kernel, peers), grid=(width // co...  8.44 us
    ppermute x3, starting transfers between devices, passed_along(): return lax.ppermute(block, 'tm', pairs)  6.71 us
    pallas_call x8, Pallas kernels, call(): pl.pallas_call(kernel, out_shape=outs, in_specs=[SMEM] * len(scalars) + [...  5.66 us
    unnamed x20, local copies, waits for them, and re-layouts  2.66 us
  transfers between devices with their start and end apart: 16, of which 11 were waited for; matrix products, arithmetic and copies ran while one was open for 0% of the time, Pallas kernels for 2%

profile of v1, /device:TPU:0, one launch (start us, length us, event | category | flops | bytes accessed | tf_op | source)
XLA Modules:
  0.0 76.6 jit_solution(13860100183846491630)
XLA Ops:
  0.6 0.0 copy-start
  0.6 1.0 %copy-done = bf16[256,768]{1,0:T(8,128)(2,1)S(1)} copy-done((bf16[256,768]{1,0:T(8,128)(2,1)S(1)}, bf16[256,768]{1,0:T(8,128)(2,1)}, u32[]{:S(2)}) %copy-start) | copy-done | bytes 393240
  1.6 1.0 %copy-done.2 = bf16[256,768]{1,0:T(8,128)(2,1)S(1)} copy-done((bf16[256,768]{1,0:T(8,128)(2,1)S(1)}, bf16[256,768]{1,0:T(8,128)(2,1)}, u32[]{:S(2)}) %copy-start.2) | copy-done | bytes 393240
  2.6 0.7 copy-done.7
  3.3 0.7 shard_map.111
  4.0 0.5 collective-permute-start.3
  4.5 1.6 %collective-permute-done.3.got_ref = bf16[3,128,768]{2,1,0:T(8,128)(2,1)S(1)} collective-permute-done((bf16[3,128,768]{2,1,0:T(8,128)(2,1)S(1)}, bf16[3,128,768]{2,1,0:T(8,128)(2,1)S(1)}, u32[]{:S(2)}, u32[]{:S(2)}) %collective-permute-start.3) | collective-permute-done | bytes 589856 | tf_op jit(solution)/shard_map/ppermute | solution.py:23
  6.1 0.6 shard_map.112
  6.7 2.9 %collective-permute-start.4 = (bf16[3,64,768]{2,1,0:T(8,128)(2,1)S(1)}, bf16[3,64,768]{2,1,0:T(8,128)(2,1)S(1)}, u32[]{:S(2)}, u32[]{:S(2)}) collective-permute-start(bf16[3,64,768]{2,1,0:T(8,128)(2,1)S(1)} %get-tuple-element.32.low_mine), channel_id=1, source_target_pairs={{0,2},{1,3},{2,0},{3,1},{4,6},{5,7},{6,4},{7,5},{8,10},{9,11},{10,... | collective-permute-start | bytes 884744 | tf_op jit(solution)/shard_map/ppermute | solution.py:23
  9.7 1.5 %collective-permute-start.5 = (bf16[3,64,768]{2,1,0:T(8,128)(2,1)S(1)}, bf16[3,64,768]{2,1,0:T(8,128)(2,1)S(1)}, u32[]{:S(2)}, u32[]{:S(2)}) collective-permute-start(bf16[3,64,768]{2,1,0:T(8,128)(2,1)S(1)} %get-tuple-element.33.high_mine), channel_id=1, source_target_pairs={{0,4},{1,5},{2,6},{3,7},{4,0},{5,1},{6,2},{7,3},{8,12},{9,13},{10,... | collective-permute-start | bytes 884744 | tf_op jit(solution)/shard_map/ppermute | solution.py:23
  11.2 5.8 %collective-permute-done.4.low_got = bf16[3,64,768]{2,1,0:T(8,128)(2,1)S(1)} collective-permute-done((bf16[3,64,768]{2,1,0:T(8,128)(2,1)S(1)}, bf16[3,64,768]{2,1,0:T(8,128)(2,1)S(1)}, u32[]{:S(2)}, u32[]{:S(2)}) %collective-permute-start.4) | collective-permute-done | bytes 294944 | tf_op jit(solution)/shard_map/ppermute | solution.py:23
  17.0 1.5 %collective-permute-done.5.high_got = bf16[3,64,768]{2,1,0:T(8,128)(2,1)S(1)} collective-permute-done((bf16[3,64,768]{2,1,0:T(8,128)(2,1)S(1)}, bf16[3,64,768]{2,1,0:T(8,128)(2,1)S(1)}, u32[]{:S(2)}, u32[]{:S(2)}) %collective-permute-start.5) | collective-permute-done | bytes 294944 | tf_op jit(solution)/shard_map/ppermute | solution.py:23
  18.4 0.6 shard_map.113
  19.1 1.6 %collective-permute-start.6 = (bf16[3,64,768]{2,1,0:T(8,128)(2,1)S(1)}, bf16[3,64,768]{2,1,0:T(8,128)(2,1)S(1)}, u32[]{:S(2)}, u32[]{:S(2)}) collective-permute-start(bf16[3,64,768]{2,1,0:T(8,128)(2,1)S(1)} %get-tuple-element.34.low_mine), channel_id=1, source_target_pairs={{0,4},{1,5},{2,6},{3,7},{4,0},{5,1},{6,2},{7,3},{8,12},{9,13},{10,... | collective-permute-start | bytes 884744 | tf_op jit(solution)/shard_map/ppermute | solution.py:23
  20.7 0.5 collective-permute-start.7
  21.2 0.0 copy-done.1
  21.2 1.3 %collective-permute-start = (bf16[256,768]{1,0:T(8,128)(2,1)S(1)}, bf16[256,768]{1,0:T(8,128)(2,1)S(1)}, u32[]{:S(2)}, u32[]{:S(2)}) collective-permute-start(bf16[256,768]{1,0:T(8,128)(2,1)S(1)} %copy-done.1), channel_id=1, source_target_pairs={{0,1},{1,2},{2,3},{3,4},{4,5},{5,6},{6,7},{8,9},{9,10},{10,11},{11... | collective-permute-start | bytes 1179656 | tf_op jit(solution)/shard_map/ppermute | solution.py:28
  22.5 4.1 %collective-permute-start.1 = (bf16[256,768]{1,0:T(8,128)(2,1)S(1)}, bf16[256,768]{1,0:T(8,128)(2,1)S(1)}, u32[]{:S(2)}, u32[]{:S(2)}) collective-permute-start(bf16[256,768]{1,0:T(8,128)(2,1)S(1)} %copy-done.3), channel_id=1, source_target_pairs={{0,1},{1,2},{2,3},{3,4},{4,5},{5,6},{6,7},{8,9},{9,10},{10,11},{11... | collective-permute-start | bytes 1179656 | tf_op jit(solution)/shard_map/ppermute | solution.py:28
  26.7 0.0 copy-done.8
  26.7 0.1 collective-permute-start.2
  26.7 1.2 %collective-permute-done.2.other_index_ref = s32[1,2]{1,0:T(1,128)S(1)} collective-permute-done((s32[1,2]{1,0:T(1,128)S(1)}, s32[1,2]{1,0:T(1,128)S(1)}, u32[]{:S(2)}, u32[]{:S(2)}) %collective-permute-start.2) | collective-permute-done | bytes 40 | tf_op jit(solution)/shard_map/ppermute | solution.py:23
  28.0 0.0 collective-permute-done.6.low_got
  28.0 2.6 %collective-permute-done.7.high_got = bf16[3,64,768]{2,1,0:T(8,128)(2,1)S(1)} collective-permute-done((bf16[3,64,768]{2,1,0:T(8,128)(2,1)S(1)}, bf16[3,64,768]{2,1,0:T(8,128)(2,1)S(1)}, u32[]{:S(2)}, u32[]{:S(2)}) %collective-permute-start.7) | collective-permute-done | bytes 294944 | tf_op jit(solution)/shard_map/ppermute | solution.py:23
  30.6 0.8 shard_map.114
  31.4 0.1 collective-permute-start.8
  31.4 0.0 collective-permute-done.prev_key_ref
  31.5 0.0 collective-permute-done.1.prev_value_ref
  31.5 1.7 %collective-permute-done.8.mem_got_ref = bf16[2,128,768]{2,1,0:T(8,128)(2,1)S(1)} collective-permute-done((bf16[2,128,768]{2,1,0:T(8,128)(2,1)S(1)}, bf16[2,128,768]{2,1,0:T(8,128)(2,1)S(1)}, u32[]{:S(2)}, u32[]{:S(2)}) %collective-permute-start.8) | collective-permute-done | bytes 393248 | tf_op jit(solution)/shard_map/ppermute | solution.py:23
  33.2 0.0 copy-done.9
  33.2 8.4 %shard_map.115 = (bf16[256,768]{1,0:T(8,128)(2,1)}, bf16[256,768]{1,0:T(8,128)(2,1)}, bf16[2,256,768]{2,1,0:T(8,128)(2,1)S(1)}, f32[2,256,768]{2,1,0:T(8,128)S(1...) custom-call(s32[16]{0:T(128)S(1)} %copy-done.9, f32[6,16,16]{2,1,0:T(8,128)S(1)} %copy-done.6, ...), custom_call_target="tpu_custom_call" | custom-call | tf_op jit(solution)/shard_map/pallas_call | solution.py:383
  41.6 1.8 %collective-permute-start.10 = (bf16[2,128,768]{2,1,0:T(8,128)(2,1)S(1)}, bf16[2,128,768]{2,1,0:T(8,128)(2,1)S(1)}, u32[]{:S(2)}, u32[]{:S(2)}) collective-permute-start(bf16[2,128,768]{2,1,0:T(8,128)(2,1)S(1)} %get-tuple-element.43), channel_id=1, source_target_pairs={{0,1},{1,0},{2,3},{3,2},{4,5},{5,4},{6,7},{7,6},{8,9},{9,8},{10,11... | collective-permute-start | bytes 1179656 | tf_op jit(solution)/shard_map/ppermute | solution.py:23
  43.4 1.3 %collective-permute-done.10.got_ref = bf16[2,128,768]{2,1,0:T(8,128)(2,1)S(1)} collective-permute-done((bf16[2,128,768]{2,1,0:T(8,128)(2,1)S(1)}, bf16[2,128,768]{2,1,0:T(8,128)(2,1)S(1)}, u32[]{:S(2)}, u32[]{:S(2)}) %collective-permute-start.10) | collective-permute-done | bytes 393248 | tf_op jit(solution)/shard_map/ppermute | solution.py:23
  44.8 1.0 %shard_map.116 = (f32[3,64,768]{2,1,0:T(8,128)S(1)}, bf16[3,64,768]{2,1,0:T(8,128)(2,1)S(1)}, f32[3,64,768]{2,1,0:T(8,128)S(1)}, bf16[3,64,768]{2,1,0:T(8,128)(2,1)S(1)}) custom-call(s32[4]{0:T(128)S(1)} %copy-done.7, s32[1,2]{1,0:T(1,128)S(1)} %copy-done.8, s32[1,2]{1,0:T(1,128)S(1)} %collective-permute-done.2.other_index_ref, ...), custom_call_target="tpu_custom_call" | custom-call | tf_op jit(solution)/shard_map/pallas_call | solution.py:340
  45.8 3.7 %collective-permute-start.11 = (bf16[3,64,768]{2,1,0:T(8,128)(2,1)S(1)}, bf16[3,64,768]{2,1,0:T(8,128)(2,1)S(1)}, u32[]{:S(2)}, u32[]{:S(2)}) collective-permute-start(bf16[3,64,768]{2,1,0:T(8,128)(2,1)S(1)} %get-tuple-element.45), channel_id=1, source_target_pairs={{0,4},{1,5},{2,6},{3,7},{4,0},{5,1},{6,2},{7,3},{8,12},{9,13},{10,... | collective-permute-start | bytes 884744 | tf_op jit(solution)/shard_map/ppermute | solution.py:23
  49.4 0.0 collective-permute-start.12
  49.4 1.3 %collective-permute-start.9 = (bf16[2,256,768]{2,1,0:T(8,128)(2,1)S(1)}, bf16[2,256,768]{2,1,0:T(8,128)(2,1)S(1)}, u32[]{:S(2)}, u32[]{:S(2)}) collective-permute-start(bf16[2,256,768]{2,1,0:T(8,128)(2,1)S(1)} %get-tuple-element.41), channel_id=1, source_target_pairs={{1,0},{2,1},{3,2},{4,3},{5,4},{6,5},{7,6},{9,8},{10,9},{11,10},{12... | collective-permute-start | bytes 2359304 | tf_op jit(solution)/shard_map/ppermute | solution.py:28
  50.7 6.0 %collective-permute-done.11.low_got = bf16[3,64,768]{2,1,0:T(8,128)(2,1)S(1)} collective-permute-done((bf16[3,64,768]{2,1,0:T(8,128)(2,1)S(1)}, bf16[3,64,768]{2,1,0:T(8,128)(2,1)S(1)}, u32[]{:S(2)}, u32[]{:S(2)}) %collective-permute-start.11) | collective-permute-done | bytes 294944 | tf_op jit(solution)/shard_map/ppermute | solution.py:23
  56.7 1.5 %collective-permute-done.12.high_got = bf16[3,64,768]{2,1,0:T(8,128)(2,1)S(1)} collective-permute-done((bf16[3,64,768]{2,1,0:T(8,128)(2,1)S(1)}, bf16[3,64,768]{2,1,0:T(8,128)(2,1)S(1)}, u32[]{:S(2)}, u32[]{:S(2)}) %collective-permute-start.12) | collective-permute-done | bytes 294944 | tf_op jit(solution)/shard_map/ppermute | solution.py:23
  58.2 0.2 shard_map.117
  58.4 0.3 collective-permute-start.13
  58.7 0.9 %collective-permute-start.14 = (bf16[3,64,768]{2,1,0:T(8,128)(2,1)S(1)}, bf16[3,64,768]{2,1,0:T(8,128)(2,1)S(1)}, u32[]{:S(2)}, u32[]{:S(2)}) collective-permute-start(bf16[3,64,768]{2,1,0:T(8,128)(2,1)S(1)} %get-tuple-element.51), channel_id=1, source_target_pairs={{0,4},{1,5},{2,6},{3,7},{4,0},{5,1},{6,2},{7,3},{8,12},{9,13},{10,... | collective-permute-start | bytes 884744 | tf_op jit(solution)/shard_map/ppermute | solution.py:23
  59.6 13.3 %collective-permute-done.13.low_got = bf16[3,64,768]{2,1,0:T(8,128)(2,1)S(1)} collective-permute-done((bf16[3,64,768]{2,1,0:T(8,128)(2,1)S(1)}, bf16[3,64,768]{2,1,0:T(8,128)(2,1)S(1)}, u32[]{:S(2)}, u32[]{:S(2)}) %collective-permute-start.13) | collective-permute-done | bytes 294944 | tf_op jit(solution)/shard_map/ppermute | solution.py:23
  72.9 0.0 collective-permute-done.14.high_got
  73.0 0.7 shard_map.118
  73.7 0.1 collective-permute-start.15
  73.7 0.0 collective-permute-done.9.back_ref
  73.8 1.7 %collective-permute-done.15.got_ref = bf16[2,128,768]{2,1,0:T(8,128)(2,1)S(1)} collective-permute-done((bf16[2,128,768]{2,1,0:T(8,128)(2,1)S(1)}, bf16[2,128,768]{2,1,0:T(8,128)(2,1)S(1)}, u32[]{:S(2)}, u32[]{:S(2)}) %collective-permute-start.15) | collective-permute-done | bytes 393248 | tf_op jit(solution)/shard_map/ppermute | solution.py:23
  75.5 1.1 %shard_map.119 = (bf16[256,768]{1,0:T(8,128)(2,1)}, bf16[256,768]{1,0:T(8,128)(2,1)}) custom-call(f32[2,256,768]{2,1,0:T(8,128)S(1)} %get-tuple-element.40.own_ref, bf16[2,256,768]{2,1,0:T(8,128)(2,1)S(1)} %collective-permute-done.9.back_ref, f32[2,128,768]{2,1,0:T(8,128)S(1)} %get-tuple-element.52.mine_ref, ...), custom_call_target="tpu_custom_call" | custom-call | tf_op jit(solution)/shard_map/pallas_call | solution.py:340
  (13 shorter events, 0.0 us)
Async XLA Ops:
  0.6 1.0 %copy-start = (bf16[256,768]{1,0:T(8,128)(2,1)S(1)}, bf16[256,768]{1,0:T(8,128)(2,1)}, u32[]{:S(2)}) copy-start(bf16[256,768]{1,0:T(8,128)(2,1)} %key_ref.3) | copy-start | bytes 1179652
  1.6 1.0 %copy-start.2 = (bf16[256,768]{1,0:T(8,128)(2,1)S(1)}, bf16[256,768]{1,0:T(8,128)(2,1)}, u32[]{:S(2)}) copy-start(bf16[256,768]{1,0:T(8,128)(2,1)} %value_ref.3) | copy-start | bytes 1179652
  2.6 0.7 copy-start.7
  3.3 17.9 %copy-start.1 = (bf16[256,768]{1,0:T(8,128)(2,1)S(1)}, bf16[256,768]{1,0:T(8,128)(2,1)}, u32[]{:S(2)}) copy-start(bf16[256,768]{1,0:T(8,128)(2,1)} %key_ref.3) | copy-start | bytes 1179652
  3.3 19.2 %copy-start.3 = (bf16[256,768]{1,0:T(8,128)(2,1)S(1)}, bf16[256,768]{1,0:T(8,128)(2,1)}, u32[]{:S(2)}) copy-start(bf16[256,768]{1,0:T(8,128)(2,1)} %value_ref.3) | copy-start | bytes 1179652
  3.3 23.4 %copy-start.8 = (s32[1,2]{1,0:T(1,128)S(1)}, s32[1,2]{1,0:T(1,128)}, u32[]{:S(2)}) copy-start(s32[1,2]{1,0:T(1,128)} %index_ref.5) | copy-start | bytes 28
  4.0 2.1 %collective-permute-start.3 = (bf16[3,128,768]{2,1,0:T(8,128)(2,1)S(1)}, bf16[3,128,768]{2,1,0:T(8,128)(2,1)S(1)}, u32[]{:S(2)}, u32[]{:S(2)}) collective-permute-start(bf16[3,128,768]{2,1,0:T(8,128)(2,1)S(1)} %get-tuple-element.31), channel_id=1, source_target_pairs={{0,1},{1,0},{2,3},{3,2},{4,5},{5,4},{6,7},{7,6},{8,9},{9,8},{10,11... | collective-permute-start | bytes 1769480 | tf_op jit(solution)/shard_map/ppermute | solution.py:23
  6.1 27.1 %copy-start.4 = (bf16[256,768]{1,0:T(8,128)(2,1)S(1)}, bf16[256,768]{1,0:T(8,128)(2,1)}, u32[]{:S(2)}) copy-start(bf16[256,768]{1,0:T(8,128)(2,1)} %query_ref.1) | copy-start | bytes 1179652
  6.1 27.1 %copy-start.5 = (bf16[256,768]{1,0:T(8,128)(2,1)S(1)}, bf16[256,768]{1,0:T(8,128)(2,1)}, u32[]{:S(2)}) copy-start(bf16[256,768]{1,0:T(8,128)(2,1)} %cotangent_ref.1) | copy-start | bytes 1179652
  6.1 27.1 %copy-start.6 = (f32[6,16,16]{2,1,0:T(8,128)S(1)}, f32[6,16,16]{2,1,0:T(8,128)}, u32[]{:S(2)}) copy-start(f32[6,16,16]{2,1,0:T(8,128)} %bias_ref.1) | copy-start | bytes 18436
  6.1 27.1 %copy-start.9 = (s32[16]{0:T(128)S(1)}, s32[16]{0:T(128)}, u32[]{:S(2)}) copy-start(s32[16]{0:T(128)} %pose_ref.1) | copy-start | bytes 196
  6.7 10.2 %collective-permute-start.4 = (bf16[3,64,768]{2,1,0:T(8,128)(2,1)S(1)}, bf16[3,64,768]{2,1,0:T(8,128)(2,1)S(1)}, u32[]{:S(2)}, u32[]{:S(2)}) collective-permute-start(bf16[3,64,768]{2,1,0:T(8,128)(2,1)S(1)} %get-tuple-element.32.low_mine), channel_id=1, source_target_pairs={{0,2},{1,3},{2,0},{3,1},{4,6},{5,7},{6,4},{7,5},{8,10},{9,11},{10,... | collective-permute-start | bytes 884744 | tf_op jit(solution)/shard_map/ppermute | solution.py:23
  9.7 8.8 %collective-permute-start.5 = (bf16[3,64,768]{2,1,0:T(8,128)(2,1)S(1)}, bf16[3,64,768]{2,1,0:T(8,128)(2,1)S(1)}, u32[]{:S(2)}, u32[]{:S(2)}) collective-permute-start(bf16[3,64,768]{2,1,0:T(8,128)(2,1)S(1)} %get-tuple-element.33.high_mine), channel_id=1, source_target_pairs={{0,4},{1,5},{2,6},{3,7},{4,0},{5,1},{6,2},{7,3},{8,12},{9,13},{10,... | collective-permute-start | bytes 884744 | tf_op jit(solution)/shard_map/ppermute | solution.py:23
  19.1 8.9 %collective-permute-start.6 = (bf16[3,64,768]{2,1,0:T(8,128)(2,1)S(1)}, bf16[3,64,768]{2,1,0:T(8,128)(2,1)S(1)}, u32[]{:S(2)}, u32[]{:S(2)}) collective-permute-start(bf16[3,64,768]{2,1,0:T(8,128)(2,1)S(1)} %get-tuple-element.34.low_mine), channel_id=1, source_target_pairs={{0,4},{1,5},{2,6},{3,7},{4,0},{5,1},{6,2},{7,3},{8,12},{9,13},{10,... | collective-permute-start | bytes 884744 | tf_op jit(solution)/shard_map/ppermute | solution.py:23
  20.7 9.9 %collective-permute-start.7 = (bf16[3,64,768]{2,1,0:T(8,128)(2,1)S(1)}, bf16[3,64,768]{2,1,0:T(8,128)(2,1)S(1)}, u32[]{:S(2)}, u32[]{:S(2)}) collective-permute-start(bf16[3,64,768]{2,1,0:T(8,128)(2,1)S(1)} %get-tuple-element.35.high_mine), channel_id=1, source_target_pairs={{0,2},{1,3},{2,0},{3,1},{4,6},{5,7},{6,4},{7,5},{8,10},{9,11},{10,... | collective-permute-start | bytes 884744 | tf_op jit(solution)/shard_map/ppermute | solution.py:23
  21.2 10.3 %collective-permute-start = (bf16[256,768]{1,0:T(8,128)(2,1)S(1)}, bf16[256,768]{1,0:T(8,128)(2,1)S(1)}, u32[]{:S(2)}, u32[]{:S(2)}) collective-permute-start(bf16[256,768]{1,0:T(8,128)(2,1)S(1)} %copy-done.1), channel_id=1, source_target_pairs={{0,1},{1,2},{2,3},{3,4},{4,5},{5,6},{6,7},{8,9},{9,10},{10,11},{11... | collective-permute-start | bytes 1179656 | tf_op jit(solution)/shard_map/ppermute | solution.py:28
  22.5 8.9 %collective-permute-start.1 = (bf16[256,768]{1,0:T(8,128)(2,1)S(1)}, bf16[256,768]{1,0:T(8,128)(2,1)S(1)}, u32[]{:S(2)}, u32[]{:S(2)}) collective-permute-start(bf16[256,768]{1,0:T(8,128)(2,1)S(1)} %copy-done.3), channel_id=1, source_target_pairs={{0,1},{1,2},{2,3},{3,4},{4,5},{5,6},{6,7},{8,9},{9,10},{10,11},{11... | collective-permute-start | bytes 1179656 | tf_op jit(solution)/shard_map/ppermute | solution.py:28
  26.7 1.3 %collective-permute-start.2 = (s32[1,2]{1,0:T(1,128)S(1)}, s32[1,2]{1,0:T(1,128)S(1)}, u32[]{:S(2)}, u32[]{:S(2)}) collective-permute-start(s32[1,2]{1,0:T(1,128)S(1)} %copy-done.8), channel_id=1, source_target_pairs={{0,1},{1,0},{2,3},{3,2},{4,5},{5,4},{6,7},{7,6},{8,9},{9,8},{10,11... | collective-permute-start | bytes 32 | tf_op jit(solution)/shard_map/ppermute | solution.py:23
  31.4 1.8 %collective-permute-start.8 = (bf16[2,128,768]{2,1,0:T(8,128)(2,1)S(1)}, bf16[2,128,768]{2,1,0:T(8,128)(2,1)S(1)}, u32[]{:S(2)}, u32[]{:S(2)}) collective-permute-start(bf16[2,128,768]{2,1,0:T(8,128)(2,1)S(1)} %get-tuple-element.37), channel_id=1, source_target_pairs={{0,1},{1,0},{2,3},{3,2},{4,5},{5,4},{6,7},{7,6},{8,9},{9,8},{10,11... | collective-permute-start | bytes 1179656 | tf_op jit(solution)/shard_map/ppermute | solution.py:23
  41.6 3.1 %collective-permute-start.10 = (bf16[2,128,768]{2,1,0:T(8,128)(2,1)S(1)}, bf16[2,128,768]{2,1,0:T(8,128)(2,1)S(1)}, u32[]{:S(2)}, u32[]{:S(2)}) collective-permute-start(bf16[2,128,768]{2,1,0:T(8,128)(2,1)S(1)} %get-tuple-element.43), channel_id=1, source_target_pairs={{0,1},{1,0},{2,3},{3,2},{4,5},{5,4},{6,7},{7,6},{8,9},{9,8},{10,11... | collective-permute-start | bytes 1179656 | tf_op jit(solution)/shard_map/ppermute | solution.py:23
  45.8 11.0 %collective-permute-start.11 = (bf16[3,64,768]{2,1,0:T(8,128)(2,1)S(1)}, bf16[3,64,768]{2,1,0:T(8,128)(2,1)S(1)}, u32[]{:S(2)}, u32[]{:S(2)}) collective-permute-start(bf16[3,64,768]{2,1,0:T(8,128)(2,1)S(1)} %get-tuple-element.45), channel_id=1, source_target_pairs={{0,4},{1,5},{2,6},{3,7},{4,0},{5,1},{6,2},{7,3},{8,12},{9,13},{10,... | collective-permute-start | bytes 884744 | tf_op jit(solution)/shard_map/ppermute | solution.py:23
  49.4 8.8 %collective-permute-start.12 = (bf16[3,64,768]{2,1,0:T(8,128)(2,1)S(1)}, bf16[3,64,768]{2,1,0:T(8,128)(2,1)S(1)}, u32[]{:S(2)}, u32[]{:S(2)}) collective-permute-start(bf16[3,64,768]{2,1,0:T(8,128)(2,1)S(1)} %get-tuple-element.47), channel_id=1, source_target_pairs={{0,2},{1,3},{2,0},{3,1},{4,6},{5,7},{6,4},{7,5},{8,10},{9,11},{10,... | collective-permute-start | bytes 884744 | tf_op jit(solution)/shard_map/ppermute | solution.py:23
  49.4 24.3 %collective-permute-start.9 = (bf16[2,256,768]{2,1,0:T(8,128)(2,1)S(1)}, bf16[2,256,768]{2,1,0:T(8,128)(2,1)S(1)}, u32[]{:S(2)}, u32[]{:S(2)}) collective-permute-start(bf16[2,256,768]{2,1,0:T(8,128)(2,1)S(1)} %get-tuple-element.41), channel_id=1, source_target_pairs={{1,0},{2,1},{3,2},{4,3},{5,4},{6,5},{7,6},{9,8},{10,9},{11,10},{12... | collective-permute-start | bytes 2359304 | tf_op jit(solution)/shard_map/ppermute | solution.py:28
  58.4 14.6 %collective-permute-start.13 = (bf16[3,64,768]{2,1,0:T(8,128)(2,1)S(1)}, bf16[3,64,768]{2,1,0:T(8,128)(2,1)S(1)}, u32[]{:S(2)}, u32[]{:S(2)}) collective-permute-start(bf16[3,64,768]{2,1,0:T(8,128)(2,1)S(1)} %get-tuple-element.49), channel_id=1, source_target_pairs={{0,2},{1,3},{2,0},{3,1},{4,6},{5,7},{6,4},{7,5},{8,10},{9,11},{10,... | collective-permute-start | bytes 884744 | tf_op jit(solution)/shard_map/ppermute | solution.py:23
  58.7 14.2 %collective-permute-start.14 = (bf16[3,64,768]{2,1,0:T(8,128)(2,1)S(1)}, bf16[3,64,768]{2,1,0:T(8,128)(2,1)S(1)}, u32[]{:S(2)}, u32[]{:S(2)}) collective-permute-start(bf16[3,64,768]{2,1,0:T(8,128)(2,1)S(1)} %get-tuple-element.51), channel_id=1, source_target_pairs={{0,4},{1,5},{2,6},{3,7},{4,0},{5,1},{6,2},{7,3},{8,12},{9,13},{10,... | collective-permute-start | bytes 884744 | tf_op jit(solution)/shard_map/ppermute | solution.py:23
  73.7 1.8 %collective-permute-start.15 = (bf16[2,128,768]{2,1,0:T(8,128)(2,1)S(1)}, bf16[2,128,768]{2,1,0:T(8,128)(2,1)S(1)}, u32[]{:S(2)}, u32[]{:S(2)}) collective-permute-start(bf16[2,128,768]{2,1,0:T(8,128)(2,1)S(1)} %get-tuple-element.53), channel_id=1, source_target_pairs={{0,1},{1,0},{2,3},{3,2},{4,5},{5,4},{6,7},{7,6},{8,9},{9,8},{10,11... | collective-permute-start | bytes 1179656 | tf_op jit(solution)/shard_map/ppermute | solution.py:23

commit v2 on v1

v2 whole, which is shorter than its diff:
```python
import functools
import math

import jax
import jax.numpy as jnp
from jax import lax
from jax.experimental import pallas as pl
from jax.experimental.pallas import tpu as pltpu
from jax.sharding import PartitionSpec as P

FR_DEV = 2
MEM = 2
DEPTH = 128

BLOCKED_LOGIT = -1e30
LOG2E = math.log2(math.e)
FACTOR = 1.0 / math.sqrt(DEPTH)

SMEM = pl.BlockSpec(memory_space=pltpu.SMEM)
VMEM = pl.BlockSpec(memory_space=pltpu.VMEM)
ANY = pl.BlockSpec(memory_space=pl.ANY)
VMEM_LIMIT = 32 * 1024 * 1024
BF16, F32 = jnp.bfloat16, jnp.float32


def shape(dtype, *dims):
    return jax.ShapeDtypeStruct(dims, dtype)


def call(kernel, outs, arrays, scalars=(), after=(), flops=0, name=None):
    count = len(scalars) + len(arrays)

    def run(*refs):
        kernel(*refs[:count], *refs[count + len(after) :])

    return pl.pallas_call(
        run,
        out_shape=outs,
        in_specs=[SMEM] * len(scalars) + [VMEM] * len(arrays) + [ANY] * len(after),
        out_specs=[VMEM] * len(outs),
        compiler_params=pltpu.CompilerParams(vmem_limit_bytes=VMEM_LIMIT),
        cost_estimate=pl.CostEstimate(flops=flops, bytes_accessed=0, transcendentals=0) if flops else None,
        name=name,
    )(*scalars, *arrays, *after)


def swap(block, bit, peers):
    return lax.ppermute(block, "tm", [(i, i ^ bit) for i in range(peers)])


def shift(block, by, start, peers):
    pairs = [(i, i + by) for i in range(start, peers, 2) if 0 <= i + by < peers]
    return lax.ppermute(block, "tm", pairs)


def read_table(table_ref, row):
    return jnp.max(table_ref[row : row + 1, :])


def dyn_frames(bank, last_frame):
    found = [jnp.int32(0)] * (len(bank) - 2)
    seen = jnp.int32(0)
    for frame in bank:
        free = jnp.logical_and(frame != 0, frame != last_frame)
        for j in range(len(found)):
            found[j] = jnp.where(jnp.logical_and(free, seen == j), frame, found[j])
        seen = seen + free.astype(jnp.int32)
    return found


def choose(out, take_first, first, second):
    @pl.when(take_first)
    def _():
        out[...] = first[...]

    @pl.when(jnp.logical_not(take_first))
    def _():
        out[...] = second[...]


def has_end(me, done, peers):
    return jnp.logical_or((me & ~done) == 0, (me | done) == peers - 1)


def has_dyn(me, frame, done):
    return ((me ^ (frame // FR_DEV)) & ~done) == 0


def table_kernel(peers, bank_ref, index_ref, pose_ref, bias_ref, table_ref, rows_ref):
    me = lax.axis_index("tm")
    slots = bank_ref.shape[0]
    heads, _, row_count = rows_ref.shape
    lanes = table_ref.shape[1]
    mem_ids = [bank_ref[index_ref[0, m]] for m in range(MEM)]
    for row, value in enumerate([bank_ref[slot] for slot in range(slots)] + mem_ids):
        table_ref[row : row + 1, :] = jnp.full((1, lanes), value, jnp.int32)
    own_ids = [me * FR_DEV + j for j in range(FR_DEV)]
    prev_ids = [jnp.maximum(own - FR_DEV, 0) for own in own_ids]
    query_poses = [pose_ref[frame] for frame in own_ids]
    key_poses = [pose_ref[frame] for frame in prev_ids + own_ids + mem_ids]
    frame_of = lax.broadcasted_iota(jnp.int32, (1, row_count), 1) // (row_count // FR_DEV)
    for head in range(heads):
        for j, key_pose in enumerate(key_poses):
            row = jnp.zeros((1, row_count), F32)
            for a, query_pose in enumerate(query_poses):
                value = bias_ref[head, query_pose, key_pose] * LOG2E
                if j < FR_DEV:
                    value = jnp.where(me == 0, BLOCKED_LOGIT, value)
                row = jnp.where(frame_of == a, value, row)
            rows_ref[head, j : j + 1, :] = row


def split_kernel(peers, slots, table_ref, key_ref, value_ref, pair_key_ref, pair_value_ref, low_ref, high_ref):
    me = lax.axis_index("tm")
    frame_len = key_ref.shape[0] // FR_DEV
    half = frame_len // 2
    dyns = dyn_frames([read_table(table_ref, slot) for slot in range(slots)], peers * FR_DEV - 1)
    even = (me & 1) == 0
    places = [(has_dyn(me, dyn, 0), dyn % FR_DEV) for dyn in dyns]
    places.append((has_end(me, 0, peers), jnp.where(me < peers // 2, 0, FR_DEV - 1)))
    for j, (local, frame) in enumerate(places):
        for source, taken in (
            (key_ref, jnp.logical_and(even, local)),
            (value_ref, jnp.logical_and(jnp.logical_not(even), local)),
            (pair_key_ref, jnp.logical_and(even, jnp.logical_not(local))),
            (pair_value_ref, jnp.logical_not(jnp.logical_or(even, local))),
        ):

            @pl.when(taken)
            def _(source=source, j=j, frame=frame):
                start = pl.multiple_of(frame * frame_len, frame_len)
                low_ref[j] = source[pl.ds(start, half)]
                high_ref[j] = source[pl.ds(start + half, half)]


def step_kernel(peers, slots, done, table_ref, mine_ref, got_ref, out_ref):
    me = lax.axis_index("tm")
    dyns = dyn_frames([read_table(table_ref, slot) for slot in range(slots)], peers * FR_DEV - 1)
    flags = [has_dyn(me, dyn, done) for dyn in dyns] + [has_end(me, done, peers)]
    for j, flag in enumerate(flags):
        choose(out_ref.at[j], flag, mine_ref.at[j], got_ref.at[j])


def pick_kernel(
    peers, slots, low_bit, high_bit, table_ref, pair_table_ref, low_mine, low_got, high_mine, high_got, own_ref, pair_ref
):
    me = lax.axis_index("tm")
    half = low_mine.shape[1]
    dyns = dyn_frames([read_table(table_ref, slot) for slot in range(slots)], peers * FR_DEV - 1)
    for out, table in ((own_ref, table_ref), (pair_ref, pair_table_ref)):
        for m in range(MEM):
            frame = read_table(table, slots + m)
            source = jnp.int32(len(dyns))
            for j, dyn in enumerate(dyns):
                source = jnp.where(frame == dyn, j, source)
            for start, mine, got, bit in ((0, low_mine, low_got, low_bit), (half, high_mine, high_got, high_bit)):
                upper = (me & bit) != 0
                local = jnp.where(frame == 0, jnp.logical_not(upper), upper)
                for dyn in dyns:
                    local = jnp.where(frame == dyn, has_dyn(me, dyn, (peers - 1) & ~bit), local)
                choose(out.at[m, pl.ds(start, half)], local, mine.at[source], got.at[source])


def dot(a, b, left, right):
    return lax.dot_general(a, b, (((left,), (right,)), ((), ())), preferred_element_type=F32)


def logits_of(keys, query, rows_ref, head, piece):
    frame_len = query.shape[0] // FR_DEV
    raw = dot(keys, query, 1, 1) * (FACTOR * LOG2E)
    parts = []
    for j in range(FR_DEV):
        row = piece * FR_DEV + j
        parts.append(raw[j * frame_len : (j + 1) * frame_len] + rows_ref[head, row : row + 1, :])
    return jnp.concatenate(parts, axis=0)


def stats_kernel(rows_ref, query_ref, cotangent_ref, prev_key_ref, prev_value_ref, key_ref, value_ref, stats_ref):
    for head in range(query_ref.shape[1] // DEPTH):
        cols = pl.ds(head * DEPTH, DEPTH)
        query, cotangent = query_ref[:, cols], cotangent_ref[:, cols]
        logits = [
            logits_of(keys[:, cols], query, rows_ref, head, piece) for piece, keys in enumerate((prev_key_ref, key_ref))
        ]
        peak = functools.reduce(jnp.maximum, [jnp.max(block, axis=0, keepdims=True) for block in logits])
        exps = [jnp.exp2(block - peak) for block in logits]
        slopes = [dot(values[:, cols], cotangent, 1, 1) for values in (prev_value_ref, value_ref)]
        stats_ref[head, 0:1, :] = peak
        stats_ref[head, 1:2, :] = sum(jnp.sum(e, axis=0, keepdims=True) for e in exps)
        stats_ref[head, 2:3, :] = sum(jnp.sum(e * s, axis=0, keepdims=True) for e, s in zip(exps, slopes))


def memory_kernel(
    rows_ref, part_ref, query_ref, cotangent_ref, mine_ref, got_ref, stats_ref, mem_same_ref, mem_other_ref
):
    even = (lax.axis_index("tm") & 1) == 0
    frame_len = mine_ref.shape[1]
    for head in range(query_ref.shape[1] // DEPTH):
        cols = pl.ds(head * DEPTH, DEPTH)
        query, cotangent = query_ref[:, cols], cotangent_ref[:, cols]
        mine = mine_ref[:, :, cols].reshape(MEM * frame_len, DEPTH)
        got = got_ref[:, :, cols].reshape(MEM * frame_len, DEPTH)
        keys, values = jnp.where(even, mine, got), jnp.where(even, got, mine)
        logits = logits_of(keys, query, rows_ref, head, 2)
        part_peak = part_ref[head, 0:1, :]
        peak = jnp.maximum(part_peak, jnp.max(logits, axis=0, keepdims=True))
        exps = jnp.exp2(logits - peak)
        slopes = dot(values, cotangent, 1, 1)
        scale = jnp.exp2(part_peak - peak)
        total = part_ref[head, 1:2, :] * scale + jnp.sum(exps, axis=0, keepdims=True)
        inverse = 1.0 / total
        spread = (part_ref[head, 2:3, :] * scale + jnp.sum(exps * slopes, axis=0, keepdims=True)) * inverse
        stats_ref[head, 0:1, :] = peak
        stats_ref[head, 1:2, :] = inverse
        stats_ref[head, 2:3, :] = spread
        probs = exps * inverse
        dlogits = (probs * (slopes - spread)).astype(BF16)
        key_part = (dot(dlogits, query, 1, 0) * FACTOR).astype(BF16).reshape(MEM, frame_len, DEPTH)
        value_part = dot(probs.astype(BF16), cotangent, 1, 0).astype(BF16).reshape(MEM, frame_len, DEPTH)
        mem_same_ref[:, :, cols] = jnp.where(even, key_part, value_part)
        mem_other_ref[:, :, cols] = jnp.where(even, value_part, key_part)


def probs_of(keys, values, query, cotangent, rows_ref, stats_ref, head, piece):
    logits = logits_of(keys, query, rows_ref, head, piece)
    probs = jnp.exp2(logits - stats_ref[head, 0:1, :]) * stats_ref[head, 1:2, :]
    dlogits = probs * (dot(values, cotangent, 1, 1) - stats_ref[head, 2:3, :])
    return probs.astype(BF16), dlogits.astype(BF16)


def back_kernel(rows_ref, stats_ref, query_ref, cotangent_ref, prev_key_ref, prev_value_ref, back_ref):
    for head in range(query_ref.shape[1] // DEPTH):
        cols = pl.ds(head * DEPTH, DEPTH)
        query, cotangent = query_ref[:, cols], cotangent_ref[:, cols]
        weights, dlogits = probs_of(
            prev_key_ref[:, cols], prev_value_ref[:, cols], query, cotangent, rows_ref, stats_ref, head, 0
        )
        back_ref[0, :, cols] = (dot(dlogits, query, 1, 0) * FACTOR).astype(BF16)
        back_ref[1, :, cols] = dot(weights, cotangent, 1, 0).astype(BF16)


def rest_kernel(
    rows_ref,
    stats_ref,
    query_ref,
    cotangent_ref,
    prev_key_ref,
    prev_value_ref,
    key_ref,
    value_ref,
    mine_ref,
    got_ref,
    attended_ref,
    grad_query_ref,
    own_ref,
):
    even = (lax.axis_index("tm") & 1) == 0
    frame_len = mine_ref.shape[1]
    for head in range(query_ref.shape[1] // DEPTH):
        cols = pl.ds(head * DEPTH, DEPTH)
        query, cotangent = query_ref[:, cols], cotangent_ref[:, cols]
        mine = mine_ref[:, :, cols].reshape(MEM * frame_len, DEPTH)
        got = got_ref[:, :, cols].reshape(MEM * frame_len, DEPTH)
        pieces = (
            (prev_key_ref[:, cols], prev_value_ref[:, cols]),
            (key_ref[:, cols], value_ref[:, cols]),
            (jnp.where(even, mine, got), jnp.where(even, got, mine)),
        )
        attended = grad_query = 0.0
        for piece, (keys, values) in enumerate(pieces):
            weights, dlogits = probs_of(keys, values, query, cotangent, rows_ref, stats_ref, head, piece)
            attended += dot(values, weights, 0, 0)
            grad_query += dot(keys, dlogits, 0, 0)
            if piece == 1:
                own_ref[0, :, cols] = dot(dlogits, query, 1, 0) * FACTOR
                own_ref[1, :, cols] = dot(weights, cotangent, 1, 0)
        attended_ref[:, cols] = attended.T.astype(BF16)
        grad_query_ref[:, cols] = (grad_query * FACTOR).T.astype(BF16)


def sum_kernel(
    peers,
    slots,
    low_bit,
    high_bit,
    table_ref,
    pair_table_ref,
    mine_ref,
    got_ref,
    low_keep,
    low_send,
    high_keep,
    high_send,
):
    me = lax.axis_index("tm")
    half = mine_ref.shape[1] // 2
    last_frame = peers * FR_DEV - 1
    dyns = dyn_frames([read_table(table_ref, slot) for slot in range(slots)], last_frame)
    named = [(read_table(table_ref, slots + m), mine_ref, m) for m in range(MEM)]
    named += [(read_table(pair_table_ref, slots + m), got_ref, m) for m in range(MEM)]
    for start, keep, send, bit in ((0, low_keep, low_send, low_bit), (half, high_keep, high_send, high_bit)):
        upper = (me & bit) != 0
        near = jnp.where(upper, last_frame, 0)
        far = jnp.where(upper, 0, last_frame)
        part = pl.ds(start, half)
        terms = [ref[m, part].astype(F32) for _, ref, m in named]

        def total(frame):
            return sum(jnp.where(name == frame, term, 0.0) for (name, _, _), term in zip(named, terms))

        for j, dyn in enumerate(dyns):
            value = total(dyn)
            keep[j] = value
            send[j] = value.astype(BF16)
        keep[len(dyns)] = total(near)
        send[len(dyns)] = total(far).astype(BF16)


def add_kernel(keep_ref, got_ref, out_ref, send_ref):
    value = keep_ref[...] + got_ref[...].astype(F32)
    out_ref[...] = value
    send_ref[...] = value.astype(BF16)


def owned_kernel(peers, slots, table_ref, low_keep, low_got, high_keep, high_got, mine_ref, pair_ref):
    me = lax.axis_index("tm")
    half = low_keep.shape[1]
    last_frame = peers * FR_DEV - 1
    dyns = dyn_frames([read_table(table_ref, slot) for slot in range(slots)], last_frame)
    for start, keep, got in ((0, low_keep, low_got), (half, high_keep, high_got)):
        part = pl.ds(start, half)
        for out, group in ((mine_ref, me), (pair_ref, me ^ 1)):
            for j in range(FR_DEV):
                frame = group * FR_DEV + j
                named = jnp.logical_or(frame == 0, frame == last_frame)
                place = jnp.int32(len(dyns))
                for d, dyn in enumerate(dyns):
                    named = jnp.logical_or(named, frame == dyn)
                    place = jnp.where(frame == dyn, d, place)

                @pl.when(named)
                def _(out=out, j=j, place=place, keep=keep, got=got, part=part):
                    value = keep[place] + got[place].astype(F32)
                    out[j, part] = value.astype(out.dtype)

                @pl.when(jnp.logical_not(named))
                def _(out=out, j=j, part=part):
                    out[j, part] = jnp.zeros((half, out.shape[2]), out.dtype)


def final_kernel(own_ref, back_inner_ref, back_outer_ref, mine_ref, got_ref, grad_key_ref, grad_value_ref):
    even = (lax.axis_index("tm") & 1) == 0
    rows = grad_key_ref.shape
    mine = mine_ref[...].reshape(rows)
    got = got_ref[...].astype(F32).reshape(rows)
    back = jnp.where(even, back_inner_ref[...], back_outer_ref[...]).astype(F32)
    grad_key_ref[...] = (own_ref[0] + back[0] + jnp.where(even, mine, got)).astype(BF16)
    grad_value_ref[...] = (own_ref[1] + back[1] + jnp.where(even, got, mine)).astype(BF16)


def body(
    query_states,
    key_states,
    value_states,
    grad_out,
    camera_pose,
    pose_bias,
    memory_index,
    bank_frames,
):
    row_count, width = query_states.shape
    frame_len = row_count // FR_DEV
    half = frame_len // 2
    heads = pose_bias.shape[0]
    slots = bank_frames.shape[0]
    kept = slots - 1
    peers = lax.axis_size("tm")
    bits = [1 << i for i in range(1, peers.bit_length() - 1)]
    even = (lax.axis_index("tm") & 1) == 0
    piece_flops = 2 * row_count * row_count * width

    outer_keys = shift(key_states, 1, 1, peers)
    outer_values = shift(value_states, 1, 1, peers)
    pair_values = shift(value_states, 1, 0, peers)
    pair_keys = shift(key_states, -1, 1, peers)
    inner_keys = shift(key_states, 1, 0, peers)

    table_rows = -(-(slots + MEM) // 8) * 8
    bias_rows = -(-(2 * FR_DEV + MEM) // 8) * 8
    table, rows = call(
        functools.partial(table_kernel, peers),
        [shape(jnp.int32, table_rows, 128), shape(F32, heads, bias_rows, row_count)],
        [],
        scalars=[bank_frames, memory_index, camera_pose, pose_bias],
        name="table",
    )
    pair_table = swap(table, 1, peers)
    halves = shape(BF16, kept, half, width)
    sums = shape(F32, kept, half, width)
    low, high = call(
        functools.partial(split_kernel, peers, slots),
        [halves] * 2,
        [table, key_states, value_states, pair_keys, pair_values],
        name="split",
    )
    low_done = high_done = 1
    low_got = swap(low, bits[0], peers)
    high_got = swap(high, bits[-1], peers)
    prev_keys = jnp.where(even, outer_keys, inner_keys)
    prev_values = jnp.where(even, outer_values, pair_values)
    stats = shape(F32, heads, 8, row_count)
    (part,) = call(
        stats_kernel,
        [stats],
        [rows, query_states, grad_out, prev_keys, prev_values, key_states, value_states],
        flops=4 * piece_flops,
        name="stats",
    )
    for step in range(1, len(bits)):
        low_done |= bits[step - 1]
        high_done |= bits[-step]
        (high,) = call(
            functools.partial(step_kernel, peers, slots, high_done & ~bits[-step]),
            [halves],
            [table, high, high_got],
            name="step_high",
        )
        high_got = swap(high, bits[-step - 1], peers)
        (low,) = call(
            functools.partial(step_kernel, peers, slots, low_done & ~bits[step - 1]),
            [halves],
            [table, low, low_got],
            name="step_low",
        )
        low_got = swap(low, bits[step], peers)
    chosen = shape(BF16, MEM, frame_len, width)
    mem_mine, mem_send = call(
        functools.partial(pick_kernel, peers, slots, bits[-1], bits[0]),
        [chosen] * 2,
        [table, pair_table, low, low_got, high, high_got],
        after=[part],
        name="pick",
    )
    mem_got = swap(mem_send, 1, peers)

    stats_all, mem_same, mem_other = call(
        memory_kernel,
        [stats, chosen, chosen],
        [rows, part, query_states, grad_out, mem_mine, mem_got],
        flops=4 * piece_flops,
        name="memory",
    )
    same_got = swap(mem_other, 1, peers)
    (back,) = call(
        back_kernel,
        [shape(BF16, 2, row_count, width)],
        [rows, stats_all, query_states, grad_out, prev_keys, prev_values],
        flops=4 * piece_flops,
        name="back",
    )
    back_outer = shift(back, -1, 2, peers)
    back_inner = shift(back, -1, 1, peers)
    low_keep, low_send, high_keep, high_send = call(
        functools.partial(sum_kernel, peers, slots, bits[-1], bits[0]),
        [sums, halves] * 2,
        [table, pair_table, mem_same, same_got],
        after=[back],
        name="sum",
    )
    low_got = swap(low_send, bits[-1], peers)
    high_got = swap(high_send, bits[0], peers)
    attended, grad_query, own = call(
        rest_kernel,
        [shape(BF16, row_count, width)] * 2 + [shape(F32, 2, row_count, width)],
        [
            rows,
            stats_all,
            query_states,
            grad_out,
            prev_keys,
            prev_values,
            key_states,
            value_states,
            mem_mine,
            mem_got,
        ],
        flops=14 * piece_flops,
        name="rest",
    )
    for step in range(1, len(bits)):
        low_keep, low_send = call(add_kernel, [sums, halves], [low_keep, low_got], name="add_low")
        low_got = swap(low_send, bits[-step - 1], peers)
        high_keep, high_send = call(add_kernel, [sums, halves], [high_keep, high_got], name="add_high")
        high_got = swap(high_send, bits[step], peers)
    owned = shape(F32, FR_DEV, frame_len, width)
    owned_mine, owned_send = call(
        functools.partial(owned_kernel, peers, slots),
        [owned, shape(BF16, FR_DEV, frame_len, width)],
        [table, low_keep, low_got, high_keep, high_got],
        after=[own],
        name="owned",
    )
    owned_got = swap(owned_send, 1, peers)
    grad_key, grad_value = call(
        final_kernel,
        [shape(BF16, row_count, width)] * 2,
        [own, back_inner, back_outer, owned_mine, owned_got],
        name="final",
    )
    return (attended, grad_query, grad_key, grad_value)


def solution(mesh):
    rows = P(("traj", "tm"), None)
    in_specs = (rows, rows, rows, rows, P("traj"), P(), rows, P("traj"))
    return jax.shard_map(body, mesh=mesh, in_specs=in_specs, out_specs=(rows,) * 4, check_vma=False)
```

time: 76.8 us -> 74.5 us (0.970)
  waiting for transfers between devices: 38.3 us -> 24.9 us
  Pallas kernels: 14.1 us -> 19 us
  starting transfers between devices: 20.7 us -> 25.2 us
  local copies, waits for them, and re-layouts: 2.66 us -> 3.77 us
    ppermute x13 -> x12, waiting for transfers between devices: 38.3 us -> 24.9 us  [swap(): return lax.ppermute(block, 'tm', [(i, i ^ bit) for i in range(peers)])]
    pallas_call x9 -> x14, Pallas kernels: 14.1 us -> 19 us  [call(): pl.pallas_call(run, out_shape=outs, in_specs=[SMEM] * len(scalars) + [VME...]
    ppermute x3 -> x7, starting transfers between devices: 6.71 us -> 10.9 us  [shift(): return lax.ppermute(block, 'tm', pairs)]
    unnamed x20 -> x16, local copies, waits for them, and re-layouts: 2.66 us -> 3.77 us
    ppermute x13 -> x12, starting transfers between devices: 14 us -> 14.4 us  [swap(): return lax.ppermute(block, 'tm', [(i, i ^ bit) for i in range(peers)])]
  transfers between devices with their start and end apart: 16 -> 19, of which waited for: 11 -> 8; matrix products, arithmetic and copies ran while one was open for 0% -> 0% of each run, Pallas kernels for 2% -> 19%
where the time goes in v2:
time: 74.5 us; the launch traced here: 74 us
  starting transfers between devices  25.2 us (34%)
  waiting for transfers between devices  24.9 us (33%)
  Pallas kernels  19 us (26%)
  local copies, waits for them, and re-layouts  3.77 us (5%)
  between operations  0.95 us (1%)
    ppermute x12, waiting for transfers between devices, swap(): return lax.ppermute(block, 'tm', [(i, i ^ bit) for i in range(peers)])  24.9 us
    pallas_call x14, Pallas kernels, call(): pl.pallas_call(run, out_shape=outs, in_specs=[SMEM] * len(scalars) + [VME...  19 us
    ppermute x12, starting transfers between devices, swap(): return lax.ppermute(block, 'tm', [(i, i ^ bit) for i in range(peers)])  14.4 us
    ppermute x7, starting transfers between devices, shift(): return lax.ppermute(block, 'tm', pairs)  10.9 us
    unnamed x16, local copies, waits for them, and re-layouts  3.77 us
  transfers between devices with their start and end apart: 19, of which 8 were waited for; matrix products, arithmetic and copies ran while one was open for 0% of the time, Pallas kernels for 19%

profile of v2, /device:TPU:0, one launch (start us, length us, event | category | flops | bytes accessed | tf_op | source)
XLA Modules:
  0.0 74.0 jit_solution(11554119272384366055)
XLA Ops:
  0.6 2.4 %collective-permute-start.3 = (bf16[256,768]{1,0:T(8,128)(2,1)}, bf16[256,768]{1,0:T(8,128)(2,1)S(1)}, u32[]{:S(2)}, u32[]{:S(2)}) collective-permute-start(bf16[256,768]{1,0:T(8,128)(2,1)} %refs_7_.1), channel_id=1, source_target_pairs={{0,1},{2,3},{4,5},{6,7},{8,9},{10,11},{12,13},{14,15},{16,17},{18,... | collective-permute-start | bytes 1179656 | tf_op jit(solution)/shard_map/ppermute | solution.py:53
  3.0 1.3 %collective-permute-start.5 = (bf16[256,768]{1,0:T(8,128)(2,1)}, bf16[256,768]{1,0:T(8,128)(2,1)S(1)}, u32[]{:S(2)}, u32[]{:S(2)}) collective-permute-start(bf16[256,768]{1,0:T(8,128)(2,1)} %refs_6_.3), channel_id=1, source_target_pairs={{1,0},{3,2},{5,4},{7,6},{9,8},{11,10},{13,12},{15,14},{17,16},{19,... | collective-permute-start | bytes 1179656 | tf_op jit(solution)/shard_map/ppermute | solution.py:53
  4.3 0.7 collective-permute-start.2
  5.0 0.8 %copy-done.4 = f32[6,16,16]{2,1,0:T(8,128)S(1)} copy-done((f32[6,16,16]{2,1,0:T(8,128)S(1)}, f32[6,16,16]{2,1,0:T(8,128)}, u32[]{:S(2)}) %copy-start.4) | copy-done | bytes 6168
  5.8 0.7 copy-done.5
  6.5 0.7 copy-done.6
  7.1 0.7 copy-done.7
  7.8 1.5 %table.1 = (s32[8,128]{1,0:T(8,128)S(1)}, f32[6,8,256]{2,1,0:T(8,128)S(1)}) custom-call(s32[4]{0:T(128)S(1)} %copy-done.5, s32[1,2]{1,0:T(1,128)S(1)} %copy-done.6, s32[16]{0:T(128)S(1)} %copy-done.7, f32[6,16,16]{2,1,0:T(8,128)S(1)} %copy-done.4), custom_call_target="tpu_custom_call" | custom-call | tf_op jit(solution)/shard_map/table/pallas_call | solution.py:36
  9.3 0.0 copy-start.2
  9.3 1.0 %copy-done.2 = bf16[256,768]{1,0:T(8,128)(2,1)S(1)} copy-done((bf16[256,768]{1,0:T(8,128)(2,1)S(1)}, bf16[256,768]{1,0:T(8,128)(2,1)}, u32[]{:S(2)}) %copy-start.2) | copy-done | bytes 393240
  10.3 1.3 %split.1 = (bf16[3,64,768]{2,1,0:T(8,128)(2,1)S(1)}, bf16[3,64,768]{2,1,0:T(8,128)(2,1)S(1)}) custom-call(s32[8,128]{1,0:T(8,128)S(1)} %get-tuple-element.29.refs_0_, bf16[256,768]{1,0:T(8,128)(2,1)} %refs_6_.3, bf16[256,768]{1,0:T(8,128)(2,1)S(1)} %copy-done.2, bf16[256,768]{1,0:T(8,128)(2,1)S(1)} %collective-permute-done.5.refs_3_, ...), custom_call_target="tpu_custom_call" | custom-call | tf_op jit(solution)/shard_map/split/pallas_call | solution.py:36
  11.6 3.0 %collective-permute-start.6 = (bf16[3,64,768]{2,1,0:T(8,128)(2,1)S(1)}, bf16[3,64,768]{2,1,0:T(8,128)(2,1)S(1)}, u32[]{:S(2)}, u32[]{:S(2)}) collective-permute-start(bf16[3,64,768]{2,1,0:T(8,128)(2,1)S(1)} %get-tuple-element.30.refs_1_), channel_id=1, source_target_pairs={{0,2},{1,3},{2,0},{3,1},{4,6},{5,7},{6,4},{7,5},{8,10},{9,11},{10,... | collective-permute-start | bytes 884744 | tf_op jit(solution)/shard_map/ppermute | solution.py:48
  14.6 1.5 %collective-permute-start.8 = (bf16[3,64,768]{2,1,0:T(8,128)(2,1)S(1)}, bf16[3,64,768]{2,1,0:T(8,128)(2,1)S(1)}, u32[]{:S(2)}, u32[]{:S(2)}) collective-permute-start(bf16[3,64,768]{2,1,0:T(8,128)(2,1)S(1)} %get-tuple-element.31.refs_1_), channel_id=1, source_target_pairs={{0,4},{1,5},{2,6},{3,7},{4,0},{5,1},{6,2},{7,3},{8,12},{9,13},{10,... | collective-permute-start | bytes 884744 | tf_op jit(solution)/shard_map/ppermute | solution.py:48
  16.1 0.7 collective-permute-start
  16.8 3.8 %collective-permute-start.1 = (bf16[256,768]{1,0:T(8,128)(2,1)}, bf16[256,768]{1,0:T(8,128)(2,1)S(1)}, u32[]{:S(2)}, u32[]{:S(2)}) collective-permute-start(bf16[256,768]{1,0:T(8,128)(2,1)} %refs_6_.3), channel_id=1, source_target_pairs={{0,1},{2,3},{4,5},{6,7},{8,9},{10,11},{12,13},{14,15},{16,17},{18,... | collective-permute-start | bytes 1179656 | tf_op jit(solution)/shard_map/ppermute | solution.py:53
  20.6 0.0 collective-permute-done.6.refs_2_
  20.7 1.9 %collective-permute-start.4 = (s32[8,128]{1,0:T(8,128)S(1)}, s32[8,128]{1,0:T(8,128)S(1)}, u32[]{:S(2)}, u32[]{:S(2)}) collective-permute-start(s32[8,128]{1,0:T(8,128)S(1)} %get-tuple-element.29.refs_0_), channel_id=1, source_target_pairs={{0,1},{1,0},{2,3},{3,2},{4,5},{5,4},{6,7},{7,6},{8,9},{9,8},{10,11... | collective-permute-start | bytes 12296 | tf_op jit(solution)/shard_map/ppermute | solution.py:48
  22.6 0.3 step_low.1.refs_2_
  22.9 4.7 %collective-permute-done.8.refs_2_ = bf16[3,64,768]{2,1,0:T(8,128)(2,1)S(1)} collective-permute-done((bf16[3,64,768]{2,1,0:T(8,128)(2,1)S(1)}, bf16[3,64,768]{2,1,0:T(8,128)(2,1)S(1)}, u32[]{:S(2)}, u32[]{:S(2)}) %collective-permute-start.8) | collective-permute-done | bytes 294944 | tf_op jit(solution)/shard_map/ppermute | solution.py:48
  27.6 2.5 %collective-permute-start.7 = (bf16[3,64,768]{2,1,0:T(8,128)(2,1)S(1)}, bf16[3,64,768]{2,1,0:T(8,128)(2,1)S(1)}, u32[]{:S(2)}, u32[]{:S(2)}) collective-permute-start(bf16[3,64,768]{2,1,0:T(8,128)(2,1)S(1)} %step_low.1.refs_2_), channel_id=1, source_target_pairs={{0,4},{1,5},{2,6},{3,7},{4,0},{5,1},{6,2},{7,3},{8,12},{9,13},{10,... | collective-permute-start | bytes 884744 | tf_op jit(solution)/shard_map/ppermute | solution.py:48
  30.1 0.3 step_high.1.refs_4_
  30.3 0.1 collective-permute-start.9
  30.6 2.3 %stats.1.refs_6_.refs_1_ = f32[6,8,256]{2,1,0:T(8,128)S(1)} custom-call(f32[6,8,256]{2,1,0:T(8,128)S(1)} %get-tuple-element.28.refs_0_, bf16[256,768]{1,0:T(8,128)(2,1)S(1)} %copy-done, bf16[256,768]{1,0:T(8,128)(2,1)S(1)} %copy-done.1, bf16[256,768]{1,0:T(8,128)(2,1)S(1)} %broadcast_select_fusion.1.refs_3_.refs_4_, ...), custom_call_target="tpu_custom_call" | custom-call | flops 402653184 | tf_op jit(solution)/shard_map/stats/pallas_call | solution.py:36
  32.9 4.3 %collective-permute-done.7.refs_3_ = bf16[3,64,768]{2,1,0:T(8,128)(2,1)S(1)} collective-permute-done((bf16[3,64,768]{2,1,0:T(8,128)(2,1)S(1)}, bf16[3,64,768]{2,1,0:T(8,128)(2,1)S(1)}, u32[]{:S(2)}, u32[]{:S(2)}) %collective-permute-start.7) | collective-permute-done | bytes 294944 | tf_op jit(solution)/shard_map/ppermute | solution.py:48
  37.2 1.8 %collective-permute-done.9.refs_5_ = bf16[3,64,768]{2,1,0:T(8,128)(2,1)S(1)} collective-permute-done((bf16[3,64,768]{2,1,0:T(8,128)(2,1)S(1)}, bf16[3,64,768]{2,1,0:T(8,128)(2,1)S(1)}, u32[]{:S(2)}, u32[]{:S(2)}) %collective-permute-start.9) | collective-permute-done | bytes 294944 | tf_op jit(solution)/shard_map/ppermute | solution.py:48
  39.0 1.0 %pick.1 = (bf16[2,128,768]{2,1,0:T(8,128)(2,1)S(1)}, bf16[2,128,768]{2,1,0:T(8,128)(2,1)S(1)}) custom-call(s32[8,128]{1,0:T(8,128)S(1)} %get-tuple-element.29.refs_0_, s32[8,128]{1,0:T(8,128)S(1)} %collective-permute-done.4.refs_1_, bf16[3,64,768]{2,1,0:T(8,128)(2,1)S(1)} %step_low.1.refs_2_, bf16[3,64,768]{2,1,0:T(8,128)(2,1)S(1)} %collective-permute-done.7.refs_3_, ...), custom_call_target="tpu_custom_call" | custom-call | tf_op jit(solution)/shard_map/pick/pallas_call | solution.py:36
  40.0 0.1 collective-permute-start.10
  40.1 1.7 %collective-permute-done.10.refs_5_.refs_9_ = bf16[2,128,768]{2,1,0:T(8,128)(2,1)S(1)} collective-permute-done((bf16[2,128,768]{2,1,0:T(8,128)(2,1)S(1)}, bf16[2,128,768]{2,1,0:T(8,128)(2,1)S(1)}, u32[]{:S(2)}, u32[]{:S(2)}) %collective-permute-start.10) | collective-permute-done | bytes 393248 | tf_op jit(solution)/shard_map/ppermute | solution.py:48
  41.8 2.4 %memory.1 = (f32[6,8,256]{2,1,0:T(8,128)S(1)}, bf16[2,128,768]{2,1,0:T(8,128)(2,1)S(1)}, bf16[2,128,768]{2,1,0:T(8,128)(2,1)S(1)}) custom-call(f32[6,8,256]{2,1,0:T(8,128)S(1)} %get-tuple-element.28.refs_0_, f32[6,8,256]{2,1,0:T(8,128)S(1)} %stats.1.refs_6_.refs_1_, bf16[256,768]{1,0:T(8,128)(2,1)S(1)} %copy-done, bf16[256,768]{1,0:T(8,128)(2,1)S(1)} %copy-done.1, ...), custom_call_target="tpu_custom_call" | custom-call | flops 402653184 | tf_op jit(solution)/shard_map/memory/pallas_call | solution.py:36
  44.2 0.2 collective-permute-start.13
  44.4 1.5 %back.1.refs_4_ = bf16[2,256,768]{2,1,0:T(8,128)(2,1)S(1)} custom-call(f32[6,8,256]{2,1,0:T(8,128)S(1)} %get-tuple-element.28.refs_0_, f32[6,8,256]{2,1,0:T(8,128)S(1)} %get-tuple-element.34.refs_1_, bf16[256,768]{1,0:T(8,128)(2,1)S(1)} %copy-done, bf16[256,768]{1,0:T(8,128)(2,1)S(1)} %copy-done.1, ...), custom_call_target="tpu_custom_call" | custom-call | flops 402653184 | tf_op jit(solution)/shard_map/back/pallas_call | solution.py:36
  45.9 0.1 collective-permute-done.13.refs_3_
  46.0 0.8 %sum.1 = (f32[3,64,768]{2,1,0:T(8,128)S(1)}, bf16[3,64,768]{2,1,0:T(8,128)(2,1)S(1)}, f32[3,64,768]{2,1,0:T(8,128)S(1)}, bf16[3,64,768]{2,1,0:T(8,128)(2,1)S(1)}) custom-call(s32[8,128]{1,0:T(8,128)S(1)} %get-tuple-element.29.refs_0_, s32[8,128]{1,0:T(8,128)S(1)} %collective-permute-done.4.refs_1_, bf16[2,128,768]{2,1,0:T(8,128)(2,1)S(1)} %get-tuple-element.38.refs_2_, ...), custom_call_target="tpu_custom_call" | custom-call | tf_op jit(solution)/shard_map/sum/pallas_call | solution.py:36
  46.8 0.3 collective-permute-start.16
  47.1 0.3 collective-permute-start.14
  47.4 1.3 %collective-permute-start.11 = (bf16[2,256,768]{2,1,0:T(8,128)(2,1)S(1)}, bf16[2,256,768]{2,1,0:T(8,128)(2,1)S(1)}, u32[]{:S(2)}, u32[]{:S(2)}) collective-permute-start(bf16[2,256,768]{2,1,0:T(8,128)(2,1)S(1)} %back.1.refs_4_), channel_id=1, source_target_pairs={{1,0},{3,2},{5,4},{7,6},{9,8},{11,10},{13,12},{15,14},{17,16},{19,... | collective-permute-start | bytes 2359304 | tf_op jit(solution)/shard_map/ppermute | solution.py:53
  48.7 0.7 collective-permute-start.12
  49.4 6.6 %collective-permute-done.16.refs_1_ = bf16[3,64,768]{2,1,0:T(8,128)(2,1)S(1)} collective-permute-done((bf16[3,64,768]{2,1,0:T(8,128)(2,1)S(1)}, bf16[3,64,768]{2,1,0:T(8,128)(2,1)S(1)}, u32[]{:S(2)}, u32[]{:S(2)}) %collective-permute-start.16) | collective-permute-done | bytes 294944 | tf_op jit(solution)/shard_map/ppermute | solution.py:48
  56.0 0.1 add_high.1
  56.1 0.3 collective-permute-start.17
  56.5 0.1 add_low.1
  56.6 4.1 %collective-permute-start.15 = (bf16[3,64,768]{2,1,0:T(8,128)(2,1)S(1)}, bf16[3,64,768]{2,1,0:T(8,128)(2,1)S(1)}, u32[]{:S(2)}, u32[]{:S(2)}) collective-permute-start(bf16[3,64,768]{2,1,0:T(8,128)(2,1)S(1)} %get-tuple-element.43), channel_id=1, source_target_pairs={{0,2},{1,3},{2,0},{3,1},{4,6},{5,7},{6,4},{7,5},{8,10},{9,11},{10,... | collective-permute-start | bytes 884744 | tf_op jit(solution)/shard_map/ppermute | solution.py:48
  60.7 6.2 %rest.1 = (bf16[256,768]{1,0:T(8,128)(2,1)}, bf16[256,768]{1,0:T(8,128)(2,1)}, f32[2,256,768]{2,1,0:T(8,128)S(1)}) custom-call(f32[6,8,256]{2,1,0:T(8,128)S(1)} %get-tuple-element.28.refs_0_, f32[6,8,256]{2,1,0:T(8,128)S(1)} %get-tuple-element.34.refs_1_, bf16[256,768]{1,0:T(8,128)(2,1)S(1)} %copy-done, bf16[256,768]{1,0:T(8,128)(2,1)S(1)} %copy-done.1, ...), custom_call_target="tpu_custom_call" | custom-call | flops 1409286144 | tf_op jit(solution)/shard_map/rest/pallas_call | solution.py:36
  66.9 3.9 %collective-permute-done.15.refs_2_ = bf16[3,64,768]{2,1,0:T(8,128)(2,1)S(1)} collective-permute-done((bf16[3,64,768]{2,1,0:T(8,128)(2,1)S(1)}, bf16[3,64,768]{2,1,0:T(8,128)(2,1)S(1)}, u32[]{:S(2)}, u32[]{:S(2)}) %collective-permute-start.15) | collective-permute-done | bytes 294944 | tf_op jit(solution)/shard_map/ppermute | solution.py:48
  70.8 0.4 owned.1
  71.1 0.1 collective-permute-start.18
  71.2 1.7 %collective-permute-done.18.refs_4_ = bf16[2,128,768]{2,1,0:T(8,128)(2,1)S(1)} collective-permute-done((bf16[2,128,768]{2,1,0:T(8,128)(2,1)S(1)}, bf16[2,128,768]{2,1,0:T(8,128)(2,1)S(1)}, u32[]{:S(2)}, u32[]{:S(2)}) %collective-permute-start.18) | collective-permute-done | bytes 393248 | tf_op jit(solution)/shard_map/ppermute | solution.py:48
  72.9 1.1 %final.1 = (bf16[256,768]{1,0:T(8,128)(2,1)}, bf16[256,768]{1,0:T(8,128)(2,1)}) custom-call(f32[2,256,768]{2,1,0:T(8,128)S(1)} %get-tuple-element.37.refs_5_.refs_0_, bf16[2,256,768]{2,1,0:T(8,128)(2,1)S(1)} %collective-permute-done.11.refs_1_, bf16[2,256,768]{2,1,0:T(8,128)(2,1)S(1)} %collective-permute-done.12.refs_2_, ...), custom_call_target="tpu_custom_call" | custom-call | tf_op jit(solution)/shard_map/final/pallas_call | solution.py:36
  (22 shorter events, 0.1 us)
Async XLA Ops:
  0.6 8.6 %collective-permute-start.3 = (bf16[256,768]{1,0:T(8,128)(2,1)}, bf16[256,768]{1,0:T(8,128)(2,1)S(1)}, u32[]{:S(2)}, u32[]{:S(2)}) collective-permute-start(bf16[256,768]{1,0:T(8,128)(2,1)} %refs_7_.1), channel_id=1, source_target_pairs={{0,1},{2,3},{4,5},{6,7},{8,9},{10,11},{12,13},{14,15},{16,17},{18,... | collective-permute-start | bytes 1179656 | tf_op jit(solution)/shard_map/ppermute | solution.py:53
  3.0 6.3 %collective-permute-start.5 = (bf16[256,768]{1,0:T(8,128)(2,1)}, bf16[256,768]{1,0:T(8,128)(2,1)S(1)}, u32[]{:S(2)}, u32[]{:S(2)}) collective-permute-start(bf16[256,768]{1,0:T(8,128)(2,1)} %refs_6_.3), channel_id=1, source_target_pairs={{1,0},{3,2},{5,4},{7,6},{9,8},{11,10},{13,12},{15,14},{17,16},{19,... | collective-permute-start | bytes 1179656 | tf_op jit(solution)/shard_map/ppermute | solution.py:53
  4.3 26.0 %collective-permute-start.2 = (bf16[256,768]{1,0:T(8,128)(2,1)}, bf16[256,768]{1,0:T(8,128)(2,1)S(1)}, u32[]{:S(2)}, u32[]{:S(2)}) collective-permute-start(bf16[256,768]{1,0:T(8,128)(2,1)} %refs_7_.1), channel_id=1, source_target_pairs={{1,2},{3,4},{5,6},{9,10},{11,12},{13,14},{17,18},{19,20},{21,22},{... | collective-permute-start | bytes 1179656 | tf_op jit(solution)/shard_map/ppermute | solution.py:53
  5.0 0.8 %copy-start.4 = (f32[6,16,16]{2,1,0:T(8,128)S(1)}, f32[6,16,16]{2,1,0:T(8,128)}, u32[]{:S(2)}) copy-start(f32[6,16,16]{2,1,0:T(8,128)} %refs_3_.4) | copy-start | bytes 18436
  5.8 0.7 copy-start.5
  6.5 0.7 copy-start.6
  7.1 0.7 copy-start.7
  9.3 1.0 %copy-start.2 = (bf16[256,768]{1,0:T(8,128)(2,1)S(1)}, bf16[256,768]{1,0:T(8,128)(2,1)}, u32[]{:S(2)}) copy-start(bf16[256,768]{1,0:T(8,128)(2,1)} %refs_7_.1) | copy-start | bytes 1179652
  11.6 9.1 %collective-permute-start.6 = (bf16[3,64,768]{2,1,0:T(8,128)(2,1)S(1)}, bf16[3,64,768]{2,1,0:T(8,128)(2,1)S(1)}, u32[]{:S(2)}, u32[]{:S(2)}) collective-permute-start(bf16[3,64,768]{2,1,0:T(8,128)(2,1)S(1)} %get-tuple-element.30.refs_1_), channel_id=1, source_target_pairs={{0,2},{1,3},{2,0},{3,1},{4,6},{5,7},{6,4},{7,5},{8,10},{9,11},{10,... | collective-permute-start | bytes 884744 | tf_op jit(solution)/shard_map/ppermute | solution.py:48
  14.6 13.0 %collective-permute-start.8 = (bf16[3,64,768]{2,1,0:T(8,128)(2,1)S(1)}, bf16[3,64,768]{2,1,0:T(8,128)(2,1)S(1)}, u32[]{:S(2)}, u32[]{:S(2)}) collective-permute-start(bf16[3,64,768]{2,1,0:T(8,128)(2,1)S(1)} %get-tuple-element.31.refs_1_), channel_id=1, source_target_pairs={{0,4},{1,5},{2,6},{3,7},{4,0},{5,1},{6,2},{7,3},{8,12},{9,13},{10,... | collective-permute-start | bytes 884744 | tf_op jit(solution)/shard_map/ppermute | solution.py:48
  16.1 14.4 %collective-permute-start = (bf16[256,768]{1,0:T(8,128)(2,1)}, bf16[256,768]{1,0:T(8,128)(2,1)S(1)}, u32[]{:S(2)}, u32[]{:S(2)}) collective-permute-start(bf16[256,768]{1,0:T(8,128)(2,1)} %refs_6_.3), channel_id=1, source_target_pairs={{1,2},{3,4},{5,6},{9,10},{11,12},{13,14},{17,18},{19,20},{21,22},{... | collective-permute-start | bytes 1179656 | tf_op jit(solution)/shard_map/ppermute | solution.py:53
  16.8 13.7 %collective-permute-start.1 = (bf16[256,768]{1,0:T(8,128)(2,1)}, bf16[256,768]{1,0:T(8,128)(2,1)S(1)}, u32[]{:S(2)}, u32[]{:S(2)}) collective-permute-start(bf16[256,768]{1,0:T(8,128)(2,1)} %refs_6_.3), channel_id=1, source_target_pairs={{0,1},{2,3},{4,5},{6,7},{8,9},{10,11},{12,13},{14,15},{16,17},{18,... | collective-permute-start | bytes 1179656 | tf_op jit(solution)/shard_map/ppermute | solution.py:53
  20.7 12.2 %collective-permute-start.4 = (s32[8,128]{1,0:T(8,128)S(1)}, s32[8,128]{1,0:T(8,128)S(1)}, u32[]{:S(2)}, u32[]{:S(2)}) collective-permute-start(s32[8,128]{1,0:T(8,128)S(1)} %get-tuple-element.29.refs_0_), channel_id=1, source_target_pairs={{0,1},{1,0},{2,3},{3,2},{4,5},{5,4},{6,7},{7,6},{8,9},{9,8},{10,11... | collective-permute-start | bytes 12296 | tf_op jit(solution)/shard_map/ppermute | solution.py:48
  22.8 7.7 %copy-start = (bf16[256,768]{1,0:T(8,128)(2,1)S(1)}, bf16[256,768]{1,0:T(8,128)(2,1)}, u32[]{:S(2)}) copy-start(bf16[256,768]{1,0:T(8,128)(2,1)} %refs_2_.11) | copy-start | bytes 1179652
  22.8 7.7 %copy-start.1 = (bf16[256,768]{1,0:T(8,128)(2,1)S(1)}, bf16[256,768]{1,0:T(8,128)(2,1)}, u32[]{:S(2)}) copy-start(bf16[256,768]{1,0:T(8,128)(2,1)} %refs_3_.7) | copy-start | bytes 1179652
  22.9 7.7 %copy-start.3 = (bf16[256,768]{1,0:T(8,128)(2,1)S(1)}, bf16[256,768]{1,0:T(8,128)(2,1)}, u32[]{:S(2)}) copy-start(bf16[256,768]{1,0:T(8,128)(2,1)} %refs_7_.1) | copy-start | bytes 1179652
  27.6 9.6 %collective-permute-start.7 = (bf16[3,64,768]{2,1,0:T(8,128)(2,1)S(1)}, bf16[3,64,768]{2,1,0:T(8,128)(2,1)S(1)}, u32[]{:S(2)}, u32[]{:S(2)}) collective-permute-start(bf16[3,64,768]{2,1,0:T(8,128)(2,1)S(1)} %step_low.1.refs_2_), channel_id=1, source_target_pairs={{0,4},{1,5},{2,6},{3,7},{4,0},{5,1},{6,2},{7,3},{8,12},{9,13},{10,... | collective-permute-start | bytes 884744 | tf_op jit(solution)/shard_map/ppermute | solution.py:48
  30.3 8.7 %collective-permute-start.9 = (bf16[3,64,768]{2,1,0:T(8,128)(2,1)S(1)}, bf16[3,64,768]{2,1,0:T(8,128)(2,1)S(1)}, u32[]{:S(2)}, u32[]{:S(2)}) collective-permute-start(bf16[3,64,768]{2,1,0:T(8,128)(2,1)S(1)} %step_high.1.refs_4_), channel_id=1, source_target_pairs={{0,2},{1,3},{2,0},{3,1},{4,6},{5,7},{6,4},{7,5},{8,10},{9,11},{10,... | collective-permute-start | bytes 884744 | tf_op jit(solution)/shard_map/ppermute | solution.py:48
  40.0 1.8 %collective-permute-start.10 = (bf16[2,128,768]{2,1,0:T(8,128)(2,1)S(1)}, bf16[2,128,768]{2,1,0:T(8,128)(2,1)S(1)}, u32[]{:S(2)}, u32[]{:S(2)}) collective-permute-start(bf16[2,128,768]{2,1,0:T(8,128)(2,1)S(1)} %get-tuple-element.33), channel_id=1, source_target_pairs={{0,1},{1,0},{2,3},{3,2},{4,5},{5,4},{6,7},{7,6},{8,9},{9,8},{10,11... | collective-permute-start | bytes 1179656 | tf_op jit(solution)/shard_map/ppermute | solution.py:48
  44.2 1.8 %collective-permute-start.13 = (bf16[2,128,768]{2,1,0:T(8,128)(2,1)S(1)}, bf16[2,128,768]{2,1,0:T(8,128)(2,1)S(1)}, u32[]{:S(2)}, u32[]{:S(2)}) collective-permute-start(bf16[2,128,768]{2,1,0:T(8,128)(2,1)S(1)} %get-tuple-element.39), channel_id=1, source_target_pairs={{0,1},{1,0},{2,3},{3,2},{4,5},{5,4},{6,7},{7,6},{8,9},{9,8},{10,11... | collective-permute-start | bytes 1179656 | tf_op jit(solution)/shard_map/ppermute | solution.py:48
  46.8 9.3 %collective-permute-start.16 = (bf16[3,64,768]{2,1,0:T(8,128)(2,1)S(1)}, bf16[3,64,768]{2,1,0:T(8,128)(2,1)S(1)}, u32[]{:S(2)}, u32[]{:S(2)}) collective-permute-start(bf16[3,64,768]{2,1,0:T(8,128)(2,1)S(1)} %get-tuple-element.45), channel_id=1, source_target_pairs={{0,2},{1,3},{2,0},{3,1},{4,6},{5,7},{6,4},{7,5},{8,10},{9,11},{10,... | collective-permute-start | bytes 884744 | tf_op jit(solution)/shard_map/ppermute | solution.py:48
  47.1 9.4 %collective-permute-start.14 = (bf16[3,64,768]{2,1,0:T(8,128)(2,1)S(1)}, bf16[3,64,768]{2,1,0:T(8,128)(2,1)S(1)}, u32[]{:S(2)}, u32[]{:S(2)}) collective-permute-start(bf16[3,64,768]{2,1,0:T(8,128)(2,1)S(1)} %get-tuple-element.41), channel_id=1, source_target_pairs={{0,4},{1,5},{2,6},{3,7},{4,0},{5,1},{6,2},{7,3},{8,12},{9,13},{10,... | collective-permute-start | bytes 884744 | tf_op jit(solution)/shard_map/ppermute | solution.py:48
  47.4 23.8 %collective-permute-start.11 = (bf16[2,256,768]{2,1,0:T(8,128)(2,1)S(1)}, bf16[2,256,768]{2,1,0:T(8,128)(2,1)S(1)}, u32[]{:S(2)}, u32[]{:S(2)}) collective-permute-start(bf16[2,256,768]{2,1,0:T(8,128)(2,1)S(1)} %back.1.refs_4_), channel_id=1, source_target_pairs={{1,0},{3,2},{5,4},{7,6},{9,8},{11,10},{13,12},{15,14},{17,16},{19,... | collective-permute-start | bytes 2359304 | tf_op jit(solution)/shard_map/ppermute | solution.py:53
  48.7 22.6 %collective-permute-start.12 = (bf16[2,256,768]{2,1,0:T(8,128)(2,1)S(1)}, bf16[2,256,768]{2,1,0:T(8,128)(2,1)S(1)}, u32[]{:S(2)}, u32[]{:S(2)}) collective-permute-start(bf16[2,256,768]{2,1,0:T(8,128)(2,1)S(1)} %back.1.refs_4_), channel_id=1, source_target_pairs={{2,1},{4,3},{6,5},{10,9},{12,11},{14,13},{18,17},{20,19},{22,21},{... | collective-permute-start | bytes 2359304 | tf_op jit(solution)/shard_map/ppermute | solution.py:53
  56.1 10.8 %collective-permute-start.17 = (bf16[3,64,768]{2,1,0:T(8,128)(2,1)S(1)}, bf16[3,64,768]{2,1,0:T(8,128)(2,1)S(1)}, u32[]{:S(2)}, u32[]{:S(2)}) collective-permute-start(bf16[3,64,768]{2,1,0:T(8,128)(2,1)S(1)} %get-tuple-element.47), channel_id=1, source_target_pairs={{0,4},{1,5},{2,6},{3,7},{4,0},{5,1},{6,2},{7,3},{8,12},{9,13},{10,... | collective-permute-start | bytes 884744 | tf_op jit(solution)/shard_map/ppermute | solution.py:48
  56.6 14.2 %collective-permute-start.15 = (bf16[3,64,768]{2,1,0:T(8,128)(2,1)S(1)}, bf16[3,64,768]{2,1,0:T(8,128)(2,1)S(1)}, u32[]{:S(2)}, u32[]{:S(2)}) collective-permute-start(bf16[3,64,768]{2,1,0:T(8,128)(2,1)S(1)} %get-tuple-element.43), channel_id=1, source_target_pairs={{0,2},{1,3},{2,0},{3,1},{4,6},{5,7},{6,4},{7,5},{8,10},{9,11},{10,... | collective-permute-start | bytes 884744 | tf_op jit(solution)/shard_map/ppermute | solution.py:48
  71.1 1.8 %collective-permute-start.18 = (bf16[2,128,768]{2,1,0:T(8,128)(2,1)S(1)}, bf16[2,128,768]{2,1,0:T(8,128)(2,1)S(1)}, u32[]{:S(2)}, u32[]{:S(2)}) collective-permute-start(bf16[2,128,768]{2,1,0:T(8,128)(2,1)S(1)} %get-tuple-element.49), channel_id=1, source_target_pairs={{0,1},{1,0},{2,3},{3,2},{4,5},{5,4},{6,7},{7,6},{8,9},{9,8},{10,11... | collective-permute-start | bytes 1179656 | tf_op jit(solution)/shard_map/ppermute | solution.py:48

commit v3 on v2

v3 whole, which is shorter than its diff:
```python
import functools
import math

import jax
import jax.numpy as jnp
from jax import lax
from jax.experimental import pallas as pl
from jax.experimental.pallas import tpu as pltpu
from jax.sharding import PartitionSpec as P

FR_DEV = 2
MEM = 2
DEPTH = 128
TAIL = 16

BLOCKED_LOGIT = -1e30
LOG2E = math.log2(math.e)
FACTOR = 1.0 / math.sqrt(DEPTH)

SMEM = pl.BlockSpec(memory_space=pltpu.SMEM)
VMEM = pl.BlockSpec(memory_space=pltpu.VMEM)
ANY = pl.BlockSpec(memory_space=pl.ANY)
VMEM_LIMIT = 32 * 1024 * 1024
BF16, F32 = jnp.bfloat16, jnp.float32


def shape(dtype, *dims):
    return jax.ShapeDtypeStruct(dims, dtype)


def call(kernel, outs, arrays, scalars=(), after=(), flops=0, name=None):
    count = len(scalars) + len(arrays)

    def run(*refs):
        kernel(*refs[:count], *refs[count + len(after) :])

    return pl.pallas_call(
        run,
        out_shape=outs,
        in_specs=[SMEM] * len(scalars) + [VMEM] * len(arrays) + [ANY] * len(after),
        out_specs=[VMEM] * len(outs),
        compiler_params=pltpu.CompilerParams(vmem_limit_bytes=VMEM_LIMIT),
        cost_estimate=pl.CostEstimate(flops=flops, bytes_accessed=0, transcendentals=0) if flops else None,
        name=name,
    )(*scalars, *arrays, *after)


def swap(block, even_bit, odd_bit, peers):
    return lax.ppermute(block, "tm", [(i, i ^ (odd_bit if i & 1 else even_bit)) for i in range(peers)])


def shift(block, by, start, peers):
    pairs = [(i, i + by) for i in range(start, peers, 2) if 0 <= i + by < peers]
    return lax.ppermute(block, "tm", pairs)


def lane_value(row, lane):
    lanes = lax.broadcasted_iota(jnp.int32, row.shape, 1)
    return jnp.max(jnp.where(lanes == lane, row, 0))


def bank_of(bank_ref):
    row = bank_ref[...]
    return [lane_value(row, slot) for slot in range(row.shape[1])]


def own_picks(bank_ref, index_ref):
    return [lane_value(bank_ref[...], lane_value(index_ref[...], m)) for m in range(MEM)]


def pair_picks(bank_ref, pair_ref):
    start = pair_ref.shape[0] - TAIL
    picks = []
    for m in range(MEM):
        slot = jnp.max(pair_ref[start : start + TAIL, m * DEPTH : (m + 1) * DEPTH].astype(F32)).astype(jnp.int32)
        picks.append(lane_value(bank_ref[...], slot))
    return picks


def dyn_frames(bank, last_frame):
    found = [jnp.int32(0)] * (len(bank) - 2)
    seen = jnp.int32(0)
    for frame in bank:
        free = jnp.logical_and(frame != 0, frame != last_frame)
        for j in range(len(found)):
            found[j] = jnp.where(jnp.logical_and(free, seen == j), frame, found[j])
        seen = seen + free.astype(jnp.int32)
    return found


def place_of(frame, dyns):
    place = jnp.int32(len(dyns))
    for j, dyn in enumerate(dyns):
        place = jnp.where(frame == dyn, j, place)
    return place


def choose(out, take_first, first, second):
    @pl.when(take_first)
    def _():
        out[...] = first[...]

    @pl.when(jnp.logical_not(take_first))
    def _():
        out[...] = second[...]


def has_end(me, done, peers):
    return jnp.logical_or((me & ~done) == 0, (me | done) == peers - 1)


def has_dyn(me, frame, done):
    return ((me ^ (frame // FR_DEV)) & ~done) == 0


def by_role(me, even_value, odd_value):
    return jnp.where((me & 1) == 0, even_value, odd_value)


def join_kernel(index_ref, key_ref, value_ref, joined_ref, index_buf, sems):
    rows = key_ref.shape[0]
    copies = [
        pltpu.make_async_copy(index_ref, index_buf, sems.at[0]),
        pltpu.make_async_copy(key_ref, joined_ref.at[pl.ds(0, rows)], sems.at[1]),
        pltpu.make_async_copy(value_ref, joined_ref.at[pl.ds(rows, rows)], sems.at[2]),
    ]
    for copy in copies:
        copy.start()
    copies[0].wait()
    width = joined_ref.shape[1]
    lane = lax.broadcasted_iota(jnp.int32, (TAIL, width), 1) // DEPTH
    tail = jnp.zeros((TAIL, width), jnp.int32)
    for m in range(MEM):
        tail = jnp.where(lane == m, index_buf[0:1, m : m + 1], tail)
    joined_ref[2 * rows : 2 * rows + TAIL, :] = tail.astype(F32).astype(BF16)
    copies[1].wait()
    copies[2].wait()


def bias_kernel(bank_ref, index_ref, pose_ref, bias_ref, rows_ref):
    me = lax.axis_index("tm")
    heads, _, row_count = rows_ref.shape
    mem_ids = [bank_ref[0, index_ref[0, m]] for m in range(MEM)]
    own_ids = [me * FR_DEV + j for j in range(FR_DEV)]
    prev_ids = [jnp.maximum(own - FR_DEV, 0) for own in own_ids]
    query_poses = [pose_ref[frame] for frame in own_ids]
    key_poses = [pose_ref[frame] for frame in prev_ids + own_ids + mem_ids]
    frame_of = lax.broadcasted_iota(jnp.int32, (1, row_count), 1) // (row_count // FR_DEV)
    for head in range(heads):
        for j, key_pose in enumerate(key_poses):
            row = jnp.zeros((1, row_count), F32)
            for a, query_pose in enumerate(query_poses):
                value = bias_ref[head, query_pose, key_pose] * LOG2E
                if j < FR_DEV:
                    value = jnp.where(me == 0, BLOCKED_LOGIT, value)
                row = jnp.where(frame_of == a, value, row)
            rows_ref[head, j : j + 1, :] = row


def split_kernel(peers, bank_ref, mine_ref, pair_ref, out_ref):
    me = lax.axis_index("tm")
    frame_len = out_ref.shape[1]
    dyns = dyn_frames(bank_of(bank_ref), peers * FR_DEV - 1)
    places = [(has_dyn(me, dyn, 0), dyn % FR_DEV) for dyn in dyns]
    places.append((has_end(me, 0, peers), jnp.where(me < peers // 2, 0, FR_DEV - 1)))
    for j, (local, frame) in enumerate(places):
        start = pl.multiple_of(((me & 1) * FR_DEV + frame) * frame_len, frame_len)
        part = pl.ds(start, frame_len)
        choose(out_ref.at[j], local, mine_ref.at[part], pair_ref.at[part])


def step_kernel(peers, even_done, odd_done, bank_ref, mine_ref, got_ref, out_ref):
    me = lax.axis_index("tm")
    done = by_role(me, even_done, odd_done)
    dyns = dyn_frames(bank_of(bank_ref), peers * FR_DEV - 1)
    flags = [has_dyn(me, dyn, done) for dyn in dyns] + [has_end(me, done, peers)]
    for j, flag in enumerate(flags):
        choose(out_ref.at[j], flag, mine_ref.at[j], got_ref.at[j])


def pick_kernel(peers, even_bit, odd_bit, bank_ref, index_ref, pair_ref, mine_ref, got_ref, own_out, pair_out):
    me = lax.axis_index("tm")
    bit = by_role(me, even_bit, odd_bit)
    upper = (me & bit) != 0
    dyns = dyn_frames(bank_of(bank_ref), peers * FR_DEV - 1)
    for out, frames in ((own_out, own_picks(bank_ref, index_ref)), (pair_out, pair_picks(bank_ref, pair_ref))):
        for m, frame in enumerate(frames):
            source = place_of(frame, dyns)
            local = jnp.where(frame == 0, jnp.logical_not(upper), upper)
            local = jnp.where(source < len(dyns), has_dyn(me, frame, (peers - 1) & ~bit), local)
            choose(out.at[m], local, mine_ref.at[source], got_ref.at[source])


def dot(a, b, left, right):
    return lax.dot_general(a, b, (((left,), (right,)), ((), ())), preferred_element_type=F32)


def logits_of(keys, query, rows_ref, head, piece):
    frame_len = query.shape[0] // FR_DEV
    raw = dot(keys, query, 1, 1) * (FACTOR * LOG2E)
    parts = []
    for j in range(FR_DEV):
        row = piece * FR_DEV + j
        parts.append(raw[j * frame_len : (j + 1) * frame_len] + rows_ref[head, row : row + 1, :])
    return jnp.concatenate(parts, axis=0)


def joined_parts(joined_ref, cols):
    rows = (joined_ref.shape[0] - TAIL) // 2
    return joined_ref[0:rows, cols], joined_ref[rows : 2 * rows, cols]


def stats_kernel(rows_ref, query_ref, cotangent_ref, prev_ref, own_ref, stats_ref):
    for head in range(query_ref.shape[1] // DEPTH):
        cols = pl.ds(head * DEPTH, DEPTH)
        query, cotangent = query_ref[:, cols], cotangent_ref[:, cols]
        pieces = [joined_parts(ref, cols) for ref in (prev_ref, own_ref)]
        logits = [logits_of(keys, query, rows_ref, head, piece) for piece, (keys, _) in enumerate(pieces)]
        peak = functools.reduce(jnp.maximum, [jnp.max(block, axis=0, keepdims=True) for block in logits])
        exps = [jnp.exp2(block - peak) for block in logits]
        slopes = [dot(values, cotangent, 1, 1) for _, values in pieces]
        stats_ref[head, 0:1, :] = peak
        stats_ref[head, 1:2, :] = sum(jnp.sum(e, axis=0, keepdims=True) for e in exps)
        stats_ref[head, 2:3, :] = sum(jnp.sum(e * s, axis=0, keepdims=True) for e, s in zip(exps, slopes))


def memory_kernel(
    rows_ref, part_ref, query_ref, cotangent_ref, mine_ref, got_ref, stats_ref, mem_same_ref, mem_other_ref
):
    even = (lax.axis_index("tm") & 1) == 0
    frame_len = mine_ref.shape[1]
    for head in range(query_ref.shape[1] // DEPTH):
        cols = pl.ds(head * DEPTH, DEPTH)
        query, cotangent = query_ref[:, cols], cotangent_ref[:, cols]
        mine = mine_ref[:, :, cols].reshape(MEM * frame_len, DEPTH)
        got = got_ref[:, :, cols].reshape(MEM * frame_len, DEPTH)
        keys, values = jnp.where(even, mine, got), jnp.where(even, got, mine)
        logits = logits_of(keys, query, rows_ref, head, 2)
        part_peak = part_ref[head, 0:1, :]
        peak = jnp.maximum(part_peak, jnp.max(logits, axis=0, keepdims=True))
        exps = jnp.exp2(logits - peak)
        slopes = dot(values, cotangent, 1, 1)
        scale = jnp.exp2(part_peak - peak)
        total = part_ref[head, 1:2, :] * scale + jnp.sum(exps, axis=0, keepdims=True)
        inverse = 1.0 / total
        spread = (part_ref[head, 2:3, :] * scale + jnp.sum(exps * slopes, axis=0, keepdims=True)) * inverse
        stats_ref[head, 0:1, :] = peak
        stats_ref[head, 1:2, :] = inverse
        stats_ref[head, 2:3, :] = spread
        probs = exps * inverse
        dlogits = (probs * (slopes - spread)).astype(BF16)
        key_part = (dot(dlogits, query, 1, 0) * FACTOR).astype(BF16).reshape(MEM, frame_len, DEPTH)
        value_part = dot(probs.astype(BF16), cotangent, 1, 0).astype(BF16).reshape(MEM, frame_len, DEPTH)
        mem_same_ref[:, :, cols] = jnp.where(even, key_part, value_part)
        mem_other_ref[:, :, cols] = jnp.where(even, value_part, key_part)


def probs_of(keys, values, query, cotangent, rows_ref, stats_ref, head, piece):
    logits = logits_of(keys, query, rows_ref, head, piece)
    probs = jnp.exp2(logits - stats_ref[head, 0:1, :]) * stats_ref[head, 1:2, :]
    dlogits = probs * (dot(values, cotangent, 1, 1) - stats_ref[head, 2:3, :])
    return probs.astype(BF16), dlogits.astype(BF16)


def back_kernel(rows_ref, stats_ref, query_ref, cotangent_ref, prev_ref, back_ref):
    for head in range(query_ref.shape[1] // DEPTH):
        cols = pl.ds(head * DEPTH, DEPTH)
        query, cotangent = query_ref[:, cols], cotangent_ref[:, cols]
        keys, values = joined_parts(prev_ref, cols)
        weights, dlogits = probs_of(keys, values, query, cotangent, rows_ref, stats_ref, head, 0)
        back_ref[0, :, cols] = (dot(dlogits, query, 1, 0) * FACTOR).astype(BF16)
        back_ref[1, :, cols] = dot(weights, cotangent, 1, 0).astype(BF16)


def rest_kernel(
    rows_ref,
    stats_ref,
    query_ref,
    cotangent_ref,
    prev_ref,
    joined_ref,
    mine_ref,
    got_ref,
    attended_ref,
    grad_query_ref,
    own_ref,
):
    even = (lax.axis_index("tm") & 1) == 0
    frame_len = mine_ref.shape[1]
    for head in range(query_ref.shape[1] // DEPTH):
        cols = pl.ds(head * DEPTH, DEPTH)
        query, cotangent = query_ref[:, cols], cotangent_ref[:, cols]
        mine = mine_ref[:, :, cols].reshape(MEM * frame_len, DEPTH)
        got = got_ref[:, :, cols].reshape(MEM * frame_len, DEPTH)
        pieces = (
            joined_parts(prev_ref, cols),
            joined_parts(joined_ref, cols),
            (jnp.where(even, mine, got), jnp.where(even, got, mine)),
        )
        attended = grad_query = 0.0
        for piece, (keys, values) in enumerate(pieces):
            weights, dlogits = probs_of(keys, values, query, cotangent, rows_ref, stats_ref, head, piece)
            attended += dot(values, weights, 0, 0)
            grad_query += dot(keys, dlogits, 0, 0)
            if piece == 1:
                own_ref[0, :, cols] = dot(dlogits, query, 1, 0) * FACTOR
                own_ref[1, :, cols] = dot(weights, cotangent, 1, 0)
        attended_ref[:, cols] = attended.T.astype(BF16)
        grad_query_ref[:, cols] = (grad_query * FACTOR).T.astype(BF16)


def sum_kernel(
    peers, even_bit, odd_bit, bank_ref, index_ref, pair_ref, mine_ref, got_ref, keep_ref, send_ref
):
    me = lax.axis_index("tm")
    last_frame = peers * FR_DEV - 1
    dyns = dyn_frames(bank_of(bank_ref), last_frame)
    named = [(frame, mine_ref, m) for m, frame in enumerate(own_picks(bank_ref, index_ref))]
    named += [(frame, got_ref, m) for m, frame in enumerate(pair_picks(bank_ref, pair_ref))]
    upper = (me & by_role(me, even_bit, odd_bit)) != 0
    near = jnp.where(upper, last_frame, 0)
    far = jnp.where(upper, 0, last_frame)
    terms = [ref[m].astype(F32) for _, ref, m in named]

    def total(frame):
        return sum(jnp.where(name == frame, term, 0.0) for (name, _, _), term in zip(named, terms))

    for j, dyn in enumerate(dyns):
        value = total(dyn)
        keep_ref[j] = value
        send_ref[j] = value.astype(BF16)
    keep_ref[len(dyns)] = total(near)
    send_ref[len(dyns)] = total(far).astype(BF16)


def add_kernel(keep_ref, got_ref, out_ref, send_ref):
    value = keep_ref[...] + got_ref[...].astype(F32)
    out_ref[...] = value
    send_ref[...] = value.astype(BF16)


def owned_kernel(peers, bank_ref, keep_ref, got_ref, mine_ref, pair_ref):
    me = lax.axis_index("tm")
    last_frame = peers * FR_DEV - 1
    dyns = dyn_frames(bank_of(bank_ref), last_frame)
    for out, group in ((mine_ref, me), (pair_ref, me ^ 1)):
        for j in range(FR_DEV):
            frame = group * FR_DEV + j
            place = place_of(frame, dyns)
            named = jnp.logical_or(place < len(dyns), jnp.logical_or(frame == 0, frame == last_frame))

            @pl.when(named)
            def _(out=out, j=j, place=place):
                value = keep_ref[place] + got_ref[place].astype(F32)
                out[j] = value.astype(out.dtype)

            @pl.when(jnp.logical_not(named))
            def _(out=out, j=j):
                out[j] = jnp.zeros(out.shape[1:], out.dtype)


def final_kernel(own_ref, back_inner_ref, back_outer_ref, mine_ref, got_ref, grad_key_ref, grad_value_ref):
    even = (lax.axis_index("tm") & 1) == 0
    rows = grad_key_ref.shape
    mine = mine_ref[...].reshape(rows)
    got = got_ref[...].astype(F32).reshape(rows)
    back = jnp.where(even, back_inner_ref[...], back_outer_ref[...]).astype(F32)
    grad_key_ref[...] = (own_ref[0] + back[0] + jnp.where(even, mine, got)).astype(BF16)
    grad_value_ref[...] = (own_ref[1] + back[1] + jnp.where(even, got, mine)).astype(BF16)


def body(
    query_states,
    key_states,
    value_states,
    grad_out,
    camera_pose,
    pose_bias,
    memory_index,
    bank_frames,
):
    row_count, width = query_states.shape
    frame_len = row_count // FR_DEV
    heads = pose_bias.shape[0]
    slots = bank_frames.shape[0]
    peers = lax.axis_size("tm")
    bits = [1 << i for i in range(1, peers.bit_length() - 1)]
    turns = list(zip(bits, bits[::-1]))
    even = (lax.axis_index("tm") & 1) == 0
    piece_flops = 2 * row_count * row_count * width
    bank_frames = bank_frames.reshape(1, slots)
    last_bits = turns[-1]

    joined_rows = 2 * row_count + TAIL
    joined = pl.pallas_call(
        join_kernel,
        out_shape=shape(BF16, joined_rows, width),
        in_specs=[pl.BlockSpec(memory_space=pltpu.HBM)] * 3,
        out_specs=VMEM,
        scratch_shapes=[pltpu.VMEM(memory_index.shape, jnp.int32), pltpu.SemaphoreType.DMA((3,))],
        compiler_params=pltpu.CompilerParams(vmem_limit_bytes=VMEM_LIMIT),
        name="join",
    )(*(pltpu.with_memory_space_constraint(x, pltpu.HBM) for x in (memory_index, key_states, value_states)))
    outer = shift(joined, 1, 1, peers)
    pair = swap(joined, 1, 1, peers)

    bias_rows = -(-(2 * FR_DEV + MEM) // 8) * 8
    (rows,) = call(
        bias_kernel,
        [shape(F32, heads, bias_rows, row_count)],
        [],
        scalars=[bank_frames, memory_index, camera_pose, pose_bias],
        flops=piece_flops,
        name="bias",
    )
    held = shape(BF16, slots - 1, frame_len, width)
    sums = shape(F32, slots - 1, frame_len, width)
    (mine,) = call(functools.partial(split_kernel, peers), [held], [bank_frames, joined, pair], name="split")
    prev = jnp.where(even, outer, pair)
    stats = shape(F32, heads, 8, row_count)
    (part,) = call(
        stats_kernel, [stats], [rows, query_states, grad_out, prev, joined], flops=4 * piece_flops, name="stats"
    )
    even_done = odd_done = 1
    for step, (even_bit, odd_bit) in enumerate(turns):
        got = swap(mine, even_bit, odd_bit, peers)
        if step + 1 < len(turns):
            kernel = functools.partial(step_kernel, peers, even_done, odd_done)
            (mine,) = call(kernel, [held], [bank_frames, mine, got], after=[outer], name="step")
        even_done |= even_bit
        odd_done |= odd_bit
    chosen = shape(BF16, MEM, frame_len, width)
    mem_mine, mem_send = call(
        functools.partial(pick_kernel, peers, *last_bits),
        [chosen] * 2,
        [bank_frames, memory_index, pair, mine, got],
        after=[part],
        name="pick",
    )
    mem_got = swap(mem_send, 1, 1, peers)

    stats_all, mem_same, mem_other = call(
        memory_kernel,
        [stats, chosen, chosen],
        [rows, part, query_states, grad_out, mem_mine, mem_got],
        flops=4 * piece_flops,
        name="memory",
    )
    same_got = swap(mem_other, 1, 1, peers)
    (back,) = call(
        back_kernel,
        [shape(BF16, 2, row_count, width)],
        [rows, stats_all, query_states, grad_out, prev],
        flops=4 * piece_flops,
        name="back",
    )
    back_outer = shift(back, -1, 2, peers)
    back_inner = shift(back, -1, 1, peers)
    keep, send = call(
        functools.partial(sum_kernel, peers, *last_bits),
        [sums, held],
        [bank_frames, memory_index, pair, mem_same, same_got],
        after=[back],
        name="sum",
    )
    attended, grad_query, own = call(
        rest_kernel,
        [shape(BF16, row_count, width)] * 2 + [shape(F32, 2, row_count, width)],
        [rows, stats_all, query_states, grad_out, prev, joined, mem_mine, mem_got],
        flops=14 * piece_flops,
        name="rest",
    )
    for step, (even_bit, odd_bit) in enumerate(turns[::-1]):
        got = swap(send, even_bit, odd_bit, peers)
        if step + 1 < len(turns):
            keep, send = call(add_kernel, [sums, held], [keep, got], after=[back_outer, own], name="add")
    owned = shape(F32, FR_DEV, frame_len, width)
    owned_mine, owned_send = call(
        functools.partial(owned_kernel, peers),
        [owned, shape(BF16, FR_DEV, frame_len, width)],
        [bank_frames, keep, got],
        name="owned",
    )
    owned_got = swap(owned_send, 1, 1, peers)
    grad_key, grad_value = call(
        final_kernel,
        [shape(BF16, row_count, width)] * 2,
        [own, back_inner, back_outer, owned_mine, owned_got],
        name="final",
    )
    return (attended, grad_query, grad_key, grad_value)


def solution(mesh):
    rows = P(("traj", "tm"), None)
    in_specs = (rows, rows, rows, rows, P("traj"), P(), rows, P("traj"))
    return jax.shard_map(body, mesh=mesh, in_specs=in_specs, out_specs=(rows,) * 4, check_vma=False)
```

time: 74.5 us -> 76.6 us (1.028)
  waiting for transfers between devices: 24.9 us -> 32.1 us
  local copies, waits for them, and re-layouts: 3.77 us -> 1.03 us
  starting transfers between devices: 25.2 us -> 23.5 us
    ppermute x7 -> x3, starting transfers between devices: 10.9 us -> 2.69 us  [shift(): return lax.ppermute(block, 'tm', pairs)]
    ppermute x12 -> x8, waiting for transfers between devices: 24.9 us -> 32.1 us  [swap(): lax.ppermute(block, 'tm', [(i, i ^ (odd_bit if i & 1 else even_bit)) for...]
    ppermute x12 -> x8, starting transfers between devices: 14.4 us -> 20.8 us  [swap(): lax.ppermute(block, 'tm', [(i, i ^ (odd_bit if i & 1 else even_bit)) for...]
    unnamed x16 -> x12, local copies, waits for them, and re-layouts: 3.77 us -> 1.03 us
    pallas_call x14 -> x12, Pallas kernels: 19 us -> 17.7 us  [call(): pl.pallas_call(run, out_shape=outs, in_specs=[SMEM] * len(scalars) + [VME...]
    pallas_call x0 -> x1, Pallas kernels: none -> 1.16 us  [body(): pl.pallas_call(join_kernel, out_shape=shape(BF16, joined_rows, width), in...]
  transfers between devices with their start and end apart: 19 -> 11, of which waited for: 8 -> 7; matrix products, arithmetic and copies ran while one was open for 0% -> 0% of each run, Pallas kernels for 19% -> 15%
where the time goes in v3:
time: 76.6 us; the launch traced here: 76.4 us
  waiting for transfers between devices  32.1 us (42%)
  starting transfers between devices  23.5 us (31%)
  Pallas kernels  18.9 us (25%)
  local copies, waits for them, and re-layouts  1.03 us (1%)
  between operations  0.83 us (1%)
    ppermute x8, waiting for transfers between devices, swap(): lax.ppermute(block, 'tm', [(i, i ^ (odd_bit if i & 1 else even_bit)) for...  32.1 us
    ppermute x8, starting transfers between devices, swap(): lax.ppermute(block, 'tm', [(i, i ^ (odd_bit if i & 1 else even_bit)) for...  20.8 us
    pallas_call x12, Pallas kernels, call(): pl.pallas_call(run, out_shape=outs, in_specs=[SMEM] * len(scalars) + [VME...  17.7 us
    ppermute x3, starting transfers between devices, shift(): return lax.ppermute(block, 'tm', pairs)  2.69 us
  transfers between devices with their start and end apart: 11, of which 7 were waited for; matrix products, arithmetic and copies ran while one was open for 0% of the time, Pallas kernels for 15%

profile of v3, /device:TPU:0, one launch (start us, length us, event | category | flops | bytes accessed | tf_op | source)
XLA Modules:
  0.0 76.4 jit_solution(5431145762063705656)
XLA Ops:
  0.6 0.0 copy-start.2
  0.6 1.2 %join.1.refs_4_.refs_1_.refs_5_ = bf16[528,768]{1,0:T(8,128)(2,1)S(1)} custom-call(s32[1,2]{1,0:T(1,128)} %refs_1_.7, bf16[256,768]{1,0:T(8,128)(2,1)} %key_ref.1, bf16[256,768]{1,0:T(8,128)(2,1)} %value_ref.1), custom_call_target="tpu_custom_call" | custom-call | tf_op jit(solution)/shard_map/join/pallas_call | solution.py:395
  1.8 0.5 collective-permute-start.1
  2.3 0.7 collective-permute-start
  3.0 1.2 %collective-permute-done.1.refs_2_ = bf16[528,768]{1,0:T(8,128)(2,1)S(1)} collective-permute-done((bf16[528,768]{1,0:T(8,128)(2,1)S(1)}, bf16[528,768]{1,0:T(8,128)(2,1)S(1)}, u32[]{:S(2)}, u32[]{:S(2)}) %collective-permute-start.1) | collective-permute-done | bytes 811040 | tf_op jit(solution)/shard_map/ppermute | solution.py:49
  4.3 0.0 copy-done.2
  4.3 0.3 split.1.refs_1_
  4.6 0.0 copy-start.3
  4.6 0.0 copy-start.4
  4.6 0.0 copy-start.5
  4.6 2.9 %collective-permute-start.2 = (bf16[3,128,768]{2,1,0:T(8,128)(2,1)S(1)}, bf16[3,128,768]{2,1,0:T(8,128)(2,1)S(1)}, u32[]{:S(2)}, u32[]{:S(2)}) collective-permute-start(bf16[3,128,768]{2,1,0:T(8,128)(2,1)S(1)} %split.1.refs_1_), channel_id=1, source_target_pairs={{0,2},{1,5},{2,0},{3,7},{4,6},{5,1},{6,4},{7,3},{8,10},{9,13},{10,... | collective-permute-start | bytes 1769480 | tf_op jit(solution)/shard_map/ppermute | solution.py:49
  7.5 0.0 collective-permute-done.refs_3_
  7.5 14.1 %collective-permute-done.2.refs_2_ = bf16[3,128,768]{2,1,0:T(8,128)(2,1)S(1)} collective-permute-done((bf16[3,128,768]{2,1,0:T(8,128)(2,1)S(1)}, bf16[3,128,768]{2,1,0:T(8,128)(2,1)S(1)}, u32[]{:S(2)}, u32[]{:S(2)}) %collective-permute-start.2) | collective-permute-done | bytes 589856 | tf_op jit(solution)/shard_map/ppermute | solution.py:49
  21.6 0.3 step.1.refs_3_
  21.9 4.1 %collective-permute-start.3 = (bf16[3,128,768]{2,1,0:T(8,128)(2,1)S(1)}, bf16[3,128,768]{2,1,0:T(8,128)(2,1)}, u32[]{:S(2)}, u32[]{:S(2)}) collective-permute-start(bf16[3,128,768]{2,1,0:T(8,128)(2,1)S(1)} %step.1.refs_3_), channel_id=1, source_target_pairs={{0,4},{1,3},{2,6},{3,1},{4,0},{5,7},{6,2},{7,5},{8,12},{9,11},{10,... | collective-permute-start | bytes 1769480 | tf_op jit(solution)/shard_map/ppermute | solution.py:49
  26.0 0.0 copy-done.3
  26.0 0.0 copy-done.4
  26.0 0.0 copy-done.5
  26.0 1.5 %bias.1.refs_0_ = f32[6,8,256]{2,1,0:T(8,128)S(1)} custom-call(s32[1,4]{1,0:T(1,128)S(1)} %bitcast.3, s32[1,2]{1,0:T(1,128)S(1)} %copy-done.3, s32[16]{0:T(128)S(1)} %copy-done.5, f32[6,16,16]{2,1,0:T(8,128)S(1)} %copy-done.4), custom_call_target="tpu_custom_call" | custom-call | flops 100663296 | tf_op jit(solution)/shard_map/bias/pallas_call | solution.py:37
  27.5 0.0 copy-start
  27.5 0.0 copy-start.1
  27.5 0.1 broadcast_select_fusion.refs_3_.refs_4_
  27.6 0.9 %copy-done = bf16[256,768]{1,0:T(8,128)(2,1)S(1)} copy-done((bf16[256,768]{1,0:T(8,128)(2,1)S(1)}, bf16[256,768]{1,0:T(8,128)(2,1)}, u32[]{:S(2)}) %copy-start) | copy-done | bytes 393240
  28.5 0.1 copy-done.1
  28.6 1.3 %stats.1.refs_5_.refs_1_ = f32[6,8,256]{2,1,0:T(8,128)S(1)} custom-call(f32[6,8,256]{2,1,0:T(8,128)S(1)} %bias.1.refs_0_, bf16[256,768]{1,0:T(8,128)(2,1)S(1)} %copy-done, bf16[256,768]{1,0:T(8,128)(2,1)S(1)} %copy-done.1, bf16[528,768]{1,0:T(8,128)(2,1)S(1)} %broadcast_select_fusion.refs_3_.refs_4_, bf16[528,768]{1,0:T(8,128)(2,1)S(1)} %join.1.refs_4_.refs_1_.refs_5_), custom_call_target="tpu_custom_call" | custom-call | flops 402653184 | tf_op jit(solution)/shard_map/stats/pallas_call | solution.py:37
  29.9 4.1 %collective-permute-done.3.refs_4_ = bf16[3,128,768]{2,1,0:T(8,128)(2,1)} collective-permute-done((bf16[3,128,768]{2,1,0:T(8,128)(2,1)S(1)}, bf16[3,128,768]{2,1,0:T(8,128)(2,1)}, u32[]{:S(2)}, u32[]{:S(2)}) %collective-permute-start.3) | collective-permute-done | bytes 589856 | tf_op jit(solution)/shard_map/ppermute | solution.py:49
  34.0 2.2 %pick.1 = (bf16[2,128,768]{2,1,0:T(8,128)(2,1)S(1)}, bf16[2,128,768]{2,1,0:T(8,128)(2,1)S(1)}) custom-call(s32[1,4]{1,0:T(1,128)S(1)} %bitcast.4, s32[1,2]{1,0:T(1,128)S(1)} %copy-done.3, bf16[528,768]{1,0:T(8,128)(2,1)S(1)} %collective-permute-done.1.refs_2_, bf16[3,128,768]{2,1,0:T(8,128)(2,1)S(1)} %step.1.refs_3_, ...), custom_call_target="tpu_custom_call" | custom-call | tf_op jit(solution)/shard_map/pick/pallas_call | solution.py:37
  36.2 0.1 collective-permute-start.4
  36.2 1.7 %collective-permute-done.4.refs_5_.refs_7_ = bf16[2,128,768]{2,1,0:T(8,128)(2,1)S(1)} collective-permute-done((bf16[2,128,768]{2,1,0:T(8,128)(2,1)S(1)}, bf16[2,128,768]{2,1,0:T(8,128)(2,1)S(1)}, u32[]{:S(2)}, u32[]{:S(2)}) %collective-permute-start.4) | collective-permute-done | bytes 393248 | tf_op jit(solution)/shard_map/ppermute | solution.py:49
  37.9 2.4 %memory.1 = (f32[6,8,256]{2,1,0:T(8,128)S(1)}, bf16[2,128,768]{2,1,0:T(8,128)(2,1)S(1)}, bf16[2,128,768]{2,1,0:T(8,128)(2,1)S(1)}) custom-call(f32[6,8,256]{2,1,0:T(8,128)S(1)} %bias.1.refs_0_, f32[6,8,256]{2,1,0:T(8,128)S(1)} %stats.1.refs_5_.refs_1_, bf16[256,768]{1,0:T(8,128)(2,1)S(1)} %copy-done, bf16[256,768]{1,0:T(8,128)(2,1)S(1)} %copy-done.1, ...), custom_call_target="tpu_custom_call" | custom-call | flops 402653184 | tf_op jit(solution)/shard_map/memory/pallas_call | solution.py:37
  40.4 0.2 collective-permute-start.7
  40.6 1.5 %back.1.refs_5_ = bf16[2,256,768]{2,1,0:T(8,128)(2,1)S(1)} custom-call(f32[6,8,256]{2,1,0:T(8,128)S(1)} %bias.1.refs_0_, f32[6,8,256]{2,1,0:T(8,128)S(1)} %get-tuple-element.22.refs_1_, bf16[256,768]{1,0:T(8,128)(2,1)S(1)} %copy-done, bf16[256,768]{1,0:T(8,128)(2,1)S(1)} %copy-done.1, bf16[528,768]{1,0:T(8,128)(2,1)S(1)} %broadcast_select_fusion.refs_3_.refs_4_), custom_call_target="tpu_custom_call" | custom-call | flops 402653184 | tf_op jit(solution)/shard_map/back/pallas_call | solution.py:37
  42.1 0.7 collective-permute-start.6
  42.8 0.0 collective-permute-done.7.refs_4_
  42.8 1.5 %sum.1 = (f32[3,128,768]{2,1,0:T(8,128)S(1)}, bf16[3,128,768]{2,1,0:T(8,128)(2,1)S(1)}) custom-call(s32[1,4]{1,0:T(1,128)S(1)} %bitcast.5, s32[1,2]{1,0:T(1,128)S(1)} %copy-done.3, bf16[528,768]{1,0:T(8,128)(2,1)S(1)} %collective-permute-done.1.refs_2_, bf16[2,128,768]{2,1,0:T(8,128)(2,1)S(1)} %get-tuple-element.26.refs_3_, ...), custom_call_target="tpu_custom_call" | custom-call | tf_op jit(solution)/shard_map/sum/pallas_call | solution.py:37
  44.3 3.8 %collective-permute-start.8 = (bf16[3,128,768]{2,1,0:T(8,128)(2,1)S(1)}, bf16[3,128,768]{2,1,0:T(8,128)(2,1)S(1)}, u32[]{:S(2)}, u32[]{:S(2)}) collective-permute-start(bf16[3,128,768]{2,1,0:T(8,128)(2,1)S(1)} %get-tuple-element.29), channel_id=1, source_target_pairs={{0,4},{1,3},{2,6},{3,1},{4,0},{5,7},{6,2},{7,5},{8,12},{9,11},{10,... | collective-permute-start | bytes 1769480 | tf_op jit(solution)/shard_map/ppermute | solution.py:49
  48.1 5.2 %rest.1 = (bf16[256,768]{1,0:T(8,128)(2,1)}, bf16[256,768]{1,0:T(8,128)(2,1)}, f32[2,256,768]{2,1,0:T(8,128)S(1)}) custom-call(f32[6,8,256]{2,1,0:T(8,128)S(1)} %bias.1.refs_0_, f32[6,8,256]{2,1,0:T(8,128)S(1)} %get-tuple-element.22.refs_1_, bf16[256,768]{1,0:T(8,128)(2,1)S(1)} %copy-done, bf16[256,768]{1,0:T(8,128)(2,1)S(1)} %copy-done.1, ...), custom_call_target="tpu_custom_call" | custom-call | flops 1409286144 | tf_op jit(solution)/shard_map/rest/pallas_call | solution.py:37
  53.3 0.0 collective-permute-done.6.refs_2_
  53.3 2.7 %collective-permute-done.8.refs_1_ = bf16[3,128,768]{2,1,0:T(8,128)(2,1)S(1)} collective-permute-done((bf16[3,128,768]{2,1,0:T(8,128)(2,1)S(1)}, bf16[3,128,768]{2,1,0:T(8,128)(2,1)S(1)}, u32[]{:S(2)}, u32[]{:S(2)}) %collective-permute-start.8) | collective-permute-done | bytes 589856 | tf_op jit(solution)/shard_map/ppermute | solution.py:49
  56.0 0.2 add.1
  56.1 9.1 %collective-permute-start.9 = (bf16[3,128,768]{2,1,0:T(8,128)(2,1)S(1)}, bf16[3,128,768]{2,1,0:T(8,128)(2,1)S(1)}, u32[]{:S(2)}, u32[]{:S(2)}) collective-permute-start(bf16[3,128,768]{2,1,0:T(8,128)(2,1)S(1)} %get-tuple-element.31), channel_id=1, source_target_pairs={{0,2},{1,5},{2,0},{3,7},{4,6},{5,1},{6,4},{7,3},{8,10},{9,13},{10,... | collective-permute-start | bytes 1769480 | tf_op jit(solution)/shard_map/ppermute | solution.py:49
  65.2 1.3 %collective-permute-start.5 = (bf16[2,256,768]{2,1,0:T(8,128)(2,1)S(1)}, bf16[2,256,768]{2,1,0:T(8,128)(2,1)S(1)}, u32[]{:S(2)}, u32[]{:S(2)}) collective-permute-start(bf16[2,256,768]{2,1,0:T(8,128)(2,1)S(1)} %back.1.refs_5_), channel_id=1, source_target_pairs={{1,0},{3,2},{5,4},{7,6},{9,8},{11,10},{13,12},{15,14},{17,16},{19,... | collective-permute-start | bytes 2359304 | tf_op jit(solution)/shard_map/ppermute | solution.py:54
  66.5 6.6 %collective-permute-done.9.refs_2_ = bf16[3,128,768]{2,1,0:T(8,128)(2,1)S(1)} collective-permute-done((bf16[3,128,768]{2,1,0:T(8,128)(2,1)S(1)}, bf16[3,128,768]{2,1,0:T(8,128)(2,1)S(1)}, u32[]{:S(2)}, u32[]{:S(2)}) %collective-permute-start.9) | collective-permute-done | bytes 589856 | tf_op jit(solution)/shard_map/ppermute | solution.py:49
  73.1 0.4 owned.1
  73.4 0.1 collective-permute-start.10
  73.5 0.0 collective-permute-done.5.refs_1_
  73.5 1.7 %collective-permute-done.10.refs_4_ = bf16[2,128,768]{2,1,0:T(8,128)(2,1)S(1)} collective-permute-done((bf16[2,128,768]{2,1,0:T(8,128)(2,1)S(1)}, bf16[2,128,768]{2,1,0:T(8,128)(2,1)S(1)}, u32[]{:S(2)}, u32[]{:S(2)}) %collective-permute-start.10) | collective-permute-done | bytes 393248 | tf_op jit(solution)/shard_map/ppermute | solution.py:49
  75.2 1.1 %final.1 = (bf16[256,768]{1,0:T(8,128)(2,1)}, bf16[256,768]{1,0:T(8,128)(2,1)}) custom-call(f32[2,256,768]{2,1,0:T(8,128)S(1)} %get-tuple-element.25.refs_3_.refs_0_, bf16[2,256,768]{2,1,0:T(8,128)(2,1)S(1)} %collective-permute-done.5.refs_1_, bf16[2,256,768]{2,1,0:T(8,128)(2,1)S(1)} %collective-permute-done.6.refs_2_, ...), custom_call_target="tpu_custom_call" | custom-call | tf_op jit(solution)/shard_map/final/pallas_call | solution.py:37
Async XLA Ops:
  0.6 3.6 %copy-start.2 = (s32[4]{0:T(128)S(1)}, s32[4]{0:T(128)}, u32[]{:S(2)}) copy-start(s32[4]{0:T(128)} %param.15) | copy-start | bytes 52
  1.8 2.5 %collective-permute-start.1 = (bf16[528,768]{1,0:T(8,128)(2,1)S(1)}, bf16[528,768]{1,0:T(8,128)(2,1)S(1)}, u32[]{:S(2)}, u32[]{:S(2)}) collective-permute-start(bf16[528,768]{1,0:T(8,128)(2,1)S(1)} %join.1.refs_4_.refs_1_.refs_5_), channel_id=1, source_target_pairs={{0,1},{1,0},{2,3},{3,2},{4,5},{5,4},{6,7},{7,6},{8,9},{9,8},{10,11... | collective-permute-start | bytes 2433032 | tf_op jit(solution)/shard_map/ppermute | solution.py:49
  2.3 5.2 %collective-permute-start = (bf16[528,768]{1,0:T(8,128)(2,1)S(1)}, bf16[528,768]{1,0:T(8,128)(2,1)S(1)}, u32[]{:S(2)}, u32[]{:S(2)}) collective-permute-start(bf16[528,768]{1,0:T(8,128)(2,1)S(1)} %join.1.refs_4_.refs_1_.refs_5_), channel_id=1, source_target_pairs={{1,2},{3,4},{5,6},{9,10},{11,12},{13,14},{17,18},{19,20},{21,22},{... | collective-permute-start | bytes 2433032 | tf_op jit(solution)/shard_map/ppermute | solution.py:54
  4.6 21.4 %copy-start.3 = (s32[1,2]{1,0:T(1,128)S(1)}, s32[1,2]{1,0:T(1,128)}, u32[]{:S(2)}) copy-start(s32[1,2]{1,0:T(1,128)} %refs_1_.7) | copy-start | bytes 28
  4.6 21.4 %copy-start.4 = (f32[6,16,16]{2,1,0:T(8,128)S(1)}, f32[6,16,16]{2,1,0:T(8,128)}, u32[]{:S(2)}) copy-start(f32[6,16,16]{2,1,0:T(8,128)} %refs_3_.4) | copy-start | bytes 18436
  4.6 21.4 %copy-start.5 = (s32[16]{0:T(128)S(1)}, s32[16]{0:T(128)}, u32[]{:S(2)}) copy-start(s32[16]{0:T(128)} %refs_2_.5) | copy-start | bytes 196
  4.6 17.0 %collective-permute-start.2 = (bf16[3,128,768]{2,1,0:T(8,128)(2,1)S(1)}, bf16[3,128,768]{2,1,0:T(8,128)(2,1)S(1)}, u32[]{:S(2)}, u32[]{:S(2)}) collective-permute-start(bf16[3,128,768]{2,1,0:T(8,128)(2,1)S(1)} %split.1.refs_1_), channel_id=1, source_target_pairs={{0,2},{1,5},{2,0},{3,7},{4,6},{5,1},{6,4},{7,3},{8,10},{9,13},{10,... | collective-permute-start | bytes 1769480 | tf_op jit(solution)/shard_map/ppermute | solution.py:49
  21.9 12.1 %collective-permute-start.3 = (bf16[3,128,768]{2,1,0:T(8,128)(2,1)S(1)}, bf16[3,128,768]{2,1,0:T(8,128)(2,1)}, u32[]{:S(2)}, u32[]{:S(2)}) collective-permute-start(bf16[3,128,768]{2,1,0:T(8,128)(2,1)S(1)} %step.1.refs_3_), channel_id=1, source_target_pairs={{0,4},{1,3},{2,6},{3,1},{4,0},{5,7},{6,2},{7,5},{8,12},{9,11},{10,... | collective-permute-start | bytes 1769480 | tf_op jit(solution)/shard_map/ppermute | solution.py:49
  27.5 1.0 %copy-start = (bf16[256,768]{1,0:T(8,128)(2,1)S(1)}, bf16[256,768]{1,0:T(8,128)(2,1)}, u32[]{:S(2)}) copy-start(bf16[256,768]{1,0:T(8,128)(2,1)} %refs_2_.9) | copy-start | bytes 1179652
  27.5 1.1 %copy-start.1 = (bf16[256,768]{1,0:T(8,128)(2,1)S(1)}, bf16[256,768]{1,0:T(8,128)(2,1)}, u32[]{:S(2)}) copy-start(bf16[256,768]{1,0:T(8,128)(2,1)} %refs_3_.7) | copy-start | bytes 1179652
  36.2 1.8 %collective-permute-start.4 = (bf16[2,128,768]{2,1,0:T(8,128)(2,1)S(1)}, bf16[2,128,768]{2,1,0:T(8,128)(2,1)S(1)}, u32[]{:S(2)}, u32[]{:S(2)}) collective-permute-start(bf16[2,128,768]{2,1,0:T(8,128)(2,1)S(1)} %get-tuple-element.21), channel_id=1, source_target_pairs={{0,1},{1,0},{2,3},{3,2},{4,5},{5,4},{6,7},{7,6},{8,9},{9,8},{10,11... | collective-permute-start | bytes 1179656 | tf_op jit(solution)/shard_map/ppermute | solution.py:49
  40.4 2.4 %collective-permute-start.7 = (bf16[2,128,768]{2,1,0:T(8,128)(2,1)S(1)}, bf16[2,128,768]{2,1,0:T(8,128)(2,1)S(1)}, u32[]{:S(2)}, u32[]{:S(2)}) collective-permute-start(bf16[2,128,768]{2,1,0:T(8,128)(2,1)S(1)} %get-tuple-element.27), channel_id=1, source_target_pairs={{0,1},{1,0},{2,3},{3,2},{4,5},{5,4},{6,7},{7,6},{8,9},{9,8},{10,11... | collective-permute-start | bytes 1179656 | tf_op jit(solution)/shard_map/ppermute | solution.py:49
  42.1 11.3 %collective-permute-start.6 = (bf16[2,256,768]{2,1,0:T(8,128)(2,1)S(1)}, bf16[2,256,768]{2,1,0:T(8,128)(2,1)S(1)}, u32[]{:S(2)}, u32[]{:S(2)}) collective-permute-start(bf16[2,256,768]{2,1,0:T(8,128)(2,1)S(1)} %back.1.refs_5_), channel_id=1, source_target_pairs={{2,1},{4,3},{6,5},{10,9},{12,11},{14,13},{18,17},{20,19},{22,21},{... | collective-permute-start | bytes 2359304 | tf_op jit(solution)/shard_map/ppermute | solution.py:54
  44.3 11.7 %collective-permute-start.8 = (bf16[3,128,768]{2,1,0:T(8,128)(2,1)S(1)}, bf16[3,128,768]{2,1,0:T(8,128)(2,1)S(1)}, u32[]{:S(2)}, u32[]{:S(2)}) collective-permute-start(bf16[3,128,768]{2,1,0:T(8,128)(2,1)S(1)} %get-tuple-element.29), channel_id=1, source_target_pairs={{0,4},{1,3},{2,6},{3,1},{4,0},{5,7},{6,2},{7,5},{8,12},{9,11},{10,... | collective-permute-start | bytes 1769480 | tf_op jit(solution)/shard_map/ppermute | solution.py:49
  56.1 16.9 %collective-permute-start.9 = (bf16[3,128,768]{2,1,0:T(8,128)(2,1)S(1)}, bf16[3,128,768]{2,1,0:T(8,128)(2,1)S(1)}, u32[]{:S(2)}, u32[]{:S(2)}) collective-permute-start(bf16[3,128,768]{2,1,0:T(8,128)(2,1)S(1)} %get-tuple-element.31), channel_id=1, source_target_pairs={{0,2},{1,5},{2,0},{3,7},{4,6},{5,1},{6,4},{7,3},{8,10},{9,13},{10,... | collective-permute-start | bytes 1769480 | tf_op jit(solution)/shard_map/ppermute | solution.py:49
  65.2 8.3 %collective-permute-start.5 = (bf16[2,256,768]{2,1,0:T(8,128)(2,1)S(1)}, bf16[2,256,768]{2,1,0:T(8,128)(2,1)S(1)}, u32[]{:S(2)}, u32[]{:S(2)}) collective-permute-start(bf16[2,256,768]{2,1,0:T(8,128)(2,1)S(1)} %back.1.refs_5_), channel_id=1, source_target_pairs={{1,0},{3,2},{5,4},{7,6},{9,8},{11,10},{13,12},{15,14},{17,16},{19,... | collective-permute-start | bytes 2359304 | tf_op jit(solution)/shard_map/ppermute | solution.py:54
  73.4 1.8 %collective-permute-start.10 = (bf16[2,128,768]{2,1,0:T(8,128)(2,1)S(1)}, bf16[2,128,768]{2,1,0:T(8,128)(2,1)S(1)}, u32[]{:S(2)}, u32[]{:S(2)}) collective-permute-start(bf16[2,128,768]{2,1,0:T(8,128)(2,1)S(1)} %get-tuple-element.33), channel_id=1, source_target_pairs={{0,1},{1,0},{2,3},{3,2},{4,5},{5,4},{6,7},{7,6},{8,9},{9,8},{10,11... | collective-permute-start | bytes 1179656 | tf_op jit(solution)/shard_map/ppermute | solution.py:49

commit v4 on v3

v4 whole, which is shorter than its diff:
```python
import functools
import math

import jax
import jax.numpy as jnp
from jax import lax
from jax.experimental import pallas as pl
from jax.experimental.pallas import tpu as pltpu
from jax.sharding import PartitionSpec as P

FR_DEV = 2
MEM = 2
DEPTH = 128
TAIL = 16

BLOCKED_LOGIT = -1e30
LOG2E = math.log2(math.e)
FACTOR = 1.0 / math.sqrt(DEPTH)

SMEM = pl.BlockSpec(memory_space=pltpu.SMEM)
VMEM = pl.BlockSpec(memory_space=pltpu.VMEM)
ANY = pl.BlockSpec(memory_space=pl.ANY)
HIDING = 200
VMEM_LIMIT = 32 * 1024 * 1024
BF16, F32 = jnp.bfloat16, jnp.float32


def shape(dtype, *dims):
    return jax.ShapeDtypeStruct(dims, dtype)


def call(kernel, outs, arrays, scalars=(), after=(), flops=0, name=None):
    count = len(scalars) + len(arrays)

    def run(*refs):
        kernel(*refs[:count], *refs[count + len(after) :])

    return pl.pallas_call(
        run,
        out_shape=outs,
        in_specs=[SMEM] * len(scalars) + [VMEM] * len(arrays) + [ANY] * len(after),
        out_specs=[VMEM] * len(outs),
        compiler_params=pltpu.CompilerParams(vmem_limit_bytes=VMEM_LIMIT),
        cost_estimate=pl.CostEstimate(flops=flops, bytes_accessed=0, transcendentals=0) if flops else None,
        name=name,
    )(*scalars, *arrays, *after)


def swap(block, even_bit, odd_bit, peers):
    return lax.ppermute(block, "tm", [(i, i ^ (odd_bit if i & 1 else even_bit)) for i in range(peers)])


def shift(block, by, start, peers):
    pairs = [(i, i + by) for i in range(start, peers, 2) if 0 <= i + by < peers]
    return lax.ppermute(block, "tm", pairs)


def lane_value(row, lane):
    lanes = lax.broadcasted_iota(jnp.int32, row.shape, 1)
    return jnp.max(jnp.where(lanes == lane, row, 0))


def bank_of(bank_ref):
    row = bank_ref[...]
    return [lane_value(row, slot) for slot in range(row.shape[1])]


def dyn_frames(bank, last_frame):
    found = [jnp.int32(0)] * (len(bank) - 2)
    seen = jnp.int32(0)
    for frame in bank:
        free = jnp.logical_and(frame != 0, frame != last_frame)
        for j in range(len(found)):
            found[j] = jnp.where(jnp.logical_and(free, seen == j), frame, found[j])
        seen = seen + free.astype(jnp.int32)
    return found


def place_of(frame, dyns):
    place = jnp.int32(len(dyns))
    for j, dyn in enumerate(dyns):
        place = jnp.where(frame == dyn, j, place)
    return place


def choose(out, take_first, first, second):
    @pl.when(take_first)
    def _():
        out[...] = first[...]

    @pl.when(jnp.logical_not(take_first))
    def _():
        out[...] = second[...]


def has_end(me, done, peers):
    return jnp.logical_or((me & ~done) == 0, (me | done) == peers - 1)


def has_dyn(me, frame, done):
    return ((me ^ (frame // FR_DEV)) & ~done) == 0


def by_role(me, even_value, odd_value):
    return jnp.where((me & 1) == 0, even_value, odd_value)


def join_kernel(index_ref, key_ref, value_ref, joined_ref, index_buf, sems):
    rows = key_ref.shape[0]
    copies = [
        pltpu.make_async_copy(index_ref, index_buf, sems.at[0]),
        pltpu.make_async_copy(key_ref, joined_ref.at[pl.ds(0, rows)], sems.at[1]),
        pltpu.make_async_copy(value_ref, joined_ref.at[pl.ds(rows, rows)], sems.at[2]),
    ]
    for copy in copies:
        copy.start()
    copies[0].wait()
    width = joined_ref.shape[1]
    lane = lax.broadcasted_iota(jnp.int32, (TAIL, width), 1) // DEPTH
    tail = jnp.zeros((TAIL, width), jnp.int32)
    for m in range(MEM):
        tail = jnp.where(lane == m, index_buf[0:1, m : m + 1], tail)
    joined_ref[2 * rows : 2 * rows + TAIL, :] = tail.astype(F32).astype(BF16)
    copies[1].wait()
    copies[2].wait()


def join_queries_kernel(query_ref, cotangent_ref, joined_ref, sems):
    rows = query_ref.shape[0]
    copies = [
        pltpu.make_async_copy(ref, joined_ref.at[pl.ds(j * rows, rows)], sems.at[j])
        for j, ref in enumerate((query_ref, cotangent_ref))
    ]
    for copy in copies:
        copy.start()
    for copy in copies:
        copy.wait()


def pack(fields, width):
    code = jnp.int32(0)
    for j, field in enumerate(fields):
        code = code | (field.astype(jnp.int32) << (j * width))
    return code


def field(code, j, width):
    return (code >> (j * width)) & ((1 << width) - 1)


def code_of(codes_ref, row):
    return jnp.max(codes_ref[row : row + 1, :])


PICK, SUM, OWNED = range(3)
PLACE_BITS = 4


def plan_kernel(peers, last_bits, bank_ref, index_ref, pose_ref, bias_ref, pair_ref, rows_ref, codes_ref):
    me = lax.axis_index("tm")
    last_frame = peers * FR_DEV - 1
    heads, _, row_count = rows_ref.shape
    bank = [bank_ref[0, slot] for slot in range(bank_ref.shape[1])]
    tail = pair_ref.shape[0] - TAIL
    pair_ids = []
    for m in range(MEM):
        slot = jnp.max(pair_ref[tail : tail + TAIL, m * DEPTH : (m + 1) * DEPTH].astype(F32)).astype(jnp.int32)
        pair_ids.append(bank_ref[0, slot])
    mem_ids = [bank_ref[0, index_ref[0, m]] for m in range(MEM)]

    own_ids = [me * FR_DEV + j for j in range(FR_DEV)]
    prev_ids = [jnp.maximum(own - FR_DEV, 0) for own in own_ids]
    next_ids = [jnp.minimum(own + FR_DEV, last_frame) for own in own_ids]
    key_ids = prev_ids + own_ids + mem_ids + own_ids
    poses = [[pose_ref[frame] for frame in ids] for ids in (own_ids, next_ids, key_ids)]
    frame_of = lax.broadcasted_iota(jnp.int32, (1, row_count), 1) // (row_count // FR_DEV)
    for head in range(heads):
        for j, key_pose in enumerate(poses[2]):
            row = jnp.zeros((1, row_count), F32)
            for a, query_pose in enumerate(poses[1] if j >= 2 * FR_DEV + MEM else poses[0]):
                value = bias_ref[head, query_pose, key_pose] * LOG2E
                if j < FR_DEV:
                    value = jnp.where(me == 0, BLOCKED_LOGIT, value)
                row = jnp.where(frame_of == a, value, row)
            rows_ref[head, j : j + 1, :] = row

    dyns = dyn_frames(bank, last_frame)
    bit = by_role(me, *last_bits)
    upper = (me & bit) != 0
    picks = []
    for frame in mem_ids + pair_ids:
        source = place_of(frame, dyns)
        local = jnp.where(frame == 0, jnp.logical_not(upper), upper)
        local = jnp.where(source < len(dyns), has_dyn(me, frame, (peers - 1) & ~bit), local)
        picks.append(source * 2 + local.astype(jnp.int32))
    places = dyns + [jnp.where(upper, last_frame, 0), jnp.where(upper, 0, last_frame)]
    terms = [name == frame for frame in places for name in mem_ids + pair_ids]
    owned = []
    for group in (me, me ^ 1):
        for j in range(FR_DEV):
            frame = group * FR_DEV + j
            place = place_of(frame, dyns)
            named = jnp.logical_or(place < len(dyns), jnp.logical_or(frame == 0, frame == last_frame))
            owned.append(place * 2 + named.astype(jnp.int32))
    lanes = codes_ref.shape[1]
    for row, code in ((PICK, pack(picks, PLACE_BITS)), (SUM, pack(terms, 1)), (OWNED, pack(owned, PLACE_BITS))):
        codes_ref[row : row + 1, :] = jnp.full((1, lanes), code, jnp.int32)


def split_kernel(peers, bank_ref, mine_ref, pair_ref, out_ref):
    me = lax.axis_index("tm")
    frame_len = out_ref.shape[1]
    dyns = dyn_frames(bank_of(bank_ref), peers * FR_DEV - 1)
    places = [(has_dyn(me, dyn, 0), dyn % FR_DEV) for dyn in dyns]
    places.append((has_end(me, 0, peers), jnp.where(me < peers // 2, 0, FR_DEV - 1)))
    for j, (local, frame) in enumerate(places):
        start = pl.multiple_of(((me & 1) * FR_DEV + frame) * frame_len, frame_len)
        part = pl.ds(start, frame_len)
        choose(out_ref.at[j], local, mine_ref.at[part], pair_ref.at[part])


def step_kernel(peers, even_done, odd_done, bank_ref, mine_ref, got_ref, out_ref):
    me = lax.axis_index("tm")
    done = by_role(me, even_done, odd_done)
    dyns = dyn_frames(bank_of(bank_ref), peers * FR_DEV - 1)
    flags = [has_dyn(me, dyn, done) for dyn in dyns] + [has_end(me, done, peers)]
    for j, flag in enumerate(flags):
        choose(out_ref.at[j], flag, mine_ref.at[j], got_ref.at[j])


def pick_kernel(codes_ref, mine_ref, got_ref, own_out, pair_out):
    code = code_of(codes_ref, PICK)
    for o, out in enumerate((own_out, pair_out)):
        for m in range(MEM):
            pick = field(code, o * MEM + m, PLACE_BITS)
            source = pick >> 1
            choose(out.at[m], (pick & 1) != 0, mine_ref.at[source], got_ref.at[source])


def dot(a, b, left, right):
    return lax.dot_general(a, b, (((left,), (right,)), ((), ())), preferred_element_type=F32)


def logits_of(keys, query, rows_ref, head, piece):
    frame_len = query.shape[0] // FR_DEV
    raw = dot(keys, query, 1, 1) * (FACTOR * LOG2E)
    parts = []
    for j in range(FR_DEV):
        row = piece * FR_DEV + j
        parts.append(raw[j * frame_len : (j + 1) * frame_len] + rows_ref[head, row : row + 1, :])
    return jnp.concatenate(parts, axis=0)


def joined_parts(joined_ref, cols):
    rows = joined_ref.shape[0] // 2 // DEPTH * DEPTH
    return joined_ref[0:rows, cols], joined_ref[rows : 2 * rows, cols]


def prev_parts(outer_ref, pair_ref, cols):
    even = (lax.axis_index("tm") & 1) == 0
    parts = zip(joined_parts(outer_ref, cols), joined_parts(pair_ref, cols))
    return tuple(jnp.where(even, outer, pair) for outer, pair in parts)


def stats_kernel(rows_ref, queries_ref, outer_ref, pair_ref, own_ref, stats_ref):
    for head in range(queries_ref.shape[1] // DEPTH):
        cols = pl.ds(head * DEPTH, DEPTH)
        query, cotangent = joined_parts(queries_ref, cols)
        pieces = [prev_parts(outer_ref, pair_ref, cols), joined_parts(own_ref, cols)]
        logits = [logits_of(keys, query, rows_ref, head, piece) for piece, (keys, _) in enumerate(pieces)]
        peak = functools.reduce(jnp.maximum, [jnp.max(block, axis=0, keepdims=True) for block in logits])
        exps = [jnp.exp2(block - peak) for block in logits]
        slopes = [dot(values, cotangent, 1, 1) for _, values in pieces]
        stats_ref[head, 0:1, :] = peak
        stats_ref[head, 1:2, :] = sum(jnp.sum(e, axis=0, keepdims=True) for e in exps)
        stats_ref[head, 2:3, :] = sum(jnp.sum(e * s, axis=0, keepdims=True) for e, s in zip(exps, slopes))


def memory_kernel(rows_ref, part_ref, queries_ref, mine_ref, got_ref, stats_ref, mem_same_ref, mem_other_ref):
    even = (lax.axis_index("tm") & 1) == 0
    frame_len = mine_ref.shape[1]
    for head in range(queries_ref.shape[1] // DEPTH):
        cols = pl.ds(head * DEPTH, DEPTH)
        query, cotangent = joined_parts(queries_ref, cols)
        mine = mine_ref[:, :, cols].reshape(MEM * frame_len, DEPTH)
        got = got_ref[:, :, cols].reshape(MEM * frame_len, DEPTH)
        keys, values = jnp.where(even, mine, got), jnp.where(even, got, mine)
        logits = logits_of(keys, query, rows_ref, head, 2)
        part_peak = part_ref[head, 0:1, :]
        peak = jnp.maximum(part_peak, jnp.max(logits, axis=0, keepdims=True))
        exps = jnp.exp2(logits - peak)
        slopes = dot(values, cotangent, 1, 1)
        scale = jnp.exp2(part_peak - peak)
        total = part_ref[head, 1:2, :] * scale + jnp.sum(exps, axis=0, keepdims=True)
        inverse = 1.0 / total
        spread = (part_ref[head, 2:3, :] * scale + jnp.sum(exps * slopes, axis=0, keepdims=True)) * inverse
        stats_ref[head, 0:1, :] = peak
        stats_ref[head, 1:2, :] = inverse
        stats_ref[head, 2:3, :] = spread
        probs = exps * inverse
        dlogits = (probs * (slopes - spread)).astype(BF16)
        key_part = (dot(dlogits, query, 1, 0) * FACTOR).astype(BF16).reshape(MEM, frame_len, DEPTH)
        value_part = dot(probs.astype(BF16), cotangent, 1, 0).astype(BF16).reshape(MEM, frame_len, DEPTH)
        mem_same_ref[:, :, cols] = jnp.where(even, key_part, value_part)
        mem_other_ref[:, :, cols] = jnp.where(even, value_part, key_part)


def probs_of(keys, values, query, cotangent, rows_ref, stats_ref, head, piece):
    logits = logits_of(keys, query, rows_ref, head, piece)
    probs = jnp.exp2(logits - stats_ref[head, 0:1, :]) * stats_ref[head, 1:2, :]
    dlogits = probs * (dot(values, cotangent, 1, 1) - stats_ref[head, 2:3, :])
    return probs.astype(BF16), dlogits.astype(BF16)


def next_kernel(rows_ref, stats_ref, queries_ref, own_ref, next_ref):
    for head in range(queries_ref.shape[1] // DEPTH):
        cols = pl.ds(head * DEPTH, DEPTH)
        query, cotangent = joined_parts(queries_ref, cols)
        keys, values = joined_parts(own_ref, cols)
        weights, dlogits = probs_of(keys, values, query, cotangent, rows_ref, stats_ref, head, 3)
        next_ref[0, :, cols] = dot(dlogits, query, 1, 0) * FACTOR
        next_ref[1, :, cols] = dot(weights, cotangent, 1, 0)


def rest_kernel(
    rows_ref,
    stats_ref,
    queries_ref,
    outer_ref,
    pair_ref,
    joined_ref,
    mine_ref,
    got_ref,
    next_ref,
    attended_ref,
    grad_query_ref,
    own_ref,
):
    even = (lax.axis_index("tm") & 1) == 0
    frame_len = mine_ref.shape[1]
    for head in range(queries_ref.shape[1] // DEPTH):
        cols = pl.ds(head * DEPTH, DEPTH)
        query, cotangent = joined_parts(queries_ref, cols)
        mine = mine_ref[:, :, cols].reshape(MEM * frame_len, DEPTH)
        got = got_ref[:, :, cols].reshape(MEM * frame_len, DEPTH)
        pieces = (
            prev_parts(outer_ref, pair_ref, cols),
            joined_parts(joined_ref, cols),
            (jnp.where(even, mine, got), jnp.where(even, got, mine)),
        )
        attended = grad_query = 0.0
        for piece, (keys, values) in enumerate(pieces):
            weights, dlogits = probs_of(keys, values, query, cotangent, rows_ref, stats_ref, head, piece)
            attended += dot(values, weights, 0, 0)
            grad_query += dot(keys, dlogits, 0, 0)
            if piece == 1:
                own_ref[0, :, cols] = dot(dlogits, query, 1, 0) * FACTOR + next_ref[0, :, cols]
                own_ref[1, :, cols] = dot(weights, cotangent, 1, 0) + next_ref[1, :, cols]
        attended_ref[:, cols] = attended.T.astype(BF16)
        grad_query_ref[:, cols] = (grad_query * FACTOR).T.astype(BF16)


def sum_kernel(codes_ref, mine_ref, got_ref, keep_ref, send_ref):
    code = code_of(codes_ref, SUM)
    kept = keep_ref.shape[0]
    terms = [ref[m].astype(F32) for ref in (mine_ref, got_ref) for m in range(MEM)]
    for place in range(kept + 1):
        value = sum(
            jnp.where(field(code, place * len(terms) + t, 1) != 0, term, 0.0) for t, term in enumerate(terms)
        )
        if place < kept:
            keep_ref[place] = value
        if place != kept - 1:
            send_ref[min(place, kept - 1)] = value.astype(BF16)


def add_kernel(keep_ref, got_ref, out_ref, send_ref):
    value = keep_ref[...] + got_ref[...].astype(F32)
    out_ref[...] = value
    send_ref[...] = value.astype(BF16)


def owned_kernel(codes_ref, keep_ref, got_ref, mine_ref, pair_ref):
    code = code_of(codes_ref, OWNED)
    for o, out in enumerate((mine_ref, pair_ref)):
        for j in range(FR_DEV):
            owned = field(code, o * FR_DEV + j, PLACE_BITS)
            place = owned >> 1
            named = (owned & 1) != 0

            @pl.when(named)
            def _(out=out, j=j, place=place):
                value = keep_ref[place] + got_ref[place].astype(F32)
                out[j] = value.astype(out.dtype)

            @pl.when(jnp.logical_not(named))
            def _(out=out, j=j):
                out[j] = jnp.zeros(out.shape[1:], out.dtype)


def final_kernel(own_ref, mine_ref, got_ref, grad_key_ref, grad_value_ref):
    even = (lax.axis_index("tm") & 1) == 0
    rows = grad_key_ref.shape
    mine = mine_ref[...].reshape(rows)
    got = got_ref[...].astype(F32).reshape(rows)
    grad_key_ref[...] = (own_ref[0] + jnp.where(even, mine, got)).astype(BF16)
    grad_value_ref[...] = (own_ref[1] + jnp.where(even, got, mine)).astype(BF16)


def body(
    query_states,
    key_states,
    value_states,
    grad_out,
    camera_pose,
    pose_bias,
    memory_index,
    bank_frames,
):
    row_count, width = query_states.shape
    frame_len = row_count // FR_DEV
    heads = pose_bias.shape[0]
    slots = bank_frames.shape[0]
    peers = lax.axis_size("tm")
    bits = [1 << i for i in range(1, peers.bit_length() - 1)]
    turns = list(zip(bits, bits[::-1]))
    piece_flops = 2 * row_count * row_count * width
    bank_frames = bank_frames.reshape(1, slots)
    last_bits = turns[-1]

    def join(kernel, rows, arrays, scratch, name):
        return pl.pallas_call(
            kernel,
            out_shape=shape(BF16, rows, width),
            in_specs=[pl.BlockSpec(memory_space=pltpu.HBM)] * len(arrays),
            out_specs=VMEM,
            scratch_shapes=[*scratch, pltpu.SemaphoreType.DMA((len(arrays),))],
            compiler_params=pltpu.CompilerParams(vmem_limit_bytes=VMEM_LIMIT),
            name=name,
        )(*(pltpu.with_memory_space_constraint(array, pltpu.HBM) for array in arrays))

    joined = join(
        join_kernel,
        2 * row_count + TAIL,
        [memory_index, key_states, value_states],
        [pltpu.VMEM(memory_index.shape, jnp.int32)],
        "join",
    )
    outer = shift(joined, 1, 1, peers)
    pair = swap(joined, 1, 1, peers)
    queries = join(join_queries_kernel, 2 * row_count, [query_states, grad_out], [], "join_queries")
    next_queries = lax.ppermute(queries, "tm", [(i, i - 1) for i in range(1, peers)])

    bias_rows = -(-(3 * FR_DEV + MEM) // 8) * 8
    rows, codes = call(
        functools.partial(plan_kernel, peers, last_bits),
        [shape(F32, heads, bias_rows, row_count), shape(jnp.int32, 8, 128)],
        [pair],
        scalars=[bank_frames, memory_index, camera_pose, pose_bias],
        flops=piece_flops,
        name="plan",
    )
    held = shape(BF16, slots - 1, frame_len, width)
    sums = shape(F32, slots - 1, frame_len, width)
    (mine,) = call(functools.partial(split_kernel, peers), [held], [bank_frames, joined, pair], name="split")
    stats = shape(F32, heads, 8, row_count)
    (part,) = call(stats_kernel, [stats], [rows, queries, outer, pair, joined], flops=HIDING * piece_flops, name="stats")
    even_done = odd_done = 1
    for step, (even_bit, odd_bit) in enumerate(turns):
        got = swap(mine, even_bit, odd_bit, peers)
        if step + 1 < len(turns):
            kernel = functools.partial(step_kernel, peers, even_done, odd_done)
            (mine,) = call(kernel, [held], [bank_frames, mine, got], name="step")
        even_done |= even_bit
        odd_done |= odd_bit
    chosen = shape(BF16, MEM, frame_len, width)
    mem_mine, mem_send = call(pick_kernel, [chosen] * 2, [codes, mine, got], after=[part], name="pick")
    mem_got = swap(mem_send, 1, 1, peers)

    stats_all, mem_same, mem_other = call(
        memory_kernel,
        [stats, chosen, chosen],
        [rows, part, queries, mem_mine, mem_got],
        flops=4 * piece_flops,
        name="memory",
    )
    same_got = swap(mem_other, 1, 1, peers)
    next_stats = lax.ppermute(stats_all, "tm", [(i, i - 1) for i in range(1, peers)])
    keep, send = call(sum_kernel, [sums, held], [codes, mem_same, same_got], name="sum")
    pair_sums = shape(F32, 2, row_count, width)
    (from_next,) = call(
        next_kernel,
        [pair_sums],
        [rows, next_stats, next_queries, joined],
        flops=HIDING * piece_flops,
        name="next",
    )
    attended, grad_query, own = call(
        rest_kernel,
        [shape(BF16, row_count, width)] * 2 + [pair_sums],
        [rows, stats_all, queries, outer, pair, joined, mem_mine, mem_got, from_next],
        flops=HIDING * piece_flops,
        name="rest",
    )
    for step, (even_bit, odd_bit) in enumerate(turns[::-1]):
        got = swap(send, even_bit, odd_bit, peers)
        if step + 1 < len(turns):
            keep, send = call(add_kernel, [sums, held], [keep, got], after=[from_next], name="add")
    owned = shape(F32, FR_DEV, frame_len, width)
    owned_mine, owned_send = call(
        owned_kernel,
        [owned, shape(BF16, FR_DEV, frame_len, width)],
        [codes, keep, got],
        after=[own],
        name="owned",
    )
    owned_got = swap(owned_send, 1, 1, peers)
    grad_key, grad_value = call(
        final_kernel, [shape(BF16, row_count, width)] * 2, [own, owned_mine, owned_got], name="final"
    )
    return (attended, grad_query, grad_key, grad_value)


def solution(mesh):
    rows = P(("traj", "tm"), None)
    in_specs = (rows, rows, rows, rows, P("traj"), P(), rows, P("traj"))
    return jax.shard_map(body, mesh=mesh, in_specs=in_specs, out_specs=(rows,) * 4, check_vma=False)
```

time: 76.6 us -> 67.6 us (0.88)
  starting transfers between devices: 23.5 us -> 18.4 us
  waiting for transfers between devices: 32.1 us -> 30.5 us
  Pallas kernels: 18.9 us -> 17.6 us
  local copies, waits for them, and re-layouts: 1.03 us -> 0.02 us
    ppermute x8, starting transfers between devices: 20.8 us -> 15.1 us  [swap(): lax.ppermute(block, 'tm', [(i, i ^ (odd_bit if i & 1 else even_bit)) for...]
    ppermute x0 -> x2, starting transfers between devices: none -> 2.56 us  [the longest x1 1.28 us: body(): lax.ppermute(queries, 'tm', [(i, i - 1) for i in range(1, peers)])]
    pallas_call x12, Pallas kernels: 17.7 us -> 15.3 us  [call(): pl.pallas_call(run, out_shape=outs, in_specs=[SMEM] * len(scalars) + [VME...]
    ppermute x3 -> x1, starting transfers between devices: 2.69 us -> 0.7 us  [shift(): return lax.ppermute(block, 'tm', pairs)]
    ppermute x8, waiting for transfers between devices: 32.1 us -> 30.5 us  [swap(): lax.ppermute(block, 'tm', [(i, i ^ (odd_bit if i & 1 else even_bit)) for...]
    pallas_call x1 -> x2, Pallas kernels: 1.16 us -> 2.29 us  [join(): pl.pallas_call(kernel, out_shape=shape(BF16, rows, width), in_specs=[pl.B...]
    unnamed x12 -> x8, local copies, waits for them, and re-layouts: 1.03 us -> 0.02 us
  transfers between devices with their start and end apart: 11 -> 11, of which waited for: 7 -> 8; matrix products, arithmetic and copies ran while one was open for 0% -> 0% of each run, Pallas kernels for 15% -> 22%
where the time goes in v4:
time: 67.6 us; the launch traced here: 67.4 us
  waiting for transfers between devices  30.5 us (45%)
  starting transfers between devices  18.4 us (27%)
  Pallas kernels  17.6 us (26%)
  between operations  0.79 us (1%)
    ppermute x8, waiting for transfers between devices, swap(): lax.ppermute(block, 'tm', [(i, i ^ (odd_bit if i & 1 else even_bit)) for...  30.5 us
    pallas_call x12, Pallas kernels, call(): pl.pallas_call(run, out_shape=outs, in_specs=[SMEM] * len(scalars) + [VME...  15.3 us
    ppermute x8, starting transfers between devices, swap(): lax.ppermute(block, 'tm', [(i, i ^ (odd_bit if i & 1 else even_bit)) for...  15.1 us
    pallas_call x2, Pallas kernels, join(): pl.pallas_call(kernel, out_shape=shape(BF16, rows, width), in_specs=[pl.B...  2.29 us
  transfers between devices with their start and end apart: 11, of which 8 were waited for; matrix products, arithmetic and copies ran while one was open for 0% of the time, Pallas kernels for 22%

profile of v4, /device:TPU:0, one launch (start us, length us, event | category | flops | bytes accessed | tf_op | source)
XLA Modules:
  0.0 67.4 jit_solution(2280137185872411057)
XLA Ops:
  0.6 0.0 copy-start.1
  0.6 1.2 %join.1.refs_4_.refs_1_.refs_3_.refs_5_ = bf16[528,768]{1,0:T(8,128)(2,1)S(1)} custom-call(s32[1,2]{1,0:T(1,128)} %refs_1_.1, bf16[256,768]{1,0:T(8,128)(2,1)} %key_ref.1, bf16[256,768]{1,0:T(8,128)(2,1)} %value_ref.1), custom_call_target="tpu_custom_call" | custom-call | tf_op jit(solution)/shard_map/join/pallas_call | solution.py:432
  1.8 0.5 collective-permute-start
  2.3 0.7 %collective-permute-start.1 = (bf16[528,768]{1,0:T(8,128)(2,1)S(1)}, bf16[528,768]{1,0:T(8,128)(2,1)S(1)}, u32[]{:S(2)}, u32[]{:S(2)}) collective-permute-start(bf16[528,768]{1,0:T(8,128)(2,1)S(1)} %join.1.refs_4_.refs_1_.refs_3_.refs_5_), channel_id=1, source_target_pairs={{1,2},{3,4},{5,6},{9,10},{11,12},{13,14},{17,18},{19,20},{21,22},{... | collective-permute-start | bytes 2433032 | tf_op jit(solution)/shard_map/ppermute | solution.py:55
  3.0 1.2 %collective-permute-done.refs_4_.refs_3_.refs_2_ = bf16[528,768]{1,0:T(8,128)(2,1)S(1)} collective-permute-done((bf16[528,768]{1,0:T(8,128)(2,1)S(1)}, bf16[528,768]{1,0:T(8,128)(2,1)S(1)}, u32[]{:S(2)}, u32[]{:S(2)}) %collective-permute-start) | collective-permute-done | bytes 811040 | tf_op jit(solution)/shard_map/ppermute | solution.py:50
  4.3 0.0 copy-done.1
  4.3 0.0 copy-start
  4.3 0.0 copy-start.2
  4.3 0.0 copy-start.3
  4.3 0.3 split.1.refs_1_
  4.6 2.9 %collective-permute-start.2 = (bf16[3,128,768]{2,1,0:T(8,128)(2,1)S(1)}, bf16[3,128,768]{2,1,0:T(8,128)(2,1)S(1)}, u32[]{:S(2)}, u32[]{:S(2)}) collective-permute-start(bf16[3,128,768]{2,1,0:T(8,128)(2,1)S(1)} %split.1.refs_1_), channel_id=1, source_target_pairs={{0,2},{1,5},{2,0},{3,7},{4,6},{5,1},{6,4},{7,3},{8,10},{9,13},{10,... | collective-permute-start | bytes 1769480 | tf_op jit(solution)/shard_map/ppermute | solution.py:50
  7.5 1.1 %join_queries.1.refs_1_.refs_2_ = bf16[512,768]{1,0:T(8,128)(2,1)S(1)} custom-call(bf16[256,768]{1,0:T(8,128)(2,1)} %query_ref.1, bf16[256,768]{1,0:T(8,128)(2,1)} %cotangent_ref.1), custom_call_target="tpu_custom_call" | custom-call | tf_op jit(solution)/shard_map/join_queries/pallas_call | solution.py:432
  8.6 0.0 copy-done
  8.7 0.0 copy-done.2
  8.7 0.0 copy-done.3
  8.7 1.7 %plan.1 = (f32[6,8,256]{2,1,0:T(8,128)S(1)}, s32[8,128]{1,0:T(8,128)S(1)}) custom-call(s32[1,4]{1,0:T(1,128)S(1)} %bitcast.2, s32[1,2]{1,0:T(1,128)S(1)} %copy-done.2, s32[16]{0:T(128)S(1)} %copy-done.3, f32[6,16,16]{2,1,0:T(8,128)S(1)} %copy-done, bf16[528,768]{1,0:T(8,128)(2,1)S(1)} %collective-permute-done.refs_4_.refs_3_.refs_2_), custom_call_target="tpu_custom_call" | custom-call | flops 100663296 | tf_op jit(solution)/shard_map/plan/pallas_call | solution.py:38
  10.3 11.2 %collective-permute-done.2.refs_2_ = bf16[3,128,768]{2,1,0:T(8,128)(2,1)S(1)} collective-permute-done((bf16[3,128,768]{2,1,0:T(8,128)(2,1)S(1)}, bf16[3,128,768]{2,1,0:T(8,128)(2,1)S(1)}, u32[]{:S(2)}, u32[]{:S(2)}) %collective-permute-start.2) | collective-permute-done | bytes 589856 | tf_op jit(solution)/shard_map/ppermute | solution.py:50
  21.6 0.3 step.1.refs_1_
  21.9 1.3 %collective-permute-start.3 = (bf16[3,128,768]{2,1,0:T(8,128)(2,1)S(1)}, bf16[3,128,768]{2,1,0:T(8,128)(2,1)S(1)}, u32[]{:S(2)}, u32[]{:S(2)}) collective-permute-start(bf16[3,128,768]{2,1,0:T(8,128)(2,1)S(1)} %step.1.refs_1_), channel_id=1, source_target_pairs={{0,4},{1,3},{2,6},{3,1},{4,0},{5,7},{6,2},{7,5},{8,12},{9,11},{10,... | collective-permute-start | bytes 1769480 | tf_op jit(solution)/shard_map/ppermute | solution.py:50
  23.1 0.0 collective-permute-done.1.refs_2_.refs_3_
  23.2 1.3 %stats.1.refs_3_.refs_1_ = f32[6,8,256]{2,1,0:T(8,128)S(1)} custom-call(f32[6,8,256]{2,1,0:T(8,128)S(1)} %get-tuple-element.22.refs_0_, bf16[512,768]{1,0:T(8,128)(2,1)S(1)} %join_queries.1.refs_1_.refs_2_, bf16[528,768]{1,0:T(8,128)(2,1)S(1)} %collective-permute-done.1.refs_2_.refs_3_, bf16[528,768]{1,0:T(8,128)(2,1)S(1)} %collective-permute-done.refs_4_.refs_3_.refs_2_, ...), custom_call_target="tpu_custom_call" | custom-call | flops 20132659200 | tf_op jit(solution)/shard_map/stats/pallas_call | solution.py:38
  24.5 7.3 %collective-permute-done.3.refs_2_ = bf16[3,128,768]{2,1,0:T(8,128)(2,1)S(1)} collective-permute-done((bf16[3,128,768]{2,1,0:T(8,128)(2,1)S(1)}, bf16[3,128,768]{2,1,0:T(8,128)(2,1)S(1)}, u32[]{:S(2)}, u32[]{:S(2)}) %collective-permute-start.3) | collective-permute-done | bytes 589856 | tf_op jit(solution)/shard_map/ppermute | solution.py:50
  31.8 0.3 pick.1
  32.1 1.0 %collective-permute-start.4 = (bf16[2,128,768]{2,1,0:T(8,128)(2,1)S(1)}, bf16[2,128,768]{2,1,0:T(8,128)(2,1)S(1)}, u32[]{:S(2)}, u32[]{:S(2)}) collective-permute-start(bf16[2,128,768]{2,1,0:T(8,128)(2,1)S(1)} %get-tuple-element.25), channel_id=1, source_target_pairs={{0,1},{1,0},{2,3},{3,2},{4,5},{5,4},{6,7},{7,6},{8,9},{9,8},{10,11... | collective-permute-start | bytes 1179656 | tf_op jit(solution)/shard_map/ppermute | solution.py:50
  33.1 1.3 %collective-permute-start.6 = (bf16[512,768]{1,0:T(8,128)(2,1)S(1)}, bf16[512,768]{1,0:T(8,128)(2,1)S(1)}, u32[]{:S(2)}, u32[]{:S(2)}) collective-permute-start(bf16[512,768]{1,0:T(8,128)(2,1)S(1)} %join_queries.1.refs_1_.refs_2_), channel_id=1, source_target_pairs={{1,0},{2,1},{3,2},{4,3},{5,4},{6,5},{7,6},{9,8},{10,9},{11,10},{12... | collective-permute-start | bytes 2359304 | tf_op jit(solution)/shard_map/ppermute | solution.py:452
  34.4 0.1 collective-permute-done.4.refs_4_.refs_7_
  34.5 2.4 %memory.1 = (f32[6,8,256]{2,1,0:T(8,128)S(1)}, bf16[2,128,768]{2,1,0:T(8,128)(2,1)S(1)}, bf16[2,128,768]{2,1,0:T(8,128)(2,1)S(1)}) custom-call(f32[6,8,256]{2,1,0:T(8,128)S(1)} %get-tuple-element.22.refs_0_, f32[6,8,256]{2,1,0:T(8,128)S(1)} %stats.1.refs_3_.refs_1_, bf16[512,768]{1,0:T(8,128)(2,1)S(1)} %join_queries.1.refs_1_.refs_2_, ...), custom_call_target="tpu_custom_call" | custom-call | flops 402653184 | tf_op jit(solution)/shard_map/memory/pallas_call | solution.py:38
  36.9 1.2 %collective-permute-start.7 = (bf16[2,128,768]{2,1,0:T(8,128)(2,1)S(1)}, bf16[2,128,768]{2,1,0:T(8,128)(2,1)S(1)}, u32[]{:S(2)}, u32[]{:S(2)}) collective-permute-start(bf16[2,128,768]{2,1,0:T(8,128)(2,1)S(1)} %get-tuple-element.31), channel_id=1, source_target_pairs={{0,1},{1,0},{2,3},{3,2},{4,5},{5,4},{6,7},{7,6},{8,9},{9,8},{10,11... | collective-permute-start | bytes 1179656 | tf_op jit(solution)/shard_map/ppermute | solution.py:50
  38.0 1.3 %collective-permute-start.5 = (f32[6,8,256]{2,1,0:T(8,128)S(1)}, f32[6,8,256]{2,1,0:T(8,128)S(1)}, u32[]{:S(2)}, u32[]{:S(2)}) collective-permute-start(f32[6,8,256]{2,1,0:T(8,128)S(1)} %get-tuple-element.26.refs_1_), channel_id=1, source_target_pairs={{1,0},{2,1},{3,2},{4,3},{5,4},{6,5},{7,6},{9,8},{10,9},{11,10},{12... | collective-permute-start | bytes 147464 | tf_op jit(solution)/shard_map/ppermute | solution.py:488
  39.3 0.1 collective-permute-done.7.refs_2_
  39.4 0.8 %sum.1 = (f32[3,128,768]{2,1,0:T(8,128)S(1)}, bf16[3,128,768]{2,1,0:T(8,128)(2,1)S(1)}) custom-call(s32[8,128]{1,0:T(8,128)S(1)} %get-tuple-element.23.refs_0_, bf16[2,128,768]{2,1,0:T(8,128)(2,1)S(1)} %get-tuple-element.30.refs_1_, bf16[2,128,768]{2,1,0:T(8,128)(2,1)S(1)} %collective-permute-done.7.refs_2_), custom_call_target="tpu_custom_call" | custom-call | tf_op jit(solution)/shard_map/sum/pallas_call | solution.py:38
  40.2 3.3 %collective-permute-start.8 = (bf16[3,128,768]{2,1,0:T(8,128)(2,1)S(1)}, bf16[3,128,768]{2,1,0:T(8,128)(2,1)S(1)}, u32[]{:S(2)}, u32[]{:S(2)}) collective-permute-start(bf16[3,128,768]{2,1,0:T(8,128)(2,1)S(1)} %get-tuple-element.33), channel_id=1, source_target_pairs={{0,4},{1,3},{2,6},{3,1},{4,0},{5,7},{6,2},{7,5},{8,12},{9,11},{10,... | collective-permute-start | bytes 1769480 | tf_op jit(solution)/shard_map/ppermute | solution.py:50
  43.5 0.0 collective-permute-done.6.refs_2_
  43.5 0.0 collective-permute-done.5.refs_1_
  43.5 1.5 %next.1.refs_8_.refs_2_ = f32[2,256,768]{2,1,0:T(8,128)S(1)} custom-call(f32[6,8,256]{2,1,0:T(8,128)S(1)} %get-tuple-element.22.refs_0_, f32[6,8,256]{2,1,0:T(8,128)S(1)} %collective-permute-done.5.refs_1_, bf16[512,768]{1,0:T(8,128)(2,1)S(1)} %collective-permute-done.6.refs_2_, bf16[528,768]{1,0:T(8,128)(2,1)S(1)} %join.1.refs_4_.refs_1_.refs_3_.refs_5_), custom_call_target="tpu_custom_call" | custom-call | flops 20132659200 | tf_op jit(solution)/shard_map/next/pallas_call | solution.py:38
  45.0 6.3 %collective-permute-done.8.refs_1_ = bf16[3,128,768]{2,1,0:T(8,128)(2,1)S(1)} collective-permute-done((bf16[3,128,768]{2,1,0:T(8,128)(2,1)S(1)}, bf16[3,128,768]{2,1,0:T(8,128)(2,1)S(1)}, u32[]{:S(2)}, u32[]{:S(2)}) %collective-permute-start.8) | collective-permute-done | bytes 589856 | tf_op jit(solution)/shard_map/ppermute | solution.py:50
  51.4 0.2 add.1
  51.5 4.8 %collective-permute-start.9 = (bf16[3,128,768]{2,1,0:T(8,128)(2,1)S(1)}, bf16[3,128,768]{2,1,0:T(8,128)(2,1)S(1)}, u32[]{:S(2)}, u32[]{:S(2)}) collective-permute-start(bf16[3,128,768]{2,1,0:T(8,128)(2,1)S(1)} %get-tuple-element.35), channel_id=1, source_target_pairs={{0,2},{1,5},{2,0},{3,7},{4,6},{5,1},{6,4},{7,3},{8,10},{9,13},{10,... | collective-permute-start | bytes 1769480 | tf_op jit(solution)/shard_map/ppermute | solution.py:50
  56.3 5.3 %rest.1 = (bf16[256,768]{1,0:T(8,128)(2,1)}, bf16[256,768]{1,0:T(8,128)(2,1)}, f32[2,256,768]{2,1,0:T(8,128)S(1)}) custom-call(f32[6,8,256]{2,1,0:T(8,128)S(1)} %get-tuple-element.22.refs_0_, f32[6,8,256]{2,1,0:T(8,128)S(1)} %get-tuple-element.26.refs_1_, bf16[512,768]{1,0:T(8,128)(2,1)S(1)} %join_queries.1.refs_1_.refs_2_, ...), custom_call_target="tpu_custom_call" | custom-call | flops 20132659200 | tf_op jit(solution)/shard_map/rest/pallas_call | solution.py:38
  61.6 2.6 %collective-permute-done.9.refs_2_ = bf16[3,128,768]{2,1,0:T(8,128)(2,1)S(1)} collective-permute-done((bf16[3,128,768]{2,1,0:T(8,128)(2,1)S(1)}, bf16[3,128,768]{2,1,0:T(8,128)(2,1)S(1)}, u32[]{:S(2)}, u32[]{:S(2)}) %collective-permute-start.9) | collective-permute-done | bytes 589856 | tf_op jit(solution)/shard_map/ppermute | solution.py:50
  64.2 0.3 owned.1
  64.5 0.1 collective-permute-start.10
  64.6 1.7 %collective-permute-done.10.refs_2_ = bf16[2,128,768]{2,1,0:T(8,128)(2,1)S(1)} collective-permute-done((bf16[2,128,768]{2,1,0:T(8,128)(2,1)S(1)}, bf16[2,128,768]{2,1,0:T(8,128)(2,1)S(1)}, u32[]{:S(2)}, u32[]{:S(2)}) %collective-permute-start.10) | collective-permute-done | bytes 393248 | tf_op jit(solution)/shard_map/ppermute | solution.py:50
  66.3 1.1 %final.1 = (bf16[256,768]{1,0:T(8,128)(2,1)}, bf16[256,768]{1,0:T(8,128)(2,1)}) custom-call(f32[2,256,768]{2,1,0:T(8,128)S(1)} %get-tuple-element.29.refs_3_.refs_0_, f32[2,128,768]{2,1,0:T(8,128)S(1)} %get-tuple-element.36.refs_1_, bf16[2,128,768]{2,1,0:T(8,128)(2,1)S(1)} %collective-permute-done.10.refs_2_), custom_call_target="tpu_custom_call" | custom-call | tf_op jit(solution)/shard_map/final/pallas_call | solution.py:38
Async XLA Ops:
  0.6 3.6 %copy-start.1 = (s32[4]{0:T(128)S(1)}, s32[4]{0:T(128)}, u32[]{:S(2)}) copy-start(s32[4]{0:T(128)} %param.15) | copy-start | bytes 52
  1.8 2.5 %collective-permute-start = (bf16[528,768]{1,0:T(8,128)(2,1)S(1)}, bf16[528,768]{1,0:T(8,128)(2,1)S(1)}, u32[]{:S(2)}, u32[]{:S(2)}) collective-permute-start(bf16[528,768]{1,0:T(8,128)(2,1)S(1)} %join.1.refs_4_.refs_1_.refs_3_.refs_5_), channel_id=1, source_target_pairs={{0,1},{1,0},{2,3},{3,2},{4,5},{5,4},{6,7},{7,6},{8,9},{9,8},{10,11... | collective-permute-start | bytes 2433032 | tf_op jit(solution)/shard_map/ppermute | solution.py:50
  2.3 20.8 %collective-permute-start.1 = (bf16[528,768]{1,0:T(8,128)(2,1)S(1)}, bf16[528,768]{1,0:T(8,128)(2,1)S(1)}, u32[]{:S(2)}, u32[]{:S(2)}) collective-permute-start(bf16[528,768]{1,0:T(8,128)(2,1)S(1)} %join.1.refs_4_.refs_1_.refs_3_.refs_5_), channel_id=1, source_target_pairs={{1,2},{3,4},{5,6},{9,10},{11,12},{13,14},{17,18},{19,20},{21,22},{... | collective-permute-start | bytes 2433032 | tf_op jit(solution)/shard_map/ppermute | solution.py:55
  4.3 4.4 %copy-start = (f32[6,16,16]{2,1,0:T(8,128)S(1)}, f32[6,16,16]{2,1,0:T(8,128)}, u32[]{:S(2)}) copy-start(f32[6,16,16]{2,1,0:T(8,128)} %refs_3_.1) | copy-start | bytes 18436
  4.3 4.4 %copy-start.2 = (s32[1,2]{1,0:T(1,128)S(1)}, s32[1,2]{1,0:T(1,128)}, u32[]{:S(2)}) copy-start(s32[1,2]{1,0:T(1,128)} %refs_1_.1) | copy-start | bytes 28
  4.3 4.4 %copy-start.3 = (s32[16]{0:T(128)S(1)}, s32[16]{0:T(128)}, u32[]{:S(2)}) copy-start(s32[16]{0:T(128)} %refs_2_.1) | copy-start | bytes 196
  4.6 17.0 %collective-permute-start.2 = (bf16[3,128,768]{2,1,0:T(8,128)(2,1)S(1)}, bf16[3,128,768]{2,1,0:T(8,128)(2,1)S(1)}, u32[]{:S(2)}, u32[]{:S(2)}) collective-permute-start(bf16[3,128,768]{2,1,0:T(8,128)(2,1)S(1)} %split.1.refs_1_), channel_id=1, source_target_pairs={{0,2},{1,5},{2,0},{3,7},{4,6},{5,1},{6,4},{7,3},{8,10},{9,13},{10,... | collective-permute-start | bytes 1769480 | tf_op jit(solution)/shard_map/ppermute | solution.py:50
  21.9 9.9 %collective-permute-start.3 = (bf16[3,128,768]{2,1,0:T(8,128)(2,1)S(1)}, bf16[3,128,768]{2,1,0:T(8,128)(2,1)S(1)}, u32[]{:S(2)}, u32[]{:S(2)}) collective-permute-start(bf16[3,128,768]{2,1,0:T(8,128)(2,1)S(1)} %step.1.refs_1_), channel_id=1, source_target_pairs={{0,4},{1,3},{2,6},{3,1},{4,0},{5,7},{6,2},{7,5},{8,12},{9,11},{10,... | collective-permute-start | bytes 1769480 | tf_op jit(solution)/shard_map/ppermute | solution.py:50
  32.1 2.4 %collective-permute-start.4 = (bf16[2,128,768]{2,1,0:T(8,128)(2,1)S(1)}, bf16[2,128,768]{2,1,0:T(8,128)(2,1)S(1)}, u32[]{:S(2)}, u32[]{:S(2)}) collective-permute-start(bf16[2,128,768]{2,1,0:T(8,128)(2,1)S(1)} %get-tuple-element.25), channel_id=1, source_target_pairs={{0,1},{1,0},{2,3},{3,2},{4,5},{5,4},{6,7},{7,6},{8,9},{9,8},{10,11... | collective-permute-start | bytes 1179656 | tf_op jit(solution)/shard_map/ppermute | solution.py:50
  33.1 10.4 %collective-permute-start.6 = (bf16[512,768]{1,0:T(8,128)(2,1)S(1)}, bf16[512,768]{1,0:T(8,128)(2,1)S(1)}, u32[]{:S(2)}, u32[]{:S(2)}) collective-permute-start(bf16[512,768]{1,0:T(8,128)(2,1)S(1)} %join_queries.1.refs_1_.refs_2_), channel_id=1, source_target_pairs={{1,0},{2,1},{3,2},{4,3},{5,4},{6,5},{7,6},{9,8},{10,9},{11,10},{12... | collective-permute-start | bytes 2359304 | tf_op jit(solution)/shard_map/ppermute | solution.py:452
  36.9 2.5 %collective-permute-start.7 = (bf16[2,128,768]{2,1,0:T(8,128)(2,1)S(1)}, bf16[2,128,768]{2,1,0:T(8,128)(2,1)S(1)}, u32[]{:S(2)}, u32[]{:S(2)}) collective-permute-start(bf16[2,128,768]{2,1,0:T(8,128)(2,1)S(1)} %get-tuple-element.31), channel_id=1, source_target_pairs={{0,1},{1,0},{2,3},{3,2},{4,5},{5,4},{6,7},{7,6},{8,9},{9,8},{10,11... | collective-permute-start | bytes 1179656 | tf_op jit(solution)/shard_map/ppermute | solution.py:50
  38.0 5.5 %collective-permute-start.5 = (f32[6,8,256]{2,1,0:T(8,128)S(1)}, f32[6,8,256]{2,1,0:T(8,128)S(1)}, u32[]{:S(2)}, u32[]{:S(2)}) collective-permute-start(f32[6,8,256]{2,1,0:T(8,128)S(1)} %get-tuple-element.26.refs_1_), channel_id=1, source_target_pairs={{1,0},{2,1},{3,2},{4,3},{5,4},{6,5},{7,6},{9,8},{10,9},{11,10},{12... | collective-permute-start | bytes 147464 | tf_op jit(solution)/shard_map/ppermute | solution.py:488
  40.2 11.2 %collective-permute-start.8 = (bf16[3,128,768]{2,1,0:T(8,128)(2,1)S(1)}, bf16[3,128,768]{2,1,0:T(8,128)(2,1)S(1)}, u32[]{:S(2)}, u32[]{:S(2)}) collective-permute-start(bf16[3,128,768]{2,1,0:T(8,128)(2,1)S(1)} %get-tuple-element.33), channel_id=1, source_target_pairs={{0,4},{1,3},{2,6},{3,1},{4,0},{5,7},{6,2},{7,5},{8,12},{9,11},{10,... | collective-permute-start | bytes 1769480 | tf_op jit(solution)/shard_map/ppermute | solution.py:50
  51.5 12.7 %collective-permute-start.9 = (bf16[3,128,768]{2,1,0:T(8,128)(2,1)S(1)}, bf16[3,128,768]{2,1,0:T(8,128)(2,1)S(1)}, u32[]{:S(2)}, u32[]{:S(2)}) collective-permute-start(bf16[3,128,768]{2,1,0:T(8,128)(2,1)S(1)} %get-tuple-element.35), channel_id=1, source_target_pairs={{0,2},{1,5},{2,0},{3,7},{4,6},{5,1},{6,4},{7,3},{8,10},{9,13},{10,... | collective-permute-start | bytes 1769480 | tf_op jit(solution)/shard_map/ppermute | solution.py:50
  64.5 1.8 %collective-permute-start.10 = (bf16[2,128,768]{2,1,0:T(8,128)(2,1)S(1)}, bf16[2,128,768]{2,1,0:T(8,128)(2,1)S(1)}, u32[]{:S(2)}, u32[]{:S(2)}) collective-permute-start(bf16[2,128,768]{2,1,0:T(8,128)(2,1)S(1)} %get-tuple-element.37), channel_id=1, source_target_pairs={{0,1},{1,0},{2,3},{3,2},{4,5},{5,4},{6,7},{7,6},{8,9},{9,8},{10,11... | collective-permute-start | bytes 1179656 | tf_op jit(solution)/shard_map/ppermute | solution.py:50

commit v5 on v4

--- a/solution.py
+++ b/solution.py
@@ -256,17 +256,17 @@
     return joined_ref[0:rows, cols], joined_ref[rows : 2 * rows, cols]
 
 
-def prev_parts(outer_ref, pair_ref, cols):
+def prev_parts(outer_refs, pair_ref, cols):
     even = (lax.axis_index("tm") & 1) == 0
-    parts = zip(joined_parts(outer_ref, cols), joined_parts(pair_ref, cols))
-    return tuple(jnp.where(even, outer, pair) for outer, pair in parts)
-
-
-def stats_kernel(rows_ref, queries_ref, outer_ref, pair_ref, own_ref, stats_ref):
+    parts = zip(outer_refs, joined_parts(pair_ref, cols))
+    return tuple(jnp.where(even, outer[:, cols], pair) for outer, pair in parts)
+
+
+def stats_kernel(rows_ref, queries_ref, outer_key_ref, outer_value_ref, pair_ref, own_ref, stats_ref):
     for head in range(queries_ref.shape[1] // DEPTH):
         cols = pl.ds(head * DEPTH, DEPTH)
         query, cotangent = joined_parts(queries_ref, cols)
-        pieces = [prev_parts(outer_ref, pair_ref, cols), joined_parts(own_ref, cols)]
+        pieces = [prev_parts((outer_key_ref, outer_value_ref), pair_ref, cols), joined_parts(own_ref, cols)]
         logits = [logits_of(keys, query, rows_ref, head, piece) for piece, (keys, _) in enumerate(pieces)]
         peak = functools.reduce(jnp.maximum, [jnp.max(block, axis=0, keepdims=True) for block in logits])
         exps = [jnp.exp2(block - peak) for block in logits]
@@ -279,17 +279,20 @@
 def memory_kernel(rows_ref, part_ref, queries_ref, mine_ref, got_ref, stats_ref, mem_same_ref, mem_other_ref):
     even = (lax.axis_index("tm") & 1) == 0
     frame_len = mine_ref.shape[1]
-    for head in range(queries_ref.shape[1] // DEPTH):
+    heads = queries_ref.shape[1] // DEPTH
+
+    def products(head):
         cols = pl.ds(head * DEPTH, DEPTH)
         query, cotangent = joined_parts(queries_ref, cols)
         mine = mine_ref[:, :, cols].reshape(MEM * frame_len, DEPTH)
         got = got_ref[:, :, cols].reshape(MEM * frame_len, DEPTH)
         keys, values = jnp.where(even, mine, got), jnp.where(even, got, mine)
-        logits = logits_of(keys, query, rows_ref, head, 2)
+        return logits_of(keys, query, rows_ref, head, 2), dot(values, cotangent, 1, 1)
+
+    def rounded(head, logits, slopes):
         part_peak = part_ref[head, 0:1, :]
         peak = jnp.maximum(part_peak, jnp.max(logits, axis=0, keepdims=True))
         exps = jnp.exp2(logits - peak)
-        slopes = dot(values, cotangent, 1, 1)
         scale = jnp.exp2(part_peak - peak)
         total = part_ref[head, 1:2, :] * scale + jnp.sum(exps, axis=0, keepdims=True)
         inverse = 1.0 / total
@@ -298,11 +301,26 @@
         stats_ref[head, 1:2, :] = inverse
         stats_ref[head, 2:3, :] = spread
         probs = exps * inverse
-        dlogits = (probs * (slopes - spread)).astype(BF16)
+        return probs.astype(BF16), (probs * (slopes - spread)).astype(BF16)
+
+    def store(head, weights, dlogits):
+        cols = pl.ds(head * DEPTH, DEPTH)
+        query, cotangent = joined_parts(queries_ref, cols)
         key_part = (dot(dlogits, query, 1, 0) * FACTOR).astype(BF16).reshape(MEM, frame_len, DEPTH)
-        value_part = dot(probs.astype(BF16), cotangent, 1, 0).astype(BF16).reshape(MEM, frame_len, DEPTH)
+        value_part = dot(weights, cotangent, 1, 0).astype(BF16).reshape(MEM, frame_len, DEPTH)
         mem_same_ref[:, :, cols] = jnp.where(even, key_part, value_part)
         mem_other_ref[:, :, cols] = jnp.where(even, value_part, key_part)
+
+    ahead = products(0)
+    behind = None
+    for head in range(heads):
+        now = ahead
+        if head + 1 < heads:
+            ahead = products(head + 1)
+        if behind is not None:
+            store(head - 1, *behind)
+        behind = rounded(head, *now)
+    store(heads - 1, *behind)
 
 
 def probs_of(keys, values, query, cotangent, rows_ref, stats_ref, head, piece):
@@ -312,39 +330,41 @@
     return probs.astype(BF16), dlogits.astype(BF16)
 
 
-def next_kernel(rows_ref, stats_ref, queries_ref, own_ref, next_ref):
+def next_kernel(rows_ref, stats_ref, queries_ref, own_ref, term_ref, sum_ref):
     for head in range(queries_ref.shape[1] // DEPTH):
         cols = pl.ds(head * DEPTH, DEPTH)
         query, cotangent = joined_parts(queries_ref, cols)
         keys, values = joined_parts(own_ref, cols)
         weights, dlogits = probs_of(keys, values, query, cotangent, rows_ref, stats_ref, head, 3)
-        next_ref[0, :, cols] = dot(dlogits, query, 1, 0) * FACTOR
-        next_ref[1, :, cols] = dot(weights, cotangent, 1, 0)
+        sum_ref[0, :, cols] = term_ref[0, :, cols] + dot(dlogits, query, 1, 0) * FACTOR
+        sum_ref[1, :, cols] = term_ref[1, :, cols] + dot(weights, cotangent, 1, 0)
 
 
 def rest_kernel(
     rows_ref,
     stats_ref,
     queries_ref,
-    outer_ref,
+    outer_key_ref,
+    outer_value_ref,
     pair_ref,
     joined_ref,
     mine_ref,
     got_ref,
-    next_ref,
     attended_ref,
     grad_query_ref,
     own_ref,
+    stats_out_ref,
 ):
     even = (lax.axis_index("tm") & 1) == 0
     frame_len = mine_ref.shape[1]
+    stats_out_ref[...] = stats_ref[...]
     for head in range(queries_ref.shape[1] // DEPTH):
         cols = pl.ds(head * DEPTH, DEPTH)
         query, cotangent = joined_parts(queries_ref, cols)
         mine = mine_ref[:, :, cols].reshape(MEM * frame_len, DEPTH)
         got = got_ref[:, :, cols].reshape(MEM * frame_len, DEPTH)
         pieces = (
-            prev_parts(outer_ref, pair_ref, cols),
+            prev_parts((outer_key_ref, outer_value_ref), pair_ref, cols),
             joined_parts(joined_ref, cols),
             (jnp.where(even, mine, got), jnp.where(even, got, mine)),
         )
@@ -354,8 +374,8 @@
             attended += dot(values, weights, 0, 0)
             grad_query += dot(keys, dlogits, 0, 0)
             if piece == 1:
-                own_ref[0, :, cols] = dot(dlogits, query, 1, 0) * FACTOR + next_ref[0, :, cols]
-                own_ref[1, :, cols] = dot(weights, cotangent, 1, 0) + next_ref[1, :, cols]
+                own_ref[0, :, cols] = dot(dlogits, query, 1, 0) * FACTOR
+                own_ref[1, :, cols] = dot(weights, cotangent, 1, 0)
         attended_ref[:, cols] = attended.T.astype(BF16)
         grad_query_ref[:, cols] = (grad_query * FACTOR).T.astype(BF16)
 
@@ -378,6 +398,10 @@
     value = keep_ref[...] + got_ref[...].astype(F32)
     out_ref[...] = value
     send_ref[...] = value.astype(BF16)
+
+
+def mark_kernel(mark_ref):
+    mark_ref[...] = jnp.zeros(mark_ref.shape, F32)
 
 
 def owned_kernel(codes_ref, keep_ref, got_ref, mine_ref, pair_ref):
@@ -446,7 +470,8 @@
         [pltpu.VMEM(memory_index.shape, jnp.int32)],
         "join",
     )
-    outer = shift(joined, 1, 1, peers)
+    outer_keys = shift(key_states, 1, 1, peers)
+    outer_values = shift(value_states, 1, 1, peers)
     pair = swap(joined, 1, 1, peers)
     queries = join(join_queries_kernel, 2 * row_count, [query_states, grad_out], [], "join_queries")
     next_queries = lax.ppermute(queries, "tm", [(i, i - 1) for i in range(1, peers)])
@@ -457,20 +482,21 @@
         [shape(F32, heads, bias_rows, row_count), shape(jnp.int32, 8, 128)],
         [pair],
         scalars=[bank_frames, memory_index, camera_pose, pose_bias],
-        flops=piece_flops,
+        after=[outer_keys],
+        flops=HIDING * piece_flops,
         name="plan",
     )
     held = shape(BF16, slots - 1, frame_len, width)
     sums = shape(F32, slots - 1, frame_len, width)
     (mine,) = call(functools.partial(split_kernel, peers), [held], [bank_frames, joined, pair], name="split")
     stats = shape(F32, heads, 8, row_count)
-    (part,) = call(stats_kernel, [stats], [rows, queries, outer, pair, joined], flops=HIDING * piece_flops, name="stats")
+    (part,) = call(stats_kernel, [stats], [rows, queries, outer_keys, outer_values, pair, joined], name="stats")
     even_done = odd_done = 1
     for step, (even_bit, odd_bit) in enumerate(turns):
         got = swap(mine, even_bit, odd_bit, peers)
         if step + 1 < len(turns):
             kernel = functools.partial(step_kernel, peers, even_done, odd_done)
-            (mine,) = call(kernel, [held], [bank_frames, mine, got], name="step")
+            (mine,) = call(kernel, [held], [bank_frames, mine, got], after=[codes], name="step")
         even_done |= even_bit
         odd_done |= odd_bit
     chosen = shape(BF16, MEM, frame_len, width)
@@ -481,31 +507,39 @@
         memory_kernel,
         [stats, chosen, chosen],
         [rows, part, queries, mem_mine, mem_got],
-        flops=4 * piece_flops,
+        flops=HIDING * piece_flops,
         name="memory",
     )
     same_got = swap(mem_other, 1, 1, peers)
-    next_stats = lax.ppermute(stats_all, "tm", [(i, i - 1) for i in range(1, peers)])
     keep, send = call(sum_kernel, [sums, held], [codes, mem_same, same_got], name="sum")
     pair_sums = shape(F32, 2, row_count, width)
-    (from_next,) = call(
+    attended, grad_query, own_terms, stats_sent = call(
+        rest_kernel,
+        [shape(BF16, row_count, width)] * 2 + [pair_sums, stats],
+        [rows, stats_all, queries, outer_keys, outer_values, pair, joined, mem_mine, mem_got],
+        after=[send],
+        name="rest",
+    )
+    next_stats = lax.ppermute(stats_sent, "tm", [(i, i - 1) for i in range(1, peers)])
+    (arrived,) = call(
+        mark_kernel,
+        [shape(F32, 8, 128)],
+        [],
+        after=[own_terms, next_queries],
+        flops=HIDING * piece_flops,
+        name="arrived",
+    )
+    (own,) = call(
         next_kernel,
         [pair_sums],
-        [rows, next_stats, next_queries, joined],
+        [rows, next_stats, next_queries, joined, own_terms],
         flops=HIDING * piece_flops,
         name="next",
-    )
-    attended, grad_query, own = call(
-        rest_kernel,
-        [shape(BF16, row_count, width)] * 2 + [pair_sums],
-        [rows, stats_all, queries, outer, pair, joined, mem_mine, mem_got, from_next],
-        flops=HIDING * piece_flops,
-        name="rest",
     )
     for step, (even_bit, odd_bit) in enumerate(turns[::-1]):
         got = swap(send, even_bit, odd_bit, peers)
         if step + 1 < len(turns):
-            keep, send = call(add_kernel, [sums, held], [keep, got], after=[from_next], name="add")
+            keep, send = call(add_kernel, [sums, held], [keep, got], after=[arrived], name="add")
     owned = shape(F32, FR_DEV, frame_len, width)
     owned_mine, owned_send = call(
         owned_kernel,

time: 67.6 us -> 67.8 us (level)
  Pallas kernels: 17.6 us -> 16.7 us
  waiting for transfers between devices: 30.5 us -> 31.3 us
    pallas_call x12 -> x13, Pallas kernels: 15.3 us -> 14.4 us  [call(): pl.pallas_call(run, out_shape=outs, in_specs=[SMEM] * len(scalars) + [VME...]
    ppermute x8, waiting for transfers between devices: 30.5 us -> 31.3 us  [swap(): lax.ppermute(block, 'tm', [(i, i ^ (odd_bit if i & 1 else even_bit)) for...]
  transfers between devices with their start and end apart: 11 -> 12, of which waited for: 8 -> 8; matrix products, arithmetic and copies ran while one was open for 0% -> 0% of each run, Pallas kernels for 22% -> 20%
where the time goes in v5:
time: 67.8 us; the launch traced here: 67.6 us
  waiting for transfers between devices  31.3 us (46%)
  starting transfers between devices  18.7 us (28%)
  Pallas kernels  16.7 us (25%)
  between operations  0.86 us (1%)
    ppermute x8, waiting for transfers between devices, swap(): lax.ppermute(block, 'tm', [(i, i ^ (odd_bit if i & 1 else even_bit)) for...  31.3 us
    ppermute x8, starting transfers between devices, swap(): lax.ppermute(block, 'tm', [(i, i ^ (odd_bit if i & 1 else even_bit)) for...  14.8 us
    pallas_call x13, Pallas kernels, call(): pl.pallas_call(run, out_shape=outs, in_specs=[SMEM] * len(scalars) + [VME...  14.4 us
    pallas_call x2, Pallas kernels, join(): pl.pallas_call(kernel, out_shape=shape(BF16, rows, width), in_specs=[pl.B...  2.34 us
  transfers between devices with their start and end apart: 12, of which 8 were waited for; matrix products, arithmetic and copies ran while one was open for 0% of the time, Pallas kernels for 20%

profile of v5, /device:TPU:0, one launch (start us, length us, event | category | flops | bytes accessed | tf_op | source)
XLA Modules:
  0.0 67.6 jit_solution(11168664388317005560)
XLA Ops:
  0.6 0.0 copy-start.1
  0.6 0.0 copy-start.4
  0.7 0.0 copy-start
  0.7 0.0 copy-start.3
  0.7 0.0 copy-start.2
  0.7 1.2 %join.1.refs_5_.refs_1_.refs_6_.refs_3_ = bf16[528,768]{1,0:T(8,128)(2,1)S(1)} custom-call(s32[1,2]{1,0:T(1,128)} %refs_1_.1, bf16[256,768]{1,0:T(8,128)(2,1)} %key_ref.1, bf16[256,768]{1,0:T(8,128)(2,1)} %value_ref.1), custom_call_target="tpu_custom_call" | custom-call | tf_op jit(solution)/shard_map/join/pallas_call | solution.py:456
  1.9 0.5 collective-permute-start
  2.4 0.0 copy-done.4
  2.4 0.7 collective-permute-start.1
  3.1 1.3 %collective-permute-done.refs_4_.refs_2_.refs_5_ = bf16[528,768]{1,0:T(8,128)(2,1)S(1)} collective-permute-done((bf16[528,768]{1,0:T(8,128)(2,1)S(1)}, bf16[528,768]{1,0:T(8,128)(2,1)S(1)}, u32[]{:S(2)}, u32[]{:S(2)}) %collective-permute-start) | collective-permute-done | bytes 811040 | tf_op jit(solution)/shard_map/ppermute | solution.py:50
  4.4 0.0 copy-done
  4.4 0.3 split.1.refs_1_
  4.7 2.9 %collective-permute-start.3 = (bf16[3,128,768]{2,1,0:T(8,128)(2,1)S(1)}, bf16[3,128,768]{2,1,0:T(8,128)(2,1)S(1)}, u32[]{:S(2)}, u32[]{:S(2)}) collective-permute-start(bf16[3,128,768]{2,1,0:T(8,128)(2,1)S(1)} %split.1.refs_1_), channel_id=1, source_target_pairs={{0,2},{1,5},{2,0},{3,7},{4,6},{5,1},{6,4},{7,3},{8,10},{9,13},{10,... | collective-permute-start | bytes 1769480 | tf_op jit(solution)/shard_map/ppermute | solution.py:50
  7.6 0.0 collective-permute-done.1.refs_5_.refs_2_.refs_3_
  7.6 0.0 copy-done.1
  7.6 1.7 %plan.1 = (f32[6,8,256]{2,1,0:T(8,128)S(1)}, s32[8,128]{1,0:T(8,128)S(1)}) custom-call(s32[1,4]{1,0:T(1,128)S(1)} %bitcast.2, s32[1,2]{1,0:T(1,128)S(1)} %copy-done.1, s32[16]{0:T(128)S(1)} %copy-done.3, f32[6,16,16]{2,1,0:T(8,128)S(1)} %copy-done.2, bf16[528,768]{1,0:T(8,128)(2,1)S(1)} %collective-permute-done.refs_4_.refs_2_.refs_5_, ...), custom_call_target="tpu_custom_call" | custom-call | flops 20132659200 | tf_op jit(solution)/shard_map/plan/pallas_call | solution.py:38
  9.3 0.0 copy-start.5
  9.3 10.4 %collective-permute-done.3.refs_2_ = bf16[3,128,768]{2,1,0:T(8,128)(2,1)S(1)} collective-permute-done((bf16[3,128,768]{2,1,0:T(8,128)(2,1)S(1)}, bf16[3,128,768]{2,1,0:T(8,128)(2,1)S(1)}, u32[]{:S(2)}, u32[]{:S(2)}) %collective-permute-start.3) | collective-permute-done | bytes 589856 | tf_op jit(solution)/shard_map/ppermute | solution.py:50
  19.7 0.3 step.1.refs_1_
  19.9 1.3 %collective-permute-start.4 = (bf16[3,128,768]{2,1,0:T(8,128)(2,1)S(1)}, bf16[3,128,768]{2,1,0:T(8,128)(2,1)S(1)}, u32[]{:S(2)}, u32[]{:S(2)}) collective-permute-start(bf16[3,128,768]{2,1,0:T(8,128)(2,1)S(1)} %step.1.refs_1_), channel_id=1, source_target_pairs={{0,4},{1,3},{2,6},{3,1},{4,0},{5,7},{6,2},{7,5},{8,12},{9,11},{10,... | collective-permute-start | bytes 1769480 | tf_op jit(solution)/shard_map/ppermute | solution.py:50
  21.2 0.0 copy-done.5
  21.2 0.7 collective-permute-start.2
  21.9 1.1 %join_queries.1.refs_1_.refs_2_ = bf16[512,768]{1,0:T(8,128)(2,1)S(1)} custom-call(bf16[256,768]{1,0:T(8,128)(2,1)} %query_ref.1, bf16[256,768]{1,0:T(8,128)(2,1)} %cotangent_ref.1), custom_call_target="tpu_custom_call" | custom-call | tf_op jit(solution)/shard_map/join_queries/pallas_call | solution.py:456
  23.0 0.0 collective-permute-done.2.refs_3_.refs_4_
  23.0 1.3 %stats.1.refs_3_.refs_1_ = f32[6,8,256]{2,1,0:T(8,128)S(1)} custom-call(f32[6,8,256]{2,1,0:T(8,128)S(1)} %get-tuple-element.23.refs_0_, bf16[512,768]{1,0:T(8,128)(2,1)S(1)} %join_queries.1.refs_1_.refs_2_, bf16[256,768]{1,0:T(8,128)(2,1)S(1)} %collective-permute-done.1.refs_5_.refs_2_.refs_3_, bf16[256,768]{1,0:T(8,128)(2,1)S(1)} %collective-permute-done.2.refs_3_.refs_4_, ...), custom_call_target="tpu_custom_call" | custom-call | tf_op jit(solution)/shard_map/stats/pallas_call | solution.py:38
  24.3 8.5 %collective-permute-done.4.refs_2_ = bf16[3,128,768]{2,1,0:T(8,128)(2,1)S(1)} collective-permute-done((bf16[3,128,768]{2,1,0:T(8,128)(2,1)S(1)}, bf16[3,128,768]{2,1,0:T(8,128)(2,1)S(1)}, u32[]{:S(2)}, u32[]{:S(2)}) %collective-permute-start.4) | collective-permute-done | bytes 589856 | tf_op jit(solution)/shard_map/ppermute | solution.py:50
  32.8 0.3 pick.1
  33.1 0.1 collective-permute-start.5
  33.2 1.3 %collective-permute-start.8 = (bf16[512,768]{1,0:T(8,128)(2,1)S(1)}, bf16[512,768]{1,0:T(8,128)(2,1)S(1)}, u32[]{:S(2)}, u32[]{:S(2)}) collective-permute-start(bf16[512,768]{1,0:T(8,128)(2,1)S(1)} %join_queries.1.refs_1_.refs_2_), channel_id=1, source_target_pairs={{1,0},{2,1},{3,2},{4,3},{5,4},{6,5},{7,6},{9,8},{10,9},{11,10},{12... | collective-permute-start | bytes 2359304 | tf_op jit(solution)/shard_map/ppermute | solution.py:477
  34.5 0.4 collective-permute-done.5.refs_4_.refs_8_
  34.9 1.6 %memory.1 = (f32[6,8,256]{2,1,0:T(8,128)S(1)}, bf16[2,128,768]{2,1,0:T(8,128)(2,1)S(1)}, bf16[2,128,768]{2,1,0:T(8,128)(2,1)S(1)}) custom-call(f32[6,8,256]{2,1,0:T(8,128)S(1)} %get-tuple-element.23.refs_0_, f32[6,8,256]{2,1,0:T(8,128)S(1)} %stats.1.refs_3_.refs_1_, bf16[512,768]{1,0:T(8,128)(2,1)S(1)} %join_queries.1.refs_1_.refs_2_, ...), custom_call_target="tpu_custom_call" | custom-call | flops 20132659200 | tf_op jit(solution)/shard_map/memory/pallas_call | solution.py:38
  36.5 0.8 %collective-permute-start.6 = (bf16[2,128,768]{2,1,0:T(8,128)(2,1)S(1)}, bf16[2,128,768]{2,1,0:T(8,128)(2,1)S(1)}, u32[]{:S(2)}, u32[]{:S(2)}) collective-permute-start(bf16[2,128,768]{2,1,0:T(8,128)(2,1)S(1)} %get-tuple-element.29), channel_id=1, source_target_pairs={{0,1},{1,0},{2,3},{3,2},{4,5},{5,4},{6,7},{7,6},{8,9},{9,8},{10,11... | collective-permute-start | bytes 1179656 | tf_op jit(solution)/shard_map/ppermute | solution.py:50
  37.3 1.3 %collective-permute-done.6.refs_2_ = bf16[2,128,768]{2,1,0:T(8,128)(2,1)S(1)} collective-permute-done((bf16[2,128,768]{2,1,0:T(8,128)(2,1)S(1)}, bf16[2,128,768]{2,1,0:T(8,128)(2,1)S(1)}, u32[]{:S(2)}, u32[]{:S(2)}) %collective-permute-start.6) | collective-permute-done | bytes 393248 | tf_op jit(solution)/shard_map/ppermute | solution.py:50
  38.7 0.8 %sum.1 = (f32[3,128,768]{2,1,0:T(8,128)S(1)}, bf16[3,128,768]{2,1,0:T(8,128)(2,1)S(1)}) custom-call(s32[8,128]{1,0:T(8,128)S(1)} %get-tuple-element.24.refs_3_.refs_0_, bf16[2,128,768]{2,1,0:T(8,128)(2,1)S(1)} %get-tuple-element.28.refs_1_, bf16[2,128,768]{2,1,0:T(8,128)(2,1)S(1)} %collective-permute-done.6.refs_2_), custom_call_target="tpu_custom_call" | custom-call | tf_op jit(solution)/shard_map/sum/pallas_call | solution.py:38
  39.4 3.0 %collective-permute-start.9 = (bf16[3,128,768]{2,1,0:T(8,128)(2,1)S(1)}, bf16[3,128,768]{2,1,0:T(8,128)(2,1)S(1)}, u32[]{:S(2)}, u32[]{:S(2)}) collective-permute-start(bf16[3,128,768]{2,1,0:T(8,128)(2,1)S(1)} %get-tuple-element.30.refs_9_), channel_id=1, source_target_pairs={{0,4},{1,3},{2,6},{3,1},{4,0},{5,7},{6,2},{7,5},{8,12},{9,11},{10,... | collective-permute-start | bytes 1769480 | tf_op jit(solution)/shard_map/ppermute | solution.py:50
  42.4 5.2 %rest.1 = (bf16[256,768]{1,0:T(8,128)(2,1)}, bf16[256,768]{1,0:T(8,128)(2,1)}, f32[2,256,768]{2,1,0:T(8,128)S(1)}, f32[6,8,256]{2,1,0:T(8,128)S(1)}) custom-call(f32[6,8,256]{2,1,0:T(8,128)S(1)} %get-tuple-element.23.refs_0_, f32[6,8,256]{2,1,0:T(8,128)S(1)} %get-tuple-element.27.refs_1_, bf16[512,768]{1,0:T(8,128)(2,1)S(1)} %join_queries.1.refs_1_.refs_2_, ...), custom_call_target="tpu_custom_call" | custom-call | tf_op jit(solution)/shard_map/rest/pallas_call | solution.py:38
  47.7 1.3 %collective-permute-start.7 = (f32[6,8,256]{2,1,0:T(8,128)S(1)}, f32[6,8,256]{2,1,0:T(8,128)S(1)}, u32[]{:S(2)}, u32[]{:S(2)}) collective-permute-start(f32[6,8,256]{2,1,0:T(8,128)S(1)} %get-tuple-element.33), channel_id=1, source_target_pairs={{1,0},{2,1},{3,2},{4,3},{5,4},{6,5},{7,6},{9,8},{10,9},{11,10},{12... | collective-permute-start | bytes 147464 | tf_op jit(solution)/shard_map/ppermute | solution.py:523
  49.0 0.0 collective-permute-done.8.refs_2_.refs_1_
  49.0 1.3 %collective-permute-done.9.refs_1_ = bf16[3,128,768]{2,1,0:T(8,128)(2,1)S(1)} collective-permute-done((bf16[3,128,768]{2,1,0:T(8,128)(2,1)S(1)}, bf16[3,128,768]{2,1,0:T(8,128)(2,1)S(1)}, u32[]{:S(2)}, u32[]{:S(2)}) %collective-permute-start.9) | collective-permute-done | bytes 589856 | tf_op jit(solution)/shard_map/ppermute | solution.py:50
  50.3 0.2 add.1
  50.4 6.2 %collective-permute-start.10 = (bf16[3,128,768]{2,1,0:T(8,128)(2,1)S(1)}, bf16[3,128,768]{2,1,0:T(8,128)(2,1)S(1)}, u32[]{:S(2)}, u32[]{:S(2)}) collective-permute-start(bf16[3,128,768]{2,1,0:T(8,128)(2,1)S(1)} %get-tuple-element.37), channel_id=1, source_target_pairs={{0,2},{1,5},{2,0},{3,7},{4,6},{5,1},{6,4},{7,3},{8,10},{9,13},{10,... | collective-permute-start | bytes 1769480 | tf_op jit(solution)/shard_map/ppermute | solution.py:50
  56.6 0.0 collective-permute-done.7.refs_1_
  56.6 1.5 %next.1.refs_3_.refs_0_ = f32[2,256,768]{2,1,0:T(8,128)S(1)} custom-call(f32[6,8,256]{2,1,0:T(8,128)S(1)} %get-tuple-element.23.refs_0_, f32[6,8,256]{2,1,0:T(8,128)S(1)} %collective-permute-done.7.refs_1_, bf16[512,768]{1,0:T(8,128)(2,1)S(1)} %collective-permute-done.8.refs_2_.refs_1_, bf16[528,768]{1,0:T(8,128)(2,1)S(1)} %join.1.refs_5_.refs_1_.refs_6_.refs_3_, ...), custom_call_target="tpu_custom_call" | custom-call | flops 20132659200 | tf_op jit(solution)/shard_map/next/pallas_call | solution.py:38
  58.1 6.3 %collective-permute-done.10.refs_2_ = bf16[3,128,768]{2,1,0:T(8,128)(2,1)S(1)} collective-permute-done((bf16[3,128,768]{2,1,0:T(8,128)(2,1)S(1)}, bf16[3,128,768]{2,1,0:T(8,128)(2,1)S(1)}, u32[]{:S(2)}, u32[]{:S(2)}) %collective-permute-start.10) | collective-permute-done | bytes 589856 | tf_op jit(solution)/shard_map/ppermute | solution.py:50
  64.5 0.3 owned.1
  64.8 0.1 collective-permute-start.11
  64.9 1.7 %collective-permute-done.11.refs_2_ = bf16[2,128,768]{2,1,0:T(8,128)(2,1)S(1)} collective-permute-done((bf16[2,128,768]{2,1,0:T(8,128)(2,1)S(1)}, bf16[2,128,768]{2,1,0:T(8,128)(2,1)S(1)}, u32[]{:S(2)}, u32[]{:S(2)}) %collective-permute-start.11) | collective-permute-done | bytes 393248 | tf_op jit(solution)/shard_map/ppermute | solution.py:50
  66.6 1.0 %final.1 = (bf16[256,768]{1,0:T(8,128)(2,1)}, bf16[256,768]{1,0:T(8,128)(2,1)}) custom-call(f32[2,256,768]{2,1,0:T(8,128)S(1)} %next.1.refs_3_.refs_0_, f32[2,128,768]{2,1,0:T(8,128)S(1)} %get-tuple-element.38.refs_1_, bf16[2,128,768]{2,1,0:T(8,128)(2,1)S(1)} %collective-permute-done.11.refs_2_), custom_call_target="tpu_custom_call" | custom-call | tf_op jit(solution)/shard_map/final/pallas_call | solution.py:38
  (3 shorter events, 0.0 us)
Async XLA Ops:
  0.6 7.0 %copy-start.1 = (s32[1,2]{1,0:T(1,128)S(1)}, s32[1,2]{1,0:T(1,128)}, u32[]{:S(2)}) copy-start(s32[1,2]{1,0:T(1,128)} %refs_1_.1) | copy-start | bytes 28
  0.6 1.8 %copy-start.4 = (bf16[256,768]{1,0:T(8,128)(2,1)S(1)}, bf16[256,768]{1,0:T(8,128)(2,1)}, u32[]{:S(2)}) copy-start(bf16[256,768]{1,0:T(8,128)(2,1)} %key_ref.1) | copy-start | bytes 1179652
  0.7 3.7 %copy-start = (s32[4]{0:T(128)S(1)}, s32[4]{0:T(128)}, u32[]{:S(2)}) copy-start(s32[4]{0:T(128)} %param.15) | copy-start | bytes 52
  0.7 6.9 %copy-start.3 = (s32[16]{0:T(128)S(1)}, s32[16]{0:T(128)}, u32[]{:S(2)}) copy-start(s32[16]{0:T(128)} %refs_2_.1) | copy-start | bytes 196
  0.7 6.9 %copy-start.2 = (f32[6,16,16]{2,1,0:T(8,128)S(1)}, f32[6,16,16]{2,1,0:T(8,128)}, u32[]{:S(2)}) copy-start(f32[6,16,16]{2,1,0:T(8,128)} %refs_3_.1) | copy-start | bytes 18436
  1.9 2.5 %collective-permute-start = (bf16[528,768]{1,0:T(8,128)(2,1)S(1)}, bf16[528,768]{1,0:T(8,128)(2,1)S(1)}, u32[]{:S(2)}, u32[]{:S(2)}) collective-permute-start(bf16[528,768]{1,0:T(8,128)(2,1)S(1)} %join.1.refs_5_.refs_1_.refs_6_.refs_3_), channel_id=1, source_target_pairs={{0,1},{1,0},{2,3},{3,2},{4,5},{5,4},{6,7},{7,6},{8,9},{9,8},{10,11... | collective-permute-start | bytes 2433032 | tf_op jit(solution)/shard_map/ppermute | solution.py:50
  2.4 5.2 %collective-permute-start.1 = (bf16[256,768]{1,0:T(8,128)(2,1)S(1)}, bf16[256,768]{1,0:T(8,128)(2,1)S(1)}, u32[]{:S(2)}, u32[]{:S(2)}) collective-permute-start(bf16[256,768]{1,0:T(8,128)(2,1)S(1)} %copy-done.4), channel_id=1, source_target_pairs={{1,2},{3,4},{5,6},{9,10},{11,12},{13,14},{17,18},{19,20},{21,22},{... | collective-permute-start | bytes 1179656 | tf_op jit(solution)/shard_map/ppermute | solution.py:55
  4.7 15.0 %collective-permute-start.3 = (bf16[3,128,768]{2,1,0:T(8,128)(2,1)S(1)}, bf16[3,128,768]{2,1,0:T(8,128)(2,1)S(1)}, u32[]{:S(2)}, u32[]{:S(2)}) collective-permute-start(bf16[3,128,768]{2,1,0:T(8,128)(2,1)S(1)} %split.1.refs_1_), channel_id=1, source_target_pairs={{0,2},{1,5},{2,0},{3,7},{4,6},{5,1},{6,4},{7,3},{8,10},{9,13},{10,... | collective-permute-start | bytes 1769480 | tf_op jit(solution)/shard_map/ppermute | solution.py:50
  9.3 11.9 %copy-start.5 = (bf16[256,768]{1,0:T(8,128)(2,1)S(1)}, bf16[256,768]{1,0:T(8,128)(2,1)}, u32[]{:S(2)}) copy-start(bf16[256,768]{1,0:T(8,128)(2,1)} %value_ref.1) | copy-start | bytes 1179652
  19.9 12.9 %collective-permute-start.4 = (bf16[3,128,768]{2,1,0:T(8,128)(2,1)S(1)}, bf16[3,128,768]{2,1,0:T(8,128)(2,1)S(1)}, u32[]{:S(2)}, u32[]{:S(2)}) collective-permute-start(bf16[3,128,768]{2,1,0:T(8,128)(2,1)S(1)} %step.1.refs_1_), channel_id=1, source_target_pairs={{0,4},{1,3},{2,6},{3,1},{4,0},{5,7},{6,2},{7,5},{8,12},{9,11},{10,... | collective-permute-start | bytes 1769480 | tf_op jit(solution)/shard_map/ppermute | solution.py:50
  21.2 1.8 %collective-permute-start.2 = (bf16[256,768]{1,0:T(8,128)(2,1)S(1)}, bf16[256,768]{1,0:T(8,128)(2,1)S(1)}, u32[]{:S(2)}, u32[]{:S(2)}) collective-permute-start(bf16[256,768]{1,0:T(8,128)(2,1)S(1)} %copy-done.5), channel_id=1, source_target_pairs={{1,2},{3,4},{5,6},{9,10},{11,12},{13,14},{17,18},{19,20},{21,22},{... | collective-permute-start | bytes 1179656 | tf_op jit(solution)/shard_map/ppermute | solution.py:55
  33.1 1.8 %collective-permute-start.5 = (bf16[2,128,768]{2,1,0:T(8,128)(2,1)S(1)}, bf16[2,128,768]{2,1,0:T(8,128)(2,1)S(1)}, u32[]{:S(2)}, u32[]{:S(2)}) collective-permute-start(bf16[2,128,768]{2,1,0:T(8,128)(2,1)S(1)} %get-tuple-element.26), channel_id=1, source_target_pairs={{0,1},{1,0},{2,3},{3,2},{4,5},{5,4},{6,7},{7,6},{8,9},{9,8},{10,11... | collective-permute-start | bytes 1179656 | tf_op jit(solution)/shard_map/ppermute | solution.py:50
  33.2 15.8 %collective-permute-start.8 = (bf16[512,768]{1,0:T(8,128)(2,1)S(1)}, bf16[512,768]{1,0:T(8,128)(2,1)S(1)}, u32[]{:S(2)}, u32[]{:S(2)}) collective-permute-start(bf16[512,768]{1,0:T(8,128)(2,1)S(1)} %join_queries.1.refs_1_.refs_2_), channel_id=1, source_target_pairs={{1,0},{2,1},{3,2},{4,3},{5,4},{6,5},{7,6},{9,8},{10,9},{11,10},{12... | collective-permute-start | bytes 2359304 | tf_op jit(solution)/shard_map/ppermute | solution.py:477
  36.5 2.1 %collective-permute-start.6 = (bf16[2,128,768]{2,1,0:T(8,128)(2,1)S(1)}, bf16[2,128,768]{2,1,0:T(8,128)(2,1)S(1)}, u32[]{:S(2)}, u32[]{:S(2)}) collective-permute-start(bf16[2,128,768]{2,1,0:T(8,128)(2,1)S(1)} %get-tuple-element.29), channel_id=1, source_target_pairs={{0,1},{1,0},{2,3},{3,2},{4,5},{5,4},{6,7},{7,6},{8,9},{9,8},{10,11... | collective-permute-start | bytes 1179656 | tf_op jit(solution)/shard_map/ppermute | solution.py:50
  39.4 10.8 %collective-permute-start.9 = (bf16[3,128,768]{2,1,0:T(8,128)(2,1)S(1)}, bf16[3,128,768]{2,1,0:T(8,128)(2,1)S(1)}, u32[]{:S(2)}, u32[]{:S(2)}) collective-permute-start(bf16[3,128,768]{2,1,0:T(8,128)(2,1)S(1)} %get-tuple-element.30.refs_9_), channel_id=1, source_target_pairs={{0,4},{1,3},{2,6},{3,1},{4,0},{5,7},{6,2},{7,5},{8,12},{9,11},{10,... | collective-permute-start | bytes 1769480 | tf_op jit(solution)/shard_map/ppermute | solution.py:50
  47.7 9.0 %collective-permute-start.7 = (f32[6,8,256]{2,1,0:T(8,128)S(1)}, f32[6,8,256]{2,1,0:T(8,128)S(1)}, u32[]{:S(2)}, u32[]{:S(2)}) collective-permute-start(f32[6,8,256]{2,1,0:T(8,128)S(1)} %get-tuple-element.33), channel_id=1, source_target_pairs={{1,0},{2,1},{3,2},{4,3},{5,4},{6,5},{7,6},{9,8},{10,9},{11,10},{12... | collective-permute-start | bytes 147464 | tf_op jit(solution)/shard_map/ppermute | solution.py:523
  50.4 14.0 %collective-permute-start.10 = (bf16[3,128,768]{2,1,0:T(8,128)(2,1)S(1)}, bf16[3,128,768]{2,1,0:T(8,128)(2,1)S(1)}, u32[]{:S(2)}, u32[]{:S(2)}) collective-permute-start(bf16[3,128,768]{2,1,0:T(8,128)(2,1)S(1)} %get-tuple-element.37), channel_id=1, source_target_pairs={{0,2},{1,5},{2,0},{3,7},{4,6},{5,1},{6,4},{7,3},{8,10},{9,13},{10,... | collective-permute-start | bytes 1769480 | tf_op jit(solution)/shard_map/ppermute | solution.py:50
  64.8 1.8 %collective-permute-start.11 = (bf16[2,128,768]{2,1,0:T(8,128)(2,1)S(1)}, bf16[2,128,768]{2,1,0:T(8,128)(2,1)S(1)}, u32[]{:S(2)}, u32[]{:S(2)}) collective-permute-start(bf16[2,128,768]{2,1,0:T(8,128)(2,1)S(1)} %get-tuple-element.39), channel_id=1, source_target_pairs={{0,1},{1,0},{2,3},{3,2},{4,5},{5,4},{6,7},{7,6},{8,9},{9,8},{10,11... | collective-permute-start | bytes 1179656 | tf_op jit(solution)/shard_map/ppermute | solution.py:50

commit v6 on v5

v6 whole, which is shorter than its diff:
```python
import functools
import math

import jax
import jax.numpy as jnp
from jax import lax
from jax.experimental import pallas as pl
from jax.experimental.pallas import tpu as pltpu
from jax.sharding import PartitionSpec as P

FR_DEV = 2
MEM = 2
DEPTH = 128
TAIL = 16

BLOCKED_LOGIT = -1e30
LOG2E = math.log2(math.e)
FACTOR = 1.0 / math.sqrt(DEPTH)

SMEM = pl.BlockSpec(memory_space=pltpu.SMEM)
VMEM = pl.BlockSpec(memory_space=pltpu.VMEM)
ANY = pl.BlockSpec(memory_space=pl.ANY)
HIDING = 200
VMEM_LIMIT = 32 * 1024 * 1024
BF16, F32 = jnp.bfloat16, jnp.float32


def shape(dtype, *dims):
    return jax.ShapeDtypeStruct(dims, dtype)


def call(kernel, outs, arrays, scalars=(), after=(), flops=0, name=None):
    count = len(scalars) + len(arrays)

    def run(*refs):
        kernel(*refs[:count], *refs[count + len(after) :])

    return pl.pallas_call(
        run,
        out_shape=outs,
        in_specs=[SMEM] * len(scalars) + [VMEM] * len(arrays) + [ANY] * len(after),
        out_specs=[VMEM] * len(outs),
        compiler_params=pltpu.CompilerParams(vmem_limit_bytes=VMEM_LIMIT),
        cost_estimate=pl.CostEstimate(flops=flops, bytes_accessed=0, transcendentals=0) if flops else None,
        name=name,
    )(*scalars, *arrays, *after)


def swap(block, even_bit, odd_bit, peers):
    return lax.ppermute(block, "tm", [(i, i ^ (odd_bit if i & 1 else even_bit)) for i in range(peers)])


def shift(block, by, start, peers):
    pairs = [(i, i + by) for i in range(start, peers, 2) if 0 <= i + by < peers]
    return lax.ppermute(block, "tm", pairs)


def lane_value(row, lane):
    lanes = lax.broadcasted_iota(jnp.int32, row.shape, 1)
    return jnp.max(jnp.where(lanes == lane, row, 0))


def bank_of(bank_ref):
    row = bank_ref[...]
    return [lane_value(row, slot) for slot in range(row.shape[1])]


def dyn_frames(bank, last_frame):
    found = [jnp.int32(0)] * (len(bank) - 2)
    seen = jnp.int32(0)
    for frame in bank:
        free = jnp.logical_and(frame != 0, frame != last_frame)
        for j in range(len(found)):
            found[j] = jnp.where(jnp.logical_and(free, seen == j), frame, found[j])
        seen = seen + free.astype(jnp.int32)
    return found


def place_of(frame, dyns):
    place = jnp.int32(len(dyns))
    for j, dyn in enumerate(dyns):
        place = jnp.where(frame == dyn, j, place)
    return place


def choose(out, take_first, first, second):
    @pl.when(take_first)
    def _():
        out[...] = first[...]

    @pl.when(jnp.logical_not(take_first))
    def _():
        out[...] = second[...]


def has_end(me, done, peers):
    return jnp.logical_or((me & ~done) == 0, (me | done) == peers - 1)


def has_dyn(me, frame, done):
    return ((me ^ (frame // FR_DEV)) & ~done) == 0


def by_role(me, even_value, odd_value):
    return jnp.where((me & 1) == 0, even_value, odd_value)


def join_kernel(index_ref, key_ref, value_ref, joined_ref, index_buf, sems):
    rows = key_ref.shape[0]
    copies = [
        pltpu.make_async_copy(index_ref, index_buf, sems.at[0]),
        pltpu.make_async_copy(key_ref, joined_ref.at[pl.ds(0, rows)], sems.at[1]),
        pltpu.make_async_copy(value_ref, joined_ref.at[pl.ds(rows, rows)], sems.at[2]),
    ]
    for copy in copies:
        copy.start()
    copies[0].wait()
    width = joined_ref.shape[1]
    lane = lax.broadcasted_iota(jnp.int32, (TAIL, width), 1) // DEPTH
    tail = jnp.zeros((TAIL, width), jnp.int32)
    for m in range(MEM):
        tail = jnp.where(lane == m, index_buf[0:1, m : m + 1], tail)
    joined_ref[2 * rows : 2 * rows + TAIL, :] = tail.astype(F32).astype(BF16)
    copies[1].wait()
    copies[2].wait()


def join_queries_kernel(query_ref, cotangent_ref, joined_ref, sems):
    rows = query_ref.shape[0]
    copies = [
        pltpu.make_async_copy(ref, joined_ref.at[pl.ds(j * rows, rows)], sems.at[j])
        for j, ref in enumerate((query_ref, cotangent_ref))
    ]
    for copy in copies:
        copy.start()
    for copy in copies:
        copy.wait()


def pack(fields, width):
    code = jnp.int32(0)
    for j, field in enumerate(fields):
        code = code | (field.astype(jnp.int32) << (j * width))
    return code


def field(code, j, width):
    return (code >> (j * width)) & ((1 << width) - 1)


def code_of(codes_ref, row):
    return jnp.max(codes_ref[row : row + 1, :])


PICK, SUM, OWNED = range(3)
PLACE_BITS = 4
PREV, OWN, MEMORY, NEXT, PAIR = range(5)


def plan_kernel(peers, last_bits, bank_ref, index_ref, pose_ref, bias_ref, pair_ref, rows_ref, codes_ref):
    me = lax.axis_index("tm")
    last_frame = peers * FR_DEV - 1
    heads, _, row_count = rows_ref.shape
    bank = [bank_ref[0, slot] for slot in range(bank_ref.shape[1])]
    tail = pair_ref.shape[0] - TAIL
    pair_ids = []
    for m in range(MEM):
        slot = jnp.max(pair_ref[tail : tail + TAIL, m * DEPTH : (m + 1) * DEPTH].astype(F32)).astype(jnp.int32)
        pair_ids.append(bank_ref[0, slot])
    mem_ids = [bank_ref[0, index_ref[0, m]] for m in range(MEM)]

    own_ids = [me * FR_DEV + j for j in range(FR_DEV)]
    prev_ids = [jnp.maximum(own - FR_DEV, 0) for own in own_ids]
    next_ids = [jnp.minimum(own + FR_DEV, last_frame) for own in own_ids]
    pair_own_ids = [(me ^ 1) * FR_DEV + j for j in range(FR_DEV)]
    pieces = ((prev_ids, own_ids), (own_ids, own_ids), (mem_ids, own_ids), (own_ids, next_ids), (pair_ids, pair_own_ids))
    poses = [([pose_ref[f] for f in key_ids], [pose_ref[f] for f in query_ids]) for key_ids, query_ids in pieces]
    frame_of = lax.broadcasted_iota(jnp.int32, (1, row_count), 1) // (row_count // FR_DEV)
    for head in range(heads):
        for piece, (key_poses, query_poses) in enumerate(poses):
            for j, key_pose in enumerate(key_poses):
                row = jnp.zeros((1, row_count), F32)
                for a, query_pose in enumerate(query_poses):
                    value = bias_ref[head, query_pose, key_pose] * LOG2E
                    if piece == PREV:
                        value = jnp.where(me == 0, BLOCKED_LOGIT, value)
                    row = jnp.where(frame_of == a, value, row)
                rows_ref[head, piece * FR_DEV + j : piece * FR_DEV + j + 1, :] = row

    dyns = dyn_frames(bank, last_frame)
    bit = by_role(me, *last_bits)
    upper = (me & bit) != 0
    picks = []
    for frame in mem_ids + pair_ids:
        source = place_of(frame, dyns)
        local = jnp.where(frame == 0, jnp.logical_not(upper), upper)
        local = jnp.where(source < len(dyns), has_dyn(me, frame, (peers - 1) & ~bit), local)
        picks.append(source * 2 + local.astype(jnp.int32))
    far = jnp.where(upper, 0, last_frame)
    sums = [jnp.where(frame == far, len(dyns) + 1, place_of(frame, dyns)) for frame in mem_ids + pair_ids]
    owned = []
    for group in (me, me ^ 1):
        for j in range(FR_DEV):
            frame = group * FR_DEV + j
            place = place_of(frame, dyns)
            named = jnp.logical_or(place < len(dyns), jnp.logical_or(frame == 0, frame == last_frame))
            owned.append(place * 2 + named.astype(jnp.int32))
    lanes = codes_ref.shape[1]
    for row, code in ((PICK, pack(picks, PLACE_BITS)), (SUM, pack(sums, PLACE_BITS)), (OWNED, pack(owned, PLACE_BITS))):
        codes_ref[row : row + 1, :] = jnp.full((1, lanes), code, jnp.int32)


def split_kernel(peers, bank_ref, mine_ref, pair_ref, out_ref):
    me = lax.axis_index("tm")
    frame_len, half_width = out_ref.shape[2:]
    dyns = dyn_frames(bank_of(bank_ref), peers * FR_DEV - 1)
    places = [(has_dyn(me, dyn, 0), dyn % FR_DEV) for dyn in dyns]
    places.append((has_end(me, 0, peers), jnp.where(me < peers // 2, 0, FR_DEV - 1)))
    for j, (local, frame) in enumerate(places):
        for role in range(2):
            for source, taken in ((mine_ref, local), (pair_ref, jnp.logical_not(local))):

                @pl.when(jnp.logical_and((me & 1) == role, taken))
                def _(source=source, j=j, frame=frame, role=role):
                    for kind in range(2):
                        start = pl.multiple_of((kind * FR_DEV + frame) * frame_len, frame_len)
                        out_ref[j, kind] = source[pl.ds(start, frame_len), role * half_width : (role + 1) * half_width]


def step_kernel(peers, even_done, odd_done, bank_ref, mine_ref, got_ref, out_ref):
    me = lax.axis_index("tm")
    done = by_role(me, even_done, odd_done)
    dyns = dyn_frames(bank_of(bank_ref), peers * FR_DEV - 1)
    flags = [has_dyn(me, dyn, done) for dyn in dyns] + [has_end(me, done, peers)]
    for j, flag in enumerate(flags):
        choose(out_ref.at[j], flag, mine_ref.at[j], got_ref.at[j])


def pick_kernel(codes_ref, mine_ref, got_ref, own_out, pair_out):
    code = code_of(codes_ref, PICK)
    for o, out in enumerate((own_out, pair_out)):
        for m in range(MEM):
            pick = field(code, o * MEM + m, PLACE_BITS)
            source = pick >> 1
            choose(out.at[m], (pick & 1) != 0, mine_ref.at[source], got_ref.at[source])


def dot(a, b, left, right):
    return lax.dot_general(a, b, (((left,), (right,)), ((), ())), preferred_element_type=F32)


def logits_of(keys, query, rows_ref, head, piece):
    frame_len = query.shape[0] // FR_DEV
    raw = dot(keys, query, 1, 1) * (FACTOR * LOG2E)
    parts = []
    for j in range(FR_DEV):
        row = piece * FR_DEV + j
        parts.append(raw[j * frame_len : (j + 1) * frame_len] + rows_ref[head, row : row + 1, :])
    return jnp.concatenate(parts, axis=0)


def joined_parts(joined_ref, cols):
    rows = joined_ref.shape[0] // 2 // DEPTH * DEPTH
    return joined_ref[0:rows, cols], joined_ref[rows : 2 * rows, cols]


def head_cols(head):
    return pl.ds(head * DEPTH, DEPTH)


def part_of(logits, slopes):
    peak = jnp.max(logits, axis=0, keepdims=True)
    exps = jnp.exp2(logits - peak)
    return peak, jnp.sum(exps, axis=0, keepdims=True), jnp.sum(exps * slopes, axis=0, keepdims=True)


def merged(left, right):
    peak = jnp.maximum(left[0], right[0])
    scales = [jnp.exp2(part[0] - peak) for part in (left, right)]
    return peak, *(left[j] * scales[0] + right[j] * scales[1] for j in (1, 2))


def load_part(ref, head):
    return tuple(ref[head, j : j + 1, :] for j in range(3))


def store_part(ref, head, part):
    for j, row in enumerate(part):
        ref[head, j : j + 1, :] = row


def ahead_kernel(rows_ref, next_queries_ref, own_ref, part_ref):
    heads = part_ref.shape[0]
    for local in range(heads):
        query, cotangent = joined_parts(next_queries_ref, head_cols(local))
        keys, values = joined_parts(own_ref, head_cols(heads + local))
        logits = logits_of(keys, query, rows_ref, heads + local, NEXT)
        store_part(part_ref, local, part_of(logits, dot(values, cotangent, 1, 1)))


def stats_kernel(rows_ref, queries_ref, outer_ref, pair_ref, own_ref, ahead_ref, part_ref, keys_out, queries_out):
    me = lax.axis_index("tm")
    even = (me & 1) == 0
    heads = queries_ref.shape[1] // DEPTH
    half = heads // 2
    rows = queries_ref.shape[0]
    half_width = half * DEPTH
    keys_out[...] = own_ref[0:rows, half_width : 2 * half_width]
    queries_out[...] = queries_ref[:, 0:half_width]

    def products(head):
        query, cotangent = joined_parts(queries_ref, head_cols(head))
        prev = joined_parts(pair_ref, head_cols(head))
        if head < half:
            outer = joined_parts(outer_ref, head_cols(head))
            prev = [jnp.where(even, there, here) for there, here in zip(outer, prev)]
        own = joined_parts(own_ref, head_cols(head))
        return [
            (logits_of(keys, query, rows_ref, head, piece), dot(values, cotangent, 1, 1))
            for piece, (keys, values) in ((PREV, prev), (OWN, own))
        ]

    ahead = products(0)
    for head in range(heads):
        now = ahead
        if head + 1 < heads:
            ahead = products(head + 1)
        prev, own = (part_of(*piece) for piece in now)
        if head >= half:
            there = load_part(ahead_ref, head - half)
            there = (jnp.where(me == 0, BLOCKED_LOGIT, there[0]), *there[1:])
            prev = tuple(jnp.where(even, a, b) for a, b in zip(there, prev))
        store_part(part_ref, head, merged(prev, own))


def rounded(part, logits, slopes):
    peak, total, spread = merged(part, part_of(logits, slopes))
    inverse = 1.0 / total
    stats = peak, inverse, spread * inverse
    return stats, *weights_of(stats, logits, slopes)


def weights_of(stats, logits, slopes):
    peak, inverse, spread = stats
    probs = jnp.exp2(logits - peak) * inverse
    return probs.astype(BF16), (probs * (slopes - spread)).astype(BF16)


def memory_kernel(
    codes_ref, rows_ref, part_ref, pair_part_ref, own_queries, pair_queries, own_mem, pair_mem, keep_ref, send_ref
):
    role = lax.axis_index("tm") & 1
    code = code_of(codes_ref, SUM)
    frame_len, half_width = own_mem.shape[2:]
    half = half_width // DEPTH
    groups = ((own_queries, own_mem, part_ref, MEMORY), (pair_queries, pair_mem, pair_part_ref, PAIR))
    work = [(g, local) for local in range(half) for g in range(len(groups))]
    keep_ref[...] = jnp.zeros(keep_ref.shape, F32)

    def products(g, local):
        queries, mem, _, piece = groups[g]
        query, cotangent = joined_parts(queries, head_cols(local))
        keys, values = (mem[:, kind, :, head_cols(local)].reshape(MEM * frame_len, DEPTH) for kind in range(2))
        return logits_of(keys, query, rows_ref, role * half + local, piece), dot(values, cotangent, 1, 1)

    def add(g, local, _, weights, dlogits):
        query, cotangent = joined_parts(groups[g][0], head_cols(local))
        terms = (dot(dlogits, query, 1, 0) * FACTOR, dot(weights, cotangent, 1, 0))
        for m in range(MEM):
            place = field(code, g * MEM + m, PLACE_BITS)
            for kind, term in enumerate(terms):
                part = term[m * frame_len : (m + 1) * frame_len].astype(BF16).astype(F32)
                keep_ref[place, kind, :, head_cols(local)] += part

    ahead = products(*work[0])
    behind = None
    for j, (g, local) in enumerate(work):
        now = ahead
        if j + 1 < len(work):
            ahead = products(*work[j + 1])
        if behind is not None:
            add(*work[j - 1], *behind)
        behind = rounded(load_part(groups[g][2], role * half + local), *now)
    add(*work[-1], *behind)
    kept = send_ref.shape[0]
    for place in range(kept):
        send_ref[place] = keep_ref[place if place + 1 < kept else kept].astype(BF16)


def next_kernel(
    rows_ref, stats_ref, pair_queries, outer_first, outer_second, own_ref, term_ref, sum_ref
):
    even = (lax.axis_index("tm") & 1) == 0
    heads = pair_queries.shape[1] // DEPTH
    half = heads // 2

    def operands(head):
        outer = joined_parts((outer_first, outer_second)[head // half], head_cols(head % half))
        return [jnp.where(even, a, b) for a, b in zip(joined_parts(pair_queries, head_cols(head)), outer)]

    def products(head):
        query, cotangent = operands(head)
        keys, values = joined_parts(own_ref, head_cols(head))
        return logits_of(keys, query, rows_ref, head, NEXT), dot(values, cotangent, 1, 1)

    ahead = products(0)
    for head in range(heads):
        now = ahead
        if head + 1 < heads:
            ahead = products(head + 1)
        weights, dlogits = weights_of(load_part(stats_ref, head), *now)
        query, cotangent = operands(head)
        cols = head_cols(head)
        sum_ref[0, :, cols] = term_ref[0, :, cols] + dot(dlogits, query, 1, 0) * FACTOR
        sum_ref[1, :, cols] = term_ref[1, :, cols] + dot(weights, cotangent, 1, 0)


def rest_kernel(
    rows_ref,
    part_ref,
    queries_ref,
    outer_first,
    outer_second,
    pair_ref,
    own_ref,
    own_mem,
    other_mem,
    attended_ref,
    grad_query_ref,
    term_ref,
    stats_ref,
):
    role = lax.axis_index("tm") & 1
    frame_len, half_width = own_mem.shape[2:]
    heads = queries_ref.shape[1] // DEPTH
    half = half_width // DEPTH

    def pieces(head):
        cols = head_cols(head % half)
        outer = joined_parts((outer_first, outer_second)[head // half], cols)
        prev = [jnp.where(role == 0, a, b) for a, b in zip(outer, joined_parts(pair_ref, head_cols(head)))]
        memory = [
            jnp.where(role == head // half, own_mem[:, kind, :, cols], other_mem[:, kind, :, cols]).reshape(
                MEM * frame_len, DEPTH
            )
            for kind in range(2)
        ]
        return (PREV, prev), (OWN, joined_parts(own_ref, head_cols(head))), (MEMORY, memory)

    def products(head):
        query, cotangent = joined_parts(queries_ref, head_cols(head))
        return [
            (logits_of(keys, query, rows_ref, head, piece), dot(values, cotangent, 1, 1))
            for piece, (keys, values) in pieces(head)
        ]

    ahead = products(0)
    for head in range(heads):
        now = ahead
        if head + 1 < heads:
            ahead = products(head + 1)
        cols = head_cols(head)
        query, cotangent = joined_parts(queries_ref, cols)
        stats, *last = rounded(load_part(part_ref, head), *now[-1])
        store_part(stats_ref, head, stats)
        rounds = [weights_of(stats, *now[PREV]), weights_of(stats, *now[OWN]), last]
        attended = grad_query = 0.0
        for (piece, (keys, values)), (weights, dlogits) in zip(pieces(head), rounds):
            attended += dot(values, weights, 0, 0)
            grad_query += dot(keys, dlogits, 0, 0)
            if piece == OWN:
                term_ref[0, :, cols] = dot(dlogits, query, 1, 0) * FACTOR
                term_ref[1, :, cols] = dot(weights, cotangent, 1, 0)
        attended_ref[:, cols] = attended.T.astype(BF16)
        grad_query_ref[:, cols] = (grad_query * FACTOR).T.astype(BF16)


def add_kernel(keep_ref, got_ref, out_ref, send_ref):
    value = keep_ref[0 : got_ref.shape[0]] + got_ref[...].astype(F32)
    out_ref[...] = value
    send_ref[...] = value.astype(BF16)


def owned_kernel(codes_ref, keep_ref, got_ref, mine_ref, pair_ref):
    code = code_of(codes_ref, OWNED)
    for o, out in enumerate((mine_ref, pair_ref)):
        for j in range(FR_DEV):
            owned = field(code, o * FR_DEV + j, PLACE_BITS)
            place = owned >> 1
            named = (owned & 1) != 0

            @pl.when(named)
            def _(out=out, j=j, place=place):
                value = keep_ref[place] + got_ref[place].astype(F32)
                out[j] = value.astype(out.dtype)

            @pl.when(jnp.logical_not(named))
            def _(out=out, j=j):
                out[j] = jnp.zeros(out.shape[1:], out.dtype)


def final_kernel(own_ref, mine_ref, got_ref, grad_key_ref, grad_value_ref):
    role = lax.axis_index("tm") & 1
    frame_len, half_width = mine_ref.shape[2:]
    for kind, out in enumerate((grad_key_ref, grad_value_ref)):
        for j in range(FR_DEV):
            rows = pl.ds(j * frame_len, frame_len)
            for half in range(2):
                cols = pl.ds(half * half_width, half_width)
                bank = jnp.where(role == half, mine_ref[j, kind], got_ref[j, kind].astype(F32))
                out[rows, cols] = (own_ref[kind, rows, cols] + bank).astype(BF16)


def body(
    query_states,
    key_states,
    value_states,
    grad_out,
    camera_pose,
    pose_bias,
    memory_index,
    bank_frames,
):
    row_count, width = query_states.shape
    frame_len = row_count // FR_DEV
    heads = pose_bias.shape[0]
    slots = bank_frames.shape[0]
    peers = lax.axis_size("tm")
    bits = [1 << i for i in range(1, peers.bit_length() - 1)]
    turns = list(zip(bits, bits[::-1]))
    even = (lax.axis_index("tm") & 1) == 0
    piece_flops = 2 * row_count * row_count * width
    bank_frames = bank_frames.reshape(1, slots)
    last_bits = turns[-1]

    def join(kernel, rows, arrays, scratch, name, after=()):
        def run(*refs):
            kernel(*refs[: len(arrays)], *refs[len(arrays) + len(after) :])

        return pl.pallas_call(
            run,
            out_shape=shape(BF16, rows, width),
            in_specs=[pl.BlockSpec(memory_space=pltpu.HBM)] * len(arrays) + [ANY] * len(after),
            out_specs=VMEM,
            scratch_shapes=[*scratch, pltpu.SemaphoreType.DMA((len(arrays),))],
            compiler_params=pltpu.CompilerParams(vmem_limit_bytes=VMEM_LIMIT),
            name=name,
        )(*(pltpu.with_memory_space_constraint(array, pltpu.HBM) for array in arrays), *after)

    joined = join(
        join_kernel,
        2 * row_count + TAIL,
        [memory_index, key_states, value_states],
        [pltpu.VMEM(memory_index.shape, jnp.int32)],
        "join",
    )
    half_width = width // 2
    first, second = slice(0, half_width), slice(half_width, width)
    outer_first = shift(joined[: 2 * row_count, first], 1, 1, peers)
    pair = swap(joined, 1, 1, peers)
    held = shape(BF16, slots - 1, 2, frame_len, half_width)
    sums = shape(F32, slots - 1, 2, frame_len, half_width)
    (mine,) = call(functools.partial(split_kernel, peers), [held], [bank_frames, joined, pair], name="split")
    queries = join(join_queries_kernel, 2 * row_count, [query_states, grad_out], [], "join_queries", after=[mine])
    pair_queries = swap(queries, 1, 1, peers)
    next_second = shift(queries[:, second], -1, 2, peers)
    own_half = jnp.where(even, queries[:, first], queries[:, second])
    pair_half = jnp.where(even, pair_queries[:, first], pair_queries[:, second])

    bias_rows = -(-(5 * FR_DEV) // 8) * 8
    rows, codes = call(
        functools.partial(plan_kernel, peers, last_bits),
        [shape(F32, heads, bias_rows, row_count), shape(jnp.int32, 8, 128)],
        [pair],
        scalars=[bank_frames, memory_index, camera_pose, pose_bias],
        after=[outer_first],
        flops=HIDING * piece_flops,
        name="plan",
    )
    even_done = odd_done = 1
    for step, (even_bit, odd_bit) in enumerate(turns):
        got = swap(mine, even_bit, odd_bit, peers)
        if step + 1 < len(turns):
            kernel = functools.partial(step_kernel, peers, even_done, odd_done)
            after = [codes, pair_queries, next_second]
            (mine,) = call(kernel, [held], [bank_frames, mine, got], after=after, name="step")
        even_done |= even_bit
        odd_done |= odd_bit

    stats = shape(F32, heads, 8, row_count)
    half_joined = shape(BF16, 2 * row_count, half_width)
    (ahead,) = call(ahead_kernel, [shape(F32, heads // 2, 8, row_count)], [rows, next_second, joined], name="ahead")
    ahead = shift(ahead, 1, 1, peers)
    part, keys_out, queries_out = call(
        stats_kernel,
        [stats, half_joined, half_joined],
        [rows, queries, outer_first, pair, joined, ahead],
        name="stats",
    )
    pair_part = swap(part, 1, 1, peers)
    outer_second = shift(keys_out, 1, 1, peers)
    next_first = shift(queries_out, -1, 2, peers)
    chosen = shape(BF16, MEM, 2, frame_len, half_width)
    own_mem, pair_mem = call(pick_kernel, [chosen] * 2, [codes, mine, got], name="pick")
    keep, send = call(
        memory_kernel,
        [shape(F32, slots, 2, frame_len, half_width), held],
        [codes, rows, part, pair_part, own_half, pair_half, own_mem, pair_mem],
        flops=HIDING * piece_flops,
        name="memory",
    )
    other_mem = swap(pair_mem, 1, 1, peers)
    pair_sums = shape(F32, 2, row_count, width)
    attended, grad_query, own_terms, stats_all = call(
        rest_kernel,
        [shape(BF16, row_count, width)] * 2 + [pair_sums, stats],
        [rows, part, queries, outer_first, outer_second, pair, joined, own_mem, other_mem],
        after=[send, next_first],
        flops=HIDING * piece_flops,
        name="rest",
    )
    next_stats = lax.ppermute(stats_all, "tm", [(i, i - 1) for i in range(1, peers)])
    (own,) = call(
        next_kernel,
        [pair_sums],
        [rows, next_stats, pair_queries, next_first, next_second, joined, own_terms],
        flops=HIDING * piece_flops,
        name="next",
    )
    for step, (even_bit, odd_bit) in enumerate(turns[::-1]):
        got = swap(send, even_bit, odd_bit, peers)
        if step + 1 < len(turns):
            keep, send = call(add_kernel, [sums, held], [keep, got], after=[own_terms], name="add")
    owned_mine, owned_send = call(
        owned_kernel,
        [shape(F32, FR_DEV, 2, frame_len, half_width), shape(BF16, FR_DEV, 2, frame_len, half_width)],
        [codes, keep, got],
        after=[own],
        name="owned",
    )
    owned_got = swap(owned_send, 1, 1, peers)
    grad_key, grad_value = call(
        final_kernel, [shape(BF16, row_count, width)] * 2, [own, owned_mine, owned_got], name="final"
    )
    return (attended, grad_query, grad_key, grad_value)


def solution(mesh):
    rows = P(("traj", "tm"), None)
    in_specs = (rows, rows, rows, rows, P("traj"), P(), rows, P("traj"))
    return jax.shard_map(body, mesh=mesh, in_specs=in_specs, out_specs=(rows,) * 4, check_vma=False)
```

time: 67.8 us -> 73.8 us (1.088)
  starting transfers between devices: 18.7 us -> 37.5 us
  waiting for transfers between devices: 31.3 us -> 18.3 us
    ppermute x8 -> x9, starting transfers between devices: 14.8 us -> 32.8 us  [swap(): lax.ppermute(block, 'tm', [(i, i ^ (odd_bit if i & 1 else even_bit)) for...]
    ppermute x8 -> x9, waiting for transfers between devices: 31.3 us -> 18.3 us  [swap(): lax.ppermute(block, 'tm', [(i, i ^ (odd_bit if i & 1 else even_bit)) for...]
    ppermute x2 -> x5, starting transfers between devices: 1.35 us -> 3.39 us  [shift(): return lax.ppermute(block, 'tm', pairs)]
    ppermute x2 -> x1, starting transfers between devices: 2.57 us -> 1.28 us  [body(): lax.ppermute(stats_all, 'tm', [(i, i - 1) for i in range(1, peers)])]
    pallas_call x13 -> x12, Pallas kernels: 14.4 us -> 14.5 us  [call(): pl.pallas_call(run, out_shape=outs, in_specs=[SMEM] * len(scalars) + [VME...]
  transfers between devices with their start and end apart: 12 -> 15, of which waited for: 8 -> 5; matrix products, arithmetic and copies ran while one was open for 0% -> 0% of each run, Pallas kernels for 20% -> 19%
where the time goes in v6:
time: 73.8 us; the launch traced here: 73.6 us
  starting transfers between devices  37.5 us (51%)
  waiting for transfers between devices  18.3 us (25%)
  Pallas kernels  16.7 us (23%)
  between operations  0.89 us (1%)
    ppermute x9, starting transfers between devices, swap(): lax.ppermute(block, 'tm', [(i, i ^ (odd_bit if i & 1 else even_bit)) for...  32.8 us
    ppermute x9, waiting for transfers between devices, swap(): lax.ppermute(block, 'tm', [(i, i ^ (odd_bit if i & 1 else even_bit)) for...  18.3 us
    pallas_call x12, Pallas kernels, call(): pl.pallas_call(run, out_shape=outs, in_specs=[SMEM] * len(scalars) + [VME...  14.5 us
    ppermute x5, starting transfers between devices, shift(): return lax.ppermute(block, 'tm', pairs)  3.39 us
    pallas_call x2, Pallas kernels, join(): pl.pallas_call(run, out_shape=shape(BF16, rows, width), in_specs=[pl.Bloc...  2.29 us
  transfers between devices with their start and end apart: 15, of which 5 were waited for; matrix products, arithmetic and copies ran while one was open for 0% of the time, Pallas kernels for 19%

profile of v6, /device:TPU:0, one launch (start us, length us, event | category | flops | bytes accessed | tf_op | source)
XLA Modules:
  0.0 73.6 jit_solution(14836965613921731999)
XLA Ops:
  0.6 1.2 %join.1.refs_1_.refs_2_.refs_4_.refs_6_.refs_5_ = bf16[528,768]{1,0:T(8,128)(2,1)S(1)} custom-call(s32[1,2]{1,0:T(1,128)} %refs_1_.4, bf16[256,768]{1,0:T(8,128)(2,1)} %refs_1_.3, bf16[256,768]{1,0:T(8,128)(2,1)} %refs_2_.2), custom_call_target="tpu_custom_call" | custom-call | tf_op jit(solution)/shard_map/join/pallas_call | solution.py:540
  1.8 0.5 collective-permute-start
  2.4 0.7 collective-permute-start.1
  3.1 1.2 %collective-permute-done.refs_4_.refs_2_.refs_3_.refs_5_ = bf16[528,768]{1,0:T(8,128)(2,1)S(1)} collective-permute-done((bf16[528,768]{1,0:T(8,128)(2,1)S(1)}, bf16[528,768]{1,0:T(8,128)(2,1)S(1)}, u32[]{:S(2)}, u32[]{:S(2)}) %collective-permute-start) | collective-permute-done | bytes 811040 | tf_op jit(solution)/shard_map/ppermute | solution.py:50
  4.3 0.3 split.1.refs_2_.refs_1_
  4.6 0.0 copy-start.1
  4.6 0.0 copy-start.2
  4.6 0.0 copy-start.3
  4.7 2.9 %collective-permute-start.5 = (bf16[3,2,128,384]{3,2,1,0:T(8,128)(2,1)S(1)}, bf16[3,2,128,384]{3,2,1,0:T(8,128)(2,1)S(1)}, u32[]{:S(2)}, u32[]{:S(2)}) collective-permute-start(bf16[3,2,128,384]{3,2,1,0:T(8,128)(2,1)S(1)} %split.1.refs_2_.refs_1_), channel_id=1, source_target_pairs={{0,2},{1,5},{2,0},{3,7},{4,6},{5,1},{6,4},{7,3},{8,10},{9,13},{10,... | collective-permute-start | bytes 1769480 | tf_op jit(solution)/shard_map/ppermute | solution.py:50
  7.6 1.1 %join_queries.1.refs_1_.refs_2_ = bf16[512,768]{1,0:T(8,128)(2,1)S(1)} custom-call(bf16[256,768]{1,0:T(8,128)(2,1)} %refs_0_.3, bf16[256,768]{1,0:T(8,128)(2,1)} %refs_1_.5, bf16[3,2,128,384]{3,2,1,0:T(8,128)(2,1)S(1)} %split.1.refs_2_.refs_1_), custom_call_target="tpu_custom_call" | custom-call | tf_op jit(solution)/shard_map/join_queries/pallas_call | solution.py:540
  8.7 1.1 %collective-permute-start.6 = (bf16[512,768]{1,0:T(8,128)(2,1)S(1)}, bf16[512,768]{1,0:T(8,128)(2,1)S(1)}, u32[]{:S(2)}, u32[]{:S(2)}) collective-permute-start(bf16[512,768]{1,0:T(8,128)(2,1)S(1)} %join_queries.1.refs_1_.refs_2_), channel_id=1, source_target_pairs={{0,1},{1,0},{2,3},{3,2},{4,5},{5,4},{6,7},{7,6},{8,9},{9,8},{10,11... | collective-permute-start | bytes 2359304 | tf_op jit(solution)/shard_map/ppermute | solution.py:50
  9.8 0.1 slice_select_fusion.1
  9.9 0.7 collective-permute-start.2
  10.6 0.0 collective-permute-done.1.refs_5_.refs_2_.refs_3_
  10.7 1.7 %plan.1 = (f32[6,16,256]{2,1,0:T(8,128)S(1)}, s32[8,128]{1,0:T(8,128)S(1)}) custom-call(s32[1,4]{1,0:T(1,128)S(1)} %bitcast.2, s32[1,2]{1,0:T(1,128)S(1)} %copy-done.1, s32[16]{0:T(128)S(1)} %copy-done.3, f32[6,16,16]{2,1,0:T(8,128)S(1)} %copy-done.2, bf16[528,768]{1,0:T(8,128)(2,1)S(1)} %collective-permute-done.refs_4_.refs_2_.refs_3_.refs_5_, ...), custom_call_target="tpu_custom_call" | custom-call | flops 20132659200 | tf_op jit(solution)/shard_map/plan/pallas_call | solution.py:38
  12.3 0.0 collective-permute-done.2.refs_1_.refs_5_.refs_4_
  12.3 7.3 %collective-permute-done.5.refs_2_ = bf16[3,2,128,384]{3,2,1,0:T(8,128)(2,1)S(1)} collective-permute-done((bf16[3,2,128,384]{3,2,1,0:T(8,128)(2,1)S(1)}, bf16[3,2,128,384]{3,2,1,0:T(8,128)(2,1)S(1)}, u32[]{:S(2)}, u32[]{:S(2)}) %collective-permute-start.5) | collective-permute-done | bytes 589856 | tf_op jit(solution)/shard_map/ppermute | solution.py:50
  19.7 0.0 collective-permute-done.6.refs_4_.refs_2_
  19.7 0.3 step.1.refs_1_
  20.0 5.1 %collective-permute-start.7 = (bf16[3,2,128,384]{3,2,1,0:T(8,128)(2,1)S(1)}, bf16[3,2,128,384]{3,2,1,0:T(8,128)(2,1)S(1)}, u32[]{:S(2)}, u32[]{:S(2)}) collective-permute-start(bf16[3,2,128,384]{3,2,1,0:T(8,128)(2,1)S(1)} %step.1.refs_1_), channel_id=1, source_target_pairs={{0,4},{1,3},{2,6},{3,1},{4,0},{5,7},{6,2},{7,5},{8,12},{9,11},{10,... | collective-permute-start | bytes 1769480 | tf_op jit(solution)/shard_map/ppermute | solution.py:50
  25.1 0.5 ahead.1
  25.6 0.7 collective-permute-start.3
  26.2 0.0 collective-permute-done.3.refs_5_
  26.2 1.4 %stats.1 = (f32[6,8,256]{2,1,0:T(8,128)S(1)}, bf16[512,384]{1,0:T(8,128)(2,1)S(1)}, bf16[512,384]{1,0:T(8,128)(2,1)S(1)}) custom-call(f32[6,16,256]{2,1,0:T(8,128)S(1)} %get-tuple-element.23.refs_0_.refs_1_, bf16[512,768]{1,0:T(8,128)(2,1)S(1)} %join_queries.1.refs_1_.refs_2_, bf16[512,384]{1,0:T(8,128)(2,1)S(1)} %collective-permute-done.1.refs_5_.refs_2_.refs_3_, ...), custom_call_target="tpu_custom_call" | custom-call | tf_op jit(solution)/shard_map/stats/pallas_call | solution.py:38
  27.6 7.5 %collective-permute-start.9 = (f32[6,8,256]{2,1,0:T(8,128)S(1)}, f32[6,8,256]{2,1,0:T(8,128)S(1)}, u32[]{:S(2)}, u32[]{:S(2)}) collective-permute-start(f32[6,8,256]{2,1,0:T(8,128)S(1)} %get-tuple-element.24.refs_2_.refs_1_), channel_id=1, source_target_pairs={{0,1},{1,0},{2,3},{3,2},{4,5},{5,4},{6,7},{7,6},{8,9},{9,8},{10,11... | collective-permute-start | bytes 147464 | tf_op jit(solution)/shard_map/ppermute | solution.py:50
  35.1 0.7 collective-permute-start.4
  35.8 0.7 collective-permute-start.10
  36.5 0.1 slice_select_fusion.refs_5_
  36.5 0.0 collective-permute-done.7.refs_2_
  36.5 0.3 pick.1
  36.8 4.4 %collective-permute-start.8 = (bf16[2,2,128,384]{3,2,1,0:T(8,128)(2,1)S(1)}, bf16[2,2,128,384]{3,2,1,0:T(8,128)(2,1)S(1)}, u32[]{:S(2)}, u32[]{:S(2)}) collective-permute-start(bf16[2,2,128,384]{3,2,1,0:T(8,128)(2,1)S(1)} %get-tuple-element.28.refs_7_), channel_id=1, source_target_pairs={{0,1},{1,0},{2,3},{3,2},{4,5},{5,4},{6,7},{7,6},{8,9},{9,8},{10,11... | collective-permute-start | bytes 1179656 | tf_op jit(solution)/shard_map/ppermute | solution.py:50
  41.3 0.0 collective-permute-done.9.refs_3_
  41.3 1.9 %memory.1 = (f32[4,2,128,384]{3,2,1,0:T(8,128)S(1)}, bf16[3,2,128,384]{3,2,1,0:T(8,128)(2,1)S(1)}) custom-call(s32[8,128]{1,0:T(8,128)S(1)} %get-tuple-element.26.refs_3_.refs_0_, f32[6,16,256]{2,1,0:T(8,128)S(1)} %get-tuple-element.23.refs_0_.refs_1_, f32[6,8,256]{2,1,0:T(8,128)S(1)} %get-tuple-element.24.refs_2_.refs_1_, ...), custom_call_target="tpu_custom_call" | custom-call | flops 20132659200 | tf_op jit(solution)/shard_map/memory/pallas_call | solution.py:38
  43.2 3.0 %collective-permute-start.12 = (bf16[3,2,128,384]{3,2,1,0:T(8,128)(2,1)S(1)}, bf16[3,2,128,384]{3,2,1,0:T(8,128)(2,1)S(1)}, u32[]{:S(2)}, u32[]{:S(2)}) collective-permute-start(bf16[3,2,128,384]{3,2,1,0:T(8,128)(2,1)S(1)} %get-tuple-element.29.refs_9_), channel_id=1, source_target_pairs={{0,4},{1,3},{2,6},{3,1},{4,0},{5,7},{6,2},{7,5},{8,12},{9,11},{10,... | collective-permute-start | bytes 1769480 | tf_op jit(solution)/shard_map/ppermute | solution.py:50
  46.1 0.0 collective-permute-done.4.refs_4_
  46.1 0.0 collective-permute-done.10.refs_10_.refs_3_
  46.1 0.0 collective-permute-done.8.refs_8_
  46.1 5.5 %rest.1 = (bf16[256,768]{1,0:T(8,128)(2,1)}, bf16[256,768]{1,0:T(8,128)(2,1)}, f32[2,256,768]{2,1,0:T(8,128)S(1)}, f32[6,8,256]{2,1,0:T(8,128)S(1)}) custom-call(f32[6,16,256]{2,1,0:T(8,128)S(1)} %get-tuple-element.23.refs_0_.refs_1_, f32[6,8,256]{2,1,0:T(8,128)S(1)} %get-tuple-element.24.refs_2_.refs_1_, bf16[512,768]{1,0:T(8,128)(2,1)S(1)} %join_queries.1.refs_1_.refs_2_, ...), custom_call_target="tpu_custom_call" | custom-call | flops 20132659200 | tf_op jit(solution)/shard_map/rest/pallas_call | solution.py:38
  51.6 1.3 %collective-permute-start.11 = (f32[6,8,256]{2,1,0:T(8,128)S(1)}, f32[6,8,256]{2,1,0:T(8,128)S(1)}, u32[]{:S(2)}, u32[]{:S(2)}) collective-permute-start(f32[6,8,256]{2,1,0:T(8,128)S(1)} %get-tuple-element.33), channel_id=1, source_target_pairs={{1,0},{2,1},{3,2},{4,3},{5,4},{6,5},{7,6},{9,8},{10,9},{11,10},{12... | collective-permute-start | bytes 147464 | tf_op jit(solution)/shard_map/ppermute | solution.py:622
  52.9 1.1 %collective-permute-done.12.refs_1_ = bf16[3,2,128,384]{3,2,1,0:T(8,128)(2,1)S(1)} collective-permute-done((bf16[3,2,128,384]{3,2,1,0:T(8,128)(2,1)S(1)}, bf16[3,2,128,384]{3,2,1,0:T(8,128)(2,1)S(1)}, u32[]{:S(2)}, u32[]{:S(2)}) %collective-permute-start.12) | collective-permute-done | bytes 589856 | tf_op jit(solution)/shard_map/ppermute | solution.py:50
  54.0 0.2 add.1
  54.2 8.2 %collective-permute-start.13 = (bf16[3,2,128,384]{3,2,1,0:T(8,128)(2,1)S(1)}, bf16[3,2,128,384]{3,2,1,0:T(8,128)(2,1)S(1)}, u32[]{:S(2)}, u32[]{:S(2)}) collective-permute-start(bf16[3,2,128,384]{3,2,1,0:T(8,128)(2,1)S(1)} %get-tuple-element.37), channel_id=1, source_target_pairs={{0,2},{1,5},{2,0},{3,7},{4,6},{5,1},{6,4},{7,3},{8,10},{9,13},{10,... | collective-permute-start | bytes 1769480 | tf_op jit(solution)/shard_map/ppermute | solution.py:50
  62.3 1.1 %next.1.refs_3_.refs_0_ = f32[2,256,768]{2,1,0:T(8,128)S(1)} custom-call(f32[6,16,256]{2,1,0:T(8,128)S(1)} %get-tuple-element.23.refs_0_.refs_1_, f32[6,8,256]{2,1,0:T(8,128)S(1)} %collective-permute-done.11.refs_1_, bf16[512,768]{1,0:T(8,128)(2,1)S(1)} %collective-permute-done.6.refs_4_.refs_2_, ...), custom_call_target="tpu_custom_call" | custom-call | flops 20132659200 | tf_op jit(solution)/shard_map/next/pallas_call | solution.py:38
  63.5 7.0 %collective-permute-done.13.refs_2_ = bf16[3,2,128,384]{3,2,1,0:T(8,128)(2,1)S(1)} collective-permute-done((bf16[3,2,128,384]{3,2,1,0:T(8,128)(2,1)S(1)}, bf16[3,2,128,384]{3,2,1,0:T(8,128)(2,1)S(1)}, u32[]{:S(2)}, u32[]{:S(2)}) %collective-permute-start.13) | collective-permute-done | bytes 589856 | tf_op jit(solution)/shard_map/ppermute | solution.py:50
  70.5 0.3 owned.1
  70.8 0.1 collective-permute-start.14
  70.9 1.7 %collective-permute-done.14.refs_2_ = bf16[2,2,128,384]{3,2,1,0:T(8,128)(2,1)S(1)} collective-permute-done((bf16[2,2,128,384]{3,2,1,0:T(8,128)(2,1)S(1)}, bf16[2,2,128,384]{3,2,1,0:T(8,128)(2,1)S(1)}, u32[]{:S(2)}, u32[]{:S(2)}) %collective-permute-start.14) | collective-permute-done | bytes 393248 | tf_op jit(solution)/shard_map/ppermute | solution.py:50
  72.6 1.0 %final.1 = (bf16[256,768]{1,0:T(8,128)(2,1)}, bf16[256,768]{1,0:T(8,128)(2,1)}) custom-call(f32[2,256,768]{2,1,0:T(8,128)S(1)} %next.1.refs_3_.refs_0_, f32[2,2,128,384]{3,2,1,0:T(8,128)S(1)} %get-tuple-element.38.refs_1_, bf16[2,2,128,384]{3,2,1,0:T(8,128)(2,1)S(1)} %collective-permute-done.14.refs_2_), custom_call_target="tpu_custom_call" | custom-call | tf_op jit(solution)/shard_map/final/pallas_call | solution.py:38
  (7 shorter events, 0.1 us)
Async XLA Ops:
  0.6 3.6 %copy-start = (s32[4]{0:T(128)S(1)}, s32[4]{0:T(128)}, u32[]{:S(2)}) copy-start(s32[4]{0:T(128)} %param.15) | copy-start | bytes 52
  1.8 2.5 %collective-permute-start = (bf16[528,768]{1,0:T(8,128)(2,1)S(1)}, bf16[528,768]{1,0:T(8,128)(2,1)S(1)}, u32[]{:S(2)}, u32[]{:S(2)}) collective-permute-start(bf16[528,768]{1,0:T(8,128)(2,1)S(1)} %join.1.refs_1_.refs_2_.refs_4_.refs_6_.refs_5_), channel_id=1, source_target_pairs={{0,1},{1,0},{2,3},{3,2},{4,5},{5,4},{6,7},{7,6},{8,9},{9,8},{10,11... | collective-permute-start | bytes 2433032 | tf_op jit(solution)/shard_map/ppermute | solution.py:50
  2.4 8.2 %collective-permute-start.1 = (bf16[512,384]{1,0:T(8,128)(2,1)S(1)}, bf16[512,384]{1,0:T(8,128)(2,1)S(1)}, u32[]{:S(2)}, u32[]{:S(2)}) collective-permute-start(bf16[512,384]{1,0:T(8,128)(2,1)S(1)} %slice.21), channel_id=1, source_target_pairs={{1,2},{3,4},{5,6},{9,10},{11,12},{13,14},{17,18},{19,20},{21,22},{... | collective-permute-start | bytes 1179656 | tf_op jit(solution)/shard_map/ppermute | solution.py:55
  4.6 6.0 %copy-start.1 = (s32[1,2]{1,0:T(1,128)S(1)}, s32[1,2]{1,0:T(1,128)}, u32[]{:S(2)}) copy-start(s32[1,2]{1,0:T(1,128)} %refs_1_.4) | copy-start | bytes 28
  4.6 6.0 %copy-start.2 = (f32[6,16,16]{2,1,0:T(8,128)S(1)}, f32[6,16,16]{2,1,0:T(8,128)}, u32[]{:S(2)}) copy-start(f32[6,16,16]{2,1,0:T(8,128)} %refs_3_.1) | copy-start | bytes 18436
  4.6 6.0 %copy-start.3 = (s32[16]{0:T(128)S(1)}, s32[16]{0:T(128)}, u32[]{:S(2)}) copy-start(s32[16]{0:T(128)} %refs_2_.3) | copy-start | bytes 196
  4.7 15.0 %collective-permute-start.5 = (bf16[3,2,128,384]{3,2,1,0:T(8,128)(2,1)S(1)}, bf16[3,2,128,384]{3,2,1,0:T(8,128)(2,1)S(1)}, u32[]{:S(2)}, u32[]{:S(2)}) collective-permute-start(bf16[3,2,128,384]{3,2,1,0:T(8,128)(2,1)S(1)} %split.1.refs_2_.refs_1_), channel_id=1, source_target_pairs={{0,2},{1,5},{2,0},{3,7},{4,6},{5,1},{6,4},{7,3},{8,10},{9,13},{10,... | collective-permute-start | bytes 1769480 | tf_op jit(solution)/shard_map/ppermute | solution.py:50
  8.7 10.9 %collective-permute-start.6 = (bf16[512,768]{1,0:T(8,128)(2,1)S(1)}, bf16[512,768]{1,0:T(8,128)(2,1)S(1)}, u32[]{:S(2)}, u32[]{:S(2)}) collective-permute-start(bf16[512,768]{1,0:T(8,128)(2,1)S(1)} %join_queries.1.refs_1_.refs_2_), channel_id=1, source_target_pairs={{0,1},{1,0},{2,3},{3,2},{4,5},{5,4},{6,7},{7,6},{8,9},{9,8},{10,11... | collective-permute-start | bytes 2359304 | tf_op jit(solution)/shard_map/ppermute | solution.py:50
  9.9 2.4 %collective-permute-start.2 = (bf16[512,384]{1,0:T(8,128)(2,1)S(1)}, bf16[512,384]{1,0:T(8,128)(2,1)S(1)}, u32[]{:S(2)}, u32[]{:S(2)}) collective-permute-start(bf16[512,384]{1,0:T(8,128)(2,1)S(1)} %get-tuple-element.43), channel_id=1, source_target_pairs={{2,1},{4,3},{6,5},{10,9},{12,11},{14,13},{18,17},{20,19},{22,21},{... | collective-permute-start | bytes 1179656 | tf_op jit(solution)/shard_map/ppermute | solution.py:55
  20.0 16.6 %collective-permute-start.7 = (bf16[3,2,128,384]{3,2,1,0:T(8,128)(2,1)S(1)}, bf16[3,2,128,384]{3,2,1,0:T(8,128)(2,1)S(1)}, u32[]{:S(2)}, u32[]{:S(2)}) collective-permute-start(bf16[3,2,128,384]{3,2,1,0:T(8,128)(2,1)S(1)} %step.1.refs_1_), channel_id=1, source_target_pairs={{0,4},{1,3},{2,6},{3,1},{4,0},{5,7},{6,2},{7,5},{8,12},{9,11},{10,... | collective-permute-start | bytes 1769480 | tf_op jit(solution)/shard_map/ppermute | solution.py:50
  25.6 0.7 collective-permute-start.3
  27.6 13.6 %collective-permute-start.9 = (f32[6,8,256]{2,1,0:T(8,128)S(1)}, f32[6,8,256]{2,1,0:T(8,128)S(1)}, u32[]{:S(2)}, u32[]{:S(2)}) collective-permute-start(f32[6,8,256]{2,1,0:T(8,128)S(1)} %get-tuple-element.24.refs_2_.refs_1_), channel_id=1, source_target_pairs={{0,1},{1,0},{2,3},{3,2},{4,5},{5,4},{6,7},{7,6},{8,9},{9,8},{10,11... | collective-permute-start | bytes 147464 | tf_op jit(solution)/shard_map/ppermute | solution.py:50
  35.1 11.0 %collective-permute-start.4 = (bf16[512,384]{1,0:T(8,128)(2,1)S(1)}, bf16[512,384]{1,0:T(8,128)(2,1)S(1)}, u32[]{:S(2)}, u32[]{:S(2)}) collective-permute-start(bf16[512,384]{1,0:T(8,128)(2,1)S(1)} %get-tuple-element.25), channel_id=1, source_target_pairs={{1,2},{3,4},{5,6},{9,10},{11,12},{13,14},{17,18},{19,20},{21,22},{... | collective-permute-start | bytes 1179656 | tf_op jit(solution)/shard_map/ppermute | solution.py:55
  35.8 10.4 %collective-permute-start.10 = (bf16[512,384]{1,0:T(8,128)(2,1)S(1)}, bf16[512,384]{1,0:T(8,128)(2,1)S(1)}, u32[]{:S(2)}, u32[]{:S(2)}) collective-permute-start(bf16[512,384]{1,0:T(8,128)(2,1)S(1)} %get-tuple-element.30), channel_id=1, source_target_pairs={{2,1},{4,3},{6,5},{10,9},{12,11},{14,13},{18,17},{20,19},{22,21},{... | collective-permute-start | bytes 1179656 | tf_op jit(solution)/shard_map/ppermute | solution.py:55
  36.8 9.3 %collective-permute-start.8 = (bf16[2,2,128,384]{3,2,1,0:T(8,128)(2,1)S(1)}, bf16[2,2,128,384]{3,2,1,0:T(8,128)(2,1)S(1)}, u32[]{:S(2)}, u32[]{:S(2)}) collective-permute-start(bf16[2,2,128,384]{3,2,1,0:T(8,128)(2,1)S(1)} %get-tuple-element.28.refs_7_), channel_id=1, source_target_pairs={{0,1},{1,0},{2,3},{3,2},{4,5},{5,4},{6,7},{7,6},{8,9},{9,8},{10,11... | collective-permute-start | bytes 1179656 | tf_op jit(solution)/shard_map/ppermute | solution.py:50
  43.2 10.8 %collective-permute-start.12 = (bf16[3,2,128,384]{3,2,1,0:T(8,128)(2,1)S(1)}, bf16[3,2,128,384]{3,2,1,0:T(8,128)(2,1)S(1)}, u32[]{:S(2)}, u32[]{:S(2)}) collective-permute-start(bf16[3,2,128,384]{3,2,1,0:T(8,128)(2,1)S(1)} %get-tuple-element.29.refs_9_), channel_id=1, source_target_pairs={{0,4},{1,3},{2,6},{3,1},{4,0},{5,7},{6,2},{7,5},{8,12},{9,11},{10,... | collective-permute-start | bytes 1769480 | tf_op jit(solution)/shard_map/ppermute | solution.py:50
  51.6 10.7 %collective-permute-start.11 = (f32[6,8,256]{2,1,0:T(8,128)S(1)}, f32[6,8,256]{2,1,0:T(8,128)S(1)}, u32[]{:S(2)}, u32[]{:S(2)}) collective-permute-start(f32[6,8,256]{2,1,0:T(8,128)S(1)} %get-tuple-element.33), channel_id=1, source_target_pairs={{1,0},{2,1},{3,2},{4,3},{5,4},{6,5},{7,6},{9,8},{10,9},{11,10},{12... | collective-permute-start | bytes 147464 | tf_op jit(solution)/shard_map/ppermute | solution.py:622
  54.2 16.3 %collective-permute-start.13 = (bf16[3,2,128,384]{3,2,1,0:T(8,128)(2,1)S(1)}, bf16[3,2,128,384]{3,2,1,0:T(8,128)(2,1)S(1)}, u32[]{:S(2)}, u32[]{:S(2)}) collective-permute-start(bf16[3,2,128,384]{3,2,1,0:T(8,128)(2,1)S(1)} %get-tuple-element.37), channel_id=1, source_target_pairs={{0,2},{1,5},{2,0},{3,7},{4,6},{5,1},{6,4},{7,3},{8,10},{9,13},{10,... | collective-permute-start | bytes 1769480 | tf_op jit(solution)/shard_map/ppermute | solution.py:50
  70.8 1.8 %collective-permute-start.14 = (bf16[2,2,128,384]{3,2,1,0:T(8,128)(2,1)S(1)}, bf16[2,2,128,384]{3,2,1,0:T(8,128)(2,1)S(1)}, u32[]{:S(2)}, u32[]{:S(2)}) collective-permute-start(bf16[2,2,128,384]{3,2,1,0:T(8,128)(2,1)S(1)} %get-tuple-element.39), channel_id=1, source_target_pairs={{0,1},{1,0},{2,3},{3,2},{4,5},{5,4},{6,7},{7,6},{8,9},{9,8},{10,11... | collective-permute-start | bytes 1179656 | tf_op jit(solution)/shard_map/ppermute | solution.py:50

commit v7 on v5

--- a/solution.py
+++ b/solution.py
@@ -156,10 +156,13 @@
 PLACE_BITS = 4
 
 
-def plan_kernel(peers, last_bits, bank_ref, index_ref, pose_ref, bias_ref, pair_ref, rows_ref, codes_ref):
+def plan_kernel(
+    peers, last_bits, bank_ref, index_ref, pose_ref, bias_ref, pair_ref, joined_ref, rows_ref, codes_ref, values_out
+):
     me = lax.axis_index("tm")
     last_frame = peers * FR_DEV - 1
     heads, _, row_count = rows_ref.shape
+    values_out[...] = joined_ref[row_count : 2 * row_count, :]
     bank = [bank_ref[0, slot] for slot in range(bank_ref.shape[1])]
     tail = pair_ref.shape[0] - TAIL
     pair_ids = []
@@ -262,7 +265,8 @@
     return tuple(jnp.where(even, outer[:, cols], pair) for outer, pair in parts)
 
 
-def stats_kernel(rows_ref, queries_ref, outer_key_ref, outer_value_ref, pair_ref, own_ref, stats_ref):
+def stats_kernel(rows_ref, queries_ref, outer_key_ref, outer_value_ref, pair_ref, own_ref, stats_ref, queries_out):
+    queries_out[...] = queries_ref[...]
     for head in range(queries_ref.shape[1] // DEPTH):
         cols = pl.ds(head * DEPTH, DEPTH)
         query, cotangent = joined_parts(queries_ref, cols)
@@ -471,26 +475,29 @@
         "join",
     )
     outer_keys = shift(key_states, 1, 1, peers)
-    outer_values = shift(value_states, 1, 1, peers)
     pair = swap(joined, 1, 1, peers)
     queries = join(join_queries_kernel, 2 * row_count, [query_states, grad_out], [], "join_queries")
-    next_queries = lax.ppermute(queries, "tm", [(i, i - 1) for i in range(1, peers)])
 
     bias_rows = -(-(3 * FR_DEV + MEM) // 8) * 8
-    rows, codes = call(
+    rows, codes, values_out = call(
         functools.partial(plan_kernel, peers, last_bits),
-        [shape(F32, heads, bias_rows, row_count), shape(jnp.int32, 8, 128)],
-        [pair],
+        [shape(F32, heads, bias_rows, row_count), shape(jnp.int32, 8, 128), shape(BF16, row_count, width)],
+        [pair, joined],
         scalars=[bank_frames, memory_index, camera_pose, pose_bias],
         after=[outer_keys],
         flops=HIDING * piece_flops,
         name="plan",
     )
+    outer_values = shift(values_out, 1, 1, peers)
     held = shape(BF16, slots - 1, frame_len, width)
     sums = shape(F32, slots - 1, frame_len, width)
     (mine,) = call(functools.partial(split_kernel, peers), [held], [bank_frames, joined, pair], name="split")
     stats = shape(F32, heads, 8, row_count)
-    (part,) = call(stats_kernel, [stats], [rows, queries, outer_keys, outer_values, pair, joined], name="stats")
+    part, queries_out = call(
+        stats_kernel,
+        [stats, shape(BF16, 2 * row_count, width)],
+        [rows, queries, outer_keys, outer_values, pair, joined], flops=HIDING * piece_flops, name="stats")
+    next_queries = lax.ppermute(queries_out, "tm", [(i, i - 1) for i in range(1, peers)])
     even_done = odd_done = 1
     for step, (even_bit, odd_bit) in enumerate(turns):
         got = swap(mine, even_bit, odd_bit, peers)
@@ -500,18 +507,25 @@
         even_done |= even_bit
         odd_done |= odd_bit
     chosen = shape(BF16, MEM, frame_len, width)
-    mem_mine, mem_send = call(pick_kernel, [chosen] * 2, [codes, mine, got], after=[part], name="pick")
+    mem_mine, mem_send = call(pick_kernel, [chosen] * 2, [codes, mine, got], after=[part], flops=HIDING * piece_flops, name="pick")
     mem_got = swap(mem_send, 1, 1, peers)
 
     stats_all, mem_same, mem_other = call(
         memory_kernel,
         [stats, chosen, chosen],
         [rows, part, queries, mem_mine, mem_got],
+        name="memory",
+    )
+    same_got = swap(mem_other, 1, 1, peers)
+    (arrived,) = call(
+        mark_kernel,
+        [shape(F32, 8, 128)],
+        [],
+        after=[next_queries],
         flops=HIDING * piece_flops,
-        name="memory",
-    )
-    same_got = swap(mem_other, 1, 1, peers)
-    keep, send = call(sum_kernel, [sums, held], [codes, mem_same, same_got], name="sum")
+        name="arrived",
+    )
+    keep, send = call(sum_kernel, [sums, held], [codes, mem_same, same_got], after=[arrived], name="sum")
     pair_sums = shape(F32, 2, row_count, width)
     attended, grad_query, own_terms, stats_sent = call(
         rest_kernel,
@@ -521,14 +535,6 @@
         name="rest",
     )
     next_stats = lax.ppermute(stats_sent, "tm", [(i, i - 1) for i in range(1, peers)])
-    (arrived,) = call(
-        mark_kernel,
-        [shape(F32, 8, 128)],
-        [],
-        after=[own_terms, next_queries],
-        flops=HIDING * piece_flops,
-        name="arrived",
-    )
     (own,) = call(
         next_kernel,
         [pair_sums],
@@ -539,7 +545,7 @@
     for step, (even_bit, odd_bit) in enumerate(turns[::-1]):
         got = swap(send, even_bit, odd_bit, peers)
         if step + 1 < len(turns):
-            keep, send = call(add_kernel, [sums, held], [keep, got], after=[arrived], name="add")
+            keep, send = call(add_kernel, [sums, held], [keep, got], after=[own_terms], name="add")
     owned = shape(F32, FR_DEV, frame_len, width)
     owned_mine, owned_send = call(
         owned_kernel,

time: 67.8 us -> 68.2 us (level)
  waiting for transfers between devices: 31.3 us -> 34.1 us
  starting transfers between devices: 18.7 us -> 16.1 us
    ppermute x8, waiting for transfers between devices: 31.3 us -> 34.1 us  [swap(): lax.ppermute(block, 'tm', [(i, i ^ (odd_bit if i & 1 else even_bit)) for...]
    ppermute x8, starting transfers between devices: 14.8 us -> 12.1 us  [swap(): lax.ppermute(block, 'tm', [(i, i ^ (odd_bit if i & 1 else even_bit)) for...]
where the time goes in v7:
time: 68.2 us; the launch traced here: 68 us
  waiting for transfers between devices  34.1 us (50%)
  Pallas kernels  17 us (25%)
  starting transfers between devices  16.1 us (24%)
  between operations  0.82 us (1%)
    ppermute x8, waiting for transfers between devices, swap(): lax.ppermute(block, 'tm', [(i, i ^ (odd_bit if i & 1 else even_bit)) for...  34.1 us
    pallas_call x13, Pallas kernels, call(): pl.pallas_call(run, out_shape=outs, in_specs=[SMEM] * len(scalars) + [VME...  14.6 us
    ppermute x8, starting transfers between devices, swap(): lax.ppermute(block, 'tm', [(i, i ^ (odd_bit if i & 1 else even_bit)) for...  12.1 us
    pallas_call x2, Pallas kernels, join(): pl.pallas_call(kernel, out_shape=shape(BF16, rows, width), in_specs=[pl.B...  2.34 us
  transfers between devices with their start and end apart: 12, of which 8 were waited for; matrix products, arithmetic and copies ran while one was open for 0% of the time, Pallas kernels for 20%

profile of v7, /device:TPU:0, one launch (start us, length us, event | category | flops | bytes accessed | tf_op | source)
XLA Modules:
  0.0 68.0 jit_solution(14396332500857308851)
XLA Ops:
  0.6 0.0 copy-start.1
  0.6 0.0 copy-start.4
  0.7 0.0 copy-start
  0.7 0.0 copy-start.2
  0.7 0.0 copy-start.3
  0.7 1.2 %join.1.refs_5_.refs_1_.refs_6_.refs_3_ = bf16[528,768]{1,0:T(8,128)(2,1)S(1)} custom-call(s32[1,2]{1,0:T(1,128)} %refs_1_.1, bf16[256,768]{1,0:T(8,128)(2,1)} %key_ref.1, bf16[256,768]{1,0:T(8,128)(2,1)} %value_ref.1), custom_call_target="tpu_custom_call" | custom-call | tf_op jit(solution)/shard_map/join/pallas_call | solution.py:460
  1.9 0.5 collective-permute-start
  2.4 0.0 copy-done.4
  2.4 0.7 collective-permute-start.1
  3.1 1.3 %collective-permute-done.refs_4_.refs_2_.refs_5_ = bf16[528,768]{1,0:T(8,128)(2,1)S(1)} collective-permute-done((bf16[528,768]{1,0:T(8,128)(2,1)S(1)}, bf16[528,768]{1,0:T(8,128)(2,1)S(1)}, u32[]{:S(2)}, u32[]{:S(2)}) %collective-permute-start) | collective-permute-done | bytes 811040 | tf_op jit(solution)/shard_map/ppermute | solution.py:50
  4.4 0.0 copy-done
  4.4 0.3 split.1.refs_1_
  4.7 2.9 %collective-permute-start.3 = (bf16[3,128,768]{2,1,0:T(8,128)(2,1)S(1)}, bf16[3,128,768]{2,1,0:T(8,128)(2,1)S(1)}, u32[]{:S(2)}, u32[]{:S(2)}) collective-permute-start(bf16[3,128,768]{2,1,0:T(8,128)(2,1)S(1)} %split.1.refs_1_), channel_id=1, source_target_pairs={{0,2},{1,5},{2,0},{3,7},{4,6},{5,1},{6,4},{7,3},{8,10},{9,13},{10,... | collective-permute-start | bytes 1769480 | tf_op jit(solution)/shard_map/ppermute | solution.py:50
  7.6 0.0 collective-permute-done.1.refs_6_.refs_2_.refs_3_
  7.6 0.0 copy-done.1
  7.6 0.0 copy-done.2
  7.6 0.0 copy-done.3
  7.6 1.7 %plan.1 = (f32[6,8,256]{2,1,0:T(8,128)S(1)}, s32[8,128]{1,0:T(8,128)S(1)}, bf16[256,768]{1,0:T(8,128)(2,1)S(1)}) custom-call(s32[1,4]{1,0:T(1,128)S(1)} %bitcast.2, s32[1,2]{1,0:T(1,128)S(1)} %copy-done.1, s32[16]{0:T(128)S(1)} %copy-done.3, f32[6,16,16]{2,1,0:T(8,128)S(1)} %copy-done.2, bf16[528,768]{1,0:T(8,128)(2,1)S(1)} %collective-permute-done.refs_4_.refs_2_.refs_5_, ...), custom_call_target="tpu_custom_call" | custom-call | flops 20132659200 | tf_op jit(solution)/shard_map/plan/pallas_call | solution.py:38
  9.3 0.7 %collective-permute-start.2 = (bf16[256,768]{1,0:T(8,128)(2,1)S(1)}, bf16[256,768]{1,0:T(8,128)(2,1)S(1)}, u32[]{:S(2)}, u32[]{:S(2)}) collective-permute-start(bf16[256,768]{1,0:T(8,128)(2,1)S(1)} %get-tuple-element.27), channel_id=1, source_target_pairs={{1,2},{3,4},{5,6},{9,10},{11,12},{13,14},{17,18},{19,20},{21,22},{... | collective-permute-start | bytes 1179656 | tf_op jit(solution)/shard_map/ppermute | solution.py:55
  10.0 1.1 %join_queries.1.refs_1_.refs_2_ = bf16[512,768]{1,0:T(8,128)(2,1)S(1)} custom-call(bf16[256,768]{1,0:T(8,128)(2,1)} %query_ref.1, bf16[256,768]{1,0:T(8,128)(2,1)} %cotangent_ref.1), custom_call_target="tpu_custom_call" | custom-call | tf_op jit(solution)/shard_map/join_queries/pallas_call | solution.py:460
  11.1 8.6 %collective-permute-done.3.refs_2_ = bf16[3,128,768]{2,1,0:T(8,128)(2,1)S(1)} collective-permute-done((bf16[3,128,768]{2,1,0:T(8,128)(2,1)S(1)}, bf16[3,128,768]{2,1,0:T(8,128)(2,1)S(1)}, u32[]{:S(2)}, u32[]{:S(2)}) %collective-permute-start.3) | collective-permute-done | bytes 589856 | tf_op jit(solution)/shard_map/ppermute | solution.py:50
  19.7 0.3 step.1.refs_1_
  19.9 3.7 %collective-permute-start.4 = (bf16[3,128,768]{2,1,0:T(8,128)(2,1)S(1)}, bf16[3,128,768]{2,1,0:T(8,128)(2,1)S(1)}, u32[]{:S(2)}, u32[]{:S(2)}) collective-permute-start(bf16[3,128,768]{2,1,0:T(8,128)(2,1)S(1)} %step.1.refs_1_), channel_id=1, source_target_pairs={{0,4},{1,3},{2,6},{3,1},{4,0},{5,7},{6,2},{7,5},{8,12},{9,11},{10,... | collective-permute-start | bytes 1769480 | tf_op jit(solution)/shard_map/ppermute | solution.py:50
  23.6 0.0 collective-permute-done.2.refs_3_.refs_4_
  23.6 1.4 %stats.1 = (f32[6,8,256]{2,1,0:T(8,128)S(1)}, bf16[512,768]{1,0:T(8,128)(2,1)S(1)}) custom-call(f32[6,8,256]{2,1,0:T(8,128)S(1)} %get-tuple-element.26.refs_0_, bf16[512,768]{1,0:T(8,128)(2,1)S(1)} %join_queries.1.refs_1_.refs_2_, bf16[256,768]{1,0:T(8,128)(2,1)S(1)} %collective-permute-done.1.refs_6_.refs_2_.refs_3_, ...), custom_call_target="tpu_custom_call" | custom-call | flops 20132659200 | tf_op jit(solution)/shard_map/stats/pallas_call | solution.py:38
  25.0 1.3 %collective-permute-start.7 = (bf16[512,768]{1,0:T(8,128)(2,1)S(1)}, bf16[512,768]{1,0:T(8,128)(2,1)S(1)}, u32[]{:S(2)}, u32[]{:S(2)}) collective-permute-start(bf16[512,768]{1,0:T(8,128)(2,1)S(1)} %get-tuple-element.35), channel_id=1, source_target_pairs={{1,0},{2,1},{3,2},{4,3},{5,4},{6,5},{7,6},{9,8},{10,9},{11,10},{12... | collective-permute-start | bytes 2359304 | tf_op jit(solution)/shard_map/ppermute | solution.py:500
  26.3 8.3 %collective-permute-done.4.refs_2_ = bf16[3,128,768]{2,1,0:T(8,128)(2,1)S(1)} collective-permute-done((bf16[3,128,768]{2,1,0:T(8,128)(2,1)S(1)}, bf16[3,128,768]{2,1,0:T(8,128)(2,1)S(1)}, u32[]{:S(2)}, u32[]{:S(2)}) %collective-permute-start.4) | collective-permute-done | bytes 589856 | tf_op jit(solution)/shard_map/ppermute | solution.py:50
  34.7 0.3 pick.1
  35.0 4.2 %collective-permute-start.5 = (bf16[2,128,768]{2,1,0:T(8,128)(2,1)S(1)}, bf16[2,128,768]{2,1,0:T(8,128)(2,1)S(1)}, u32[]{:S(2)}, u32[]{:S(2)}) collective-permute-start(bf16[2,128,768]{2,1,0:T(8,128)(2,1)S(1)} %get-tuple-element.31), channel_id=1, source_target_pairs={{0,1},{1,0},{2,3},{3,2},{4,5},{5,4},{6,7},{7,6},{8,9},{9,8},{10,11... | collective-permute-start | bytes 1179656 | tf_op jit(solution)/shard_map/ppermute | solution.py:50
  39.1 1.3 %collective-permute-done.5.refs_4_.refs_8_ = bf16[2,128,768]{2,1,0:T(8,128)(2,1)S(1)} collective-permute-done((bf16[2,128,768]{2,1,0:T(8,128)(2,1)S(1)}, bf16[2,128,768]{2,1,0:T(8,128)(2,1)S(1)}, u32[]{:S(2)}, u32[]{:S(2)}) %collective-permute-start.5) | collective-permute-done | bytes 393248 | tf_op jit(solution)/shard_map/ppermute | solution.py:50
  40.5 1.7 %memory.1 = (f32[6,8,256]{2,1,0:T(8,128)S(1)}, bf16[2,128,768]{2,1,0:T(8,128)(2,1)S(1)}, bf16[2,128,768]{2,1,0:T(8,128)(2,1)S(1)}) custom-call(f32[6,8,256]{2,1,0:T(8,128)S(1)} %get-tuple-element.26.refs_0_, f32[6,8,256]{2,1,0:T(8,128)S(1)} %get-tuple-element.28.refs_3_.refs_1_, bf16[512,768]{1,0:T(8,128)(2,1)S(1)} %join_queries.1.refs_1_.refs_2_, ...), custom_call_target="tpu_custom_call" | custom-call | tf_op jit(solution)/shard_map/memory/pallas_call | solution.py:38
  42.2 0.4 collective-permute-start.6
  42.6 0.0 collective-permute-done.7.refs_0_.refs_2_
  42.6 1.3 %collective-permute-done.6.refs_2_ = bf16[2,128,768]{2,1,0:T(8,128)(2,1)S(1)} collective-permute-done((bf16[2,128,768]{2,1,0:T(8,128)(2,1)S(1)}, bf16[2,128,768]{2,1,0:T(8,128)(2,1)S(1)}, u32[]{:S(2)}, u32[]{:S(2)}) %collective-permute-start.6) | collective-permute-done | bytes 393248 | tf_op jit(solution)/shard_map/ppermute | solution.py:50
  44.0 0.8 %sum.1 = (f32[3,128,768]{2,1,0:T(8,128)S(1)}, bf16[3,128,768]{2,1,0:T(8,128)(2,1)S(1)}) custom-call(s32[8,128]{1,0:T(8,128)S(1)} %get-tuple-element.29.refs_3_.refs_0_, bf16[2,128,768]{2,1,0:T(8,128)(2,1)S(1)} %get-tuple-element.33.refs_1_, bf16[2,128,768]{2,1,0:T(8,128)(2,1)S(1)} %collective-permute-done.6.refs_2_, f32[8,128]{1,0:T(8,128)S(1)} %arrived.1.refs_3_), custom_call_target="tpu_custom_call" | custom-call | tf_op jit(solution)/shard_map/sum/pallas_call | solution.py:38
  44.7 0.1 collective-permute-start.9
  44.8 5.3 %rest.1 = (bf16[256,768]{1,0:T(8,128)(2,1)}, bf16[256,768]{1,0:T(8,128)(2,1)}, f32[2,256,768]{2,1,0:T(8,128)S(1)}, f32[6,8,256]{2,1,0:T(8,128)S(1)}) custom-call(f32[6,8,256]{2,1,0:T(8,128)S(1)} %get-tuple-element.26.refs_0_, f32[6,8,256]{2,1,0:T(8,128)S(1)} %get-tuple-element.32.refs_1_, bf16[512,768]{1,0:T(8,128)(2,1)S(1)} %join_queries.1.refs_1_.refs_2_, ...), custom_call_target="tpu_custom_call" | custom-call | tf_op jit(solution)/shard_map/rest/pallas_call | solution.py:38
  50.1 1.3 %collective-permute-start.8 = (f32[6,8,256]{2,1,0:T(8,128)S(1)}, f32[6,8,256]{2,1,0:T(8,128)S(1)}, u32[]{:S(2)}, u32[]{:S(2)}) collective-permute-start(f32[6,8,256]{2,1,0:T(8,128)S(1)} %get-tuple-element.39), channel_id=1, source_target_pairs={{1,0},{2,1},{3,2},{4,3},{5,4},{6,5},{7,6},{9,8},{10,9},{11,10},{12... | collective-permute-start | bytes 147464 | tf_op jit(solution)/shard_map/ppermute | solution.py:537
  51.4 3.3 %collective-permute-done.9.refs_1_ = bf16[3,128,768]{2,1,0:T(8,128)(2,1)S(1)} collective-permute-done((bf16[3,128,768]{2,1,0:T(8,128)(2,1)S(1)}, bf16[3,128,768]{2,1,0:T(8,128)(2,1)S(1)}, u32[]{:S(2)}, u32[]{:S(2)}) %collective-permute-start.9) | collective-permute-done | bytes 589856 | tf_op jit(solution)/shard_map/ppermute | solution.py:50
  54.7 0.2 add.1
  54.8 0.2 collective-permute-start.10
  55.1 0.0 collective-permute-done.8.refs_1_
  55.1 1.5 %next.1.refs_3_.refs_0_ = f32[2,256,768]{2,1,0:T(8,128)S(1)} custom-call(f32[6,8,256]{2,1,0:T(8,128)S(1)} %get-tuple-element.26.refs_0_, f32[6,8,256]{2,1,0:T(8,128)S(1)} %collective-permute-done.8.refs_1_, bf16[512,768]{1,0:T(8,128)(2,1)S(1)} %collective-permute-done.7.refs_0_.refs_2_, bf16[528,768]{1,0:T(8,128)(2,1)S(1)} %join.1.refs_5_.refs_1_.refs_6_.refs_3_, ...), custom_call_target="tpu_custom_call" | custom-call | flops 20132659200 | tf_op jit(solution)/shard_map/next/pallas_call | solution.py:38
  56.6 8.2 %collective-permute-done.10.refs_2_ = bf16[3,128,768]{2,1,0:T(8,128)(2,1)S(1)} collective-permute-done((bf16[3,128,768]{2,1,0:T(8,128)(2,1)S(1)}, bf16[3,128,768]{2,1,0:T(8,128)(2,1)S(1)}, u32[]{:S(2)}, u32[]{:S(2)}) %collective-permute-start.10) | collective-permute-done | bytes 589856 | tf_op jit(solution)/shard_map/ppermute | solution.py:50
  64.8 0.4 owned.1
  65.1 0.1 collective-permute-start.11
  65.2 1.7 %collective-permute-done.11.refs_2_ = bf16[2,128,768]{2,1,0:T(8,128)(2,1)S(1)} collective-permute-done((bf16[2,128,768]{2,1,0:T(8,128)(2,1)S(1)}, bf16[2,128,768]{2,1,0:T(8,128)(2,1)S(1)}, u32[]{:S(2)}, u32[]{:S(2)}) %collective-permute-start.11) | collective-permute-done | bytes 393248 | tf_op jit(solution)/shard_map/ppermute | solution.py:50
  66.9 1.0 %final.1 = (bf16[256,768]{1,0:T(8,128)(2,1)}, bf16[256,768]{1,0:T(8,128)(2,1)}) custom-call(f32[2,256,768]{2,1,0:T(8,128)S(1)} %next.1.refs_3_.refs_0_, f32[2,128,768]{2,1,0:T(8,128)S(1)} %get-tuple-element.44.refs_1_, bf16[2,128,768]{2,1,0:T(8,128)(2,1)S(1)} %collective-permute-done.11.refs_2_), custom_call_target="tpu_custom_call" | custom-call | tf_op jit(solution)/shard_map/final/pallas_call | solution.py:38
  (1 shorter events, 0.0 us)
Async XLA Ops:
  0.6 7.0 %copy-start.1 = (s32[1,2]{1,0:T(1,128)S(1)}, s32[1,2]{1,0:T(1,128)}, u32[]{:S(2)}) copy-start(s32[1,2]{1,0:T(1,128)} %refs_1_.1) | copy-start | bytes 28
  0.6 1.8 %copy-start.4 = (bf16[256,768]{1,0:T(8,128)(2,1)S(1)}, bf16[256,768]{1,0:T(8,128)(2,1)}, u32[]{:S(2)}) copy-start(bf16[256,768]{1,0:T(8,128)(2,1)} %key_ref.1) | copy-start | bytes 1179652
  0.7 3.7 %copy-start = (s32[4]{0:T(128)S(1)}, s32[4]{0:T(128)}, u32[]{:S(2)}) copy-start(s32[4]{0:T(128)} %param.15) | copy-start | bytes 52
  0.7 6.9 %copy-start.2 = (f32[6,16,16]{2,1,0:T(8,128)S(1)}, f32[6,16,16]{2,1,0:T(8,128)}, u32[]{:S(2)}) copy-start(f32[6,16,16]{2,1,0:T(8,128)} %refs_3_.1) | copy-start | bytes 18436
  0.7 6.9 %copy-start.3 = (s32[16]{0:T(128)S(1)}, s32[16]{0:T(128)}, u32[]{:S(2)}) copy-start(s32[16]{0:T(128)} %refs_2_.1) | copy-start | bytes 196
  1.9 2.5 %collective-permute-start = (bf16[528,768]{1,0:T(8,128)(2,1)S(1)}, bf16[528,768]{1,0:T(8,128)(2,1)S(1)}, u32[]{:S(2)}, u32[]{:S(2)}) collective-permute-start(bf16[528,768]{1,0:T(8,128)(2,1)S(1)} %join.1.refs_5_.refs_1_.refs_6_.refs_3_), channel_id=1, source_target_pairs={{0,1},{1,0},{2,3},{3,2},{4,5},{5,4},{6,7},{7,6},{8,9},{9,8},{10,11... | collective-permute-start | bytes 2433032 | tf_op jit(solution)/shard_map/ppermute | solution.py:50
  2.4 5.2 %collective-permute-start.1 = (bf16[256,768]{1,0:T(8,128)(2,1)S(1)}, bf16[256,768]{1,0:T(8,128)(2,1)S(1)}, u32[]{:S(2)}, u32[]{:S(2)}) collective-permute-start(bf16[256,768]{1,0:T(8,128)(2,1)S(1)} %copy-done.4), channel_id=1, source_target_pairs={{1,2},{3,4},{5,6},{9,10},{11,12},{13,14},{17,18},{19,20},{21,22},{... | collective-permute-start | bytes 1179656 | tf_op jit(solution)/shard_map/ppermute | solution.py:55
  4.7 15.0 %collective-permute-start.3 = (bf16[3,128,768]{2,1,0:T(8,128)(2,1)S(1)}, bf16[3,128,768]{2,1,0:T(8,128)(2,1)S(1)}, u32[]{:S(2)}, u32[]{:S(2)}) collective-permute-start(bf16[3,128,768]{2,1,0:T(8,128)(2,1)S(1)} %split.1.refs_1_), channel_id=1, source_target_pairs={{0,2},{1,5},{2,0},{3,7},{4,6},{5,1},{6,4},{7,3},{8,10},{9,13},{10,... | collective-permute-start | bytes 1769480 | tf_op jit(solution)/shard_map/ppermute | solution.py:50
  9.3 14.4 %collective-permute-start.2 = (bf16[256,768]{1,0:T(8,128)(2,1)S(1)}, bf16[256,768]{1,0:T(8,128)(2,1)S(1)}, u32[]{:S(2)}, u32[]{:S(2)}) collective-permute-start(bf16[256,768]{1,0:T(8,128)(2,1)S(1)} %get-tuple-element.27), channel_id=1, source_target_pairs={{1,2},{3,4},{5,6},{9,10},{11,12},{13,14},{17,18},{19,20},{21,22},{... | collective-permute-start | bytes 1179656 | tf_op jit(solution)/shard_map/ppermute | solution.py:55
  19.9 14.7 %collective-permute-start.4 = (bf16[3,128,768]{2,1,0:T(8,128)(2,1)S(1)}, bf16[3,128,768]{2,1,0:T(8,128)(2,1)S(1)}, u32[]{:S(2)}, u32[]{:S(2)}) collective-permute-start(bf16[3,128,768]{2,1,0:T(8,128)(2,1)S(1)} %step.1.refs_1_), channel_id=1, source_target_pairs={{0,4},{1,3},{2,6},{3,1},{4,0},{5,7},{6,2},{7,5},{8,12},{9,11},{10,... | collective-permute-start | bytes 1769480 | tf_op jit(solution)/shard_map/ppermute | solution.py:50
  25.0 17.6 %collective-permute-start.7 = (bf16[512,768]{1,0:T(8,128)(2,1)S(1)}, bf16[512,768]{1,0:T(8,128)(2,1)S(1)}, u32[]{:S(2)}, u32[]{:S(2)}) collective-permute-start(bf16[512,768]{1,0:T(8,128)(2,1)S(1)} %get-tuple-element.35), channel_id=1, source_target_pairs={{1,0},{2,1},{3,2},{4,3},{5,4},{6,5},{7,6},{9,8},{10,9},{11,10},{12... | collective-permute-start | bytes 2359304 | tf_op jit(solution)/shard_map/ppermute | solution.py:500
  35.0 5.5 %collective-permute-start.5 = (bf16[2,128,768]{2,1,0:T(8,128)(2,1)S(1)}, bf16[2,128,768]{2,1,0:T(8,128)(2,1)S(1)}, u32[]{:S(2)}, u32[]{:S(2)}) collective-permute-start(bf16[2,128,768]{2,1,0:T(8,128)(2,1)S(1)} %get-tuple-element.31), channel_id=1, source_target_pairs={{0,1},{1,0},{2,3},{3,2},{4,5},{5,4},{6,7},{7,6},{8,9},{9,8},{10,11... | collective-permute-start | bytes 1179656 | tf_op jit(solution)/shard_map/ppermute | solution.py:50
  42.2 1.8 %collective-permute-start.6 = (bf16[2,128,768]{2,1,0:T(8,128)(2,1)S(1)}, bf16[2,128,768]{2,1,0:T(8,128)(2,1)S(1)}, u32[]{:S(2)}, u32[]{:S(2)}) collective-permute-start(bf16[2,128,768]{2,1,0:T(8,128)(2,1)S(1)} %get-tuple-element.34), channel_id=1, source_target_pairs={{0,1},{1,0},{2,3},{3,2},{4,5},{5,4},{6,7},{7,6},{8,9},{9,8},{10,11... | collective-permute-start | bytes 1179656 | tf_op jit(solution)/shard_map/ppermute | solution.py:50
  44.7 9.9 %collective-permute-start.9 = (bf16[3,128,768]{2,1,0:T(8,128)(2,1)S(1)}, bf16[3,128,768]{2,1,0:T(8,128)(2,1)S(1)}, u32[]{:S(2)}, u32[]{:S(2)}) collective-permute-start(bf16[3,128,768]{2,1,0:T(8,128)(2,1)S(1)} %get-tuple-element.36.refs_9_), channel_id=1, source_target_pairs={{0,4},{1,3},{2,6},{3,1},{4,0},{5,7},{6,2},{7,5},{8,12},{9,11},{10,... | collective-permute-start | bytes 1769480 | tf_op jit(solution)/shard_map/ppermute | solution.py:50
  50.1 5.0 %collective-permute-start.8 = (f32[6,8,256]{2,1,0:T(8,128)S(1)}, f32[6,8,256]{2,1,0:T(8,128)S(1)}, u32[]{:S(2)}, u32[]{:S(2)}) collective-permute-start(f32[6,8,256]{2,1,0:T(8,128)S(1)} %get-tuple-element.39), channel_id=1, source_target_pairs={{1,0},{2,1},{3,2},{4,3},{5,4},{6,5},{7,6},{9,8},{10,9},{11,10},{12... | collective-permute-start | bytes 147464 | tf_op jit(solution)/shard_map/ppermute | solution.py:537
  54.8 9.9 %collective-permute-start.10 = (bf16[3,128,768]{2,1,0:T(8,128)(2,1)S(1)}, bf16[3,128,768]{2,1,0:T(8,128)(2,1)S(1)}, u32[]{:S(2)}, u32[]{:S(2)}) collective-permute-start(bf16[3,128,768]{2,1,0:T(8,128)(2,1)S(1)} %get-tuple-element.43), channel_id=1, source_target_pairs={{0,2},{1,5},{2,0},{3,7},{4,6},{5,1},{6,4},{7,3},{8,10},{9,13},{10,... | collective-permute-start | bytes 1769480 | tf_op jit(solution)/shard_map/ppermute | solution.py:50
  65.1 1.8 %collective-permute-start.11 = (bf16[2,128,768]{2,1,0:T(8,128)(2,1)S(1)}, bf16[2,128,768]{2,1,0:T(8,128)(2,1)S(1)}, u32[]{:S(2)}, u32[]{:S(2)}) collective-permute-start(bf16[2,128,768]{2,1,0:T(8,128)(2,1)S(1)} %get-tuple-element.45), channel_id=1, source_target_pairs={{0,1},{1,0},{2,3},{3,2},{4,5},{5,4},{6,7},{7,6},{8,9},{9,8},{10,11... | collective-permute-start | bytes 1179656 | tf_op jit(solution)/shard_map/ppermute | solution.py:50

commit v8 on v6

--- a/solution.py
+++ b/solution.py
@@ -157,10 +157,13 @@
 PREV, OWN, MEMORY, NEXT, PAIR = range(5)
 
 
-def plan_kernel(peers, last_bits, bank_ref, index_ref, pose_ref, bias_ref, pair_ref, rows_ref, codes_ref):
+def plan_kernel(
+    peers, last_bits, bank_ref, index_ref, pose_ref, bias_ref, pair_ref, joined_ref, rows_ref, codes_ref, values_out
+):
     me = lax.axis_index("tm")
     last_frame = peers * FR_DEV - 1
     heads, _, row_count = rows_ref.shape
+    values_out[...] = joined_ref[row_count : 2 * row_count, :]
     bank = [bank_ref[0, slot] for slot in range(bank_ref.shape[1])]
     tail = pair_ref.shape[0] - TAIL
     pair_ids = []
@@ -289,35 +292,23 @@
         ref[head, j : j + 1, :] = row
 
 
-def ahead_kernel(rows_ref, next_queries_ref, own_ref, part_ref):
-    heads = part_ref.shape[0]
-    for local in range(heads):
-        query, cotangent = joined_parts(next_queries_ref, head_cols(local))
-        keys, values = joined_parts(own_ref, head_cols(heads + local))
-        logits = logits_of(keys, query, rows_ref, heads + local, NEXT)
-        store_part(part_ref, local, part_of(logits, dot(values, cotangent, 1, 1)))
-
-
-def stats_kernel(rows_ref, queries_ref, outer_ref, pair_ref, own_ref, ahead_ref, part_ref, keys_out, queries_out):
-    me = lax.axis_index("tm")
-    even = (me & 1) == 0
+def prev_parts(outer_refs, pair_ref, cols):
+    even = (lax.axis_index("tm") & 1) == 0
+    parts = zip(outer_refs, joined_parts(pair_ref, cols))
+    return tuple(jnp.where(even, outer[:, cols], pair) for outer, pair in parts)
+
+
+def stats_kernel(rows_ref, queries_ref, outer_keys, outer_values, pair_ref, own_ref, part_ref, queries_out):
     heads = queries_ref.shape[1] // DEPTH
-    half = heads // 2
-    rows = queries_ref.shape[0]
-    half_width = half * DEPTH
-    keys_out[...] = own_ref[0:rows, half_width : 2 * half_width]
-    queries_out[...] = queries_ref[:, 0:half_width]
+    queries_out[...] = queries_ref[...]
 
     def products(head):
-        query, cotangent = joined_parts(queries_ref, head_cols(head))
-        prev = joined_parts(pair_ref, head_cols(head))
-        if head < half:
-            outer = joined_parts(outer_ref, head_cols(head))
-            prev = [jnp.where(even, there, here) for there, here in zip(outer, prev)]
-        own = joined_parts(own_ref, head_cols(head))
+        cols = head_cols(head)
+        query, cotangent = joined_parts(queries_ref, cols)
+        pieces = ((PREV, prev_parts((outer_keys, outer_values), pair_ref, cols)), (OWN, joined_parts(own_ref, cols)))
         return [
             (logits_of(keys, query, rows_ref, head, piece), dot(values, cotangent, 1, 1))
-            for piece, (keys, values) in ((PREV, prev), (OWN, own))
+            for piece, (keys, values) in pieces
         ]
 
     ahead = products(0)
@@ -325,12 +316,7 @@
         now = ahead
         if head + 1 < heads:
             ahead = products(head + 1)
-        prev, own = (part_of(*piece) for piece in now)
-        if head >= half:
-            there = load_part(ahead_ref, head - half)
-            there = (jnp.where(me == 0, BLOCKED_LOGIT, there[0]), *there[1:])
-            prev = tuple(jnp.where(even, a, b) for a, b in zip(there, prev))
-        store_part(part_ref, head, merged(prev, own))
+        store_part(part_ref, head, merged(*(part_of(*piece) for piece in now)))
 
 
 def rounded(part, logits, slopes):
@@ -387,16 +373,13 @@
         send_ref[place] = keep_ref[place if place + 1 < kept else kept].astype(BF16)
 
 
-def next_kernel(
-    rows_ref, stats_ref, pair_queries, outer_first, outer_second, own_ref, term_ref, sum_ref
-):
+def next_kernel(rows_ref, stats_ref, pair_queries, outer_queries, own_ref, term_ref, sum_ref):
     even = (lax.axis_index("tm") & 1) == 0
     heads = pair_queries.shape[1] // DEPTH
-    half = heads // 2
 
     def operands(head):
-        outer = joined_parts((outer_first, outer_second)[head // half], head_cols(head % half))
-        return [jnp.where(even, a, b) for a, b in zip(joined_parts(pair_queries, head_cols(head)), outer)]
+        cols = head_cols(head)
+        return [jnp.where(even, a, b) for a, b in zip(joined_parts(pair_queries, cols), joined_parts(outer_queries, cols))]
 
     def products(head):
         query, cotangent = operands(head)
@@ -419,8 +402,8 @@
     rows_ref,
     part_ref,
     queries_ref,
-    outer_first,
-    outer_second,
+    outer_keys,
+    outer_values,
     pair_ref,
     own_ref,
     own_mem,
@@ -437,8 +420,7 @@
 
     def pieces(head):
         cols = head_cols(head % half)
-        outer = joined_parts((outer_first, outer_second)[head // half], cols)
-        prev = [jnp.where(role == 0, a, b) for a, b in zip(outer, joined_parts(pair_ref, head_cols(head)))]
+        prev = prev_parts((outer_keys, outer_values), pair_ref, head_cols(head))
         memory = [
             jnp.where(role == head // half, own_mem[:, kind, :, cols], other_mem[:, kind, :, cols]).reshape(
                 MEM * frame_len, DEPTH
@@ -556,50 +538,47 @@
     )
     half_width = width // 2
     first, second = slice(0, half_width), slice(half_width, width)
-    outer_first = shift(joined[: 2 * row_count, first], 1, 1, peers)
+    outer_keys = shift(key_states, 1, 1, peers)
     pair = swap(joined, 1, 1, peers)
     held = shape(BF16, slots - 1, 2, frame_len, half_width)
     sums = shape(F32, slots - 1, 2, frame_len, half_width)
     (mine,) = call(functools.partial(split_kernel, peers), [held], [bank_frames, joined, pair], name="split")
     queries = join(join_queries_kernel, 2 * row_count, [query_states, grad_out], [], "join_queries", after=[mine])
     pair_queries = swap(queries, 1, 1, peers)
-    next_second = shift(queries[:, second], -1, 2, peers)
     own_half = jnp.where(even, queries[:, first], queries[:, second])
     pair_half = jnp.where(even, pair_queries[:, first], pair_queries[:, second])
 
     bias_rows = -(-(5 * FR_DEV) // 8) * 8
-    rows, codes = call(
+    rows, codes, values_out = call(
         functools.partial(plan_kernel, peers, last_bits),
-        [shape(F32, heads, bias_rows, row_count), shape(jnp.int32, 8, 128)],
-        [pair],
+        [shape(F32, heads, bias_rows, row_count), shape(jnp.int32, 8, 128), shape(BF16, row_count, width)],
+        [pair, joined],
         scalars=[bank_frames, memory_index, camera_pose, pose_bias],
-        after=[outer_first],
+        after=[outer_keys],
         flops=HIDING * piece_flops,
         name="plan",
     )
+    outer_values = shift(values_out, 1, 1, peers)
     even_done = odd_done = 1
     for step, (even_bit, odd_bit) in enumerate(turns):
         got = swap(mine, even_bit, odd_bit, peers)
         if step + 1 < len(turns):
             kernel = functools.partial(step_kernel, peers, even_done, odd_done)
-            after = [codes, pair_queries, next_second]
+            after = [codes, pair_queries]
             (mine,) = call(kernel, [held], [bank_frames, mine, got], after=after, name="step")
         even_done |= even_bit
         odd_done |= odd_bit
 
     stats = shape(F32, heads, 8, row_count)
-    half_joined = shape(BF16, 2 * row_count, half_width)
-    (ahead,) = call(ahead_kernel, [shape(F32, heads // 2, 8, row_count)], [rows, next_second, joined], name="ahead")
-    ahead = shift(ahead, 1, 1, peers)
-    part, keys_out, queries_out = call(
+    part, queries_out = call(
         stats_kernel,
-        [stats, half_joined, half_joined],
-        [rows, queries, outer_first, pair, joined, ahead],
+        [stats, shape(BF16, 2 * row_count, width)],
+        [rows, queries, outer_keys, outer_values, pair, joined],
+        flops=HIDING * piece_flops,
         name="stats",
     )
     pair_part = swap(part, 1, 1, peers)
-    outer_second = shift(keys_out, 1, 1, peers)
-    next_first = shift(queries_out, -1, 2, peers)
+    next_queries = shift(queries_out, -1, 2, peers)
     chosen = shape(BF16, MEM, 2, frame_len, half_width)
     own_mem, pair_mem = call(pick_kernel, [chosen] * 2, [codes, mine, got], name="pick")
     keep, send = call(
@@ -614,8 +593,8 @@
     attended, grad_query, own_terms, stats_all = call(
         rest_kernel,
         [shape(BF16, row_count, width)] * 2 + [pair_sums, stats],
-        [rows, part, queries, outer_first, outer_second, pair, joined, own_mem, other_mem],
-        after=[send, next_first],
+        [rows, part, queries, outer_keys, outer_values, pair, joined, own_mem, other_mem],
+        after=[send],
         flops=HIDING * piece_flops,
         name="rest",
     )
@@ -623,7 +602,7 @@
     (own,) = call(
         next_kernel,
         [pair_sums],
-        [rows, next_stats, pair_queries, next_first, next_second, joined, own_terms],
+        [rows, next_stats, pair_queries, next_queries, joined, own_terms],
         flops=HIDING * piece_flops,
         name="next",
     )

time: 73.8 us -> 66.2 us (0.90)
  starting transfers between devices: 37.5 us -> 22.4 us
  waiting for transfers between devices: 18.3 us -> 22.2 us
  Pallas kernels: 16.7 us -> 20.3 us
    ppermute x9, starting transfers between devices: 32.8 us -> 18.4 us  [swap(): lax.ppermute(block, 'tm', [(i, i ^ (odd_bit if i & 1 else even_bit)) for...]
    ppermute x9, waiting for transfers between devices: 18.3 us -> 22.2 us  [swap(): lax.ppermute(block, 'tm', [(i, i ^ (odd_bit if i & 1 else even_bit)) for...]
    pallas_call x12 -> x11, Pallas kernels: 14.5 us -> 17.9 us  [call(): pl.pallas_call(run, out_shape=outs, in_specs=[SMEM] * len(scalars) + [VME...]
    ppermute x5 -> x3, starting transfers between devices: 3.39 us -> 2.78 us  [shift(): return lax.ppermute(block, 'tm', pairs)]
  transfers between devices with their start and end apart: 15 -> 13, of which waited for: 5 -> 6; matrix products, arithmetic and copies ran while one was open for 0% -> 0% of each run, Pallas kernels for 19% -> 27%
where the time goes in v8:
time: 66.2 us; the launch traced here: 65.8 us
  starting transfers between devices  22.4 us (34%)
  waiting for transfers between devices  22.2 us (34%)
  Pallas kernels  20.3 us (31%)
  between operations  0.82 us (1%)
    ppermute x9, waiting for transfers between devices, swap(): lax.ppermute(block, 'tm', [(i, i ^ (odd_bit if i & 1 else even_bit)) for...  22.2 us
    ppermute x9, starting transfers between devices, swap(): lax.ppermute(block, 'tm', [(i, i ^ (odd_bit if i & 1 else even_bit)) for...  18.4 us
    pallas_call x11, Pallas kernels, call(): pl.pallas_call(run, out_shape=outs, in_specs=[SMEM] * len(scalars) + [VME...  17.9 us
    ppermute x3, starting transfers between devices, shift(): return lax.ppermute(block, 'tm', pairs)  2.78 us
    pallas_call x2, Pallas kernels, join(): pl.pallas_call(run, out_shape=shape(BF16, rows, width), in_specs=[pl.Bloc...  2.34 us
  transfers between devices with their start and end apart: 13, of which 6 were waited for; matrix products, arithmetic and copies ran while one was open for 0% of the time, Pallas kernels for 27%

profile of v8, /device:TPU:0, one launch (start us, length us, event | category | flops | bytes accessed | tf_op | source)
XLA Modules:
  0.0 65.8 jit_solution(7679419682607864894)
XLA Ops:
  0.6 0.0 copy-start.6
  0.6 0.0 copy-start.2
  0.7 1.2 %join.1.refs_5_.refs_1_.refs_6_.refs_4_ = bf16[528,768]{1,0:T(8,128)(2,1)S(1)} custom-call(s32[1,2]{1,0:T(1,128)} %refs_1_.4, bf16[256,768]{1,0:T(8,128)(2,1)} %refs_1_.3, bf16[256,768]{1,0:T(8,128)(2,1)} %refs_2_.2), custom_call_target="tpu_custom_call" | custom-call | tf_op jit(solution)/shard_map/join/pallas_call | solution.py:522
  1.9 0.5 collective-permute-start
  2.4 0.7 %collective-permute-start.1 = (bf16[256,768]{1,0:T(8,128)(2,1)S(1)}, bf16[256,768]{1,0:T(8,128)(2,1)S(1)}, u32[]{:S(2)}, u32[]{:S(2)}) collective-permute-start(bf16[256,768]{1,0:T(8,128)(2,1)S(1)} %copy-done.6), channel_id=1, source_target_pairs={{1,2},{3,4},{5,6},{9,10},{11,12},{13,14},{17,18},{19,20},{21,22},{... | collective-permute-start | bytes 1179656 | tf_op jit(solution)/shard_map/ppermute | solution.py:55
  3.1 1.3 %collective-permute-done.refs_4_.refs_2_.refs_5_ = bf16[528,768]{1,0:T(8,128)(2,1)S(1)} collective-permute-done((bf16[528,768]{1,0:T(8,128)(2,1)S(1)}, bf16[528,768]{1,0:T(8,128)(2,1)S(1)}, u32[]{:S(2)}, u32[]{:S(2)}) %collective-permute-start) | collective-permute-done | bytes 811040 | tf_op jit(solution)/shard_map/ppermute | solution.py:50
  4.3 0.0 copy-done.2
  4.3 0.3 split.1.refs_2_.refs_1_
  4.7 0.0 copy-start.3
  4.7 0.0 copy-start.4
  4.7 0.0 copy-start.5
  4.7 2.9 %collective-permute-start.3 = (bf16[3,2,128,384]{3,2,1,0:T(8,128)(2,1)S(1)}, bf16[3,2,128,384]{3,2,1,0:T(8,128)(2,1)}, u32[]{:S(2)}, u32[]{:S(2)}) collective-permute-start(bf16[3,2,128,384]{3,2,1,0:T(8,128)(2,1)S(1)} %split.1.refs_2_.refs_1_), channel_id=1, source_target_pairs={{0,2},{1,5},{2,0},{3,7},{4,6},{5,1},{6,4},{7,3},{8,10},{9,13},{10,... | collective-permute-start | bytes 1769480 | tf_op jit(solution)/shard_map/ppermute | solution.py:50
  7.6 1.1 %join_queries.1.refs_1_.refs_2_ = bf16[512,768]{1,0:T(8,128)(2,1)S(1)} custom-call(bf16[256,768]{1,0:T(8,128)(2,1)} %refs_0_.3, bf16[256,768]{1,0:T(8,128)(2,1)} %refs_1_.5, bf16[3,2,128,384]{3,2,1,0:T(8,128)(2,1)S(1)} %split.1.refs_2_.refs_1_), custom_call_target="tpu_custom_call" | custom-call | tf_op jit(solution)/shard_map/join_queries/pallas_call | solution.py:522
  8.8 1.1 %collective-permute-start.4 = (bf16[512,768]{1,0:T(8,128)(2,1)S(1)}, bf16[512,768]{1,0:T(8,128)(2,1)S(1)}, u32[]{:S(2)}, u32[]{:S(2)}) collective-permute-start(bf16[512,768]{1,0:T(8,128)(2,1)S(1)} %join_queries.1.refs_1_.refs_2_), channel_id=1, source_target_pairs={{0,1},{1,0},{2,3},{3,2},{4,5},{5,4},{6,7},{7,6},{8,9},{9,8},{10,11... | collective-permute-start | bytes 2359304 | tf_op jit(solution)/shard_map/ppermute | solution.py:50
  9.9 0.0 collective-permute-done.1.refs_6_.refs_2_.refs_3_
  9.9 0.0 copy-done
  9.9 2.4 %plan.1 = (f32[6,16,256]{2,1,0:T(8,128)S(1)}, s32[8,128]{1,0:T(8,128)S(1)}, bf16[256,768]{1,0:T(8,128)(2,1)}) custom-call(s32[1,4]{1,0:T(1,128)S(1)} %bitcast.2, s32[1,2]{1,0:T(1,128)S(1)} %copy-done.3, s32[16]{0:T(128)S(1)} %copy-done.5, f32[6,16,16]{2,1,0:T(8,128)S(1)} %copy-done.4, bf16[528,768]{1,0:T(8,128)(2,1)S(1)} %collective-permute-done.refs_4_.refs_2_.refs_5_, ...), custom_call_target="tpu_custom_call" | custom-call | flops 20132659200 | tf_op jit(solution)/shard_map/plan/pallas_call | solution.py:38
  12.3 1.4 %collective-permute-start.2 = (bf16[256,768]{1,0:T(8,128)(2,1)}, bf16[256,768]{1,0:T(8,128)(2,1)}, u32[]{:S(2)}, u32[]{:S(2)}) collective-permute-start(bf16[256,768]{1,0:T(8,128)(2,1)} %get-tuple-element.24), channel_id=1, source_target_pairs={{1,2},{3,4},{5,6},{9,10},{11,12},{13,14},{17,18},{19,20},{21,22},{... | collective-permute-start | bytes 1179656 | tf_op jit(solution)/shard_map/ppermute | solution.py:55
  13.8 6.0 %collective-permute-done.3.refs_2_ = bf16[3,2,128,384]{3,2,1,0:T(8,128)(2,1)} collective-permute-done((bf16[3,2,128,384]{3,2,1,0:T(8,128)(2,1)S(1)}, bf16[3,2,128,384]{3,2,1,0:T(8,128)(2,1)}, u32[]{:S(2)}, u32[]{:S(2)}) %collective-permute-start.3) | collective-permute-done | bytes 589856 | tf_op jit(solution)/shard_map/ppermute | solution.py:50
  19.8 0.0 collective-permute-done.4.refs_4_.refs_2_
  19.8 1.4 %step.1.refs_1_ = bf16[3,2,128,384]{3,2,1,0:T(8,128)(2,1)S(1)} custom-call(s32[1,4]{1,0:T(1,128)S(1)} %bitcast.3, bf16[3,2,128,384]{3,2,1,0:T(8,128)(2,1)S(1)} %split.1.refs_2_.refs_1_, bf16[3,2,128,384]{3,2,1,0:T(8,128)(2,1)} %collective-permute-done.3.refs_2_, s32[8,128]{1,0:T(8,128)S(1)} %get-tuple-element.26.refs_3_.refs_0_, ...), custom_call_target="tpu_custom_call" | custom-call | tf_op jit(solution)/shard_map/step/pallas_call | solution.py:38
  21.2 3.3 %collective-permute-start.5 = (bf16[3,2,128,384]{3,2,1,0:T(8,128)(2,1)S(1)}, bf16[3,2,128,384]{3,2,1,0:T(8,128)(2,1)S(1)}, u32[]{:S(2)}, u32[]{:S(2)}) collective-permute-start(bf16[3,2,128,384]{3,2,1,0:T(8,128)(2,1)S(1)} %step.1.refs_1_), channel_id=1, source_target_pairs={{0,4},{1,3},{2,6},{3,1},{4,0},{5,7},{6,2},{7,5},{8,12},{9,11},{10,... | collective-permute-start | bytes 1769480 | tf_op jit(solution)/shard_map/ppermute | solution.py:50
  24.5 0.0 collective-permute-done.2.refs_3_.refs_4_
  24.5 0.0 copy-done.1
  24.5 2.5 %stats.1 = (f32[6,8,256]{2,1,0:T(8,128)S(1)}, bf16[512,768]{1,0:T(8,128)(2,1)S(1)}) custom-call(f32[6,16,256]{2,1,0:T(8,128)S(1)} %get-tuple-element.23.refs_0_.refs_1_, bf16[512,768]{1,0:T(8,128)(2,1)S(1)} %join_queries.1.refs_1_.refs_2_, bf16[256,768]{1,0:T(8,128)(2,1)S(1)} %collective-permute-done.1.refs_6_.refs_2_.refs_3_, ...), custom_call_target="tpu_custom_call" | custom-call | flops 20132659200 | tf_op jit(solution)/shard_map/stats/pallas_call | solution.py:38
  26.9 2.7 %collective-permute-start.7 = (f32[6,8,256]{2,1,0:T(8,128)S(1)}, f32[6,8,256]{2,1,0:T(8,128)S(1)}, u32[]{:S(2)}, u32[]{:S(2)}) collective-permute-start(f32[6,8,256]{2,1,0:T(8,128)S(1)} %get-tuple-element.25.refs_2_.refs_1_), channel_id=1, source_target_pairs={{0,1},{1,0},{2,3},{3,2},{4,5},{5,4},{6,7},{7,6},{8,9},{9,8},{10,11... | collective-permute-start | bytes 147464 | tf_op jit(solution)/shard_map/ppermute | solution.py:50
  29.6 0.7 %collective-permute-start.9 = (bf16[512,768]{1,0:T(8,128)(2,1)S(1)}, bf16[512,768]{1,0:T(8,128)(2,1)S(1)}, u32[]{:S(2)}, u32[]{:S(2)}) collective-permute-start(bf16[512,768]{1,0:T(8,128)(2,1)S(1)} %get-tuple-element.33), channel_id=1, source_target_pairs={{2,1},{4,3},{6,5},{10,9},{12,11},{14,13},{18,17},{20,19},{22,21},{... | collective-permute-start | bytes 2359304 | tf_op jit(solution)/shard_map/ppermute | solution.py:55
  30.4 0.1 slice_select_fusion.refs_5_
  30.4 5.2 %collective-permute-done.5.refs_2_ = bf16[3,2,128,384]{3,2,1,0:T(8,128)(2,1)S(1)} collective-permute-done((bf16[3,2,128,384]{3,2,1,0:T(8,128)(2,1)S(1)}, bf16[3,2,128,384]{3,2,1,0:T(8,128)(2,1)S(1)}, u32[]{:S(2)}, u32[]{:S(2)}) %collective-permute-start.5) | collective-permute-done | bytes 589856 | tf_op jit(solution)/shard_map/ppermute | solution.py:50
  35.6 0.3 pick.1
  35.9 2.1 %collective-permute-start.6 = (bf16[2,2,128,384]{3,2,1,0:T(8,128)(2,1)S(1)}, bf16[2,2,128,384]{3,2,1,0:T(8,128)(2,1)S(1)}, u32[]{:S(2)}, u32[]{:S(2)}) collective-permute-start(bf16[2,2,128,384]{3,2,1,0:T(8,128)(2,1)S(1)} %get-tuple-element.28.refs_7_), channel_id=1, source_target_pairs={{0,1},{1,0},{2,3},{3,2},{4,5},{5,4},{6,7},{7,6},{8,9},{9,8},{10,11... | collective-permute-start | bytes 1179656 | tf_op jit(solution)/shard_map/ppermute | solution.py:50
  38.0 0.0 collective-permute-done.7.refs_3_
  38.0 1.8 %memory.1 = (f32[4,2,128,384]{3,2,1,0:T(8,128)S(1)}, bf16[3,2,128,384]{3,2,1,0:T(8,128)(2,1)S(1)}) custom-call(s32[8,128]{1,0:T(8,128)S(1)} %get-tuple-element.26.refs_3_.refs_0_, f32[6,16,256]{2,1,0:T(8,128)S(1)} %get-tuple-element.23.refs_0_.refs_1_, f32[6,8,256]{2,1,0:T(8,128)S(1)} %get-tuple-element.25.refs_2_.refs_1_, ...), custom_call_target="tpu_custom_call" | custom-call | flops 20132659200 | tf_op jit(solution)/shard_map/memory/pallas_call | solution.py:38
  39.9 0.6 collective-permute-start.10
  40.4 0.0 collective-permute-done.6.refs_8_
  40.4 6.5 %rest.1 = (bf16[256,768]{1,0:T(8,128)(2,1)}, bf16[256,768]{1,0:T(8,128)(2,1)}, f32[2,256,768]{2,1,0:T(8,128)S(1)}, f32[6,8,256]{2,1,0:T(8,128)S(1)}) custom-call(f32[6,16,256]{2,1,0:T(8,128)S(1)} %get-tuple-element.23.refs_0_.refs_1_, f32[6,8,256]{2,1,0:T(8,128)S(1)} %get-tuple-element.25.refs_2_.refs_1_, bf16[512,768]{1,0:T(8,128)(2,1)S(1)} %join_queries.1.refs_1_.refs_2_, ...), custom_call_target="tpu_custom_call" | custom-call | flops 20132659200 | tf_op jit(solution)/shard_map/rest/pallas_call | solution.py:38
  46.9 1.3 %collective-permute-start.8 = (f32[6,8,256]{2,1,0:T(8,128)S(1)}, f32[6,8,256]{2,1,0:T(8,128)S(1)}, u32[]{:S(2)}, u32[]{:S(2)}) collective-permute-start(f32[6,8,256]{2,1,0:T(8,128)S(1)} %get-tuple-element.32), channel_id=1, source_target_pairs={{1,0},{2,1},{3,2},{4,3},{5,4},{6,5},{7,6},{9,8},{10,9},{11,10},{12... | collective-permute-start | bytes 147464 | tf_op jit(solution)/shard_map/ppermute | solution.py:601
  48.2 1.6 %collective-permute-done.10.refs_1_ = bf16[3,2,128,384]{3,2,1,0:T(8,128)(2,1)S(1)} collective-permute-done((bf16[3,2,128,384]{3,2,1,0:T(8,128)(2,1)S(1)}, bf16[3,2,128,384]{3,2,1,0:T(8,128)(2,1)S(1)}, u32[]{:S(2)}, u32[]{:S(2)}) %collective-permute-start.10) | collective-permute-done | bytes 589856 | tf_op jit(solution)/shard_map/ppermute | solution.py:50
  49.8 0.2 add.1
  50.0 3.8 %collective-permute-start.11 = (bf16[3,2,128,384]{3,2,1,0:T(8,128)(2,1)S(1)}, bf16[3,2,128,384]{3,2,1,0:T(8,128)(2,1)S(1)}, u32[]{:S(2)}, u32[]{:S(2)}) collective-permute-start(bf16[3,2,128,384]{3,2,1,0:T(8,128)(2,1)S(1)} %get-tuple-element.37), channel_id=1, source_target_pairs={{0,2},{1,5},{2,0},{3,7},{4,6},{5,1},{6,4},{7,3},{8,10},{9,13},{10,... | collective-permute-start | bytes 1769480 | tf_op jit(solution)/shard_map/ppermute | solution.py:50
  53.9 0.0 collective-permute-done.9.refs_3_
  53.9 0.0 collective-permute-done.8.refs_1_
  53.9 1.2 %next.1.refs_3_.refs_0_ = f32[2,256,768]{2,1,0:T(8,128)S(1)} custom-call(f32[6,16,256]{2,1,0:T(8,128)S(1)} %get-tuple-element.23.refs_0_.refs_1_, f32[6,8,256]{2,1,0:T(8,128)S(1)} %collective-permute-done.8.refs_1_, bf16[512,768]{1,0:T(8,128)(2,1)S(1)} %collective-permute-done.4.refs_4_.refs_2_, bf16[512,768]{1,0:T(8,128)(2,1)S(1)} %collective-permute-done.9.refs_3_, ...), custom_call_target="tpu_custom_call" | custom-call | flops 20132659200 | tf_op jit(solution)/shard_map/next/pallas_call | solution.py:38
  55.0 6.7 %collective-permute-done.11.refs_2_ = bf16[3,2,128,384]{3,2,1,0:T(8,128)(2,1)S(1)} collective-permute-done((bf16[3,2,128,384]{3,2,1,0:T(8,128)(2,1)S(1)}, bf16[3,2,128,384]{3,2,1,0:T(8,128)(2,1)S(1)}, u32[]{:S(2)}, u32[]{:S(2)}) %collective-permute-start.11) | collective-permute-done | bytes 589856 | tf_op jit(solution)/shard_map/ppermute | solution.py:50
  61.7 0.3 owned.1
  62.0 1.4 %collective-permute-start.12 = (bf16[2,2,128,384]{3,2,1,0:T(8,128)(2,1)S(1)}, bf16[2,2,128,384]{3,2,1,0:T(8,128)(2,1)S(1)}, u32[]{:S(2)}, u32[]{:S(2)}) collective-permute-start(bf16[2,2,128,384]{3,2,1,0:T(8,128)(2,1)S(1)} %get-tuple-element.39), channel_id=1, source_target_pairs={{0,1},{1,0},{2,3},{3,2},{4,5},{5,4},{6,7},{7,6},{8,9},{9,8},{10,11... | collective-permute-start | bytes 1179656 | tf_op jit(solution)/shard_map/ppermute | solution.py:50
  63.5 1.3 %collective-permute-done.12.refs_2_ = bf16[2,2,128,384]{3,2,1,0:T(8,128)(2,1)S(1)} collective-permute-done((bf16[2,2,128,384]{3,2,1,0:T(8,128)(2,1)S(1)}, bf16[2,2,128,384]{3,2,1,0:T(8,128)(2,1)S(1)}, u32[]{:S(2)}, u32[]{:S(2)}) %collective-permute-start.12) | collective-permute-done | bytes 393248 | tf_op jit(solution)/shard_map/ppermute | solution.py:50
  64.8 1.0 %final.1 = (bf16[256,768]{1,0:T(8,128)(2,1)}, bf16[256,768]{1,0:T(8,128)(2,1)}) custom-call(f32[2,256,768]{2,1,0:T(8,128)S(1)} %next.1.refs_3_.refs_0_, f32[2,2,128,384]{3,2,1,0:T(8,128)S(1)} %get-tuple-element.38.refs_1_, bf16[2,2,128,384]{3,2,1,0:T(8,128)(2,1)S(1)} %collective-permute-done.12.refs_2_), custom_call_target="tpu_custom_call" | custom-call | tf_op jit(solution)/shard_map/final/pallas_call | solution.py:38
  (7 shorter events, 0.1 us)
Async XLA Ops:
  0.6 1.8 %copy-start.6 = (bf16[256,768]{1,0:T(8,128)(2,1)S(1)}, bf16[256,768]{1,0:T(8,128)(2,1)}, u32[]{:S(2)}) copy-start(bf16[256,768]{1,0:T(8,128)(2,1)} %refs_1_.3) | copy-start | bytes 1179652
  0.6 3.7 %copy-start.2 = (s32[4]{0:T(128)S(1)}, s32[4]{0:T(128)}, u32[]{:S(2)}) copy-start(s32[4]{0:T(128)} %param.15) | copy-start | bytes 52
  1.9 2.5 %collective-permute-start = (bf16[528,768]{1,0:T(8,128)(2,1)S(1)}, bf16[528,768]{1,0:T(8,128)(2,1)S(1)}, u32[]{:S(2)}, u32[]{:S(2)}) collective-permute-start(bf16[528,768]{1,0:T(8,128)(2,1)S(1)} %join.1.refs_5_.refs_1_.refs_6_.refs_4_), channel_id=1, source_target_pairs={{0,1},{1,0},{2,3},{3,2},{4,5},{5,4},{6,7},{7,6},{8,9},{9,8},{10,11... | collective-permute-start | bytes 2433032 | tf_op jit(solution)/shard_map/ppermute | solution.py:50
  2.4 7.5 %collective-permute-start.1 = (bf16[256,768]{1,0:T(8,128)(2,1)S(1)}, bf16[256,768]{1,0:T(8,128)(2,1)S(1)}, u32[]{:S(2)}, u32[]{:S(2)}) collective-permute-start(bf16[256,768]{1,0:T(8,128)(2,1)S(1)} %copy-done.6), channel_id=1, source_target_pairs={{1,2},{3,4},{5,6},{9,10},{11,12},{13,14},{17,18},{19,20},{21,22},{... | collective-permute-start | bytes 1179656 | tf_op jit(solution)/shard_map/ppermute | solution.py:55
  4.3 5.5 %copy-start = (bf16[528,768]{1,0:T(8,128)(2,1)}, bf16[528,768]{1,0:T(8,128)(2,1)S(1)}, u32[]{:S(2)}) copy-start(bf16[528,768]{1,0:T(8,128)(2,1)S(1)} %collective-permute-done.refs_4_.refs_2_.refs_5_) | copy-start | bytes 2433028
  4.7 5.2 %copy-start.3 = (s32[1,2]{1,0:T(1,128)S(1)}, s32[1,2]{1,0:T(1,128)}, u32[]{:S(2)}) copy-start(s32[1,2]{1,0:T(1,128)} %refs_1_.4) | copy-start | bytes 28
  4.7 5.2 %copy-start.4 = (f32[6,16,16]{2,1,0:T(8,128)S(1)}, f32[6,16,16]{2,1,0:T(8,128)}, u32[]{:S(2)}) copy-start(f32[6,16,16]{2,1,0:T(8,128)} %refs_3_.1) | copy-start | bytes 18436
  4.7 5.2 %copy-start.5 = (s32[16]{0:T(128)S(1)}, s32[16]{0:T(128)}, u32[]{:S(2)}) copy-start(s32[16]{0:T(128)} %refs_2_.3) | copy-start | bytes 196
  4.7 15.1 %collective-permute-start.3 = (bf16[3,2,128,384]{3,2,1,0:T(8,128)(2,1)S(1)}, bf16[3,2,128,384]{3,2,1,0:T(8,128)(2,1)}, u32[]{:S(2)}, u32[]{:S(2)}) collective-permute-start(bf16[3,2,128,384]{3,2,1,0:T(8,128)(2,1)S(1)} %split.1.refs_2_.refs_1_), channel_id=1, source_target_pairs={{0,2},{1,5},{2,0},{3,7},{4,6},{5,1},{6,4},{7,3},{8,10},{9,13},{10,... | collective-permute-start | bytes 1769480 | tf_op jit(solution)/shard_map/ppermute | solution.py:50
  8.8 11.0 %collective-permute-start.4 = (bf16[512,768]{1,0:T(8,128)(2,1)S(1)}, bf16[512,768]{1,0:T(8,128)(2,1)S(1)}, u32[]{:S(2)}, u32[]{:S(2)}) collective-permute-start(bf16[512,768]{1,0:T(8,128)(2,1)S(1)} %join_queries.1.refs_1_.refs_2_), channel_id=1, source_target_pairs={{0,1},{1,0},{2,3},{3,2},{4,5},{5,4},{6,7},{7,6},{8,9},{9,8},{10,11... | collective-permute-start | bytes 2359304 | tf_op jit(solution)/shard_map/ppermute | solution.py:50
  12.3 12.1 %collective-permute-start.2 = (bf16[256,768]{1,0:T(8,128)(2,1)}, bf16[256,768]{1,0:T(8,128)(2,1)}, u32[]{:S(2)}, u32[]{:S(2)}) collective-permute-start(bf16[256,768]{1,0:T(8,128)(2,1)} %get-tuple-element.24), channel_id=1, source_target_pairs={{1,2},{3,4},{5,6},{9,10},{11,12},{13,14},{17,18},{19,20},{21,22},{... | collective-permute-start | bytes 1179656 | tf_op jit(solution)/shard_map/ppermute | solution.py:55
  13.8 10.7 %copy-start.1 = (bf16[528,768]{1,0:T(8,128)(2,1)S(1)}, bf16[528,768]{1,0:T(8,128)(2,1)}, u32[]{:S(2)}) copy-start(bf16[528,768]{1,0:T(8,128)(2,1)} %copy-done) | copy-start | bytes 2433028
  21.2 14.4 %collective-permute-start.5 = (bf16[3,2,128,384]{3,2,1,0:T(8,128)(2,1)S(1)}, bf16[3,2,128,384]{3,2,1,0:T(8,128)(2,1)S(1)}, u32[]{:S(2)}, u32[]{:S(2)}) collective-permute-start(bf16[3,2,128,384]{3,2,1,0:T(8,128)(2,1)S(1)} %step.1.refs_1_), channel_id=1, source_target_pairs={{0,4},{1,3},{2,6},{3,1},{4,0},{5,7},{6,2},{7,5},{8,12},{9,11},{10,... | collective-permute-start | bytes 1769480 | tf_op jit(solution)/shard_map/ppermute | solution.py:50
  26.9 11.1 %collective-permute-start.7 = (f32[6,8,256]{2,1,0:T(8,128)S(1)}, f32[6,8,256]{2,1,0:T(8,128)S(1)}, u32[]{:S(2)}, u32[]{:S(2)}) collective-permute-start(f32[6,8,256]{2,1,0:T(8,128)S(1)} %get-tuple-element.25.refs_2_.refs_1_), channel_id=1, source_target_pairs={{0,1},{1,0},{2,3},{3,2},{4,5},{5,4},{6,7},{7,6},{8,9},{9,8},{10,11... | collective-permute-start | bytes 147464 | tf_op jit(solution)/shard_map/ppermute | solution.py:50
  29.6 24.2 %collective-permute-start.9 = (bf16[512,768]{1,0:T(8,128)(2,1)S(1)}, bf16[512,768]{1,0:T(8,128)(2,1)S(1)}, u32[]{:S(2)}, u32[]{:S(2)}) collective-permute-start(bf16[512,768]{1,0:T(8,128)(2,1)S(1)} %get-tuple-element.33), channel_id=1, source_target_pairs={{2,1},{4,3},{6,5},{10,9},{12,11},{14,13},{18,17},{20,19},{22,21},{... | collective-permute-start | bytes 2359304 | tf_op jit(solution)/shard_map/ppermute | solution.py:55
  35.9 4.5 %collective-permute-start.6 = (bf16[2,2,128,384]{3,2,1,0:T(8,128)(2,1)S(1)}, bf16[2,2,128,384]{3,2,1,0:T(8,128)(2,1)S(1)}, u32[]{:S(2)}, u32[]{:S(2)}) collective-permute-start(bf16[2,2,128,384]{3,2,1,0:T(8,128)(2,1)S(1)} %get-tuple-element.28.refs_7_), channel_id=1, source_target_pairs={{0,1},{1,0},{2,3},{3,2},{4,5},{5,4},{6,7},{7,6},{8,9},{9,8},{10,11... | collective-permute-start | bytes 1179656 | tf_op jit(solution)/shard_map/ppermute | solution.py:50
  39.9 9.9 %collective-permute-start.10 = (bf16[3,2,128,384]{3,2,1,0:T(8,128)(2,1)S(1)}, bf16[3,2,128,384]{3,2,1,0:T(8,128)(2,1)S(1)}, u32[]{:S(2)}, u32[]{:S(2)}) collective-permute-start(bf16[3,2,128,384]{3,2,1,0:T(8,128)(2,1)S(1)} %get-tuple-element.29.refs_9_), channel_id=1, source_target_pairs={{0,4},{1,3},{2,6},{3,1},{4,0},{5,7},{6,2},{7,5},{8,12},{9,11},{10,... | collective-permute-start | bytes 1769480 | tf_op jit(solution)/shard_map/ppermute | solution.py:50
  46.9 7.0 %collective-permute-start.8 = (f32[6,8,256]{2,1,0:T(8,128)S(1)}, f32[6,8,256]{2,1,0:T(8,128)S(1)}, u32[]{:S(2)}, u32[]{:S(2)}) collective-permute-start(f32[6,8,256]{2,1,0:T(8,128)S(1)} %get-tuple-element.32), channel_id=1, source_target_pairs={{1,0},{2,1},{3,2},{4,3},{5,4},{6,5},{7,6},{9,8},{10,9},{11,10},{12... | collective-permute-start | bytes 147464 | tf_op jit(solution)/shard_map/ppermute | solution.py:601
  50.0 11.7 %collective-permute-start.11 = (bf16[3,2,128,384]{3,2,1,0:T(8,128)(2,1)S(1)}, bf16[3,2,128,384]{3,2,1,0:T(8,128)(2,1)S(1)}, u32[]{:S(2)}, u32[]{:S(2)}) collective-permute-start(bf16[3,2,128,384]{3,2,1,0:T(8,128)(2,1)S(1)} %get-tuple-element.37), channel_id=1, source_target_pairs={{0,2},{1,5},{2,0},{3,7},{4,6},{5,1},{6,4},{7,3},{8,10},{9,13},{10,... | collective-permute-start | bytes 1769480 | tf_op jit(solution)/shard_map/ppermute | solution.py:50
  62.0 2.8 %collective-permute-start.12 = (bf16[2,2,128,384]{3,2,1,0:T(8,128)(2,1)S(1)}, bf16[2,2,128,384]{3,2,1,0:T(8,128)(2,1)S(1)}, u32[]{:S(2)}, u32[]{:S(2)}) collective-permute-start(bf16[2,2,128,384]{3,2,1,0:T(8,128)(2,1)S(1)} %get-tuple-element.39), channel_id=1, source_target_pairs={{0,1},{1,0},{2,3},{3,2},{4,5},{5,4},{6,7},{7,6},{8,9},{9,8},{10,11... | collective-permute-start | bytes 1179656 | tf_op jit(solution)/shard_map/ppermute | solution.py:50

commit v9 on v8

--- a/solution.py
+++ b/solution.py
@@ -21,7 +21,7 @@
 VMEM = pl.BlockSpec(memory_space=pltpu.VMEM)
 ANY = pl.BlockSpec(memory_space=pl.ANY)
 HIDING = 200
-VMEM_LIMIT = 32 * 1024 * 1024
+VMEM_LIMIT = 16 * 1024 * 1024
 BF16, F32 = jnp.bfloat16, jnp.float32
 
 
@@ -53,6 +53,27 @@
 def shift(block, by, start, peers):
     pairs = [(i, i + by) for i in range(start, peers, 2) if 0 <= i + by < peers]
     return lax.ppermute(block, "tm", pairs)
+
+
+def relays_of(by, start, peers):
+    pairs = [(i, i + by) for i in range(start, peers, 2) if 0 <= i + by < peers]
+    return {(i, j): i ^ 4 for i, j in pairs if peers == 8 and (i ^ j) >> 1 == 3}
+
+
+def shift_first(block, by, start, peers):
+    relays = relays_of(by, start, peers)
+    pairs = [(i, i + by) for i in range(start, peers, 2) if 0 <= i + by < peers]
+    return lax.ppermute(block, "tm", [(i, relays.get((i, j), j)) for i, j in pairs])
+
+
+def shift_second(block, by, start, peers):
+    pairs = [(relay, j) for (_, j), relay in relays_of(by, start, peers).items()]
+    return lax.ppermute(block, "tm", pairs) if pairs else block
+
+
+def through_relay(by, start, peers):
+    me = lax.axis_index("tm")
+    return functools.reduce(jnp.logical_or, [me == j for _, j in relays_of(by, start, peers)], me < 0)
 
 
 def lane_value(row, lane):
@@ -158,12 +179,25 @@
 
 
 def plan_kernel(
-    peers, last_bits, bank_ref, index_ref, pose_ref, bias_ref, pair_ref, joined_ref, rows_ref, codes_ref, values_out
+    peers,
+    last_bits,
+    bank_ref,
+    index_ref,
+    pose_ref,
+    bias_ref,
+    pair_ref,
+    joined_ref,
+    direct_keys,
+    rows_ref,
+    codes_ref,
+    values_out,
+    keys_out,
 ):
     me = lax.axis_index("tm")
     last_frame = peers * FR_DEV - 1
     heads, _, row_count = rows_ref.shape
     values_out[...] = joined_ref[row_count : 2 * row_count, :]
+    keys_out[...] = direct_keys[...]
     bank = [bank_ref[0, slot] for slot in range(bank_ref.shape[1])]
     tail = pair_ref.shape[0] - TAIL
     pair_ids = []
@@ -292,20 +326,35 @@
         ref[head, j : j + 1, :] = row
 
 
-def prev_parts(outer_refs, pair_ref, cols):
+def prev_parts(peers, direct_keys, relayed_keys, outer_values, pair_ref, cols):
     even = (lax.axis_index("tm") & 1) == 0
-    parts = zip(outer_refs, joined_parts(pair_ref, cols))
-    return tuple(jnp.where(even, outer[:, cols], pair) for outer, pair in parts)
-
-
-def stats_kernel(rows_ref, queries_ref, outer_keys, outer_values, pair_ref, own_ref, part_ref, queries_out):
+    keys = jnp.where(through_relay(1, 1, peers), relayed_keys[:, cols], direct_keys[:, cols])
+    parts = zip((keys, outer_values[:, cols]), joined_parts(pair_ref, cols))
+    return tuple(jnp.where(even, outer, pair) for outer, pair in parts)
+
+
+def stats_kernel(
+    peers,
+    rows_ref,
+    queries_ref,
+    direct_keys,
+    relayed_keys,
+    outer_values,
+    pair_ref,
+    own_ref,
+    part_ref,
+    queries_out,
+    cotangent_out,
+):
     heads = queries_ref.shape[1] // DEPTH
-    queries_out[...] = queries_ref[...]
+    rows = queries_out.shape[0]
+    queries_out[...] = queries_ref[0:rows]
+    cotangent_out[...] = queries_ref[rows : 2 * rows]
 
     def products(head):
         cols = head_cols(head)
         query, cotangent = joined_parts(queries_ref, cols)
-        pieces = ((PREV, prev_parts((outer_keys, outer_values), pair_ref, cols)), (OWN, joined_parts(own_ref, cols)))
+        pieces = ((PREV, prev_parts(peers, direct_keys, relayed_keys, outer_values, pair_ref, cols)), (OWN, joined_parts(own_ref, cols)))
         return [
             (logits_of(keys, query, rows_ref, head, piece), dot(values, cotangent, 1, 1))
             for piece, (keys, values) in pieces
@@ -373,13 +422,27 @@
         send_ref[place] = keep_ref[place if place + 1 < kept else kept].astype(BF16)
 
 
-def next_kernel(rows_ref, stats_ref, pair_queries, outer_queries, own_ref, term_ref, sum_ref):
+def next_kernel(
+    peers,
+    rows_ref,
+    stats_ref,
+    pair_queries,
+    outer_queries,
+    direct_cotangent,
+    relayed_cotangent,
+    own_ref,
+    term_ref,
+    sum_ref,
+):
     even = (lax.axis_index("tm") & 1) == 0
+    relayed = through_relay(-1, 2, peers)
     heads = pair_queries.shape[1] // DEPTH
 
     def operands(head):
         cols = head_cols(head)
-        return [jnp.where(even, a, b) for a, b in zip(joined_parts(pair_queries, cols), joined_parts(outer_queries, cols))]
+        cotangent = jnp.where(relayed, relayed_cotangent[:, cols], direct_cotangent[:, cols])
+        outer = outer_queries[:, cols], cotangent
+        return [jnp.where(even, a, b) for a, b in zip(joined_parts(pair_queries, cols), outer)]
 
     def products(head):
         query, cotangent = operands(head)
@@ -399,28 +462,33 @@
 
 
 def rest_kernel(
+    peers,
     rows_ref,
     part_ref,
     queries_ref,
-    outer_keys,
+    direct_keys,
+    relayed_keys,
     outer_values,
     pair_ref,
     own_ref,
     own_mem,
     other_mem,
+    passed_ref,
     attended_ref,
     grad_query_ref,
     term_ref,
     stats_ref,
+    passed_out,
 ):
     role = lax.axis_index("tm") & 1
     frame_len, half_width = own_mem.shape[2:]
     heads = queries_ref.shape[1] // DEPTH
     half = half_width // DEPTH
+    passed_out[...] = passed_ref[...]
 
     def pieces(head):
         cols = head_cols(head % half)
-        prev = prev_parts((outer_keys, outer_values), pair_ref, head_cols(head))
+        prev = prev_parts(peers, direct_keys, relayed_keys, outer_values, pair_ref, head_cols(head))
         memory = [
             jnp.where(role == head // half, own_mem[:, kind, :, cols], other_mem[:, kind, :, cols]).reshape(
                 MEM * frame_len, DEPTH
@@ -538,7 +606,7 @@
     )
     half_width = width // 2
     first, second = slice(0, half_width), slice(half_width, width)
-    outer_keys = shift(key_states, 1, 1, peers)
+    direct_keys = shift_first(key_states, 1, 1, peers)
     pair = swap(joined, 1, 1, peers)
     held = shape(BF16, slots - 1, 2, frame_len, half_width)
     sums = shape(F32, slots - 1, 2, frame_len, half_width)
@@ -549,16 +617,15 @@
     pair_half = jnp.where(even, pair_queries[:, first], pair_queries[:, second])
 
     bias_rows = -(-(5 * FR_DEV) // 8) * 8
-    rows, codes, values_out = call(
+    rows, codes, values_out, keys_out = call(
         functools.partial(plan_kernel, peers, last_bits),
-        [shape(F32, heads, bias_rows, row_count), shape(jnp.int32, 8, 128), shape(BF16, row_count, width)],
-        [pair, joined],
+        [shape(F32, heads, bias_rows, row_count), shape(jnp.int32, 8, 128)] + [shape(BF16, row_count, width)] * 2,
+        [pair, joined, direct_keys],
         scalars=[bank_frames, memory_index, camera_pose, pose_bias],
-        after=[outer_keys],
         flops=HIDING * piece_flops,
         name="plan",
     )
-    outer_values = shift(values_out, 1, 1, peers)
+    outer = [direct_keys, shift_second(keys_out, 1, 1, peers), shift(values_out, 1, 1, peers)]
     even_done = odd_done = 1
     for step, (even_bit, odd_bit) in enumerate(turns):
         got = swap(mine, even_bit, odd_bit, peers)
@@ -570,15 +637,16 @@
         odd_done |= odd_bit
 
     stats = shape(F32, heads, 8, row_count)
-    part, queries_out = call(
-        stats_kernel,
-        [stats, shape(BF16, 2 * row_count, width)],
-        [rows, queries, outer_keys, outer_values, pair, joined],
+    part, queries_out, cotangent_out = call(
+        functools.partial(stats_kernel, peers),
+        [stats] + [shape(BF16, row_count, width)] * 2,
+        [rows, queries, *outer, pair, joined],
         flops=HIDING * piece_flops,
         name="stats",
     )
     pair_part = swap(part, 1, 1, peers)
     next_queries = shift(queries_out, -1, 2, peers)
+    direct_cotangent = shift_first(cotangent_out, -1, 2, peers)
     chosen = shape(BF16, MEM, 2, frame_len, half_width)
     own_mem, pair_mem = call(pick_kernel, [chosen] * 2, [codes, mine, got], name="pick")
     keep, send = call(
@@ -590,19 +658,20 @@
     )
     other_mem = swap(pair_mem, 1, 1, peers)
     pair_sums = shape(F32, 2, row_count, width)
-    attended, grad_query, own_terms, stats_all = call(
-        rest_kernel,
-        [shape(BF16, row_count, width)] * 2 + [pair_sums, stats],
-        [rows, part, queries, outer_keys, outer_values, pair, joined, own_mem, other_mem],
+    attended, grad_query, own_terms, stats_all, passed_on = call(
+        functools.partial(rest_kernel, peers),
+        [shape(BF16, row_count, width)] * 2 + [pair_sums, stats, shape(BF16, row_count, width)],
+        [rows, part, queries, *outer, pair, joined, own_mem, other_mem, direct_cotangent],
         after=[send],
         flops=HIDING * piece_flops,
         name="rest",
     )
     next_stats = lax.ppermute(stats_all, "tm", [(i, i - 1) for i in range(1, peers)])
+    relayed_cotangent = shift_second(passed_on, -1, 2, peers)
     (own,) = call(
-        next_kernel,
+        functools.partial(next_kernel, peers),
         [pair_sums],
-        [rows, next_stats, pair_queries, next_queries, joined, own_terms],
+        [rows, next_stats, pair_queries, next_queries, direct_cotangent, relayed_cotangent, joined, own_terms],
         flops=HIDING * piece_flops,
         name="next",
     )

time: 66.2 us -> 63.2 us (0.955)
  waiting for transfers between devices: 22.2 us -> 13.2 us
  starting transfers between devices: 22.4 us -> 27.8 us
    ppermute x9, waiting for transfers between devices: 22.2 us -> 10.6 us  [swap(): lax.ppermute(block, 'tm', [(i, i ^ (odd_bit if i & 1 else even_bit)) for...]
    ppermute x0 -> x4, starting transfers between devices: none -> 4.68 us  [the longest x2 2.73 us: shift_second(): return lax.ppermute(block, 'tm', pairs) if pairs else block]
    ppermute x0 -> x4, waiting for transfers between devices: none -> 2.65 us  [the longest x2 1.98 us: shift_second(): return lax.ppermute(block, 'tm', pairs) if pairs else block]
    ppermute x9, starting transfers between devices: 18.4 us -> 19.7 us  [swap(): lax.ppermute(block, 'tm', [(i, i ^ (odd_bit if i & 1 else even_bit)) for...]
    ppermute x3 -> x2, starting transfers between devices: 2.78 us -> 2.08 us  [shift(): return lax.ppermute(block, 'tm', pairs)]
  transfers between devices with their start and end apart: 13 -> 16, of which waited for: 6 -> 6; matrix products, arithmetic and copies ran while one was open for 0% -> 0% of each run, Pallas kernels for 27% -> 29%
where the time goes in v9:
time: 63.2 us; the launch traced here: 62.8 us
  starting transfers between devices  27.8 us (44%)
  Pallas kernels  20.8 us (33%)
  waiting for transfers between devices  13.2 us (21%)
  between operations  0.86 us (1%)
    ppermute x9, starting transfers between devices, swap(): lax.ppermute(block, 'tm', [(i, i ^ (odd_bit if i & 1 else even_bit)) for...  19.7 us
    pallas_call x11, Pallas kernels, call(): pl.pallas_call(run, out_shape=outs, in_specs=[SMEM] * len(scalars) + [VME...  18.5 us
    ppermute x9, waiting for transfers between devices, swap(): lax.ppermute(block, 'tm', [(i, i ^ (odd_bit if i & 1 else even_bit)) for...  10.6 us
    ppermute x2, starting transfers between devices, shift_second(): return lax.ppermute(block, 'tm', pairs) if pairs else block  2.73 us
    pallas_call x2, Pallas kernels, join(): pl.pallas_call(run, out_shape=shape(BF16, rows, width), in_specs=[pl.Bloc...  2.34 us
    ppermute x2, starting transfers between devices, shift(): return lax.ppermute(block, 'tm', pairs)  2.08 us
    ppermute x2, waiting for transfers between devices, shift_second(): return lax.ppermute(block, 'tm', pairs) if pairs else block  1.98 us
    ppermute x2, starting transfers between devices, shift_first(): lax.ppermute(block, 'tm', [(i, relays.get((i, j), j)) for i, j in pairs])  1.95 us
  transfers between devices with their start and end apart: 16, of which 6 were waited for; matrix products, arithmetic and copies ran while one was open for 0% of the time, Pallas kernels for 29%

profile of v9, /device:TPU:0, one launch (start us, length us, event | category | flops | bytes accessed | tf_op | source)
XLA Modules:
  0.0 62.8 jit_solution(12755638402575298351)
XLA Ops:
  0.7 1.2 %join.1.refs_5_.refs_1_.refs_6_.refs_7_ = bf16[528,768]{1,0:T(8,128)(2,1)S(1)} custom-call(s32[1,2]{1,0:T(1,128)} %refs_1_.4, bf16[256,768]{1,0:T(8,128)(2,1)} %refs_1_.3, bf16[256,768]{1,0:T(8,128)(2,1)} %refs_2_.2), custom_call_target="tpu_custom_call" | custom-call | tf_op jit(solution)/shard_map/join/pallas_call | solution.py:590
  1.9 0.5 collective-permute-start
  2.4 0.7 %collective-permute-start.1 = (bf16[256,768]{1,0:T(8,128)(2,1)S(1)}, bf16[256,768]{1,0:T(8,128)(2,1)S(1)}, u32[]{:S(2)}, u32[]{:S(2)}) collective-permute-start(bf16[256,768]{1,0:T(8,128)(2,1)S(1)} %copy-done.6), channel_id=1, source_target_pairs={{1,2},{3,7},{5,6},{9,10},{11,15},{13,14},{17,18},{19,23},{21,22},{... | collective-permute-start | bytes 1179656 | tf_op jit(solution)/shard_map/ppermute | solution.py:66
  3.1 1.3 %collective-permute-done.refs_4_.refs_2_.refs_5_.refs_6_ = bf16[528,768]{1,0:T(8,128)(2,1)S(1)} collective-permute-done((bf16[528,768]{1,0:T(8,128)(2,1)S(1)}, bf16[528,768]{1,0:T(8,128)(2,1)S(1)}, u32[]{:S(2)}, u32[]{:S(2)}) %collective-permute-start) | collective-permute-done | bytes 811040 | tf_op jit(solution)/shard_map/ppermute | solution.py:50
  4.3 0.3 split.1.refs_2_.refs_1_
  4.7 0.0 copy-start.3
  4.7 0.0 copy-start.4
  4.7 0.0 copy-start.5
  4.7 2.9 %collective-permute-start.4 = (bf16[3,2,128,384]{3,2,1,0:T(8,128)(2,1)S(1)}, bf16[3,2,128,384]{3,2,1,0:T(8,128)(2,1)}, u32[]{:S(2)}, u32[]{:S(2)}) collective-permute-start(bf16[3,2,128,384]{3,2,1,0:T(8,128)(2,1)S(1)} %split.1.refs_2_.refs_1_), channel_id=1, source_target_pairs={{0,2},{1,5},{2,0},{3,7},{4,6},{5,1},{6,4},{7,3},{8,10},{9,13},{10,... | collective-permute-start | bytes 1769480 | tf_op jit(solution)/shard_map/ppermute | solution.py:50
  7.6 1.1 %join_queries.1.refs_1_.refs_2_ = bf16[512,768]{1,0:T(8,128)(2,1)S(1)} custom-call(bf16[256,768]{1,0:T(8,128)(2,1)} %refs_0_.3, bf16[256,768]{1,0:T(8,128)(2,1)} %refs_1_.5, bf16[3,2,128,384]{3,2,1,0:T(8,128)(2,1)S(1)} %split.1.refs_2_.refs_1_), custom_call_target="tpu_custom_call" | custom-call | tf_op jit(solution)/shard_map/join_queries/pallas_call | solution.py:590
  8.8 1.1 %collective-permute-start.5 = (bf16[512,768]{1,0:T(8,128)(2,1)S(1)}, bf16[512,768]{1,0:T(8,128)(2,1)S(1)}, u32[]{:S(2)}, u32[]{:S(2)}) collective-permute-start(bf16[512,768]{1,0:T(8,128)(2,1)S(1)} %join_queries.1.refs_1_.refs_2_), channel_id=1, source_target_pairs={{0,1},{1,0},{2,3},{3,2},{4,5},{5,4},{6,7},{7,6},{8,9},{9,8},{10,11... | collective-permute-start | bytes 2359304 | tf_op jit(solution)/shard_map/ppermute | solution.py:50
  9.9 0.0 collective-permute-done.1.refs_6_.refs_2_.refs_3_
  9.9 2.6 %plan.1 = (f32[6,16,256]{2,1,0:T(8,128)S(1)}, s32[8,128]{1,0:T(8,128)S(1)}, bf16[256,768]{1,0:T(8,128)(2,1)}, bf16[256,768]{1,0:T(8,128)(2,1)}) custom-call(s32[1,4]{1,0:T(1,128)S(1)} %bitcast.2, s32[1,2]{1,0:T(1,128)S(1)} %copy-done.3, s32[16]{0:T(128)S(1)} %copy-done.5, f32[6,16,16]{2,1,0:T(8,128)S(1)} %copy-done.4, ...), custom_call_target="tpu_custom_call" | custom-call | flops 20132659200 | tf_op jit(solution)/shard_map/plan/pallas_call | solution.py:38
  12.4 1.4 %collective-permute-start.2 = (bf16[256,768]{1,0:T(8,128)(2,1)}, bf16[256,768]{1,0:T(8,128)(2,1)}, u32[]{:S(2)}, u32[]{:S(2)}) collective-permute-start(bf16[256,768]{1,0:T(8,128)(2,1)} %get-tuple-element.27), channel_id=1, source_target_pairs={{7,4},{15,12},{23,20},{31,28}} | collective-permute-start | bytes 1179656 | tf_op jit(solution)/shard_map/ppermute | solution.py:71
  13.9 1.4 %collective-permute-start.3 = (bf16[256,768]{1,0:T(8,128)(2,1)}, bf16[256,768]{1,0:T(8,128)(2,1)}, u32[]{:S(2)}, u32[]{:S(2)}) collective-permute-start(bf16[256,768]{1,0:T(8,128)(2,1)} %get-tuple-element.28), channel_id=1, source_target_pairs={{1,2},{3,4},{5,6},{9,10},{11,12},{13,14},{17,18},{19,20},{21,22},{... | collective-permute-start | bytes 1179656 | tf_op jit(solution)/shard_map/ppermute | solution.py:55
  15.3 2.5 %collective-permute-done.4.refs_2_ = bf16[3,2,128,384]{3,2,1,0:T(8,128)(2,1)} collective-permute-done((bf16[3,2,128,384]{3,2,1,0:T(8,128)(2,1)S(1)}, bf16[3,2,128,384]{3,2,1,0:T(8,128)(2,1)}, u32[]{:S(2)}, u32[]{:S(2)}) %collective-permute-start.4) | collective-permute-done | bytes 589856 | tf_op jit(solution)/shard_map/ppermute | solution.py:50
  17.8 0.0 collective-permute-done.5.refs_4_.refs_2_
  17.8 1.4 %step.1.refs_1_ = bf16[3,2,128,384]{3,2,1,0:T(8,128)(2,1)S(1)} custom-call(s32[1,4]{1,0:T(1,128)S(1)} %bitcast.3, bf16[3,2,128,384]{3,2,1,0:T(8,128)(2,1)S(1)} %split.1.refs_2_.refs_1_, bf16[3,2,128,384]{3,2,1,0:T(8,128)(2,1)} %collective-permute-done.4.refs_2_, s32[8,128]{1,0:T(8,128)S(1)} %get-tuple-element.30.refs_3_.refs_0_, ...), custom_call_target="tpu_custom_call" | custom-call | tf_op jit(solution)/shard_map/step/pallas_call | solution.py:38
  19.2 1.6 %collective-permute-start.6 = (bf16[3,2,128,384]{3,2,1,0:T(8,128)(2,1)S(1)}, bf16[3,2,128,384]{3,2,1,0:T(8,128)(2,1)S(1)}, u32[]{:S(2)}, u32[]{:S(2)}) collective-permute-start(bf16[3,2,128,384]{3,2,1,0:T(8,128)(2,1)S(1)} %step.1.refs_1_), channel_id=1, source_target_pairs={{0,4},{1,3},{2,6},{3,1},{4,0},{5,7},{6,2},{7,5},{8,12},{9,11},{10,... | collective-permute-start | bytes 1769480 | tf_op jit(solution)/shard_map/ppermute | solution.py:50
  20.8 0.0 collective-permute-done.2.refs_3_.refs_4_
  20.8 0.0 collective-permute-done.3.refs_4_.refs_5_
  20.8 2.6 %stats.1 = (f32[6,8,256]{2,1,0:T(8,128)S(1)}, bf16[256,768]{1,0:T(8,128)(2,1)S(1)}, bf16[256,768]{1,0:T(8,128)(2,1)S(1)}) custom-call(f32[6,16,256]{2,1,0:T(8,128)S(1)} %get-tuple-element.26.refs_0_.refs_1_, bf16[512,768]{1,0:T(8,128)(2,1)S(1)} %join_queries.1.refs_1_.refs_2_, bf16[256,768]{1,0:T(8,128)(2,1)S(1)} %collective-permute-done.1.refs_6_.refs_2_.refs_3_, ...), custom_call_target="tpu_custom_call" | custom-call | flops 20132659200 | tf_op jit(solution)/shard_map/stats/pallas_call | solution.py:38
  23.4 7.0 %collective-permute-start.9 = (f32[6,8,256]{2,1,0:T(8,128)S(1)}, f32[6,8,256]{2,1,0:T(8,128)S(1)}, u32[]{:S(2)}, u32[]{:S(2)}) collective-permute-start(f32[6,8,256]{2,1,0:T(8,128)S(1)} %get-tuple-element.29.refs_2_.refs_1_), channel_id=1, source_target_pairs={{0,1},{1,0},{2,3},{3,2},{4,5},{5,4},{6,7},{7,6},{8,9},{9,8},{10,11... | collective-permute-start | bytes 147464 | tf_op jit(solution)/shard_map/ppermute | solution.py:50
  30.5 1.3 %collective-permute-start.8 = (bf16[256,768]{1,0:T(8,128)(2,1)S(1)}, bf16[256,768]{1,0:T(8,128)(2,1)S(1)}, u32[]{:S(2)}, u32[]{:S(2)}) collective-permute-start(bf16[256,768]{1,0:T(8,128)(2,1)S(1)} %get-tuple-element.33), channel_id=1, source_target_pairs={{2,1},{4,0},{6,5},{10,9},{12,8},{14,13},{18,17},{20,16},{22,21},{2... | collective-permute-start | bytes 1179656 | tf_op jit(solution)/shard_map/ppermute | solution.py:66
  31.8 0.7 %collective-permute-start.11 = (bf16[256,768]{1,0:T(8,128)(2,1)S(1)}, bf16[256,768]{1,0:T(8,128)(2,1)S(1)}, u32[]{:S(2)}, u32[]{:S(2)}) collective-permute-start(bf16[256,768]{1,0:T(8,128)(2,1)S(1)} %get-tuple-element.38), channel_id=1, source_target_pairs={{2,1},{4,3},{6,5},{10,9},{12,11},{14,13},{18,17},{20,19},{22,21},{... | collective-permute-start | bytes 1179656 | tf_op jit(solution)/shard_map/ppermute | solution.py:55
  32.4 0.1 slice_select_fusion.refs_5_
  32.5 0.0 collective-permute-done.6.refs_2_
  32.5 0.3 pick.1
  32.8 1.5 %collective-permute-start.7 = (bf16[2,2,128,384]{3,2,1,0:T(8,128)(2,1)S(1)}, bf16[2,2,128,384]{3,2,1,0:T(8,128)(2,1)S(1)}, u32[]{:S(2)}, u32[]{:S(2)}) collective-permute-start(bf16[2,2,128,384]{3,2,1,0:T(8,128)(2,1)S(1)} %get-tuple-element.32.refs_7_), channel_id=1, source_target_pairs={{0,1},{1,0},{2,3},{3,2},{4,5},{5,4},{6,7},{7,6},{8,9},{9,8},{10,11... | collective-permute-start | bytes 1179656 | tf_op jit(solution)/shard_map/ppermute | solution.py:50
  34.3 0.0 collective-permute-done.9.refs_3_
  34.3 1.9 %memory.1 = (f32[4,2,128,384]{3,2,1,0:T(8,128)S(1)}, bf16[3,2,128,384]{3,2,1,0:T(8,128)(2,1)S(1)}) custom-call(s32[8,128]{1,0:T(8,128)S(1)} %get-tuple-element.30.refs_3_.refs_0_, f32[6,16,256]{2,1,0:T(8,128)S(1)} %get-tuple-element.26.refs_0_.refs_1_, f32[6,8,256]{2,1,0:T(8,128)S(1)} %get-tuple-element.29.refs_2_.refs_1_, ...), custom_call_target="tpu_custom_call" | custom-call | flops 20132659200 | tf_op jit(solution)/shard_map/memory/pallas_call | solution.py:38
  36.2 3.2 %collective-permute-start.13 = (bf16[3,2,128,384]{3,2,1,0:T(8,128)(2,1)S(1)}, bf16[3,2,128,384]{3,2,1,0:T(8,128)(2,1)S(1)}, u32[]{:S(2)}, u32[]{:S(2)}) collective-permute-start(bf16[3,2,128,384]{3,2,1,0:T(8,128)(2,1)S(1)} %get-tuple-element.34.refs_11_), channel_id=1, source_target_pairs={{0,4},{1,3},{2,6},{3,1},{4,0},{5,7},{6,2},{7,5},{8,12},{9,11},{10,... | collective-permute-start | bytes 1769480 | tf_op jit(solution)/shard_map/ppermute | solution.py:50
  39.5 0.7 %collective-permute-done.8.refs_10_.refs_4_ = bf16[256,768]{1,0:T(8,128)(2,1)S(1)} collective-permute-done((bf16[256,768]{1,0:T(8,128)(2,1)S(1)}, bf16[256,768]{1,0:T(8,128)(2,1)S(1)}, u32[]{:S(2)}, u32[]{:S(2)}) %collective-permute-start.8) | collective-permute-done | bytes 393248 | tf_op jit(solution)/shard_map/ppermute | solution.py:66
  40.1 0.0 collective-permute-done.7.refs_9_
  40.1 6.6 %rest.1 = (bf16[256,768]{1,0:T(8,128)(2,1)}, bf16[256,768]{1,0:T(8,128)(2,1)}, f32[2,256,768]{2,1,0:T(8,128)S(1)}, f32[6,8,256]{2,1,0:T(8,128)S(1)}, bf16[256,768]{1,0:T(8,128)(2,1)S(1)}) custom-call(f32[6,16,256]{2,1,0:T(8,128)S(1)} %get-tuple-element.26.refs_0_.refs_1_, f32[6,8,256]{2,1,0:T(8,128)S(1)} %get-tuple-element.29.refs_2_.refs_1_, ...), custom_call_target="tpu_custom_call" | custom-call | flops 20132659200 | tf_op jit(solution)/shard_map/rest/pallas_call | solution.py:38
  46.8 1.3 %collective-permute-start.12 = (bf16[256,768]{1,0:T(8,128)(2,1)S(1)}, bf16[256,768]{1,0:T(8,128)(2,1)S(1)}, u32[]{:S(2)}, u32[]{:S(2)}) collective-permute-start(bf16[256,768]{1,0:T(8,128)(2,1)S(1)} %get-tuple-element.39), channel_id=1, source_target_pairs={{0,3},{8,11},{16,19},{24,27}} | collective-permute-start | bytes 1179656 | tf_op jit(solution)/shard_map/ppermute | solution.py:71
  48.1 1.3 %collective-permute-start.10 = (f32[6,8,256]{2,1,0:T(8,128)S(1)}, f32[6,8,256]{2,1,0:T(8,128)S(1)}, u32[]{:S(2)}, u32[]{:S(2)}) collective-permute-start(f32[6,8,256]{2,1,0:T(8,128)S(1)} %get-tuple-element.37), channel_id=1, source_target_pairs={{1,0},{2,1},{3,2},{4,3},{5,4},{6,5},{7,6},{9,8},{10,9},{11,10},{12... | collective-permute-start | bytes 147464 | tf_op jit(solution)/shard_map/ppermute | solution.py:669
  49.4 0.0 collective-permute-done.13.refs_1_
  49.4 0.2 add.1
  49.6 1.8 %collective-permute-start.14 = (bf16[3,2,128,384]{3,2,1,0:T(8,128)(2,1)S(1)}, bf16[3,2,128,384]{3,2,1,0:T(8,128)(2,1)S(1)}, u32[]{:S(2)}, u32[]{:S(2)}) collective-permute-start(bf16[3,2,128,384]{3,2,1,0:T(8,128)(2,1)S(1)} %get-tuple-element.43), channel_id=1, source_target_pairs={{0,2},{1,5},{2,0},{3,7},{4,6},{5,1},{6,4},{7,3},{8,10},{9,13},{10,... | collective-permute-start | bytes 1769480 | tf_op jit(solution)/shard_map/ppermute | solution.py:50
  51.4 0.0 collective-permute-done.11.refs_3_
  51.4 2.0 %collective-permute-done.12.refs_5_ = bf16[256,768]{1,0:T(8,128)(2,1)S(1)} collective-permute-done((bf16[256,768]{1,0:T(8,128)(2,1)S(1)}, bf16[256,768]{1,0:T(8,128)(2,1)S(1)}, u32[]{:S(2)}, u32[]{:S(2)}) %collective-permute-start.12) | collective-permute-done | bytes 393248 | tf_op jit(solution)/shard_map/ppermute | solution.py:71
  53.3 1.2 %next.1.refs_3_.refs_0_ = f32[2,256,768]{2,1,0:T(8,128)S(1)} custom-call(f32[6,16,256]{2,1,0:T(8,128)S(1)} %get-tuple-element.26.refs_0_.refs_1_, f32[6,8,256]{2,1,0:T(8,128)S(1)} %collective-permute-done.10.refs_1_, bf16[512,768]{1,0:T(8,128)(2,1)S(1)} %collective-permute-done.5.refs_4_.refs_2_, bf16[256,768]{1,0:T(8,128)(2,1)S(1)} %collective-permute-done.11.refs_3_, ...), custom_call_target="tpu_custom_call" | custom-call | flops 20132659200 | tf_op jit(solution)/shard_map/next/pallas_call | solution.py:38
  54.6 5.1 %collective-permute-done.14.refs_2_ = bf16[3,2,128,384]{3,2,1,0:T(8,128)(2,1)S(1)} collective-permute-done((bf16[3,2,128,384]{3,2,1,0:T(8,128)(2,1)S(1)}, bf16[3,2,128,384]{3,2,1,0:T(8,128)(2,1)S(1)}, u32[]{:S(2)}, u32[]{:S(2)}) %collective-permute-start.14) | collective-permute-done | bytes 589856 | tf_op jit(solution)/shard_map/ppermute | solution.py:50
  59.7 0.4 owned.1
  60.0 0.1 collective-permute-start.15
  60.1 1.7 %collective-permute-done.15.refs_2_ = bf16[2,2,128,384]{3,2,1,0:T(8,128)(2,1)S(1)} collective-permute-done((bf16[2,2,128,384]{3,2,1,0:T(8,128)(2,1)S(1)}, bf16[2,2,128,384]{3,2,1,0:T(8,128)(2,1)S(1)}, u32[]{:S(2)}, u32[]{:S(2)}) %collective-permute-start.15) | collective-permute-done | bytes 393248 | tf_op jit(solution)/shard_map/ppermute | solution.py:50
  61.8 1.0 %final.1 = (bf16[256,768]{1,0:T(8,128)(2,1)}, bf16[256,768]{1,0:T(8,128)(2,1)}) custom-call(f32[2,256,768]{2,1,0:T(8,128)S(1)} %next.1.refs_3_.refs_0_, f32[2,2,128,384]{3,2,1,0:T(8,128)S(1)} %get-tuple-element.44.refs_1_, bf16[2,2,128,384]{3,2,1,0:T(8,128)(2,1)S(1)} %collective-permute-done.15.refs_2_), custom_call_target="tpu_custom_call" | custom-call | tf_op jit(solution)/shard_map/final/pallas_call | solution.py:38
  (13 shorter events, 0.1 us)
Async XLA Ops:
  0.6 1.8 %copy-start.6 = (bf16[256,768]{1,0:T(8,128)(2,1)S(1)}, bf16[256,768]{1,0:T(8,128)(2,1)}, u32[]{:S(2)}) copy-start(bf16[256,768]{1,0:T(8,128)(2,1)} %refs_1_.3) | copy-start | bytes 1179652
  0.6 3.7 %copy-start.2 = (s32[4]{0:T(128)S(1)}, s32[4]{0:T(128)}, u32[]{:S(2)}) copy-start(s32[4]{0:T(128)} %param.15) | copy-start | bytes 52
  1.9 2.5 %collective-permute-start = (bf16[528,768]{1,0:T(8,128)(2,1)S(1)}, bf16[528,768]{1,0:T(8,128)(2,1)S(1)}, u32[]{:S(2)}, u32[]{:S(2)}) collective-permute-start(bf16[528,768]{1,0:T(8,128)(2,1)S(1)} %join.1.refs_5_.refs_1_.refs_6_.refs_7_), channel_id=1, source_target_pairs={{0,1},{1,0},{2,3},{3,2},{4,5},{5,4},{6,7},{7,6},{8,9},{9,8},{10,11... | collective-permute-start | bytes 2433032 | tf_op jit(solution)/shard_map/ppermute | solution.py:50
  2.4 7.5 %collective-permute-start.1 = (bf16[256,768]{1,0:T(8,128)(2,1)S(1)}, bf16[256,768]{1,0:T(8,128)(2,1)S(1)}, u32[]{:S(2)}, u32[]{:S(2)}) collective-permute-start(bf16[256,768]{1,0:T(8,128)(2,1)S(1)} %copy-done.6), channel_id=1, source_target_pairs={{1,2},{3,7},{5,6},{9,10},{11,15},{13,14},{17,18},{19,23},{21,22},{... | collective-permute-start | bytes 1179656 | tf_op jit(solution)/shard_map/ppermute | solution.py:66
  4.3 5.5 %copy-start = (bf16[528,768]{1,0:T(8,128)(2,1)}, bf16[528,768]{1,0:T(8,128)(2,1)S(1)}, u32[]{:S(2)}) copy-start(bf16[528,768]{1,0:T(8,128)(2,1)S(1)} %collective-permute-done.refs_4_.refs_2_.refs_5_.refs_6_) | copy-start | bytes 2433028
  4.7 5.2 %copy-start.3 = (s32[1,2]{1,0:T(1,128)S(1)}, s32[1,2]{1,0:T(1,128)}, u32[]{:S(2)}) copy-start(s32[1,2]{1,0:T(1,128)} %refs_1_.4) | copy-start | bytes 28
  4.7 5.2 %copy-start.4 = (f32[6,16,16]{2,1,0:T(8,128)S(1)}, f32[6,16,16]{2,1,0:T(8,128)}, u32[]{:S(2)}) copy-start(f32[6,16,16]{2,1,0:T(8,128)} %refs_3_.1) | copy-start | bytes 18436
  4.7 5.2 %copy-start.5 = (s32[16]{0:T(128)S(1)}, s32[16]{0:T(128)}, u32[]{:S(2)}) copy-start(s32[16]{0:T(128)} %refs_2_.3) | copy-start | bytes 196
  4.7 13.1 %collective-permute-start.4 = (bf16[3,2,128,384]{3,2,1,0:T(8,128)(2,1)S(1)}, bf16[3,2,128,384]{3,2,1,0:T(8,128)(2,1)}, u32[]{:S(2)}, u32[]{:S(2)}) collective-permute-start(bf16[3,2,128,384]{3,2,1,0:T(8,128)(2,1)S(1)} %split.1.refs_2_.refs_1_), channel_id=1, source_target_pairs={{0,2},{1,5},{2,0},{3,7},{4,6},{5,1},{6,4},{7,3},{8,10},{9,13},{10,... | collective-permute-start | bytes 1769480 | tf_op jit(solution)/shard_map/ppermute | solution.py:50
  8.8 9.1 %collective-permute-start.5 = (bf16[512,768]{1,0:T(8,128)(2,1)S(1)}, bf16[512,768]{1,0:T(8,128)(2,1)S(1)}, u32[]{:S(2)}, u32[]{:S(2)}) collective-permute-start(bf16[512,768]{1,0:T(8,128)(2,1)S(1)} %join_queries.1.refs_1_.refs_2_), channel_id=1, source_target_pairs={{0,1},{1,0},{2,3},{3,2},{4,5},{5,4},{6,7},{7,6},{8,9},{9,8},{10,11... | collective-permute-start | bytes 2359304 | tf_op jit(solution)/shard_map/ppermute | solution.py:50
  12.4 8.3 %collective-permute-start.2 = (bf16[256,768]{1,0:T(8,128)(2,1)}, bf16[256,768]{1,0:T(8,128)(2,1)}, u32[]{:S(2)}, u32[]{:S(2)}) collective-permute-start(bf16[256,768]{1,0:T(8,128)(2,1)} %get-tuple-element.27), channel_id=1, source_target_pairs={{7,4},{15,12},{23,20},{31,28}} | collective-permute-start | bytes 1179656 | tf_op jit(solution)/shard_map/ppermute | solution.py:71
  13.9 6.9 %collective-permute-start.3 = (bf16[256,768]{1,0:T(8,128)(2,1)}, bf16[256,768]{1,0:T(8,128)(2,1)}, u32[]{:S(2)}, u32[]{:S(2)}) collective-permute-start(bf16[256,768]{1,0:T(8,128)(2,1)} %get-tuple-element.28), channel_id=1, source_target_pairs={{1,2},{3,4},{5,6},{9,10},{11,12},{13,14},{17,18},{19,20},{21,22},{... | collective-permute-start | bytes 1179656 | tf_op jit(solution)/shard_map/ppermute | solution.py:55
  15.3 5.5 %copy-start.1 = (bf16[528,768]{1,0:T(8,128)(2,1)S(1)}, bf16[528,768]{1,0:T(8,128)(2,1)}, u32[]{:S(2)}) copy-start(bf16[528,768]{1,0:T(8,128)(2,1)} %copy-done) | copy-start | bytes 2433028
  19.2 13.3 %collective-permute-start.6 = (bf16[3,2,128,384]{3,2,1,0:T(8,128)(2,1)S(1)}, bf16[3,2,128,384]{3,2,1,0:T(8,128)(2,1)S(1)}, u32[]{:S(2)}, u32[]{:S(2)}) collective-permute-start(bf16[3,2,128,384]{3,2,1,0:T(8,128)(2,1)S(1)} %step.1.refs_1_), channel_id=1, source_target_pairs={{0,4},{1,3},{2,6},{3,1},{4,0},{5,7},{6,2},{7,5},{8,12},{9,11},{10,... | collective-permute-start | bytes 1769480 | tf_op jit(solution)/shard_map/ppermute | solution.py:50
  23.4 10.9 %collective-permute-start.9 = (f32[6,8,256]{2,1,0:T(8,128)S(1)}, f32[6,8,256]{2,1,0:T(8,128)S(1)}, u32[]{:S(2)}, u32[]{:S(2)}) collective-permute-start(f32[6,8,256]{2,1,0:T(8,128)S(1)} %get-tuple-element.29.refs_2_.refs_1_), channel_id=1, source_target_pairs={{0,1},{1,0},{2,3},{3,2},{4,5},{5,4},{6,7},{7,6},{8,9},{9,8},{10,11... | collective-permute-start | bytes 147464 | tf_op jit(solution)/shard_map/ppermute | solution.py:50
  30.5 9.7 %collective-permute-start.8 = (bf16[256,768]{1,0:T(8,128)(2,1)S(1)}, bf16[256,768]{1,0:T(8,128)(2,1)S(1)}, u32[]{:S(2)}, u32[]{:S(2)}) collective-permute-start(bf16[256,768]{1,0:T(8,128)(2,1)S(1)} %get-tuple-element.33), channel_id=1, source_target_pairs={{2,1},{4,0},{6,5},{10,9},{12,8},{14,13},{18,17},{20,16},{22,21},{2... | collective-permute-start | bytes 1179656 | tf_op jit(solution)/shard_map/ppermute | solution.py:66
  31.8 19.6 %collective-permute-start.11 = (bf16[256,768]{1,0:T(8,128)(2,1)S(1)}, bf16[256,768]{1,0:T(8,128)(2,1)S(1)}, u32[]{:S(2)}, u32[]{:S(2)}) collective-permute-start(bf16[256,768]{1,0:T(8,128)(2,1)S(1)} %get-tuple-element.38), channel_id=1, source_target_pairs={{2,1},{4,3},{6,5},{10,9},{12,11},{14,13},{18,17},{20,19},{22,21},{... | collective-permute-start | bytes 1179656 | tf_op jit(solution)/shard_map/ppermute | solution.py:55
  32.8 7.3 %collective-permute-start.7 = (bf16[2,2,128,384]{3,2,1,0:T(8,128)(2,1)S(1)}, bf16[2,2,128,384]{3,2,1,0:T(8,128)(2,1)S(1)}, u32[]{:S(2)}, u32[]{:S(2)}) collective-permute-start(bf16[2,2,128,384]{3,2,1,0:T(8,128)(2,1)S(1)} %get-tuple-element.32.refs_7_), channel_id=1, source_target_pairs={{0,1},{1,0},{2,3},{3,2},{4,5},{5,4},{6,7},{7,6},{8,9},{9,8},{10,11... | collective-permute-start | bytes 1179656 | tf_op jit(solution)/shard_map/ppermute | solution.py:50
  36.2 13.1 %collective-permute-start.13 = (bf16[3,2,128,384]{3,2,1,0:T(8,128)(2,1)S(1)}, bf16[3,2,128,384]{3,2,1,0:T(8,128)(2,1)S(1)}, u32[]{:S(2)}, u32[]{:S(2)}) collective-permute-start(bf16[3,2,128,384]{3,2,1,0:T(8,128)(2,1)S(1)} %get-tuple-element.34.refs_11_), channel_id=1, source_target_pairs={{0,4},{1,3},{2,6},{3,1},{4,0},{5,7},{6,2},{7,5},{8,12},{9,11},{10,... | collective-permute-start | bytes 1769480 | tf_op jit(solution)/shard_map/ppermute | solution.py:50
  46.8 6.6 %collective-permute-start.12 = (bf16[256,768]{1,0:T(8,128)(2,1)S(1)}, bf16[256,768]{1,0:T(8,128)(2,1)S(1)}, u32[]{:S(2)}, u32[]{:S(2)}) collective-permute-start(bf16[256,768]{1,0:T(8,128)(2,1)S(1)} %get-tuple-element.39), channel_id=1, source_target_pairs={{0,3},{8,11},{16,19},{24,27}} | collective-permute-start | bytes 1179656 | tf_op jit(solution)/shard_map/ppermute | solution.py:71
  48.1 3.3 %collective-permute-start.10 = (f32[6,8,256]{2,1,0:T(8,128)S(1)}, f32[6,8,256]{2,1,0:T(8,128)S(1)}, u32[]{:S(2)}, u32[]{:S(2)}) collective-permute-start(f32[6,8,256]{2,1,0:T(8,128)S(1)} %get-tuple-element.37), channel_id=1, source_target_pairs={{1,0},{2,1},{3,2},{4,3},{5,4},{6,5},{7,6},{9,8},{10,9},{11,10},{12... | collective-permute-start | bytes 147464 | tf_op jit(solution)/shard_map/ppermute | solution.py:669
  49.6 10.1 %collective-permute-start.14 = (bf16[3,2,128,384]{3,2,1,0:T(8,128)(2,1)S(1)}, bf16[3,2,128,384]{3,2,1,0:T(8,128)(2,1)S(1)}, u32[]{:S(2)}, u32[]{:S(2)}) collective-permute-start(bf16[3,2,128,384]{3,2,1,0:T(8,128)(2,1)S(1)} %get-tuple-element.43), channel_id=1, source_target_pairs={{0,2},{1,5},{2,0},{3,7},{4,6},{5,1},{6,4},{7,3},{8,10},{9,13},{10,... | collective-permute-start | bytes 1769480 | tf_op jit(solution)/shard_map/ppermute | solution.py:50
  60.0 1.8 %collective-permute-start.15 = (bf16[2,2,128,384]{3,2,1,0:T(8,128)(2,1)S(1)}, bf16[2,2,128,384]{3,2,1,0:T(8,128)(2,1)S(1)}, u32[]{:S(2)}, u32[]{:S(2)}) collective-permute-start(bf16[2,2,128,384]{3,2,1,0:T(8,128)(2,1)S(1)} %get-tuple-element.45), channel_id=1, source_target_pairs={{0,1},{1,0},{2,3},{3,2},{4,5},{5,4},{6,7},{7,6},{8,9},{9,8},{10,11... | collective-permute-start | bytes 1179656 | tf_op jit(solution)/shard_map/ppermute | solution.py:50

commit v10 on v9

--- a/solution.py
+++ b/solution.py
@@ -392,14 +392,18 @@
     work = [(g, local) for local in range(half) for g in range(len(groups))]
     keep_ref[...] = jnp.zeros(keep_ref.shape, F32)
 
+    def operands(g, local):
+        cols = pl.ds(pl.multiple_of((role * half + local) * DEPTH, DEPTH), DEPTH)
+        return joined_parts(groups[g][0], cols)
+
     def products(g, local):
-        queries, mem, _, piece = groups[g]
-        query, cotangent = joined_parts(queries, head_cols(local))
+        _, mem, _, piece = groups[g]
+        query, cotangent = operands(g, local)
         keys, values = (mem[:, kind, :, head_cols(local)].reshape(MEM * frame_len, DEPTH) for kind in range(2))
         return logits_of(keys, query, rows_ref, role * half + local, piece), dot(values, cotangent, 1, 1)
 
     def add(g, local, _, weights, dlogits):
-        query, cotangent = joined_parts(groups[g][0], head_cols(local))
+        query, cotangent = operands(g, local)
         terms = (dot(dlogits, query, 1, 0) * FACTOR, dot(weights, cotangent, 1, 0))
         for m in range(MEM):
             place = field(code, g * MEM + m, PLACE_BITS)
@@ -473,18 +477,15 @@
     own_ref,
     own_mem,
     other_mem,
-    passed_ref,
     attended_ref,
     grad_query_ref,
     term_ref,
     stats_ref,
-    passed_out,
 ):
     role = lax.axis_index("tm") & 1
     frame_len, half_width = own_mem.shape[2:]
     heads = queries_ref.shape[1] // DEPTH
     half = half_width // DEPTH
-    passed_out[...] = passed_ref[...]
 
     def pieces(head):
         cols = head_cols(head % half)
@@ -525,7 +526,11 @@
         grad_query_ref[:, cols] = (grad_query * FACTOR).T.astype(BF16)
 
 
-def add_kernel(keep_ref, got_ref, out_ref, send_ref):
+def add_kernel(keep_ref, got_ref, *refs):
+    passed = len(refs) // 2 - 1
+    for source, out in zip(refs[:passed], refs[passed + 2 :]):
+        out[...] = source[...]
+    out_ref, send_ref = refs[passed : passed + 2]
     value = keep_ref[0 : got_ref.shape[0]] + got_ref[...].astype(F32)
     out_ref[...] = value
     send_ref[...] = value.astype(BF16)
@@ -578,7 +583,6 @@
     peers = lax.axis_size("tm")
     bits = [1 << i for i in range(1, peers.bit_length() - 1)]
     turns = list(zip(bits, bits[::-1]))
-    even = (lax.axis_index("tm") & 1) == 0
     piece_flops = 2 * row_count * row_count * width
     bank_frames = bank_frames.reshape(1, slots)
     last_bits = turns[-1]
@@ -605,7 +609,6 @@
         "join",
     )
     half_width = width // 2
-    first, second = slice(0, half_width), slice(half_width, width)
     direct_keys = shift_first(key_states, 1, 1, peers)
     pair = swap(joined, 1, 1, peers)
     held = shape(BF16, slots - 1, 2, frame_len, half_width)
@@ -613,8 +616,6 @@
     (mine,) = call(functools.partial(split_kernel, peers), [held], [bank_frames, joined, pair], name="split")
     queries = join(join_queries_kernel, 2 * row_count, [query_states, grad_out], [], "join_queries", after=[mine])
     pair_queries = swap(queries, 1, 1, peers)
-    own_half = jnp.where(even, queries[:, first], queries[:, second])
-    pair_half = jnp.where(even, pair_queries[:, first], pair_queries[:, second])
 
     bias_rows = -(-(5 * FR_DEV) // 8) * 8
     rows, codes, values_out, keys_out = call(
@@ -652,33 +653,39 @@
     keep, send = call(
         memory_kernel,
         [shape(F32, slots, 2, frame_len, half_width), held],
-        [codes, rows, part, pair_part, own_half, pair_half, own_mem, pair_mem],
+        [codes, rows, part, pair_part, queries, pair_queries, own_mem, pair_mem],
         flops=HIDING * piece_flops,
         name="memory",
     )
     other_mem = swap(pair_mem, 1, 1, peers)
     pair_sums = shape(F32, 2, row_count, width)
-    attended, grad_query, own_terms, stats_all, passed_on = call(
+    attended, grad_query, own_terms, stats_all = call(
         functools.partial(rest_kernel, peers),
-        [shape(BF16, row_count, width)] * 2 + [pair_sums, stats, shape(BF16, row_count, width)],
-        [rows, part, queries, *outer, pair, joined, own_mem, other_mem, direct_cotangent],
+        [shape(BF16, row_count, width)] * 2 + [pair_sums, stats],
+        [rows, part, queries, *outer, pair, joined, own_mem, other_mem],
         after=[send],
         flops=HIDING * piece_flops,
         name="rest",
     )
-    next_stats = lax.ppermute(stats_all, "tm", [(i, i - 1) for i in range(1, peers)])
-    relayed_cotangent = shift_second(passed_on, -1, 2, peers)
+    passing = [stats_all, direct_cotangent]
+    for step, (even_bit, odd_bit) in enumerate(turns[::-1]):
+        got = swap(send, even_bit, odd_bit, peers)
+        if step + 1 < len(turns):
+            keep, send, *passing = call(
+                add_kernel,
+                [sums, held, stats, shape(BF16, row_count, width)],
+                [keep, got, *passing],
+                after=[own_terms, next_queries],
+                name="add",
+            )
+    next_stats = lax.ppermute(passing[0], "tm", [(i, i - 1) for i in range(1, peers)])
+    relayed_cotangent = shift_second(passing[1], -1, 2, peers)
     (own,) = call(
         functools.partial(next_kernel, peers),
         [pair_sums],
         [rows, next_stats, pair_queries, next_queries, direct_cotangent, relayed_cotangent, joined, own_terms],
-        flops=HIDING * piece_flops,
         name="next",
     )
-    for step, (even_bit, odd_bit) in enumerate(turns[::-1]):
-        got = swap(send, even_bit, odd_bit, peers)
-        if step + 1 < len(turns):
-            keep, send = call(add_kernel, [sums, held], [keep, got], after=[own_terms], name="add")
     owned_mine, owned_send = call(
         owned_kernel,
         [shape(F32, FR_DEV, 2, frame_len, half_width), shape(BF16, FR_DEV, 2, frame_len, half_width)],

time: 63.2 us -> 64.1 us (1.014)
  waiting for transfers between devices: 13.2 us -> 18.3 us
  Pallas kernels: 20.8 us -> 16.9 us
    ppermute x2, waiting for transfers between devices: 1.98 us -> 6.17 us  [shift_second(): return lax.ppermute(block, 'tm', pairs) if pairs else block]
    pallas_call x11, Pallas kernels: 18.5 us -> 14.5 us  [call(): pl.pallas_call(run, out_shape=outs, in_specs=[SMEM] * len(scalars) + [VME...]
    ppermute x1, waiting for transfers between devices: 0.01 us -> 1.82 us  [body(): lax.ppermute(passing[0], 'tm', [(i, i - 1) for i in range(1, peers)])]
    ppermute x2, starting transfers between devices: 2.08 us -> 1.37 us  [shift(): return lax.ppermute(block, 'tm', pairs)]
    ppermute x2, waiting for transfers between devices: 0.67 us -> 0.01 us  [shift_first(): lax.ppermute(block, 'tm', [(i, relays.get((i, j), j)) for i, j in pairs])]
  transfers between devices with their start and end apart: 16 -> 16, of which waited for: 6 -> 6; matrix products, arithmetic and copies ran while one was open for 0% -> 0% of each run, Pallas kernels for 29% -> 22%
where the time goes in v10:
time: 64.1 us; the launch traced here: 63.9 us
  starting transfers between devices  27.9 us (44%)
  waiting for transfers between devices  18.3 us (29%)
  Pallas kernels  16.9 us (26%)
  between operations  0.85 us (1%)
    ppermute x9, starting transfers between devices, swap(): lax.ppermute(block, 'tm', [(i, i ^ (odd_bit if i & 1 else even_bit)) for...  20.2 us
    pallas_call x11, Pallas kernels, call(): pl.pallas_call(run, out_shape=outs, in_specs=[SMEM] * len(scalars) + [VME...  14.5 us
    ppermute x9, waiting for transfers between devices, swap(): lax.ppermute(block, 'tm', [(i, i ^ (odd_bit if i & 1 else even_bit)) for...  10.3 us
    ppermute x2, waiting for transfers between devices, shift_second(): return lax.ppermute(block, 'tm', pairs) if pairs else block  6.17 us
    ppermute x2, starting transfers between devices, shift_second(): return lax.ppermute(block, 'tm', pairs) if pairs else block  3 us
    pallas_call x2, Pallas kernels, join(): pl.pallas_call(run, out_shape=shape(BF16, rows, width), in_specs=[pl.Bloc...  2.34 us
    ppermute x2, starting transfers between devices, shift_first(): lax.ppermute(block, 'tm', [(i, relays.get((i, j), j)) for i, j in pairs])  1.95 us
    ppermute x1, waiting for transfers between devices, body(): lax.ppermute(passing[0], 'tm', [(i, i - 1) for i in range(1, peers)])  1.82 us
  transfers between devices with their start and end apart: 16, of which 6 were waited for; matrix products, arithmetic and copies ran while one was open for 0% of the time, Pallas kernels for 22%

profile of v10, /device:TPU:0, one launch (start us, length us, event | category | flops | bytes accessed | tf_op | source)
XLA Modules:
  0.0 63.9 jit_solution(5759056806897571143)
XLA Ops:
  0.7 1.2 %join.1.refs_5_.refs_1_.refs_6_.refs_7_ = bf16[528,768]{1,0:T(8,128)(2,1)S(1)} custom-call(s32[1,2]{1,0:T(1,128)} %refs_1_.4, bf16[256,768]{1,0:T(8,128)(2,1)} %refs_1_.3, bf16[256,768]{1,0:T(8,128)(2,1)} %refs_2_.2), custom_call_target="tpu_custom_call" | custom-call | tf_op jit(solution)/shard_map/join/pallas_call | solution.py:594
  1.9 0.5 collective-permute-start
  2.4 0.7 %collective-permute-start.1 = (bf16[256,768]{1,0:T(8,128)(2,1)S(1)}, bf16[256,768]{1,0:T(8,128)(2,1)S(1)}, u32[]{:S(2)}, u32[]{:S(2)}) collective-permute-start(bf16[256,768]{1,0:T(8,128)(2,1)S(1)} %copy-done.4), channel_id=1, source_target_pairs={{1,2},{3,7},{5,6},{9,10},{11,15},{13,14},{17,18},{19,23},{21,22},{... | collective-permute-start | bytes 1179656 | tf_op jit(solution)/shard_map/ppermute | solution.py:66
  3.1 1.3 %collective-permute-done.refs_4_.refs_2_.refs_5_.refs_6_ = bf16[528,768]{1,0:T(8,128)(2,1)S(1)} collective-permute-done((bf16[528,768]{1,0:T(8,128)(2,1)S(1)}, bf16[528,768]{1,0:T(8,128)(2,1)S(1)}, u32[]{:S(2)}, u32[]{:S(2)}) %collective-permute-start) | collective-permute-done | bytes 811040 | tf_op jit(solution)/shard_map/ppermute | solution.py:50
  4.3 0.3 split.1.refs_2_.refs_1_
  4.7 0.0 copy-start.1
  4.7 0.0 copy-start.2
  4.7 0.0 copy-start.3
  4.7 2.9 %collective-permute-start.4 = (bf16[3,2,128,384]{3,2,1,0:T(8,128)(2,1)S(1)}, bf16[3,2,128,384]{3,2,1,0:T(8,128)(2,1)S(1)}, u32[]{:S(2)}, u32[]{:S(2)}) collective-permute-start(bf16[3,2,128,384]{3,2,1,0:T(8,128)(2,1)S(1)} %split.1.refs_2_.refs_1_), channel_id=1, source_target_pairs={{0,2},{1,5},{2,0},{3,7},{4,6},{5,1},{6,4},{7,3},{8,10},{9,13},{10,... | collective-permute-start | bytes 1769480 | tf_op jit(solution)/shard_map/ppermute | solution.py:50
  7.6 1.1 %join_queries.1.refs_1_.refs_4_.refs_2_ = bf16[512,768]{1,0:T(8,128)(2,1)S(1)} custom-call(bf16[256,768]{1,0:T(8,128)(2,1)} %refs_0_.3, bf16[256,768]{1,0:T(8,128)(2,1)} %refs_1_.5, bf16[3,2,128,384]{3,2,1,0:T(8,128)(2,1)S(1)} %split.1.refs_2_.refs_1_), custom_call_target="tpu_custom_call" | custom-call | tf_op jit(solution)/shard_map/join_queries/pallas_call | solution.py:594
  8.8 1.1 %collective-permute-start.5 = (bf16[512,768]{1,0:T(8,128)(2,1)S(1)}, bf16[512,768]{1,0:T(8,128)(2,1)S(1)}, u32[]{:S(2)}, u32[]{:S(2)}) collective-permute-start(bf16[512,768]{1,0:T(8,128)(2,1)S(1)} %join_queries.1.refs_1_.refs_4_.refs_2_), channel_id=1, source_target_pairs={{0,1},{1,0},{2,3},{3,2},{4,5},{5,4},{6,7},{7,6},{8,9},{9,8},{10,11... | collective-permute-start | bytes 2359304 | tf_op jit(solution)/shard_map/ppermute | solution.py:50
  9.9 0.0 collective-permute-done.1.refs_6_.refs_2_.refs_3_
  9.9 1.7 %plan.1 = (f32[6,16,256]{2,1,0:T(8,128)S(1)}, s32[8,128]{1,0:T(8,128)S(1)}, bf16[256,768]{1,0:T(8,128)(2,1)S(1)}, bf16[256,768]{1,0:T(8,128)(2,1)S(1)}) custom-call(s32[1,4]{1,0:T(1,128)S(1)} %bitcast.2, s32[1,2]{1,0:T(1,128)S(1)} %copy-done.1, s32[16]{0:T(128)S(1)} %copy-done.3, f32[6,16,16]{2,1,0:T(8,128)S(1)} %copy-done.2, ...), custom_call_target="tpu_custom_call" | custom-call | flops 20132659200 | tf_op jit(solution)/shard_map/plan/pallas_call | solution.py:38
  11.6 0.7 %collective-permute-start.2 = (bf16[256,768]{1,0:T(8,128)(2,1)S(1)}, bf16[256,768]{1,0:T(8,128)(2,1)S(1)}, u32[]{:S(2)}, u32[]{:S(2)}) collective-permute-start(bf16[256,768]{1,0:T(8,128)(2,1)S(1)} %get-tuple-element.28), channel_id=1, source_target_pairs={{7,4},{15,12},{23,20},{31,28}} | collective-permute-start | bytes 1179656 | tf_op jit(solution)/shard_map/ppermute | solution.py:71
  12.3 0.7 %collective-permute-start.3 = (bf16[256,768]{1,0:T(8,128)(2,1)S(1)}, bf16[256,768]{1,0:T(8,128)(2,1)S(1)}, u32[]{:S(2)}, u32[]{:S(2)}) collective-permute-start(bf16[256,768]{1,0:T(8,128)(2,1)S(1)} %get-tuple-element.29), channel_id=1, source_target_pairs={{1,2},{3,4},{5,6},{9,10},{11,12},{13,14},{17,18},{19,20},{21,22},{... | collective-permute-start | bytes 1179656 | tf_op jit(solution)/shard_map/ppermute | solution.py:55
  12.9 4.9 %collective-permute-done.4.refs_2_ = bf16[3,2,128,384]{3,2,1,0:T(8,128)(2,1)S(1)} collective-permute-done((bf16[3,2,128,384]{3,2,1,0:T(8,128)(2,1)S(1)}, bf16[3,2,128,384]{3,2,1,0:T(8,128)(2,1)S(1)}, u32[]{:S(2)}, u32[]{:S(2)}) %collective-permute-start.4) | collective-permute-done | bytes 589856 | tf_op jit(solution)/shard_map/ppermute | solution.py:50
  17.8 0.0 collective-permute-done.5.refs_4_.refs_5_.refs_2_
  17.8 0.3 step.1.refs_1_
  18.1 1.6 %collective-permute-start.6 = (bf16[3,2,128,384]{3,2,1,0:T(8,128)(2,1)S(1)}, bf16[3,2,128,384]{3,2,1,0:T(8,128)(2,1)S(1)}, u32[]{:S(2)}, u32[]{:S(2)}) collective-permute-start(bf16[3,2,128,384]{3,2,1,0:T(8,128)(2,1)S(1)} %step.1.refs_1_), channel_id=1, source_target_pairs={{0,4},{1,3},{2,6},{3,1},{4,0},{5,7},{6,2},{7,5},{8,12},{9,11},{10,... | collective-permute-start | bytes 1769480 | tf_op jit(solution)/shard_map/ppermute | solution.py:50
  19.7 0.0 collective-permute-done.2.refs_3_.refs_4_
  19.7 0.0 collective-permute-done.3.refs_4_.refs_5_
  19.7 1.6 %stats.1 = (f32[6,8,256]{2,1,0:T(8,128)S(1)}, bf16[256,768]{1,0:T(8,128)(2,1)S(1)}, bf16[256,768]{1,0:T(8,128)(2,1)S(1)}) custom-call(f32[6,16,256]{2,1,0:T(8,128)S(1)} %get-tuple-element.27.refs_0_.refs_1_, bf16[512,768]{1,0:T(8,128)(2,1)S(1)} %join_queries.1.refs_1_.refs_4_.refs_2_, bf16[256,768]{1,0:T(8,128)(2,1)S(1)} %collective-permute-done.1.refs_6_.refs_2_.refs_3_, ...), custom_call_target="tpu_custom_call" | custom-call | flops 20132659200 | tf_op jit(solution)/shard_map/stats/pallas_call | solution.py:38
  21.3 6.2 %collective-permute-start.8 = (f32[6,8,256]{2,1,0:T(8,128)S(1)}, f32[6,8,256]{2,1,0:T(8,128)S(1)}, u32[]{:S(2)}, u32[]{:S(2)}) collective-permute-start(f32[6,8,256]{2,1,0:T(8,128)S(1)} %get-tuple-element.30.refs_2_.refs_1_), channel_id=1, source_target_pairs={{0,1},{1,0},{2,3},{3,2},{4,5},{5,4},{6,7},{7,6},{8,9},{9,8},{10,11... | collective-permute-start | bytes 147464 | tf_op jit(solution)/shard_map/ppermute | solution.py:50
  27.5 1.3 %collective-permute-start.10 = (bf16[256,768]{1,0:T(8,128)(2,1)S(1)}, bf16[256,768]{1,0:T(8,128)(2,1)S(1)}, u32[]{:S(2)}, u32[]{:S(2)}) collective-permute-start(bf16[256,768]{1,0:T(8,128)(2,1)S(1)} %get-tuple-element.39), channel_id=1, source_target_pairs={{2,1},{4,0},{6,5},{10,9},{12,8},{14,13},{18,17},{20,16},{22,21},{2... | collective-permute-start | bytes 1179656 | tf_op jit(solution)/shard_map/ppermute | solution.py:66
  28.7 0.7 %collective-permute-start.11 = (bf16[256,768]{1,0:T(8,128)(2,1)S(1)}, bf16[256,768]{1,0:T(8,128)(2,1)S(1)}, u32[]{:S(2)}, u32[]{:S(2)}) collective-permute-start(bf16[256,768]{1,0:T(8,128)(2,1)S(1)} %get-tuple-element.41), channel_id=1, source_target_pairs={{2,1},{4,3},{6,5},{10,9},{12,11},{14,13},{18,17},{20,19},{22,21},{... | collective-permute-start | bytes 1179656 | tf_op jit(solution)/shard_map/ppermute | solution.py:55
  29.4 0.0 collective-permute-done.6.refs_2_
  29.5 0.3 pick.1
  29.8 2.8 %collective-permute-start.7 = (bf16[2,2,128,384]{3,2,1,0:T(8,128)(2,1)S(1)}, bf16[2,2,128,384]{3,2,1,0:T(8,128)(2,1)S(1)}, u32[]{:S(2)}, u32[]{:S(2)}) collective-permute-start(bf16[2,2,128,384]{3,2,1,0:T(8,128)(2,1)S(1)} %get-tuple-element.33.refs_7_), channel_id=1, source_target_pairs={{0,1},{1,0},{2,3},{3,2},{4,5},{5,4},{6,7},{7,6},{8,9},{9,8},{10,11... | collective-permute-start | bytes 1179656 | tf_op jit(solution)/shard_map/ppermute | solution.py:50
  32.5 0.0 collective-permute-done.8.refs_3_
  32.5 1.9 %memory.1 = (f32[4,2,128,384]{3,2,1,0:T(8,128)S(1)}, bf16[3,2,128,384]{3,2,1,0:T(8,128)(2,1)S(1)}) custom-call(s32[8,128]{1,0:T(8,128)S(1)} %get-tuple-element.31.refs_3_.refs_0_, f32[6,16,256]{2,1,0:T(8,128)S(1)} %get-tuple-element.27.refs_0_.refs_1_, f32[6,8,256]{2,1,0:T(8,128)S(1)} %get-tuple-element.30.refs_2_.refs_1_, ...), custom_call_target="tpu_custom_call" | custom-call | flops 20132659200 | tf_op jit(solution)/shard_map/memory/pallas_call | solution.py:38
  34.5 2.0 %collective-permute-start.9 = (bf16[3,2,128,384]{3,2,1,0:T(8,128)(2,1)S(1)}, bf16[3,2,128,384]{3,2,1,0:T(8,128)(2,1)S(1)}, u32[]{:S(2)}, u32[]{:S(2)}) collective-permute-start(bf16[3,2,128,384]{3,2,1,0:T(8,128)(2,1)S(1)} %get-tuple-element.34.refs_10_), channel_id=1, source_target_pairs={{0,4},{1,3},{2,6},{3,1},{4,0},{5,7},{6,2},{7,5},{8,12},{9,11},{10,... | collective-permute-start | bytes 1769480 | tf_op jit(solution)/shard_map/ppermute | solution.py:50
  36.5 0.0 collective-permute-done.7.refs_9_
  36.5 5.6 %rest.1 = (bf16[256,768]{1,0:T(8,128)(2,1)}, bf16[256,768]{1,0:T(8,128)(2,1)}, f32[2,256,768]{2,1,0:T(8,128)S(1)}, f32[6,8,256]{2,1,0:T(8,128)S(1)}) custom-call(f32[6,16,256]{2,1,0:T(8,128)S(1)} %get-tuple-element.27.refs_0_.refs_1_, f32[6,8,256]{2,1,0:T(8,128)S(1)} %get-tuple-element.30.refs_2_.refs_1_, ...), custom_call_target="tpu_custom_call" | custom-call | flops 20132659200 | tf_op jit(solution)/shard_map/rest/pallas_call | solution.py:38
  42.0 0.0 collective-permute-done.10.refs_3_.refs_4_
  42.0 0.0 collective-permute-done.11.refs_5_.refs_3_
  42.0 2.4 %collective-permute-done.9.refs_1_ = bf16[3,2,128,384]{3,2,1,0:T(8,128)(2,1)S(1)} collective-permute-done((bf16[3,2,128,384]{3,2,1,0:T(8,128)(2,1)S(1)}, bf16[3,2,128,384]{3,2,1,0:T(8,128)(2,1)S(1)}, u32[]{:S(2)}, u32[]{:S(2)}) %collective-permute-start.9) | collective-permute-done | bytes 589856 | tf_op jit(solution)/shard_map/ppermute | solution.py:50
  44.4 0.2 add.1
  44.7 3.1 %collective-permute-start.14 = (bf16[3,2,128,384]{3,2,1,0:T(8,128)(2,1)S(1)}, bf16[3,2,128,384]{3,2,1,0:T(8,128)(2,1)S(1)}, u32[]{:S(2)}, u32[]{:S(2)}) collective-permute-start(bf16[3,2,128,384]{3,2,1,0:T(8,128)(2,1)S(1)} %get-tuple-element.45), channel_id=1, source_target_pairs={{0,2},{1,5},{2,0},{3,7},{4,6},{5,1},{6,4},{7,3},{8,10},{9,13},{10,... | collective-permute-start | bytes 1769480 | tf_op jit(solution)/shard_map/ppermute | solution.py:50
  47.8 2.3 %collective-permute-start.13 = (bf16[256,768]{1,0:T(8,128)(2,1)S(1)}, bf16[256,768]{1,0:T(8,128)(2,1)S(1)}, u32[]{:S(2)}, u32[]{:S(2)}) collective-permute-start(bf16[256,768]{1,0:T(8,128)(2,1)S(1)} %get-tuple-element.43), channel_id=1, source_target_pairs={{0,3},{8,11},{16,19},{24,27}} | collective-permute-start | bytes 1179656 | tf_op jit(solution)/shard_map/ppermute | solution.py:71
  50.2 1.3 %collective-permute-start.12 = (f32[6,8,256]{2,1,0:T(8,128)S(1)}, f32[6,8,256]{2,1,0:T(8,128)S(1)}, u32[]{:S(2)}, u32[]{:S(2)}) collective-permute-start(f32[6,8,256]{2,1,0:T(8,128)S(1)} %get-tuple-element.42), channel_id=1, source_target_pairs={{1,0},{2,1},{3,2},{4,3},{5,4},{6,5},{7,6},{9,8},{10,9},{11,10},{12... | collective-permute-start | bytes 147464 | tf_op jit(solution)/shard_map/ppermute | solution.py:681
  51.5 1.8 %collective-permute-done.12.refs_1_ = f32[6,8,256]{2,1,0:T(8,128)S(1)} collective-permute-done((f32[6,8,256]{2,1,0:T(8,128)S(1)}, f32[6,8,256]{2,1,0:T(8,128)S(1)}, u32[]{:S(2)}, u32[]{:S(2)}) %collective-permute-start.12) | collective-permute-done | bytes 49184 | tf_op jit(solution)/shard_map/ppermute | solution.py:681
  53.3 6.2 %collective-permute-done.13.refs_5_ = bf16[256,768]{1,0:T(8,128)(2,1)S(1)} collective-permute-done((bf16[256,768]{1,0:T(8,128)(2,1)S(1)}, bf16[256,768]{1,0:T(8,128)(2,1)S(1)}, u32[]{:S(2)}, u32[]{:S(2)}) %collective-permute-start.13) | collective-permute-done | bytes 393248 | tf_op jit(solution)/shard_map/ppermute | solution.py:71
  59.4 1.3 %next.1.refs_3_.refs_0_ = f32[2,256,768]{2,1,0:T(8,128)S(1)} custom-call(f32[6,16,256]{2,1,0:T(8,128)S(1)} %get-tuple-element.27.refs_0_.refs_1_, f32[6,8,256]{2,1,0:T(8,128)S(1)} %collective-permute-done.12.refs_1_, bf16[512,768]{1,0:T(8,128)(2,1)S(1)} %collective-permute-done.5.refs_4_.refs_5_.refs_2_, ...), custom_call_target="tpu_custom_call" | custom-call | tf_op jit(solution)/shard_map/next/pallas_call | solution.py:38
  60.7 0.0 collective-permute-done.14.refs_2_
  60.7 0.3 owned.1
  61.1 0.1 collective-permute-start.15
  61.1 1.7 %collective-permute-done.15.refs_2_ = bf16[2,2,128,384]{3,2,1,0:T(8,128)(2,1)S(1)} collective-permute-done((bf16[2,2,128,384]{3,2,1,0:T(8,128)(2,1)S(1)}, bf16[2,2,128,384]{3,2,1,0:T(8,128)(2,1)S(1)}, u32[]{:S(2)}, u32[]{:S(2)}) %collective-permute-start.15) | collective-permute-done | bytes 393248 | tf_op jit(solution)/shard_map/ppermute | solution.py:50
  62.9 1.0 %final.1 = (bf16[256,768]{1,0:T(8,128)(2,1)}, bf16[256,768]{1,0:T(8,128)(2,1)}) custom-call(f32[2,256,768]{2,1,0:T(8,128)S(1)} %next.1.refs_3_.refs_0_, f32[2,2,128,384]{3,2,1,0:T(8,128)S(1)} %get-tuple-element.46.refs_1_, bf16[2,2,128,384]{3,2,1,0:T(8,128)(2,1)S(1)} %collective-permute-done.15.refs_2_), custom_call_target="tpu_custom_call" | custom-call | tf_op jit(solution)/shard_map/final/pallas_call | solution.py:38
  (7 shorter events, 0.0 us)
Async XLA Ops:
  0.6 1.8 %copy-start.4 = (bf16[256,768]{1,0:T(8,128)(2,1)S(1)}, bf16[256,768]{1,0:T(8,128)(2,1)}, u32[]{:S(2)}) copy-start(bf16[256,768]{1,0:T(8,128)(2,1)} %refs_1_.3) | copy-start | bytes 1179652
  0.6 3.7 %copy-start = (s32[4]{0:T(128)S(1)}, s32[4]{0:T(128)}, u32[]{:S(2)}) copy-start(s32[4]{0:T(128)} %param.15) | copy-start | bytes 52
  1.9 2.5 %collective-permute-start = (bf16[528,768]{1,0:T(8,128)(2,1)S(1)}, bf16[528,768]{1,0:T(8,128)(2,1)S(1)}, u32[]{:S(2)}, u32[]{:S(2)}) collective-permute-start(bf16[528,768]{1,0:T(8,128)(2,1)S(1)} %join.1.refs_5_.refs_1_.refs_6_.refs_7_), channel_id=1, source_target_pairs={{0,1},{1,0},{2,3},{3,2},{4,5},{5,4},{6,7},{7,6},{8,9},{9,8},{10,11... | collective-permute-start | bytes 2433032 | tf_op jit(solution)/shard_map/ppermute | solution.py:50
  2.4 7.5 %collective-permute-start.1 = (bf16[256,768]{1,0:T(8,128)(2,1)S(1)}, bf16[256,768]{1,0:T(8,128)(2,1)S(1)}, u32[]{:S(2)}, u32[]{:S(2)}) collective-permute-start(bf16[256,768]{1,0:T(8,128)(2,1)S(1)} %copy-done.4), channel_id=1, source_target_pairs={{1,2},{3,7},{5,6},{9,10},{11,15},{13,14},{17,18},{19,23},{21,22},{... | collective-permute-start | bytes 1179656 | tf_op jit(solution)/shard_map/ppermute | solution.py:66
  4.7 5.2 %copy-start.1 = (s32[1,2]{1,0:T(1,128)S(1)}, s32[1,2]{1,0:T(1,128)}, u32[]{:S(2)}) copy-start(s32[1,2]{1,0:T(1,128)} %refs_1_.4) | copy-start | bytes 28
  4.7 5.2 %copy-start.2 = (f32[6,16,16]{2,1,0:T(8,128)S(1)}, f32[6,16,16]{2,1,0:T(8,128)}, u32[]{:S(2)}) copy-start(f32[6,16,16]{2,1,0:T(8,128)} %refs_3_.1) | copy-start | bytes 18436
  4.7 5.2 %copy-start.3 = (s32[16]{0:T(128)S(1)}, s32[16]{0:T(128)}, u32[]{:S(2)}) copy-start(s32[16]{0:T(128)} %refs_2_.3) | copy-start | bytes 196
  4.7 13.1 %collective-permute-start.4 = (bf16[3,2,128,384]{3,2,1,0:T(8,128)(2,1)S(1)}, bf16[3,2,128,384]{3,2,1,0:T(8,128)(2,1)S(1)}, u32[]{:S(2)}, u32[]{:S(2)}) collective-permute-start(bf16[3,2,128,384]{3,2,1,0:T(8,128)(2,1)S(1)} %split.1.refs_2_.refs_1_), channel_id=1, source_target_pairs={{0,2},{1,5},{2,0},{3,7},{4,6},{5,1},{6,4},{7,3},{8,10},{9,13},{10,... | collective-permute-start | bytes 1769480 | tf_op jit(solution)/shard_map/ppermute | solution.py:50
  8.8 9.1 %collective-permute-start.5 = (bf16[512,768]{1,0:T(8,128)(2,1)S(1)}, bf16[512,768]{1,0:T(8,128)(2,1)S(1)}, u32[]{:S(2)}, u32[]{:S(2)}) collective-permute-start(bf16[512,768]{1,0:T(8,128)(2,1)S(1)} %join_queries.1.refs_1_.refs_4_.refs_2_), channel_id=1, source_target_pairs={{0,1},{1,0},{2,3},{3,2},{4,5},{5,4},{6,7},{7,6},{8,9},{9,8},{10,11... | collective-permute-start | bytes 2359304 | tf_op jit(solution)/shard_map/ppermute | solution.py:50
  11.6 8.2 %collective-permute-start.2 = (bf16[256,768]{1,0:T(8,128)(2,1)S(1)}, bf16[256,768]{1,0:T(8,128)(2,1)S(1)}, u32[]{:S(2)}, u32[]{:S(2)}) collective-permute-start(bf16[256,768]{1,0:T(8,128)(2,1)S(1)} %get-tuple-element.28), channel_id=1, source_target_pairs={{7,4},{15,12},{23,20},{31,28}} | collective-permute-start | bytes 1179656 | tf_op jit(solution)/shard_map/ppermute | solution.py:71
  12.3 7.5 %collective-permute-start.3 = (bf16[256,768]{1,0:T(8,128)(2,1)S(1)}, bf16[256,768]{1,0:T(8,128)(2,1)S(1)}, u32[]{:S(2)}, u32[]{:S(2)}) collective-permute-start(bf16[256,768]{1,0:T(8,128)(2,1)S(1)} %get-tuple-element.29), channel_id=1, source_target_pairs={{1,2},{3,4},{5,6},{9,10},{11,12},{13,14},{17,18},{19,20},{21,22},{... | collective-permute-start | bytes 1179656 | tf_op jit(solution)/shard_map/ppermute | solution.py:55
  18.1 11.3 %collective-permute-start.6 = (bf16[3,2,128,384]{3,2,1,0:T(8,128)(2,1)S(1)}, bf16[3,2,128,384]{3,2,1,0:T(8,128)(2,1)S(1)}, u32[]{:S(2)}, u32[]{:S(2)}) collective-permute-start(bf16[3,2,128,384]{3,2,1,0:T(8,128)(2,1)S(1)} %step.1.refs_1_), channel_id=1, source_target_pairs={{0,4},{1,3},{2,6},{3,1},{4,0},{5,7},{6,2},{7,5},{8,12},{9,11},{10,... | collective-permute-start | bytes 1769480 | tf_op jit(solution)/shard_map/ppermute | solution.py:50
  21.3 11.3 %collective-permute-start.8 = (f32[6,8,256]{2,1,0:T(8,128)S(1)}, f32[6,8,256]{2,1,0:T(8,128)S(1)}, u32[]{:S(2)}, u32[]{:S(2)}) collective-permute-start(f32[6,8,256]{2,1,0:T(8,128)S(1)} %get-tuple-element.30.refs_2_.refs_1_), channel_id=1, source_target_pairs={{0,1},{1,0},{2,3},{3,2},{4,5},{5,4},{6,7},{7,6},{8,9},{9,8},{10,11... | collective-permute-start | bytes 147464 | tf_op jit(solution)/shard_map/ppermute | solution.py:50
  27.5 14.6 %collective-permute-start.10 = (bf16[256,768]{1,0:T(8,128)(2,1)S(1)}, bf16[256,768]{1,0:T(8,128)(2,1)S(1)}, u32[]{:S(2)}, u32[]{:S(2)}) collective-permute-start(bf16[256,768]{1,0:T(8,128)(2,1)S(1)} %get-tuple-element.39), channel_id=1, source_target_pairs={{2,1},{4,0},{6,5},{10,9},{12,8},{14,13},{18,17},{20,16},{22,21},{2... | collective-permute-start | bytes 1179656 | tf_op jit(solution)/shard_map/ppermute | solution.py:66
  28.7 13.3 %collective-permute-start.11 = (bf16[256,768]{1,0:T(8,128)(2,1)S(1)}, bf16[256,768]{1,0:T(8,128)(2,1)S(1)}, u32[]{:S(2)}, u32[]{:S(2)}) collective-permute-start(bf16[256,768]{1,0:T(8,128)(2,1)S(1)} %get-tuple-element.41), channel_id=1, source_target_pairs={{2,1},{4,3},{6,5},{10,9},{12,11},{14,13},{18,17},{20,19},{22,21},{... | collective-permute-start | bytes 1179656 | tf_op jit(solution)/shard_map/ppermute | solution.py:55
  29.8 6.7 %collective-permute-start.7 = (bf16[2,2,128,384]{3,2,1,0:T(8,128)(2,1)S(1)}, bf16[2,2,128,384]{3,2,1,0:T(8,128)(2,1)S(1)}, u32[]{:S(2)}, u32[]{:S(2)}) collective-permute-start(bf16[2,2,128,384]{3,2,1,0:T(8,128)(2,1)S(1)} %get-tuple-element.33.refs_7_), channel_id=1, source_target_pairs={{0,1},{1,0},{2,3},{3,2},{4,5},{5,4},{6,7},{7,6},{8,9},{9,8},{10,11... | collective-permute-start | bytes 1179656 | tf_op jit(solution)/shard_map/ppermute | solution.py:50
  34.5 9.9 %collective-permute-start.9 = (bf16[3,2,128,384]{3,2,1,0:T(8,128)(2,1)S(1)}, bf16[3,2,128,384]{3,2,1,0:T(8,128)(2,1)S(1)}, u32[]{:S(2)}, u32[]{:S(2)}) collective-permute-start(bf16[3,2,128,384]{3,2,1,0:T(8,128)(2,1)S(1)} %get-tuple-element.34.refs_10_), channel_id=1, source_target_pairs={{0,4},{1,3},{2,6},{3,1},{4,0},{5,7},{6,2},{7,5},{8,12},{9,11},{10,... | collective-permute-start | bytes 1769480 | tf_op jit(solution)/shard_map/ppermute | solution.py:50
  44.7 16.0 %collective-permute-start.14 = (bf16[3,2,128,384]{3,2,1,0:T(8,128)(2,1)S(1)}, bf16[3,2,128,384]{3,2,1,0:T(8,128)(2,1)S(1)}, u32[]{:S(2)}, u32[]{:S(2)}) collective-permute-start(bf16[3,2,128,384]{3,2,1,0:T(8,128)(2,1)S(1)} %get-tuple-element.45), channel_id=1, source_target_pairs={{0,2},{1,5},{2,0},{3,7},{4,6},{5,1},{6,4},{7,3},{8,10},{9,13},{10,... | collective-permute-start | bytes 1769480 | tf_op jit(solution)/shard_map/ppermute | solution.py:50
  47.8 11.6 %collective-permute-start.13 = (bf16[256,768]{1,0:T(8,128)(2,1)S(1)}, bf16[256,768]{1,0:T(8,128)(2,1)S(1)}, u32[]{:S(2)}, u32[]{:S(2)}) collective-permute-start(bf16[256,768]{1,0:T(8,128)(2,1)S(1)} %get-tuple-element.43), channel_id=1, source_target_pairs={{0,3},{8,11},{16,19},{24,27}} | collective-permute-start | bytes 1179656 | tf_op jit(solution)/shard_map/ppermute | solution.py:71
  50.2 3.1 %collective-permute-start.12 = (f32[6,8,256]{2,1,0:T(8,128)S(1)}, f32[6,8,256]{2,1,0:T(8,128)S(1)}, u32[]{:S(2)}, u32[]{:S(2)}) collective-permute-start(f32[6,8,256]{2,1,0:T(8,128)S(1)} %get-tuple-element.42), channel_id=1, source_target_pairs={{1,0},{2,1},{3,2},{4,3},{5,4},{6,5},{7,6},{9,8},{10,9},{11,10},{12... | collective-permute-start | bytes 147464 | tf_op jit(solution)/shard_map/ppermute | solution.py:681
  61.1 1.8 %collective-permute-start.15 = (bf16[2,2,128,384]{3,2,1,0:T(8,128)(2,1)S(1)}, bf16[2,2,128,384]{3,2,1,0:T(8,128)(2,1)S(1)}, u32[]{:S(2)}, u32[]{:S(2)}) collective-permute-start(bf16[2,2,128,384]{3,2,1,0:T(8,128)(2,1)S(1)} %get-tuple-element.47), channel_id=1, source_target_pairs={{0,1},{1,0},{2,3},{3,2},{4,5},{5,4},{6,7},{7,6},{8,9},{9,8},{10,11... | collective-permute-start | bytes 1179656 | tf_op jit(solution)/shard_map/ppermute | solution.py:50

commit v11 on v10

--- a/solution.py
+++ b/solution.py
@@ -526,14 +526,14 @@
         grad_query_ref[:, cols] = (grad_query * FACTOR).T.astype(BF16)
 
 
-def add_kernel(keep_ref, got_ref, *refs):
-    passed = len(refs) // 2 - 1
-    for source, out in zip(refs[:passed], refs[passed + 2 :]):
-        out[...] = source[...]
-    out_ref, send_ref = refs[passed : passed + 2]
+def add_kernel(keep_ref, got_ref, out_ref, send_ref):
     value = keep_ref[0 : got_ref.shape[0]] + got_ref[...].astype(F32)
     out_ref[...] = value
     send_ref[...] = value.astype(BF16)
+
+
+def pass_kernel(in_ref, out_ref):
+    out_ref[...] = in_ref[...]
 
 
 def owned_kernel(codes_ref, keep_ref, got_ref, mine_ref, pair_ref):
@@ -667,25 +667,23 @@
         flops=HIDING * piece_flops,
         name="rest",
     )
-    passing = [stats_all, direct_cotangent]
-    for step, (even_bit, odd_bit) in enumerate(turns[::-1]):
-        got = swap(send, even_bit, odd_bit, peers)
-        if step + 1 < len(turns):
-            keep, send, *passing = call(
-                add_kernel,
-                [sums, held, stats, shape(BF16, row_count, width)],
-                [keep, got, *passing],
-                after=[own_terms, next_queries],
-                name="add",
-            )
-    next_stats = lax.ppermute(passing[0], "tm", [(i, i - 1) for i in range(1, peers)])
-    relayed_cotangent = shift_second(passing[1], -1, 2, peers)
+    next_stats = lax.ppermute(stats_all, "tm", [(i, i - 1) for i in range(1, peers)])
+    (passed_on,) = call(
+        pass_kernel, [shape(BF16, row_count, width)], [direct_cotangent], after=[own_terms], name="pass_on"
+    )
+    relayed_cotangent = shift_second(passed_on, -1, 2, peers)
     (own,) = call(
         functools.partial(next_kernel, peers),
         [pair_sums],
         [rows, next_stats, pair_queries, next_queries, direct_cotangent, relayed_cotangent, joined, own_terms],
+        flops=HIDING * piece_flops,
         name="next",
     )
+    for step, (even_bit, odd_bit) in enumerate(turns[::-1]):
+        got = swap(send, even_bit, odd_bit, peers)
+        if step + 1 < len(turns):
+            after = [own_terms, next_queries]
+            keep, send = call(add_kernel, [sums, held], [keep, got], after=after, name="add")
     owned_mine, owned_send = call(
         owned_kernel,
         [shape(F32, FR_DEV, 2, frame_len, half_width), shape(BF16, FR_DEV, 2, frame_len, half_width)],

time: 64.1 us -> 60.7 us (0.947)
  waiting for transfers between devices: 18.3 us -> 16 us
  starting transfers between devices: 27.9 us -> 26.7 us
    ppermute x2, waiting for transfers between devices: 6.17 us -> 0.18 us  [shift_second(): return lax.ppermute(block, 'tm', pairs) if pairs else block]
    ppermute x9, waiting for transfers between devices: 10.3 us -> 15.8 us  [swap(): lax.ppermute(block, 'tm', [(i, i ^ (odd_bit if i & 1 else even_bit)) for...]
    ppermute x1, waiting for transfers between devices: 1.82 us -> 0.01 us  [body(): lax.ppermute(stats_all, 'tm', [(i, i - 1) for i in range(1, peers)])]
    ppermute x2, starting transfers between devices: 3 us -> 2 us  [shift_second(): return lax.ppermute(block, 'tm', pairs) if pairs else block]
    pallas_call x11 -> x12, Pallas kernels: 14.5 us -> 14.6 us  [call(): pl.pallas_call(run, out_shape=outs, in_specs=[SMEM] * len(scalars) + [VME...]
  transfers between devices with their start and end apart: 16 -> 16, of which waited for: 6 -> 6; matrix products, arithmetic and copies ran while one was open for 0% -> 0% of each run, Pallas kernels for 22% -> 24%
where the time goes in v11:
time: 60.7 us; the launch traced here: 60.4 us
  starting transfers between devices  26.7 us (44%)
  Pallas kernels  16.9 us (28%)
  waiting for transfers between devices  16 us (26%)
  between operations  0.86 us (1%)
    ppermute x9, starting transfers between devices, swap(): lax.ppermute(block, 'tm', [(i, i ^ (odd_bit if i & 1 else even_bit)) for...  20 us
    ppermute x9, waiting for transfers between devices, swap(): lax.ppermute(block, 'tm', [(i, i ^ (odd_bit if i & 1 else even_bit)) for...  15.8 us
    pallas_call x12, Pallas kernels, call(): pl.pallas_call(run, out_shape=outs, in_specs=[SMEM] * len(scalars) + [VME...  14.6 us
    pallas_call x2, Pallas kernels, join(): pl.pallas_call(run, out_shape=shape(BF16, rows, width), in_specs=[pl.Bloc...  2.34 us
    ppermute x2, starting transfers between devices, shift_second(): return lax.ppermute(block, 'tm', pairs) if pairs else block  2 us
    ppermute x2, starting transfers between devices, shift_first(): lax.ppermute(block, 'tm', [(i, relays.get((i, j), j)) for i, j in pairs])  1.97 us
    ppermute x2, starting transfers between devices, shift(): return lax.ppermute(block, 'tm', pairs)  1.36 us
    ppermute x1, starting transfers between devices, body(): lax.ppermute(stats_all, 'tm', [(i, i - 1) for i in range(1, peers)])  1.29 us
  transfers between devices with their start and end apart: 16, of which 6 were waited for; matrix products, arithmetic and copies ran while one was open for 0% of the time, Pallas kernels for 24%

profile of v11, /device:TPU:0, one launch (start us, length us, event | category | flops | bytes accessed | tf_op | source)
XLA Modules:
  0.0 60.4 jit_solution(3699016698386077765)
XLA Ops:
  0.7 1.2 %join.1.refs_5_.refs_1_.refs_6_.refs_7_ = bf16[528,768]{1,0:T(8,128)(2,1)S(1)} custom-call(s32[1,2]{1,0:T(1,128)} %refs_1_.4, bf16[256,768]{1,0:T(8,128)(2,1)} %refs_1_.3, bf16[256,768]{1,0:T(8,128)(2,1)} %refs_2_.2), custom_call_target="tpu_custom_call" | custom-call | tf_op jit(solution)/shard_map/join/pallas_call | solution.py:594
  1.9 0.5 collective-permute-start
  2.4 0.7 %collective-permute-start.1 = (bf16[256,768]{1,0:T(8,128)(2,1)S(1)}, bf16[256,768]{1,0:T(8,128)(2,1)S(1)}, u32[]{:S(2)}, u32[]{:S(2)}) collective-permute-start(bf16[256,768]{1,0:T(8,128)(2,1)S(1)} %copy-done.4), channel_id=1, source_target_pairs={{1,2},{3,7},{5,6},{9,10},{11,15},{13,14},{17,18},{19,23},{21,22},{... | collective-permute-start | bytes 1179656 | tf_op jit(solution)/shard_map/ppermute | solution.py:66
  3.1 1.3 %collective-permute-done.refs_4_.refs_2_.refs_5_.refs_6_ = bf16[528,768]{1,0:T(8,128)(2,1)S(1)} collective-permute-done((bf16[528,768]{1,0:T(8,128)(2,1)S(1)}, bf16[528,768]{1,0:T(8,128)(2,1)S(1)}, u32[]{:S(2)}, u32[]{:S(2)}) %collective-permute-start) | collective-permute-done | bytes 811040 | tf_op jit(solution)/shard_map/ppermute | solution.py:50
  4.3 0.3 split.1.refs_2_.refs_1_
  4.7 0.0 copy-start.1
  4.7 0.0 copy-start.2
  4.7 0.0 copy-start.3
  4.7 2.9 %collective-permute-start.4 = (bf16[3,2,128,384]{3,2,1,0:T(8,128)(2,1)S(1)}, bf16[3,2,128,384]{3,2,1,0:T(8,128)(2,1)S(1)}, u32[]{:S(2)}, u32[]{:S(2)}) collective-permute-start(bf16[3,2,128,384]{3,2,1,0:T(8,128)(2,1)S(1)} %split.1.refs_2_.refs_1_), channel_id=1, source_target_pairs={{0,2},{1,5},{2,0},{3,7},{4,6},{5,1},{6,4},{7,3},{8,10},{9,13},{10,... | collective-permute-start | bytes 1769480 | tf_op jit(solution)/shard_map/ppermute | solution.py:50
  7.6 1.1 %join_queries.1.refs_1_.refs_4_.refs_2_ = bf16[512,768]{1,0:T(8,128)(2,1)S(1)} custom-call(bf16[256,768]{1,0:T(8,128)(2,1)} %refs_0_.3, bf16[256,768]{1,0:T(8,128)(2,1)} %refs_1_.5, bf16[3,2,128,384]{3,2,1,0:T(8,128)(2,1)S(1)} %split.1.refs_2_.refs_1_), custom_call_target="tpu_custom_call" | custom-call | tf_op jit(solution)/shard_map/join_queries/pallas_call | solution.py:594
  8.8 1.1 %collective-permute-start.5 = (bf16[512,768]{1,0:T(8,128)(2,1)S(1)}, bf16[512,768]{1,0:T(8,128)(2,1)S(1)}, u32[]{:S(2)}, u32[]{:S(2)}) collective-permute-start(bf16[512,768]{1,0:T(8,128)(2,1)S(1)} %join_queries.1.refs_1_.refs_4_.refs_2_), channel_id=1, source_target_pairs={{0,1},{1,0},{2,3},{3,2},{4,5},{5,4},{6,7},{7,6},{8,9},{9,8},{10,11... | collective-permute-start | bytes 2359304 | tf_op jit(solution)/shard_map/ppermute | solution.py:50
  9.9 0.0 collective-permute-done.1.refs_6_.refs_2_.refs_3_
  9.9 1.7 %plan.1 = (f32[6,16,256]{2,1,0:T(8,128)S(1)}, s32[8,128]{1,0:T(8,128)S(1)}, bf16[256,768]{1,0:T(8,128)(2,1)S(1)}, bf16[256,768]{1,0:T(8,128)(2,1)S(1)}) custom-call(s32[1,4]{1,0:T(1,128)S(1)} %bitcast.2, s32[1,2]{1,0:T(1,128)S(1)} %copy-done.1, s32[16]{0:T(128)S(1)} %copy-done.3, f32[6,16,16]{2,1,0:T(8,128)S(1)} %copy-done.2, ...), custom_call_target="tpu_custom_call" | custom-call | flops 20132659200 | tf_op jit(solution)/shard_map/plan/pallas_call | solution.py:38
  11.6 0.7 %collective-permute-start.2 = (bf16[256,768]{1,0:T(8,128)(2,1)S(1)}, bf16[256,768]{1,0:T(8,128)(2,1)S(1)}, u32[]{:S(2)}, u32[]{:S(2)}) collective-permute-start(bf16[256,768]{1,0:T(8,128)(2,1)S(1)} %get-tuple-element.26), channel_id=1, source_target_pairs={{7,4},{15,12},{23,20},{31,28}} | collective-permute-start | bytes 1179656 | tf_op jit(solution)/shard_map/ppermute | solution.py:71
  12.3 0.7 %collective-permute-start.3 = (bf16[256,768]{1,0:T(8,128)(2,1)S(1)}, bf16[256,768]{1,0:T(8,128)(2,1)S(1)}, u32[]{:S(2)}, u32[]{:S(2)}) collective-permute-start(bf16[256,768]{1,0:T(8,128)(2,1)S(1)} %get-tuple-element.27), channel_id=1, source_target_pairs={{1,2},{3,4},{5,6},{9,10},{11,12},{13,14},{17,18},{19,20},{21,22},{... | collective-permute-start | bytes 1179656 | tf_op jit(solution)/shard_map/ppermute | solution.py:55
  12.9 4.9 %collective-permute-done.4.refs_2_ = bf16[3,2,128,384]{3,2,1,0:T(8,128)(2,1)S(1)} collective-permute-done((bf16[3,2,128,384]{3,2,1,0:T(8,128)(2,1)S(1)}, bf16[3,2,128,384]{3,2,1,0:T(8,128)(2,1)S(1)}, u32[]{:S(2)}, u32[]{:S(2)}) %collective-permute-start.4) | collective-permute-done | bytes 589856 | tf_op jit(solution)/shard_map/ppermute | solution.py:50
  17.8 0.0 collective-permute-done.5.refs_4_.refs_5_.refs_2_
  17.8 0.3 step.1.refs_1_
  18.1 1.6 %collective-permute-start.6 = (bf16[3,2,128,384]{3,2,1,0:T(8,128)(2,1)S(1)}, bf16[3,2,128,384]{3,2,1,0:T(8,128)(2,1)S(1)}, u32[]{:S(2)}, u32[]{:S(2)}) collective-permute-start(bf16[3,2,128,384]{3,2,1,0:T(8,128)(2,1)S(1)} %step.1.refs_1_), channel_id=1, source_target_pairs={{0,4},{1,3},{2,6},{3,1},{4,0},{5,7},{6,2},{7,5},{8,12},{9,11},{10,... | collective-permute-start | bytes 1769480 | tf_op jit(solution)/shard_map/ppermute | solution.py:50
  19.7 0.0 collective-permute-done.2.refs_3_.refs_4_
  19.7 0.0 collective-permute-done.3.refs_4_.refs_5_
  19.7 1.6 %stats.1 = (f32[6,8,256]{2,1,0:T(8,128)S(1)}, bf16[256,768]{1,0:T(8,128)(2,1)S(1)}, bf16[256,768]{1,0:T(8,128)(2,1)S(1)}) custom-call(f32[6,16,256]{2,1,0:T(8,128)S(1)} %get-tuple-element.25.refs_0_.refs_1_, bf16[512,768]{1,0:T(8,128)(2,1)S(1)} %join_queries.1.refs_1_.refs_4_.refs_2_, bf16[256,768]{1,0:T(8,128)(2,1)S(1)} %collective-permute-done.1.refs_6_.refs_2_.refs_3_, ...), custom_call_target="tpu_custom_call" | custom-call | flops 20132659200 | tf_op jit(solution)/shard_map/stats/pallas_call | solution.py:38
  21.3 6.2 %collective-permute-start.8 = (f32[6,8,256]{2,1,0:T(8,128)S(1)}, f32[6,8,256]{2,1,0:T(8,128)S(1)}, u32[]{:S(2)}, u32[]{:S(2)}) collective-permute-start(f32[6,8,256]{2,1,0:T(8,128)S(1)} %get-tuple-element.28.refs_2_.refs_1_), channel_id=1, source_target_pairs={{0,1},{1,0},{2,3},{3,2},{4,5},{5,4},{6,7},{7,6},{8,9},{9,8},{10,11... | collective-permute-start | bytes 147464 | tf_op jit(solution)/shard_map/ppermute | solution.py:50
  27.5 0.7 %collective-permute-start.10 = (bf16[256,768]{1,0:T(8,128)(2,1)S(1)}, bf16[256,768]{1,0:T(8,128)(2,1)S(1)}, u32[]{:S(2)}, u32[]{:S(2)}) collective-permute-start(bf16[256,768]{1,0:T(8,128)(2,1)S(1)} %get-tuple-element.36), channel_id=1, source_target_pairs={{2,1},{4,3},{6,5},{10,9},{12,11},{14,13},{18,17},{20,19},{22,21},{... | collective-permute-start | bytes 1179656 | tf_op jit(solution)/shard_map/ppermute | solution.py:55
  28.2 1.3 %collective-permute-start.11 = (bf16[256,768]{1,0:T(8,128)(2,1)S(1)}, bf16[256,768]{1,0:T(8,128)(2,1)S(1)}, u32[]{:S(2)}, u32[]{:S(2)}) collective-permute-start(bf16[256,768]{1,0:T(8,128)(2,1)S(1)} %get-tuple-element.37), channel_id=1, source_target_pairs={{2,1},{4,0},{6,5},{10,9},{12,8},{14,13},{18,17},{20,16},{22,21},{2... | collective-permute-start | bytes 1179656 | tf_op jit(solution)/shard_map/ppermute | solution.py:66
  29.5 0.0 collective-permute-done.6.refs_2_
  29.5 0.3 pick.1
  29.8 2.7 %collective-permute-start.7 = (bf16[2,2,128,384]{3,2,1,0:T(8,128)(2,1)S(1)}, bf16[2,2,128,384]{3,2,1,0:T(8,128)(2,1)S(1)}, u32[]{:S(2)}, u32[]{:S(2)}) collective-permute-start(bf16[2,2,128,384]{3,2,1,0:T(8,128)(2,1)S(1)} %get-tuple-element.31.refs_7_), channel_id=1, source_target_pairs={{0,1},{1,0},{2,3},{3,2},{4,5},{5,4},{6,7},{7,6},{8,9},{9,8},{10,11... | collective-permute-start | bytes 1179656 | tf_op jit(solution)/shard_map/ppermute | solution.py:50
  32.5 0.0 collective-permute-done.8.refs_3_
  32.5 2.0 %memory.1 = (f32[4,2,128,384]{3,2,1,0:T(8,128)S(1)}, bf16[3,2,128,384]{3,2,1,0:T(8,128)(2,1)S(1)}) custom-call(s32[8,128]{1,0:T(8,128)S(1)} %get-tuple-element.29.refs_3_.refs_0_, f32[6,16,256]{2,1,0:T(8,128)S(1)} %get-tuple-element.25.refs_0_.refs_1_, f32[6,8,256]{2,1,0:T(8,128)S(1)} %get-tuple-element.28.refs_2_.refs_1_, ...), custom_call_target="tpu_custom_call" | custom-call | flops 20132659200 | tf_op jit(solution)/shard_map/memory/pallas_call | solution.py:38
  34.5 2.6 %collective-permute-start.13 = (bf16[3,2,128,384]{3,2,1,0:T(8,128)(2,1)S(1)}, bf16[3,2,128,384]{3,2,1,0:T(8,128)(2,1)S(1)}, u32[]{:S(2)}, u32[]{:S(2)}) collective-permute-start(bf16[3,2,128,384]{3,2,1,0:T(8,128)(2,1)S(1)} %get-tuple-element.32.refs_10_), channel_id=1, source_target_pairs={{0,4},{1,3},{2,6},{3,1},{4,0},{5,7},{6,2},{7,5},{8,12},{9,11},{10,... | collective-permute-start | bytes 1769480 | tf_op jit(solution)/shard_map/ppermute | solution.py:50
  37.1 0.0 collective-permute-done.7.refs_9_
  37.1 5.6 %rest.1 = (bf16[256,768]{1,0:T(8,128)(2,1)}, bf16[256,768]{1,0:T(8,128)(2,1)}, f32[2,256,768]{2,1,0:T(8,128)S(1)}, f32[6,8,256]{2,1,0:T(8,128)S(1)}) custom-call(f32[6,16,256]{2,1,0:T(8,128)S(1)} %get-tuple-element.25.refs_0_.refs_1_, f32[6,8,256]{2,1,0:T(8,128)S(1)} %get-tuple-element.28.refs_2_.refs_1_, ...), custom_call_target="tpu_custom_call" | custom-call | flops 20132659200 | tf_op jit(solution)/shard_map/rest/pallas_call | solution.py:38
  42.8 0.0 collective-permute-done.11.refs_0_.refs_4_
  42.8 1.3 %collective-permute-start.12 = (bf16[256,768]{1,0:T(8,128)(2,1)S(1)}, bf16[256,768]{1,0:T(8,128)(2,1)S(1)}, u32[]{:S(2)}, u32[]{:S(2)}) collective-permute-start(bf16[256,768]{1,0:T(8,128)(2,1)S(1)} %pass_on.1), channel_id=1, source_target_pairs={{0,3},{8,11},{16,19},{24,27}} | collective-permute-start | bytes 1179656 | tf_op jit(solution)/shard_map/ppermute | solution.py:71
  44.1 1.3 %collective-permute-start.9 = (f32[6,8,256]{2,1,0:T(8,128)S(1)}, f32[6,8,256]{2,1,0:T(8,128)S(1)}, u32[]{:S(2)}, u32[]{:S(2)}) collective-permute-start(f32[6,8,256]{2,1,0:T(8,128)S(1)} %get-tuple-element.35), channel_id=1, source_target_pairs={{1,0},{2,1},{3,2},{4,3},{5,4},{6,5},{7,6},{9,8},{10,9},{11,10},{12... | collective-permute-start | bytes 147464 | tf_op jit(solution)/shard_map/ppermute | solution.py:670
  45.4 0.0 collective-permute-done.10.refs_3_
  45.4 1.3 %collective-permute-done.13.refs_1_ = bf16[3,2,128,384]{3,2,1,0:T(8,128)(2,1)S(1)} collective-permute-done((bf16[3,2,128,384]{3,2,1,0:T(8,128)(2,1)S(1)}, bf16[3,2,128,384]{3,2,1,0:T(8,128)(2,1)S(1)}, u32[]{:S(2)}, u32[]{:S(2)}) %collective-permute-start.13) | collective-permute-done | bytes 589856 | tf_op jit(solution)/shard_map/ppermute | solution.py:50
  46.7 0.2 add.1
  46.9 2.3 %collective-permute-start.14 = (bf16[3,2,128,384]{3,2,1,0:T(8,128)(2,1)S(1)}, bf16[3,2,128,384]{3,2,1,0:T(8,128)(2,1)S(1)}, u32[]{:S(2)}, u32[]{:S(2)}) collective-permute-start(bf16[3,2,128,384]{3,2,1,0:T(8,128)(2,1)S(1)} %get-tuple-element.41), channel_id=1, source_target_pairs={{0,2},{1,5},{2,0},{3,7},{4,6},{5,1},{6,4},{7,3},{8,10},{9,13},{10,... | collective-permute-start | bytes 1769480 | tf_op jit(solution)/shard_map/ppermute | solution.py:50
  49.2 0.0 collective-permute-done.9.refs_1_
  49.2 0.2 collective-permute-done.12.refs_5_
  49.4 1.3 %next.1.refs_3_.refs_0_ = f32[2,256,768]{2,1,0:T(8,128)S(1)} custom-call(f32[6,16,256]{2,1,0:T(8,128)S(1)} %get-tuple-element.25.refs_0_.refs_1_, f32[6,8,256]{2,1,0:T(8,128)S(1)} %collective-permute-done.9.refs_1_, bf16[512,768]{1,0:T(8,128)(2,1)S(1)} %collective-permute-done.5.refs_4_.refs_5_.refs_2_, ...), custom_call_target="tpu_custom_call" | custom-call | flops 20132659200 | tf_op jit(solution)/shard_map/next/pallas_call | solution.py:38
  50.7 6.6 %collective-permute-done.14.refs_2_ = bf16[3,2,128,384]{3,2,1,0:T(8,128)(2,1)S(1)} collective-permute-done((bf16[3,2,128,384]{3,2,1,0:T(8,128)(2,1)S(1)}, bf16[3,2,128,384]{3,2,1,0:T(8,128)(2,1)S(1)}, u32[]{:S(2)}, u32[]{:S(2)}) %collective-permute-start.14) | collective-permute-done | bytes 589856 | tf_op jit(solution)/shard_map/ppermute | solution.py:50
  57.3 0.3 owned.1
  57.6 0.1 collective-permute-start.15
  57.7 1.7 %collective-permute-done.15.refs_2_ = bf16[2,2,128,384]{3,2,1,0:T(8,128)(2,1)S(1)} collective-permute-done((bf16[2,2,128,384]{3,2,1,0:T(8,128)(2,1)S(1)}, bf16[2,2,128,384]{3,2,1,0:T(8,128)(2,1)S(1)}, u32[]{:S(2)}, u32[]{:S(2)}) %collective-permute-start.15) | collective-permute-done | bytes 393248 | tf_op jit(solution)/shard_map/ppermute | solution.py:50
  59.4 1.0 %final.1 = (bf16[256,768]{1,0:T(8,128)(2,1)}, bf16[256,768]{1,0:T(8,128)(2,1)}) custom-call(f32[2,256,768]{2,1,0:T(8,128)S(1)} %next.1.refs_3_.refs_0_, f32[2,2,128,384]{3,2,1,0:T(8,128)S(1)} %get-tuple-element.42.refs_1_, bf16[2,2,128,384]{3,2,1,0:T(8,128)(2,1)S(1)} %collective-permute-done.15.refs_2_), custom_call_target="tpu_custom_call" | custom-call | tf_op jit(solution)/shard_map/final/pallas_call | solution.py:38
  (8 shorter events, 0.0 us)
Async XLA Ops:
  0.6 1.8 %copy-start.4 = (bf16[256,768]{1,0:T(8,128)(2,1)S(1)}, bf16[256,768]{1,0:T(8,128)(2,1)}, u32[]{:S(2)}) copy-start(bf16[256,768]{1,0:T(8,128)(2,1)} %refs_1_.3) | copy-start | bytes 1179652
  0.6 3.7 %copy-start = (s32[4]{0:T(128)S(1)}, s32[4]{0:T(128)}, u32[]{:S(2)}) copy-start(s32[4]{0:T(128)} %param.15) | copy-start | bytes 52
  1.9 2.5 %collective-permute-start = (bf16[528,768]{1,0:T(8,128)(2,1)S(1)}, bf16[528,768]{1,0:T(8,128)(2,1)S(1)}, u32[]{:S(2)}, u32[]{:S(2)}) collective-permute-start(bf16[528,768]{1,0:T(8,128)(2,1)S(1)} %join.1.refs_5_.refs_1_.refs_6_.refs_7_), channel_id=1, source_target_pairs={{0,1},{1,0},{2,3},{3,2},{4,5},{5,4},{6,7},{7,6},{8,9},{9,8},{10,11... | collective-permute-start | bytes 2433032 | tf_op jit(solution)/shard_map/ppermute | solution.py:50
  2.4 7.5 %collective-permute-start.1 = (bf16[256,768]{1,0:T(8,128)(2,1)S(1)}, bf16[256,768]{1,0:T(8,128)(2,1)S(1)}, u32[]{:S(2)}, u32[]{:S(2)}) collective-permute-start(bf16[256,768]{1,0:T(8,128)(2,1)S(1)} %copy-done.4), channel_id=1, source_target_pairs={{1,2},{3,7},{5,6},{9,10},{11,15},{13,14},{17,18},{19,23},{21,22},{... | collective-permute-start | bytes 1179656 | tf_op jit(solution)/shard_map/ppermute | solution.py:66
  4.7 5.2 %copy-start.1 = (s32[1,2]{1,0:T(1,128)S(1)}, s32[1,2]{1,0:T(1,128)}, u32[]{:S(2)}) copy-start(s32[1,2]{1,0:T(1,128)} %refs_1_.4) | copy-start | bytes 28
  4.7 5.2 %copy-start.2 = (f32[6,16,16]{2,1,0:T(8,128)S(1)}, f32[6,16,16]{2,1,0:T(8,128)}, u32[]{:S(2)}) copy-start(f32[6,16,16]{2,1,0:T(8,128)} %refs_3_.1) | copy-start | bytes 18436
  4.7 5.2 %copy-start.3 = (s32[16]{0:T(128)S(1)}, s32[16]{0:T(128)}, u32[]{:S(2)}) copy-start(s32[16]{0:T(128)} %refs_2_.3) | copy-start | bytes 196
  4.7 13.1 %collective-permute-start.4 = (bf16[3,2,128,384]{3,2,1,0:T(8,128)(2,1)S(1)}, bf16[3,2,128,384]{3,2,1,0:T(8,128)(2,1)S(1)}, u32[]{:S(2)}, u32[]{:S(2)}) collective-permute-start(bf16[3,2,128,384]{3,2,1,0:T(8,128)(2,1)S(1)} %split.1.refs_2_.refs_1_), channel_id=1, source_target_pairs={{0,2},{1,5},{2,0},{3,7},{4,6},{5,1},{6,4},{7,3},{8,10},{9,13},{10,... | collective-permute-start | bytes 1769480 | tf_op jit(solution)/shard_map/ppermute | solution.py:50
  8.8 9.1 %collective-permute-start.5 = (bf16[512,768]{1,0:T(8,128)(2,1)S(1)}, bf16[512,768]{1,0:T(8,128)(2,1)S(1)}, u32[]{:S(2)}, u32[]{:S(2)}) collective-permute-start(bf16[512,768]{1,0:T(8,128)(2,1)S(1)} %join_queries.1.refs_1_.refs_4_.refs_2_), channel_id=1, source_target_pairs={{0,1},{1,0},{2,3},{3,2},{4,5},{5,4},{6,7},{7,6},{8,9},{9,8},{10,11... | collective-permute-start | bytes 2359304 | tf_op jit(solution)/shard_map/ppermute | solution.py:50
  11.6 8.2 %collective-permute-start.2 = (bf16[256,768]{1,0:T(8,128)(2,1)S(1)}, bf16[256,768]{1,0:T(8,128)(2,1)S(1)}, u32[]{:S(2)}, u32[]{:S(2)}) collective-permute-start(bf16[256,768]{1,0:T(8,128)(2,1)S(1)} %get-tuple-element.26), channel_id=1, source_target_pairs={{7,4},{15,12},{23,20},{31,28}} | collective-permute-start | bytes 1179656 | tf_op jit(solution)/shard_map/ppermute | solution.py:71
  12.3 7.5 %collective-permute-start.3 = (bf16[256,768]{1,0:T(8,128)(2,1)S(1)}, bf16[256,768]{1,0:T(8,128)(2,1)S(1)}, u32[]{:S(2)}, u32[]{:S(2)}) collective-permute-start(bf16[256,768]{1,0:T(8,128)(2,1)S(1)} %get-tuple-element.27), channel_id=1, source_target_pairs={{1,2},{3,4},{5,6},{9,10},{11,12},{13,14},{17,18},{19,20},{21,22},{... | collective-permute-start | bytes 1179656 | tf_op jit(solution)/shard_map/ppermute | solution.py:55
  18.1 11.3 %collective-permute-start.6 = (bf16[3,2,128,384]{3,2,1,0:T(8,128)(2,1)S(1)}, bf16[3,2,128,384]{3,2,1,0:T(8,128)(2,1)S(1)}, u32[]{:S(2)}, u32[]{:S(2)}) collective-permute-start(bf16[3,2,128,384]{3,2,1,0:T(8,128)(2,1)S(1)} %step.1.refs_1_), channel_id=1, source_target_pairs={{0,4},{1,3},{2,6},{3,1},{4,0},{5,7},{6,2},{7,5},{8,12},{9,11},{10,... | collective-permute-start | bytes 1769480 | tf_op jit(solution)/shard_map/ppermute | solution.py:50
  21.3 11.2 %collective-permute-start.8 = (f32[6,8,256]{2,1,0:T(8,128)S(1)}, f32[6,8,256]{2,1,0:T(8,128)S(1)}, u32[]{:S(2)}, u32[]{:S(2)}) collective-permute-start(f32[6,8,256]{2,1,0:T(8,128)S(1)} %get-tuple-element.28.refs_2_.refs_1_), channel_id=1, source_target_pairs={{0,1},{1,0},{2,3},{3,2},{4,5},{5,4},{6,7},{7,6},{8,9},{9,8},{10,11... | collective-permute-start | bytes 147464 | tf_op jit(solution)/shard_map/ppermute | solution.py:50
  27.5 17.9 %collective-permute-start.10 = (bf16[256,768]{1,0:T(8,128)(2,1)S(1)}, bf16[256,768]{1,0:T(8,128)(2,1)S(1)}, u32[]{:S(2)}, u32[]{:S(2)}) collective-permute-start(bf16[256,768]{1,0:T(8,128)(2,1)S(1)} %get-tuple-element.36), channel_id=1, source_target_pairs={{2,1},{4,3},{6,5},{10,9},{12,11},{14,13},{18,17},{20,19},{22,21},{... | collective-permute-start | bytes 1179656 | tf_op jit(solution)/shard_map/ppermute | solution.py:55
  28.2 14.6 %collective-permute-start.11 = (bf16[256,768]{1,0:T(8,128)(2,1)S(1)}, bf16[256,768]{1,0:T(8,128)(2,1)S(1)}, u32[]{:S(2)}, u32[]{:S(2)}) collective-permute-start(bf16[256,768]{1,0:T(8,128)(2,1)S(1)} %get-tuple-element.37), channel_id=1, source_target_pairs={{2,1},{4,0},{6,5},{10,9},{12,8},{14,13},{18,17},{20,16},{22,21},{2... | collective-permute-start | bytes 1179656 | tf_op jit(solution)/shard_map/ppermute | solution.py:66
  29.8 7.3 %collective-permute-start.7 = (bf16[2,2,128,384]{3,2,1,0:T(8,128)(2,1)S(1)}, bf16[2,2,128,384]{3,2,1,0:T(8,128)(2,1)S(1)}, u32[]{:S(2)}, u32[]{:S(2)}) collective-permute-start(bf16[2,2,128,384]{3,2,1,0:T(8,128)(2,1)S(1)} %get-tuple-element.31.refs_7_), channel_id=1, source_target_pairs={{0,1},{1,0},{2,3},{3,2},{4,5},{5,4},{6,7},{7,6},{8,9},{9,8},{10,11... | collective-permute-start | bytes 1179656 | tf_op jit(solution)/shard_map/ppermute | solution.py:50
  34.5 12.2 %collective-permute-start.13 = (bf16[3,2,128,384]{3,2,1,0:T(8,128)(2,1)S(1)}, bf16[3,2,128,384]{3,2,1,0:T(8,128)(2,1)S(1)}, u32[]{:S(2)}, u32[]{:S(2)}) collective-permute-start(bf16[3,2,128,384]{3,2,1,0:T(8,128)(2,1)S(1)} %get-tuple-element.32.refs_10_), channel_id=1, source_target_pairs={{0,4},{1,3},{2,6},{3,1},{4,0},{5,7},{6,2},{7,5},{8,12},{9,11},{10,... | collective-permute-start | bytes 1769480 | tf_op jit(solution)/shard_map/ppermute | solution.py:50
  42.8 6.6 %collective-permute-start.12 = (bf16[256,768]{1,0:T(8,128)(2,1)S(1)}, bf16[256,768]{1,0:T(8,128)(2,1)S(1)}, u32[]{:S(2)}, u32[]{:S(2)}) collective-permute-start(bf16[256,768]{1,0:T(8,128)(2,1)S(1)} %pass_on.1), channel_id=1, source_target_pairs={{0,3},{8,11},{16,19},{24,27}} | collective-permute-start | bytes 1179656 | tf_op jit(solution)/shard_map/ppermute | solution.py:71
  44.1 5.1 %collective-permute-start.9 = (f32[6,8,256]{2,1,0:T(8,128)S(1)}, f32[6,8,256]{2,1,0:T(8,128)S(1)}, u32[]{:S(2)}, u32[]{:S(2)}) collective-permute-start(f32[6,8,256]{2,1,0:T(8,128)S(1)} %get-tuple-element.35), channel_id=1, source_target_pairs={{1,0},{2,1},{3,2},{4,3},{5,4},{6,5},{7,6},{9,8},{10,9},{11,10},{12... | collective-permute-start | bytes 147464 | tf_op jit(solution)/shard_map/ppermute | solution.py:670
  46.9 10.4 %collective-permute-start.14 = (bf16[3,2,128,384]{3,2,1,0:T(8,128)(2,1)S(1)}, bf16[3,2,128,384]{3,2,1,0:T(8,128)(2,1)S(1)}, u32[]{:S(2)}, u32[]{:S(2)}) collective-permute-start(bf16[3,2,128,384]{3,2,1,0:T(8,128)(2,1)S(1)} %get-tuple-element.41), channel_id=1, source_target_pairs={{0,2},{1,5},{2,0},{3,7},{4,6},{5,1},{6,4},{7,3},{8,10},{9,13},{10,... | collective-permute-start | bytes 1769480 | tf_op jit(solution)/shard_map/ppermute | solution.py:50
  57.6 1.8 %collective-permute-start.15 = (bf16[2,2,128,384]{3,2,1,0:T(8,128)(2,1)S(1)}, bf16[2,2,128,384]{3,2,1,0:T(8,128)(2,1)S(1)}, u32[]{:S(2)}, u32[]{:S(2)}) collective-permute-start(bf16[2,2,128,384]{3,2,1,0:T(8,128)(2,1)S(1)} %get-tuple-element.43), channel_id=1, source_target_pairs={{0,1},{1,0},{2,3},{3,2},{4,5},{5,4},{6,7},{7,6},{8,9},{9,8},{10,11... | collective-permute-start | bytes 1179656 | tf_op jit(solution)/shard_map/ppermute | solution.py:50

commit v12 on v11

--- a/solution.py
+++ b/solution.py
@@ -64,6 +64,17 @@
     relays = relays_of(by, start, peers)
     pairs = [(i, i + by) for i in range(start, peers, 2) if 0 <= i + by < peers]
     return lax.ppermute(block, "tm", [(i, relays.get((i, j), j)) for i, j in pairs])
+
+
+def shift_straight(block, by, start, peers):
+    relays = relays_of(by, start, peers)
+    pairs = [(i, i + by) for i in range(start, peers, 2) if 0 <= i + by < peers]
+    return lax.ppermute(block, "tm", [pair for pair in pairs if pair not in relays])
+
+
+def shift_diagonal(block, by, start, peers):
+    pairs = list(relays_of(by, start, peers))
+    return lax.ppermute(block, "tm", pairs) if pairs else block
 
 
 def shift_second(block, by, start, peers):
@@ -188,16 +199,19 @@
     pair_ref,
     joined_ref,
     direct_keys,
+    queries_ref,
     rows_ref,
     codes_ref,
     values_out,
     keys_out,
+    queries_out,
 ):
     me = lax.axis_index("tm")
     last_frame = peers * FR_DEV - 1
     heads, _, row_count = rows_ref.shape
     values_out[...] = joined_ref[row_count : 2 * row_count, :]
     keys_out[...] = direct_keys[...]
+    queries_out[...] = queries_ref[0:row_count]
     bank = [bank_ref[0, slot] for slot in range(bank_ref.shape[1])]
     tail = pair_ref.shape[0] - TAIL
     pair_ids = []
@@ -431,7 +445,8 @@
     rows_ref,
     stats_ref,
     pair_queries,
-    outer_queries,
+    straight_queries,
+    diagonal_queries,
     direct_cotangent,
     relayed_cotangent,
     own_ref,
@@ -444,8 +459,9 @@
 
     def operands(head):
         cols = head_cols(head)
+        query = jnp.where(relayed, diagonal_queries[:, cols], straight_queries[:, cols])
         cotangent = jnp.where(relayed, relayed_cotangent[:, cols], direct_cotangent[:, cols])
-        outer = outer_queries[:, cols], cotangent
+        outer = query, cotangent
         return [jnp.where(even, a, b) for a, b in zip(joined_parts(pair_queries, cols), outer)]
 
     def products(head):
@@ -618,15 +634,16 @@
     pair_queries = swap(queries, 1, 1, peers)
 
     bias_rows = -(-(5 * FR_DEV) // 8) * 8
-    rows, codes, values_out, keys_out = call(
+    rows, codes, values_out, keys_out, queries_out = call(
         functools.partial(plan_kernel, peers, last_bits),
-        [shape(F32, heads, bias_rows, row_count), shape(jnp.int32, 8, 128)] + [shape(BF16, row_count, width)] * 2,
-        [pair, joined, direct_keys],
+        [shape(F32, heads, bias_rows, row_count), shape(jnp.int32, 8, 128)] + [shape(BF16, row_count, width)] * 3,
+        [pair, joined, direct_keys, queries],
         scalars=[bank_frames, memory_index, camera_pose, pose_bias],
         flops=HIDING * piece_flops,
         name="plan",
     )
     outer = [direct_keys, shift_second(keys_out, 1, 1, peers), shift(values_out, 1, 1, peers)]
+    straight_queries = shift_straight(queries_out, -1, 2, peers)
     even_done = odd_done = 1
     for step, (even_bit, odd_bit) in enumerate(turns):
         got = swap(mine, even_bit, odd_bit, peers)
@@ -642,11 +659,12 @@
         functools.partial(stats_kernel, peers),
         [stats] + [shape(BF16, row_count, width)] * 2,
         [rows, queries, *outer, pair, joined],
+        after=[straight_queries],
         flops=HIDING * piece_flops,
         name="stats",
     )
     pair_part = swap(part, 1, 1, peers)
-    next_queries = shift(queries_out, -1, 2, peers)
+    diagonal_queries = shift_diagonal(queries_out, -1, 2, peers)
     direct_cotangent = shift_first(cotangent_out, -1, 2, peers)
     chosen = shape(BF16, MEM, 2, frame_len, half_width)
     own_mem, pair_mem = call(pick_kernel, [chosen] * 2, [codes, mine, got], name="pick")
@@ -675,14 +693,14 @@
     (own,) = call(
         functools.partial(next_kernel, peers),
         [pair_sums],
-        [rows, next_stats, pair_queries, next_queries, direct_cotangent, relayed_cotangent, joined, own_terms],
+        [rows, next_stats, pair_queries, straight_queries, diagonal_queries, direct_cotangent, relayed_cotangent, joined, own_terms],
         flops=HIDING * piece_flops,
         name="next",
     )
     for step, (even_bit, odd_bit) in enumerate(turns[::-1]):
         got = swap(send, even_bit, odd_bit, peers)
         if step + 1 < len(turns):
-            after = [own_terms, next_queries]
+            after = [own_terms, diagonal_queries]
             keep, send = call(add_kernel, [sums, held], [keep, got], after=after, name="add")
     owned_mine, owned_send = call(
         owned_kernel,

time: 60.7 us -> 66.3 us (1.092)
  starting transfers between devices: 26.7 us -> 31.5 us
  waiting for transfers between devices: 16 us -> 16.7 us
    ppermute x9, starting transfers between devices: 20 us -> 23.9 us  [swap(): lax.ppermute(block, 'tm', [(i, i ^ (odd_bit if i & 1 else even_bit)) for...]
    ppermute x2, waiting for transfers between devices: 0.18 us -> 2.13 us  [shift_second(): return lax.ppermute(block, 'tm', pairs) if pairs else block]
    ppermute x9, waiting for transfers between devices: 15.8 us -> 14.2 us  [swap(): lax.ppermute(block, 'tm', [(i, i ^ (odd_bit if i & 1 else even_bit)) for...]
    ppermute x0 -> x2, starting transfers between devices: none -> 1.36 us  [the longest x1 0.69 us: shift_straight(): lax.ppermute(block, 'tm', [pair for pair in pairs if pair not in relays])]
    ppermute x2 -> x1, starting transfers between devices: 1.36 us -> 0.69 us  [shift(): return lax.ppermute(block, 'tm', pairs)]
  transfers between devices with their start and end apart: 16 -> 17, of which waited for: 6 -> 7; matrix products, arithmetic and copies ran while one was open for 0% -> 0% of each run, Pallas kernels for 24% -> 22%
where the time goes in v12:
time: 66.3 us; the launch traced here: 66.1 us
  starting transfers between devices  31.5 us (48%)
  Pallas kernels  17 us (26%)
  waiting for transfers between devices  16.7 us (25%)
  between operations  0.87 us (1%)
    ppermute x9, starting transfers between devices, swap(): lax.ppermute(block, 'tm', [(i, i ^ (odd_bit if i & 1 else even_bit)) for...  23.9 us
    pallas_call x12, Pallas kernels, call(): pl.pallas_call(run, out_shape=outs, in_specs=[SMEM] * len(scalars) + [VME...  14.6 us
    ppermute x9, waiting for transfers between devices, swap(): lax.ppermute(block, 'tm', [(i, i ^ (odd_bit if i & 1 else even_bit)) for...  14.2 us
    pallas_call x2, Pallas kernels, join(): pl.pallas_call(run, out_shape=shape(BF16, rows, width), in_specs=[pl.Bloc...  2.34 us
    ppermute x2, starting transfers between devices, shift_second(): return lax.ppermute(block, 'tm', pairs) if pairs else block  2.31 us
    ppermute x2, waiting for transfers between devices, shift_second(): return lax.ppermute(block, 'tm', pairs) if pairs else block  2.13 us
    ppermute x2, starting transfers between devices, shift_first(): lax.ppermute(block, 'tm', [(i, relays.get((i, j), j)) for i, j in pairs])  1.97 us
  transfers between devices with their start and end apart: 17, of which 7 were waited for; matrix products, arithmetic and copies ran while one was open for 0% of the time, Pallas kernels for 22%

profile of v12, /device:TPU:0, one launch (start us, length us, event | category | flops | bytes accessed | tf_op | source)
XLA Modules:
  0.0 66.1 jit_solution(73296303209799866)
XLA Ops:
  0.7 1.2 %join.1.refs_1_.refs_5_.refs_6_.refs_7_ = bf16[528,768]{1,0:T(8,128)(2,1)S(1)} custom-call(s32[1,2]{1,0:T(1,128)} %refs_1_.5, bf16[256,768]{1,0:T(8,128)(2,1)} %refs_1_.3, bf16[256,768]{1,0:T(8,128)(2,1)} %refs_2_.2), custom_call_target="tpu_custom_call" | custom-call | tf_op jit(solution)/shard_map/join/pallas_call | solution.py:610
  1.9 0.5 collective-permute-start
  2.4 0.7 %collective-permute-start.1 = (bf16[256,768]{1,0:T(8,128)(2,1)S(1)}, bf16[256,768]{1,0:T(8,128)(2,1)S(1)}, u32[]{:S(2)}, u32[]{:S(2)}) collective-permute-start(bf16[256,768]{1,0:T(8,128)(2,1)S(1)} %copy-done.4), channel_id=1, source_target_pairs={{1,2},{3,7},{5,6},{9,10},{11,15},{13,14},{17,18},{19,23},{21,22},{... | collective-permute-start | bytes 1179656 | tf_op jit(solution)/shard_map/ppermute | solution.py:66
  3.1 1.3 %collective-permute-done.refs_2_.refs_4_.refs_5_.refs_6_ = bf16[528,768]{1,0:T(8,128)(2,1)S(1)} collective-permute-done((bf16[528,768]{1,0:T(8,128)(2,1)S(1)}, bf16[528,768]{1,0:T(8,128)(2,1)S(1)}, u32[]{:S(2)}, u32[]{:S(2)}) %collective-permute-start) | collective-permute-done | bytes 811040 | tf_op jit(solution)/shard_map/ppermute | solution.py:50
  4.3 0.3 split.1.refs_2_.refs_1_
  4.7 0.0 copy-start.1
  4.7 0.0 copy-start.2
  4.7 0.0 copy-start.3
  4.7 2.9 %collective-permute-start.5 = (bf16[3,2,128,384]{3,2,1,0:T(8,128)(2,1)S(1)}, bf16[3,2,128,384]{3,2,1,0:T(8,128)(2,1)S(1)}, u32[]{:S(2)}, u32[]{:S(2)}) collective-permute-start(bf16[3,2,128,384]{3,2,1,0:T(8,128)(2,1)S(1)} %split.1.refs_2_.refs_1_), channel_id=1, source_target_pairs={{0,2},{1,5},{2,0},{3,7},{4,6},{5,1},{6,4},{7,3},{8,10},{9,13},{10,... | collective-permute-start | bytes 1769480 | tf_op jit(solution)/shard_map/ppermute | solution.py:50
  7.6 1.1 %join_queries.1.refs_7_.refs_1_.refs_4_.refs_2_ = bf16[512,768]{1,0:T(8,128)(2,1)S(1)} custom-call(bf16[256,768]{1,0:T(8,128)(2,1)} %refs_0_.3, bf16[256,768]{1,0:T(8,128)(2,1)} %refs_1_.4, bf16[3,2,128,384]{3,2,1,0:T(8,128)(2,1)S(1)} %split.1.refs_2_.refs_1_), custom_call_target="tpu_custom_call" | custom-call | tf_op jit(solution)/shard_map/join_queries/pallas_call | solution.py:610
  8.8 1.1 %collective-permute-start.6 = (bf16[512,768]{1,0:T(8,128)(2,1)S(1)}, bf16[512,768]{1,0:T(8,128)(2,1)S(1)}, u32[]{:S(2)}, u32[]{:S(2)}) collective-permute-start(bf16[512,768]{1,0:T(8,128)(2,1)S(1)} %join_queries.1.refs_7_.refs_1_.refs_4_.refs_2_), channel_id=1, source_target_pairs={{0,1},{1,0},{2,3},{3,2},{4,5},{5,4},{6,7},{7,6},{8,9},{9,8},{10,11... | collective-permute-start | bytes 2359304 | tf_op jit(solution)/shard_map/ppermute | solution.py:50
  9.9 0.0 collective-permute-done.1.refs_6_.refs_2_.refs_3_
  9.9 1.7 %plan.1 = (f32[6,16,256]{2,1,0:T(8,128)S(1)}, s32[8,128]{1,0:T(8,128)S(1)}, bf16[256,768]{1,0:T(8,128)(2,1)S(1)}, bf16[256,768]{1,0:T(8,128)(2,1)S(1)}, bf16[256,768]{1,0:T(8,128)(2,1)S(1)}) custom-call(s32[1,4]{1,0:T(1,128)S(1)} %bitcast.2, s32[1,2]{1,0:T(1,128)S(1)} %copy-done.1, s32[16]{0:T(128)S(1)} %copy-done.3, f32[6,16,16]{2,1,0:T(8,128)S(1)} %copy-done.2, ...), custom_call_target="tpu_custom_call" | custom-call | flops 20132659200 | tf_op jit(solution)/shard_map/plan/pallas_call | solution.py:38
  11.6 0.7 %collective-permute-start.2 = (bf16[256,768]{1,0:T(8,128)(2,1)S(1)}, bf16[256,768]{1,0:T(8,128)(2,1)S(1)}, u32[]{:S(2)}, u32[]{:S(2)}) collective-permute-start(bf16[256,768]{1,0:T(8,128)(2,1)S(1)} %get-tuple-element.27), channel_id=1, source_target_pairs={{7,4},{15,12},{23,20},{31,28}} | collective-permute-start | bytes 1179656 | tf_op jit(solution)/shard_map/ppermute | solution.py:82
  12.3 0.7 %collective-permute-start.3 = (bf16[256,768]{1,0:T(8,128)(2,1)S(1)}, bf16[256,768]{1,0:T(8,128)(2,1)S(1)}, u32[]{:S(2)}, u32[]{:S(2)}) collective-permute-start(bf16[256,768]{1,0:T(8,128)(2,1)S(1)} %get-tuple-element.28), channel_id=1, source_target_pairs={{1,2},{3,4},{5,6},{9,10},{11,12},{13,14},{17,18},{19,20},{21,22},{... | collective-permute-start | bytes 1179656 | tf_op jit(solution)/shard_map/ppermute | solution.py:55
  13.0 0.7 %collective-permute-start.4 = (bf16[256,768]{1,0:T(8,128)(2,1)S(1)}, bf16[256,768]{1,0:T(8,128)(2,1)S(1)}, u32[]{:S(2)}, u32[]{:S(2)}) collective-permute-start(bf16[256,768]{1,0:T(8,128)(2,1)S(1)} %get-tuple-element.29), channel_id=1, source_target_pairs={{2,1},{6,5},{10,9},{14,13},{18,17},{22,21},{26,25},{30,29}} | collective-permute-start | bytes 1179656 | tf_op jit(solution)/shard_map/ppermute | solution.py:72
  13.6 4.2 %collective-permute-done.5.refs_2_ = bf16[3,2,128,384]{3,2,1,0:T(8,128)(2,1)S(1)} collective-permute-done((bf16[3,2,128,384]{3,2,1,0:T(8,128)(2,1)S(1)}, bf16[3,2,128,384]{3,2,1,0:T(8,128)(2,1)S(1)}, u32[]{:S(2)}, u32[]{:S(2)}) %collective-permute-start.5) | collective-permute-done | bytes 589856 | tf_op jit(solution)/shard_map/ppermute | solution.py:50
  17.8 0.0 collective-permute-done.6.refs_4_.refs_5_.refs_2_
  17.8 0.3 step.1.refs_1_
  18.1 1.6 %collective-permute-start.7 = (bf16[3,2,128,384]{3,2,1,0:T(8,128)(2,1)S(1)}, bf16[3,2,128,384]{3,2,1,0:T(8,128)(2,1)S(1)}, u32[]{:S(2)}, u32[]{:S(2)}) collective-permute-start(bf16[3,2,128,384]{3,2,1,0:T(8,128)(2,1)S(1)} %step.1.refs_1_), channel_id=1, source_target_pairs={{0,4},{1,3},{2,6},{3,1},{4,0},{5,7},{6,2},{7,5},{8,12},{9,11},{10,... | collective-permute-start | bytes 1769480 | tf_op jit(solution)/shard_map/ppermute | solution.py:50
  19.7 0.0 collective-permute-done.2.refs_3_.refs_4_
  19.7 0.0 collective-permute-done.3.refs_4_.refs_5_
  19.7 0.0 collective-permute-done.4.refs_7_.refs_3_
  19.7 1.6 %stats.1 = (f32[6,8,256]{2,1,0:T(8,128)S(1)}, bf16[256,768]{1,0:T(8,128)(2,1)S(1)}, bf16[256,768]{1,0:T(8,128)(2,1)S(1)}) custom-call(f32[6,16,256]{2,1,0:T(8,128)S(1)} %get-tuple-element.26.refs_0_.refs_1_, bf16[512,768]{1,0:T(8,128)(2,1)S(1)} %join_queries.1.refs_7_.refs_1_.refs_4_.refs_2_, ...), custom_call_target="tpu_custom_call" | custom-call | flops 20132659200 | tf_op jit(solution)/shard_map/stats/pallas_call | solution.py:38
  21.3 14.8 %collective-permute-start.9 = (f32[6,8,256]{2,1,0:T(8,128)S(1)}, f32[6,8,256]{2,1,0:T(8,128)S(1)}, u32[]{:S(2)}, u32[]{:S(2)}) collective-permute-start(f32[6,8,256]{2,1,0:T(8,128)S(1)} %get-tuple-element.30.refs_2_.refs_1_), channel_id=1, source_target_pairs={{0,1},{1,0},{2,3},{3,2},{4,5},{5,4},{6,7},{7,6},{8,9},{9,8},{10,11... | collective-permute-start | bytes 147464 | tf_op jit(solution)/shard_map/ppermute | solution.py:50
  36.1 0.7 %collective-permute-start.11 = (bf16[256,768]{1,0:T(8,128)(2,1)S(1)}, bf16[256,768]{1,0:T(8,128)(2,1)S(1)}, u32[]{:S(2)}, u32[]{:S(2)}) collective-permute-start(bf16[256,768]{1,0:T(8,128)(2,1)S(1)} %get-tuple-element.38), channel_id=1, source_target_pairs={{4,3},{12,11},{20,19},{28,27}} | collective-permute-start | bytes 1179656 | tf_op jit(solution)/shard_map/ppermute | solution.py:77
  36.7 1.3 %collective-permute-start.12 = (bf16[256,768]{1,0:T(8,128)(2,1)S(1)}, bf16[256,768]{1,0:T(8,128)(2,1)S(1)}, u32[]{:S(2)}, u32[]{:S(2)}) collective-permute-start(bf16[256,768]{1,0:T(8,128)(2,1)S(1)} %get-tuple-element.39), channel_id=1, source_target_pairs={{2,1},{4,0},{6,5},{10,9},{12,8},{14,13},{18,17},{20,16},{22,21},{2... | collective-permute-start | bytes 1179656 | tf_op jit(solution)/shard_map/ppermute | solution.py:66
  38.0 0.0 collective-permute-done.7.refs_2_
  38.1 0.3 pick.1
  38.4 0.1 collective-permute-start.8
  38.5 1.9 %memory.1 = (f32[4,2,128,384]{3,2,1,0:T(8,128)S(1)}, bf16[3,2,128,384]{3,2,1,0:T(8,128)(2,1)S(1)}) custom-call(s32[8,128]{1,0:T(8,128)S(1)} %get-tuple-element.31.refs_3_.refs_0_, f32[6,16,256]{2,1,0:T(8,128)S(1)} %get-tuple-element.26.refs_0_.refs_1_, f32[6,8,256]{2,1,0:T(8,128)S(1)} %get-tuple-element.30.refs_2_.refs_1_, ...), custom_call_target="tpu_custom_call" | custom-call | flops 20132659200 | tf_op jit(solution)/shard_map/memory/pallas_call | solution.py:38
  40.4 2.7 %collective-permute-start.14 = (bf16[3,2,128,384]{3,2,1,0:T(8,128)(2,1)S(1)}, bf16[3,2,128,384]{3,2,1,0:T(8,128)(2,1)S(1)}, u32[]{:S(2)}, u32[]{:S(2)}) collective-permute-start(bf16[3,2,128,384]{3,2,1,0:T(8,128)(2,1)S(1)} %get-tuple-element.34.refs_10_), channel_id=1, source_target_pairs={{0,4},{1,3},{2,6},{3,1},{4,0},{5,7},{6,2},{7,5},{8,12},{9,11},{10,... | collective-permute-start | bytes 1769480 | tf_op jit(solution)/shard_map/ppermute | solution.py:50
  43.1 0.0 collective-permute-done.8.refs_9_
  43.1 5.6 %rest.1 = (bf16[256,768]{1,0:T(8,128)(2,1)}, bf16[256,768]{1,0:T(8,128)(2,1)}, f32[2,256,768]{2,1,0:T(8,128)S(1)}, f32[6,8,256]{2,1,0:T(8,128)S(1)}) custom-call(f32[6,16,256]{2,1,0:T(8,128)S(1)} %get-tuple-element.26.refs_0_.refs_1_, f32[6,8,256]{2,1,0:T(8,128)S(1)} %get-tuple-element.30.refs_2_.refs_1_, ...), custom_call_target="tpu_custom_call" | custom-call | flops 20132659200 | tf_op jit(solution)/shard_map/rest/pallas_call | solution.py:38
  48.7 0.0 collective-permute-done.12.refs_0_.refs_5_
  48.7 1.6 %collective-permute-start.13 = (bf16[256,768]{1,0:T(8,128)(2,1)S(1)}, bf16[256,768]{1,0:T(8,128)(2,1)S(1)}, u32[]{:S(2)}, u32[]{:S(2)}) collective-permute-start(bf16[256,768]{1,0:T(8,128)(2,1)S(1)} %pass_on.1), channel_id=1, source_target_pairs={{0,3},{8,11},{16,19},{24,27}} | collective-permute-start | bytes 1179656 | tf_op jit(solution)/shard_map/ppermute | solution.py:82
  50.4 1.3 %collective-permute-start.10 = (f32[6,8,256]{2,1,0:T(8,128)S(1)}, f32[6,8,256]{2,1,0:T(8,128)S(1)}, u32[]{:S(2)}, u32[]{:S(2)}) collective-permute-start(f32[6,8,256]{2,1,0:T(8,128)S(1)} %get-tuple-element.37), channel_id=1, source_target_pairs={{1,0},{2,1},{3,2},{4,3},{5,4},{6,5},{7,6},{9,8},{10,9},{11,10},{12... | collective-permute-start | bytes 147464 | tf_op jit(solution)/shard_map/ppermute | solution.py:688
  51.7 1.0 %collective-permute-done.14.refs_1_ = bf16[3,2,128,384]{3,2,1,0:T(8,128)(2,1)S(1)} collective-permute-done((bf16[3,2,128,384]{3,2,1,0:T(8,128)(2,1)S(1)}, bf16[3,2,128,384]{3,2,1,0:T(8,128)(2,1)S(1)}, u32[]{:S(2)}, u32[]{:S(2)}) %collective-permute-start.14) | collective-permute-done | bytes 589856 | tf_op jit(solution)/shard_map/ppermute | solution.py:50
  52.7 0.2 add.1
  53.0 0.1 collective-permute-start.15
  53.1 0.4 collective-permute-done.10.refs_1_
  53.5 2.1 %collective-permute-done.13.refs_6_ = bf16[256,768]{1,0:T(8,128)(2,1)S(1)} collective-permute-done((bf16[256,768]{1,0:T(8,128)(2,1)S(1)}, bf16[256,768]{1,0:T(8,128)(2,1)S(1)}, u32[]{:S(2)}, u32[]{:S(2)}) %collective-permute-start.13) | collective-permute-done | bytes 393248 | tf_op jit(solution)/shard_map/ppermute | solution.py:82
  55.6 1.3 %next.1.refs_3_.refs_0_ = f32[2,256,768]{2,1,0:T(8,128)S(1)} custom-call(f32[6,16,256]{2,1,0:T(8,128)S(1)} %get-tuple-element.26.refs_0_.refs_1_, f32[6,8,256]{2,1,0:T(8,128)S(1)} %collective-permute-done.10.refs_1_, bf16[512,768]{1,0:T(8,128)(2,1)S(1)} %collective-permute-done.6.refs_4_.refs_5_.refs_2_, ...), custom_call_target="tpu_custom_call" | custom-call | flops 20132659200 | tf_op jit(solution)/shard_map/next/pallas_call | solution.py:38
  57.0 5.9 %collective-permute-done.15.refs_2_ = bf16[3,2,128,384]{3,2,1,0:T(8,128)(2,1)S(1)} collective-permute-done((bf16[3,2,128,384]{3,2,1,0:T(8,128)(2,1)S(1)}, bf16[3,2,128,384]{3,2,1,0:T(8,128)(2,1)S(1)}, u32[]{:S(2)}, u32[]{:S(2)}) %collective-permute-start.15) | collective-permute-done | bytes 589856 | tf_op jit(solution)/shard_map/ppermute | solution.py:50
  62.9 0.3 owned.1
  63.2 0.1 collective-permute-start.16
  63.3 1.7 %collective-permute-done.16.refs_2_ = bf16[2,2,128,384]{3,2,1,0:T(8,128)(2,1)S(1)} collective-permute-done((bf16[2,2,128,384]{3,2,1,0:T(8,128)(2,1)S(1)}, bf16[2,2,128,384]{3,2,1,0:T(8,128)(2,1)S(1)}, u32[]{:S(2)}, u32[]{:S(2)}) %collective-permute-start.16) | collective-permute-done | bytes 393248 | tf_op jit(solution)/shard_map/ppermute | solution.py:50
  65.0 1.1 %final.1 = (bf16[256,768]{1,0:T(8,128)(2,1)}, bf16[256,768]{1,0:T(8,128)(2,1)}) custom-call(f32[2,256,768]{2,1,0:T(8,128)S(1)} %next.1.refs_3_.refs_0_, f32[2,2,128,384]{3,2,1,0:T(8,128)S(1)} %get-tuple-element.44.refs_1_, bf16[2,2,128,384]{3,2,1,0:T(8,128)(2,1)S(1)} %collective-permute-done.16.refs_2_), custom_call_target="tpu_custom_call" | custom-call | tf_op jit(solution)/shard_map/final/pallas_call | solution.py:38
  (10 shorter events, 0.0 us)
Async XLA Ops:
  0.6 1.8 %copy-start.4 = (bf16[256,768]{1,0:T(8,128)(2,1)S(1)}, bf16[256,768]{1,0:T(8,128)(2,1)}, u32[]{:S(2)}) copy-start(bf16[256,768]{1,0:T(8,128)(2,1)} %refs_1_.3) | copy-start | bytes 1179652
  0.6 3.7 %copy-start = (s32[4]{0:T(128)S(1)}, s32[4]{0:T(128)}, u32[]{:S(2)}) copy-start(s32[4]{0:T(128)} %param.15) | copy-start | bytes 52
  1.9 2.5 %collective-permute-start = (bf16[528,768]{1,0:T(8,128)(2,1)S(1)}, bf16[528,768]{1,0:T(8,128)(2,1)S(1)}, u32[]{:S(2)}, u32[]{:S(2)}) collective-permute-start(bf16[528,768]{1,0:T(8,128)(2,1)S(1)} %join.1.refs_1_.refs_5_.refs_6_.refs_7_), channel_id=1, source_target_pairs={{0,1},{1,0},{2,3},{3,2},{4,5},{5,4},{6,7},{7,6},{8,9},{9,8},{10,11... | collective-permute-start | bytes 2433032 | tf_op jit(solution)/shard_map/ppermute | solution.py:50
  2.4 7.5 %collective-permute-start.1 = (bf16[256,768]{1,0:T(8,128)(2,1)S(1)}, bf16[256,768]{1,0:T(8,128)(2,1)S(1)}, u32[]{:S(2)}, u32[]{:S(2)}) collective-permute-start(bf16[256,768]{1,0:T(8,128)(2,1)S(1)} %copy-done.4), channel_id=1, source_target_pairs={{1,2},{3,7},{5,6},{9,10},{11,15},{13,14},{17,18},{19,23},{21,22},{... | collective-permute-start | bytes 1179656 | tf_op jit(solution)/shard_map/ppermute | solution.py:66
  4.7 5.2 %copy-start.1 = (s32[1,2]{1,0:T(1,128)S(1)}, s32[1,2]{1,0:T(1,128)}, u32[]{:S(2)}) copy-start(s32[1,2]{1,0:T(1,128)} %refs_1_.5) | copy-start | bytes 28
  4.7 5.2 %copy-start.2 = (f32[6,16,16]{2,1,0:T(8,128)S(1)}, f32[6,16,16]{2,1,0:T(8,128)}, u32[]{:S(2)}) copy-start(f32[6,16,16]{2,1,0:T(8,128)} %refs_3_.1) | copy-start | bytes 18436
  4.7 5.2 %copy-start.3 = (s32[16]{0:T(128)S(1)}, s32[16]{0:T(128)}, u32[]{:S(2)}) copy-start(s32[16]{0:T(128)} %refs_2_.3) | copy-start | bytes 196
  4.7 13.1 %collective-permute-start.5 = (bf16[3,2,128,384]{3,2,1,0:T(8,128)(2,1)S(1)}, bf16[3,2,128,384]{3,2,1,0:T(8,128)(2,1)S(1)}, u32[]{:S(2)}, u32[]{:S(2)}) collective-permute-start(bf16[3,2,128,384]{3,2,1,0:T(8,128)(2,1)S(1)} %split.1.refs_2_.refs_1_), channel_id=1, source_target_pairs={{0,2},{1,5},{2,0},{3,7},{4,6},{5,1},{6,4},{7,3},{8,10},{9,13},{10,... | collective-permute-start | bytes 1769480 | tf_op jit(solution)/shard_map/ppermute | solution.py:50
  8.8 9.1 %collective-permute-start.6 = (bf16[512,768]{1,0:T(8,128)(2,1)S(1)}, bf16[512,768]{1,0:T(8,128)(2,1)S(1)}, u32[]{:S(2)}, u32[]{:S(2)}) collective-permute-start(bf16[512,768]{1,0:T(8,128)(2,1)S(1)} %join_queries.1.refs_7_.refs_1_.refs_4_.refs_2_), channel_id=1, source_target_pairs={{0,1},{1,0},{2,3},{3,2},{4,5},{5,4},{6,7},{7,6},{8,9},{9,8},{10,11... | collective-permute-start | bytes 2359304 | tf_op jit(solution)/shard_map/ppermute | solution.py:50
  11.6 8.2 %collective-permute-start.2 = (bf16[256,768]{1,0:T(8,128)(2,1)S(1)}, bf16[256,768]{1,0:T(8,128)(2,1)S(1)}, u32[]{:S(2)}, u32[]{:S(2)}) collective-permute-start(bf16[256,768]{1,0:T(8,128)(2,1)S(1)} %get-tuple-element.27), channel_id=1, source_target_pairs={{7,4},{15,12},{23,20},{31,28}} | collective-permute-start | bytes 1179656 | tf_op jit(solution)/shard_map/ppermute | solution.py:82
  12.3 7.5 %collective-permute-start.3 = (bf16[256,768]{1,0:T(8,128)(2,1)S(1)}, bf16[256,768]{1,0:T(8,128)(2,1)S(1)}, u32[]{:S(2)}, u32[]{:S(2)}) collective-permute-start(bf16[256,768]{1,0:T(8,128)(2,1)S(1)} %get-tuple-element.28), channel_id=1, source_target_pairs={{1,2},{3,4},{5,6},{9,10},{11,12},{13,14},{17,18},{19,20},{21,22},{... | collective-permute-start | bytes 1179656 | tf_op jit(solution)/shard_map/ppermute | solution.py:55
  13.0 6.8 %collective-permute-start.4 = (bf16[256,768]{1,0:T(8,128)(2,1)S(1)}, bf16[256,768]{1,0:T(8,128)(2,1)S(1)}, u32[]{:S(2)}, u32[]{:S(2)}) collective-permute-start(bf16[256,768]{1,0:T(8,128)(2,1)S(1)} %get-tuple-element.29), channel_id=1, source_target_pairs={{2,1},{6,5},{10,9},{14,13},{18,17},{22,21},{26,25},{30,29}} | collective-permute-start | bytes 1179656 | tf_op jit(solution)/shard_map/ppermute | solution.py:72
  18.1 19.9 %collective-permute-start.7 = (bf16[3,2,128,384]{3,2,1,0:T(8,128)(2,1)S(1)}, bf16[3,2,128,384]{3,2,1,0:T(8,128)(2,1)S(1)}, u32[]{:S(2)}, u32[]{:S(2)}) collective-permute-start(bf16[3,2,128,384]{3,2,1,0:T(8,128)(2,1)S(1)} %step.1.refs_1_), channel_id=1, source_target_pairs={{0,4},{1,3},{2,6},{3,1},{4,0},{5,7},{6,2},{7,5},{8,12},{9,11},{10,... | collective-permute-start | bytes 1769480 | tf_op jit(solution)/shard_map/ppermute | solution.py:50
  21.3 17.2 %collective-permute-start.9 = (f32[6,8,256]{2,1,0:T(8,128)S(1)}, f32[6,8,256]{2,1,0:T(8,128)S(1)}, u32[]{:S(2)}, u32[]{:S(2)}) collective-permute-start(f32[6,8,256]{2,1,0:T(8,128)S(1)} %get-tuple-element.30.refs_2_.refs_1_), channel_id=1, source_target_pairs={{0,1},{1,0},{2,3},{3,2},{4,5},{5,4},{6,7},{7,6},{8,9},{9,8},{10,11... | collective-permute-start | bytes 147464 | tf_op jit(solution)/shard_map/ppermute | solution.py:50
  36.1 15.6 %collective-permute-start.11 = (bf16[256,768]{1,0:T(8,128)(2,1)S(1)}, bf16[256,768]{1,0:T(8,128)(2,1)S(1)}, u32[]{:S(2)}, u32[]{:S(2)}) collective-permute-start(bf16[256,768]{1,0:T(8,128)(2,1)S(1)} %get-tuple-element.38), channel_id=1, source_target_pairs={{4,3},{12,11},{20,19},{28,27}} | collective-permute-start | bytes 1179656 | tf_op jit(solution)/shard_map/ppermute | solution.py:77
  36.7 12.0 %collective-permute-start.12 = (bf16[256,768]{1,0:T(8,128)(2,1)S(1)}, bf16[256,768]{1,0:T(8,128)(2,1)S(1)}, u32[]{:S(2)}, u32[]{:S(2)}) collective-permute-start(bf16[256,768]{1,0:T(8,128)(2,1)S(1)} %get-tuple-element.39), channel_id=1, source_target_pairs={{2,1},{4,0},{6,5},{10,9},{12,8},{14,13},{18,17},{20,16},{22,21},{2... | collective-permute-start | bytes 1179656 | tf_op jit(solution)/shard_map/ppermute | solution.py:66
  38.4 4.8 %collective-permute-start.8 = (bf16[2,2,128,384]{3,2,1,0:T(8,128)(2,1)S(1)}, bf16[2,2,128,384]{3,2,1,0:T(8,128)(2,1)S(1)}, u32[]{:S(2)}, u32[]{:S(2)}) collective-permute-start(bf16[2,2,128,384]{3,2,1,0:T(8,128)(2,1)S(1)} %get-tuple-element.33.refs_7_), channel_id=1, source_target_pairs={{0,1},{1,0},{2,3},{3,2},{4,5},{5,4},{6,7},{7,6},{8,9},{9,8},{10,11... | collective-permute-start | bytes 1179656 | tf_op jit(solution)/shard_map/ppermute | solution.py:50
  40.4 12.3 %collective-permute-start.14 = (bf16[3,2,128,384]{3,2,1,0:T(8,128)(2,1)S(1)}, bf16[3,2,128,384]{3,2,1,0:T(8,128)(2,1)S(1)}, u32[]{:S(2)}, u32[]{:S(2)}) collective-permute-start(bf16[3,2,128,384]{3,2,1,0:T(8,128)(2,1)S(1)} %get-tuple-element.34.refs_10_), channel_id=1, source_target_pairs={{0,4},{1,3},{2,6},{3,1},{4,0},{5,7},{6,2},{7,5},{8,12},{9,11},{10,... | collective-permute-start | bytes 1769480 | tf_op jit(solution)/shard_map/ppermute | solution.py:50
  48.7 6.9 %collective-permute-start.13 = (bf16[256,768]{1,0:T(8,128)(2,1)S(1)}, bf16[256,768]{1,0:T(8,128)(2,1)S(1)}, u32[]{:S(2)}, u32[]{:S(2)}) collective-permute-start(bf16[256,768]{1,0:T(8,128)(2,1)S(1)} %pass_on.1), channel_id=1, source_target_pairs={{0,3},{8,11},{16,19},{24,27}} | collective-permute-start | bytes 1179656 | tf_op jit(solution)/shard_map/ppermute | solution.py:82
  50.4 3.1 %collective-permute-start.10 = (f32[6,8,256]{2,1,0:T(8,128)S(1)}, f32[6,8,256]{2,1,0:T(8,128)S(1)}, u32[]{:S(2)}, u32[]{:S(2)}) collective-permute-start(f32[6,8,256]{2,1,0:T(8,128)S(1)} %get-tuple-element.37), channel_id=1, source_target_pairs={{1,0},{2,1},{3,2},{4,3},{5,4},{6,5},{7,6},{9,8},{10,9},{11,10},{12... | collective-permute-start | bytes 147464 | tf_op jit(solution)/shard_map/ppermute | solution.py:688
  53.0 9.9 %collective-permute-start.15 = (bf16[3,2,128,384]{3,2,1,0:T(8,128)(2,1)S(1)}, bf16[3,2,128,384]{3,2,1,0:T(8,128)(2,1)S(1)}, u32[]{:S(2)}, u32[]{:S(2)}) collective-permute-start(bf16[3,2,128,384]{3,2,1,0:T(8,128)(2,1)S(1)} %get-tuple-element.43), channel_id=1, source_target_pairs={{0,2},{1,5},{2,0},{3,7},{4,6},{5,1},{6,4},{7,3},{8,10},{9,13},{10,... | collective-permute-start | bytes 1769480 | tf_op jit(solution)/shard_map/ppermute | solution.py:50
  63.2 1.8 %collective-permute-start.16 = (bf16[2,2,128,384]{3,2,1,0:T(8,128)(2,1)S(1)}, bf16[2,2,128,384]{3,2,1,0:T(8,128)(2,1)S(1)}, u32[]{:S(2)}, u32[]{:S(2)}) collective-permute-start(bf16[2,2,128,384]{3,2,1,0:T(8,128)(2,1)S(1)} %get-tuple-element.45), channel_id=1, source_target_pairs={{0,1},{1,0},{2,3},{3,2},{4,5},{5,4},{6,7},{7,6},{8,9},{9,8},{10,11... | collective-permute-start | bytes 1179656 | tf_op jit(solution)/shard_map/ppermute | solution.py:50

commit v13 on v11

--- a/solution.py
+++ b/solution.py
@@ -344,12 +344,9 @@
     own_ref,
     part_ref,
     queries_out,
-    cotangent_out,
 ):
     heads = queries_ref.shape[1] // DEPTH
-    rows = queries_out.shape[0]
-    queries_out[...] = queries_ref[0:rows]
-    cotangent_out[...] = queries_ref[rows : 2 * rows]
+    queries_out[...] = queries_ref[...]
 
     def products(head):
         cols = head_cols(head)
@@ -426,27 +423,14 @@
         send_ref[place] = keep_ref[place if place + 1 < kept else kept].astype(BF16)
 
 
-def next_kernel(
-    peers,
-    rows_ref,
-    stats_ref,
-    pair_queries,
-    outer_queries,
-    direct_cotangent,
-    relayed_cotangent,
-    own_ref,
-    term_ref,
-    sum_ref,
-):
+def next_kernel(rows_ref, stats_ref, pair_queries, outer_queries, own_ref, term_ref, sum_ref):
     even = (lax.axis_index("tm") & 1) == 0
-    relayed = through_relay(-1, 2, peers)
     heads = pair_queries.shape[1] // DEPTH
 
     def operands(head):
         cols = head_cols(head)
-        cotangent = jnp.where(relayed, relayed_cotangent[:, cols], direct_cotangent[:, cols])
-        outer = outer_queries[:, cols], cotangent
-        return [jnp.where(even, a, b) for a, b in zip(joined_parts(pair_queries, cols), outer)]
+        both = zip(joined_parts(pair_queries, cols), joined_parts(outer_queries, cols))
+        return [jnp.where(even, a, b) for a, b in both]
 
     def products(head):
         query, cotangent = operands(head)
@@ -532,10 +516,6 @@
     send_ref[...] = value.astype(BF16)
 
 
-def pass_kernel(in_ref, out_ref):
-    out_ref[...] = in_ref[...]
-
-
 def owned_kernel(codes_ref, keep_ref, got_ref, mine_ref, pair_ref):
     code = code_of(codes_ref, OWNED)
     for o, out in enumerate((mine_ref, pair_ref)):
@@ -638,16 +618,15 @@
         odd_done |= odd_bit
 
     stats = shape(F32, heads, 8, row_count)
-    part, queries_out, cotangent_out = call(
+    part, queries_out = call(
         functools.partial(stats_kernel, peers),
-        [stats] + [shape(BF16, row_count, width)] * 2,
+        [stats, shape(BF16, 2 * row_count, width)],
         [rows, queries, *outer, pair, joined],
         flops=HIDING * piece_flops,
         name="stats",
     )
     pair_part = swap(part, 1, 1, peers)
     next_queries = shift(queries_out, -1, 2, peers)
-    direct_cotangent = shift_first(cotangent_out, -1, 2, peers)
     chosen = shape(BF16, MEM, 2, frame_len, half_width)
     own_mem, pair_mem = call(pick_kernel, [chosen] * 2, [codes, mine, got], name="pick")
     keep, send = call(
@@ -668,14 +647,10 @@
         name="rest",
     )
     next_stats = lax.ppermute(stats_all, "tm", [(i, i - 1) for i in range(1, peers)])
-    (passed_on,) = call(
-        pass_kernel, [shape(BF16, row_count, width)], [direct_cotangent], after=[own_terms], name="pass_on"
-    )
-    relayed_cotangent = shift_second(passed_on, -1, 2, peers)
     (own,) = call(
-        functools.partial(next_kernel, peers),
+        next_kernel,
         [pair_sums],
-        [rows, next_stats, pair_queries, next_queries, direct_cotangent, relayed_cotangent, joined, own_terms],
+        [rows, next_stats, pair_queries, next_queries, joined, own_terms],
         flops=HIDING * piece_flops,
         name="next",
     )

time: 60.7 us -> 63.1 us (1.040)
  starting transfers between devices: 26.7 us -> 29.2 us
    ppermute x9, starting transfers between devices: 20 us -> 25.2 us  [swap(): lax.ppermute(block, 'tm', [(i, i ^ (odd_bit if i & 1 else even_bit)) for...]
    ppermute x2 -> x1, starting transfers between devices: 2 us -> 0.69 us  [shift_second(): return lax.ppermute(block, 'tm', pairs) if pairs else block]
    ppermute x2 -> x1, starting transfers between devices: 1.97 us -> 0.67 us  [shift_first(): lax.ppermute(block, 'tm', [(i, relays.get((i, j), j)) for i, j in pairs])]
    pallas_call x12 -> x11, Pallas kernels: 14.6 us -> 14.4 us  [call(): pl.pallas_call(run, out_shape=outs, in_specs=[SMEM] * len(scalars) + [VME...]
  transfers between devices with their start and end apart: 16 -> 14, of which waited for: 6 -> 5; matrix products, arithmetic and copies ran while one was open for 0% -> 0% of each run, Pallas kernels for 24% -> 23%
where the time goes in v13:
time: 63.1 us; the launch traced here: 62.9 us
  starting transfers between devices  29.2 us (46%)
  Pallas kernels  16.8 us (27%)
  waiting for transfers between devices  16.1 us (26%)
  between operations  0.84 us (1%)
    ppermute x9, starting transfers between devices, swap(): lax.ppermute(block, 'tm', [(i, i ^ (odd_bit if i & 1 else even_bit)) for...  25.2 us
    ppermute x9, waiting for transfers between devices, swap(): lax.ppermute(block, 'tm', [(i, i ^ (odd_bit if i & 1 else even_bit)) for...  16.1 us
    pallas_call x11, Pallas kernels, call(): pl.pallas_call(run, out_shape=outs, in_specs=[SMEM] * len(scalars) + [VME...  14.4 us
    pallas_call x2, Pallas kernels, join(): pl.pallas_call(run, out_shape=shape(BF16, rows, width), in_specs=[pl.Bloc...  2.34 us
    ppermute x2, starting transfers between devices, shift(): return lax.ppermute(block, 'tm', pairs)  1.38 us
    ppermute x1, starting transfers between devices, body(): lax.ppermute(stats_all, 'tm', [(i, i - 1) for i in range(1, peers)])  1.28 us
  transfers between devices with their start and end apart: 14, of which 5 were waited for; matrix products, arithmetic and copies ran while one was open for 0% of the time, Pallas kernels for 23%

profile of v13, /device:TPU:0, one launch (start us, length us, event | category | flops | bytes accessed | tf_op | source)
XLA Modules:
  0.0 62.9 jit_solution(9690675473753019719)
XLA Ops:
  0.6 0.0 copy-start.4
  0.6 0.0 copy-start
  0.7 1.2 %join.1.refs_5_.refs_1_.refs_6_.refs_7_.refs_4_ = bf16[528,768]{1,0:T(8,128)(2,1)S(1)} custom-call(s32[1,2]{1,0:T(1,128)} %refs_1_.4, bf16[256,768]{1,0:T(8,128)(2,1)} %refs_1_.3, bf16[256,768]{1,0:T(8,128)(2,1)} %refs_2_.2), custom_call_target="tpu_custom_call" | custom-call | tf_op jit(solution)/shard_map/join/pallas_call | solution.py:574
  1.9 0.5 collective-permute-start
  2.4 0.0 copy-done.4
  2.4 0.7 %collective-permute-start.1 = (bf16[256,768]{1,0:T(8,128)(2,1)S(1)}, bf16[256,768]{1,0:T(8,128)(2,1)S(1)}, u32[]{:S(2)}, u32[]{:S(2)}) collective-permute-start(bf16[256,768]{1,0:T(8,128)(2,1)S(1)} %copy-done.4), channel_id=1, source_target_pairs={{1,2},{3,7},{5,6},{9,10},{11,15},{13,14},{17,18},{19,23},{21,22},{... | collective-permute-start | bytes 1179656 | tf_op jit(solution)/shard_map/ppermute | solution.py:66
  3.1 1.3 %collective-permute-done.refs_4_.refs_2_.refs_5_.refs_6_ = bf16[528,768]{1,0:T(8,128)(2,1)S(1)} collective-permute-done((bf16[528,768]{1,0:T(8,128)(2,1)S(1)}, bf16[528,768]{1,0:T(8,128)(2,1)S(1)}, u32[]{:S(2)}, u32[]{:S(2)}) %collective-permute-start) | collective-permute-done | bytes 811040 | tf_op jit(solution)/shard_map/ppermute | solution.py:50
  4.3 0.3 split.1.refs_2_.refs_1_
  4.7 0.0 copy-start.1
  4.7 0.0 copy-start.2
  4.7 0.0 copy-start.3
  4.7 2.9 %collective-permute-start.4 = (bf16[3,2,128,384]{3,2,1,0:T(8,128)(2,1)S(1)}, bf16[3,2,128,384]{3,2,1,0:T(8,128)(2,1)S(1)}, u32[]{:S(2)}, u32[]{:S(2)}) collective-permute-start(bf16[3,2,128,384]{3,2,1,0:T(8,128)(2,1)S(1)} %split.1.refs_2_.refs_1_), channel_id=1, source_target_pairs={{0,2},{1,5},{2,0},{3,7},{4,6},{5,1},{6,4},{7,3},{8,10},{9,13},{10,... | collective-permute-start | bytes 1769480 | tf_op jit(solution)/shard_map/ppermute | solution.py:50
  7.6 1.1 %join_queries.1.refs_1_.refs_4_.refs_2_ = bf16[512,768]{1,0:T(8,128)(2,1)S(1)} custom-call(bf16[256,768]{1,0:T(8,128)(2,1)} %refs_0_.3, bf16[256,768]{1,0:T(8,128)(2,1)} %refs_1_.5, bf16[3,2,128,384]{3,2,1,0:T(8,128)(2,1)S(1)} %split.1.refs_2_.refs_1_), custom_call_target="tpu_custom_call" | custom-call | tf_op jit(solution)/shard_map/join_queries/pallas_call | solution.py:574
  8.8 1.1 %collective-permute-start.5 = (bf16[512,768]{1,0:T(8,128)(2,1)S(1)}, bf16[512,768]{1,0:T(8,128)(2,1)S(1)}, u32[]{:S(2)}, u32[]{:S(2)}) collective-permute-start(bf16[512,768]{1,0:T(8,128)(2,1)S(1)} %join_queries.1.refs_1_.refs_4_.refs_2_), channel_id=1, source_target_pairs={{0,1},{1,0},{2,3},{3,2},{4,5},{5,4},{6,7},{7,6},{8,9},{9,8},{10,11... | collective-permute-start | bytes 2359304 | tf_op jit(solution)/shard_map/ppermute | solution.py:50
  9.9 0.0 collective-permute-done.1.refs_6_.refs_2_.refs_3_
  9.9 0.0 copy-done.2
  9.9 1.7 %plan.1 = (f32[6,16,256]{2,1,0:T(8,128)S(1)}, s32[8,128]{1,0:T(8,128)S(1)}, bf16[256,768]{1,0:T(8,128)(2,1)S(1)}, bf16[256,768]{1,0:T(8,128)(2,1)S(1)}) custom-call(s32[1,4]{1,0:T(1,128)S(1)} %bitcast.2, s32[1,2]{1,0:T(1,128)S(1)} %copy-done.1, s32[16]{0:T(128)S(1)} %copy-done.3, f32[6,16,16]{2,1,0:T(8,128)S(1)} %copy-done.2, ...), custom_call_target="tpu_custom_call" | custom-call | flops 20132659200 | tf_op jit(solution)/shard_map/plan/pallas_call | solution.py:38
  11.6 0.7 %collective-permute-start.2 = (bf16[256,768]{1,0:T(8,128)(2,1)S(1)}, bf16[256,768]{1,0:T(8,128)(2,1)S(1)}, u32[]{:S(2)}, u32[]{:S(2)}) collective-permute-start(bf16[256,768]{1,0:T(8,128)(2,1)S(1)} %get-tuple-element.25), channel_id=1, source_target_pairs={{7,4},{15,12},{23,20},{31,28}} | collective-permute-start | bytes 1179656 | tf_op jit(solution)/shard_map/ppermute | solution.py:71
  12.3 0.7 %collective-permute-start.3 = (bf16[256,768]{1,0:T(8,128)(2,1)S(1)}, bf16[256,768]{1,0:T(8,128)(2,1)S(1)}, u32[]{:S(2)}, u32[]{:S(2)}) collective-permute-start(bf16[256,768]{1,0:T(8,128)(2,1)S(1)} %get-tuple-element.26), channel_id=1, source_target_pairs={{1,2},{3,4},{5,6},{9,10},{11,12},{13,14},{17,18},{19,20},{21,22},{... | collective-permute-start | bytes 1179656 | tf_op jit(solution)/shard_map/ppermute | solution.py:55
  12.9 4.9 %collective-permute-done.4.refs_2_ = bf16[3,2,128,384]{3,2,1,0:T(8,128)(2,1)S(1)} collective-permute-done((bf16[3,2,128,384]{3,2,1,0:T(8,128)(2,1)S(1)}, bf16[3,2,128,384]{3,2,1,0:T(8,128)(2,1)S(1)}, u32[]{:S(2)}, u32[]{:S(2)}) %collective-permute-start.4) | collective-permute-done | bytes 589856 | tf_op jit(solution)/shard_map/ppermute | solution.py:50
  17.8 0.0 collective-permute-done.5.refs_4_.refs_5_.refs_2_
  17.8 0.3 step.1.refs_1_
  18.1 1.6 %collective-permute-start.6 = (bf16[3,2,128,384]{3,2,1,0:T(8,128)(2,1)S(1)}, bf16[3,2,128,384]{3,2,1,0:T(8,128)(2,1)S(1)}, u32[]{:S(2)}, u32[]{:S(2)}) collective-permute-start(bf16[3,2,128,384]{3,2,1,0:T(8,128)(2,1)S(1)} %step.1.refs_1_), channel_id=1, source_target_pairs={{0,4},{1,3},{2,6},{3,1},{4,0},{5,7},{6,2},{7,5},{8,12},{9,11},{10,... | collective-permute-start | bytes 1769480 | tf_op jit(solution)/shard_map/ppermute | solution.py:50
  19.7 0.0 collective-permute-done.2.refs_3_.refs_4_
  19.7 0.0 collective-permute-done.3.refs_4_.refs_5_
  19.7 1.6 %stats.1 = (f32[6,8,256]{2,1,0:T(8,128)S(1)}, bf16[512,768]{1,0:T(8,128)(2,1)S(1)}) custom-call(f32[6,16,256]{2,1,0:T(8,128)S(1)} %get-tuple-element.24.refs_0_.refs_1_, bf16[512,768]{1,0:T(8,128)(2,1)S(1)} %join_queries.1.refs_1_.refs_4_.refs_2_, bf16[256,768]{1,0:T(8,128)(2,1)S(1)} %collective-permute-done.1.refs_6_.refs_2_.refs_3_, ...), custom_call_target="tpu_custom_call" | custom-call | flops 20132659200 | tf_op jit(solution)/shard_map/stats/pallas_call | solution.py:38
  21.3 6.2 %collective-permute-start.8 = (f32[6,8,256]{2,1,0:T(8,128)S(1)}, f32[6,8,256]{2,1,0:T(8,128)S(1)}, u32[]{:S(2)}, u32[]{:S(2)}) collective-permute-start(f32[6,8,256]{2,1,0:T(8,128)S(1)} %get-tuple-element.27.refs_2_.refs_1_), channel_id=1, source_target_pairs={{0,1},{1,0},{2,3},{3,2},{4,5},{5,4},{6,7},{7,6},{8,9},{9,8},{10,11... | collective-permute-start | bytes 147464 | tf_op jit(solution)/shard_map/ppermute | solution.py:50
  27.5 0.7 %collective-permute-start.10 = (bf16[512,768]{1,0:T(8,128)(2,1)S(1)}, bf16[512,768]{1,0:T(8,128)(2,1)S(1)}, u32[]{:S(2)}, u32[]{:S(2)}) collective-permute-start(bf16[512,768]{1,0:T(8,128)(2,1)S(1)} %get-tuple-element.35), channel_id=1, source_target_pairs={{2,1},{4,3},{6,5},{10,9},{12,11},{14,13},{18,17},{20,19},{22,21},{... | collective-permute-start | bytes 2359304 | tf_op jit(solution)/shard_map/ppermute | solution.py:55
  28.2 0.0 collective-permute-done.6.refs_2_
  28.2 0.3 pick.1
  28.5 4.0 %collective-permute-start.7 = (bf16[2,2,128,384]{3,2,1,0:T(8,128)(2,1)S(1)}, bf16[2,2,128,384]{3,2,1,0:T(8,128)(2,1)S(1)}, u32[]{:S(2)}, u32[]{:S(2)}) collective-permute-start(bf16[2,2,128,384]{3,2,1,0:T(8,128)(2,1)S(1)} %get-tuple-element.30.refs_7_), channel_id=1, source_target_pairs={{0,1},{1,0},{2,3},{3,2},{4,5},{5,4},{6,7},{7,6},{8,9},{9,8},{10,11... | collective-permute-start | bytes 1179656 | tf_op jit(solution)/shard_map/ppermute | solution.py:50
  32.5 0.0 collective-permute-done.8.refs_3_
  32.5 1.9 %memory.1 = (f32[4,2,128,384]{3,2,1,0:T(8,128)S(1)}, bf16[3,2,128,384]{3,2,1,0:T(8,128)(2,1)S(1)}) custom-call(s32[8,128]{1,0:T(8,128)S(1)} %get-tuple-element.28.refs_3_.refs_0_, f32[6,16,256]{2,1,0:T(8,128)S(1)} %get-tuple-element.24.refs_0_.refs_1_, f32[6,8,256]{2,1,0:T(8,128)S(1)} %get-tuple-element.27.refs_2_.refs_1_, ...), custom_call_target="tpu_custom_call" | custom-call | flops 20132659200 | tf_op jit(solution)/shard_map/memory/pallas_call | solution.py:38
  34.5 1.6 %collective-permute-start.11 = (bf16[3,2,128,384]{3,2,1,0:T(8,128)(2,1)S(1)}, bf16[3,2,128,384]{3,2,1,0:T(8,128)(2,1)S(1)}, u32[]{:S(2)}, u32[]{:S(2)}) collective-permute-start(bf16[3,2,128,384]{3,2,1,0:T(8,128)(2,1)S(1)} %get-tuple-element.31.refs_10_), channel_id=1, source_target_pairs={{0,4},{1,3},{2,6},{3,1},{4,0},{5,7},{6,2},{7,5},{8,12},{9,11},{10,... | collective-permute-start | bytes 1769480 | tf_op jit(solution)/shard_map/ppermute | solution.py:50
  36.1 0.0 collective-permute-done.7.refs_9_
  36.1 5.6 %rest.1 = (bf16[256,768]{1,0:T(8,128)(2,1)}, bf16[256,768]{1,0:T(8,128)(2,1)}, f32[2,256,768]{2,1,0:T(8,128)S(1)}, f32[6,8,256]{2,1,0:T(8,128)S(1)}) custom-call(f32[6,16,256]{2,1,0:T(8,128)S(1)} %get-tuple-element.24.refs_0_.refs_1_, f32[6,8,256]{2,1,0:T(8,128)S(1)} %get-tuple-element.27.refs_2_.refs_1_, ...), custom_call_target="tpu_custom_call" | custom-call | flops 20132659200 | tf_op jit(solution)/shard_map/rest/pallas_call | solution.py:38
  41.6 1.3 %collective-permute-start.9 = (f32[6,8,256]{2,1,0:T(8,128)S(1)}, f32[6,8,256]{2,1,0:T(8,128)S(1)}, u32[]{:S(2)}, u32[]{:S(2)}) collective-permute-start(f32[6,8,256]{2,1,0:T(8,128)S(1)} %get-tuple-element.34), channel_id=1, source_target_pairs={{1,0},{2,1},{3,2},{4,3},{5,4},{6,5},{7,6},{9,8},{10,9},{11,10},{12... | collective-permute-start | bytes 147464 | tf_op jit(solution)/shard_map/ppermute | solution.py:649
  42.9 0.0 collective-permute-done.10.refs_3_
  42.9 1.5 %collective-permute-done.11.refs_1_ = bf16[3,2,128,384]{3,2,1,0:T(8,128)(2,1)S(1)} collective-permute-done((bf16[3,2,128,384]{3,2,1,0:T(8,128)(2,1)S(1)}, bf16[3,2,128,384]{3,2,1,0:T(8,128)(2,1)S(1)}, u32[]{:S(2)}, u32[]{:S(2)}) %collective-permute-start.11) | collective-permute-done | bytes 589856 | tf_op jit(solution)/shard_map/ppermute | solution.py:50
  44.4 0.2 add.1
  44.7 7.2 %collective-permute-start.12 = (bf16[3,2,128,384]{3,2,1,0:T(8,128)(2,1)S(1)}, bf16[3,2,128,384]{3,2,1,0:T(8,128)(2,1)S(1)}, u32[]{:S(2)}, u32[]{:S(2)}) collective-permute-start(bf16[3,2,128,384]{3,2,1,0:T(8,128)(2,1)S(1)} %get-tuple-element.39), channel_id=1, source_target_pairs={{0,2},{1,5},{2,0},{3,7},{4,6},{5,1},{6,4},{7,3},{8,10},{9,13},{10,... | collective-permute-start | bytes 1769480 | tf_op jit(solution)/shard_map/ppermute | solution.py:50
  51.9 0.0 collective-permute-done.9.refs_1_
  51.9 1.2 %next.1.refs_3_.refs_0_ = f32[2,256,768]{2,1,0:T(8,128)S(1)} custom-call(f32[6,16,256]{2,1,0:T(8,128)S(1)} %get-tuple-element.24.refs_0_.refs_1_, f32[6,8,256]{2,1,0:T(8,128)S(1)} %collective-permute-done.9.refs_1_, bf16[512,768]{1,0:T(8,128)(2,1)S(1)} %collective-permute-done.5.refs_4_.refs_5_.refs_2_, ...), custom_call_target="tpu_custom_call" | custom-call | flops 20132659200 | tf_op jit(solution)/shard_map/next/pallas_call | solution.py:38
  53.0 6.7 %collective-permute-done.12.refs_2_ = bf16[3,2,128,384]{3,2,1,0:T(8,128)(2,1)S(1)} collective-permute-done((bf16[3,2,128,384]{3,2,1,0:T(8,128)(2,1)S(1)}, bf16[3,2,128,384]{3,2,1,0:T(8,128)(2,1)S(1)}, u32[]{:S(2)}, u32[]{:S(2)}) %collective-permute-start.12) | collective-permute-done | bytes 589856 | tf_op jit(solution)/shard_map/ppermute | solution.py:50
  59.7 0.3 owned.1
  60.1 0.1 collective-permute-start.13
  60.2 1.7 %collective-permute-done.13.refs_2_ = bf16[2,2,128,384]{3,2,1,0:T(8,128)(2,1)S(1)} collective-permute-done((bf16[2,2,128,384]{3,2,1,0:T(8,128)(2,1)S(1)}, bf16[2,2,128,384]{3,2,1,0:T(8,128)(2,1)S(1)}, u32[]{:S(2)}, u32[]{:S(2)}) %collective-permute-start.13) | collective-permute-done | bytes 393248 | tf_op jit(solution)/shard_map/ppermute | solution.py:50
  61.9 1.0 %final.1 = (bf16[256,768]{1,0:T(8,128)(2,1)}, bf16[256,768]{1,0:T(8,128)(2,1)}) custom-call(f32[2,256,768]{2,1,0:T(8,128)S(1)} %next.1.refs_3_.refs_0_, f32[2,2,128,384]{3,2,1,0:T(8,128)S(1)} %get-tuple-element.40.refs_1_, bf16[2,2,128,384]{3,2,1,0:T(8,128)(2,1)S(1)} %collective-permute-done.13.refs_2_), custom_call_target="tpu_custom_call" | custom-call | tf_op jit(solution)/shard_map/final/pallas_call | solution.py:38
  (3 shorter events, 0.0 us)
Async XLA Ops:
  0.6 1.8 %copy-start.4 = (bf16[256,768]{1,0:T(8,128)(2,1)S(1)}, bf16[256,768]{1,0:T(8,128)(2,1)}, u32[]{:S(2)}) copy-start(bf16[256,768]{1,0:T(8,128)(2,1)} %refs_1_.3) | copy-start | bytes 1179652
  0.6 3.7 %copy-start = (s32[4]{0:T(128)S(1)}, s32[4]{0:T(128)}, u32[]{:S(2)}) copy-start(s32[4]{0:T(128)} %param.15) | copy-start | bytes 52
  1.9 2.5 %collective-permute-start = (bf16[528,768]{1,0:T(8,128)(2,1)S(1)}, bf16[528,768]{1,0:T(8,128)(2,1)S(1)}, u32[]{:S(2)}, u32[]{:S(2)}) collective-permute-start(bf16[528,768]{1,0:T(8,128)(2,1)S(1)} %join.1.refs_5_.refs_1_.refs_6_.refs_7_.refs_4_), channel_id=1, source_target_pairs={{0,1},{1,0},{2,3},{3,2},{4,5},{5,4},{6,7},{7,6},{8,9},{9,8},{10,11... | collective-permute-start | bytes 2433032 | tf_op jit(solution)/shard_map/ppermute | solution.py:50
  2.4 7.5 %collective-permute-start.1 = (bf16[256,768]{1,0:T(8,128)(2,1)S(1)}, bf16[256,768]{1,0:T(8,128)(2,1)S(1)}, u32[]{:S(2)}, u32[]{:S(2)}) collective-permute-start(bf16[256,768]{1,0:T(8,128)(2,1)S(1)} %copy-done.4), channel_id=1, source_target_pairs={{1,2},{3,7},{5,6},{9,10},{11,15},{13,14},{17,18},{19,23},{21,22},{... | collective-permute-start | bytes 1179656 | tf_op jit(solution)/shard_map/ppermute | solution.py:66
  4.7 5.2 %copy-start.1 = (s32[1,2]{1,0:T(1,128)S(1)}, s32[1,2]{1,0:T(1,128)}, u32[]{:S(2)}) copy-start(s32[1,2]{1,0:T(1,128)} %refs_1_.4) | copy-start | bytes 28
  4.7 5.2 %copy-start.2 = (f32[6,16,16]{2,1,0:T(8,128)S(1)}, f32[6,16,16]{2,1,0:T(8,128)}, u32[]{:S(2)}) copy-start(f32[6,16,16]{2,1,0:T(8,128)} %refs_3_.1) | copy-start | bytes 18436
  4.7 5.2 %copy-start.3 = (s32[16]{0:T(128)S(1)}, s32[16]{0:T(128)}, u32[]{:S(2)}) copy-start(s32[16]{0:T(128)} %refs_2_.3) | copy-start | bytes 196
  4.7 13.1 %collective-permute-start.4 = (bf16[3,2,128,384]{3,2,1,0:T(8,128)(2,1)S(1)}, bf16[3,2,128,384]{3,2,1,0:T(8,128)(2,1)S(1)}, u32[]{:S(2)}, u32[]{:S(2)}) collective-permute-start(bf16[3,2,128,384]{3,2,1,0:T(8,128)(2,1)S(1)} %split.1.refs_2_.refs_1_), channel_id=1, source_target_pairs={{0,2},{1,5},{2,0},{3,7},{4,6},{5,1},{6,4},{7,3},{8,10},{9,13},{10,... | collective-permute-start | bytes 1769480 | tf_op jit(solution)/shard_map/ppermute | solution.py:50
  8.8 9.1 %collective-permute-start.5 = (bf16[512,768]{1,0:T(8,128)(2,1)S(1)}, bf16[512,768]{1,0:T(8,128)(2,1)S(1)}, u32[]{:S(2)}, u32[]{:S(2)}) collective-permute-start(bf16[512,768]{1,0:T(8,128)(2,1)S(1)} %join_queries.1.refs_1_.refs_4_.refs_2_), channel_id=1, source_target_pairs={{0,1},{1,0},{2,3},{3,2},{4,5},{5,4},{6,7},{7,6},{8,9},{9,8},{10,11... | collective-permute-start | bytes 2359304 | tf_op jit(solution)/shard_map/ppermute | solution.py:50
  11.6 8.2 %collective-permute-start.2 = (bf16[256,768]{1,0:T(8,128)(2,1)S(1)}, bf16[256,768]{1,0:T(8,128)(2,1)S(1)}, u32[]{:S(2)}, u32[]{:S(2)}) collective-permute-start(bf16[256,768]{1,0:T(8,128)(2,1)S(1)} %get-tuple-element.25), channel_id=1, source_target_pairs={{7,4},{15,12},{23,20},{31,28}} | collective-permute-start | bytes 1179656 | tf_op jit(solution)/shard_map/ppermute | solution.py:71
  12.3 7.5 %collective-permute-start.3 = (bf16[256,768]{1,0:T(8,128)(2,1)S(1)}, bf16[256,768]{1,0:T(8,128)(2,1)S(1)}, u32[]{:S(2)}, u32[]{:S(2)}) collective-permute-start(bf16[256,768]{1,0:T(8,128)(2,1)S(1)} %get-tuple-element.26), channel_id=1, source_target_pairs={{1,2},{3,4},{5,6},{9,10},{11,12},{13,14},{17,18},{19,20},{21,22},{... | collective-permute-start | bytes 1179656 | tf_op jit(solution)/shard_map/ppermute | solution.py:55
  18.1 10.1 %collective-permute-start.6 = (bf16[3,2,128,384]{3,2,1,0:T(8,128)(2,1)S(1)}, bf16[3,2,128,384]{3,2,1,0:T(8,128)(2,1)S(1)}, u32[]{:S(2)}, u32[]{:S(2)}) collective-permute-start(bf16[3,2,128,384]{3,2,1,0:T(8,128)(2,1)S(1)} %step.1.refs_1_), channel_id=1, source_target_pairs={{0,4},{1,3},{2,6},{3,1},{4,0},{5,7},{6,2},{7,5},{8,12},{9,11},{10,... | collective-permute-start | bytes 1769480 | tf_op jit(solution)/shard_map/ppermute | solution.py:50
  21.3 11.2 %collective-permute-start.8 = (f32[6,8,256]{2,1,0:T(8,128)S(1)}, f32[6,8,256]{2,1,0:T(8,128)S(1)}, u32[]{:S(2)}, u32[]{:S(2)}) collective-permute-start(f32[6,8,256]{2,1,0:T(8,128)S(1)} %get-tuple-element.27.refs_2_.refs_1_), channel_id=1, source_target_pairs={{0,1},{1,0},{2,3},{3,2},{4,5},{5,4},{6,7},{7,6},{8,9},{9,8},{10,11... | collective-permute-start | bytes 147464 | tf_op jit(solution)/shard_map/ppermute | solution.py:50
  27.5 15.4 %collective-permute-start.10 = (bf16[512,768]{1,0:T(8,128)(2,1)S(1)}, bf16[512,768]{1,0:T(8,128)(2,1)S(1)}, u32[]{:S(2)}, u32[]{:S(2)}) collective-permute-start(bf16[512,768]{1,0:T(8,128)(2,1)S(1)} %get-tuple-element.35), channel_id=1, source_target_pairs={{2,1},{4,3},{6,5},{10,9},{12,11},{14,13},{18,17},{20,19},{22,21},{... | collective-permute-start | bytes 2359304 | tf_op jit(solution)/shard_map/ppermute | solution.py:55
  28.5 7.6 %collective-permute-start.7 = (bf16[2,2,128,384]{3,2,1,0:T(8,128)(2,1)S(1)}, bf16[2,2,128,384]{3,2,1,0:T(8,128)(2,1)S(1)}, u32[]{:S(2)}, u32[]{:S(2)}) collective-permute-start(bf16[2,2,128,384]{3,2,1,0:T(8,128)(2,1)S(1)} %get-tuple-element.30.refs_7_), channel_id=1, source_target_pairs={{0,1},{1,0},{2,3},{3,2},{4,5},{5,4},{6,7},{7,6},{8,9},{9,8},{10,11... | collective-permute-start | bytes 1179656 | tf_op jit(solution)/shard_map/ppermute | solution.py:50
  34.5 9.9 %collective-permute-start.11 = (bf16[3,2,128,384]{3,2,1,0:T(8,128)(2,1)S(1)}, bf16[3,2,128,384]{3,2,1,0:T(8,128)(2,1)S(1)}, u32[]{:S(2)}, u32[]{:S(2)}) collective-permute-start(bf16[3,2,128,384]{3,2,1,0:T(8,128)(2,1)S(1)} %get-tuple-element.31.refs_10_), channel_id=1, source_target_pairs={{0,4},{1,3},{2,6},{3,1},{4,0},{5,7},{6,2},{7,5},{8,12},{9,11},{10,... | collective-permute-start | bytes 1769480 | tf_op jit(solution)/shard_map/ppermute | solution.py:50
  41.6 10.2 %collective-permute-start.9 = (f32[6,8,256]{2,1,0:T(8,128)S(1)}, f32[6,8,256]{2,1,0:T(8,128)S(1)}, u32[]{:S(2)}, u32[]{:S(2)}) collective-permute-start(f32[6,8,256]{2,1,0:T(8,128)S(1)} %get-tuple-element.34), channel_id=1, source_target_pairs={{1,0},{2,1},{3,2},{4,3},{5,4},{6,5},{7,6},{9,8},{10,9},{11,10},{12... | collective-permute-start | bytes 147464 | tf_op jit(solution)/shard_map/ppermute | solution.py:649
  44.7 15.1 %collective-permute-start.12 = (bf16[3,2,128,384]{3,2,1,0:T(8,128)(2,1)S(1)}, bf16[3,2,128,384]{3,2,1,0:T(8,128)(2,1)S(1)}, u32[]{:S(2)}, u32[]{:S(2)}) collective-permute-start(bf16[3,2,128,384]{3,2,1,0:T(8,128)(2,1)S(1)} %get-tuple-element.39), channel_id=1, source_target_pairs={{0,2},{1,5},{2,0},{3,7},{4,6},{5,1},{6,4},{7,3},{8,10},{9,13},{10,... | collective-permute-start | bytes 1769480 | tf_op jit(solution)/shard_map/ppermute | solution.py:50
  60.1 1.8 %collective-permute-start.13 = (bf16[2,2,128,384]{3,2,1,0:T(8,128)(2,1)S(1)}, bf16[2,2,128,384]{3,2,1,0:T(8,128)(2,1)S(1)}, u32[]{:S(2)}, u32[]{:S(2)}) collective-permute-start(bf16[2,2,128,384]{3,2,1,0:T(8,128)(2,1)S(1)} %get-tuple-element.41), channel_id=1, source_target_pairs={{0,1},{1,0},{2,3},{3,2},{4,5},{5,4},{6,7},{7,6},{8,9},{9,8},{10,11... | collective-permute-start | bytes 1179656 | tf_op jit(solution)/shard_map/ppermute | solution.py:50

commit v14 on v11

--- a/solution.py
+++ b/solution.py
@@ -465,10 +465,50 @@
         sum_ref[1, :, cols] = term_ref[1, :, cols] + dot(weights, cotangent, 1, 0)
 
 
-def rest_kernel(
+def memory_parts(own_mem, other_mem, head):
+    role = lax.axis_index("tm") & 1
+    frame_len, half_width = own_mem.shape[2:]
+    half = half_width // DEPTH
+    cols = head_cols(head % half)
+    return [
+        jnp.where(role == head // half, own_mem[:, kind, :, cols], other_mem[:, kind, :, cols]).reshape(
+            MEM * frame_len, DEPTH
+        )
+        for kind in range(2)
+    ]
+
+
+def own_kernel(rows_ref, part_ref, queries_ref, own_ref, own_mem, other_mem, term_ref, stats_ref):
+    heads = queries_ref.shape[1] // DEPTH
+
+    def products(head):
+        query, cotangent = joined_parts(queries_ref, head_cols(head))
+        pieces = ((OWN, joined_parts(own_ref, head_cols(head))), (MEMORY, memory_parts(own_mem, other_mem, head)))
+        return [
+            (logits_of(keys, query, rows_ref, head, piece), dot(values, cotangent, 1, 1))
+            for piece, (keys, values) in pieces
+        ]
+
+    ahead = products(0)
+    for head in range(heads):
+        own, memory = ahead
+        if head + 1 < heads:
+            ahead = products(head + 1)
+        cols = head_cols(head)
+        query, cotangent = joined_parts(queries_ref, cols)
+        peak, total, spread = merged(load_part(part_ref, head), part_of(*memory))
+        inverse = 1.0 / total
+        stats = peak, inverse, spread * inverse
+        store_part(stats_ref, head, stats)
+        weights, dlogits = weights_of(stats, *own)
+        term_ref[0, :, cols] = dot(dlogits, query, 1, 0) * FACTOR
+        term_ref[1, :, cols] = dot(weights, cotangent, 1, 0)
+
+
+def attend_kernel(
     peers,
     rows_ref,
-    part_ref,
+    stats_ref,
     queries_ref,
     direct_keys,
     relayed_keys,
@@ -479,24 +519,15 @@
     other_mem,
     attended_ref,
     grad_query_ref,
-    term_ref,
-    stats_ref,
+    mark_ref,
 ):
-    role = lax.axis_index("tm") & 1
-    frame_len, half_width = own_mem.shape[2:]
+    mark_ref[...] = jnp.zeros(mark_ref.shape, F32)
     heads = queries_ref.shape[1] // DEPTH
-    half = half_width // DEPTH
 
     def pieces(head):
-        cols = head_cols(head % half)
-        prev = prev_parts(peers, direct_keys, relayed_keys, outer_values, pair_ref, head_cols(head))
-        memory = [
-            jnp.where(role == head // half, own_mem[:, kind, :, cols], other_mem[:, kind, :, cols]).reshape(
-                MEM * frame_len, DEPTH
-            )
-            for kind in range(2)
-        ]
-        return (PREV, prev), (OWN, joined_parts(own_ref, head_cols(head))), (MEMORY, memory)
+        cols = head_cols(head)
+        prev = prev_parts(peers, direct_keys, relayed_keys, outer_values, pair_ref, cols)
+        return (PREV, prev), (OWN, joined_parts(own_ref, cols)), (MEMORY, memory_parts(own_mem, other_mem, head))
 
     def products(head):
         query, cotangent = joined_parts(queries_ref, head_cols(head))
@@ -511,17 +542,12 @@
         if head + 1 < heads:
             ahead = products(head + 1)
         cols = head_cols(head)
-        query, cotangent = joined_parts(queries_ref, cols)
-        stats, *last = rounded(load_part(part_ref, head), *now[-1])
-        store_part(stats_ref, head, stats)
-        rounds = [weights_of(stats, *now[PREV]), weights_of(stats, *now[OWN]), last]
+        stats = load_part(stats_ref, head)
         attended = grad_query = 0.0
-        for (piece, (keys, values)), (weights, dlogits) in zip(pieces(head), rounds):
+        for (_, (keys, values)), piece in zip(pieces(head), now):
+            weights, dlogits = weights_of(stats, *piece)
             attended += dot(values, weights, 0, 0)
             grad_query += dot(keys, dlogits, 0, 0)
-            if piece == OWN:
-                term_ref[0, :, cols] = dot(dlogits, query, 1, 0) * FACTOR
-                term_ref[1, :, cols] = dot(weights, cotangent, 1, 0)
         attended_ref[:, cols] = attended.T.astype(BF16)
         grad_query_ref[:, cols] = (grad_query * FACTOR).T.astype(BF16)
 
@@ -659,13 +685,13 @@
     )
     other_mem = swap(pair_mem, 1, 1, peers)
     pair_sums = shape(F32, 2, row_count, width)
-    attended, grad_query, own_terms, stats_all = call(
-        functools.partial(rest_kernel, peers),
-        [shape(BF16, row_count, width)] * 2 + [pair_sums, stats],
-        [rows, part, queries, *outer, pair, joined, own_mem, other_mem],
+    own_terms, stats_all = call(
+        own_kernel,
+        [pair_sums, stats],
+        [rows, part, queries, joined, own_mem, other_mem],
         after=[send],
         flops=HIDING * piece_flops,
-        name="rest",
+        name="own",
     )
     next_stats = lax.ppermute(stats_all, "tm", [(i, i - 1) for i in range(1, peers)])
     (passed_on,) = call(
@@ -684,11 +710,19 @@
         if step + 1 < len(turns):
             after = [own_terms, next_queries]
             keep, send = call(add_kernel, [sums, held], [keep, got], after=after, name="add")
+    attended, grad_query, mark = call(
+        functools.partial(attend_kernel, peers),
+        [shape(BF16, row_count, width)] * 2 + [shape(F32, 8, 128)],
+        [rows, stats_all, queries, *outer, pair, joined, own_mem, other_mem],
+        after=[send],
+        flops=HIDING * piece_flops,
+        name="attend",
+    )
     owned_mine, owned_send = call(
         owned_kernel,
         [shape(F32, FR_DEV, 2, frame_len, half_width), shape(BF16, FR_DEV, 2, frame_len, half_width)],
         [codes, keep, got],
-        after=[own],
+        after=[own, mark],
         name="owned",
     )
     owned_got = swap(owned_send, 1, 1, peers)

time: 60.7 us -> 60.2 us (level)
  waiting for transfers between devices: 16 us -> 13.9 us
  starting transfers between devices: 26.7 us -> 27.7 us
    ppermute x2, starting transfers between devices: 2 us -> 4.48 us  [shift_second(): return lax.ppermute(block, 'tm', pairs) if pairs else block]
    ppermute x9, waiting for transfers between devices: 15.8 us -> 13.9 us  [swap(): lax.ppermute(block, 'tm', [(i, i ^ (odd_bit if i & 1 else even_bit)) for...]
    ppermute x9, starting transfers between devices: 20 us -> 18.6 us  [swap(): lax.ppermute(block, 'tm', [(i, i ^ (odd_bit if i & 1 else even_bit)) for...]
    pallas_call x12 -> x13, Pallas kernels: 14.6 us -> 15.2 us  [call(): pl.pallas_call(run, out_shape=outs, in_specs=[SMEM] * len(scalars) + [VME...]
  transfers between devices with their start and end apart: 16 -> 16, of which waited for: 6 -> 5; matrix products, arithmetic and copies ran while one was open for 0% -> 0% of each run, Pallas kernels for 24% -> 25%
where the time goes in v14:
time: 60.2 us; the launch traced here: 60 us
  starting transfers between devices  27.7 us (46%)
  Pallas kernels  17.5 us (29%)
  waiting for transfers between devices  13.9 us (23%)
  between operations  0.87 us (1%)
    ppermute x9, starting transfers between devices, swap(): lax.ppermute(block, 'tm', [(i, i ^ (odd_bit if i & 1 else even_bit)) for...  18.6 us
    pallas_call x13, Pallas kernels, call(): pl.pallas_call(run, out_shape=outs, in_specs=[SMEM] * len(scalars) + [VME...  15.2 us
    ppermute x9, waiting for transfers between devices, swap(): lax.ppermute(block, 'tm', [(i, i ^ (odd_bit if i & 1 else even_bit)) for...  13.9 us
    ppermute x2, starting transfers between devices, shift_second(): return lax.ppermute(block, 'tm', pairs) if pairs else block  4.48 us
    pallas_call x2, Pallas kernels, join(): pl.pallas_call(run, out_shape=shape(BF16, rows, width), in_specs=[pl.Bloc...  2.34 us
    ppermute x2, starting transfers between devices, shift_first(): lax.ppermute(block, 'tm', [(i, relays.get((i, j), j)) for i, j in pairs])  1.97 us
    ppermute x2, starting transfers between devices, shift(): return lax.ppermute(block, 'tm', pairs)  1.36 us
    ppermute x1, starting transfers between devices, body(): lax.ppermute(stats_all, 'tm', [(i, i - 1) for i in range(1, peers)])  1.29 us
  transfers between devices with their start and end apart: 16, of which 5 were waited for; matrix products, arithmetic and copies ran while one was open for 0% of the time, Pallas kernels for 25%

profile of v14, /device:TPU:0, one launch (start us, length us, event | category | flops | bytes accessed | tf_op | source)
XLA Modules:
  0.0 60.0 jit_solution(1558434648433061661)
XLA Ops:
  0.7 1.2 %join.1.refs_5_.refs_1_.refs_6_.refs_3_.refs_7_ = bf16[528,768]{1,0:T(8,128)(2,1)S(1)} custom-call(s32[1,2]{1,0:T(1,128)} %refs_1_.4, bf16[256,768]{1,0:T(8,128)(2,1)} %refs_1_.3, bf16[256,768]{1,0:T(8,128)(2,1)} %refs_2_.2), custom_call_target="tpu_custom_call" | custom-call | tf_op jit(solution)/shard_map/join/pallas_call | solution.py:620
  1.9 0.5 collective-permute-start
  2.4 0.7 %collective-permute-start.1 = (bf16[256,768]{1,0:T(8,128)(2,1)S(1)}, bf16[256,768]{1,0:T(8,128)(2,1)S(1)}, u32[]{:S(2)}, u32[]{:S(2)}) collective-permute-start(bf16[256,768]{1,0:T(8,128)(2,1)S(1)} %copy-done.4), channel_id=1, source_target_pairs={{1,2},{3,7},{5,6},{9,10},{11,15},{13,14},{17,18},{19,23},{21,22},{... | collective-permute-start | bytes 1179656 | tf_op jit(solution)/shard_map/ppermute | solution.py:66
  3.1 1.3 %collective-permute-done.refs_4_.refs_2_.refs_5_.refs_6_ = bf16[528,768]{1,0:T(8,128)(2,1)S(1)} collective-permute-done((bf16[528,768]{1,0:T(8,128)(2,1)S(1)}, bf16[528,768]{1,0:T(8,128)(2,1)S(1)}, u32[]{:S(2)}, u32[]{:S(2)}) %collective-permute-start) | collective-permute-done | bytes 811040 | tf_op jit(solution)/shard_map/ppermute | solution.py:50
  4.3 0.3 split.1.refs_2_.refs_1_
  4.7 0.0 copy-start.1
  4.7 0.0 copy-start.2
  4.7 0.0 copy-start.3
  4.7 2.9 %collective-permute-start.4 = (bf16[3,2,128,384]{3,2,1,0:T(8,128)(2,1)S(1)}, bf16[3,2,128,384]{3,2,1,0:T(8,128)(2,1)S(1)}, u32[]{:S(2)}, u32[]{:S(2)}) collective-permute-start(bf16[3,2,128,384]{3,2,1,0:T(8,128)(2,1)S(1)} %split.1.refs_2_.refs_1_), channel_id=1, source_target_pairs={{0,2},{1,5},{2,0},{3,7},{4,6},{5,1},{6,4},{7,3},{8,10},{9,13},{10,... | collective-permute-start | bytes 1769480 | tf_op jit(solution)/shard_map/ppermute | solution.py:50
  7.6 1.1 %join_queries.1.refs_1_.refs_4_.refs_2_ = bf16[512,768]{1,0:T(8,128)(2,1)S(1)} custom-call(bf16[256,768]{1,0:T(8,128)(2,1)} %refs_0_.3, bf16[256,768]{1,0:T(8,128)(2,1)} %refs_1_.5, bf16[3,2,128,384]{3,2,1,0:T(8,128)(2,1)S(1)} %split.1.refs_2_.refs_1_), custom_call_target="tpu_custom_call" | custom-call | tf_op jit(solution)/shard_map/join_queries/pallas_call | solution.py:620
  8.8 1.1 %collective-permute-start.5 = (bf16[512,768]{1,0:T(8,128)(2,1)S(1)}, bf16[512,768]{1,0:T(8,128)(2,1)S(1)}, u32[]{:S(2)}, u32[]{:S(2)}) collective-permute-start(bf16[512,768]{1,0:T(8,128)(2,1)S(1)} %join_queries.1.refs_1_.refs_4_.refs_2_), channel_id=1, source_target_pairs={{0,1},{1,0},{2,3},{3,2},{4,5},{5,4},{6,7},{7,6},{8,9},{9,8},{10,11... | collective-permute-start | bytes 2359304 | tf_op jit(solution)/shard_map/ppermute | solution.py:50
  9.9 0.0 collective-permute-done.1.refs_6_.refs_2_.refs_3_
  9.9 1.7 %plan.1 = (f32[6,16,256]{2,1,0:T(8,128)S(1)}, s32[8,128]{1,0:T(8,128)S(1)}, bf16[256,768]{1,0:T(8,128)(2,1)S(1)}, bf16[256,768]{1,0:T(8,128)(2,1)S(1)}) custom-call(s32[1,4]{1,0:T(1,128)S(1)} %bitcast.2, s32[1,2]{1,0:T(1,128)S(1)} %copy-done.1, s32[16]{0:T(128)S(1)} %copy-done.3, f32[6,16,16]{2,1,0:T(8,128)S(1)} %copy-done.2, ...), custom_call_target="tpu_custom_call" | custom-call | flops 20132659200 | tf_op jit(solution)/shard_map/plan/pallas_call | solution.py:38
  11.6 0.7 %collective-permute-start.2 = (bf16[256,768]{1,0:T(8,128)(2,1)S(1)}, bf16[256,768]{1,0:T(8,128)(2,1)S(1)}, u32[]{:S(2)}, u32[]{:S(2)}) collective-permute-start(bf16[256,768]{1,0:T(8,128)(2,1)S(1)} %get-tuple-element.27), channel_id=1, source_target_pairs={{7,4},{15,12},{23,20},{31,28}} | collective-permute-start | bytes 1179656 | tf_op jit(solution)/shard_map/ppermute | solution.py:71
  12.3 0.7 %collective-permute-start.3 = (bf16[256,768]{1,0:T(8,128)(2,1)S(1)}, bf16[256,768]{1,0:T(8,128)(2,1)S(1)}, u32[]{:S(2)}, u32[]{:S(2)}) collective-permute-start(bf16[256,768]{1,0:T(8,128)(2,1)S(1)} %get-tuple-element.28), channel_id=1, source_target_pairs={{1,2},{3,4},{5,6},{9,10},{11,12},{13,14},{17,18},{19,20},{21,22},{... | collective-permute-start | bytes 1179656 | tf_op jit(solution)/shard_map/ppermute | solution.py:55
  12.9 4.9 %collective-permute-done.4.refs_2_ = bf16[3,2,128,384]{3,2,1,0:T(8,128)(2,1)S(1)} collective-permute-done((bf16[3,2,128,384]{3,2,1,0:T(8,128)(2,1)S(1)}, bf16[3,2,128,384]{3,2,1,0:T(8,128)(2,1)S(1)}, u32[]{:S(2)}, u32[]{:S(2)}) %collective-permute-start.4) | collective-permute-done | bytes 589856 | tf_op jit(solution)/shard_map/ppermute | solution.py:50
  17.8 0.0 collective-permute-done.5.refs_4_.refs_5_.refs_2_
  17.8 0.3 step.1.refs_1_
  18.1 1.6 %collective-permute-start.6 = (bf16[3,2,128,384]{3,2,1,0:T(8,128)(2,1)S(1)}, bf16[3,2,128,384]{3,2,1,0:T(8,128)(2,1)S(1)}, u32[]{:S(2)}, u32[]{:S(2)}) collective-permute-start(bf16[3,2,128,384]{3,2,1,0:T(8,128)(2,1)S(1)} %step.1.refs_1_), channel_id=1, source_target_pairs={{0,4},{1,3},{2,6},{3,1},{4,0},{5,7},{6,2},{7,5},{8,12},{9,11},{10,... | collective-permute-start | bytes 1769480 | tf_op jit(solution)/shard_map/ppermute | solution.py:50
  19.7 0.0 collective-permute-done.2.refs_3_.refs_4_
  19.7 0.0 collective-permute-done.3.refs_4_.refs_5_
  19.7 1.6 %stats.1 = (f32[6,8,256]{2,1,0:T(8,128)S(1)}, bf16[256,768]{1,0:T(8,128)(2,1)S(1)}, bf16[256,768]{1,0:T(8,128)(2,1)S(1)}) custom-call(f32[6,16,256]{2,1,0:T(8,128)S(1)} %get-tuple-element.26.refs_0_.refs_1_, bf16[512,768]{1,0:T(8,128)(2,1)S(1)} %join_queries.1.refs_1_.refs_4_.refs_2_, bf16[256,768]{1,0:T(8,128)(2,1)S(1)} %collective-permute-done.1.refs_6_.refs_2_.refs_3_, ...), custom_call_target="tpu_custom_call" | custom-call | flops 20132659200 | tf_op jit(solution)/shard_map/stats/pallas_call | solution.py:38
  21.3 6.2 %collective-permute-start.8 = (f32[6,8,256]{2,1,0:T(8,128)S(1)}, f32[6,8,256]{2,1,0:T(8,128)S(1)}, u32[]{:S(2)}, u32[]{:S(2)}) collective-permute-start(f32[6,8,256]{2,1,0:T(8,128)S(1)} %get-tuple-element.29.refs_2_.refs_1_), channel_id=1, source_target_pairs={{0,1},{1,0},{2,3},{3,2},{4,5},{5,4},{6,7},{7,6},{8,9},{9,8},{10,11... | collective-permute-start | bytes 147464 | tf_op jit(solution)/shard_map/ppermute | solution.py:50
  27.5 0.7 %collective-permute-start.10 = (bf16[256,768]{1,0:T(8,128)(2,1)S(1)}, bf16[256,768]{1,0:T(8,128)(2,1)S(1)}, u32[]{:S(2)}, u32[]{:S(2)}) collective-permute-start(bf16[256,768]{1,0:T(8,128)(2,1)S(1)} %get-tuple-element.37), channel_id=1, source_target_pairs={{2,1},{4,3},{6,5},{10,9},{12,11},{14,13},{18,17},{20,19},{22,21},{... | collective-permute-start | bytes 1179656 | tf_op jit(solution)/shard_map/ppermute | solution.py:55
  28.2 1.3 %collective-permute-start.12 = (bf16[256,768]{1,0:T(8,128)(2,1)S(1)}, bf16[256,768]{1,0:T(8,128)(2,1)S(1)}, u32[]{:S(2)}, u32[]{:S(2)}) collective-permute-start(bf16[256,768]{1,0:T(8,128)(2,1)S(1)} %get-tuple-element.41), channel_id=1, source_target_pairs={{2,1},{4,0},{6,5},{10,9},{12,8},{14,13},{18,17},{20,16},{22,21},{2... | collective-permute-start | bytes 1179656 | tf_op jit(solution)/shard_map/ppermute | solution.py:66
  29.5 0.0 collective-permute-done.6.refs_2_
  29.5 0.3 pick.1
  29.8 2.7 %collective-permute-start.7 = (bf16[2,2,128,384]{3,2,1,0:T(8,128)(2,1)S(1)}, bf16[2,2,128,384]{3,2,1,0:T(8,128)(2,1)S(1)}, u32[]{:S(2)}, u32[]{:S(2)}) collective-permute-start(bf16[2,2,128,384]{3,2,1,0:T(8,128)(2,1)S(1)} %get-tuple-element.32.refs_7_), channel_id=1, source_target_pairs={{0,1},{1,0},{2,3},{3,2},{4,5},{5,4},{6,7},{7,6},{8,9},{9,8},{10,11... | collective-permute-start | bytes 1179656 | tf_op jit(solution)/shard_map/ppermute | solution.py:50
  32.5 0.0 collective-permute-done.8.refs_3_
  32.5 1.9 %memory.1 = (f32[4,2,128,384]{3,2,1,0:T(8,128)S(1)}, bf16[3,2,128,384]{3,2,1,0:T(8,128)(2,1)S(1)}) custom-call(s32[8,128]{1,0:T(8,128)S(1)} %get-tuple-element.30.refs_3_.refs_0_, f32[6,16,256]{2,1,0:T(8,128)S(1)} %get-tuple-element.26.refs_0_.refs_1_, f32[6,8,256]{2,1,0:T(8,128)S(1)} %get-tuple-element.29.refs_2_.refs_1_, ...), custom_call_target="tpu_custom_call" | custom-call | flops 20132659200 | tf_op jit(solution)/shard_map/memory/pallas_call | solution.py:38
  34.5 2.6 %collective-permute-start.9 = (bf16[3,2,128,384]{3,2,1,0:T(8,128)(2,1)S(1)}, bf16[3,2,128,384]{3,2,1,0:T(8,128)(2,1)S(1)}, u32[]{:S(2)}, u32[]{:S(2)}) collective-permute-start(bf16[3,2,128,384]{3,2,1,0:T(8,128)(2,1)S(1)} %get-tuple-element.33.refs_6_), channel_id=1, source_target_pairs={{0,4},{1,3},{2,6},{3,1},{4,0},{5,7},{6,2},{7,5},{8,12},{9,11},{10,... | collective-permute-start | bytes 1769480 | tf_op jit(solution)/shard_map/ppermute | solution.py:50
  37.1 0.0 collective-permute-done.7.refs_5_.refs_9_
  37.1 2.5 %own.1 = (f32[2,256,768]{2,1,0:T(8,128)S(1)}, f32[6,8,256]{2,1,0:T(8,128)S(1)}) custom-call(f32[6,16,256]{2,1,0:T(8,128)S(1)} %get-tuple-element.26.refs_0_.refs_1_, f32[6,8,256]{2,1,0:T(8,128)S(1)} %get-tuple-element.29.refs_2_.refs_1_, bf16[512,768]{1,0:T(8,128)(2,1)S(1)} %join_queries.1.refs_1_.refs_4_.refs_2_, ...), custom_call_target="tpu_custom_call" | custom-call | flops 20132659200 | tf_op jit(solution)/shard_map/own/pallas_call | solution.py:38
  39.6 1.3 %collective-permute-start.11 = (f32[6,8,256]{2,1,0:T(8,128)S(1)}, f32[6,8,256]{2,1,0:T(8,128)S(1)}, u32[]{:S(2)}, u32[]{:S(2)}) collective-permute-start(f32[6,8,256]{2,1,0:T(8,128)S(1)} %get-tuple-element.34.refs_1_), channel_id=1, source_target_pairs={{1,0},{2,1},{3,2},{4,3},{5,4},{6,5},{7,6},{9,8},{10,9},{11,10},{12... | collective-permute-start | bytes 147464 | tf_op jit(solution)/shard_map/ppermute | solution.py:696
  40.9 0.0 collective-permute-done.12.refs_0_.refs_4_
  41.0 3.8 %collective-permute-start.13 = (bf16[256,768]{1,0:T(8,128)(2,1)S(1)}, bf16[256,768]{1,0:T(8,128)(2,1)S(1)}, u32[]{:S(2)}, u32[]{:S(2)}) collective-permute-start(bf16[256,768]{1,0:T(8,128)(2,1)S(1)} %pass_on.1), channel_id=1, source_target_pairs={{0,3},{8,11},{16,19},{24,27}} | collective-permute-start | bytes 1179656 | tf_op jit(solution)/shard_map/ppermute | solution.py:71
  44.8 0.0 collective-permute-done.10.refs_3_
  44.8 1.9 %collective-permute-done.9.refs_1_ = bf16[3,2,128,384]{3,2,1,0:T(8,128)(2,1)S(1)} collective-permute-done((bf16[3,2,128,384]{3,2,1,0:T(8,128)(2,1)S(1)}, bf16[3,2,128,384]{3,2,1,0:T(8,128)(2,1)S(1)}, u32[]{:S(2)}, u32[]{:S(2)}) %collective-permute-start.9) | collective-permute-done | bytes 589856 | tf_op jit(solution)/shard_map/ppermute | solution.py:50
  46.7 0.2 add.1
  46.9 0.7 %collective-permute-start.14 = (bf16[3,2,128,384]{3,2,1,0:T(8,128)(2,1)S(1)}, bf16[3,2,128,384]{3,2,1,0:T(8,128)(2,1)S(1)}, u32[]{:S(2)}, u32[]{:S(2)}) collective-permute-start(bf16[3,2,128,384]{3,2,1,0:T(8,128)(2,1)S(1)} %get-tuple-element.38.refs_10_), channel_id=1, source_target_pairs={{0,2},{1,5},{2,0},{3,7},{4,6},{5,1},{6,4},{7,3},{8,10},{9,13},{10,... | collective-permute-start | bytes 1769480 | tf_op jit(solution)/shard_map/ppermute | solution.py:50
  47.6 3.8 %attend.1 = (bf16[256,768]{1,0:T(8,128)(2,1)}, bf16[256,768]{1,0:T(8,128)(2,1)}, f32[8,128]{1,0:T(8,128)S(1)}) custom-call(f32[6,16,256]{2,1,0:T(8,128)S(1)} %get-tuple-element.26.refs_0_.refs_1_, f32[6,8,256]{2,1,0:T(8,128)S(1)} %get-tuple-element.34.refs_1_, bf16[512,768]{1,0:T(8,128)(2,1)S(1)} %join_queries.1.refs_1_.refs_4_.refs_2_, ...), custom_call_target="tpu_custom_call" | custom-call | flops 20132659200 | tf_op jit(solution)/shard_map/attend/pallas_call | solution.py:38
  51.4 0.0 collective-permute-done.11.refs_1_
  51.4 1.2 %next.1.refs_3_.refs_0_ = f32[2,256,768]{2,1,0:T(8,128)S(1)} custom-call(f32[6,16,256]{2,1,0:T(8,128)S(1)} %get-tuple-element.26.refs_0_.refs_1_, f32[6,8,256]{2,1,0:T(8,128)S(1)} %collective-permute-done.11.refs_1_, bf16[512,768]{1,0:T(8,128)(2,1)S(1)} %collective-permute-done.5.refs_4_.refs_5_.refs_2_, ...), custom_call_target="tpu_custom_call" | custom-call | flops 20132659200 | tf_op jit(solution)/shard_map/next/pallas_call | solution.py:38
  52.6 4.2 %collective-permute-done.14.refs_2_ = bf16[3,2,128,384]{3,2,1,0:T(8,128)(2,1)S(1)} collective-permute-done((bf16[3,2,128,384]{3,2,1,0:T(8,128)(2,1)S(1)}, bf16[3,2,128,384]{3,2,1,0:T(8,128)(2,1)S(1)}, u32[]{:S(2)}, u32[]{:S(2)}) %collective-permute-start.14) | collective-permute-done | bytes 589856 | tf_op jit(solution)/shard_map/ppermute | solution.py:50
  56.8 0.3 owned.1
  57.1 0.2 collective-permute-start.15
  57.3 1.6 %collective-permute-done.15.refs_2_ = bf16[2,2,128,384]{3,2,1,0:T(8,128)(2,1)S(1)} collective-permute-done((bf16[2,2,128,384]{3,2,1,0:T(8,128)(2,1)S(1)}, bf16[2,2,128,384]{3,2,1,0:T(8,128)(2,1)S(1)}, u32[]{:S(2)}, u32[]{:S(2)}) %collective-permute-start.15) | collective-permute-done | bytes 393248 | tf_op jit(solution)/shard_map/ppermute | solution.py:50
  58.9 1.0 %final.1 = (bf16[256,768]{1,0:T(8,128)(2,1)}, bf16[256,768]{1,0:T(8,128)(2,1)}) custom-call(f32[2,256,768]{2,1,0:T(8,128)S(1)} %next.1.refs_3_.refs_0_, f32[2,2,128,384]{3,2,1,0:T(8,128)S(1)} %get-tuple-element.44.refs_1_, bf16[2,2,128,384]{3,2,1,0:T(8,128)(2,1)S(1)} %collective-permute-done.15.refs_2_), custom_call_target="tpu_custom_call" | custom-call | tf_op jit(solution)/shard_map/final/pallas_call | solution.py:38
  (9 shorter events, 0.0 us)
Async XLA Ops:
  0.6 1.8 %copy-start.4 = (bf16[256,768]{1,0:T(8,128)(2,1)S(1)}, bf16[256,768]{1,0:T(8,128)(2,1)}, u32[]{:S(2)}) copy-start(bf16[256,768]{1,0:T(8,128)(2,1)} %refs_1_.3) | copy-start | bytes 1179652
  0.6 3.7 %copy-start = (s32[4]{0:T(128)S(1)}, s32[4]{0:T(128)}, u32[]{:S(2)}) copy-start(s32[4]{0:T(128)} %param.15) | copy-start | bytes 52
  1.9 2.5 %collective-permute-start = (bf16[528,768]{1,0:T(8,128)(2,1)S(1)}, bf16[528,768]{1,0:T(8,128)(2,1)S(1)}, u32[]{:S(2)}, u32[]{:S(2)}) collective-permute-start(bf16[528,768]{1,0:T(8,128)(2,1)S(1)} %join.1.refs_5_.refs_1_.refs_6_.refs_3_.refs_7_), channel_id=1, source_target_pairs={{0,1},{1,0},{2,3},{3,2},{4,5},{5,4},{6,7},{7,6},{8,9},{9,8},{10,11... | collective-permute-start | bytes 2433032 | tf_op jit(solution)/shard_map/ppermute | solution.py:50
  2.4 7.5 %collective-permute-start.1 = (bf16[256,768]{1,0:T(8,128)(2,1)S(1)}, bf16[256,768]{1,0:T(8,128)(2,1)S(1)}, u32[]{:S(2)}, u32[]{:S(2)}) collective-permute-start(bf16[256,768]{1,0:T(8,128)(2,1)S(1)} %copy-done.4), channel_id=1, source_target_pairs={{1,2},{3,7},{5,6},{9,10},{11,15},{13,14},{17,18},{19,23},{21,22},{... | collective-permute-start | bytes 1179656 | tf_op jit(solution)/shard_map/ppermute | solution.py:66
  4.7 5.2 %copy-start.1 = (s32[1,2]{1,0:T(1,128)S(1)}, s32[1,2]{1,0:T(1,128)}, u32[]{:S(2)}) copy-start(s32[1,2]{1,0:T(1,128)} %refs_1_.4) | copy-start | bytes 28
  4.7 5.2 %copy-start.2 = (f32[6,16,16]{2,1,0:T(8,128)S(1)}, f32[6,16,16]{2,1,0:T(8,128)}, u32[]{:S(2)}) copy-start(f32[6,16,16]{2,1,0:T(8,128)} %refs_3_.1) | copy-start | bytes 18436
  4.7 5.2 %copy-start.3 = (s32[16]{0:T(128)S(1)}, s32[16]{0:T(128)}, u32[]{:S(2)}) copy-start(s32[16]{0:T(128)} %refs_2_.3) | copy-start | bytes 196
  4.7 13.1 %collective-permute-start.4 = (bf16[3,2,128,384]{3,2,1,0:T(8,128)(2,1)S(1)}, bf16[3,2,128,384]{3,2,1,0:T(8,128)(2,1)S(1)}, u32[]{:S(2)}, u32[]{:S(2)}) collective-permute-start(bf16[3,2,128,384]{3,2,1,0:T(8,128)(2,1)S(1)} %split.1.refs_2_.refs_1_), channel_id=1, source_target_pairs={{0,2},{1,5},{2,0},{3,7},{4,6},{5,1},{6,4},{7,3},{8,10},{9,13},{10,... | collective-permute-start | bytes 1769480 | tf_op jit(solution)/shard_map/ppermute | solution.py:50
  8.8 9.1 %collective-permute-start.5 = (bf16[512,768]{1,0:T(8,128)(2,1)S(1)}, bf16[512,768]{1,0:T(8,128)(2,1)S(1)}, u32[]{:S(2)}, u32[]{:S(2)}) collective-permute-start(bf16[512,768]{1,0:T(8,128)(2,1)S(1)} %join_queries.1.refs_1_.refs_4_.refs_2_), channel_id=1, source_target_pairs={{0,1},{1,0},{2,3},{3,2},{4,5},{5,4},{6,7},{7,6},{8,9},{9,8},{10,11... | collective-permute-start | bytes 2359304 | tf_op jit(solution)/shard_map/ppermute | solution.py:50
  11.6 8.2 %collective-permute-start.2 = (bf16[256,768]{1,0:T(8,128)(2,1)S(1)}, bf16[256,768]{1,0:T(8,128)(2,1)S(1)}, u32[]{:S(2)}, u32[]{:S(2)}) collective-permute-start(bf16[256,768]{1,0:T(8,128)(2,1)S(1)} %get-tuple-element.27), channel_id=1, source_target_pairs={{7,4},{15,12},{23,20},{31,28}} | collective-permute-start | bytes 1179656 | tf_op jit(solution)/shard_map/ppermute | solution.py:71
  12.3 7.5 %collective-permute-start.3 = (bf16[256,768]{1,0:T(8,128)(2,1)S(1)}, bf16[256,768]{1,0:T(8,128)(2,1)S(1)}, u32[]{:S(2)}, u32[]{:S(2)}) collective-permute-start(bf16[256,768]{1,0:T(8,128)(2,1)S(1)} %get-tuple-element.28), channel_id=1, source_target_pairs={{1,2},{3,4},{5,6},{9,10},{11,12},{13,14},{17,18},{19,20},{21,22},{... | collective-permute-start | bytes 1179656 | tf_op jit(solution)/shard_map/ppermute | solution.py:55
  18.1 11.3 %collective-permute-start.6 = (bf16[3,2,128,384]{3,2,1,0:T(8,128)(2,1)S(1)}, bf16[3,2,128,384]{3,2,1,0:T(8,128)(2,1)S(1)}, u32[]{:S(2)}, u32[]{:S(2)}) collective-permute-start(bf16[3,2,128,384]{3,2,1,0:T(8,128)(2,1)S(1)} %step.1.refs_1_), channel_id=1, source_target_pairs={{0,4},{1,3},{2,6},{3,1},{4,0},{5,7},{6,2},{7,5},{8,12},{9,11},{10,... | collective-permute-start | bytes 1769480 | tf_op jit(solution)/shard_map/ppermute | solution.py:50
  21.3 11.2 %collective-permute-start.8 = (f32[6,8,256]{2,1,0:T(8,128)S(1)}, f32[6,8,256]{2,1,0:T(8,128)S(1)}, u32[]{:S(2)}, u32[]{:S(2)}) collective-permute-start(f32[6,8,256]{2,1,0:T(8,128)S(1)} %get-tuple-element.29.refs_2_.refs_1_), channel_id=1, source_target_pairs={{0,1},{1,0},{2,3},{3,2},{4,5},{5,4},{6,7},{7,6},{8,9},{9,8},{10,11... | collective-permute-start | bytes 147464 | tf_op jit(solution)/shard_map/ppermute | solution.py:50
  27.5 17.3 %collective-permute-start.10 = (bf16[256,768]{1,0:T(8,128)(2,1)S(1)}, bf16[256,768]{1,0:T(8,128)(2,1)S(1)}, u32[]{:S(2)}, u32[]{:S(2)}) collective-permute-start(bf16[256,768]{1,0:T(8,128)(2,1)S(1)} %get-tuple-element.37), channel_id=1, source_target_pairs={{2,1},{4,3},{6,5},{10,9},{12,11},{14,13},{18,17},{20,19},{22,21},{... | collective-permute-start | bytes 1179656 | tf_op jit(solution)/shard_map/ppermute | solution.py:55
  28.2 12.7 %collective-permute-start.12 = (bf16[256,768]{1,0:T(8,128)(2,1)S(1)}, bf16[256,768]{1,0:T(8,128)(2,1)S(1)}, u32[]{:S(2)}, u32[]{:S(2)}) collective-permute-start(bf16[256,768]{1,0:T(8,128)(2,1)S(1)} %get-tuple-element.41), channel_id=1, source_target_pairs={{2,1},{4,0},{6,5},{10,9},{12,8},{14,13},{18,17},{20,16},{22,21},{2... | collective-permute-start | bytes 1179656 | tf_op jit(solution)/shard_map/ppermute | solution.py:66
  29.8 7.3 %collective-permute-start.7 = (bf16[2,2,128,384]{3,2,1,0:T(8,128)(2,1)S(1)}, bf16[2,2,128,384]{3,2,1,0:T(8,128)(2,1)S(1)}, u32[]{:S(2)}, u32[]{:S(2)}) collective-permute-start(bf16[2,2,128,384]{3,2,1,0:T(8,128)(2,1)S(1)} %get-tuple-element.32.refs_7_), channel_id=1, source_target_pairs={{0,1},{1,0},{2,3},{3,2},{4,5},{5,4},{6,7},{7,6},{8,9},{9,8},{10,11... | collective-permute-start | bytes 1179656 | tf_op jit(solution)/shard_map/ppermute | solution.py:50
  34.5 12.2 %collective-permute-start.9 = (bf16[3,2,128,384]{3,2,1,0:T(8,128)(2,1)S(1)}, bf16[3,2,128,384]{3,2,1,0:T(8,128)(2,1)S(1)}, u32[]{:S(2)}, u32[]{:S(2)}) collective-permute-start(bf16[3,2,128,384]{3,2,1,0:T(8,128)(2,1)S(1)} %get-tuple-element.33.refs_6_), channel_id=1, source_target_pairs={{0,4},{1,3},{2,6},{3,1},{4,0},{5,7},{6,2},{7,5},{8,12},{9,11},{10,... | collective-permute-start | bytes 1769480 | tf_op jit(solution)/shard_map/ppermute | solution.py:50
  39.6 11.8 %collective-permute-start.11 = (f32[6,8,256]{2,1,0:T(8,128)S(1)}, f32[6,8,256]{2,1,0:T(8,128)S(1)}, u32[]{:S(2)}, u32[]{:S(2)}) collective-permute-start(f32[6,8,256]{2,1,0:T(8,128)S(1)} %get-tuple-element.34.refs_1_), channel_id=1, source_target_pairs={{1,0},{2,1},{3,2},{4,3},{5,4},{6,5},{7,6},{9,8},{10,9},{11,10},{12... | collective-permute-start | bytes 147464 | tf_op jit(solution)/shard_map/ppermute | solution.py:696
  41.0 10.4 %collective-permute-start.13 = (bf16[256,768]{1,0:T(8,128)(2,1)S(1)}, bf16[256,768]{1,0:T(8,128)(2,1)S(1)}, u32[]{:S(2)}, u32[]{:S(2)}) collective-permute-start(bf16[256,768]{1,0:T(8,128)(2,1)S(1)} %pass_on.1), channel_id=1, source_target_pairs={{0,3},{8,11},{16,19},{24,27}} | collective-permute-start | bytes 1179656 | tf_op jit(solution)/shard_map/ppermute | solution.py:71
  46.9 9.9 %collective-permute-start.14 = (bf16[3,2,128,384]{3,2,1,0:T(8,128)(2,1)S(1)}, bf16[3,2,128,384]{3,2,1,0:T(8,128)(2,1)S(1)}, u32[]{:S(2)}, u32[]{:S(2)}) collective-permute-start(bf16[3,2,128,384]{3,2,1,0:T(8,128)(2,1)S(1)} %get-tuple-element.38.refs_10_), channel_id=1, source_target_pairs={{0,2},{1,5},{2,0},{3,7},{4,6},{5,1},{6,4},{7,3},{8,10},{9,13},{10,... | collective-permute-start | bytes 1769480 | tf_op jit(solution)/shard_map/ppermute | solution.py:50
  57.1 1.8 %collective-permute-start.15 = (bf16[2,2,128,384]{3,2,1,0:T(8,128)(2,1)S(1)}, bf16[2,2,128,384]{3,2,1,0:T(8,128)(2,1)S(1)}, u32[]{:S(2)}, u32[]{:S(2)}) collective-permute-start(bf16[2,2,128,384]{3,2,1,0:T(8,128)(2,1)S(1)} %get-tuple-element.45), channel_id=1, source_target_pairs={{0,1},{1,0},{2,3},{3,2},{4,5},{5,4},{6,7},{7,6},{8,9},{9,8},{10,11... | collective-permute-start | bytes 1179656 | tf_op jit(solution)/shard_map/ppermute | solution.py:50

commit v15 on v14

--- a/solution.py
+++ b/solution.py
@@ -11,7 +11,6 @@
 FR_DEV = 2
 MEM = 2
 DEPTH = 128
-TAIL = 16
 
 BLOCKED_LOGIT = -1e30
 LOG2E = math.log2(math.e)
@@ -126,32 +125,12 @@
     return jnp.where((me & 1) == 0, even_value, odd_value)
 
 
-def join_kernel(index_ref, key_ref, value_ref, joined_ref, index_buf, sems):
-    rows = key_ref.shape[0]
-    copies = [
-        pltpu.make_async_copy(index_ref, index_buf, sems.at[0]),
-        pltpu.make_async_copy(key_ref, joined_ref.at[pl.ds(0, rows)], sems.at[1]),
-        pltpu.make_async_copy(value_ref, joined_ref.at[pl.ds(rows, rows)], sems.at[2]),
-    ]
-    for copy in copies:
-        copy.start()
-    copies[0].wait()
-    width = joined_ref.shape[1]
-    lane = lax.broadcasted_iota(jnp.int32, (TAIL, width), 1) // DEPTH
-    tail = jnp.zeros((TAIL, width), jnp.int32)
-    for m in range(MEM):
-        tail = jnp.where(lane == m, index_buf[0:1, m : m + 1], tail)
-    joined_ref[2 * rows : 2 * rows + TAIL, :] = tail.astype(F32).astype(BF16)
-    copies[1].wait()
-    copies[2].wait()
-
-
-def join_queries_kernel(query_ref, cotangent_ref, joined_ref, sems):
-    rows = query_ref.shape[0]
-    copies = [
-        pltpu.make_async_copy(ref, joined_ref.at[pl.ds(j * rows, rows)], sems.at[j])
-        for j, ref in enumerate((query_ref, cotangent_ref))
-    ]
+def load_kernel(count, *refs):
+    arrays, outs, sems = refs[:count], refs[count:-1], refs[-1]
+    if len(outs) == 1:
+        rows = arrays[0].shape[0]
+        outs = [outs[0].at[pl.ds(j * rows, rows)] for j in range(count)]
+    copies = [pltpu.make_async_copy(ref, out, sems.at[j]) for j, (ref, out) in enumerate(zip(arrays, outs))]
     for copy in copies:
         copy.start()
     for copy in copies:
@@ -183,10 +162,10 @@
     last_bits,
     bank_ref,
     index_ref,
+    pair_index_ref,
     pose_ref,
     bias_ref,
-    pair_ref,
-    joined_ref,
+    value_ref,
     direct_keys,
     rows_ref,
     codes_ref,
@@ -196,14 +175,10 @@
     me = lax.axis_index("tm")
     last_frame = peers * FR_DEV - 1
     heads, _, row_count = rows_ref.shape
-    values_out[...] = joined_ref[row_count : 2 * row_count, :]
+    values_out[...] = value_ref[...]
     keys_out[...] = direct_keys[...]
     bank = [bank_ref[0, slot] for slot in range(bank_ref.shape[1])]
-    tail = pair_ref.shape[0] - TAIL
-    pair_ids = []
-    for m in range(MEM):
-        slot = jnp.max(pair_ref[tail : tail + TAIL, m * DEPTH : (m + 1) * DEPTH].astype(F32)).astype(jnp.int32)
-        pair_ids.append(bank_ref[0, slot])
+    pair_ids = [bank_ref[0, pair_index_ref[0, m]] for m in range(MEM)]
     mem_ids = [bank_ref[0, index_ref[0, m]] for m in range(MEM)]
 
     own_ids = [me * FR_DEV + j for j in range(FR_DEV)]
@@ -247,7 +222,7 @@
         codes_ref[row : row + 1, :] = jnp.full((1, lanes), code, jnp.int32)
 
 
-def split_kernel(peers, bank_ref, mine_ref, pair_ref, out_ref):
+def split_kernel(peers, bank_ref, key_ref, value_ref, pair_keys, pair_values, out_ref):
     me = lax.axis_index("tm")
     frame_len, half_width = out_ref.shape[2:]
     dyns = dyn_frames(bank_of(bank_ref), peers * FR_DEV - 1)
@@ -255,13 +230,13 @@
     places.append((has_end(me, 0, peers), jnp.where(me < peers // 2, 0, FR_DEV - 1)))
     for j, (local, frame) in enumerate(places):
         for role in range(2):
-            for source, taken in ((mine_ref, local), (pair_ref, jnp.logical_not(local))):
+            for sources, taken in (((key_ref, value_ref), local), ((pair_keys, pair_values), jnp.logical_not(local))):
 
                 @pl.when(jnp.logical_and((me & 1) == role, taken))
-                def _(source=source, j=j, frame=frame, role=role):
-                    for kind in range(2):
-                        start = pl.multiple_of((kind * FR_DEV + frame) * frame_len, frame_len)
-                        out_ref[j, kind] = source[pl.ds(start, frame_len), role * half_width : (role + 1) * half_width]
+                def _(sources=sources, j=j, frame=frame, role=role):
+                    part = pl.ds(pl.multiple_of(frame * frame_len, frame_len), frame_len)
+                    for kind, source in enumerate(sources):
+                        out_ref[j, kind] = source[part, role * half_width : (role + 1) * half_width]
 
 
 def step_kernel(peers, even_done, odd_done, bank_ref, mine_ref, got_ref, out_ref):
@@ -326,10 +301,10 @@
         ref[head, j : j + 1, :] = row
 
 
-def prev_parts(peers, direct_keys, relayed_keys, outer_values, pair_ref, cols):
+def prev_parts(peers, direct_keys, relayed_keys, outer_values, pair_keys, pair_values, cols):
     even = (lax.axis_index("tm") & 1) == 0
     keys = jnp.where(through_relay(1, 1, peers), relayed_keys[:, cols], direct_keys[:, cols])
-    parts = zip((keys, outer_values[:, cols]), joined_parts(pair_ref, cols))
+    parts = zip((keys, outer_values[:, cols]), (pair_keys[:, cols], pair_values[:, cols]))
     return tuple(jnp.where(even, outer, pair) for outer, pair in parts)
 
 
@@ -340,8 +315,10 @@
     direct_keys,
     relayed_keys,
     outer_values,
-    pair_ref,
-    own_ref,
+    pair_keys,
+    pair_values,
+    key_ref,
+    value_ref,
     part_ref,
     queries_out,
     cotangent_out,
@@ -354,7 +331,8 @@
     def products(head):
         cols = head_cols(head)
         query, cotangent = joined_parts(queries_ref, cols)
-        pieces = ((PREV, prev_parts(peers, direct_keys, relayed_keys, outer_values, pair_ref, cols)), (OWN, joined_parts(own_ref, cols)))
+        prev = prev_parts(peers, direct_keys, relayed_keys, outer_values, pair_keys, pair_values, cols)
+        pieces = ((PREV, prev), (OWN, (key_ref[:, cols], value_ref[:, cols])))
         return [
             (logits_of(keys, query, rows_ref, head, piece), dot(values, cotangent, 1, 1))
             for piece, (keys, values) in pieces
@@ -434,7 +412,8 @@
     outer_queries,
     direct_cotangent,
     relayed_cotangent,
-    own_ref,
+    key_ref,
+    value_ref,
     term_ref,
     sum_ref,
 ):
@@ -450,7 +429,7 @@
 
     def products(head):
         query, cotangent = operands(head)
-        keys, values = joined_parts(own_ref, head_cols(head))
+        keys, values = key_ref[:, head_cols(head)], value_ref[:, head_cols(head)]
         return logits_of(keys, query, rows_ref, head, NEXT), dot(values, cotangent, 1, 1)
 
     ahead = products(0)
@@ -478,12 +457,14 @@
     ]
 
 
-def own_kernel(rows_ref, part_ref, queries_ref, own_ref, own_mem, other_mem, term_ref, stats_ref):
+def own_kernel(rows_ref, part_ref, queries_ref, key_ref, value_ref, own_mem, other_mem, term_ref, stats_ref):
     heads = queries_ref.shape[1] // DEPTH
 
     def products(head):
-        query, cotangent = joined_parts(queries_ref, head_cols(head))
-        pieces = ((OWN, joined_parts(own_ref, head_cols(head))), (MEMORY, memory_parts(own_mem, other_mem, head)))
+        cols = head_cols(head)
+        query, cotangent = joined_parts(queries_ref, cols)
+        own = key_ref[:, cols], value_ref[:, cols]
+        pieces = ((OWN, own), (MEMORY, memory_parts(own_mem, other_mem, head)))
         return [
             (logits_of(keys, query, rows_ref, head, piece), dot(values, cotangent, 1, 1))
             for piece, (keys, values) in pieces
@@ -513,8 +494,10 @@
     direct_keys,
     relayed_keys,
     outer_values,
-    pair_ref,
-    own_ref,
+    pair_keys,
+    pair_values,
+    key_ref,
+    value_ref,
     own_mem,
     other_mem,
     attended_ref,
@@ -526,8 +509,8 @@
 
     def pieces(head):
         cols = head_cols(head)
-        prev = prev_parts(peers, direct_keys, relayed_keys, outer_values, pair_ref, cols)
-        return (PREV, prev), (OWN, joined_parts(own_ref, cols)), (MEMORY, memory_parts(own_mem, other_mem, head))
+        prev = prev_parts(peers, direct_keys, relayed_keys, outer_values, pair_keys, pair_values, cols)
+        return (PREV, prev), (OWN, (key_ref[:, cols], value_ref[:, cols])), (MEMORY, memory_parts(own_mem, other_mem, head))
 
     def products(head):
         query, cotangent = joined_parts(queries_ref, head_cols(head))
@@ -613,42 +596,40 @@
     bank_frames = bank_frames.reshape(1, slots)
     last_bits = turns[-1]
 
-    def join(kernel, rows, arrays, scratch, name, after=()):
+    def load(outs, arrays, name, after=()):
         def run(*refs):
-            kernel(*refs[: len(arrays)], *refs[len(arrays) + len(after) :])
+            load_kernel(len(arrays), *refs[: len(arrays)], *refs[len(arrays) + len(after) :])
 
         return pl.pallas_call(
             run,
-            out_shape=shape(BF16, rows, width),
+            out_shape=outs,
             in_specs=[pl.BlockSpec(memory_space=pltpu.HBM)] * len(arrays) + [ANY] * len(after),
-            out_specs=VMEM,
-            scratch_shapes=[*scratch, pltpu.SemaphoreType.DMA((len(arrays),))],
+            out_specs=[VMEM] * len(outs),
+            scratch_shapes=[pltpu.SemaphoreType.DMA((len(arrays),))],
             compiler_params=pltpu.CompilerParams(vmem_limit_bytes=VMEM_LIMIT),
             name=name,
         )(*(pltpu.with_memory_space_constraint(array, pltpu.HBM) for array in arrays), *after)
 
-    joined = join(
-        join_kernel,
-        2 * row_count + TAIL,
-        [memory_index, key_states, value_states],
-        [pltpu.VMEM(memory_index.shape, jnp.int32)],
-        "join",
-    )
     half_width = width // 2
-    direct_keys = shift_first(key_states, 1, 1, peers)
-    pair = swap(joined, 1, 1, peers)
+    pair = [swap(array, 1, 1, peers) for array in (key_states, value_states)]
+    pair_index = swap(memory_index, 1, 1, peers)
+    rows_shape = shape(BF16, row_count, width)
+    keys, values, bank = load(
+        [rows_shape, rows_shape, shape(jnp.int32, 1, slots)], [key_states, value_states, bank_frames], "load"
+    )
+    direct_keys = shift_first(keys, 1, 1, peers)
     held = shape(BF16, slots - 1, 2, frame_len, half_width)
     sums = shape(F32, slots - 1, 2, frame_len, half_width)
-    (mine,) = call(functools.partial(split_kernel, peers), [held], [bank_frames, joined, pair], name="split")
-    queries = join(join_queries_kernel, 2 * row_count, [query_states, grad_out], [], "join_queries", after=[mine])
+    (mine,) = call(functools.partial(split_kernel, peers), [held], [bank, keys, values, *pair], name="split")
+    (queries,) = load([shape(BF16, 2 * row_count, width)], [query_states, grad_out], "load_queries", after=[mine])
     pair_queries = swap(queries, 1, 1, peers)
 
     bias_rows = -(-(5 * FR_DEV) // 8) * 8
     rows, codes, values_out, keys_out = call(
         functools.partial(plan_kernel, peers, last_bits),
         [shape(F32, heads, bias_rows, row_count), shape(jnp.int32, 8, 128)] + [shape(BF16, row_count, width)] * 2,
-        [pair, joined, direct_keys],
-        scalars=[bank_frames, memory_index, camera_pose, pose_bias],
+        [values, direct_keys],
+        scalars=[bank_frames, memory_index, pair_index, camera_pose, pose_bias],
         flops=HIDING * piece_flops,
         name="plan",
     )
@@ -659,7 +640,7 @@
         if step + 1 < len(turns):
             kernel = functools.partial(step_kernel, peers, even_done, odd_done)
             after = [codes, pair_queries]
-            (mine,) = call(kernel, [held], [bank_frames, mine, got], after=after, name="step")
+            (mine,) = call(kernel, [held], [bank, mine, got], after=after, name="step")
         even_done |= even_bit
         odd_done |= odd_bit
 
@@ -667,7 +648,7 @@
     part, queries_out, cotangent_out = call(
         functools.partial(stats_kernel, peers),
         [stats] + [shape(BF16, row_count, width)] * 2,
-        [rows, queries, *outer, pair, joined],
+        [rows, queries, *outer, *pair, keys, values],
         flops=HIDING * piece_flops,
         name="stats",
     )
@@ -688,7 +669,7 @@
     own_terms, stats_all = call(
         own_kernel,
         [pair_sums, stats],
-        [rows, part, queries, joined, own_mem, other_mem],
+        [rows, part, queries, keys, values, own_mem, other_mem],
         after=[send],
         flops=HIDING * piece_flops,
         name="own",
@@ -701,7 +682,7 @@
     (own,) = call(
         functools.partial(next_kernel, peers),
         [pair_sums],
-        [rows, next_stats, pair_queries, next_queries, direct_cotangent, relayed_cotangent, joined, own_terms],
+        [rows, next_stats, pair_queries, next_queries, direct_cotangent, relayed_cotangent, keys, values, own_terms],
         flops=HIDING * piece_flops,
         name="next",
     )
@@ -713,7 +694,7 @@
     attended, grad_query, mark = call(
         functools.partial(attend_kernel, peers),
         [shape(BF16, row_count, width)] * 2 + [shape(F32, 8, 128)],
-        [rows, stats_all, queries, *outer, pair, joined, own_mem, other_mem],
+        [rows, stats_all, queries, *outer, *pair, keys, values, own_mem, other_mem],
         after=[send],
         flops=HIDING * piece_flops,
         name="attend",

time: 60.2 us -> 60.6 us (level)
  starting transfers between devices: 27.7 us -> 31 us
  waiting for transfers between devices: 13.9 us -> 11.4 us
    ppermute x9 -> x11, waiting for transfers between devices: 13.9 us -> 11.4 us  [swap(): lax.ppermute(block, 'tm', [(i, i ^ (odd_bit if i & 1 else even_bit)) for...]
    ppermute x9 -> x11, starting transfers between devices: 18.6 us -> 20.8 us  [swap(): lax.ppermute(block, 'tm', [(i, i ^ (odd_bit if i & 1 else even_bit)) for...]
    ppermute x2, starting transfers between devices: 4.48 us -> 5.55 us  [shift_second(): return lax.ppermute(block, 'tm', pairs) if pairs else block]
  transfers between devices with their start and end apart: 16 -> 18, of which waited for: 5 -> 4; matrix products, arithmetic and copies ran while one was open for 0% -> 0% of each run, Pallas kernels for 25% -> 26%
where the time goes in v15:
time: 60.6 us; the launch traced here: 60.3 us
  starting transfers between devices  31 us (51%)
  Pallas kernels  17 us (28%)
  waiting for transfers between devices  11.4 us (19%)
  between operations  0.88 us (1%)
    ppermute x11, starting transfers between devices, swap(): lax.ppermute(block, 'tm', [(i, i ^ (odd_bit if i & 1 else even_bit)) for...  20.8 us
    pallas_call x13, Pallas kernels, call(): pl.pallas_call(run, out_shape=outs, in_specs=[SMEM] * len(scalars) + [VME...  14.8 us
    ppermute x11, waiting for transfers between devices, swap(): lax.ppermute(block, 'tm', [(i, i ^ (odd_bit if i & 1 else even_bit)) for...  11.4 us
    ppermute x2, starting transfers between devices, shift_second(): return lax.ppermute(block, 'tm', pairs) if pairs else block  5.55 us
    pallas_call x2, Pallas kernels, load(): pl.pallas_call(run, out_shape=outs, in_specs=[pl.BlockSpec(memory_space=p...  2.27 us
    ppermute x2, starting transfers between devices, shift_first(): lax.ppermute(block, 'tm', [(i, relays.get((i, j), j)) for i, j in pairs])  1.98 us
    ppermute x2, starting transfers between devices, shift(): return lax.ppermute(block, 'tm', pairs)  1.36 us
    ppermute x1, starting transfers between devices, body(): lax.ppermute(stats_all, 'tm', [(i, i - 1) for i in range(1, peers)])  1.29 us
  transfers between devices with their start and end apart: 18, of which 4 were waited for; matrix products, arithmetic and copies ran while one was open for 0% of the time, Pallas kernels for 26%

profile of v15, /device:TPU:0, one launch (start us, length us, event | category | flops | bytes accessed | tf_op | source)
XLA Modules:
  0.0 60.3 jit_solution(8553791902024779064)
XLA Ops:
  0.6 0.5 collective-permute-start.2
  1.1 0.1 collective-permute-start.3
  1.2 1.1 %load.1 = (bf16[256,768]{1,0:T(8,128)(2,1)S(1)}, bf16[256,768]{1,0:T(8,128)(2,1)S(1)}, s32[1,4]{1,0:T(1,128)S(1)}) custom-call(bf16[256,768]{1,0:T(8,128)(2,1)} %refs_0_.2, bf16[256,768]{1,0:T(8,128)(2,1)} %refs_1_.3, s32[1,4]{1,0:T(1,128)} %bitcast.1), custom_call_target="tpu_custom_call" | custom-call | tf_op jit(solution)/shard_map/load/pallas_call | solution.py:603
  2.4 0.7 %collective-permute-start.1 = (bf16[256,768]{1,0:T(8,128)(2,1)S(1)}, bf16[256,768]{1,0:T(8,128)(2,1)S(1)}, u32[]{:S(2)}, u32[]{:S(2)}) collective-permute-start(bf16[256,768]{1,0:T(8,128)(2,1)S(1)} %get-tuple-element.30.refs_1_.refs_7_.refs_3_.refs_8_.refs_6_), channel_id=1, source_target_pairs={{1,2},{3,7},{5,6},{9,10},{11,15},{13,14},{17,18},{19,23},{21,22},{... | collective-permute-start | bytes 1179656 | tf_op jit(solution)/shard_map/ppermute | solution.py:65
  3.1 4.3 %collective-permute-start = (s32[1,2]{1,0:T(1,128)}, s32[1,2]{1,0:T(1,128)S(1)}, u32[]{:S(2)}, u32[]{:S(2)}) collective-permute-start(s32[1,2]{1,0:T(1,128)} %refs_1_.4), channel_id=1, source_target_pairs={{0,1},{1,0},{2,3},{3,2},{4,5},{5,4},{6,7},{7,6},{8,9},{9,8},{10,11... | collective-permute-start | bytes 32 | tf_op jit(solution)/shard_map/ppermute | solution.py:49
  7.4 0.0 collective-permute-done.2.refs_3_.refs_5_.refs_6_
  7.4 0.3 split.1.refs_2_.refs_1_
  7.8 0.0 copy-start
  7.8 0.0 copy-start.1
  7.8 0.0 copy-start.2
  7.8 0.0 copy-start.3
  7.8 1.3 %collective-permute-start.6 = (bf16[3,2,128,384]{3,2,1,0:T(8,128)(2,1)S(1)}, bf16[3,2,128,384]{3,2,1,0:T(8,128)(2,1)S(1)}, u32[]{:S(2)}, u32[]{:S(2)}) collective-permute-start(bf16[3,2,128,384]{3,2,1,0:T(8,128)(2,1)S(1)} %split.1.refs_2_.refs_1_), channel_id=1, source_target_pairs={{0,2},{1,5},{2,0},{3,7},{4,6},{5,1},{6,4},{7,3},{8,10},{9,13},{10,... | collective-permute-start | bytes 1769480 | tf_op jit(solution)/shard_map/ppermute | solution.py:49
  9.1 1.1 %load_queries.1.refs_1_.refs_4_.refs_2_ = bf16[512,768]{1,0:T(8,128)(2,1)S(1)} custom-call(bf16[256,768]{1,0:T(8,128)(2,1)} %refs_0_.3, bf16[256,768]{1,0:T(8,128)(2,1)} %refs_1_.5, bf16[3,2,128,384]{3,2,1,0:T(8,128)(2,1)S(1)} %split.1.refs_2_.refs_1_), custom_call_target="tpu_custom_call" | custom-call | tf_op jit(solution)/shard_map/load_queries/pallas_call | solution.py:603
  10.2 0.1 collective-permute-start.7
  10.3 0.0 collective-permute-done.refs_2_
  10.4 0.0 collective-permute-done.1.refs_6_.refs_2_.refs_3_
  10.4 1.7 %plan.1 = (f32[6,16,256]{2,1,0:T(8,128)S(1)}, s32[8,128]{1,0:T(8,128)S(1)}, bf16[256,768]{1,0:T(8,128)(2,1)S(1)}, bf16[256,768]{1,0:T(8,128)(2,1)S(1)}) custom-call(s32[1,4]{1,0:T(1,128)S(1)} %bitcast.2, s32[1,2]{1,0:T(1,128)S(1)} %copy-done.2, s32[1,2]{1,0:T(1,128)S(1)} %collective-permute-done.refs_2_, s32[16]{0:T(128)S(1)} %copy-done.3, ...), custom_call_target="tpu_custom_call" | custom-call | flops 20132659200 | tf_op jit(solution)/shard_map/plan/pallas_call | solution.py:37
  12.1 0.7 %collective-permute-start.4 = (bf16[256,768]{1,0:T(8,128)(2,1)S(1)}, bf16[256,768]{1,0:T(8,128)(2,1)S(1)}, u32[]{:S(2)}, u32[]{:S(2)}) collective-permute-start(bf16[256,768]{1,0:T(8,128)(2,1)S(1)} %get-tuple-element.33), channel_id=1, source_target_pairs={{7,4},{15,12},{23,20},{31,28}} | collective-permute-start | bytes 1179656 | tf_op jit(solution)/shard_map/ppermute | solution.py:70
  12.7 0.7 %collective-permute-start.5 = (bf16[256,768]{1,0:T(8,128)(2,1)S(1)}, bf16[256,768]{1,0:T(8,128)(2,1)S(1)}, u32[]{:S(2)}, u32[]{:S(2)}) collective-permute-start(bf16[256,768]{1,0:T(8,128)(2,1)S(1)} %get-tuple-element.34), channel_id=1, source_target_pairs={{1,2},{3,4},{5,6},{9,10},{11,12},{13,14},{17,18},{19,20},{21,22},{... | collective-permute-start | bytes 1179656 | tf_op jit(solution)/shard_map/ppermute | solution.py:54
  13.4 4.8 %collective-permute-done.6.refs_2_ = bf16[3,2,128,384]{3,2,1,0:T(8,128)(2,1)S(1)} collective-permute-done((bf16[3,2,128,384]{3,2,1,0:T(8,128)(2,1)S(1)}, bf16[3,2,128,384]{3,2,1,0:T(8,128)(2,1)S(1)}, u32[]{:S(2)}, u32[]{:S(2)}) %collective-permute-start.6) | collective-permute-done | bytes 589856 | tf_op jit(solution)/shard_map/ppermute | solution.py:49
  18.2 0.3 step.1.refs_1_
  18.5 1.6 %collective-permute-start.8 = (bf16[3,2,128,384]{3,2,1,0:T(8,128)(2,1)S(1)}, bf16[3,2,128,384]{3,2,1,0:T(8,128)(2,1)S(1)}, u32[]{:S(2)}, u32[]{:S(2)}) collective-permute-start(bf16[3,2,128,384]{3,2,1,0:T(8,128)(2,1)S(1)} %step.1.refs_1_), channel_id=1, source_target_pairs={{0,4},{1,3},{2,6},{3,1},{4,0},{5,7},{6,2},{7,5},{8,12},{9,11},{10,... | collective-permute-start | bytes 1769480 | tf_op jit(solution)/shard_map/ppermute | solution.py:49
  20.1 0.0 collective-permute-done.4.refs_3_.refs_4_
  20.1 0.0 collective-permute-done.5.refs_4_.refs_5_
  20.1 1.5 %stats.1 = (f32[6,8,256]{2,1,0:T(8,128)S(1)}, bf16[256,768]{1,0:T(8,128)(2,1)S(1)}, bf16[256,768]{1,0:T(8,128)(2,1)S(1)}) custom-call(f32[6,16,256]{2,1,0:T(8,128)S(1)} %get-tuple-element.31.refs_0_.refs_1_, bf16[512,768]{1,0:T(8,128)(2,1)S(1)} %load_queries.1.refs_1_.refs_4_.refs_2_, bf16[256,768]{1,0:T(8,128)(2,1)S(1)} %collective-permute-done.1.refs_6_.refs_2_.refs_3_, ...), custom_call_target="tpu_custom_call" | custom-call | flops 20132659200 | tf_op jit(solution)/shard_map/stats/pallas_call | solution.py:37
  21.6 5.1 %collective-permute-start.10 = (f32[6,8,256]{2,1,0:T(8,128)S(1)}, f32[6,8,256]{2,1,0:T(8,128)S(1)}, u32[]{:S(2)}, u32[]{:S(2)}) collective-permute-start(f32[6,8,256]{2,1,0:T(8,128)S(1)} %get-tuple-element.35.refs_2_.refs_1_), channel_id=1, source_target_pairs={{0,1},{1,0},{2,3},{3,2},{4,5},{5,4},{6,7},{7,6},{8,9},{9,8},{10,11... | collective-permute-start | bytes 147464 | tf_op jit(solution)/shard_map/ppermute | solution.py:49
  26.7 0.7 %collective-permute-start.12 = (bf16[256,768]{1,0:T(8,128)(2,1)S(1)}, bf16[256,768]{1,0:T(8,128)(2,1)S(1)}, u32[]{:S(2)}, u32[]{:S(2)}) collective-permute-start(bf16[256,768]{1,0:T(8,128)(2,1)S(1)} %get-tuple-element.43), channel_id=1, source_target_pairs={{2,1},{4,3},{6,5},{10,9},{12,11},{14,13},{18,17},{20,19},{22,21},{... | collective-permute-start | bytes 1179656 | tf_op jit(solution)/shard_map/ppermute | solution.py:54
  27.4 1.3 %collective-permute-start.14 = (bf16[256,768]{1,0:T(8,128)(2,1)S(1)}, bf16[256,768]{1,0:T(8,128)(2,1)S(1)}, u32[]{:S(2)}, u32[]{:S(2)}) collective-permute-start(bf16[256,768]{1,0:T(8,128)(2,1)S(1)} %get-tuple-element.47), channel_id=1, source_target_pairs={{2,1},{4,0},{6,5},{10,9},{12,8},{14,13},{18,17},{20,16},{22,21},{2... | collective-permute-start | bytes 1179656 | tf_op jit(solution)/shard_map/ppermute | solution.py:65
  28.7 0.0 collective-permute-done.8.refs_2_
  28.7 0.3 pick.1
  29.0 2.8 %collective-permute-start.9 = (bf16[2,2,128,384]{3,2,1,0:T(8,128)(2,1)S(1)}, bf16[2,2,128,384]{3,2,1,0:T(8,128)(2,1)S(1)}, u32[]{:S(2)}, u32[]{:S(2)}) collective-permute-start(bf16[2,2,128,384]{3,2,1,0:T(8,128)(2,1)S(1)} %get-tuple-element.38.refs_7_), channel_id=1, source_target_pairs={{0,1},{1,0},{2,3},{3,2},{4,5},{5,4},{6,7},{7,6},{8,9},{9,8},{10,11... | collective-permute-start | bytes 1179656 | tf_op jit(solution)/shard_map/ppermute | solution.py:49
  31.9 1.9 %memory.1 = (f32[4,2,128,384]{3,2,1,0:T(8,128)S(1)}, bf16[3,2,128,384]{3,2,1,0:T(8,128)(2,1)S(1)}) custom-call(s32[8,128]{1,0:T(8,128)S(1)} %get-tuple-element.36.refs_3_.refs_0_, f32[6,16,256]{2,1,0:T(8,128)S(1)} %get-tuple-element.31.refs_0_.refs_1_, f32[6,8,256]{2,1,0:T(8,128)S(1)} %get-tuple-element.35.refs_2_.refs_1_, ...), custom_call_target="tpu_custom_call" | custom-call | flops 20132659200 | tf_op jit(solution)/shard_map/memory/pallas_call | solution.py:37
  33.8 3.2 %collective-permute-start.11 = (bf16[3,2,128,384]{3,2,1,0:T(8,128)(2,1)S(1)}, bf16[3,2,128,384]{3,2,1,0:T(8,128)(2,1)S(1)}, u32[]{:S(2)}, u32[]{:S(2)}) collective-permute-start(bf16[3,2,128,384]{3,2,1,0:T(8,128)(2,1)S(1)} %get-tuple-element.39.refs_7_), channel_id=1, source_target_pairs={{0,4},{1,3},{2,6},{3,1},{4,0},{5,7},{6,2},{7,5},{8,12},{9,11},{10,... | collective-permute-start | bytes 1769480 | tf_op jit(solution)/shard_map/ppermute | solution.py:49
  37.0 2.4 %own.1 = (f32[2,256,768]{2,1,0:T(8,128)S(1)}, f32[6,8,256]{2,1,0:T(8,128)S(1)}) custom-call(f32[6,16,256]{2,1,0:T(8,128)S(1)} %get-tuple-element.31.refs_0_.refs_1_, f32[6,8,256]{2,1,0:T(8,128)S(1)} %get-tuple-element.35.refs_2_.refs_1_, bf16[512,768]{1,0:T(8,128)(2,1)S(1)} %load_queries.1.refs_1_.refs_4_.refs_2_, ...), custom_call_target="tpu_custom_call" | custom-call | flops 20132659200 | tf_op jit(solution)/shard_map/own/pallas_call | solution.py:37
  39.4 1.3 %collective-permute-start.13 = (f32[6,8,256]{2,1,0:T(8,128)S(1)}, f32[6,8,256]{2,1,0:T(8,128)S(1)}, u32[]{:S(2)}, u32[]{:S(2)}) collective-permute-start(f32[6,8,256]{2,1,0:T(8,128)S(1)} %get-tuple-element.40.refs_1_), channel_id=1, source_target_pairs={{1,0},{2,1},{3,2},{4,3},{5,4},{6,5},{7,6},{9,8},{10,9},{11,10},{12... | collective-permute-start | bytes 147464 | tf_op jit(solution)/shard_map/ppermute | solution.py:677
  40.7 0.0 collective-permute-done.14.refs_0_.refs_4_
  40.7 4.9 %collective-permute-start.15 = (bf16[256,768]{1,0:T(8,128)(2,1)S(1)}, bf16[256,768]{1,0:T(8,128)(2,1)S(1)}, u32[]{:S(2)}, u32[]{:S(2)}) collective-permute-start(bf16[256,768]{1,0:T(8,128)(2,1)S(1)} %pass_on.1), channel_id=1, source_target_pairs={{0,3},{8,11},{16,19},{24,27}} | collective-permute-start | bytes 1179656 | tf_op jit(solution)/shard_map/ppermute | solution.py:70
  45.6 0.0 collective-permute-done.12.refs_3_
  45.6 0.4 collective-permute-done.11.refs_1_
  46.0 0.2 add.1
  46.1 1.7 %collective-permute-start.16 = (bf16[3,2,128,384]{3,2,1,0:T(8,128)(2,1)S(1)}, bf16[3,2,128,384]{3,2,1,0:T(8,128)(2,1)S(1)}, u32[]{:S(2)}, u32[]{:S(2)}) collective-permute-start(bf16[3,2,128,384]{3,2,1,0:T(8,128)(2,1)S(1)} %get-tuple-element.44.refs_12_), channel_id=1, source_target_pairs={{0,2},{1,5},{2,0},{3,7},{4,6},{5,1},{6,4},{7,3},{8,10},{9,13},{10,... | collective-permute-start | bytes 1769480 | tf_op jit(solution)/shard_map/ppermute | solution.py:49
  47.8 3.6 %attend.1 = (bf16[256,768]{1,0:T(8,128)(2,1)}, bf16[256,768]{1,0:T(8,128)(2,1)}, f32[8,128]{1,0:T(8,128)S(1)}) custom-call(f32[6,16,256]{2,1,0:T(8,128)S(1)} %get-tuple-element.31.refs_0_.refs_1_, f32[6,8,256]{2,1,0:T(8,128)S(1)} %get-tuple-element.40.refs_1_, bf16[512,768]{1,0:T(8,128)(2,1)S(1)} %load_queries.1.refs_1_.refs_4_.refs_2_, ...), custom_call_target="tpu_custom_call" | custom-call | flops 20132659200 | tf_op jit(solution)/shard_map/attend/pallas_call | solution.py:37
  51.5 1.2 %next.1.refs_3_.refs_0_ = f32[2,256,768]{2,1,0:T(8,128)S(1)} custom-call(f32[6,16,256]{2,1,0:T(8,128)S(1)} %get-tuple-element.31.refs_0_.refs_1_, f32[6,8,256]{2,1,0:T(8,128)S(1)} %collective-permute-done.13.refs_1_, bf16[512,768]{1,0:T(8,128)(2,1)S(1)} %collective-permute-done.7.refs_4_.refs_5_.refs_2_, ...), custom_call_target="tpu_custom_call" | custom-call | flops 20132659200 | tf_op jit(solution)/shard_map/next/pallas_call | solution.py:37
  52.7 4.5 %collective-permute-done.16.refs_2_ = bf16[3,2,128,384]{3,2,1,0:T(8,128)(2,1)S(1)} collective-permute-done((bf16[3,2,128,384]{3,2,1,0:T(8,128)(2,1)S(1)}, bf16[3,2,128,384]{3,2,1,0:T(8,128)(2,1)S(1)}, u32[]{:S(2)}, u32[]{:S(2)}) %collective-permute-start.16) | collective-permute-done | bytes 589856 | tf_op jit(solution)/shard_map/ppermute | solution.py:49
  57.2 0.3 owned.1
  57.5 0.1 collective-permute-start.17
  57.6 1.7 %collective-permute-done.17.refs_2_ = bf16[2,2,128,384]{3,2,1,0:T(8,128)(2,1)S(1)} collective-permute-done((bf16[2,2,128,384]{3,2,1,0:T(8,128)(2,1)S(1)}, bf16[2,2,128,384]{3,2,1,0:T(8,128)(2,1)S(1)}, u32[]{:S(2)}, u32[]{:S(2)}) %collective-permute-start.17) | collective-permute-done | bytes 393248 | tf_op jit(solution)/shard_map/ppermute | solution.py:49
  59.3 1.0 %final.1 = (bf16[256,768]{1,0:T(8,128)(2,1)}, bf16[256,768]{1,0:T(8,128)(2,1)}) custom-call(f32[2,256,768]{2,1,0:T(8,128)S(1)} %next.1.refs_3_.refs_0_, f32[2,2,128,384]{3,2,1,0:T(8,128)S(1)} %get-tuple-element.50.refs_1_, bf16[2,2,128,384]{3,2,1,0:T(8,128)(2,1)S(1)} %collective-permute-done.17.refs_2_), custom_call_target="tpu_custom_call" | custom-call | tf_op jit(solution)/shard_map/final/pallas_call | solution.py:37
  (11 shorter events, 0.1 us)
Async XLA Ops:
  0.6 6.8 %collective-permute-start.2 = (bf16[256,768]{1,0:T(8,128)(2,1)}, bf16[256,768]{1,0:T(8,128)(2,1)S(1)}, u32[]{:S(2)}, u32[]{:S(2)}) collective-permute-start(bf16[256,768]{1,0:T(8,128)(2,1)} %refs_0_.2), channel_id=1, source_target_pairs={{0,1},{1,0},{2,3},{3,2},{4,5},{5,4},{6,7},{7,6},{8,9},{9,8},{10,11... | collective-permute-start | bytes 1179656 | tf_op jit(solution)/shard_map/ppermute | solution.py:49
  1.1 6.3 %collective-permute-start.3 = (bf16[256,768]{1,0:T(8,128)(2,1)}, bf16[256,768]{1,0:T(8,128)(2,1)S(1)}, u32[]{:S(2)}, u32[]{:S(2)}) collective-permute-start(bf16[256,768]{1,0:T(8,128)(2,1)} %refs_1_.3), channel_id=1, source_target_pairs={{0,1},{1,0},{2,3},{3,2},{4,5},{5,4},{6,7},{7,6},{8,9},{9,8},{10,11... | collective-permute-start | bytes 1179656 | tf_op jit(solution)/shard_map/ppermute | solution.py:49
  2.4 8.0 %collective-permute-start.1 = (bf16[256,768]{1,0:T(8,128)(2,1)S(1)}, bf16[256,768]{1,0:T(8,128)(2,1)S(1)}, u32[]{:S(2)}, u32[]{:S(2)}) collective-permute-start(bf16[256,768]{1,0:T(8,128)(2,1)S(1)} %get-tuple-element.30.refs_1_.refs_7_.refs_3_.refs_8_.refs_6_), channel_id=1, source_target_pairs={{1,2},{3,7},{5,6},{9,10},{11,15},{13,14},{17,18},{19,23},{21,22},{... | collective-permute-start | bytes 1179656 | tf_op jit(solution)/shard_map/ppermute | solution.py:65
  3.1 7.3 %collective-permute-start = (s32[1,2]{1,0:T(1,128)}, s32[1,2]{1,0:T(1,128)S(1)}, u32[]{:S(2)}, u32[]{:S(2)}) collective-permute-start(s32[1,2]{1,0:T(1,128)} %refs_1_.4), channel_id=1, source_target_pairs={{0,1},{1,0},{2,3},{3,2},{4,5},{5,4},{6,7},{7,6},{8,9},{9,8},{10,11... | collective-permute-start | bytes 32 | tf_op jit(solution)/shard_map/ppermute | solution.py:49
  7.8 2.6 %copy-start = (s32[4]{0:T(128)S(1)}, s32[4]{0:T(128)}, u32[]{:S(2)}) copy-start(s32[4]{0:T(128)} %param.15) | copy-start | bytes 52
  7.8 2.6 %copy-start.1 = (f32[6,16,16]{2,1,0:T(8,128)S(1)}, f32[6,16,16]{2,1,0:T(8,128)}, u32[]{:S(2)}) copy-start(f32[6,16,16]{2,1,0:T(8,128)} %refs_4_.1) | copy-start | bytes 18436
  7.8 2.6 %copy-start.2 = (s32[1,2]{1,0:T(1,128)S(1)}, s32[1,2]{1,0:T(1,128)}, u32[]{:S(2)}) copy-start(s32[1,2]{1,0:T(1,128)} %refs_1_.4) | copy-start | bytes 28
  7.8 2.6 %copy-start.3 = (s32[16]{0:T(128)S(1)}, s32[16]{0:T(128)}, u32[]{:S(2)}) copy-start(s32[16]{0:T(128)} %refs_3_.1) | copy-start | bytes 196
  7.8 10.4 %collective-permute-start.6 = (bf16[3,2,128,384]{3,2,1,0:T(8,128)(2,1)S(1)}, bf16[3,2,128,384]{3,2,1,0:T(8,128)(2,1)S(1)}, u32[]{:S(2)}, u32[]{:S(2)}) collective-permute-start(bf16[3,2,128,384]{3,2,1,0:T(8,128)(2,1)S(1)} %split.1.refs_2_.refs_1_), channel_id=1, source_target_pairs={{0,2},{1,5},{2,0},{3,7},{4,6},{5,1},{6,4},{7,3},{8,10},{9,13},{10,... | collective-permute-start | bytes 1769480 | tf_op jit(solution)/shard_map/ppermute | solution.py:49
  10.2 8.0 %collective-permute-start.7 = (bf16[512,768]{1,0:T(8,128)(2,1)S(1)}, bf16[512,768]{1,0:T(8,128)(2,1)S(1)}, u32[]{:S(2)}, u32[]{:S(2)}) collective-permute-start(bf16[512,768]{1,0:T(8,128)(2,1)S(1)} %load_queries.1.refs_1_.refs_4_.refs_2_), channel_id=1, source_target_pairs={{0,1},{1,0},{2,3},{3,2},{4,5},{5,4},{6,7},{7,6},{8,9},{9,8},{10,11... | collective-permute-start | bytes 2359304 | tf_op jit(solution)/shard_map/ppermute | solution.py:49
  12.1 8.1 %collective-permute-start.4 = (bf16[256,768]{1,0:T(8,128)(2,1)S(1)}, bf16[256,768]{1,0:T(8,128)(2,1)S(1)}, u32[]{:S(2)}, u32[]{:S(2)}) collective-permute-start(bf16[256,768]{1,0:T(8,128)(2,1)S(1)} %get-tuple-element.33), channel_id=1, source_target_pairs={{7,4},{15,12},{23,20},{31,28}} | collective-permute-start | bytes 1179656 | tf_op jit(solution)/shard_map/ppermute | solution.py:70
  12.7 7.4 %collective-permute-start.5 = (bf16[256,768]{1,0:T(8,128)(2,1)S(1)}, bf16[256,768]{1,0:T(8,128)(2,1)S(1)}, u32[]{:S(2)}, u32[]{:S(2)}) collective-permute-start(bf16[256,768]{1,0:T(8,128)(2,1)S(1)} %get-tuple-element.34), channel_id=1, source_target_pairs={{1,2},{3,4},{5,6},{9,10},{11,12},{13,14},{17,18},{19,20},{21,22},{... | collective-permute-start | bytes 1179656 | tf_op jit(solution)/shard_map/ppermute | solution.py:54
  18.5 10.2 %collective-permute-start.8 = (bf16[3,2,128,384]{3,2,1,0:T(8,128)(2,1)S(1)}, bf16[3,2,128,384]{3,2,1,0:T(8,128)(2,1)S(1)}, u32[]{:S(2)}, u32[]{:S(2)}) collective-permute-start(bf16[3,2,128,384]{3,2,1,0:T(8,128)(2,1)S(1)} %step.1.refs_1_), channel_id=1, source_target_pairs={{0,4},{1,3},{2,6},{3,1},{4,0},{5,7},{6,2},{7,5},{8,12},{9,11},{10,... | collective-permute-start | bytes 1769480 | tf_op jit(solution)/shard_map/ppermute | solution.py:49
  21.6 10.2 %collective-permute-start.10 = (f32[6,8,256]{2,1,0:T(8,128)S(1)}, f32[6,8,256]{2,1,0:T(8,128)S(1)}, u32[]{:S(2)}, u32[]{:S(2)}) collective-permute-start(f32[6,8,256]{2,1,0:T(8,128)S(1)} %get-tuple-element.35.refs_2_.refs_1_), channel_id=1, source_target_pairs={{0,1},{1,0},{2,3},{3,2},{4,5},{5,4},{6,7},{7,6},{8,9},{9,8},{10,11... | collective-permute-start | bytes 147464 | tf_op jit(solution)/shard_map/ppermute | solution.py:49
  26.7 18.9 %collective-permute-start.12 = (bf16[256,768]{1,0:T(8,128)(2,1)S(1)}, bf16[256,768]{1,0:T(8,128)(2,1)S(1)}, u32[]{:S(2)}, u32[]{:S(2)}) collective-permute-start(bf16[256,768]{1,0:T(8,128)(2,1)S(1)} %get-tuple-element.43), channel_id=1, source_target_pairs={{2,1},{4,3},{6,5},{10,9},{12,11},{14,13},{18,17},{20,19},{22,21},{... | collective-permute-start | bytes 1179656 | tf_op jit(solution)/shard_map/ppermute | solution.py:54
  27.4 13.3 %collective-permute-start.14 = (bf16[256,768]{1,0:T(8,128)(2,1)S(1)}, bf16[256,768]{1,0:T(8,128)(2,1)S(1)}, u32[]{:S(2)}, u32[]{:S(2)}) collective-permute-start(bf16[256,768]{1,0:T(8,128)(2,1)S(1)} %get-tuple-element.47), channel_id=1, source_target_pairs={{2,1},{4,0},{6,5},{10,9},{12,8},{14,13},{18,17},{20,16},{22,21},{2... | collective-permute-start | bytes 1179656 | tf_op jit(solution)/shard_map/ppermute | solution.py:65
  29.0 7.9 %collective-permute-start.9 = (bf16[2,2,128,384]{3,2,1,0:T(8,128)(2,1)S(1)}, bf16[2,2,128,384]{3,2,1,0:T(8,128)(2,1)S(1)}, u32[]{:S(2)}, u32[]{:S(2)}) collective-permute-start(bf16[2,2,128,384]{3,2,1,0:T(8,128)(2,1)S(1)} %get-tuple-element.38.refs_7_), channel_id=1, source_target_pairs={{0,1},{1,0},{2,3},{3,2},{4,5},{5,4},{6,7},{7,6},{8,9},{9,8},{10,11... | collective-permute-start | bytes 1179656 | tf_op jit(solution)/shard_map/ppermute | solution.py:49
  33.8 12.2 %collective-permute-start.11 = (bf16[3,2,128,384]{3,2,1,0:T(8,128)(2,1)S(1)}, bf16[3,2,128,384]{3,2,1,0:T(8,128)(2,1)S(1)}, u32[]{:S(2)}, u32[]{:S(2)}) collective-permute-start(bf16[3,2,128,384]{3,2,1,0:T(8,128)(2,1)S(1)} %get-tuple-element.39.refs_7_), channel_id=1, source_target_pairs={{0,4},{1,3},{2,6},{3,1},{4,0},{5,7},{6,2},{7,5},{8,12},{9,11},{10,... | collective-permute-start | bytes 1769480 | tf_op jit(solution)/shard_map/ppermute | solution.py:49
  39.4 12.1 %collective-permute-start.13 = (f32[6,8,256]{2,1,0:T(8,128)S(1)}, f32[6,8,256]{2,1,0:T(8,128)S(1)}, u32[]{:S(2)}, u32[]{:S(2)}) collective-permute-start(f32[6,8,256]{2,1,0:T(8,128)S(1)} %get-tuple-element.40.refs_1_), channel_id=1, source_target_pairs={{1,0},{2,1},{3,2},{4,3},{5,4},{6,5},{7,6},{9,8},{10,9},{11,10},{12... | collective-permute-start | bytes 147464 | tf_op jit(solution)/shard_map/ppermute | solution.py:677
  40.7 10.7 %collective-permute-start.15 = (bf16[256,768]{1,0:T(8,128)(2,1)S(1)}, bf16[256,768]{1,0:T(8,128)(2,1)S(1)}, u32[]{:S(2)}, u32[]{:S(2)}) collective-permute-start(bf16[256,768]{1,0:T(8,128)(2,1)S(1)} %pass_on.1), channel_id=1, source_target_pairs={{0,3},{8,11},{16,19},{24,27}} | collective-permute-start | bytes 1179656 | tf_op jit(solution)/shard_map/ppermute | solution.py:70
  46.1 11.0 %collective-permute-start.16 = (bf16[3,2,128,384]{3,2,1,0:T(8,128)(2,1)S(1)}, bf16[3,2,128,384]{3,2,1,0:T(8,128)(2,1)S(1)}, u32[]{:S(2)}, u32[]{:S(2)}) collective-permute-start(bf16[3,2,128,384]{3,2,1,0:T(8,128)(2,1)S(1)} %get-tuple-element.44.refs_12_), channel_id=1, source_target_pairs={{0,2},{1,5},{2,0},{3,7},{4,6},{5,1},{6,4},{7,3},{8,10},{9,13},{10,... | collective-permute-start | bytes 1769480 | tf_op jit(solution)/shard_map/ppermute | solution.py:49
  57.5 1.8 %collective-permute-start.17 = (bf16[2,2,128,384]{3,2,1,0:T(8,128)(2,1)S(1)}, bf16[2,2,128,384]{3,2,1,0:T(8,128)(2,1)S(1)}, u32[]{:S(2)}, u32[]{:S(2)}) collective-permute-start(bf16[2,2,128,384]{3,2,1,0:T(8,128)(2,1)S(1)} %get-tuple-element.51), channel_id=1, source_target_pairs={{0,1},{1,0},{2,3},{3,2},{4,5},{5,4},{6,7},{7,6},{8,9},{9,8},{10,11... | collective-permute-start | bytes 1179656 | tf_op jit(solution)/shard_map/ppermute | solution.py:49

commit v16 on v15

--- a/solution.py
+++ b/solution.py
@@ -125,12 +125,11 @@
     return jnp.where((me & 1) == 0, even_value, odd_value)
 
 
-def load_kernel(count, *refs):
+def load_kernel(count, stacked, *refs):
     arrays, outs, sems = refs[:count], refs[count:-1], refs[-1]
-    if len(outs) == 1:
-        rows = arrays[0].shape[0]
-        outs = [outs[0].at[pl.ds(j * rows, rows)] for j in range(count)]
-    copies = [pltpu.make_async_copy(ref, out, sems.at[j]) for j, (ref, out) in enumerate(zip(arrays, outs))]
+    rows = arrays[0].shape[0]
+    targets = [outs[0].at[pl.ds(j * rows, rows)] for j in range(stacked)] + list(outs[1 if stacked else 0 :])
+    copies = [pltpu.make_async_copy(ref, out, sems.at[j]) for j, (ref, out) in enumerate(zip(arrays, targets))]
     for copy in copies:
         copy.start()
     for copy in copies:
@@ -596,9 +595,9 @@
     bank_frames = bank_frames.reshape(1, slots)
     last_bits = turns[-1]
 
-    def load(outs, arrays, name, after=()):
+    def load(outs, arrays, name, stacked=0, after=()):
         def run(*refs):
-            load_kernel(len(arrays), *refs[: len(arrays)], *refs[len(arrays) + len(after) :])
+            load_kernel(len(arrays), stacked, *refs[: len(arrays)], *refs[len(arrays) + len(after) :])
 
         return pl.pallas_call(
             run,
@@ -612,7 +611,6 @@
 
     half_width = width // 2
     pair = [swap(array, 1, 1, peers) for array in (key_states, value_states)]
-    pair_index = swap(memory_index, 1, 1, peers)
     rows_shape = shape(BF16, row_count, width)
     keys, values, bank = load(
         [rows_shape, rows_shape, shape(jnp.int32, 1, slots)], [key_states, value_states, bank_frames], "load"
@@ -621,7 +619,14 @@
     held = shape(BF16, slots - 1, 2, frame_len, half_width)
     sums = shape(F32, slots - 1, 2, frame_len, half_width)
     (mine,) = call(functools.partial(split_kernel, peers), [held], [bank, keys, values, *pair], name="split")
-    (queries,) = load([shape(BF16, 2 * row_count, width)], [query_states, grad_out], "load_queries", after=[mine])
+    queries, index = load(
+        [shape(BF16, 2 * row_count, width), shape(jnp.int32, 1, MEM)],
+        [query_states, grad_out, memory_index],
+        "load_queries",
+        stacked=2,
+        after=[mine],
+    )
+    pair_index = swap(index, 1, 1, peers)
     pair_queries = swap(queries, 1, 1, peers)
 
     bias_rows = -(-(5 * FR_DEV) // 8) * 8

time: 60.6 us -> 61.7 us (1.018)
  waiting for transfers between devices: 11.4 us -> 13.1 us
    ppermute x11, waiting for transfers between devices: 11.4 us -> 13.1 us  [swap(): lax.ppermute(block, 'tm', [(i, i ^ (odd_bit if i & 1 else even_bit)) for...]
    ppermute x2, starting transfers between devices: 5.55 us -> 4.57 us  [shift_second(): return lax.ppermute(block, 'tm', pairs) if pairs else block]
  transfers between devices with their start and end apart: 18 -> 18, of which waited for: 4 -> 6; matrix products, arithmetic and copies ran while one was open for 0% -> 0% of each run, Pallas kernels for 26% -> 25%
where the time goes in v16:
time: 61.7 us; the launch traced here: 61.4 us
  starting transfers between devices  30.5 us (49%)
  Pallas kernels  16.9 us (27%)
  waiting for transfers between devices  13.1 us (21%)
  between operations  0.83 us (1%)
    ppermute x11, starting transfers between devices, swap(): lax.ppermute(block, 'tm', [(i, i ^ (odd_bit if i & 1 else even_bit)) for...  21.3 us
    pallas_call x13, Pallas kernels, call(): pl.pallas_call(run, out_shape=outs, in_specs=[SMEM] * len(scalars) + [VME...  14.7 us
    ppermute x11, waiting for transfers between devices, swap(): lax.ppermute(block, 'tm', [(i, i ^ (odd_bit if i & 1 else even_bit)) for...  13.1 us
    ppermute x2, starting transfers between devices, shift_second(): return lax.ppermute(block, 'tm', pairs) if pairs else block  4.57 us
    pallas_call x2, Pallas kernels, load(): pl.pallas_call(run, out_shape=outs, in_specs=[pl.BlockSpec(memory_space=p...  2.28 us
    ppermute x2, starting transfers between devices, shift_first(): lax.ppermute(block, 'tm', [(i, relays.get((i, j), j)) for i, j in pairs])  1.98 us
    ppermute x2, starting transfers between devices, shift(): return lax.ppermute(block, 'tm', pairs)  1.36 us
    ppermute x1, starting transfers between devices, body(): lax.ppermute(stats_all, 'tm', [(i, i - 1) for i in range(1, peers)])  1.29 us
  transfers between devices with their start and end apart: 18, of which 6 were waited for; matrix products, arithmetic and copies ran while one was open for 0% of the time, Pallas kernels for 25%

profile of v16, /device:TPU:0, one launch (start us, length us, event | category | flops | bytes accessed | tf_op | source)
XLA Modules:
  0.0 61.4 jit_solution(1763147011697349961)
XLA Ops:
  0.6 0.5 collective-permute-start
  1.1 0.1 collective-permute-start.1
  1.2 1.1 %load.1 = (bf16[256,768]{1,0:T(8,128)(2,1)S(1)}, bf16[256,768]{1,0:T(8,128)(2,1)S(1)}, s32[1,4]{1,0:T(1,128)S(1)}) custom-call(bf16[256,768]{1,0:T(8,128)(2,1)} %refs_0_.2, bf16[256,768]{1,0:T(8,128)(2,1)} %refs_1_.3, s32[1,4]{1,0:T(1,128)} %bitcast.1), custom_call_target="tpu_custom_call" | custom-call | tf_op jit(solution)/shard_map/load/pallas_call | solution.py:602
  2.4 0.7 %collective-permute-start.3 = (bf16[256,768]{1,0:T(8,128)(2,1)S(1)}, bf16[256,768]{1,0:T(8,128)(2,1)S(1)}, u32[]{:S(2)}, u32[]{:S(2)}) collective-permute-start(bf16[256,768]{1,0:T(8,128)(2,1)S(1)} %get-tuple-element.32.refs_1_.refs_7_.refs_3_.refs_8_.refs_6_), channel_id=1, source_target_pairs={{1,2},{3,7},{5,6},{9,10},{11,15},{13,14},{17,18},{19,23},{21,22},{... | collective-permute-start | bytes 1179656 | tf_op jit(solution)/shard_map/ppermute | solution.py:65
  3.1 0.0 collective-permute-done.refs_3_.refs_5_.refs_6_
  3.1 0.2 collective-permute-done.1.refs_4_.refs_6_.refs_7_
  3.3 0.3 split.1.refs_3_.refs_1_
  3.6 3.5 %collective-permute-start.6 = (bf16[3,2,128,384]{3,2,1,0:T(8,128)(2,1)S(1)}, bf16[3,2,128,384]{3,2,1,0:T(8,128)(2,1)S(1)}, u32[]{:S(2)}, u32[]{:S(2)}) collective-permute-start(bf16[3,2,128,384]{3,2,1,0:T(8,128)(2,1)S(1)} %split.1.refs_3_.refs_1_), channel_id=1, source_target_pairs={{0,2},{1,5},{2,0},{3,7},{4,6},{5,1},{6,4},{7,3},{8,10},{9,13},{10,... | collective-permute-start | bytes 1769480 | tf_op jit(solution)/shard_map/ppermute | solution.py:49
  7.1 1.1 %load_queries.1 = (bf16[512,768]{1,0:T(8,128)(2,1)S(1)}, s32[1,2]{1,0:T(1,128)S(1)}) custom-call(bf16[256,768]{1,0:T(8,128)(2,1)} %refs_0_.3, bf16[256,768]{1,0:T(8,128)(2,1)} %refs_1_.4, s32[1,2]{1,0:T(1,128)} %refs_1_.5, bf16[3,2,128,384]{3,2,1,0:T(8,128)(2,1)S(1)} %split.1.refs_3_.refs_1_), custom_call_target="tpu_custom_call" | custom-call | tf_op jit(solution)/shard_map/load_queries/pallas_call | solution.py:602
  8.2 2.1 %collective-permute-start.2 = (s32[1,2]{1,0:T(1,128)S(1)}, s32[1,2]{1,0:T(1,128)S(1)}, u32[]{:S(2)}, u32[]{:S(2)}) collective-permute-start(s32[1,2]{1,0:T(1,128)S(1)} %get-tuple-element.34), channel_id=1, source_target_pairs={{0,1},{1,0},{2,3},{3,2},{4,5},{5,4},{6,7},{7,6},{8,9},{9,8},{10,11... | collective-permute-start | bytes 32 | tf_op jit(solution)/shard_map/ppermute | solution.py:49
  10.3 0.1 collective-permute-start.7
  10.4 0.0 collective-permute-done.3.refs_6_.refs_2_.refs_3_
  10.4 0.7 %collective-permute-done.2.refs_2_ = s32[1,2]{1,0:T(1,128)S(1)} collective-permute-done((s32[1,2]{1,0:T(1,128)S(1)}, s32[1,2]{1,0:T(1,128)S(1)}, u32[]{:S(2)}, u32[]{:S(2)}) %collective-permute-start.2) | collective-permute-done | bytes 40 | tf_op jit(solution)/shard_map/ppermute | solution.py:49
  11.1 1.7 %plan.1 = (f32[6,16,256]{2,1,0:T(8,128)S(1)}, s32[8,128]{1,0:T(8,128)S(1)}, bf16[256,768]{1,0:T(8,128)(2,1)S(1)}, bf16[256,768]{1,0:T(8,128)(2,1)S(1)}) custom-call(s32[1,4]{1,0:T(1,128)S(1)} %bitcast.2, s32[1,2]{1,0:T(1,128)S(1)} %copy-done, s32[1,2]{1,0:T(1,128)S(1)} %collective-permute-done.2.refs_2_, s32[16]{0:T(128)S(1)} %copy-done.3, ...), custom_call_target="tpu_custom_call" | custom-call | flops 20132659200 | tf_op jit(solution)/shard_map/plan/pallas_call | solution.py:37
  12.8 0.7 %collective-permute-start.4 = (bf16[256,768]{1,0:T(8,128)(2,1)S(1)}, bf16[256,768]{1,0:T(8,128)(2,1)S(1)}, u32[]{:S(2)}, u32[]{:S(2)}) collective-permute-start(bf16[256,768]{1,0:T(8,128)(2,1)S(1)} %get-tuple-element.37), channel_id=1, source_target_pairs={{7,4},{15,12},{23,20},{31,28}} | collective-permute-start | bytes 1179656 | tf_op jit(solution)/shard_map/ppermute | solution.py:70
  13.5 0.7 %collective-permute-start.5 = (bf16[256,768]{1,0:T(8,128)(2,1)S(1)}, bf16[256,768]{1,0:T(8,128)(2,1)S(1)}, u32[]{:S(2)}, u32[]{:S(2)}) collective-permute-start(bf16[256,768]{1,0:T(8,128)(2,1)S(1)} %get-tuple-element.38), channel_id=1, source_target_pairs={{1,2},{3,4},{5,6},{9,10},{11,12},{13,14},{17,18},{19,20},{21,22},{... | collective-permute-start | bytes 1179656 | tf_op jit(solution)/shard_map/ppermute | solution.py:54
  14.2 4.1 %collective-permute-done.6.refs_2_ = bf16[3,2,128,384]{3,2,1,0:T(8,128)(2,1)S(1)} collective-permute-done((bf16[3,2,128,384]{3,2,1,0:T(8,128)(2,1)S(1)}, bf16[3,2,128,384]{3,2,1,0:T(8,128)(2,1)S(1)}, u32[]{:S(2)}, u32[]{:S(2)}) %collective-permute-start.6) | collective-permute-done | bytes 589856 | tf_op jit(solution)/shard_map/ppermute | solution.py:49
  18.2 0.0 collective-permute-done.7.refs_4_.refs_5_.refs_2_
  18.2 0.3 step.1.refs_1_
  18.5 1.6 %collective-permute-start.8 = (bf16[3,2,128,384]{3,2,1,0:T(8,128)(2,1)S(1)}, bf16[3,2,128,384]{3,2,1,0:T(8,128)(2,1)S(1)}, u32[]{:S(2)}, u32[]{:S(2)}) collective-permute-start(bf16[3,2,128,384]{3,2,1,0:T(8,128)(2,1)S(1)} %step.1.refs_1_), channel_id=1, source_target_pairs={{0,4},{1,3},{2,6},{3,1},{4,0},{5,7},{6,2},{7,5},{8,12},{9,11},{10,... | collective-permute-start | bytes 1769480 | tf_op jit(solution)/shard_map/ppermute | solution.py:49
  20.1 0.0 collective-permute-done.4.refs_3_.refs_4_
  20.1 0.0 collective-permute-done.5.refs_4_.refs_5_
  20.1 1.5 %stats.1 = (f32[6,8,256]{2,1,0:T(8,128)S(1)}, bf16[256,768]{1,0:T(8,128)(2,1)S(1)}, bf16[256,768]{1,0:T(8,128)(2,1)S(1)}) custom-call(f32[6,16,256]{2,1,0:T(8,128)S(1)} %get-tuple-element.35.refs_0_.refs_1_, bf16[512,768]{1,0:T(8,128)(2,1)S(1)} %get-tuple-element.36.refs_1_.refs_4_.refs_2_, ...), custom_call_target="tpu_custom_call" | custom-call | flops 20132659200 | tf_op jit(solution)/shard_map/stats/pallas_call | solution.py:37
  21.6 7.3 %collective-permute-start.10 = (f32[6,8,256]{2,1,0:T(8,128)S(1)}, f32[6,8,256]{2,1,0:T(8,128)S(1)}, u32[]{:S(2)}, u32[]{:S(2)}) collective-permute-start(f32[6,8,256]{2,1,0:T(8,128)S(1)} %get-tuple-element.39.refs_2_.refs_1_), channel_id=1, source_target_pairs={{0,1},{1,0},{2,3},{3,2},{4,5},{5,4},{6,7},{7,6},{8,9},{9,8},{10,11... | collective-permute-start | bytes 147464 | tf_op jit(solution)/shard_map/ppermute | solution.py:49
  28.9 0.7 %collective-permute-start.12 = (bf16[256,768]{1,0:T(8,128)(2,1)S(1)}, bf16[256,768]{1,0:T(8,128)(2,1)S(1)}, u32[]{:S(2)}, u32[]{:S(2)}) collective-permute-start(bf16[256,768]{1,0:T(8,128)(2,1)S(1)} %get-tuple-element.47), channel_id=1, source_target_pairs={{2,1},{4,3},{6,5},{10,9},{12,11},{14,13},{18,17},{20,19},{22,21},{... | collective-permute-start | bytes 1179656 | tf_op jit(solution)/shard_map/ppermute | solution.py:54
  29.6 1.3 %collective-permute-start.14 = (bf16[256,768]{1,0:T(8,128)(2,1)S(1)}, bf16[256,768]{1,0:T(8,128)(2,1)S(1)}, u32[]{:S(2)}, u32[]{:S(2)}) collective-permute-start(bf16[256,768]{1,0:T(8,128)(2,1)S(1)} %get-tuple-element.51), channel_id=1, source_target_pairs={{2,1},{4,0},{6,5},{10,9},{12,8},{14,13},{18,17},{20,16},{22,21},{2... | collective-permute-start | bytes 1179656 | tf_op jit(solution)/shard_map/ppermute | solution.py:65
  30.9 0.0 collective-permute-done.8.refs_2_
  30.9 0.3 pick.1
  31.2 2.8 %collective-permute-start.9 = (bf16[2,2,128,384]{3,2,1,0:T(8,128)(2,1)S(1)}, bf16[2,2,128,384]{3,2,1,0:T(8,128)(2,1)S(1)}, u32[]{:S(2)}, u32[]{:S(2)}) collective-permute-start(bf16[2,2,128,384]{3,2,1,0:T(8,128)(2,1)S(1)} %get-tuple-element.42.refs_7_), channel_id=1, source_target_pairs={{0,1},{1,0},{2,3},{3,2},{4,5},{5,4},{6,7},{7,6},{8,9},{9,8},{10,11... | collective-permute-start | bytes 1179656 | tf_op jit(solution)/shard_map/ppermute | solution.py:49
  34.0 1.9 %memory.1 = (f32[4,2,128,384]{3,2,1,0:T(8,128)S(1)}, bf16[3,2,128,384]{3,2,1,0:T(8,128)(2,1)S(1)}) custom-call(s32[8,128]{1,0:T(8,128)S(1)} %get-tuple-element.40.refs_3_.refs_0_, f32[6,16,256]{2,1,0:T(8,128)S(1)} %get-tuple-element.35.refs_0_.refs_1_, f32[6,8,256]{2,1,0:T(8,128)S(1)} %get-tuple-element.39.refs_2_.refs_1_, ...), custom_call_target="tpu_custom_call" | custom-call | flops 20132659200 | tf_op jit(solution)/shard_map/memory/pallas_call | solution.py:37
  35.9 2.5 %collective-permute-start.11 = (bf16[3,2,128,384]{3,2,1,0:T(8,128)(2,1)S(1)}, bf16[3,2,128,384]{3,2,1,0:T(8,128)(2,1)S(1)}, u32[]{:S(2)}, u32[]{:S(2)}) collective-permute-start(bf16[3,2,128,384]{3,2,1,0:T(8,128)(2,1)S(1)} %get-tuple-element.43.refs_7_), channel_id=1, source_target_pairs={{0,4},{1,3},{2,6},{3,1},{4,0},{5,7},{6,2},{7,5},{8,12},{9,11},{10,... | collective-permute-start | bytes 1769480 | tf_op jit(solution)/shard_map/ppermute | solution.py:49
  38.5 2.4 %own.1 = (f32[2,256,768]{2,1,0:T(8,128)S(1)}, f32[6,8,256]{2,1,0:T(8,128)S(1)}) custom-call(f32[6,16,256]{2,1,0:T(8,128)S(1)} %get-tuple-element.35.refs_0_.refs_1_, f32[6,8,256]{2,1,0:T(8,128)S(1)} %get-tuple-element.39.refs_2_.refs_1_, bf16[512,768]{1,0:T(8,128)(2,1)S(1)} %get-tuple-element.36.refs_1_.refs_4_.refs_2_, ...), custom_call_target="tpu_custom_call" | custom-call | flops 20132659200 | tf_op jit(solution)/shard_map/own/pallas_call | solution.py:37
  40.9 1.3 %collective-permute-start.13 = (f32[6,8,256]{2,1,0:T(8,128)S(1)}, f32[6,8,256]{2,1,0:T(8,128)S(1)}, u32[]{:S(2)}, u32[]{:S(2)}) collective-permute-start(f32[6,8,256]{2,1,0:T(8,128)S(1)} %get-tuple-element.44.refs_1_), channel_id=1, source_target_pairs={{1,0},{2,1},{3,2},{4,3},{5,4},{6,5},{7,6},{9,8},{10,9},{11,10},{12... | collective-permute-start | bytes 147464 | tf_op jit(solution)/shard_map/ppermute | solution.py:682
  42.2 0.0 collective-permute-done.14.refs_0_.refs_4_
  42.2 3.9 %collective-permute-start.15 = (bf16[256,768]{1,0:T(8,128)(2,1)S(1)}, bf16[256,768]{1,0:T(8,128)(2,1)S(1)}, u32[]{:S(2)}, u32[]{:S(2)}) collective-permute-start(bf16[256,768]{1,0:T(8,128)(2,1)S(1)} %pass_on.1), channel_id=1, source_target_pairs={{0,3},{8,11},{16,19},{24,27}} | collective-permute-start | bytes 1179656 | tf_op jit(solution)/shard_map/ppermute | solution.py:70
  46.1 0.0 collective-permute-done.12.refs_3_
  46.1 2.0 %collective-permute-done.11.refs_1_ = bf16[3,2,128,384]{3,2,1,0:T(8,128)(2,1)S(1)} collective-permute-done((bf16[3,2,128,384]{3,2,1,0:T(8,128)(2,1)S(1)}, bf16[3,2,128,384]{3,2,1,0:T(8,128)(2,1)S(1)}, u32[]{:S(2)}, u32[]{:S(2)}) %collective-permute-start.11) | collective-permute-done | bytes 589856 | tf_op jit(solution)/shard_map/ppermute | solution.py:49
  48.1 0.2 add.1
  48.3 0.7 %collective-permute-start.16 = (bf16[3,2,128,384]{3,2,1,0:T(8,128)(2,1)S(1)}, bf16[3,2,128,384]{3,2,1,0:T(8,128)(2,1)S(1)}, u32[]{:S(2)}, u32[]{:S(2)}) collective-permute-start(bf16[3,2,128,384]{3,2,1,0:T(8,128)(2,1)S(1)} %get-tuple-element.48.refs_12_), channel_id=1, source_target_pairs={{0,2},{1,5},{2,0},{3,7},{4,6},{5,1},{6,4},{7,3},{8,10},{9,13},{10,... | collective-permute-start | bytes 1769480 | tf_op jit(solution)/shard_map/ppermute | solution.py:49
  49.0 3.6 %attend.1 = (bf16[256,768]{1,0:T(8,128)(2,1)}, bf16[256,768]{1,0:T(8,128)(2,1)}, f32[8,128]{1,0:T(8,128)S(1)}) custom-call(f32[6,16,256]{2,1,0:T(8,128)S(1)} %get-tuple-element.35.refs_0_.refs_1_, f32[6,8,256]{2,1,0:T(8,128)S(1)} %get-tuple-element.44.refs_1_, bf16[512,768]{1,0:T(8,128)(2,1)S(1)} %get-tuple-element.36.refs_1_.refs_4_.refs_2_, ...), custom_call_target="tpu_custom_call" | custom-call | flops 20132659200 | tf_op jit(solution)/shard_map/attend/pallas_call | solution.py:37
  52.6 0.0 collective-permute-done.13.refs_1_
  52.6 0.0 collective-permute-done.15.refs_5_
  52.6 1.1 %next.1.refs_3_.refs_0_ = f32[2,256,768]{2,1,0:T(8,128)S(1)} custom-call(f32[6,16,256]{2,1,0:T(8,128)S(1)} %get-tuple-element.35.refs_0_.refs_1_, f32[6,8,256]{2,1,0:T(8,128)S(1)} %collective-permute-done.13.refs_1_, bf16[512,768]{1,0:T(8,128)(2,1)S(1)} %collective-permute-done.7.refs_4_.refs_5_.refs_2_, ...), custom_call_target="tpu_custom_call" | custom-call | flops 20132659200 | tf_op jit(solution)/shard_map/next/pallas_call | solution.py:37
  53.8 4.5 %collective-permute-done.16.refs_2_ = bf16[3,2,128,384]{3,2,1,0:T(8,128)(2,1)S(1)} collective-permute-done((bf16[3,2,128,384]{3,2,1,0:T(8,128)(2,1)S(1)}, bf16[3,2,128,384]{3,2,1,0:T(8,128)(2,1)S(1)}, u32[]{:S(2)}, u32[]{:S(2)}) %collective-permute-start.16) | collective-permute-done | bytes 589856 | tf_op jit(solution)/shard_map/ppermute | solution.py:49
  58.2 0.3 owned.1
  58.6 0.2 collective-permute-start.17
  58.8 1.6 %collective-permute-done.17.refs_2_ = bf16[2,2,128,384]{3,2,1,0:T(8,128)(2,1)S(1)} collective-permute-done((bf16[2,2,128,384]{3,2,1,0:T(8,128)(2,1)S(1)}, bf16[2,2,128,384]{3,2,1,0:T(8,128)(2,1)S(1)}, u32[]{:S(2)}, u32[]{:S(2)}) %collective-permute-start.17) | collective-permute-done | bytes 393248 | tf_op jit(solution)/shard_map/ppermute | solution.py:49
  60.4 1.0 %final.1 = (bf16[256,768]{1,0:T(8,128)(2,1)}, bf16[256,768]{1,0:T(8,128)(2,1)}) custom-call(f32[2,256,768]{2,1,0:T(8,128)S(1)} %next.1.refs_3_.refs_0_, f32[2,2,128,384]{3,2,1,0:T(8,128)S(1)} %get-tuple-element.54.refs_1_, bf16[2,2,128,384]{3,2,1,0:T(8,128)(2,1)S(1)} %collective-permute-done.17.refs_2_), custom_call_target="tpu_custom_call" | custom-call | tf_op jit(solution)/shard_map/final/pallas_call | solution.py:37
  (11 shorter events, 0.0 us)
Async XLA Ops:
  0.6 2.4 %collective-permute-start = (bf16[256,768]{1,0:T(8,128)(2,1)}, bf16[256,768]{1,0:T(8,128)(2,1)S(1)}, u32[]{:S(2)}, u32[]{:S(2)}) collective-permute-start(bf16[256,768]{1,0:T(8,128)(2,1)} %refs_0_.2), channel_id=1, source_target_pairs={{0,1},{1,0},{2,3},{3,2},{4,5},{5,4},{6,7},{7,6},{8,9},{9,8},{10,11... | collective-permute-start | bytes 1179656 | tf_op jit(solution)/shard_map/ppermute | solution.py:49
  1.1 2.1 %collective-permute-start.1 = (bf16[256,768]{1,0:T(8,128)(2,1)}, bf16[256,768]{1,0:T(8,128)(2,1)S(1)}, u32[]{:S(2)}, u32[]{:S(2)}) collective-permute-start(bf16[256,768]{1,0:T(8,128)(2,1)} %refs_1_.3), channel_id=1, source_target_pairs={{0,1},{1,0},{2,3},{3,2},{4,5},{5,4},{6,7},{7,6},{8,9},{9,8},{10,11... | collective-permute-start | bytes 1179656 | tf_op jit(solution)/shard_map/ppermute | solution.py:49
  2.4 8.0 %collective-permute-start.3 = (bf16[256,768]{1,0:T(8,128)(2,1)S(1)}, bf16[256,768]{1,0:T(8,128)(2,1)S(1)}, u32[]{:S(2)}, u32[]{:S(2)}) collective-permute-start(bf16[256,768]{1,0:T(8,128)(2,1)S(1)} %get-tuple-element.32.refs_1_.refs_7_.refs_3_.refs_8_.refs_6_), channel_id=1, source_target_pairs={{1,2},{3,7},{5,6},{9,10},{11,15},{13,14},{17,18},{19,23},{21,22},{... | collective-permute-start | bytes 1179656 | tf_op jit(solution)/shard_map/ppermute | solution.py:65
  3.3 7.8 %copy-start = (s32[1,2]{1,0:T(1,128)S(1)}, s32[1,2]{1,0:T(1,128)}, u32[]{:S(2)}) copy-start(s32[1,2]{1,0:T(1,128)} %refs_1_.5) | copy-start | bytes 28
  3.3 7.8 %copy-start.1 = (s32[4]{0:T(128)S(1)}, s32[4]{0:T(128)}, u32[]{:S(2)}) copy-start(s32[4]{0:T(128)} %param.15) | copy-start | bytes 52
  3.3 7.8 %copy-start.2 = (f32[6,16,16]{2,1,0:T(8,128)S(1)}, f32[6,16,16]{2,1,0:T(8,128)}, u32[]{:S(2)}) copy-start(f32[6,16,16]{2,1,0:T(8,128)} %refs_4_.1) | copy-start | bytes 18436
  3.3 7.8 %copy-start.3 = (s32[16]{0:T(128)S(1)}, s32[16]{0:T(128)}, u32[]{:S(2)}) copy-start(s32[16]{0:T(128)} %refs_3_.1) | copy-start | bytes 196
  3.6 14.6 %collective-permute-start.6 = (bf16[3,2,128,384]{3,2,1,0:T(8,128)(2,1)S(1)}, bf16[3,2,128,384]{3,2,1,0:T(8,128)(2,1)S(1)}, u32[]{:S(2)}, u32[]{:S(2)}) collective-permute-start(bf16[3,2,128,384]{3,2,1,0:T(8,128)(2,1)S(1)} %split.1.refs_3_.refs_1_), channel_id=1, source_target_pairs={{0,2},{1,5},{2,0},{3,7},{4,6},{5,1},{6,4},{7,3},{8,10},{9,13},{10,... | collective-permute-start | bytes 1769480 | tf_op jit(solution)/shard_map/ppermute | solution.py:49
  8.2 2.9 %collective-permute-start.2 = (s32[1,2]{1,0:T(1,128)S(1)}, s32[1,2]{1,0:T(1,128)S(1)}, u32[]{:S(2)}, u32[]{:S(2)}) collective-permute-start(s32[1,2]{1,0:T(1,128)S(1)} %get-tuple-element.34), channel_id=1, source_target_pairs={{0,1},{1,0},{2,3},{3,2},{4,5},{5,4},{6,7},{7,6},{8,9},{9,8},{10,11... | collective-permute-start | bytes 32 | tf_op jit(solution)/shard_map/ppermute | solution.py:49
  10.3 8.0 %collective-permute-start.7 = (bf16[512,768]{1,0:T(8,128)(2,1)S(1)}, bf16[512,768]{1,0:T(8,128)(2,1)S(1)}, u32[]{:S(2)}, u32[]{:S(2)}) collective-permute-start(bf16[512,768]{1,0:T(8,128)(2,1)S(1)} %get-tuple-element.36.refs_1_.refs_4_.refs_2_), channel_id=1, source_target_pairs={{0,1},{1,0},{2,3},{3,2},{4,5},{5,4},{6,7},{7,6},{8,9},{9,8},{10,11... | collective-permute-start | bytes 2359304 | tf_op jit(solution)/shard_map/ppermute | solution.py:49
  12.8 7.3 %collective-permute-start.4 = (bf16[256,768]{1,0:T(8,128)(2,1)S(1)}, bf16[256,768]{1,0:T(8,128)(2,1)S(1)}, u32[]{:S(2)}, u32[]{:S(2)}) collective-permute-start(bf16[256,768]{1,0:T(8,128)(2,1)S(1)} %get-tuple-element.37), channel_id=1, source_target_pairs={{7,4},{15,12},{23,20},{31,28}} | collective-permute-start | bytes 1179656 | tf_op jit(solution)/shard_map/ppermute | solution.py:70
  13.5 6.7 %collective-permute-start.5 = (bf16[256,768]{1,0:T(8,128)(2,1)S(1)}, bf16[256,768]{1,0:T(8,128)(2,1)S(1)}, u32[]{:S(2)}, u32[]{:S(2)}) collective-permute-start(bf16[256,768]{1,0:T(8,128)(2,1)S(1)} %get-tuple-element.38), channel_id=1, source_target_pairs={{1,2},{3,4},{5,6},{9,10},{11,12},{13,14},{17,18},{19,20},{21,22},{... | collective-permute-start | bytes 1179656 | tf_op jit(solution)/shard_map/ppermute | solution.py:54
  18.5 12.4 %collective-permute-start.8 = (bf16[3,2,128,384]{3,2,1,0:T(8,128)(2,1)S(1)}, bf16[3,2,128,384]{3,2,1,0:T(8,128)(2,1)S(1)}, u32[]{:S(2)}, u32[]{:S(2)}) collective-permute-start(bf16[3,2,128,384]{3,2,1,0:T(8,128)(2,1)S(1)} %step.1.refs_1_), channel_id=1, source_target_pairs={{0,4},{1,3},{2,6},{3,1},{4,0},{5,7},{6,2},{7,5},{8,12},{9,11},{10,... | collective-permute-start | bytes 1769480 | tf_op jit(solution)/shard_map/ppermute | solution.py:49
  21.6 12.4 %collective-permute-start.10 = (f32[6,8,256]{2,1,0:T(8,128)S(1)}, f32[6,8,256]{2,1,0:T(8,128)S(1)}, u32[]{:S(2)}, u32[]{:S(2)}) collective-permute-start(f32[6,8,256]{2,1,0:T(8,128)S(1)} %get-tuple-element.39.refs_2_.refs_1_), channel_id=1, source_target_pairs={{0,1},{1,0},{2,3},{3,2},{4,5},{5,4},{6,7},{7,6},{8,9},{9,8},{10,11... | collective-permute-start | bytes 147464 | tf_op jit(solution)/shard_map/ppermute | solution.py:49
  28.9 17.2 %collective-permute-start.12 = (bf16[256,768]{1,0:T(8,128)(2,1)S(1)}, bf16[256,768]{1,0:T(8,128)(2,1)S(1)}, u32[]{:S(2)}, u32[]{:S(2)}) collective-permute-start(bf16[256,768]{1,0:T(8,128)(2,1)S(1)} %get-tuple-element.47), channel_id=1, source_target_pairs={{2,1},{4,3},{6,5},{10,9},{12,11},{14,13},{18,17},{20,19},{22,21},{... | collective-permute-start | bytes 1179656 | tf_op jit(solution)/shard_map/ppermute | solution.py:54
  29.6 12.6 %collective-permute-start.14 = (bf16[256,768]{1,0:T(8,128)(2,1)S(1)}, bf16[256,768]{1,0:T(8,128)(2,1)S(1)}, u32[]{:S(2)}, u32[]{:S(2)}) collective-permute-start(bf16[256,768]{1,0:T(8,128)(2,1)S(1)} %get-tuple-element.51), channel_id=1, source_target_pairs={{2,1},{4,0},{6,5},{10,9},{12,8},{14,13},{18,17},{20,16},{22,21},{2... | collective-permute-start | bytes 1179656 | tf_op jit(solution)/shard_map/ppermute | solution.py:65
  31.2 7.3 %collective-permute-start.9 = (bf16[2,2,128,384]{3,2,1,0:T(8,128)(2,1)S(1)}, bf16[2,2,128,384]{3,2,1,0:T(8,128)(2,1)S(1)}, u32[]{:S(2)}, u32[]{:S(2)}) collective-permute-start(bf16[2,2,128,384]{3,2,1,0:T(8,128)(2,1)S(1)} %get-tuple-element.42.refs_7_), channel_id=1, source_target_pairs={{0,1},{1,0},{2,3},{3,2},{4,5},{5,4},{6,7},{7,6},{8,9},{9,8},{10,11... | collective-permute-start | bytes 1179656 | tf_op jit(solution)/shard_map/ppermute | solution.py:49
  35.9 12.2 %collective-permute-start.11 = (bf16[3,2,128,384]{3,2,1,0:T(8,128)(2,1)S(1)}, bf16[3,2,128,384]{3,2,1,0:T(8,128)(2,1)S(1)}, u32[]{:S(2)}, u32[]{:S(2)}) collective-permute-start(bf16[3,2,128,384]{3,2,1,0:T(8,128)(2,1)S(1)} %get-tuple-element.43.refs_7_), channel_id=1, source_target_pairs={{0,4},{1,3},{2,6},{3,1},{4,0},{5,7},{6,2},{7,5},{8,12},{9,11},{10,... | collective-permute-start | bytes 1769480 | tf_op jit(solution)/shard_map/ppermute | solution.py:49
  40.9 11.8 %collective-permute-start.13 = (f32[6,8,256]{2,1,0:T(8,128)S(1)}, f32[6,8,256]{2,1,0:T(8,128)S(1)}, u32[]{:S(2)}, u32[]{:S(2)}) collective-permute-start(f32[6,8,256]{2,1,0:T(8,128)S(1)} %get-tuple-element.44.refs_1_), channel_id=1, source_target_pairs={{1,0},{2,1},{3,2},{4,3},{5,4},{6,5},{7,6},{9,8},{10,9},{11,10},{12... | collective-permute-start | bytes 147464 | tf_op jit(solution)/shard_map/ppermute | solution.py:682
  42.2 10.4 %collective-permute-start.15 = (bf16[256,768]{1,0:T(8,128)(2,1)S(1)}, bf16[256,768]{1,0:T(8,128)(2,1)S(1)}, u32[]{:S(2)}, u32[]{:S(2)}) collective-permute-start(bf16[256,768]{1,0:T(8,128)(2,1)S(1)} %pass_on.1), channel_id=1, source_target_pairs={{0,3},{8,11},{16,19},{24,27}} | collective-permute-start | bytes 1179656 | tf_op jit(solution)/shard_map/ppermute | solution.py:70
  48.3 9.9 %collective-permute-start.16 = (bf16[3,2,128,384]{3,2,1,0:T(8,128)(2,1)S(1)}, bf16[3,2,128,384]{3,2,1,0:T(8,128)(2,1)S(1)}, u32[]{:S(2)}, u32[]{:S(2)}) collective-permute-start(bf16[3,2,128,384]{3,2,1,0:T(8,128)(2,1)S(1)} %get-tuple-element.48.refs_12_), channel_id=1, source_target_pairs={{0,2},{1,5},{2,0},{3,7},{4,6},{5,1},{6,4},{7,3},{8,10},{9,13},{10,... | collective-permute-start | bytes 1769480 | tf_op jit(solution)/shard_map/ppermute | solution.py:49
  58.6 1.8 %collective-permute-start.17 = (bf16[2,2,128,384]{3,2,1,0:T(8,128)(2,1)S(1)}, bf16[2,2,128,384]{3,2,1,0:T(8,128)(2,1)S(1)}, u32[]{:S(2)}, u32[]{:S(2)}) collective-permute-start(bf16[2,2,128,384]{3,2,1,0:T(8,128)(2,1)S(1)} %get-tuple-element.55), channel_id=1, source_target_pairs={{0,1},{1,0},{2,3},{3,2},{4,5},{5,4},{6,7},{7,6},{8,9},{9,8},{10,11... | collective-permute-start | bytes 1179656 | tf_op jit(solution)/shard_map/ppermute | solution.py:49

commit v17 on v14

--- a/solution.py
+++ b/solution.py
@@ -186,18 +186,12 @@
     pose_ref,
     bias_ref,
     pair_ref,
-    joined_ref,
-    direct_keys,
     rows_ref,
     codes_ref,
-    values_out,
-    keys_out,
 ):
     me = lax.axis_index("tm")
     last_frame = peers * FR_DEV - 1
     heads, _, row_count = rows_ref.shape
-    values_out[...] = joined_ref[row_count : 2 * row_count, :]
-    keys_out[...] = direct_keys[...]
     bank = [bank_ref[0, slot] for slot in range(bank_ref.shape[1])]
     tail = pair_ref.shape[0] - TAIL
     pair_ids = []
@@ -247,6 +241,12 @@
         codes_ref[row : row + 1, :] = jnp.full((1, lanes), code, jnp.int32)
 
 
+def release_kernel(joined_ref, direct_keys, values_out, keys_out):
+    rows = values_out.shape[0]
+    values_out[...] = joined_ref[rows : 2 * rows, :]
+    keys_out[...] = direct_keys[...]
+
+
 def split_kernel(peers, bank_ref, mine_ref, pair_ref, out_ref):
     me = lax.axis_index("tm")
     frame_len, half_width = out_ref.shape[2:]
@@ -644,13 +644,20 @@
     pair_queries = swap(queries, 1, 1, peers)
 
     bias_rows = -(-(5 * FR_DEV) // 8) * 8
-    rows, codes, values_out, keys_out = call(
+    rows, codes = call(
         functools.partial(plan_kernel, peers, last_bits),
-        [shape(F32, heads, bias_rows, row_count), shape(jnp.int32, 8, 128)] + [shape(BF16, row_count, width)] * 2,
-        [pair, joined, direct_keys],
+        [shape(F32, heads, bias_rows, row_count), shape(jnp.int32, 8, 128)],
+        [pair],
         scalars=[bank_frames, memory_index, camera_pose, pose_bias],
+        name="plan",
+    )
+    values_out, keys_out = call(
+        release_kernel,
+        [shape(BF16, row_count, width)] * 2,
+        [joined, direct_keys],
+        after=[codes],
         flops=HIDING * piece_flops,
-        name="plan",
+        name="release",
     )
     outer = [direct_keys, shift_second(keys_out, 1, 1, peers), shift(values_out, 1, 1, peers)]
     even_done = odd_done = 1

time: 60.2 us -> 58.6 us (0.973)
  starting transfers between devices: 27.7 us -> 25.8 us
    ppermute x9, starting transfers between devices: 18.6 us -> 16.7 us  [swap(): lax.ppermute(block, 'tm', [(i, i ^ (odd_bit if i & 1 else even_bit)) for...]
    pallas_call x13 -> x14, Pallas kernels: 15.2 us -> 15.1 us  [call(): pl.pallas_call(run, out_shape=outs, in_specs=[SMEM] * len(scalars) + [VME...]
  transfers between devices with their start and end apart: 16 -> 16, of which waited for: 5 -> 6; matrix products, arithmetic and copies ran while one was open for 0% -> 0% of each run, Pallas kernels for 25% -> 25%
where the time goes in v17:
time: 58.6 us; the launch traced here: 58.3 us
  starting transfers between devices  25.8 us (44%)
  Pallas kernels  17.4 us (30%)
  waiting for transfers between devices  14.2 us (24%)
  between operations  0.87 us (1%)
    ppermute x9, starting transfers between devices, swap(): lax.ppermute(block, 'tm', [(i, i ^ (odd_bit if i & 1 else even_bit)) for...  16.7 us
    pallas_call x14, Pallas kernels, call(): pl.pallas_call(run, out_shape=outs, in_specs=[SMEM] * len(scalars) + [VME...  15.1 us
    ppermute x9, waiting for transfers between devices, swap(): lax.ppermute(block, 'tm', [(i, i ^ (odd_bit if i & 1 else even_bit)) for...  14.2 us
    ppermute x2, starting transfers between devices, shift_second(): return lax.ppermute(block, 'tm', pairs) if pairs else block  4.54 us
    pallas_call x2, Pallas kernels, join(): pl.pallas_call(run, out_shape=shape(BF16, rows, width), in_specs=[pl.Bloc...  2.34 us
    ppermute x2, starting transfers between devices, shift_first(): lax.ppermute(block, 'tm', [(i, relays.get((i, j), j)) for i, j in pairs])  1.97 us
    ppermute x2, starting transfers between devices, shift(): return lax.ppermute(block, 'tm', pairs)  1.36 us
    ppermute x1, starting transfers between devices, body(): lax.ppermute(stats_all, 'tm', [(i, i - 1) for i in range(1, peers)])  1.29 us
  transfers between devices with their start and end apart: 16, of which 6 were waited for; matrix products, arithmetic and copies ran while one was open for 0% of the time, Pallas kernels for 25%

profile of v17, /device:TPU:0, one launch (start us, length us, event | category | flops | bytes accessed | tf_op | source)
XLA Modules:
  0.0 58.3 jit_solution(7313613520397766073)
XLA Ops:
  0.7 1.2 %join.1.refs_1_.refs_0_.refs_6_.refs_3_.refs_7_ = bf16[528,768]{1,0:T(8,128)(2,1)S(1)} custom-call(s32[1,2]{1,0:T(1,128)} %refs_1_.4, bf16[256,768]{1,0:T(8,128)(2,1)} %refs_1_.3, bf16[256,768]{1,0:T(8,128)(2,1)} %refs_2_.2), custom_call_target="tpu_custom_call" | custom-call | tf_op jit(solution)/shard_map/join/pallas_call | solution.py:620
  1.9 0.5 collective-permute-start
  2.4 0.7 %collective-permute-start.1 = (bf16[256,768]{1,0:T(8,128)(2,1)S(1)}, bf16[256,768]{1,0:T(8,128)(2,1)S(1)}, u32[]{:S(2)}, u32[]{:S(2)}) collective-permute-start(bf16[256,768]{1,0:T(8,128)(2,1)S(1)} %copy-done.4), channel_id=1, source_target_pairs={{1,2},{3,7},{5,6},{9,10},{11,15},{13,14},{17,18},{19,23},{21,22},{... | collective-permute-start | bytes 1179656 | tf_op jit(solution)/shard_map/ppermute | solution.py:66
  3.1 1.3 %collective-permute-done.refs_4_.refs_2_.refs_5_.refs_6_ = bf16[528,768]{1,0:T(8,128)(2,1)S(1)} collective-permute-done((bf16[528,768]{1,0:T(8,128)(2,1)S(1)}, bf16[528,768]{1,0:T(8,128)(2,1)S(1)}, u32[]{:S(2)}, u32[]{:S(2)}) %collective-permute-start) | collective-permute-done | bytes 811040 | tf_op jit(solution)/shard_map/ppermute | solution.py:50
  4.3 0.3 split.1.refs_2_.refs_1_
  4.7 0.0 copy-start
  4.7 0.0 copy-start.2
  4.7 0.0 copy-start.3
  4.7 2.9 %collective-permute-start.4 = (bf16[3,2,128,384]{3,2,1,0:T(8,128)(2,1)S(1)}, bf16[3,2,128,384]{3,2,1,0:T(8,128)(2,1)S(1)}, u32[]{:S(2)}, u32[]{:S(2)}) collective-permute-start(bf16[3,2,128,384]{3,2,1,0:T(8,128)(2,1)S(1)} %split.1.refs_2_.refs_1_), channel_id=1, source_target_pairs={{0,2},{1,5},{2,0},{3,7},{4,6},{5,1},{6,4},{7,3},{8,10},{9,13},{10,... | collective-permute-start | bytes 1769480 | tf_op jit(solution)/shard_map/ppermute | solution.py:50
  7.6 1.1 %join_queries.1.refs_1_.refs_4_.refs_2_ = bf16[512,768]{1,0:T(8,128)(2,1)S(1)} custom-call(bf16[256,768]{1,0:T(8,128)(2,1)} %refs_0_.3, bf16[256,768]{1,0:T(8,128)(2,1)} %refs_1_.5, bf16[3,2,128,384]{3,2,1,0:T(8,128)(2,1)S(1)} %split.1.refs_2_.refs_1_), custom_call_target="tpu_custom_call" | custom-call | tf_op jit(solution)/shard_map/join_queries/pallas_call | solution.py:620
  8.8 1.1 %collective-permute-start.5 = (bf16[512,768]{1,0:T(8,128)(2,1)S(1)}, bf16[512,768]{1,0:T(8,128)(2,1)S(1)}, u32[]{:S(2)}, u32[]{:S(2)}) collective-permute-start(bf16[512,768]{1,0:T(8,128)(2,1)S(1)} %join_queries.1.refs_1_.refs_4_.refs_2_), channel_id=1, source_target_pairs={{0,1},{1,0},{2,3},{3,2},{4,5},{5,4},{6,7},{7,6},{8,9},{9,8},{10,11... | collective-permute-start | bytes 2359304 | tf_op jit(solution)/shard_map/ppermute | solution.py:50
  9.9 1.7 %plan.1 = (f32[6,16,256]{2,1,0:T(8,128)S(1)}, s32[8,128]{1,0:T(8,128)S(1)}) custom-call(s32[1,4]{1,0:T(1,128)S(1)} %bitcast.2, s32[1,2]{1,0:T(1,128)S(1)} %copy-done.2, s32[16]{0:T(128)S(1)} %copy-done.3, f32[6,16,16]{2,1,0:T(8,128)S(1)} %copy-done, bf16[528,768]{1,0:T(8,128)(2,1)S(1)} %collective-permute-done.refs_4_.refs_2_.refs_5_.refs_6_), custom_call_target="tpu_custom_call" | custom-call | tf_op jit(solution)/shard_map/plan/pallas_call | solution.py:38
  11.5 0.0 collective-permute-done.1.refs_1_.refs_2_.refs_3_
  11.6 0.1 release.1
  11.6 0.7 %collective-permute-start.2 = (bf16[256,768]{1,0:T(8,128)(2,1)S(1)}, bf16[256,768]{1,0:T(8,128)(2,1)S(1)}, u32[]{:S(2)}, u32[]{:S(2)}) collective-permute-start(bf16[256,768]{1,0:T(8,128)(2,1)S(1)} %get-tuple-element.28), channel_id=1, source_target_pairs={{7,4},{15,12},{23,20},{31,28}} | collective-permute-start | bytes 1179656 | tf_op jit(solution)/shard_map/ppermute | solution.py:71
  12.3 0.7 %collective-permute-start.3 = (bf16[256,768]{1,0:T(8,128)(2,1)S(1)}, bf16[256,768]{1,0:T(8,128)(2,1)S(1)}, u32[]{:S(2)}, u32[]{:S(2)}) collective-permute-start(bf16[256,768]{1,0:T(8,128)(2,1)S(1)} %get-tuple-element.29), channel_id=1, source_target_pairs={{1,2},{3,4},{5,6},{9,10},{11,12},{13,14},{17,18},{19,20},{21,22},{... | collective-permute-start | bytes 1179656 | tf_op jit(solution)/shard_map/ppermute | solution.py:55
  13.0 4.8 %collective-permute-done.4.refs_2_ = bf16[3,2,128,384]{3,2,1,0:T(8,128)(2,1)S(1)} collective-permute-done((bf16[3,2,128,384]{3,2,1,0:T(8,128)(2,1)S(1)}, bf16[3,2,128,384]{3,2,1,0:T(8,128)(2,1)S(1)}, u32[]{:S(2)}, u32[]{:S(2)}) %collective-permute-start.4) | collective-permute-done | bytes 589856 | tf_op jit(solution)/shard_map/ppermute | solution.py:50
  17.8 0.0 collective-permute-done.5.refs_4_.refs_5_.refs_2_
  17.8 0.3 step.1.refs_1_
  18.1 1.6 %collective-permute-start.6 = (bf16[3,2,128,384]{3,2,1,0:T(8,128)(2,1)S(1)}, bf16[3,2,128,384]{3,2,1,0:T(8,128)(2,1)S(1)}, u32[]{:S(2)}, u32[]{:S(2)}) collective-permute-start(bf16[3,2,128,384]{3,2,1,0:T(8,128)(2,1)S(1)} %step.1.refs_1_), channel_id=1, source_target_pairs={{0,4},{1,3},{2,6},{3,1},{4,0},{5,7},{6,2},{7,5},{8,12},{9,11},{10,... | collective-permute-start | bytes 1769480 | tf_op jit(solution)/shard_map/ppermute | solution.py:50
  19.7 0.0 collective-permute-done.2.refs_3_.refs_4_
  19.7 1.5 %stats.1 = (f32[6,8,256]{2,1,0:T(8,128)S(1)}, bf16[256,768]{1,0:T(8,128)(2,1)S(1)}, bf16[256,768]{1,0:T(8,128)(2,1)S(1)}) custom-call(f32[6,16,256]{2,1,0:T(8,128)S(1)} %get-tuple-element.26.refs_0_.refs_1_, bf16[512,768]{1,0:T(8,128)(2,1)S(1)} %join_queries.1.refs_1_.refs_4_.refs_2_, bf16[256,768]{1,0:T(8,128)(2,1)S(1)} %collective-permute-done.1.refs_1_.refs_2_.refs_3_, ...), custom_call_target="tpu_custom_call" | custom-call | flops 20132659200 | tf_op jit(solution)/shard_map/stats/pallas_call | solution.py:38
  21.3 4.5 %collective-permute-start.8 = (f32[6,8,256]{2,1,0:T(8,128)S(1)}, f32[6,8,256]{2,1,0:T(8,128)S(1)}, u32[]{:S(2)}, u32[]{:S(2)}) collective-permute-start(f32[6,8,256]{2,1,0:T(8,128)S(1)} %get-tuple-element.30.refs_2_.refs_1_), channel_id=1, source_target_pairs={{0,1},{1,0},{2,3},{3,2},{4,5},{5,4},{6,7},{7,6},{8,9},{9,8},{10,11... | collective-permute-start | bytes 147464 | tf_op jit(solution)/shard_map/ppermute | solution.py:50
  25.8 0.7 %collective-permute-start.10 = (bf16[256,768]{1,0:T(8,128)(2,1)S(1)}, bf16[256,768]{1,0:T(8,128)(2,1)S(1)}, u32[]{:S(2)}, u32[]{:S(2)}) collective-permute-start(bf16[256,768]{1,0:T(8,128)(2,1)S(1)} %get-tuple-element.37), channel_id=1, source_target_pairs={{2,1},{4,3},{6,5},{10,9},{12,11},{14,13},{18,17},{20,19},{22,21},{... | collective-permute-start | bytes 1179656 | tf_op jit(solution)/shard_map/ppermute | solution.py:55
  26.5 1.3 %collective-permute-start.12 = (bf16[256,768]{1,0:T(8,128)(2,1)S(1)}, bf16[256,768]{1,0:T(8,128)(2,1)S(1)}, u32[]{:S(2)}, u32[]{:S(2)}) collective-permute-start(bf16[256,768]{1,0:T(8,128)(2,1)S(1)} %get-tuple-element.41), channel_id=1, source_target_pairs={{2,1},{4,0},{6,5},{10,9},{12,8},{14,13},{18,17},{20,16},{22,21},{2... | collective-permute-start | bytes 1179656 | tf_op jit(solution)/shard_map/ppermute | solution.py:66
  27.8 0.3 collective-permute-done.6.refs_2_
  28.1 0.3 pick.1
  28.4 2.5 %collective-permute-start.7 = (bf16[2,2,128,384]{3,2,1,0:T(8,128)(2,1)S(1)}, bf16[2,2,128,384]{3,2,1,0:T(8,128)(2,1)S(1)}, u32[]{:S(2)}, u32[]{:S(2)}) collective-permute-start(bf16[2,2,128,384]{3,2,1,0:T(8,128)(2,1)S(1)} %get-tuple-element.32.refs_7_), channel_id=1, source_target_pairs={{0,1},{1,0},{2,3},{3,2},{4,5},{5,4},{6,7},{7,6},{8,9},{9,8},{10,11... | collective-permute-start | bytes 1179656 | tf_op jit(solution)/shard_map/ppermute | solution.py:50
  30.9 0.0 collective-permute-done.8.refs_3_
  30.9 1.9 %memory.1 = (f32[4,2,128,384]{3,2,1,0:T(8,128)S(1)}, bf16[3,2,128,384]{3,2,1,0:T(8,128)(2,1)S(1)}) custom-call(s32[8,128]{1,0:T(8,128)S(1)} %get-tuple-element.27.refs_2_.refs_3_.refs_0_, f32[6,16,256]{2,1,0:T(8,128)S(1)} %get-tuple-element.26.refs_0_.refs_1_, f32[6,8,256]{2,1,0:T(8,128)S(1)} %get-tuple-element.30.refs_2_.refs_1_, ...), custom_call_target="tpu_custom_call" | custom-call | flops 20132659200 | tf_op jit(solution)/shard_map/memory/pallas_call | solution.py:38
  32.8 2.6 %collective-permute-start.9 = (bf16[3,2,128,384]{3,2,1,0:T(8,128)(2,1)S(1)}, bf16[3,2,128,384]{3,2,1,0:T(8,128)(2,1)S(1)}, u32[]{:S(2)}, u32[]{:S(2)}) collective-permute-start(bf16[3,2,128,384]{3,2,1,0:T(8,128)(2,1)S(1)} %get-tuple-element.33.refs_6_), channel_id=1, source_target_pairs={{0,4},{1,3},{2,6},{3,1},{4,0},{5,7},{6,2},{7,5},{8,12},{9,11},{10,... | collective-permute-start | bytes 1769480 | tf_op jit(solution)/shard_map/ppermute | solution.py:50
  35.4 0.0 collective-permute-done.7.refs_5_.refs_9_
  35.4 2.4 %own.1 = (f32[2,256,768]{2,1,0:T(8,128)S(1)}, f32[6,8,256]{2,1,0:T(8,128)S(1)}) custom-call(f32[6,16,256]{2,1,0:T(8,128)S(1)} %get-tuple-element.26.refs_0_.refs_1_, f32[6,8,256]{2,1,0:T(8,128)S(1)} %get-tuple-element.30.refs_2_.refs_1_, bf16[512,768]{1,0:T(8,128)(2,1)S(1)} %join_queries.1.refs_1_.refs_4_.refs_2_, ...), custom_call_target="tpu_custom_call" | custom-call | flops 20132659200 | tf_op jit(solution)/shard_map/own/pallas_call | solution.py:38
  37.8 1.3 %collective-permute-start.11 = (f32[6,8,256]{2,1,0:T(8,128)S(1)}, f32[6,8,256]{2,1,0:T(8,128)S(1)}, u32[]{:S(2)}, u32[]{:S(2)}) collective-permute-start(f32[6,8,256]{2,1,0:T(8,128)S(1)} %get-tuple-element.34.refs_1_), channel_id=1, source_target_pairs={{1,0},{2,1},{3,2},{4,3},{5,4},{6,5},{7,6},{9,8},{10,9},{11,10},{12... | collective-permute-start | bytes 147464 | tf_op jit(solution)/shard_map/ppermute | solution.py:703
  39.1 0.0 collective-permute-done.12.refs_0_.refs_4_
  39.2 3.9 %collective-permute-start.13 = (bf16[256,768]{1,0:T(8,128)(2,1)S(1)}, bf16[256,768]{1,0:T(8,128)(2,1)S(1)}, u32[]{:S(2)}, u32[]{:S(2)}) collective-permute-start(bf16[256,768]{1,0:T(8,128)(2,1)S(1)} %pass_on.1), channel_id=1, source_target_pairs={{0,3},{8,11},{16,19},{24,27}} | collective-permute-start | bytes 1179656 | tf_op jit(solution)/shard_map/ppermute | solution.py:71
  43.0 2.0 %collective-permute-done.9.refs_1_ = bf16[3,2,128,384]{3,2,1,0:T(8,128)(2,1)S(1)} collective-permute-done((bf16[3,2,128,384]{3,2,1,0:T(8,128)(2,1)S(1)}, bf16[3,2,128,384]{3,2,1,0:T(8,128)(2,1)S(1)}, u32[]{:S(2)}, u32[]{:S(2)}) %collective-permute-start.9) | collective-permute-done | bytes 589856 | tf_op jit(solution)/shard_map/ppermute | solution.py:50
  45.0 0.2 add.1
  45.2 0.7 %collective-permute-start.14 = (bf16[3,2,128,384]{3,2,1,0:T(8,128)(2,1)S(1)}, bf16[3,2,128,384]{3,2,1,0:T(8,128)(2,1)S(1)}, u32[]{:S(2)}, u32[]{:S(2)}) collective-permute-start(bf16[3,2,128,384]{3,2,1,0:T(8,128)(2,1)S(1)} %get-tuple-element.38.refs_10_), channel_id=1, source_target_pairs={{0,2},{1,5},{2,0},{3,7},{4,6},{5,1},{6,4},{7,3},{8,10},{9,13},{10,... | collective-permute-start | bytes 1769480 | tf_op jit(solution)/shard_map/ppermute | solution.py:50
  46.0 3.8 %attend.1 = (bf16[256,768]{1,0:T(8,128)(2,1)}, bf16[256,768]{1,0:T(8,128)(2,1)}, f32[8,128]{1,0:T(8,128)S(1)}) custom-call(f32[6,16,256]{2,1,0:T(8,128)S(1)} %get-tuple-element.26.refs_0_.refs_1_, f32[6,8,256]{2,1,0:T(8,128)S(1)} %get-tuple-element.34.refs_1_, bf16[512,768]{1,0:T(8,128)(2,1)S(1)} %join_queries.1.refs_1_.refs_4_.refs_2_, ...), custom_call_target="tpu_custom_call" | custom-call | flops 20132659200 | tf_op jit(solution)/shard_map/attend/pallas_call | solution.py:38
  49.8 0.0 collective-permute-done.11.refs_1_
  49.8 0.0 collective-permute-done.13.refs_5_
  49.8 1.2 %next.1.refs_3_.refs_0_ = f32[2,256,768]{2,1,0:T(8,128)S(1)} custom-call(f32[6,16,256]{2,1,0:T(8,128)S(1)} %get-tuple-element.26.refs_0_.refs_1_, f32[6,8,256]{2,1,0:T(8,128)S(1)} %collective-permute-done.11.refs_1_, bf16[512,768]{1,0:T(8,128)(2,1)S(1)} %collective-permute-done.5.refs_4_.refs_5_.refs_2_, ...), custom_call_target="tpu_custom_call" | custom-call | flops 20132659200 | tf_op jit(solution)/shard_map/next/pallas_call | solution.py:38
  51.0 4.2 %collective-permute-done.14.refs_2_ = bf16[3,2,128,384]{3,2,1,0:T(8,128)(2,1)S(1)} collective-permute-done((bf16[3,2,128,384]{3,2,1,0:T(8,128)(2,1)S(1)}, bf16[3,2,128,384]{3,2,1,0:T(8,128)(2,1)S(1)}, u32[]{:S(2)}, u32[]{:S(2)}) %collective-permute-start.14) | collective-permute-done | bytes 589856 | tf_op jit(solution)/shard_map/ppermute | solution.py:50
  55.2 0.3 owned.1
  55.5 0.2 collective-permute-start.15
  55.7 1.6 %collective-permute-done.15.refs_2_ = bf16[2,2,128,384]{3,2,1,0:T(8,128)(2,1)S(1)} collective-permute-done((bf16[2,2,128,384]{3,2,1,0:T(8,128)(2,1)S(1)}, bf16[2,2,128,384]{3,2,1,0:T(8,128)(2,1)S(1)}, u32[]{:S(2)}, u32[]{:S(2)}) %collective-permute-start.15) | collective-permute-done | bytes 393248 | tf_op jit(solution)/shard_map/ppermute | solution.py:50
  57.3 1.0 %final.1 = (bf16[256,768]{1,0:T(8,128)(2,1)}, bf16[256,768]{1,0:T(8,128)(2,1)}) custom-call(f32[2,256,768]{2,1,0:T(8,128)S(1)} %next.1.refs_3_.refs_0_, f32[2,2,128,384]{3,2,1,0:T(8,128)S(1)} %get-tuple-element.44.refs_1_, bf16[2,2,128,384]{3,2,1,0:T(8,128)(2,1)S(1)} %collective-permute-done.15.refs_2_), custom_call_target="tpu_custom_call" | custom-call | tf_op jit(solution)/shard_map/final/pallas_call | solution.py:38
  (10 shorter events, 0.0 us)
Async XLA Ops:
  0.6 1.8 %copy-start.4 = (bf16[256,768]{1,0:T(8,128)(2,1)S(1)}, bf16[256,768]{1,0:T(8,128)(2,1)}, u32[]{:S(2)}) copy-start(bf16[256,768]{1,0:T(8,128)(2,1)} %refs_1_.3) | copy-start | bytes 1179652
  0.6 3.7 %copy-start.1 = (s32[4]{0:T(128)S(1)}, s32[4]{0:T(128)}, u32[]{:S(2)}) copy-start(s32[4]{0:T(128)} %param.15) | copy-start | bytes 52
  1.9 2.5 %collective-permute-start = (bf16[528,768]{1,0:T(8,128)(2,1)S(1)}, bf16[528,768]{1,0:T(8,128)(2,1)S(1)}, u32[]{:S(2)}, u32[]{:S(2)}) collective-permute-start(bf16[528,768]{1,0:T(8,128)(2,1)S(1)} %join.1.refs_1_.refs_0_.refs_6_.refs_3_.refs_7_), channel_id=1, source_target_pairs={{0,1},{1,0},{2,3},{3,2},{4,5},{5,4},{6,7},{7,6},{8,9},{9,8},{10,11... | collective-permute-start | bytes 2433032 | tf_op jit(solution)/shard_map/ppermute | solution.py:50
  2.4 9.2 %collective-permute-start.1 = (bf16[256,768]{1,0:T(8,128)(2,1)S(1)}, bf16[256,768]{1,0:T(8,128)(2,1)S(1)}, u32[]{:S(2)}, u32[]{:S(2)}) collective-permute-start(bf16[256,768]{1,0:T(8,128)(2,1)S(1)} %copy-done.4), channel_id=1, source_target_pairs={{1,2},{3,7},{5,6},{9,10},{11,15},{13,14},{17,18},{19,23},{21,22},{... | collective-permute-start | bytes 1179656 | tf_op jit(solution)/shard_map/ppermute | solution.py:66
  4.7 5.2 %copy-start = (f32[6,16,16]{2,1,0:T(8,128)S(1)}, f32[6,16,16]{2,1,0:T(8,128)}, u32[]{:S(2)}) copy-start(f32[6,16,16]{2,1,0:T(8,128)} %refs_3_.1) | copy-start | bytes 18436
  4.7 5.2 %copy-start.2 = (s32[1,2]{1,0:T(1,128)S(1)}, s32[1,2]{1,0:T(1,128)}, u32[]{:S(2)}) copy-start(s32[1,2]{1,0:T(1,128)} %refs_1_.4) | copy-start | bytes 28
  4.7 5.2 %copy-start.3 = (s32[16]{0:T(128)S(1)}, s32[16]{0:T(128)}, u32[]{:S(2)}) copy-start(s32[16]{0:T(128)} %refs_2_.3) | copy-start | bytes 196
  4.7 13.1 %collective-permute-start.4 = (bf16[3,2,128,384]{3,2,1,0:T(8,128)(2,1)S(1)}, bf16[3,2,128,384]{3,2,1,0:T(8,128)(2,1)S(1)}, u32[]{:S(2)}, u32[]{:S(2)}) collective-permute-start(bf16[3,2,128,384]{3,2,1,0:T(8,128)(2,1)S(1)} %split.1.refs_2_.refs_1_), channel_id=1, source_target_pairs={{0,2},{1,5},{2,0},{3,7},{4,6},{5,1},{6,4},{7,3},{8,10},{9,13},{10,... | collective-permute-start | bytes 1769480 | tf_op jit(solution)/shard_map/ppermute | solution.py:50
  8.8 9.1 %collective-permute-start.5 = (bf16[512,768]{1,0:T(8,128)(2,1)S(1)}, bf16[512,768]{1,0:T(8,128)(2,1)S(1)}, u32[]{:S(2)}, u32[]{:S(2)}) collective-permute-start(bf16[512,768]{1,0:T(8,128)(2,1)S(1)} %join_queries.1.refs_1_.refs_4_.refs_2_), channel_id=1, source_target_pairs={{0,1},{1,0},{2,3},{3,2},{4,5},{5,4},{6,7},{7,6},{8,9},{9,8},{10,11... | collective-permute-start | bytes 2359304 | tf_op jit(solution)/shard_map/ppermute | solution.py:50
  11.6 8.1 %collective-permute-start.2 = (bf16[256,768]{1,0:T(8,128)(2,1)S(1)}, bf16[256,768]{1,0:T(8,128)(2,1)S(1)}, u32[]{:S(2)}, u32[]{:S(2)}) collective-permute-start(bf16[256,768]{1,0:T(8,128)(2,1)S(1)} %get-tuple-element.28), channel_id=1, source_target_pairs={{7,4},{15,12},{23,20},{31,28}} | collective-permute-start | bytes 1179656 | tf_op jit(solution)/shard_map/ppermute | solution.py:71
  12.3 7.4 %collective-permute-start.3 = (bf16[256,768]{1,0:T(8,128)(2,1)S(1)}, bf16[256,768]{1,0:T(8,128)(2,1)S(1)}, u32[]{:S(2)}, u32[]{:S(2)}) collective-permute-start(bf16[256,768]{1,0:T(8,128)(2,1)S(1)} %get-tuple-element.29), channel_id=1, source_target_pairs={{1,2},{3,4},{5,6},{9,10},{11,12},{13,14},{17,18},{19,20},{21,22},{... | collective-permute-start | bytes 1179656 | tf_op jit(solution)/shard_map/ppermute | solution.py:55
  18.1 9.9 %collective-permute-start.6 = (bf16[3,2,128,384]{3,2,1,0:T(8,128)(2,1)S(1)}, bf16[3,2,128,384]{3,2,1,0:T(8,128)(2,1)S(1)}, u32[]{:S(2)}, u32[]{:S(2)}) collective-permute-start(bf16[3,2,128,384]{3,2,1,0:T(8,128)(2,1)S(1)} %step.1.refs_1_), channel_id=1, source_target_pairs={{0,4},{1,3},{2,6},{3,1},{4,0},{5,7},{6,2},{7,5},{8,12},{9,11},{10,... | collective-permute-start | bytes 1769480 | tf_op jit(solution)/shard_map/ppermute | solution.py:50
  21.3 9.6 %collective-permute-start.8 = (f32[6,8,256]{2,1,0:T(8,128)S(1)}, f32[6,8,256]{2,1,0:T(8,128)S(1)}, u32[]{:S(2)}, u32[]{:S(2)}) collective-permute-start(f32[6,8,256]{2,1,0:T(8,128)S(1)} %get-tuple-element.30.refs_2_.refs_1_), channel_id=1, source_target_pairs={{0,1},{1,0},{2,3},{3,2},{4,5},{5,4},{6,7},{7,6},{8,9},{9,8},{10,11... | collective-permute-start | bytes 147464 | tf_op jit(solution)/shard_map/ppermute | solution.py:50
  25.8 17.2 %collective-permute-start.10 = (bf16[256,768]{1,0:T(8,128)(2,1)S(1)}, bf16[256,768]{1,0:T(8,128)(2,1)S(1)}, u32[]{:S(2)}, u32[]{:S(2)}) collective-permute-start(bf16[256,768]{1,0:T(8,128)(2,1)S(1)} %get-tuple-element.37), channel_id=1, source_target_pairs={{2,1},{4,3},{6,5},{10,9},{12,11},{14,13},{18,17},{20,19},{22,21},{... | collective-permute-start | bytes 1179656 | tf_op jit(solution)/shard_map/ppermute | solution.py:55
  26.5 12.6 %collective-permute-start.12 = (bf16[256,768]{1,0:T(8,128)(2,1)S(1)}, bf16[256,768]{1,0:T(8,128)(2,1)S(1)}, u32[]{:S(2)}, u32[]{:S(2)}) collective-permute-start(bf16[256,768]{1,0:T(8,128)(2,1)S(1)} %get-tuple-element.41), channel_id=1, source_target_pairs={{2,1},{4,0},{6,5},{10,9},{12,8},{14,13},{18,17},{20,16},{22,21},{2... | collective-permute-start | bytes 1179656 | tf_op jit(solution)/shard_map/ppermute | solution.py:66
  28.4 7.0 %collective-permute-start.7 = (bf16[2,2,128,384]{3,2,1,0:T(8,128)(2,1)S(1)}, bf16[2,2,128,384]{3,2,1,0:T(8,128)(2,1)S(1)}, u32[]{:S(2)}, u32[]{:S(2)}) collective-permute-start(bf16[2,2,128,384]{3,2,1,0:T(8,128)(2,1)S(1)} %get-tuple-element.32.refs_7_), channel_id=1, source_target_pairs={{0,1},{1,0},{2,3},{3,2},{4,5},{5,4},{6,7},{7,6},{8,9},{9,8},{10,11... | collective-permute-start | bytes 1179656 | tf_op jit(solution)/shard_map/ppermute | solution.py:50
  32.8 12.2 %collective-permute-start.9 = (bf16[3,2,128,384]{3,2,1,0:T(8,128)(2,1)S(1)}, bf16[3,2,128,384]{3,2,1,0:T(8,128)(2,1)S(1)}, u32[]{:S(2)}, u32[]{:S(2)}) collective-permute-start(bf16[3,2,128,384]{3,2,1,0:T(8,128)(2,1)S(1)} %get-tuple-element.33.refs_6_), channel_id=1, source_target_pairs={{0,4},{1,3},{2,6},{3,1},{4,0},{5,7},{6,2},{7,5},{8,12},{9,11},{10,... | collective-permute-start | bytes 1769480 | tf_op jit(solution)/shard_map/ppermute | solution.py:50
  37.8 11.9 %collective-permute-start.11 = (f32[6,8,256]{2,1,0:T(8,128)S(1)}, f32[6,8,256]{2,1,0:T(8,128)S(1)}, u32[]{:S(2)}, u32[]{:S(2)}) collective-permute-start(f32[6,8,256]{2,1,0:T(8,128)S(1)} %get-tuple-element.34.refs_1_), channel_id=1, source_target_pairs={{1,0},{2,1},{3,2},{4,3},{5,4},{6,5},{7,6},{9,8},{10,9},{11,10},{12... | collective-permute-start | bytes 147464 | tf_op jit(solution)/shard_map/ppermute | solution.py:703
  39.2 10.6 %collective-permute-start.13 = (bf16[256,768]{1,0:T(8,128)(2,1)S(1)}, bf16[256,768]{1,0:T(8,128)(2,1)S(1)}, u32[]{:S(2)}, u32[]{:S(2)}) collective-permute-start(bf16[256,768]{1,0:T(8,128)(2,1)S(1)} %pass_on.1), channel_id=1, source_target_pairs={{0,3},{8,11},{16,19},{24,27}} | collective-permute-start | bytes 1179656 | tf_op jit(solution)/shard_map/ppermute | solution.py:71
  45.2 9.9 %collective-permute-start.14 = (bf16[3,2,128,384]{3,2,1,0:T(8,128)(2,1)S(1)}, bf16[3,2,128,384]{3,2,1,0:T(8,128)(2,1)S(1)}, u32[]{:S(2)}, u32[]{:S(2)}) collective-permute-start(bf16[3,2,128,384]{3,2,1,0:T(8,128)(2,1)S(1)} %get-tuple-element.38.refs_10_), channel_id=1, source_target_pairs={{0,2},{1,5},{2,0},{3,7},{4,6},{5,1},{6,4},{7,3},{8,10},{9,13},{10,... | collective-permute-start | bytes 1769480 | tf_op jit(solution)/shard_map/ppermute | solution.py:50
  55.5 1.8 %collective-permute-start.15 = (bf16[2,2,128,384]{3,2,1,0:T(8,128)(2,1)S(1)}, bf16[2,2,128,384]{3,2,1,0:T(8,128)(2,1)S(1)}, u32[]{:S(2)}, u32[]{:S(2)}) collective-permute-start(bf16[2,2,128,384]{3,2,1,0:T(8,128)(2,1)S(1)} %get-tuple-element.45), channel_id=1, source_target_pairs={{0,1},{1,0},{2,3},{3,2},{4,5},{5,4},{6,7},{7,6},{8,9},{9,8},{10,11... | collective-permute-start | bytes 1179656 | tf_op jit(solution)/shard_map/ppermute | solution.py:50

commit v18 on v16

--- a/solution.py
+++ b/solution.py
@@ -164,18 +164,12 @@
     pair_index_ref,
     pose_ref,
     bias_ref,
-    value_ref,
-    direct_keys,
     rows_ref,
     codes_ref,
-    values_out,
-    keys_out,
 ):
     me = lax.axis_index("tm")
     last_frame = peers * FR_DEV - 1
     heads, _, row_count = rows_ref.shape
-    values_out[...] = value_ref[...]
-    keys_out[...] = direct_keys[...]
     bank = [bank_ref[0, slot] for slot in range(bank_ref.shape[1])]
     pair_ids = [bank_ref[0, pair_index_ref[0, m]] for m in range(MEM)]
     mem_ids = [bank_ref[0, index_ref[0, m]] for m in range(MEM)]
@@ -221,6 +215,11 @@
         codes_ref[row : row + 1, :] = jnp.full((1, lanes), code, jnp.int32)
 
 
+def release_kernel(value_ref, direct_keys, values_out, keys_out):
+    values_out[...] = value_ref[...]
+    keys_out[...] = direct_keys[...]
+
+
 def split_kernel(peers, bank_ref, key_ref, value_ref, pair_keys, pair_values, out_ref):
     me = lax.axis_index("tm")
     frame_len, half_width = out_ref.shape[2:]
@@ -630,13 +629,20 @@
     pair_queries = swap(queries, 1, 1, peers)
 
     bias_rows = -(-(5 * FR_DEV) // 8) * 8
-    rows, codes, values_out, keys_out = call(
+    rows, codes = call(
         functools.partial(plan_kernel, peers, last_bits),
-        [shape(F32, heads, bias_rows, row_count), shape(jnp.int32, 8, 128)] + [shape(BF16, row_count, width)] * 2,
+        [shape(F32, heads, bias_rows, row_count), shape(jnp.int32, 8, 128)],
+        [],
+        scalars=[bank_frames, memory_index, pair_index, camera_pose, pose_bias],
+        name="plan",
+    )
+    values_out, keys_out = call(
+        release_kernel,
+        [rows_shape] * 2,
         [values, direct_keys],
-        scalars=[bank_frames, memory_index, pair_index, camera_pose, pose_bias],
+        after=[codes],
         flops=HIDING * piece_flops,
-        name="plan",
+        name="release",
     )
     outer = [direct_keys, shift_second(keys_out, 1, 1, peers), shift(values_out, 1, 1, peers)]
     even_done = odd_done = 1

time: 61.7 us -> 60 us (0.972)
  starting transfers between devices: 30.5 us -> 28.9 us
    ppermute x11, starting transfers between devices: 21.3 us -> 19.7 us  [swap(): lax.ppermute(block, 'tm', [(i, i ^ (odd_bit if i & 1 else even_bit)) for...]
    pallas_call x13 -> x14, Pallas kernels: 14.7 us -> 14.7 us  [call(): pl.pallas_call(run, out_shape=outs, in_specs=[SMEM] * len(scalars) + [VME...]
  transfers between devices with their start and end apart: 18 -> 18, of which waited for: 6 -> 6; matrix products, arithmetic and copies ran while one was open for 0% -> 0% of each run, Pallas kernels for 25% -> 26%
where the time goes in v18:
time: 60 us; the launch traced here: 59.8 us
  starting transfers between devices  28.9 us (48%)
  Pallas kernels  17 us (28%)
  waiting for transfers between devices  13 us (22%)
  between operations  0.85 us (1%)
    ppermute x11, starting transfers between devices, swap(): lax.ppermute(block, 'tm', [(i, i ^ (odd_bit if i & 1 else even_bit)) for...  19.7 us
    pallas_call x14, Pallas kernels, call(): pl.pallas_call(run, out_shape=outs, in_specs=[SMEM] * len(scalars) + [VME...  14.7 us
    ppermute x11, waiting for transfers between devices, swap(): lax.ppermute(block, 'tm', [(i, i ^ (odd_bit if i & 1 else even_bit)) for...  13 us
    ppermute x2, starting transfers between devices, shift_second(): return lax.ppermute(block, 'tm', pairs) if pairs else block  4.57 us
    pallas_call x2, Pallas kernels, load(): pl.pallas_call(run, out_shape=outs, in_specs=[pl.BlockSpec(memory_space=p...  2.28 us
    ppermute x2, starting transfers between devices, shift_first(): lax.ppermute(block, 'tm', [(i, relays.get((i, j), j)) for i, j in pairs])  1.98 us
    ppermute x2, starting transfers between devices, shift(): return lax.ppermute(block, 'tm', pairs)  1.36 us
    ppermute x1, starting transfers between devices, body(): lax.ppermute(stats_all, 'tm', [(i, i - 1) for i in range(1, peers)])  1.29 us
  transfers between devices with their start and end apart: 18, of which 6 were waited for; matrix products, arithmetic and copies ran while one was open for 0% of the time, Pallas kernels for 26%

profile of v18, /device:TPU:0, one launch (start us, length us, event | category | flops | bytes accessed | tf_op | source)
XLA Modules:
  0.0 59.8 jit_solution(8869905848934912204)
XLA Ops:
  0.6 0.5 collective-permute-start
  1.1 0.1 collective-permute-start.1
  1.2 1.1 %load.1 = (bf16[256,768]{1,0:T(8,128)(2,1)S(1)}, bf16[256,768]{1,0:T(8,128)(2,1)S(1)}, s32[1,4]{1,0:T(1,128)S(1)}) custom-call(bf16[256,768]{1,0:T(8,128)(2,1)} %refs_0_.2, bf16[256,768]{1,0:T(8,128)(2,1)} %refs_1_.3, s32[1,4]{1,0:T(1,128)} %bitcast.1), custom_call_target="tpu_custom_call" | custom-call | tf_op jit(solution)/shard_map/load/pallas_call | solution.py:601
  2.4 0.7 %collective-permute-start.3 = (bf16[256,768]{1,0:T(8,128)(2,1)S(1)}, bf16[256,768]{1,0:T(8,128)(2,1)S(1)}, u32[]{:S(2)}, u32[]{:S(2)}) collective-permute-start(bf16[256,768]{1,0:T(8,128)(2,1)S(1)} %get-tuple-element.32.refs_1_.refs_7_.refs_3_.refs_8_.refs_6_), channel_id=1, source_target_pairs={{1,2},{3,7},{5,6},{9,10},{11,15},{13,14},{17,18},{19,23},{21,22},{... | collective-permute-start | bytes 1179656 | tf_op jit(solution)/shard_map/ppermute | solution.py:65
  3.1 0.0 collective-permute-done.refs_3_.refs_5_.refs_6_
  3.1 0.2 collective-permute-done.1.refs_4_.refs_6_.refs_7_
  3.3 0.3 split.1.refs_3_.refs_1_
  3.6 3.5 %collective-permute-start.6 = (bf16[3,2,128,384]{3,2,1,0:T(8,128)(2,1)S(1)}, bf16[3,2,128,384]{3,2,1,0:T(8,128)(2,1)S(1)}, u32[]{:S(2)}, u32[]{:S(2)}) collective-permute-start(bf16[3,2,128,384]{3,2,1,0:T(8,128)(2,1)S(1)} %split.1.refs_3_.refs_1_), channel_id=1, source_target_pairs={{0,2},{1,5},{2,0},{3,7},{4,6},{5,1},{6,4},{7,3},{8,10},{9,13},{10,... | collective-permute-start | bytes 1769480 | tf_op jit(solution)/shard_map/ppermute | solution.py:49
  7.1 1.1 %load_queries.1 = (bf16[512,768]{1,0:T(8,128)(2,1)S(1)}, s32[1,2]{1,0:T(1,128)S(1)}) custom-call(bf16[256,768]{1,0:T(8,128)(2,1)} %refs_0_.3, bf16[256,768]{1,0:T(8,128)(2,1)} %refs_1_.4, s32[1,2]{1,0:T(1,128)} %refs_1_.5, bf16[3,2,128,384]{3,2,1,0:T(8,128)(2,1)S(1)} %split.1.refs_3_.refs_1_), custom_call_target="tpu_custom_call" | custom-call | tf_op jit(solution)/shard_map/load_queries/pallas_call | solution.py:601
  8.2 2.1 %collective-permute-start.2 = (s32[1,2]{1,0:T(1,128)S(1)}, s32[1,2]{1,0:T(1,128)S(1)}, u32[]{:S(2)}, u32[]{:S(2)}) collective-permute-start(s32[1,2]{1,0:T(1,128)S(1)} %get-tuple-element.34), channel_id=1, source_target_pairs={{0,1},{1,0},{2,3},{3,2},{4,5},{5,4},{6,7},{7,6},{8,9},{9,8},{10,11... | collective-permute-start | bytes 32 | tf_op jit(solution)/shard_map/ppermute | solution.py:49
  10.3 0.1 collective-permute-start.7
  10.4 0.7 %collective-permute-done.2.refs_2_ = s32[1,2]{1,0:T(1,128)S(1)} collective-permute-done((s32[1,2]{1,0:T(1,128)S(1)}, s32[1,2]{1,0:T(1,128)S(1)}, u32[]{:S(2)}, u32[]{:S(2)}) %collective-permute-start.2) | collective-permute-done | bytes 40 | tf_op jit(solution)/shard_map/ppermute | solution.py:49
  11.1 1.6 %plan.1 = (f32[6,16,256]{2,1,0:T(8,128)S(1)}, s32[8,128]{1,0:T(8,128)S(1)}) custom-call(s32[1,4]{1,0:T(1,128)S(1)} %bitcast.2, s32[1,2]{1,0:T(1,128)S(1)} %copy-done.1, s32[1,2]{1,0:T(1,128)S(1)} %collective-permute-done.2.refs_2_, s32[16]{0:T(128)S(1)} %copy-done.3, f32[6,16,16]{2,1,0:T(8,128)S(1)} %copy-done), custom_call_target="tpu_custom_call" | custom-call | tf_op jit(solution)/shard_map/plan/pallas_call | solution.py:37
  12.8 0.0 collective-permute-done.3.refs_1_.refs_2_.refs_3_
  12.8 0.1 release.1
  12.8 0.7 %collective-permute-start.4 = (bf16[256,768]{1,0:T(8,128)(2,1)S(1)}, bf16[256,768]{1,0:T(8,128)(2,1)S(1)}, u32[]{:S(2)}, u32[]{:S(2)}) collective-permute-start(bf16[256,768]{1,0:T(8,128)(2,1)S(1)} %get-tuple-element.38), channel_id=1, source_target_pairs={{7,4},{15,12},{23,20},{31,28}} | collective-permute-start | bytes 1179656 | tf_op jit(solution)/shard_map/ppermute | solution.py:70
  13.5 0.7 %collective-permute-start.5 = (bf16[256,768]{1,0:T(8,128)(2,1)S(1)}, bf16[256,768]{1,0:T(8,128)(2,1)S(1)}, u32[]{:S(2)}, u32[]{:S(2)}) collective-permute-start(bf16[256,768]{1,0:T(8,128)(2,1)S(1)} %get-tuple-element.39), channel_id=1, source_target_pairs={{1,2},{3,4},{5,6},{9,10},{11,12},{13,14},{17,18},{19,20},{21,22},{... | collective-permute-start | bytes 1179656 | tf_op jit(solution)/shard_map/ppermute | solution.py:54
  14.2 4.0 %collective-permute-done.6.refs_2_ = bf16[3,2,128,384]{3,2,1,0:T(8,128)(2,1)S(1)} collective-permute-done((bf16[3,2,128,384]{3,2,1,0:T(8,128)(2,1)S(1)}, bf16[3,2,128,384]{3,2,1,0:T(8,128)(2,1)S(1)}, u32[]{:S(2)}, u32[]{:S(2)}) %collective-permute-start.6) | collective-permute-done | bytes 589856 | tf_op jit(solution)/shard_map/ppermute | solution.py:49
  18.2 0.0 collective-permute-done.7.refs_4_.refs_5_.refs_2_
  18.2 0.3 step.1.refs_1_
  18.5 1.6 %collective-permute-start.8 = (bf16[3,2,128,384]{3,2,1,0:T(8,128)(2,1)S(1)}, bf16[3,2,128,384]{3,2,1,0:T(8,128)(2,1)S(1)}, u32[]{:S(2)}, u32[]{:S(2)}) collective-permute-start(bf16[3,2,128,384]{3,2,1,0:T(8,128)(2,1)S(1)} %step.1.refs_1_), channel_id=1, source_target_pairs={{0,4},{1,3},{2,6},{3,1},{4,0},{5,7},{6,2},{7,5},{8,12},{9,11},{10,... | collective-permute-start | bytes 1769480 | tf_op jit(solution)/shard_map/ppermute | solution.py:49
  20.1 0.0 collective-permute-done.4.refs_3_.refs_4_
  20.1 0.0 collective-permute-done.5.refs_4_.refs_5_
  20.1 1.5 %stats.1 = (f32[6,8,256]{2,1,0:T(8,128)S(1)}, bf16[256,768]{1,0:T(8,128)(2,1)S(1)}, bf16[256,768]{1,0:T(8,128)(2,1)S(1)}) custom-call(f32[6,16,256]{2,1,0:T(8,128)S(1)} %get-tuple-element.35.refs_0_.refs_1_, bf16[512,768]{1,0:T(8,128)(2,1)S(1)} %get-tuple-element.36.refs_1_.refs_4_.refs_2_, ...), custom_call_target="tpu_custom_call" | custom-call | flops 20132659200 | tf_op jit(solution)/shard_map/stats/pallas_call | solution.py:37
  21.6 5.6 %collective-permute-start.10 = (f32[6,8,256]{2,1,0:T(8,128)S(1)}, f32[6,8,256]{2,1,0:T(8,128)S(1)}, u32[]{:S(2)}, u32[]{:S(2)}) collective-permute-start(f32[6,8,256]{2,1,0:T(8,128)S(1)} %get-tuple-element.40.refs_2_.refs_1_), channel_id=1, source_target_pairs={{0,1},{1,0},{2,3},{3,2},{4,5},{5,4},{6,7},{7,6},{8,9},{9,8},{10,11... | collective-permute-start | bytes 147464 | tf_op jit(solution)/shard_map/ppermute | solution.py:49
  27.3 0.7 %collective-permute-start.12 = (bf16[256,768]{1,0:T(8,128)(2,1)S(1)}, bf16[256,768]{1,0:T(8,128)(2,1)S(1)}, u32[]{:S(2)}, u32[]{:S(2)}) collective-permute-start(bf16[256,768]{1,0:T(8,128)(2,1)S(1)} %get-tuple-element.47), channel_id=1, source_target_pairs={{2,1},{4,3},{6,5},{10,9},{12,11},{14,13},{18,17},{20,19},{22,21},{... | collective-permute-start | bytes 1179656 | tf_op jit(solution)/shard_map/ppermute | solution.py:54
  28.0 1.3 %collective-permute-start.14 = (bf16[256,768]{1,0:T(8,128)(2,1)S(1)}, bf16[256,768]{1,0:T(8,128)(2,1)S(1)}, u32[]{:S(2)}, u32[]{:S(2)}) collective-permute-start(bf16[256,768]{1,0:T(8,128)(2,1)S(1)} %get-tuple-element.51), channel_id=1, source_target_pairs={{2,1},{4,0},{6,5},{10,9},{12,8},{14,13},{18,17},{20,16},{22,21},{2... | collective-permute-start | bytes 1179656 | tf_op jit(solution)/shard_map/ppermute | solution.py:65
  29.3 0.0 collective-permute-done.8.refs_2_
  29.3 0.3 pick.1
  29.6 2.8 %collective-permute-start.9 = (bf16[2,2,128,384]{3,2,1,0:T(8,128)(2,1)S(1)}, bf16[2,2,128,384]{3,2,1,0:T(8,128)(2,1)S(1)}, u32[]{:S(2)}, u32[]{:S(2)}) collective-permute-start(bf16[2,2,128,384]{3,2,1,0:T(8,128)(2,1)S(1)} %get-tuple-element.42.refs_7_), channel_id=1, source_target_pairs={{0,1},{1,0},{2,3},{3,2},{4,5},{5,4},{6,7},{7,6},{8,9},{9,8},{10,11... | collective-permute-start | bytes 1179656 | tf_op jit(solution)/shard_map/ppermute | solution.py:49
  32.4 1.9 %memory.1 = (f32[4,2,128,384]{3,2,1,0:T(8,128)S(1)}, bf16[3,2,128,384]{3,2,1,0:T(8,128)(2,1)S(1)}) custom-call(s32[8,128]{1,0:T(8,128)S(1)} %get-tuple-element.37.refs_2_.refs_3_.refs_0_, f32[6,16,256]{2,1,0:T(8,128)S(1)} %get-tuple-element.35.refs_0_.refs_1_, f32[6,8,256]{2,1,0:T(8,128)S(1)} %get-tuple-element.40.refs_2_.refs_1_, ...), custom_call_target="tpu_custom_call" | custom-call | flops 20132659200 | tf_op jit(solution)/shard_map/memory/pallas_call | solution.py:37
  34.3 2.5 %collective-permute-start.11 = (bf16[3,2,128,384]{3,2,1,0:T(8,128)(2,1)S(1)}, bf16[3,2,128,384]{3,2,1,0:T(8,128)(2,1)S(1)}, u32[]{:S(2)}, u32[]{:S(2)}) collective-permute-start(bf16[3,2,128,384]{3,2,1,0:T(8,128)(2,1)S(1)} %get-tuple-element.43.refs_7_), channel_id=1, source_target_pairs={{0,4},{1,3},{2,6},{3,1},{4,0},{5,7},{6,2},{7,5},{8,12},{9,11},{10,... | collective-permute-start | bytes 1769480 | tf_op jit(solution)/shard_map/ppermute | solution.py:49
  36.8 0.0 collective-permute-done.9.refs_6_.refs_11_
  36.8 2.4 %own.1 = (f32[2,256,768]{2,1,0:T(8,128)S(1)}, f32[6,8,256]{2,1,0:T(8,128)S(1)}) custom-call(f32[6,16,256]{2,1,0:T(8,128)S(1)} %get-tuple-element.35.refs_0_.refs_1_, f32[6,8,256]{2,1,0:T(8,128)S(1)} %get-tuple-element.40.refs_2_.refs_1_, bf16[512,768]{1,0:T(8,128)(2,1)S(1)} %get-tuple-element.36.refs_1_.refs_4_.refs_2_, ...), custom_call_target="tpu_custom_call" | custom-call | flops 20132659200 | tf_op jit(solution)/shard_map/own/pallas_call | solution.py:37
  39.2 1.3 %collective-permute-start.13 = (f32[6,8,256]{2,1,0:T(8,128)S(1)}, f32[6,8,256]{2,1,0:T(8,128)S(1)}, u32[]{:S(2)}, u32[]{:S(2)}) collective-permute-start(f32[6,8,256]{2,1,0:T(8,128)S(1)} %get-tuple-element.44.refs_1_), channel_id=1, source_target_pairs={{1,0},{2,1},{3,2},{4,3},{5,4},{6,5},{7,6},{9,8},{10,9},{11,10},{12... | collective-permute-start | bytes 147464 | tf_op jit(solution)/shard_map/ppermute | solution.py:688
  40.5 0.0 collective-permute-done.14.refs_0_.refs_4_
  40.6 3.9 %collective-permute-start.15 = (bf16[256,768]{1,0:T(8,128)(2,1)S(1)}, bf16[256,768]{1,0:T(8,128)(2,1)S(1)}, u32[]{:S(2)}, u32[]{:S(2)}) collective-permute-start(bf16[256,768]{1,0:T(8,128)(2,1)S(1)} %pass_on.1), channel_id=1, source_target_pairs={{0,3},{8,11},{16,19},{24,27}} | collective-permute-start | bytes 1179656 | tf_op jit(solution)/shard_map/ppermute | solution.py:70
  44.5 0.0 collective-permute-done.12.refs_3_
  44.5 2.0 %collective-permute-done.11.refs_1_ = bf16[3,2,128,384]{3,2,1,0:T(8,128)(2,1)S(1)} collective-permute-done((bf16[3,2,128,384]{3,2,1,0:T(8,128)(2,1)S(1)}, bf16[3,2,128,384]{3,2,1,0:T(8,128)(2,1)S(1)}, u32[]{:S(2)}, u32[]{:S(2)}) %collective-permute-start.11) | collective-permute-done | bytes 589856 | tf_op jit(solution)/shard_map/ppermute | solution.py:49
  46.5 0.2 add.1
  46.6 0.7 %collective-permute-start.16 = (bf16[3,2,128,384]{3,2,1,0:T(8,128)(2,1)S(1)}, bf16[3,2,128,384]{3,2,1,0:T(8,128)(2,1)S(1)}, u32[]{:S(2)}, u32[]{:S(2)}) collective-permute-start(bf16[3,2,128,384]{3,2,1,0:T(8,128)(2,1)S(1)} %get-tuple-element.48.refs_12_), channel_id=1, source_target_pairs={{0,2},{1,5},{2,0},{3,7},{4,6},{5,1},{6,4},{7,3},{8,10},{9,13},{10,... | collective-permute-start | bytes 1769480 | tf_op jit(solution)/shard_map/ppermute | solution.py:49
  47.4 3.6 %attend.1 = (bf16[256,768]{1,0:T(8,128)(2,1)}, bf16[256,768]{1,0:T(8,128)(2,1)}, f32[8,128]{1,0:T(8,128)S(1)}) custom-call(f32[6,16,256]{2,1,0:T(8,128)S(1)} %get-tuple-element.35.refs_0_.refs_1_, f32[6,8,256]{2,1,0:T(8,128)S(1)} %get-tuple-element.44.refs_1_, bf16[512,768]{1,0:T(8,128)(2,1)S(1)} %get-tuple-element.36.refs_1_.refs_4_.refs_2_, ...), custom_call_target="tpu_custom_call" | custom-call | flops 20132659200 | tf_op jit(solution)/shard_map/attend/pallas_call | solution.py:37
  51.0 1.1 %next.1.refs_3_.refs_0_ = f32[2,256,768]{2,1,0:T(8,128)S(1)} custom-call(f32[6,16,256]{2,1,0:T(8,128)S(1)} %get-tuple-element.35.refs_0_.refs_1_, f32[6,8,256]{2,1,0:T(8,128)S(1)} %collective-permute-done.13.refs_1_, bf16[512,768]{1,0:T(8,128)(2,1)S(1)} %collective-permute-done.7.refs_4_.refs_5_.refs_2_, ...), custom_call_target="tpu_custom_call" | custom-call | flops 20132659200 | tf_op jit(solution)/shard_map/next/pallas_call | solution.py:37
  52.1 4.5 %collective-permute-done.16.refs_2_ = bf16[3,2,128,384]{3,2,1,0:T(8,128)(2,1)S(1)} collective-permute-done((bf16[3,2,128,384]{3,2,1,0:T(8,128)(2,1)S(1)}, bf16[3,2,128,384]{3,2,1,0:T(8,128)(2,1)S(1)}, u32[]{:S(2)}, u32[]{:S(2)}) %collective-permute-start.16) | collective-permute-done | bytes 589856 | tf_op jit(solution)/shard_map/ppermute | solution.py:49
  56.6 0.3 owned.1
  57.0 0.2 collective-permute-start.17
  57.1 1.6 %collective-permute-done.17.refs_2_ = bf16[2,2,128,384]{3,2,1,0:T(8,128)(2,1)S(1)} collective-permute-done((bf16[2,2,128,384]{3,2,1,0:T(8,128)(2,1)S(1)}, bf16[2,2,128,384]{3,2,1,0:T(8,128)(2,1)S(1)}, u32[]{:S(2)}, u32[]{:S(2)}) %collective-permute-start.17) | collective-permute-done | bytes 393248 | tf_op jit(solution)/shard_map/ppermute | solution.py:49
  58.7 1.0 %final.1 = (bf16[256,768]{1,0:T(8,128)(2,1)}, bf16[256,768]{1,0:T(8,128)(2,1)}) custom-call(f32[2,256,768]{2,1,0:T(8,128)S(1)} %next.1.refs_3_.refs_0_, f32[2,2,128,384]{3,2,1,0:T(8,128)S(1)} %get-tuple-element.54.refs_1_, bf16[2,2,128,384]{3,2,1,0:T(8,128)(2,1)S(1)} %collective-permute-done.17.refs_2_), custom_call_target="tpu_custom_call" | custom-call | tf_op jit(solution)/shard_map/final/pallas_call | solution.py:37
  (12 shorter events, 0.1 us)
Async XLA Ops:
  0.6 2.4 %collective-permute-start = (bf16[256,768]{1,0:T(8,128)(2,1)}, bf16[256,768]{1,0:T(8,128)(2,1)S(1)}, u32[]{:S(2)}, u32[]{:S(2)}) collective-permute-start(bf16[256,768]{1,0:T(8,128)(2,1)} %refs_0_.2), channel_id=1, source_target_pairs={{0,1},{1,0},{2,3},{3,2},{4,5},{5,4},{6,7},{7,6},{8,9},{9,8},{10,11... | collective-permute-start | bytes 1179656 | tf_op jit(solution)/shard_map/ppermute | solution.py:49
  1.1 2.1 %collective-permute-start.1 = (bf16[256,768]{1,0:T(8,128)(2,1)}, bf16[256,768]{1,0:T(8,128)(2,1)S(1)}, u32[]{:S(2)}, u32[]{:S(2)}) collective-permute-start(bf16[256,768]{1,0:T(8,128)(2,1)} %refs_1_.3), channel_id=1, source_target_pairs={{0,1},{1,0},{2,3},{3,2},{4,5},{5,4},{6,7},{7,6},{8,9},{9,8},{10,11... | collective-permute-start | bytes 1179656 | tf_op jit(solution)/shard_map/ppermute | solution.py:49
  2.4 10.4 %collective-permute-start.3 = (bf16[256,768]{1,0:T(8,128)(2,1)S(1)}, bf16[256,768]{1,0:T(8,128)(2,1)S(1)}, u32[]{:S(2)}, u32[]{:S(2)}) collective-permute-start(bf16[256,768]{1,0:T(8,128)(2,1)S(1)} %get-tuple-element.32.refs_1_.refs_7_.refs_3_.refs_8_.refs_6_), channel_id=1, source_target_pairs={{1,2},{3,7},{5,6},{9,10},{11,15},{13,14},{17,18},{19,23},{21,22},{... | collective-permute-start | bytes 1179656 | tf_op jit(solution)/shard_map/ppermute | solution.py:65
  3.3 7.8 %copy-start = (f32[6,16,16]{2,1,0:T(8,128)S(1)}, f32[6,16,16]{2,1,0:T(8,128)}, u32[]{:S(2)}) copy-start(f32[6,16,16]{2,1,0:T(8,128)} %refs_4_.1) | copy-start | bytes 18436
  3.3 7.8 %copy-start.1 = (s32[1,2]{1,0:T(1,128)S(1)}, s32[1,2]{1,0:T(1,128)}, u32[]{:S(2)}) copy-start(s32[1,2]{1,0:T(1,128)} %refs_1_.5) | copy-start | bytes 28
  3.3 7.8 %copy-start.2 = (s32[4]{0:T(128)S(1)}, s32[4]{0:T(128)}, u32[]{:S(2)}) copy-start(s32[4]{0:T(128)} %param.15) | copy-start | bytes 52
  3.3 7.8 %copy-start.3 = (s32[16]{0:T(128)S(1)}, s32[16]{0:T(128)}, u32[]{:S(2)}) copy-start(s32[16]{0:T(128)} %refs_3_.1) | copy-start | bytes 196
  3.6 14.6 %collective-permute-start.6 = (bf16[3,2,128,384]{3,2,1,0:T(8,128)(2,1)S(1)}, bf16[3,2,128,384]{3,2,1,0:T(8,128)(2,1)S(1)}, u32[]{:S(2)}, u32[]{:S(2)}) collective-permute-start(bf16[3,2,128,384]{3,2,1,0:T(8,128)(2,1)S(1)} %split.1.refs_3_.refs_1_), channel_id=1, source_target_pairs={{0,2},{1,5},{2,0},{3,7},{4,6},{5,1},{6,4},{7,3},{8,10},{9,13},{10,... | collective-permute-start | bytes 1769480 | tf_op jit(solution)/shard_map/ppermute | solution.py:49
  8.2 2.9 %collective-permute-start.2 = (s32[1,2]{1,0:T(1,128)S(1)}, s32[1,2]{1,0:T(1,128)S(1)}, u32[]{:S(2)}, u32[]{:S(2)}) collective-permute-start(s32[1,2]{1,0:T(1,128)S(1)} %get-tuple-element.34), channel_id=1, source_target_pairs={{0,1},{1,0},{2,3},{3,2},{4,5},{5,4},{6,7},{7,6},{8,9},{9,8},{10,11... | collective-permute-start | bytes 32 | tf_op jit(solution)/shard_map/ppermute | solution.py:49
  10.3 8.0 %collective-permute-start.7 = (bf16[512,768]{1,0:T(8,128)(2,1)S(1)}, bf16[512,768]{1,0:T(8,128)(2,1)S(1)}, u32[]{:S(2)}, u32[]{:S(2)}) collective-permute-start(bf16[512,768]{1,0:T(8,128)(2,1)S(1)} %get-tuple-element.36.refs_1_.refs_4_.refs_2_), channel_id=1, source_target_pairs={{0,1},{1,0},{2,3},{3,2},{4,5},{5,4},{6,7},{7,6},{8,9},{9,8},{10,11... | collective-permute-start | bytes 2359304 | tf_op jit(solution)/shard_map/ppermute | solution.py:49
  12.8 7.3 %collective-permute-start.4 = (bf16[256,768]{1,0:T(8,128)(2,1)S(1)}, bf16[256,768]{1,0:T(8,128)(2,1)S(1)}, u32[]{:S(2)}, u32[]{:S(2)}) collective-permute-start(bf16[256,768]{1,0:T(8,128)(2,1)S(1)} %get-tuple-element.38), channel_id=1, source_target_pairs={{7,4},{15,12},{23,20},{31,28}} | collective-permute-start | bytes 1179656 | tf_op jit(solution)/shard_map/ppermute | solution.py:70
  13.5 6.6 %collective-permute-start.5 = (bf16[256,768]{1,0:T(8,128)(2,1)S(1)}, bf16[256,768]{1,0:T(8,128)(2,1)S(1)}, u32[]{:S(2)}, u32[]{:S(2)}) collective-permute-start(bf16[256,768]{1,0:T(8,128)(2,1)S(1)} %get-tuple-element.39), channel_id=1, source_target_pairs={{1,2},{3,4},{5,6},{9,10},{11,12},{13,14},{17,18},{19,20},{21,22},{... | collective-permute-start | bytes 1179656 | tf_op jit(solution)/shard_map/ppermute | solution.py:54
  18.5 10.7 %collective-permute-start.8 = (bf16[3,2,128,384]{3,2,1,0:T(8,128)(2,1)S(1)}, bf16[3,2,128,384]{3,2,1,0:T(8,128)(2,1)S(1)}, u32[]{:S(2)}, u32[]{:S(2)}) collective-permute-start(bf16[3,2,128,384]{3,2,1,0:T(8,128)(2,1)S(1)} %step.1.refs_1_), channel_id=1, source_target_pairs={{0,4},{1,3},{2,6},{3,1},{4,0},{5,7},{6,2},{7,5},{8,12},{9,11},{10,... | collective-permute-start | bytes 1769480 | tf_op jit(solution)/shard_map/ppermute | solution.py:49
  21.6 10.8 %collective-permute-start.10 = (f32[6,8,256]{2,1,0:T(8,128)S(1)}, f32[6,8,256]{2,1,0:T(8,128)S(1)}, u32[]{:S(2)}, u32[]{:S(2)}) collective-permute-start(f32[6,8,256]{2,1,0:T(8,128)S(1)} %get-tuple-element.40.refs_2_.refs_1_), channel_id=1, source_target_pairs={{0,1},{1,0},{2,3},{3,2},{4,5},{5,4},{6,7},{7,6},{8,9},{9,8},{10,11... | collective-permute-start | bytes 147464 | tf_op jit(solution)/shard_map/ppermute | solution.py:49
  27.3 17.2 %collective-permute-start.12 = (bf16[256,768]{1,0:T(8,128)(2,1)S(1)}, bf16[256,768]{1,0:T(8,128)(2,1)S(1)}, u32[]{:S(2)}, u32[]{:S(2)}) collective-permute-start(bf16[256,768]{1,0:T(8,128)(2,1)S(1)} %get-tuple-element.47), channel_id=1, source_target_pairs={{2,1},{4,3},{6,5},{10,9},{12,11},{14,13},{18,17},{20,19},{22,21},{... | collective-permute-start | bytes 1179656 | tf_op jit(solution)/shard_map/ppermute | solution.py:54
  28.0 12.6 %collective-permute-start.14 = (bf16[256,768]{1,0:T(8,128)(2,1)S(1)}, bf16[256,768]{1,0:T(8,128)(2,1)S(1)}, u32[]{:S(2)}, u32[]{:S(2)}) collective-permute-start(bf16[256,768]{1,0:T(8,128)(2,1)S(1)} %get-tuple-element.51), channel_id=1, source_target_pairs={{2,1},{4,0},{6,5},{10,9},{12,8},{14,13},{18,17},{20,16},{22,21},{2... | collective-permute-start | bytes 1179656 | tf_op jit(solution)/shard_map/ppermute | solution.py:65
  29.6 7.3 %collective-permute-start.9 = (bf16[2,2,128,384]{3,2,1,0:T(8,128)(2,1)S(1)}, bf16[2,2,128,384]{3,2,1,0:T(8,128)(2,1)S(1)}, u32[]{:S(2)}, u32[]{:S(2)}) collective-permute-start(bf16[2,2,128,384]{3,2,1,0:T(8,128)(2,1)S(1)} %get-tuple-element.42.refs_7_), channel_id=1, source_target_pairs={{0,1},{1,0},{2,3},{3,2},{4,5},{5,4},{6,7},{7,6},{8,9},{9,8},{10,11... | collective-permute-start | bytes 1179656 | tf_op jit(solution)/shard_map/ppermute | solution.py:49
  34.3 12.2 %collective-permute-start.11 = (bf16[3,2,128,384]{3,2,1,0:T(8,128)(2,1)S(1)}, bf16[3,2,128,384]{3,2,1,0:T(8,128)(2,1)S(1)}, u32[]{:S(2)}, u32[]{:S(2)}) collective-permute-start(bf16[3,2,128,384]{3,2,1,0:T(8,128)(2,1)S(1)} %get-tuple-element.43.refs_7_), channel_id=1, source_target_pairs={{0,4},{1,3},{2,6},{3,1},{4,0},{5,7},{6,2},{7,5},{8,12},{9,11},{10,... | collective-permute-start | bytes 1769480 | tf_op jit(solution)/shard_map/ppermute | solution.py:49
  39.2 11.8 %collective-permute-start.13 = (f32[6,8,256]{2,1,0:T(8,128)S(1)}, f32[6,8,256]{2,1,0:T(8,128)S(1)}, u32[]{:S(2)}, u32[]{:S(2)}) collective-permute-start(f32[6,8,256]{2,1,0:T(8,128)S(1)} %get-tuple-element.44.refs_1_), channel_id=1, source_target_pairs={{1,0},{2,1},{3,2},{4,3},{5,4},{6,5},{7,6},{9,8},{10,9},{11,10},{12... | collective-permute-start | bytes 147464 | tf_op jit(solution)/shard_map/ppermute | solution.py:688
  40.6 10.4 %collective-permute-start.15 = (bf16[256,768]{1,0:T(8,128)(2,1)S(1)}, bf16[256,768]{1,0:T(8,128)(2,1)S(1)}, u32[]{:S(2)}, u32[]{:S(2)}) collective-permute-start(bf16[256,768]{1,0:T(8,128)(2,1)S(1)} %pass_on.1), channel_id=1, source_target_pairs={{0,3},{8,11},{16,19},{24,27}} | collective-permute-start | bytes 1179656 | tf_op jit(solution)/shard_map/ppermute | solution.py:70
  46.6 9.9 %collective-permute-start.16 = (bf16[3,2,128,384]{3,2,1,0:T(8,128)(2,1)S(1)}, bf16[3,2,128,384]{3,2,1,0:T(8,128)(2,1)S(1)}, u32[]{:S(2)}, u32[]{:S(2)}) collective-permute-start(bf16[3,2,128,384]{3,2,1,0:T(8,128)(2,1)S(1)} %get-tuple-element.48.refs_12_), channel_id=1, source_target_pairs={{0,2},{1,5},{2,0},{3,7},{4,6},{5,1},{6,4},{7,3},{8,10},{9,13},{10,... | collective-permute-start | bytes 1769480 | tf_op jit(solution)/shard_map/ppermute | solution.py:49
  57.0 1.8 %collective-permute-start.17 = (bf16[2,2,128,384]{3,2,1,0:T(8,128)(2,1)S(1)}, bf16[2,2,128,384]{3,2,1,0:T(8,128)(2,1)S(1)}, u32[]{:S(2)}, u32[]{:S(2)}) collective-permute-start(bf16[2,2,128,384]{3,2,1,0:T(8,128)(2,1)S(1)} %get-tuple-element.55), channel_id=1, source_target_pairs={{0,1},{1,0},{2,3},{3,2},{4,5},{5,4},{6,7},{7,6},{8,9},{9,8},{10,11... | collective-permute-start | bytes 1179656 | tf_op jit(solution)/shard_map/ppermute | solution.py:49

commit v19 on v17

--- a/solution.py
+++ b/solution.py
@@ -338,8 +338,8 @@
     rows_ref,
     queries_ref,
     direct_keys,
+    outer_values,
     relayed_keys,
-    outer_values,
     pair_ref,
     own_ref,
     part_ref,
@@ -511,8 +511,8 @@
     stats_ref,
     queries_ref,
     direct_keys,
+    outer_values,
     relayed_keys,
-    outer_values,
     pair_ref,
     own_ref,
     own_mem,
@@ -659,7 +659,7 @@
         flops=HIDING * piece_flops,
         name="release",
     )
-    outer = [direct_keys, shift_second(keys_out, 1, 1, peers), shift(values_out, 1, 1, peers)]
+    outer = [direct_keys, shift(values_out, 1, 1, peers), shift_second(keys_out, 1, 1, peers)]
     even_done = odd_done = 1
     for step, (even_bit, odd_bit) in enumerate(turns):
         got = swap(mine, even_bit, odd_bit, peers)

time: 58.6 us -> 57.9 us (0.988)
  starting transfers between devices: 25.8 us -> 24.4 us
  waiting for transfers between devices: 14.2 us -> 14.9 us
    ppermute x9, starting transfers between devices: 16.7 us -> 15.3 us  [swap(): lax.ppermute(block, 'tm', [(i, i ^ (odd_bit if i & 1 else even_bit)) for...]
    ppermute x9, waiting for transfers between devices: 14.2 us -> 14.9 us  [swap(): lax.ppermute(block, 'tm', [(i, i ^ (odd_bit if i & 1 else even_bit)) for...]
  transfers between devices with their start and end apart: 16 -> 16, of which waited for: 6 -> 6; matrix products, arithmetic and copies ran while one was open for 0% -> 0% of each run, Pallas kernels for 25% -> 26%
where the time goes in v19:
time: 57.9 us; the launch traced here: 57.7 us
  starting transfers between devices  24.4 us (42%)
  Pallas kernels  17.5 us (30%)
  waiting for transfers between devices  14.9 us (26%)
  between operations  0.87 us (2%)
    ppermute x9, starting transfers between devices, swap(): lax.ppermute(block, 'tm', [(i, i ^ (odd_bit if i & 1 else even_bit)) for...  15.3 us
    pallas_call x14, Pallas kernels, call(): pl.pallas_call(run, out_shape=outs, in_specs=[SMEM] * len(scalars) + [VME...  15.1 us
    ppermute x9, waiting for transfers between devices, swap(): lax.ppermute(block, 'tm', [(i, i ^ (odd_bit if i & 1 else even_bit)) for...  14.9 us
    ppermute x2, starting transfers between devices, shift_second(): return lax.ppermute(block, 'tm', pairs) if pairs else block  4.52 us
    pallas_call x2, Pallas kernels, join(): pl.pallas_call(run, out_shape=shape(BF16, rows, width), in_specs=[pl.Bloc...  2.34 us
    ppermute x2, starting transfers between devices, shift_first(): lax.ppermute(block, 'tm', [(i, relays.get((i, j), j)) for i, j in pairs])  1.97 us
    ppermute x2, starting transfers between devices, shift(): return lax.ppermute(block, 'tm', pairs)  1.36 us
    ppermute x1, starting transfers between devices, body(): lax.ppermute(stats_all, 'tm', [(i, i - 1) for i in range(1, peers)])  1.29 us
  transfers between devices with their start and end apart: 16, of which 6 were waited for; matrix products, arithmetic and copies ran while one was open for 0% of the time, Pallas kernels for 26%

profile of v19, /device:TPU:0, one launch (start us, length us, event | category | flops | bytes accessed | tf_op | source)
XLA Modules:
  0.0 57.7 jit_solution(15065056066017091664)
XLA Ops:
  0.7 1.2 %join.1.refs_1_.refs_0_.refs_6_.refs_3_.refs_7_ = bf16[528,768]{1,0:T(8,128)(2,1)S(1)} custom-call(s32[1,2]{1,0:T(1,128)} %refs_1_.4, bf16[256,768]{1,0:T(8,128)(2,1)} %refs_1_.3, bf16[256,768]{1,0:T(8,128)(2,1)} %refs_2_.2), custom_call_target="tpu_custom_call" | custom-call | tf_op jit(solution)/shard_map/join/pallas_call | solution.py:620
  1.9 0.5 collective-permute-start
  2.4 0.7 %collective-permute-start.1 = (bf16[256,768]{1,0:T(8,128)(2,1)S(1)}, bf16[256,768]{1,0:T(8,128)(2,1)S(1)}, u32[]{:S(2)}, u32[]{:S(2)}) collective-permute-start(bf16[256,768]{1,0:T(8,128)(2,1)S(1)} %copy-done.4), channel_id=1, source_target_pairs={{1,2},{3,7},{5,6},{9,10},{11,15},{13,14},{17,18},{19,23},{21,22},{... | collective-permute-start | bytes 1179656 | tf_op jit(solution)/shard_map/ppermute | solution.py:66
  3.1 1.3 %collective-permute-done.refs_4_.refs_2_.refs_5_.refs_6_ = bf16[528,768]{1,0:T(8,128)(2,1)S(1)} collective-permute-done((bf16[528,768]{1,0:T(8,128)(2,1)S(1)}, bf16[528,768]{1,0:T(8,128)(2,1)S(1)}, u32[]{:S(2)}, u32[]{:S(2)}) %collective-permute-start) | collective-permute-done | bytes 811040 | tf_op jit(solution)/shard_map/ppermute | solution.py:50
  4.3 0.3 split.1.refs_2_.refs_1_
  4.7 0.0 copy-start
  4.7 0.0 copy-start.2
  4.7 0.0 copy-start.3
  4.7 2.9 %collective-permute-start.4 = (bf16[3,2,128,384]{3,2,1,0:T(8,128)(2,1)S(1)}, bf16[3,2,128,384]{3,2,1,0:T(8,128)(2,1)S(1)}, u32[]{:S(2)}, u32[]{:S(2)}) collective-permute-start(bf16[3,2,128,384]{3,2,1,0:T(8,128)(2,1)S(1)} %split.1.refs_2_.refs_1_), channel_id=1, source_target_pairs={{0,2},{1,5},{2,0},{3,7},{4,6},{5,1},{6,4},{7,3},{8,10},{9,13},{10,... | collective-permute-start | bytes 1769480 | tf_op jit(solution)/shard_map/ppermute | solution.py:50
  7.6 1.1 %join_queries.1.refs_1_.refs_4_.refs_2_ = bf16[512,768]{1,0:T(8,128)(2,1)S(1)} custom-call(bf16[256,768]{1,0:T(8,128)(2,1)} %refs_0_.3, bf16[256,768]{1,0:T(8,128)(2,1)} %refs_1_.5, bf16[3,2,128,384]{3,2,1,0:T(8,128)(2,1)S(1)} %split.1.refs_2_.refs_1_), custom_call_target="tpu_custom_call" | custom-call | tf_op jit(solution)/shard_map/join_queries/pallas_call | solution.py:620
  8.8 1.1 %collective-permute-start.5 = (bf16[512,768]{1,0:T(8,128)(2,1)S(1)}, bf16[512,768]{1,0:T(8,128)(2,1)S(1)}, u32[]{:S(2)}, u32[]{:S(2)}) collective-permute-start(bf16[512,768]{1,0:T(8,128)(2,1)S(1)} %join_queries.1.refs_1_.refs_4_.refs_2_), channel_id=1, source_target_pairs={{0,1},{1,0},{2,3},{3,2},{4,5},{5,4},{6,7},{7,6},{8,9},{9,8},{10,11... | collective-permute-start | bytes 2359304 | tf_op jit(solution)/shard_map/ppermute | solution.py:50
  9.9 1.7 %plan.1 = (f32[6,16,256]{2,1,0:T(8,128)S(1)}, s32[8,128]{1,0:T(8,128)S(1)}) custom-call(s32[1,4]{1,0:T(1,128)S(1)} %bitcast.2, s32[1,2]{1,0:T(1,128)S(1)} %copy-done.2, s32[16]{0:T(128)S(1)} %copy-done.3, f32[6,16,16]{2,1,0:T(8,128)S(1)} %copy-done, bf16[528,768]{1,0:T(8,128)(2,1)S(1)} %collective-permute-done.refs_4_.refs_2_.refs_5_.refs_6_), custom_call_target="tpu_custom_call" | custom-call | tf_op jit(solution)/shard_map/plan/pallas_call | solution.py:38
  11.5 0.0 collective-permute-done.1.refs_1_.refs_2_.refs_3_
  11.6 0.1 release.1
  11.6 0.7 %collective-permute-start.2 = (bf16[256,768]{1,0:T(8,128)(2,1)S(1)}, bf16[256,768]{1,0:T(8,128)(2,1)S(1)}, u32[]{:S(2)}, u32[]{:S(2)}) collective-permute-start(bf16[256,768]{1,0:T(8,128)(2,1)S(1)} %get-tuple-element.28), channel_id=1, source_target_pairs={{1,2},{3,4},{5,6},{9,10},{11,12},{13,14},{17,18},{19,20},{21,22},{... | collective-permute-start | bytes 1179656 | tf_op jit(solution)/shard_map/ppermute | solution.py:55
  12.3 0.7 %collective-permute-start.3 = (bf16[256,768]{1,0:T(8,128)(2,1)S(1)}, bf16[256,768]{1,0:T(8,128)(2,1)S(1)}, u32[]{:S(2)}, u32[]{:S(2)}) collective-permute-start(bf16[256,768]{1,0:T(8,128)(2,1)S(1)} %get-tuple-element.29), channel_id=1, source_target_pairs={{7,4},{15,12},{23,20},{31,28}} | collective-permute-start | bytes 1179656 | tf_op jit(solution)/shard_map/ppermute | solution.py:71
  13.0 4.8 %collective-permute-done.4.refs_2_ = bf16[3,2,128,384]{3,2,1,0:T(8,128)(2,1)S(1)} collective-permute-done((bf16[3,2,128,384]{3,2,1,0:T(8,128)(2,1)S(1)}, bf16[3,2,128,384]{3,2,1,0:T(8,128)(2,1)S(1)}, u32[]{:S(2)}, u32[]{:S(2)}) %collective-permute-start.4) | collective-permute-done | bytes 589856 | tf_op jit(solution)/shard_map/ppermute | solution.py:50
  17.8 0.0 collective-permute-done.5.refs_4_.refs_5_.refs_2_
  17.8 0.3 step.1.refs_1_
  18.1 1.6 %collective-permute-start.6 = (bf16[3,2,128,384]{3,2,1,0:T(8,128)(2,1)S(1)}, bf16[3,2,128,384]{3,2,1,0:T(8,128)(2,1)S(1)}, u32[]{:S(2)}, u32[]{:S(2)}) collective-permute-start(bf16[3,2,128,384]{3,2,1,0:T(8,128)(2,1)S(1)} %step.1.refs_1_), channel_id=1, source_target_pairs={{0,4},{1,3},{2,6},{3,1},{4,0},{5,7},{6,2},{7,5},{8,12},{9,11},{10,... | collective-permute-start | bytes 1769480 | tf_op jit(solution)/shard_map/ppermute | solution.py:50
  19.7 0.0 collective-permute-done.2.refs_3_.refs_4_
  19.7 0.0 collective-permute-done.3.refs_4_.refs_5_
  19.7 1.5 %stats.1 = (f32[6,8,256]{2,1,0:T(8,128)S(1)}, bf16[256,768]{1,0:T(8,128)(2,1)S(1)}, bf16[256,768]{1,0:T(8,128)(2,1)S(1)}) custom-call(f32[6,16,256]{2,1,0:T(8,128)S(1)} %get-tuple-element.26.refs_0_.refs_1_, bf16[512,768]{1,0:T(8,128)(2,1)S(1)} %join_queries.1.refs_1_.refs_4_.refs_2_, bf16[256,768]{1,0:T(8,128)(2,1)S(1)} %collective-permute-done.1.refs_1_.refs_2_.refs_3_, ...), custom_call_target="tpu_custom_call" | custom-call | flops 20132659200 | tf_op jit(solution)/shard_map/stats/pallas_call | solution.py:38
  21.3 3.9 %collective-permute-start.8 = (f32[6,8,256]{2,1,0:T(8,128)S(1)}, f32[6,8,256]{2,1,0:T(8,128)S(1)}, u32[]{:S(2)}, u32[]{:S(2)}) collective-permute-start(f32[6,8,256]{2,1,0:T(8,128)S(1)} %get-tuple-element.30.refs_2_.refs_1_), channel_id=1, source_target_pairs={{0,1},{1,0},{2,3},{3,2},{4,5},{5,4},{6,7},{7,6},{8,9},{9,8},{10,11... | collective-permute-start | bytes 147464 | tf_op jit(solution)/shard_map/ppermute | solution.py:50
  25.1 0.7 %collective-permute-start.10 = (bf16[256,768]{1,0:T(8,128)(2,1)S(1)}, bf16[256,768]{1,0:T(8,128)(2,1)S(1)}, u32[]{:S(2)}, u32[]{:S(2)}) collective-permute-start(bf16[256,768]{1,0:T(8,128)(2,1)S(1)} %get-tuple-element.37), channel_id=1, source_target_pairs={{2,1},{4,3},{6,5},{10,9},{12,11},{14,13},{18,17},{20,19},{22,21},{... | collective-permute-start | bytes 1179656 | tf_op jit(solution)/shard_map/ppermute | solution.py:55
  25.8 1.3 %collective-permute-start.12 = (bf16[256,768]{1,0:T(8,128)(2,1)S(1)}, bf16[256,768]{1,0:T(8,128)(2,1)S(1)}, u32[]{:S(2)}, u32[]{:S(2)}) collective-permute-start(bf16[256,768]{1,0:T(8,128)(2,1)S(1)} %get-tuple-element.41), channel_id=1, source_target_pairs={{2,1},{4,0},{6,5},{10,9},{12,8},{14,13},{18,17},{20,16},{22,21},{2... | collective-permute-start | bytes 1179656 | tf_op jit(solution)/shard_map/ppermute | solution.py:66
  27.1 1.0 %collective-permute-done.6.refs_2_ = bf16[3,2,128,384]{3,2,1,0:T(8,128)(2,1)S(1)} collective-permute-done((bf16[3,2,128,384]{3,2,1,0:T(8,128)(2,1)S(1)}, bf16[3,2,128,384]{3,2,1,0:T(8,128)(2,1)S(1)}, u32[]{:S(2)}, u32[]{:S(2)}) %collective-permute-start.6) | collective-permute-done | bytes 589856 | tf_op jit(solution)/shard_map/ppermute | solution.py:50
  28.1 0.3 pick.1
  28.4 1.8 %collective-permute-start.7 = (bf16[2,2,128,384]{3,2,1,0:T(8,128)(2,1)S(1)}, bf16[2,2,128,384]{3,2,1,0:T(8,128)(2,1)S(1)}, u32[]{:S(2)}, u32[]{:S(2)}) collective-permute-start(bf16[2,2,128,384]{3,2,1,0:T(8,128)(2,1)S(1)} %get-tuple-element.32.refs_7_), channel_id=1, source_target_pairs={{0,1},{1,0},{2,3},{3,2},{4,5},{5,4},{6,7},{7,6},{8,9},{9,8},{10,11... | collective-permute-start | bytes 1179656 | tf_op jit(solution)/shard_map/ppermute | solution.py:50
  30.2 1.9 %memory.1 = (f32[4,2,128,384]{3,2,1,0:T(8,128)S(1)}, bf16[3,2,128,384]{3,2,1,0:T(8,128)(2,1)S(1)}) custom-call(s32[8,128]{1,0:T(8,128)S(1)} %get-tuple-element.27.refs_2_.refs_3_.refs_0_, f32[6,16,256]{2,1,0:T(8,128)S(1)} %get-tuple-element.26.refs_0_.refs_1_, f32[6,8,256]{2,1,0:T(8,128)S(1)} %get-tuple-element.30.refs_2_.refs_1_, ...), custom_call_target="tpu_custom_call" | custom-call | flops 20132659200 | tf_op jit(solution)/shard_map/memory/pallas_call | solution.py:38
  32.1 2.6 %collective-permute-start.9 = (bf16[3,2,128,384]{3,2,1,0:T(8,128)(2,1)S(1)}, bf16[3,2,128,384]{3,2,1,0:T(8,128)(2,1)S(1)}, u32[]{:S(2)}, u32[]{:S(2)}) collective-permute-start(bf16[3,2,128,384]{3,2,1,0:T(8,128)(2,1)S(1)} %get-tuple-element.33.refs_6_), channel_id=1, source_target_pairs={{0,4},{1,3},{2,6},{3,1},{4,0},{5,7},{6,2},{7,5},{8,12},{9,11},{10,... | collective-permute-start | bytes 1769480 | tf_op jit(solution)/shard_map/ppermute | solution.py:50
  34.7 0.0 collective-permute-done.7.refs_5_.refs_9_
  34.7 2.5 %own.1 = (f32[2,256,768]{2,1,0:T(8,128)S(1)}, f32[6,8,256]{2,1,0:T(8,128)S(1)}) custom-call(f32[6,16,256]{2,1,0:T(8,128)S(1)} %get-tuple-element.26.refs_0_.refs_1_, f32[6,8,256]{2,1,0:T(8,128)S(1)} %get-tuple-element.30.refs_2_.refs_1_, bf16[512,768]{1,0:T(8,128)(2,1)S(1)} %join_queries.1.refs_1_.refs_4_.refs_2_, ...), custom_call_target="tpu_custom_call" | custom-call | flops 20132659200 | tf_op jit(solution)/shard_map/own/pallas_call | solution.py:38
  37.1 1.3 %collective-permute-start.11 = (f32[6,8,256]{2,1,0:T(8,128)S(1)}, f32[6,8,256]{2,1,0:T(8,128)S(1)}, u32[]{:S(2)}, u32[]{:S(2)}) collective-permute-start(f32[6,8,256]{2,1,0:T(8,128)S(1)} %get-tuple-element.34.refs_1_), channel_id=1, source_target_pairs={{1,0},{2,1},{3,2},{4,3},{5,4},{6,5},{7,6},{9,8},{10,9},{11,10},{12... | collective-permute-start | bytes 147464 | tf_op jit(solution)/shard_map/ppermute | solution.py:703
  38.4 0.0 collective-permute-done.12.refs_0_.refs_4_
  38.5 3.8 %collective-permute-start.13 = (bf16[256,768]{1,0:T(8,128)(2,1)S(1)}, bf16[256,768]{1,0:T(8,128)(2,1)S(1)}, u32[]{:S(2)}, u32[]{:S(2)}) collective-permute-start(bf16[256,768]{1,0:T(8,128)(2,1)S(1)} %pass_on.1), channel_id=1, source_target_pairs={{0,3},{8,11},{16,19},{24,27}} | collective-permute-start | bytes 1179656 | tf_op jit(solution)/shard_map/ppermute | solution.py:71
  42.3 0.0 collective-permute-done.10.refs_3_
  42.3 2.0 %collective-permute-done.9.refs_1_ = bf16[3,2,128,384]{3,2,1,0:T(8,128)(2,1)S(1)} collective-permute-done((bf16[3,2,128,384]{3,2,1,0:T(8,128)(2,1)S(1)}, bf16[3,2,128,384]{3,2,1,0:T(8,128)(2,1)S(1)}, u32[]{:S(2)}, u32[]{:S(2)}) %collective-permute-start.9) | collective-permute-done | bytes 589856 | tf_op jit(solution)/shard_map/ppermute | solution.py:50
  44.3 0.2 add.1
  44.6 0.7 %collective-permute-start.14 = (bf16[3,2,128,384]{3,2,1,0:T(8,128)(2,1)S(1)}, bf16[3,2,128,384]{3,2,1,0:T(8,128)(2,1)S(1)}, u32[]{:S(2)}, u32[]{:S(2)}) collective-permute-start(bf16[3,2,128,384]{3,2,1,0:T(8,128)(2,1)S(1)} %get-tuple-element.38.refs_10_), channel_id=1, source_target_pairs={{0,2},{1,5},{2,0},{3,7},{4,6},{5,1},{6,4},{7,3},{8,10},{9,13},{10,... | collective-permute-start | bytes 1769480 | tf_op jit(solution)/shard_map/ppermute | solution.py:50
  45.3 3.8 %attend.1 = (bf16[256,768]{1,0:T(8,128)(2,1)}, bf16[256,768]{1,0:T(8,128)(2,1)}, f32[8,128]{1,0:T(8,128)S(1)}) custom-call(f32[6,16,256]{2,1,0:T(8,128)S(1)} %get-tuple-element.26.refs_0_.refs_1_, f32[6,8,256]{2,1,0:T(8,128)S(1)} %get-tuple-element.34.refs_1_, bf16[512,768]{1,0:T(8,128)(2,1)S(1)} %join_queries.1.refs_1_.refs_4_.refs_2_, ...), custom_call_target="tpu_custom_call" | custom-call | flops 20132659200 | tf_op jit(solution)/shard_map/attend/pallas_call | solution.py:38
  49.1 0.0 collective-permute-done.11.refs_1_
  49.1 1.2 %next.1.refs_3_.refs_0_ = f32[2,256,768]{2,1,0:T(8,128)S(1)} custom-call(f32[6,16,256]{2,1,0:T(8,128)S(1)} %get-tuple-element.26.refs_0_.refs_1_, f32[6,8,256]{2,1,0:T(8,128)S(1)} %collective-permute-done.11.refs_1_, bf16[512,768]{1,0:T(8,128)(2,1)S(1)} %collective-permute-done.5.refs_4_.refs_5_.refs_2_, ...), custom_call_target="tpu_custom_call" | custom-call | flops 20132659200 | tf_op jit(solution)/shard_map/next/pallas_call | solution.py:38
  50.3 4.2 %collective-permute-done.14.refs_2_ = bf16[3,2,128,384]{3,2,1,0:T(8,128)(2,1)S(1)} collective-permute-done((bf16[3,2,128,384]{3,2,1,0:T(8,128)(2,1)S(1)}, bf16[3,2,128,384]{3,2,1,0:T(8,128)(2,1)S(1)}, u32[]{:S(2)}, u32[]{:S(2)}) %collective-permute-start.14) | collective-permute-done | bytes 589856 | tf_op jit(solution)/shard_map/ppermute | solution.py:50
  54.5 0.3 owned.1
  54.9 0.2 collective-permute-start.15
  55.0 1.6 %collective-permute-done.15.refs_2_ = bf16[2,2,128,384]{3,2,1,0:T(8,128)(2,1)S(1)} collective-permute-done((bf16[2,2,128,384]{3,2,1,0:T(8,128)(2,1)S(1)}, bf16[2,2,128,384]{3,2,1,0:T(8,128)(2,1)S(1)}, u32[]{:S(2)}, u32[]{:S(2)}) %collective-permute-start.15) | collective-permute-done | bytes 393248 | tf_op jit(solution)/shard_map/ppermute | solution.py:50
  56.6 1.0 %final.1 = (bf16[256,768]{1,0:T(8,128)(2,1)}, bf16[256,768]{1,0:T(8,128)(2,1)}) custom-call(f32[2,256,768]{2,1,0:T(8,128)S(1)} %next.1.refs_3_.refs_0_, f32[2,2,128,384]{3,2,1,0:T(8,128)S(1)} %get-tuple-element.44.refs_1_, bf16[2,2,128,384]{3,2,1,0:T(8,128)(2,1)S(1)} %collective-permute-done.15.refs_2_), custom_call_target="tpu_custom_call" | custom-call | tf_op jit(solution)/shard_map/final/pallas_call | solution.py:38
  (10 shorter events, 0.0 us)
Async XLA Ops:
  0.6 1.8 %copy-start.4 = (bf16[256,768]{1,0:T(8,128)(2,1)S(1)}, bf16[256,768]{1,0:T(8,128)(2,1)}, u32[]{:S(2)}) copy-start(bf16[256,768]{1,0:T(8,128)(2,1)} %refs_1_.3) | copy-start | bytes 1179652
  0.6 3.7 %copy-start.1 = (s32[4]{0:T(128)S(1)}, s32[4]{0:T(128)}, u32[]{:S(2)}) copy-start(s32[4]{0:T(128)} %param.15) | copy-start | bytes 52
  1.9 2.5 %collective-permute-start = (bf16[528,768]{1,0:T(8,128)(2,1)S(1)}, bf16[528,768]{1,0:T(8,128)(2,1)S(1)}, u32[]{:S(2)}, u32[]{:S(2)}) collective-permute-start(bf16[528,768]{1,0:T(8,128)(2,1)S(1)} %join.1.refs_1_.refs_0_.refs_6_.refs_3_.refs_7_), channel_id=1, source_target_pairs={{0,1},{1,0},{2,3},{3,2},{4,5},{5,4},{6,7},{7,6},{8,9},{9,8},{10,11... | collective-permute-start | bytes 2433032 | tf_op jit(solution)/shard_map/ppermute | solution.py:50
  2.4 9.2 %collective-permute-start.1 = (bf16[256,768]{1,0:T(8,128)(2,1)S(1)}, bf16[256,768]{1,0:T(8,128)(2,1)S(1)}, u32[]{:S(2)}, u32[]{:S(2)}) collective-permute-start(bf16[256,768]{1,0:T(8,128)(2,1)S(1)} %copy-done.4), channel_id=1, source_target_pairs={{1,2},{3,7},{5,6},{9,10},{11,15},{13,14},{17,18},{19,23},{21,22},{... | collective-permute-start | bytes 1179656 | tf_op jit(solution)/shard_map/ppermute | solution.py:66
  4.7 5.2 %copy-start = (f32[6,16,16]{2,1,0:T(8,128)S(1)}, f32[6,16,16]{2,1,0:T(8,128)}, u32[]{:S(2)}) copy-start(f32[6,16,16]{2,1,0:T(8,128)} %refs_3_.1) | copy-start | bytes 18436
  4.7 5.2 %copy-start.2 = (s32[1,2]{1,0:T(1,128)S(1)}, s32[1,2]{1,0:T(1,128)}, u32[]{:S(2)}) copy-start(s32[1,2]{1,0:T(1,128)} %refs_1_.4) | copy-start | bytes 28
  4.7 5.2 %copy-start.3 = (s32[16]{0:T(128)S(1)}, s32[16]{0:T(128)}, u32[]{:S(2)}) copy-start(s32[16]{0:T(128)} %refs_2_.3) | copy-start | bytes 196
  4.7 13.1 %collective-permute-start.4 = (bf16[3,2,128,384]{3,2,1,0:T(8,128)(2,1)S(1)}, bf16[3,2,128,384]{3,2,1,0:T(8,128)(2,1)S(1)}, u32[]{:S(2)}, u32[]{:S(2)}) collective-permute-start(bf16[3,2,128,384]{3,2,1,0:T(8,128)(2,1)S(1)} %split.1.refs_2_.refs_1_), channel_id=1, source_target_pairs={{0,2},{1,5},{2,0},{3,7},{4,6},{5,1},{6,4},{7,3},{8,10},{9,13},{10,... | collective-permute-start | bytes 1769480 | tf_op jit(solution)/shard_map/ppermute | solution.py:50
  8.8 9.1 %collective-permute-start.5 = (bf16[512,768]{1,0:T(8,128)(2,1)S(1)}, bf16[512,768]{1,0:T(8,128)(2,1)S(1)}, u32[]{:S(2)}, u32[]{:S(2)}) collective-permute-start(bf16[512,768]{1,0:T(8,128)(2,1)S(1)} %join_queries.1.refs_1_.refs_4_.refs_2_), channel_id=1, source_target_pairs={{0,1},{1,0},{2,3},{3,2},{4,5},{5,4},{6,7},{7,6},{8,9},{9,8},{10,11... | collective-permute-start | bytes 2359304 | tf_op jit(solution)/shard_map/ppermute | solution.py:50
  11.6 8.1 %collective-permute-start.2 = (bf16[256,768]{1,0:T(8,128)(2,1)S(1)}, bf16[256,768]{1,0:T(8,128)(2,1)S(1)}, u32[]{:S(2)}, u32[]{:S(2)}) collective-permute-start(bf16[256,768]{1,0:T(8,128)(2,1)S(1)} %get-tuple-element.28), channel_id=1, source_target_pairs={{1,2},{3,4},{5,6},{9,10},{11,12},{13,14},{17,18},{19,20},{21,22},{... | collective-permute-start | bytes 1179656 | tf_op jit(solution)/shard_map/ppermute | solution.py:55
  12.3 7.4 %collective-permute-start.3 = (bf16[256,768]{1,0:T(8,128)(2,1)S(1)}, bf16[256,768]{1,0:T(8,128)(2,1)S(1)}, u32[]{:S(2)}, u32[]{:S(2)}) collective-permute-start(bf16[256,768]{1,0:T(8,128)(2,1)S(1)} %get-tuple-element.29), channel_id=1, source_target_pairs={{7,4},{15,12},{23,20},{31,28}} | collective-permute-start | bytes 1179656 | tf_op jit(solution)/shard_map/ppermute | solution.py:71
  18.1 9.9 %collective-permute-start.6 = (bf16[3,2,128,384]{3,2,1,0:T(8,128)(2,1)S(1)}, bf16[3,2,128,384]{3,2,1,0:T(8,128)(2,1)S(1)}, u32[]{:S(2)}, u32[]{:S(2)}) collective-permute-start(bf16[3,2,128,384]{3,2,1,0:T(8,128)(2,1)S(1)} %step.1.refs_1_), channel_id=1, source_target_pairs={{0,4},{1,3},{2,6},{3,1},{4,0},{5,7},{6,2},{7,5},{8,12},{9,11},{10,... | collective-permute-start | bytes 1769480 | tf_op jit(solution)/shard_map/ppermute | solution.py:50
  21.3 8.9 %collective-permute-start.8 = (f32[6,8,256]{2,1,0:T(8,128)S(1)}, f32[6,8,256]{2,1,0:T(8,128)S(1)}, u32[]{:S(2)}, u32[]{:S(2)}) collective-permute-start(f32[6,8,256]{2,1,0:T(8,128)S(1)} %get-tuple-element.30.refs_2_.refs_1_), channel_id=1, source_target_pairs={{0,1},{1,0},{2,3},{3,2},{4,5},{5,4},{6,7},{7,6},{8,9},{9,8},{10,11... | collective-permute-start | bytes 147464 | tf_op jit(solution)/shard_map/ppermute | solution.py:50
  25.1 17.2 %collective-permute-start.10 = (bf16[256,768]{1,0:T(8,128)(2,1)S(1)}, bf16[256,768]{1,0:T(8,128)(2,1)S(1)}, u32[]{:S(2)}, u32[]{:S(2)}) collective-permute-start(bf16[256,768]{1,0:T(8,128)(2,1)S(1)} %get-tuple-element.37), channel_id=1, source_target_pairs={{2,1},{4,3},{6,5},{10,9},{12,11},{14,13},{18,17},{20,19},{22,21},{... | collective-permute-start | bytes 1179656 | tf_op jit(solution)/shard_map/ppermute | solution.py:55
  25.8 12.7 %collective-permute-start.12 = (bf16[256,768]{1,0:T(8,128)(2,1)S(1)}, bf16[256,768]{1,0:T(8,128)(2,1)S(1)}, u32[]{:S(2)}, u32[]{:S(2)}) collective-permute-start(bf16[256,768]{1,0:T(8,128)(2,1)S(1)} %get-tuple-element.41), channel_id=1, source_target_pairs={{2,1},{4,0},{6,5},{10,9},{12,8},{14,13},{18,17},{20,16},{22,21},{2... | collective-permute-start | bytes 1179656 | tf_op jit(solution)/shard_map/ppermute | solution.py:66
  28.4 6.3 %collective-permute-start.7 = (bf16[2,2,128,384]{3,2,1,0:T(8,128)(2,1)S(1)}, bf16[2,2,128,384]{3,2,1,0:T(8,128)(2,1)S(1)}, u32[]{:S(2)}, u32[]{:S(2)}) collective-permute-start(bf16[2,2,128,384]{3,2,1,0:T(8,128)(2,1)S(1)} %get-tuple-element.32.refs_7_), channel_id=1, source_target_pairs={{0,1},{1,0},{2,3},{3,2},{4,5},{5,4},{6,7},{7,6},{8,9},{9,8},{10,11... | collective-permute-start | bytes 1179656 | tf_op jit(solution)/shard_map/ppermute | solution.py:50
  32.1 12.2 %collective-permute-start.9 = (bf16[3,2,128,384]{3,2,1,0:T(8,128)(2,1)S(1)}, bf16[3,2,128,384]{3,2,1,0:T(8,128)(2,1)S(1)}, u32[]{:S(2)}, u32[]{:S(2)}) collective-permute-start(bf16[3,2,128,384]{3,2,1,0:T(8,128)(2,1)S(1)} %get-tuple-element.33.refs_6_), channel_id=1, source_target_pairs={{0,4},{1,3},{2,6},{3,1},{4,0},{5,7},{6,2},{7,5},{8,12},{9,11},{10,... | collective-permute-start | bytes 1769480 | tf_op jit(solution)/shard_map/ppermute | solution.py:50
  37.1 11.9 %collective-permute-start.11 = (f32[6,8,256]{2,1,0:T(8,128)S(1)}, f32[6,8,256]{2,1,0:T(8,128)S(1)}, u32[]{:S(2)}, u32[]{:S(2)}) collective-permute-start(f32[6,8,256]{2,1,0:T(8,128)S(1)} %get-tuple-element.34.refs_1_), channel_id=1, source_target_pairs={{1,0},{2,1},{3,2},{4,3},{5,4},{6,5},{7,6},{9,8},{10,9},{11,10},{12... | collective-permute-start | bytes 147464 | tf_op jit(solution)/shard_map/ppermute | solution.py:703
  38.5 10.6 %collective-permute-start.13 = (bf16[256,768]{1,0:T(8,128)(2,1)S(1)}, bf16[256,768]{1,0:T(8,128)(2,1)S(1)}, u32[]{:S(2)}, u32[]{:S(2)}) collective-permute-start(bf16[256,768]{1,0:T(8,128)(2,1)S(1)} %pass_on.1), channel_id=1, source_target_pairs={{0,3},{8,11},{16,19},{24,27}} | collective-permute-start | bytes 1179656 | tf_op jit(solution)/shard_map/ppermute | solution.py:71
  44.6 9.9 %collective-permute-start.14 = (bf16[3,2,128,384]{3,2,1,0:T(8,128)(2,1)S(1)}, bf16[3,2,128,384]{3,2,1,0:T(8,128)(2,1)S(1)}, u32[]{:S(2)}, u32[]{:S(2)}) collective-permute-start(bf16[3,2,128,384]{3,2,1,0:T(8,128)(2,1)S(1)} %get-tuple-element.38.refs_10_), channel_id=1, source_target_pairs={{0,2},{1,5},{2,0},{3,7},{4,6},{5,1},{6,4},{7,3},{8,10},{9,13},{10,... | collective-permute-start | bytes 1769480 | tf_op jit(solution)/shard_map/ppermute | solution.py:50
  54.9 1.8 %collective-permute-start.15 = (bf16[2,2,128,384]{3,2,1,0:T(8,128)(2,1)S(1)}, bf16[2,2,128,384]{3,2,1,0:T(8,128)(2,1)S(1)}, u32[]{:S(2)}, u32[]{:S(2)}) collective-permute-start(bf16[2,2,128,384]{3,2,1,0:T(8,128)(2,1)S(1)} %get-tuple-element.45), channel_id=1, source_target_pairs={{0,1},{1,0},{2,3},{3,2},{4,5},{5,4},{6,7},{7,6},{8,9},{9,8},{10,11... | collective-permute-start | bytes 1179656 | tf_op jit(solution)/shard_map/ppermute | solution.py:50

commit v20 on v19

--- a/solution.py
+++ b/solution.py
@@ -580,16 +580,21 @@
                 out[j] = jnp.zeros(out.shape[1:], out.dtype)
 
 
-def final_kernel(own_ref, mine_ref, got_ref, grad_key_ref, grad_value_ref):
+def final_kernel(own_ref, mine_ref, got_ref, grad_key_ref, grad_value_ref, sums, sems):
     role = lax.axis_index("tm") & 1
     frame_len, half_width = mine_ref.shape[2:]
+    copies = []
     for kind, out in enumerate((grad_key_ref, grad_value_ref)):
         for j in range(FR_DEV):
             rows = pl.ds(j * frame_len, frame_len)
             for half in range(2):
                 cols = pl.ds(half * half_width, half_width)
                 bank = jnp.where(role == half, mine_ref[j, kind], got_ref[j, kind].astype(F32))
-                out[rows, cols] = (own_ref[kind, rows, cols] + bank).astype(BF16)
+                sums[kind, rows, cols] = (own_ref[kind, rows, cols] + bank).astype(BF16)
+            copies.append(pltpu.make_async_copy(sums.at[kind, rows], out.at[rows], sems.at[kind * FR_DEV + j]))
+            copies[-1].start()
+    for copy in copies:
+        copy.wait()
 
 
 def body(
@@ -733,9 +738,15 @@
         name="owned",
     )
     owned_got = swap(owned_send, 1, 1, peers)
-    grad_key, grad_value = call(
-        final_kernel, [shape(BF16, row_count, width)] * 2, [own, owned_mine, owned_got], name="final"
-    )
+    grad_key, grad_value = pl.pallas_call(
+        final_kernel,
+        out_shape=[shape(BF16, row_count, width)] * 2,
+        in_specs=[VMEM] * 3,
+        out_specs=[pl.BlockSpec(memory_space=pltpu.HBM)] * 2,
+        scratch_shapes=[pltpu.VMEM((2, row_count, width), BF16), pltpu.SemaphoreType.DMA((2 * FR_DEV,))],
+        compiler_params=pltpu.CompilerParams(vmem_limit_bytes=VMEM_LIMIT),
+        name="final",
+    )(own, owned_mine, owned_got)
     return (attended, grad_query, grad_key, grad_value)
 
 

time: 57.9 us -> 57.9 us (level)
    pallas_call x14 -> x13, Pallas kernels: 15.1 us -> 14.1 us  [call(): pl.pallas_call(run, out_shape=outs, in_specs=[SMEM] * len(scalars) + [VME...]
    pallas_call x0 -> x1, Pallas kernels: none -> 0.97 us  [body(): pl.pallas_call(final_kernel, out_shape=[shape(BF16, row_count, width)] *...]
where the time goes in v20:
time: 57.9 us; the launch traced here: 57.6 us
  starting transfers between devices  24.4 us (42%)
  Pallas kernels  17.4 us (30%)
  waiting for transfers between devices  14.9 us (26%)
  between operations  0.87 us (2%)
    ppermute x9, starting transfers between devices, swap(): lax.ppermute(block, 'tm', [(i, i ^ (odd_bit if i & 1 else even_bit)) for...  15.3 us
    ppermute x9, waiting for transfers between devices, swap(): lax.ppermute(block, 'tm', [(i, i ^ (odd_bit if i & 1 else even_bit)) for...  14.9 us
    pallas_call x13, Pallas kernels, call(): pl.pallas_call(run, out_shape=outs, in_specs=[SMEM] * len(scalars) + [VME...  14.1 us
    ppermute x2, starting transfers between devices, shift_second(): return lax.ppermute(block, 'tm', pairs) if pairs else block  4.53 us
    pallas_call x2, Pallas kernels, join(): pl.pallas_call(run, out_shape=shape(BF16, rows, width), in_specs=[pl.Bloc...  2.34 us
    ppermute x2, starting transfers between devices, shift_first(): lax.ppermute(block, 'tm', [(i, relays.get((i, j), j)) for i, j in pairs])  1.97 us
    ppermute x2, starting transfers between devices, shift(): return lax.ppermute(block, 'tm', pairs)  1.36 us
    ppermute x1, starting transfers between devices, body(): lax.ppermute(stats_all, 'tm', [(i, i - 1) for i in range(1, peers)])  1.29 us
  transfers between devices with their start and end apart: 16, of which 6 were waited for; matrix products, arithmetic and copies ran while one was open for 0% of the time, Pallas kernels for 26%

profile of v20, /device:TPU:0, one launch (start us, length us, event | category | flops | bytes accessed | tf_op | source)
XLA Modules:
  0.0 57.6 jit_solution(17507751734987933998)
XLA Ops:
  0.7 1.2 %join.1.refs_1_.refs_0_.refs_6_.refs_3_.refs_7_ = bf16[528,768]{1,0:T(8,128)(2,1)S(1)} custom-call(s32[1,2]{1,0:T(1,128)} %refs_1_.4, bf16[256,768]{1,0:T(8,128)(2,1)} %refs_1_.3, bf16[256,768]{1,0:T(8,128)(2,1)} %refs_2_.2), custom_call_target="tpu_custom_call" | custom-call | tf_op jit(solution)/shard_map/join/pallas_call | solution.py:625
  1.9 0.5 collective-permute-start
  2.4 0.7 %collective-permute-start.1 = (bf16[256,768]{1,0:T(8,128)(2,1)S(1)}, bf16[256,768]{1,0:T(8,128)(2,1)S(1)}, u32[]{:S(2)}, u32[]{:S(2)}) collective-permute-start(bf16[256,768]{1,0:T(8,128)(2,1)S(1)} %copy-done.4), channel_id=1, source_target_pairs={{1,2},{3,7},{5,6},{9,10},{11,15},{13,14},{17,18},{19,23},{21,22},{... | collective-permute-start | bytes 1179656 | tf_op jit(solution)/shard_map/ppermute | solution.py:66
  3.1 1.3 %collective-permute-done.refs_4_.refs_2_.refs_5_.refs_6_ = bf16[528,768]{1,0:T(8,128)(2,1)S(1)} collective-permute-done((bf16[528,768]{1,0:T(8,128)(2,1)S(1)}, bf16[528,768]{1,0:T(8,128)(2,1)S(1)}, u32[]{:S(2)}, u32[]{:S(2)}) %collective-permute-start) | collective-permute-done | bytes 811040 | tf_op jit(solution)/shard_map/ppermute | solution.py:50
  4.3 0.3 split.1.refs_2_.refs_1_
  4.7 0.0 copy-start
  4.7 0.0 copy-start.2
  4.7 0.0 copy-start.3
  4.7 2.9 %collective-permute-start.4 = (bf16[3,2,128,384]{3,2,1,0:T(8,128)(2,1)S(1)}, bf16[3,2,128,384]{3,2,1,0:T(8,128)(2,1)S(1)}, u32[]{:S(2)}, u32[]{:S(2)}) collective-permute-start(bf16[3,2,128,384]{3,2,1,0:T(8,128)(2,1)S(1)} %split.1.refs_2_.refs_1_), channel_id=1, source_target_pairs={{0,2},{1,5},{2,0},{3,7},{4,6},{5,1},{6,4},{7,3},{8,10},{9,13},{10,... | collective-permute-start | bytes 1769480 | tf_op jit(solution)/shard_map/ppermute | solution.py:50
  7.6 1.1 %join_queries.1.refs_1_.refs_4_.refs_2_ = bf16[512,768]{1,0:T(8,128)(2,1)S(1)} custom-call(bf16[256,768]{1,0:T(8,128)(2,1)} %refs_0_.3, bf16[256,768]{1,0:T(8,128)(2,1)} %refs_1_.5, bf16[3,2,128,384]{3,2,1,0:T(8,128)(2,1)S(1)} %split.1.refs_2_.refs_1_), custom_call_target="tpu_custom_call" | custom-call | tf_op jit(solution)/shard_map/join_queries/pallas_call | solution.py:625
  8.8 1.1 %collective-permute-start.5 = (bf16[512,768]{1,0:T(8,128)(2,1)S(1)}, bf16[512,768]{1,0:T(8,128)(2,1)S(1)}, u32[]{:S(2)}, u32[]{:S(2)}) collective-permute-start(bf16[512,768]{1,0:T(8,128)(2,1)S(1)} %join_queries.1.refs_1_.refs_4_.refs_2_), channel_id=1, source_target_pairs={{0,1},{1,0},{2,3},{3,2},{4,5},{5,4},{6,7},{7,6},{8,9},{9,8},{10,11... | collective-permute-start | bytes 2359304 | tf_op jit(solution)/shard_map/ppermute | solution.py:50
  9.9 1.7 %plan.1 = (f32[6,16,256]{2,1,0:T(8,128)S(1)}, s32[8,128]{1,0:T(8,128)S(1)}) custom-call(s32[1,4]{1,0:T(1,128)S(1)} %bitcast.2, s32[1,2]{1,0:T(1,128)S(1)} %copy-done.2, s32[16]{0:T(128)S(1)} %copy-done.3, f32[6,16,16]{2,1,0:T(8,128)S(1)} %copy-done, bf16[528,768]{1,0:T(8,128)(2,1)S(1)} %collective-permute-done.refs_4_.refs_2_.refs_5_.refs_6_), custom_call_target="tpu_custom_call" | custom-call | tf_op jit(solution)/shard_map/plan/pallas_call | solution.py:38
  11.5 0.0 collective-permute-done.1.refs_1_.refs_2_.refs_3_
  11.6 0.1 release.1
  11.6 0.7 %collective-permute-start.2 = (bf16[256,768]{1,0:T(8,128)(2,1)S(1)}, bf16[256,768]{1,0:T(8,128)(2,1)S(1)}, u32[]{:S(2)}, u32[]{:S(2)}) collective-permute-start(bf16[256,768]{1,0:T(8,128)(2,1)S(1)} %get-tuple-element.28), channel_id=1, source_target_pairs={{1,2},{3,4},{5,6},{9,10},{11,12},{13,14},{17,18},{19,20},{21,22},{... | collective-permute-start | bytes 1179656 | tf_op jit(solution)/shard_map/ppermute | solution.py:55
  12.3 0.7 %collective-permute-start.3 = (bf16[256,768]{1,0:T(8,128)(2,1)S(1)}, bf16[256,768]{1,0:T(8,128)(2,1)S(1)}, u32[]{:S(2)}, u32[]{:S(2)}) collective-permute-start(bf16[256,768]{1,0:T(8,128)(2,1)S(1)} %get-tuple-element.29), channel_id=1, source_target_pairs={{7,4},{15,12},{23,20},{31,28}} | collective-permute-start | bytes 1179656 | tf_op jit(solution)/shard_map/ppermute | solution.py:71
  13.0 4.8 %collective-permute-done.4.refs_2_ = bf16[3,2,128,384]{3,2,1,0:T(8,128)(2,1)S(1)} collective-permute-done((bf16[3,2,128,384]{3,2,1,0:T(8,128)(2,1)S(1)}, bf16[3,2,128,384]{3,2,1,0:T(8,128)(2,1)S(1)}, u32[]{:S(2)}, u32[]{:S(2)}) %collective-permute-start.4) | collective-permute-done | bytes 589856 | tf_op jit(solution)/shard_map/ppermute | solution.py:50
  17.8 0.0 collective-permute-done.5.refs_4_.refs_5_.refs_2_
  17.8 0.3 step.1.refs_1_
  18.1 1.6 %collective-permute-start.6 = (bf16[3,2,128,384]{3,2,1,0:T(8,128)(2,1)S(1)}, bf16[3,2,128,384]{3,2,1,0:T(8,128)(2,1)S(1)}, u32[]{:S(2)}, u32[]{:S(2)}) collective-permute-start(bf16[3,2,128,384]{3,2,1,0:T(8,128)(2,1)S(1)} %step.1.refs_1_), channel_id=1, source_target_pairs={{0,4},{1,3},{2,6},{3,1},{4,0},{5,7},{6,2},{7,5},{8,12},{9,11},{10,... | collective-permute-start | bytes 1769480 | tf_op jit(solution)/shard_map/ppermute | solution.py:50
  19.7 0.0 collective-permute-done.2.refs_3_.refs_4_
  19.7 0.0 collective-permute-done.3.refs_4_.refs_5_
  19.7 1.5 %stats.1 = (f32[6,8,256]{2,1,0:T(8,128)S(1)}, bf16[256,768]{1,0:T(8,128)(2,1)S(1)}, bf16[256,768]{1,0:T(8,128)(2,1)S(1)}) custom-call(f32[6,16,256]{2,1,0:T(8,128)S(1)} %get-tuple-element.26.refs_0_.refs_1_, bf16[512,768]{1,0:T(8,128)(2,1)S(1)} %join_queries.1.refs_1_.refs_4_.refs_2_, bf16[256,768]{1,0:T(8,128)(2,1)S(1)} %collective-permute-done.1.refs_1_.refs_2_.refs_3_, ...), custom_call_target="tpu_custom_call" | custom-call | flops 20132659200 | tf_op jit(solution)/shard_map/stats/pallas_call | solution.py:38
  21.3 3.9 %collective-permute-start.8 = (f32[6,8,256]{2,1,0:T(8,128)S(1)}, f32[6,8,256]{2,1,0:T(8,128)S(1)}, u32[]{:S(2)}, u32[]{:S(2)}) collective-permute-start(f32[6,8,256]{2,1,0:T(8,128)S(1)} %get-tuple-element.30.refs_2_.refs_1_), channel_id=1, source_target_pairs={{0,1},{1,0},{2,3},{3,2},{4,5},{5,4},{6,7},{7,6},{8,9},{9,8},{10,11... | collective-permute-start | bytes 147464 | tf_op jit(solution)/shard_map/ppermute | solution.py:50
  25.1 0.7 %collective-permute-start.10 = (bf16[256,768]{1,0:T(8,128)(2,1)S(1)}, bf16[256,768]{1,0:T(8,128)(2,1)S(1)}, u32[]{:S(2)}, u32[]{:S(2)}) collective-permute-start(bf16[256,768]{1,0:T(8,128)(2,1)S(1)} %get-tuple-element.37), channel_id=1, source_target_pairs={{2,1},{4,3},{6,5},{10,9},{12,11},{14,13},{18,17},{20,19},{22,21},{... | collective-permute-start | bytes 1179656 | tf_op jit(solution)/shard_map/ppermute | solution.py:55
  25.8 1.3 %collective-permute-start.12 = (bf16[256,768]{1,0:T(8,128)(2,1)S(1)}, bf16[256,768]{1,0:T(8,128)(2,1)S(1)}, u32[]{:S(2)}, u32[]{:S(2)}) collective-permute-start(bf16[256,768]{1,0:T(8,128)(2,1)S(1)} %get-tuple-element.41), channel_id=1, source_target_pairs={{2,1},{4,0},{6,5},{10,9},{12,8},{14,13},{18,17},{20,16},{22,21},{2... | collective-permute-start | bytes 1179656 | tf_op jit(solution)/shard_map/ppermute | solution.py:66
  27.1 1.0 %collective-permute-done.6.refs_2_ = bf16[3,2,128,384]{3,2,1,0:T(8,128)(2,1)S(1)} collective-permute-done((bf16[3,2,128,384]{3,2,1,0:T(8,128)(2,1)S(1)}, bf16[3,2,128,384]{3,2,1,0:T(8,128)(2,1)S(1)}, u32[]{:S(2)}, u32[]{:S(2)}) %collective-permute-start.6) | collective-permute-done | bytes 589856 | tf_op jit(solution)/shard_map/ppermute | solution.py:50
  28.1 0.3 pick.1
  28.4 1.8 %collective-permute-start.7 = (bf16[2,2,128,384]{3,2,1,0:T(8,128)(2,1)S(1)}, bf16[2,2,128,384]{3,2,1,0:T(8,128)(2,1)S(1)}, u32[]{:S(2)}, u32[]{:S(2)}) collective-permute-start(bf16[2,2,128,384]{3,2,1,0:T(8,128)(2,1)S(1)} %get-tuple-element.32.refs_7_), channel_id=1, source_target_pairs={{0,1},{1,0},{2,3},{3,2},{4,5},{5,4},{6,7},{7,6},{8,9},{9,8},{10,11... | collective-permute-start | bytes 1179656 | tf_op jit(solution)/shard_map/ppermute | solution.py:50
  30.2 1.9 %memory.1 = (f32[4,2,128,384]{3,2,1,0:T(8,128)S(1)}, bf16[3,2,128,384]{3,2,1,0:T(8,128)(2,1)S(1)}) custom-call(s32[8,128]{1,0:T(8,128)S(1)} %get-tuple-element.27.refs_2_.refs_3_.refs_0_, f32[6,16,256]{2,1,0:T(8,128)S(1)} %get-tuple-element.26.refs_0_.refs_1_, f32[6,8,256]{2,1,0:T(8,128)S(1)} %get-tuple-element.30.refs_2_.refs_1_, ...), custom_call_target="tpu_custom_call" | custom-call | flops 20132659200 | tf_op jit(solution)/shard_map/memory/pallas_call | solution.py:38
  32.1 2.6 %collective-permute-start.9 = (bf16[3,2,128,384]{3,2,1,0:T(8,128)(2,1)S(1)}, bf16[3,2,128,384]{3,2,1,0:T(8,128)(2,1)S(1)}, u32[]{:S(2)}, u32[]{:S(2)}) collective-permute-start(bf16[3,2,128,384]{3,2,1,0:T(8,128)(2,1)S(1)} %get-tuple-element.33.refs_6_), channel_id=1, source_target_pairs={{0,4},{1,3},{2,6},{3,1},{4,0},{5,7},{6,2},{7,5},{8,12},{9,11},{10,... | collective-permute-start | bytes 1769480 | tf_op jit(solution)/shard_map/ppermute | solution.py:50
  34.7 0.0 collective-permute-done.7.refs_5_.refs_9_
  34.7 2.4 %own.1 = (f32[2,256,768]{2,1,0:T(8,128)S(1)}, f32[6,8,256]{2,1,0:T(8,128)S(1)}) custom-call(f32[6,16,256]{2,1,0:T(8,128)S(1)} %get-tuple-element.26.refs_0_.refs_1_, f32[6,8,256]{2,1,0:T(8,128)S(1)} %get-tuple-element.30.refs_2_.refs_1_, bf16[512,768]{1,0:T(8,128)(2,1)S(1)} %join_queries.1.refs_1_.refs_4_.refs_2_, ...), custom_call_target="tpu_custom_call" | custom-call | flops 20132659200 | tf_op jit(solution)/shard_map/own/pallas_call | solution.py:38
  37.1 1.3 %collective-permute-start.11 = (f32[6,8,256]{2,1,0:T(8,128)S(1)}, f32[6,8,256]{2,1,0:T(8,128)S(1)}, u32[]{:S(2)}, u32[]{:S(2)}) collective-permute-start(f32[6,8,256]{2,1,0:T(8,128)S(1)} %get-tuple-element.34.refs_1_), channel_id=1, source_target_pairs={{1,0},{2,1},{3,2},{4,3},{5,4},{6,5},{7,6},{9,8},{10,9},{11,10},{12... | collective-permute-start | bytes 147464 | tf_op jit(solution)/shard_map/ppermute | solution.py:708
  38.4 0.0 collective-permute-done.12.refs_0_.refs_4_
  38.5 3.8 %collective-permute-start.13 = (bf16[256,768]{1,0:T(8,128)(2,1)S(1)}, bf16[256,768]{1,0:T(8,128)(2,1)S(1)}, u32[]{:S(2)}, u32[]{:S(2)}) collective-permute-start(bf16[256,768]{1,0:T(8,128)(2,1)S(1)} %pass_on.1), channel_id=1, source_target_pairs={{0,3},{8,11},{16,19},{24,27}} | collective-permute-start | bytes 1179656 | tf_op jit(solution)/shard_map/ppermute | solution.py:71
  42.3 0.0 collective-permute-done.10.refs_3_
  42.3 2.0 %collective-permute-done.9.refs_1_ = bf16[3,2,128,384]{3,2,1,0:T(8,128)(2,1)S(1)} collective-permute-done((bf16[3,2,128,384]{3,2,1,0:T(8,128)(2,1)S(1)}, bf16[3,2,128,384]{3,2,1,0:T(8,128)(2,1)S(1)}, u32[]{:S(2)}, u32[]{:S(2)}) %collective-permute-start.9) | collective-permute-done | bytes 589856 | tf_op jit(solution)/shard_map/ppermute | solution.py:50
  44.3 0.2 add.1
  44.6 0.7 %collective-permute-start.14 = (bf16[3,2,128,384]{3,2,1,0:T(8,128)(2,1)S(1)}, bf16[3,2,128,384]{3,2,1,0:T(8,128)(2,1)S(1)}, u32[]{:S(2)}, u32[]{:S(2)}) collective-permute-start(bf16[3,2,128,384]{3,2,1,0:T(8,128)(2,1)S(1)} %get-tuple-element.38.refs_10_), channel_id=1, source_target_pairs={{0,2},{1,5},{2,0},{3,7},{4,6},{5,1},{6,4},{7,3},{8,10},{9,13},{10,... | collective-permute-start | bytes 1769480 | tf_op jit(solution)/shard_map/ppermute | solution.py:50
  45.3 3.8 %attend.1 = (bf16[256,768]{1,0:T(8,128)(2,1)}, bf16[256,768]{1,0:T(8,128)(2,1)}, f32[8,128]{1,0:T(8,128)S(1)}) custom-call(f32[6,16,256]{2,1,0:T(8,128)S(1)} %get-tuple-element.26.refs_0_.refs_1_, f32[6,8,256]{2,1,0:T(8,128)S(1)} %get-tuple-element.34.refs_1_, bf16[512,768]{1,0:T(8,128)(2,1)S(1)} %join_queries.1.refs_1_.refs_4_.refs_2_, ...), custom_call_target="tpu_custom_call" | custom-call | flops 20132659200 | tf_op jit(solution)/shard_map/attend/pallas_call | solution.py:38
  49.1 0.0 collective-permute-done.11.refs_1_
  49.1 1.2 %next.1.refs_3_.own_ref = f32[2,256,768]{2,1,0:T(8,128)S(1)} custom-call(f32[6,16,256]{2,1,0:T(8,128)S(1)} %get-tuple-element.26.refs_0_.refs_1_, f32[6,8,256]{2,1,0:T(8,128)S(1)} %collective-permute-done.11.refs_1_, bf16[512,768]{1,0:T(8,128)(2,1)S(1)} %collective-permute-done.5.refs_4_.refs_5_.refs_2_, ...), custom_call_target="tpu_custom_call" | custom-call | flops 20132659200 | tf_op jit(solution)/shard_map/next/pallas_call | solution.py:38
  50.3 4.2 %collective-permute-done.14.refs_2_ = bf16[3,2,128,384]{3,2,1,0:T(8,128)(2,1)S(1)} collective-permute-done((bf16[3,2,128,384]{3,2,1,0:T(8,128)(2,1)S(1)}, bf16[3,2,128,384]{3,2,1,0:T(8,128)(2,1)S(1)}, u32[]{:S(2)}, u32[]{:S(2)}) %collective-permute-start.14) | collective-permute-done | bytes 589856 | tf_op jit(solution)/shard_map/ppermute | solution.py:50
  54.5 0.3 owned.1
  54.8 0.2 collective-permute-start.15
  55.0 1.6 %collective-permute-done.15.got_ref = bf16[2,2,128,384]{3,2,1,0:T(8,128)(2,1)S(1)} collective-permute-done((bf16[2,2,128,384]{3,2,1,0:T(8,128)(2,1)S(1)}, bf16[2,2,128,384]{3,2,1,0:T(8,128)(2,1)S(1)}, u32[]{:S(2)}, u32[]{:S(2)}) %collective-permute-start.15) | collective-permute-done | bytes 393248 | tf_op jit(solution)/shard_map/ppermute | solution.py:50
  56.6 1.0 %final.1 = (bf16[256,768]{1,0:T(8,128)(2,1)}, bf16[256,768]{1,0:T(8,128)(2,1)}) custom-call(f32[2,256,768]{2,1,0:T(8,128)S(1)} %next.1.refs_3_.own_ref, f32[2,2,128,384]{3,2,1,0:T(8,128)S(1)} %get-tuple-element.44.mine_ref, bf16[2,2,128,384]{3,2,1,0:T(8,128)(2,1)S(1)} %collective-permute-done.15.got_ref), custom_call_target="tpu_custom_call" | custom-call | tf_op jit(solution)/shard_map/final/pallas_call | solution.py:741
  (10 shorter events, 0.0 us)
Async XLA Ops:
  0.6 1.8 %copy-start.4 = (bf16[256,768]{1,0:T(8,128)(2,1)S(1)}, bf16[256,768]{1,0:T(8,128)(2,1)}, u32[]{:S(2)}) copy-start(bf16[256,768]{1,0:T(8,128)(2,1)} %refs_1_.3) | copy-start | bytes 1179652
  0.6 3.7 %copy-start.1 = (s32[4]{0:T(128)S(1)}, s32[4]{0:T(128)}, u32[]{:S(2)}) copy-start(s32[4]{0:T(128)} %param.15) | copy-start | bytes 52
  1.9 2.5 %collective-permute-start = (bf16[528,768]{1,0:T(8,128)(2,1)S(1)}, bf16[528,768]{1,0:T(8,128)(2,1)S(1)}, u32[]{:S(2)}, u32[]{:S(2)}) collective-permute-start(bf16[528,768]{1,0:T(8,128)(2,1)S(1)} %join.1.refs_1_.refs_0_.refs_6_.refs_3_.refs_7_), channel_id=1, source_target_pairs={{0,1},{1,0},{2,3},{3,2},{4,5},{5,4},{6,7},{7,6},{8,9},{9,8},{10,11... | collective-permute-start | bytes 2433032 | tf_op jit(solution)/shard_map/ppermute | solution.py:50
  2.4 9.2 %collective-permute-start.1 = (bf16[256,768]{1,0:T(8,128)(2,1)S(1)}, bf16[256,768]{1,0:T(8,128)(2,1)S(1)}, u32[]{:S(2)}, u32[]{:S(2)}) collective-permute-start(bf16[256,768]{1,0:T(8,128)(2,1)S(1)} %copy-done.4), channel_id=1, source_target_pairs={{1,2},{3,7},{5,6},{9,10},{11,15},{13,14},{17,18},{19,23},{21,22},{... | collective-permute-start | bytes 1179656 | tf_op jit(solution)/shard_map/ppermute | solution.py:66
  4.7 5.2 %copy-start = (f32[6,16,16]{2,1,0:T(8,128)S(1)}, f32[6,16,16]{2,1,0:T(8,128)}, u32[]{:S(2)}) copy-start(f32[6,16,16]{2,1,0:T(8,128)} %refs_3_.1) | copy-start | bytes 18436
  4.7 5.2 %copy-start.2 = (s32[1,2]{1,0:T(1,128)S(1)}, s32[1,2]{1,0:T(1,128)}, u32[]{:S(2)}) copy-start(s32[1,2]{1,0:T(1,128)} %refs_1_.4) | copy-start | bytes 28
  4.7 5.2 %copy-start.3 = (s32[16]{0:T(128)S(1)}, s32[16]{0:T(128)}, u32[]{:S(2)}) copy-start(s32[16]{0:T(128)} %refs_2_.3) | copy-start | bytes 196
  4.7 13.1 %collective-permute-start.4 = (bf16[3,2,128,384]{3,2,1,0:T(8,128)(2,1)S(1)}, bf16[3,2,128,384]{3,2,1,0:T(8,128)(2,1)S(1)}, u32[]{:S(2)}, u32[]{:S(2)}) collective-permute-start(bf16[3,2,128,384]{3,2,1,0:T(8,128)(2,1)S(1)} %split.1.refs_2_.refs_1_), channel_id=1, source_target_pairs={{0,2},{1,5},{2,0},{3,7},{4,6},{5,1},{6,4},{7,3},{8,10},{9,13},{10,... | collective-permute-start | bytes 1769480 | tf_op jit(solution)/shard_map/ppermute | solution.py:50
  8.8 9.1 %collective-permute-start.5 = (bf16[512,768]{1,0:T(8,128)(2,1)S(1)}, bf16[512,768]{1,0:T(8,128)(2,1)S(1)}, u32[]{:S(2)}, u32[]{:S(2)}) collective-permute-start(bf16[512,768]{1,0:T(8,128)(2,1)S(1)} %join_queries.1.refs_1_.refs_4_.refs_2_), channel_id=1, source_target_pairs={{0,1},{1,0},{2,3},{3,2},{4,5},{5,4},{6,7},{7,6},{8,9},{9,8},{10,11... | collective-permute-start | bytes 2359304 | tf_op jit(solution)/shard_map/ppermute | solution.py:50
  11.6 8.1 %collective-permute-start.2 = (bf16[256,768]{1,0:T(8,128)(2,1)S(1)}, bf16[256,768]{1,0:T(8,128)(2,1)S(1)}, u32[]{:S(2)}, u32[]{:S(2)}) collective-permute-start(bf16[256,768]{1,0:T(8,128)(2,1)S(1)} %get-tuple-element.28), channel_id=1, source_target_pairs={{1,2},{3,4},{5,6},{9,10},{11,12},{13,14},{17,18},{19,20},{21,22},{... | collective-permute-start | bytes 1179656 | tf_op jit(solution)/shard_map/ppermute | solution.py:55
  12.3 7.4 %collective-permute-start.3 = (bf16[256,768]{1,0:T(8,128)(2,1)S(1)}, bf16[256,768]{1,0:T(8,128)(2,1)S(1)}, u32[]{:S(2)}, u32[]{:S(2)}) collective-permute-start(bf16[256,768]{1,0:T(8,128)(2,1)S(1)} %get-tuple-element.29), channel_id=1, source_target_pairs={{7,4},{15,12},{23,20},{31,28}} | collective-permute-start | bytes 1179656 | tf_op jit(solution)/shard_map/ppermute | solution.py:71
  18.1 9.9 %collective-permute-start.6 = (bf16[3,2,128,384]{3,2,1,0:T(8,128)(2,1)S(1)}, bf16[3,2,128,384]{3,2,1,0:T(8,128)(2,1)S(1)}, u32[]{:S(2)}, u32[]{:S(2)}) collective-permute-start(bf16[3,2,128,384]{3,2,1,0:T(8,128)(2,1)S(1)} %step.1.refs_1_), channel_id=1, source_target_pairs={{0,4},{1,3},{2,6},{3,1},{4,0},{5,7},{6,2},{7,5},{8,12},{9,11},{10,... | collective-permute-start | bytes 1769480 | tf_op jit(solution)/shard_map/ppermute | solution.py:50
  21.3 8.9 %collective-permute-start.8 = (f32[6,8,256]{2,1,0:T(8,128)S(1)}, f32[6,8,256]{2,1,0:T(8,128)S(1)}, u32[]{:S(2)}, u32[]{:S(2)}) collective-permute-start(f32[6,8,256]{2,1,0:T(8,128)S(1)} %get-tuple-element.30.refs_2_.refs_1_), channel_id=1, source_target_pairs={{0,1},{1,0},{2,3},{3,2},{4,5},{5,4},{6,7},{7,6},{8,9},{9,8},{10,11... | collective-permute-start | bytes 147464 | tf_op jit(solution)/shard_map/ppermute | solution.py:50
  25.1 17.2 %collective-permute-start.10 = (bf16[256,768]{1,0:T(8,128)(2,1)S(1)}, bf16[256,768]{1,0:T(8,128)(2,1)S(1)}, u32[]{:S(2)}, u32[]{:S(2)}) collective-permute-start(bf16[256,768]{1,0:T(8,128)(2,1)S(1)} %get-tuple-element.37), channel_id=1, source_target_pairs={{2,1},{4,3},{6,5},{10,9},{12,11},{14,13},{18,17},{20,19},{22,21},{... | collective-permute-start | bytes 1179656 | tf_op jit(solution)/shard_map/ppermute | solution.py:55
  25.8 12.6 %collective-permute-start.12 = (bf16[256,768]{1,0:T(8,128)(2,1)S(1)}, bf16[256,768]{1,0:T(8,128)(2,1)S(1)}, u32[]{:S(2)}, u32[]{:S(2)}) collective-permute-start(bf16[256,768]{1,0:T(8,128)(2,1)S(1)} %get-tuple-element.41), channel_id=1, source_target_pairs={{2,1},{4,0},{6,5},{10,9},{12,8},{14,13},{18,17},{20,16},{22,21},{2... | collective-permute-start | bytes 1179656 | tf_op jit(solution)/shard_map/ppermute | solution.py:66
  28.4 6.3 %collective-permute-start.7 = (bf16[2,2,128,384]{3,2,1,0:T(8,128)(2,1)S(1)}, bf16[2,2,128,384]{3,2,1,0:T(8,128)(2,1)S(1)}, u32[]{:S(2)}, u32[]{:S(2)}) collective-permute-start(bf16[2,2,128,384]{3,2,1,0:T(8,128)(2,1)S(1)} %get-tuple-element.32.refs_7_), channel_id=1, source_target_pairs={{0,1},{1,0},{2,3},{3,2},{4,5},{5,4},{6,7},{7,6},{8,9},{9,8},{10,11... | collective-permute-start | bytes 1179656 | tf_op jit(solution)/shard_map/ppermute | solution.py:50
  32.1 12.2 %collective-permute-start.9 = (bf16[3,2,128,384]{3,2,1,0:T(8,128)(2,1)S(1)}, bf16[3,2,128,384]{3,2,1,0:T(8,128)(2,1)S(1)}, u32[]{:S(2)}, u32[]{:S(2)}) collective-permute-start(bf16[3,2,128,384]{3,2,1,0:T(8,128)(2,1)S(1)} %get-tuple-element.33.refs_6_), channel_id=1, source_target_pairs={{0,4},{1,3},{2,6},{3,1},{4,0},{5,7},{6,2},{7,5},{8,12},{9,11},{10,... | collective-permute-start | bytes 1769480 | tf_op jit(solution)/shard_map/ppermute | solution.py:50
  37.1 11.9 %collective-permute-start.11 = (f32[6,8,256]{2,1,0:T(8,128)S(1)}, f32[6,8,256]{2,1,0:T(8,128)S(1)}, u32[]{:S(2)}, u32[]{:S(2)}) collective-permute-start(f32[6,8,256]{2,1,0:T(8,128)S(1)} %get-tuple-element.34.refs_1_), channel_id=1, source_target_pairs={{1,0},{2,1},{3,2},{4,3},{5,4},{6,5},{7,6},{9,8},{10,9},{11,10},{12... | collective-permute-start | bytes 147464 | tf_op jit(solution)/shard_map/ppermute | solution.py:708
  38.5 10.6 %collective-permute-start.13 = (bf16[256,768]{1,0:T(8,128)(2,1)S(1)}, bf16[256,768]{1,0:T(8,128)(2,1)S(1)}, u32[]{:S(2)}, u32[]{:S(2)}) collective-permute-start(bf16[256,768]{1,0:T(8,128)(2,1)S(1)} %pass_on.1), channel_id=1, source_target_pairs={{0,3},{8,11},{16,19},{24,27}} | collective-permute-start | bytes 1179656 | tf_op jit(solution)/shard_map/ppermute | solution.py:71
  44.6 9.9 %collective-permute-start.14 = (bf16[3,2,128,384]{3,2,1,0:T(8,128)(2,1)S(1)}, bf16[3,2,128,384]{3,2,1,0:T(8,128)(2,1)S(1)}, u32[]{:S(2)}, u32[]{:S(2)}) collective-permute-start(bf16[3,2,128,384]{3,2,1,0:T(8,128)(2,1)S(1)} %get-tuple-element.38.refs_10_), channel_id=1, source_target_pairs={{0,2},{1,5},{2,0},{3,7},{4,6},{5,1},{6,4},{7,3},{8,10},{9,13},{10,... | collective-permute-start | bytes 1769480 | tf_op jit(solution)/shard_map/ppermute | solution.py:50
  54.8 1.8 %collective-permute-start.15 = (bf16[2,2,128,384]{3,2,1,0:T(8,128)(2,1)S(1)}, bf16[2,2,128,384]{3,2,1,0:T(8,128)(2,1)S(1)}, u32[]{:S(2)}, u32[]{:S(2)}) collective-permute-start(bf16[2,2,128,384]{3,2,1,0:T(8,128)(2,1)S(1)} %get-tuple-element.45), channel_id=1, source_target_pairs={{0,1},{1,0},{2,3},{3,2},{4,5},{5,4},{6,7},{7,6},{8,9},{9,8},{10,11... | collective-permute-start | bytes 1179656 | tf_op jit(solution)/shard_map/ppermute | solution.py:50

commit v21 on v20

--- a/solution.py
+++ b/solution.py
@@ -562,9 +562,9 @@
     out_ref[...] = in_ref[...]
 
 
-def owned_kernel(codes_ref, keep_ref, got_ref, mine_ref, pair_ref):
+def owned_kernel(groups, codes_ref, keep_ref, got_ref, *outs):
     code = code_of(codes_ref, OWNED)
-    for o, out in enumerate((mine_ref, pair_ref)):
+    for o, out in zip(groups, outs):
         for j in range(FR_DEV):
             owned = field(code, o * FR_DEV + j, PLACE_BITS)
             place = owned >> 1
@@ -730,11 +730,18 @@
         flops=HIDING * piece_flops,
         name="attend",
     )
-    owned_mine, owned_send = call(
-        owned_kernel,
-        [shape(F32, FR_DEV, 2, frame_len, half_width), shape(BF16, FR_DEV, 2, frame_len, half_width)],
+    (owned_send,) = call(
+        functools.partial(owned_kernel, (1,)),
+        [shape(BF16, FR_DEV, 2, frame_len, half_width)],
         [codes, keep, got],
         after=[own, mark],
+        name="owned_pair",
+    )
+    (owned_mine,) = call(
+        functools.partial(owned_kernel, (0,)),
+        [shape(F32, FR_DEV, 2, frame_len, half_width)],
+        [codes, keep, got],
+        after=[owned_send],
         name="owned",
     )
     owned_got = swap(owned_send, 1, 1, peers)

time: 57.9 us -> 57.8 us (level)
    pallas_call x13 -> x14, Pallas kernels: 14.1 us -> 14.4 us  [call(): pl.pallas_call(run, out_shape=outs, in_specs=[SMEM] * len(scalars) + [VME...]
  transfers between devices with their start and end apart: 16 -> 16, of which waited for: 6 -> 6; matrix products, arithmetic and copies ran while one was open for 0% -> 0% of each run, Pallas kernels for 26% -> 27%
where the time goes in v21:
time: 57.8 us; the launch traced here: 57.5 us
  starting transfers between devices  24.4 us (42%)
  Pallas kernels  17.7 us (31%)
  waiting for transfers between devices  14.5 us (25%)
  between operations  0.87 us (2%)
    ppermute x9, starting transfers between devices, swap(): lax.ppermute(block, 'tm', [(i, i ^ (odd_bit if i & 1 else even_bit)) for...  15.3 us
    ppermute x9, waiting for transfers between devices, swap(): lax.ppermute(block, 'tm', [(i, i ^ (odd_bit if i & 1 else even_bit)) for...  14.5 us
    pallas_call x14, Pallas kernels, call(): pl.pallas_call(run, out_shape=outs, in_specs=[SMEM] * len(scalars) + [VME...  14.4 us
    ppermute x2, starting transfers between devices, shift_second(): return lax.ppermute(block, 'tm', pairs) if pairs else block  4.48 us
    pallas_call x2, Pallas kernels, join(): pl.pallas_call(run, out_shape=shape(BF16, rows, width), in_specs=[pl.Bloc...  2.34 us
    ppermute x2, starting transfers between devices, shift_first(): lax.ppermute(block, 'tm', [(i, relays.get((i, j), j)) for i, j in pairs])  1.97 us
    ppermute x2, starting transfers between devices, shift(): return lax.ppermute(block, 'tm', pairs)  1.36 us
    ppermute x1, starting transfers between devices, body(): lax.ppermute(stats_all, 'tm', [(i, i - 1) for i in range(1, peers)])  1.29 us
  transfers between devices with their start and end apart: 16, of which 6 were waited for; matrix products, arithmetic and copies ran while one was open for 0% of the time, Pallas kernels for 27%

profile of v21, /device:TPU:0, one launch (start us, length us, event | category | flops | bytes accessed | tf_op | source)
XLA Modules:
  0.0 57.5 jit_solution(13079746714533531602)
XLA Ops:
  0.7 1.2 %join.1.refs_1_.refs_0_.refs_6_.refs_3_.refs_7_ = bf16[528,768]{1,0:T(8,128)(2,1)S(1)} custom-call(s32[1,2]{1,0:T(1,128)} %refs_1_.4, bf16[256,768]{1,0:T(8,128)(2,1)} %refs_1_.3, bf16[256,768]{1,0:T(8,128)(2,1)} %refs_2_.2), custom_call_target="tpu_custom_call" | custom-call | tf_op jit(solution)/shard_map/join/pallas_call | solution.py:625
  1.9 0.5 collective-permute-start
  2.4 0.7 %collective-permute-start.1 = (bf16[256,768]{1,0:T(8,128)(2,1)S(1)}, bf16[256,768]{1,0:T(8,128)(2,1)S(1)}, u32[]{:S(2)}, u32[]{:S(2)}) collective-permute-start(bf16[256,768]{1,0:T(8,128)(2,1)S(1)} %copy-done.4), channel_id=1, source_target_pairs={{1,2},{3,7},{5,6},{9,10},{11,15},{13,14},{17,18},{19,23},{21,22},{... | collective-permute-start | bytes 1179656 | tf_op jit(solution)/shard_map/ppermute | solution.py:66
  3.1 1.3 %collective-permute-done.refs_4_.refs_2_.refs_5_.refs_6_ = bf16[528,768]{1,0:T(8,128)(2,1)S(1)} collective-permute-done((bf16[528,768]{1,0:T(8,128)(2,1)S(1)}, bf16[528,768]{1,0:T(8,128)(2,1)S(1)}, u32[]{:S(2)}, u32[]{:S(2)}) %collective-permute-start) | collective-permute-done | bytes 811040 | tf_op jit(solution)/shard_map/ppermute | solution.py:50
  4.3 0.3 split.1.refs_2_.refs_1_
  4.7 0.0 copy-start
  4.7 0.0 copy-start.2
  4.7 0.0 copy-start.3
  4.7 2.9 %collective-permute-start.4 = (bf16[3,2,128,384]{3,2,1,0:T(8,128)(2,1)S(1)}, bf16[3,2,128,384]{3,2,1,0:T(8,128)(2,1)S(1)}, u32[]{:S(2)}, u32[]{:S(2)}) collective-permute-start(bf16[3,2,128,384]{3,2,1,0:T(8,128)(2,1)S(1)} %split.1.refs_2_.refs_1_), channel_id=1, source_target_pairs={{0,2},{1,5},{2,0},{3,7},{4,6},{5,1},{6,4},{7,3},{8,10},{9,13},{10,... | collective-permute-start | bytes 1769480 | tf_op jit(solution)/shard_map/ppermute | solution.py:50
  7.6 1.1 %join_queries.1.refs_1_.refs_4_.refs_2_ = bf16[512,768]{1,0:T(8,128)(2,1)S(1)} custom-call(bf16[256,768]{1,0:T(8,128)(2,1)} %refs_0_.3, bf16[256,768]{1,0:T(8,128)(2,1)} %refs_1_.5, bf16[3,2,128,384]{3,2,1,0:T(8,128)(2,1)S(1)} %split.1.refs_2_.refs_1_), custom_call_target="tpu_custom_call" | custom-call | tf_op jit(solution)/shard_map/join_queries/pallas_call | solution.py:625
  8.8 1.1 %collective-permute-start.5 = (bf16[512,768]{1,0:T(8,128)(2,1)S(1)}, bf16[512,768]{1,0:T(8,128)(2,1)S(1)}, u32[]{:S(2)}, u32[]{:S(2)}) collective-permute-start(bf16[512,768]{1,0:T(8,128)(2,1)S(1)} %join_queries.1.refs_1_.refs_4_.refs_2_), channel_id=1, source_target_pairs={{0,1},{1,0},{2,3},{3,2},{4,5},{5,4},{6,7},{7,6},{8,9},{9,8},{10,11... | collective-permute-start | bytes 2359304 | tf_op jit(solution)/shard_map/ppermute | solution.py:50
  9.9 1.7 %plan.1 = (f32[6,16,256]{2,1,0:T(8,128)S(1)}, s32[8,128]{1,0:T(8,128)S(1)}) custom-call(s32[1,4]{1,0:T(1,128)S(1)} %bitcast.2, s32[1,2]{1,0:T(1,128)S(1)} %copy-done.2, s32[16]{0:T(128)S(1)} %copy-done.3, f32[6,16,16]{2,1,0:T(8,128)S(1)} %copy-done, bf16[528,768]{1,0:T(8,128)(2,1)S(1)} %collective-permute-done.refs_4_.refs_2_.refs_5_.refs_6_), custom_call_target="tpu_custom_call" | custom-call | tf_op jit(solution)/shard_map/plan/pallas_call | solution.py:38
  11.5 0.0 collective-permute-done.1.refs_1_.refs_2_.refs_3_
  11.6 0.1 release.1
  11.6 0.7 %collective-permute-start.2 = (bf16[256,768]{1,0:T(8,128)(2,1)S(1)}, bf16[256,768]{1,0:T(8,128)(2,1)S(1)}, u32[]{:S(2)}, u32[]{:S(2)}) collective-permute-start(bf16[256,768]{1,0:T(8,128)(2,1)S(1)} %get-tuple-element.26), channel_id=1, source_target_pairs={{1,2},{3,4},{5,6},{9,10},{11,12},{13,14},{17,18},{19,20},{21,22},{... | collective-permute-start | bytes 1179656 | tf_op jit(solution)/shard_map/ppermute | solution.py:55
  12.3 0.7 %collective-permute-start.3 = (bf16[256,768]{1,0:T(8,128)(2,1)S(1)}, bf16[256,768]{1,0:T(8,128)(2,1)S(1)}, u32[]{:S(2)}, u32[]{:S(2)}) collective-permute-start(bf16[256,768]{1,0:T(8,128)(2,1)S(1)} %get-tuple-element.27), channel_id=1, source_target_pairs={{7,4},{15,12},{23,20},{31,28}} | collective-permute-start | bytes 1179656 | tf_op jit(solution)/shard_map/ppermute | solution.py:71
  13.0 4.8 %collective-permute-done.4.refs_2_ = bf16[3,2,128,384]{3,2,1,0:T(8,128)(2,1)S(1)} collective-permute-done((bf16[3,2,128,384]{3,2,1,0:T(8,128)(2,1)S(1)}, bf16[3,2,128,384]{3,2,1,0:T(8,128)(2,1)S(1)}, u32[]{:S(2)}, u32[]{:S(2)}) %collective-permute-start.4) | collective-permute-done | bytes 589856 | tf_op jit(solution)/shard_map/ppermute | solution.py:50
  17.8 0.0 collective-permute-done.5.refs_4_.refs_5_.refs_2_
  17.8 0.3 step.1.refs_1_
  18.1 1.6 %collective-permute-start.6 = (bf16[3,2,128,384]{3,2,1,0:T(8,128)(2,1)S(1)}, bf16[3,2,128,384]{3,2,1,0:T(8,128)(2,1)S(1)}, u32[]{:S(2)}, u32[]{:S(2)}) collective-permute-start(bf16[3,2,128,384]{3,2,1,0:T(8,128)(2,1)S(1)} %step.1.refs_1_), channel_id=1, source_target_pairs={{0,4},{1,3},{2,6},{3,1},{4,0},{5,7},{6,2},{7,5},{8,12},{9,11},{10,... | collective-permute-start | bytes 1769480 | tf_op jit(solution)/shard_map/ppermute | solution.py:50
  19.7 0.0 collective-permute-done.2.refs_3_.refs_4_
  19.7 0.0 collective-permute-done.3.refs_4_.refs_5_
  19.7 1.6 %stats.1 = (f32[6,8,256]{2,1,0:T(8,128)S(1)}, bf16[256,768]{1,0:T(8,128)(2,1)S(1)}, bf16[256,768]{1,0:T(8,128)(2,1)S(1)}) custom-call(f32[6,16,256]{2,1,0:T(8,128)S(1)} %get-tuple-element.24.refs_0_.refs_1_, bf16[512,768]{1,0:T(8,128)(2,1)S(1)} %join_queries.1.refs_1_.refs_4_.refs_2_, bf16[256,768]{1,0:T(8,128)(2,1)S(1)} %collective-permute-done.1.refs_1_.refs_2_.refs_3_, ...), custom_call_target="tpu_custom_call" | custom-call | flops 20132659200 | tf_op jit(solution)/shard_map/stats/pallas_call | solution.py:38
  21.3 3.9 %collective-permute-start.8 = (f32[6,8,256]{2,1,0:T(8,128)S(1)}, f32[6,8,256]{2,1,0:T(8,128)S(1)}, u32[]{:S(2)}, u32[]{:S(2)}) collective-permute-start(f32[6,8,256]{2,1,0:T(8,128)S(1)} %get-tuple-element.28.refs_2_.refs_1_), channel_id=1, source_target_pairs={{0,1},{1,0},{2,3},{3,2},{4,5},{5,4},{6,7},{7,6},{8,9},{9,8},{10,11... | collective-permute-start | bytes 147464 | tf_op jit(solution)/shard_map/ppermute | solution.py:50
  25.2 0.7 %collective-permute-start.10 = (bf16[256,768]{1,0:T(8,128)(2,1)S(1)}, bf16[256,768]{1,0:T(8,128)(2,1)S(1)}, u32[]{:S(2)}, u32[]{:S(2)}) collective-permute-start(bf16[256,768]{1,0:T(8,128)(2,1)S(1)} %get-tuple-element.35), channel_id=1, source_target_pairs={{2,1},{4,3},{6,5},{10,9},{12,11},{14,13},{18,17},{20,19},{22,21},{... | collective-permute-start | bytes 1179656 | tf_op jit(solution)/shard_map/ppermute | solution.py:55
  25.9 1.3 %collective-permute-start.12 = (bf16[256,768]{1,0:T(8,128)(2,1)S(1)}, bf16[256,768]{1,0:T(8,128)(2,1)S(1)}, u32[]{:S(2)}, u32[]{:S(2)}) collective-permute-start(bf16[256,768]{1,0:T(8,128)(2,1)S(1)} %get-tuple-element.39), channel_id=1, source_target_pairs={{2,1},{4,0},{6,5},{10,9},{12,8},{14,13},{18,17},{20,16},{22,21},{2... | collective-permute-start | bytes 1179656 | tf_op jit(solution)/shard_map/ppermute | solution.py:66
  27.2 0.9 %collective-permute-done.6.refs_2_ = bf16[3,2,128,384]{3,2,1,0:T(8,128)(2,1)S(1)} collective-permute-done((bf16[3,2,128,384]{3,2,1,0:T(8,128)(2,1)S(1)}, bf16[3,2,128,384]{3,2,1,0:T(8,128)(2,1)S(1)}, u32[]{:S(2)}, u32[]{:S(2)}) %collective-permute-start.6) | collective-permute-done | bytes 589856 | tf_op jit(solution)/shard_map/ppermute | solution.py:50
  28.1 0.3 pick.1
  28.4 1.8 %collective-permute-start.7 = (bf16[2,2,128,384]{3,2,1,0:T(8,128)(2,1)S(1)}, bf16[2,2,128,384]{3,2,1,0:T(8,128)(2,1)S(1)}, u32[]{:S(2)}, u32[]{:S(2)}) collective-permute-start(bf16[2,2,128,384]{3,2,1,0:T(8,128)(2,1)S(1)} %get-tuple-element.30.refs_7_), channel_id=1, source_target_pairs={{0,1},{1,0},{2,3},{3,2},{4,5},{5,4},{6,7},{7,6},{8,9},{9,8},{10,11... | collective-permute-start | bytes 1179656 | tf_op jit(solution)/shard_map/ppermute | solution.py:50
  30.2 0.0 collective-permute-done.8.refs_3_
  30.2 1.9 %memory.1 = (f32[4,2,128,384]{3,2,1,0:T(8,128)S(1)}, bf16[3,2,128,384]{3,2,1,0:T(8,128)(2,1)S(1)}) custom-call(s32[8,128]{1,0:T(8,128)S(1)} %get-tuple-element.25.refs_2_.refs_3_.refs_0_, f32[6,16,256]{2,1,0:T(8,128)S(1)} %get-tuple-element.24.refs_0_.refs_1_, f32[6,8,256]{2,1,0:T(8,128)S(1)} %get-tuple-element.28.refs_2_.refs_1_, ...), custom_call_target="tpu_custom_call" | custom-call | flops 20132659200 | tf_op jit(solution)/shard_map/memory/pallas_call | solution.py:38
  32.2 2.6 %collective-permute-start.9 = (bf16[3,2,128,384]{3,2,1,0:T(8,128)(2,1)S(1)}, bf16[3,2,128,384]{3,2,1,0:T(8,128)(2,1)S(1)}, u32[]{:S(2)}, u32[]{:S(2)}) collective-permute-start(bf16[3,2,128,384]{3,2,1,0:T(8,128)(2,1)S(1)} %get-tuple-element.31.refs_6_), channel_id=1, source_target_pairs={{0,4},{1,3},{2,6},{3,1},{4,0},{5,7},{6,2},{7,5},{8,12},{9,11},{10,... | collective-permute-start | bytes 1769480 | tf_op jit(solution)/shard_map/ppermute | solution.py:50
  34.8 2.5 %own.1 = (f32[2,256,768]{2,1,0:T(8,128)S(1)}, f32[6,8,256]{2,1,0:T(8,128)S(1)}) custom-call(f32[6,16,256]{2,1,0:T(8,128)S(1)} %get-tuple-element.24.refs_0_.refs_1_, f32[6,8,256]{2,1,0:T(8,128)S(1)} %get-tuple-element.28.refs_2_.refs_1_, bf16[512,768]{1,0:T(8,128)(2,1)S(1)} %join_queries.1.refs_1_.refs_4_.refs_2_, ...), custom_call_target="tpu_custom_call" | custom-call | flops 20132659200 | tf_op jit(solution)/shard_map/own/pallas_call | solution.py:38
  37.3 1.3 %collective-permute-start.11 = (f32[6,8,256]{2,1,0:T(8,128)S(1)}, f32[6,8,256]{2,1,0:T(8,128)S(1)}, u32[]{:S(2)}, u32[]{:S(2)}) collective-permute-start(f32[6,8,256]{2,1,0:T(8,128)S(1)} %get-tuple-element.32.refs_1_), channel_id=1, source_target_pairs={{1,0},{2,1},{3,2},{4,3},{5,4},{6,5},{7,6},{9,8},{10,9},{11,10},{12... | collective-permute-start | bytes 147464 | tf_op jit(solution)/shard_map/ppermute | solution.py:708
  38.6 0.0 collective-permute-done.12.refs_0_.refs_4_
  38.6 3.8 %collective-permute-start.13 = (bf16[256,768]{1,0:T(8,128)(2,1)S(1)}, bf16[256,768]{1,0:T(8,128)(2,1)S(1)}, u32[]{:S(2)}, u32[]{:S(2)}) collective-permute-start(bf16[256,768]{1,0:T(8,128)(2,1)S(1)} %pass_on.1), channel_id=1, source_target_pairs={{0,3},{8,11},{16,19},{24,27}} | collective-permute-start | bytes 1179656 | tf_op jit(solution)/shard_map/ppermute | solution.py:71
  42.4 2.0 %collective-permute-done.9.refs_1_ = bf16[3,2,128,384]{3,2,1,0:T(8,128)(2,1)S(1)} collective-permute-done((bf16[3,2,128,384]{3,2,1,0:T(8,128)(2,1)S(1)}, bf16[3,2,128,384]{3,2,1,0:T(8,128)(2,1)S(1)}, u32[]{:S(2)}, u32[]{:S(2)}) %collective-permute-start.9) | collective-permute-done | bytes 589856 | tf_op jit(solution)/shard_map/ppermute | solution.py:50
  44.4 0.2 add.1
  44.5 0.7 %collective-permute-start.14 = (bf16[3,2,128,384]{3,2,1,0:T(8,128)(2,1)S(1)}, bf16[3,2,128,384]{3,2,1,0:T(8,128)(2,1)S(1)}, u32[]{:S(2)}, u32[]{:S(2)}) collective-permute-start(bf16[3,2,128,384]{3,2,1,0:T(8,128)(2,1)S(1)} %get-tuple-element.36.refs_10_), channel_id=1, source_target_pairs={{0,2},{1,5},{2,0},{3,7},{4,6},{5,1},{6,4},{7,3},{8,10},{9,13},{10,... | collective-permute-start | bytes 1769480 | tf_op jit(solution)/shard_map/ppermute | solution.py:50
  45.3 3.8 %attend.1 = (bf16[256,768]{1,0:T(8,128)(2,1)}, bf16[256,768]{1,0:T(8,128)(2,1)}, f32[8,128]{1,0:T(8,128)S(1)}) custom-call(f32[6,16,256]{2,1,0:T(8,128)S(1)} %get-tuple-element.24.refs_0_.refs_1_, f32[6,8,256]{2,1,0:T(8,128)S(1)} %get-tuple-element.32.refs_1_, bf16[512,768]{1,0:T(8,128)(2,1)S(1)} %join_queries.1.refs_1_.refs_4_.refs_2_, ...), custom_call_target="tpu_custom_call" | custom-call | flops 20132659200 | tf_op jit(solution)/shard_map/attend/pallas_call | solution.py:38
  49.1 0.0 collective-permute-done.11.refs_1_
  49.1 1.3 %next.1.refs_3_.own_ref = f32[2,256,768]{2,1,0:T(8,128)S(1)} custom-call(f32[6,16,256]{2,1,0:T(8,128)S(1)} %get-tuple-element.24.refs_0_.refs_1_, f32[6,8,256]{2,1,0:T(8,128)S(1)} %collective-permute-done.11.refs_1_, bf16[512,768]{1,0:T(8,128)(2,1)S(1)} %collective-permute-done.5.refs_4_.refs_5_.refs_2_, ...), custom_call_target="tpu_custom_call" | custom-call | flops 20132659200 | tf_op jit(solution)/shard_map/next/pallas_call | solution.py:38
  50.3 4.2 %collective-permute-done.14.refs_2_ = bf16[3,2,128,384]{3,2,1,0:T(8,128)(2,1)S(1)} collective-permute-done((bf16[3,2,128,384]{3,2,1,0:T(8,128)(2,1)S(1)}, bf16[3,2,128,384]{3,2,1,0:T(8,128)(2,1)S(1)}, u32[]{:S(2)}, u32[]{:S(2)}) %collective-permute-start.14) | collective-permute-done | bytes 589856 | tf_op jit(solution)/shard_map/ppermute | solution.py:50
  54.5 0.2 owned_pair.1.refs_3_
  54.7 0.2 collective-permute-start.15
  55.0 0.3 owned.1.mine_ref
  55.2 1.3 %collective-permute-done.15.got_ref = bf16[2,2,128,384]{3,2,1,0:T(8,128)(2,1)S(1)} collective-permute-done((bf16[2,2,128,384]{3,2,1,0:T(8,128)(2,1)S(1)}, bf16[2,2,128,384]{3,2,1,0:T(8,128)(2,1)S(1)}, u32[]{:S(2)}, u32[]{:S(2)}) %collective-permute-start.15) | collective-permute-done | bytes 393248 | tf_op jit(solution)/shard_map/ppermute | solution.py:50
  56.5 1.0 %final.1 = (bf16[256,768]{1,0:T(8,128)(2,1)}, bf16[256,768]{1,0:T(8,128)(2,1)}) custom-call(f32[2,256,768]{2,1,0:T(8,128)S(1)} %next.1.refs_3_.own_ref, f32[2,2,128,384]{3,2,1,0:T(8,128)S(1)} %owned.1.mine_ref, bf16[2,2,128,384]{3,2,1,0:T(8,128)(2,1)S(1)} %collective-permute-done.15.got_ref), custom_call_target="tpu_custom_call" | custom-call | tf_op jit(solution)/shard_map/final/pallas_call | solution.py:748
  (11 shorter events, 0.1 us)
Async XLA Ops:
  0.6 1.8 %copy-start.4 = (bf16[256,768]{1,0:T(8,128)(2,1)S(1)}, bf16[256,768]{1,0:T(8,128)(2,1)}, u32[]{:S(2)}) copy-start(bf16[256,768]{1,0:T(8,128)(2,1)} %refs_1_.3) | copy-start | bytes 1179652
  0.6 3.7 %copy-start.1 = (s32[4]{0:T(128)S(1)}, s32[4]{0:T(128)}, u32[]{:S(2)}) copy-start(s32[4]{0:T(128)} %param.15) | copy-start | bytes 52
  1.9 2.5 %collective-permute-start = (bf16[528,768]{1,0:T(8,128)(2,1)S(1)}, bf16[528,768]{1,0:T(8,128)(2,1)S(1)}, u32[]{:S(2)}, u32[]{:S(2)}) collective-permute-start(bf16[528,768]{1,0:T(8,128)(2,1)S(1)} %join.1.refs_1_.refs_0_.refs_6_.refs_3_.refs_7_), channel_id=1, source_target_pairs={{0,1},{1,0},{2,3},{3,2},{4,5},{5,4},{6,7},{7,6},{8,9},{9,8},{10,11... | collective-permute-start | bytes 2433032 | tf_op jit(solution)/shard_map/ppermute | solution.py:50
  2.4 9.2 %collective-permute-start.1 = (bf16[256,768]{1,0:T(8,128)(2,1)S(1)}, bf16[256,768]{1,0:T(8,128)(2,1)S(1)}, u32[]{:S(2)}, u32[]{:S(2)}) collective-permute-start(bf16[256,768]{1,0:T(8,128)(2,1)S(1)} %copy-done.4), channel_id=1, source_target_pairs={{1,2},{3,7},{5,6},{9,10},{11,15},{13,14},{17,18},{19,23},{21,22},{... | collective-permute-start | bytes 1179656 | tf_op jit(solution)/shard_map/ppermute | solution.py:66
  4.7 5.2 %copy-start = (f32[6,16,16]{2,1,0:T(8,128)S(1)}, f32[6,16,16]{2,1,0:T(8,128)}, u32[]{:S(2)}) copy-start(f32[6,16,16]{2,1,0:T(8,128)} %refs_3_.1) | copy-start | bytes 18436
  4.7 5.2 %copy-start.2 = (s32[1,2]{1,0:T(1,128)S(1)}, s32[1,2]{1,0:T(1,128)}, u32[]{:S(2)}) copy-start(s32[1,2]{1,0:T(1,128)} %refs_1_.4) | copy-start | bytes 28
  4.7 5.2 %copy-start.3 = (s32[16]{0:T(128)S(1)}, s32[16]{0:T(128)}, u32[]{:S(2)}) copy-start(s32[16]{0:T(128)} %refs_2_.3) | copy-start | bytes 196
  4.7 13.1 %collective-permute-start.4 = (bf16[3,2,128,384]{3,2,1,0:T(8,128)(2,1)S(1)}, bf16[3,2,128,384]{3,2,1,0:T(8,128)(2,1)S(1)}, u32[]{:S(2)}, u32[]{:S(2)}) collective-permute-start(bf16[3,2,128,384]{3,2,1,0:T(8,128)(2,1)S(1)} %split.1.refs_2_.refs_1_), channel_id=1, source_target_pairs={{0,2},{1,5},{2,0},{3,7},{4,6},{5,1},{6,4},{7,3},{8,10},{9,13},{10,... | collective-permute-start | bytes 1769480 | tf_op jit(solution)/shard_map/ppermute | solution.py:50
  8.8 9.1 %collective-permute-start.5 = (bf16[512,768]{1,0:T(8,128)(2,1)S(1)}, bf16[512,768]{1,0:T(8,128)(2,1)S(1)}, u32[]{:S(2)}, u32[]{:S(2)}) collective-permute-start(bf16[512,768]{1,0:T(8,128)(2,1)S(1)} %join_queries.1.refs_1_.refs_4_.refs_2_), channel_id=1, source_target_pairs={{0,1},{1,0},{2,3},{3,2},{4,5},{5,4},{6,7},{7,6},{8,9},{9,8},{10,11... | collective-permute-start | bytes 2359304 | tf_op jit(solution)/shard_map/ppermute | solution.py:50
  11.6 8.1 %collective-permute-start.2 = (bf16[256,768]{1,0:T(8,128)(2,1)S(1)}, bf16[256,768]{1,0:T(8,128)(2,1)S(1)}, u32[]{:S(2)}, u32[]{:S(2)}) collective-permute-start(bf16[256,768]{1,0:T(8,128)(2,1)S(1)} %get-tuple-element.26), channel_id=1, source_target_pairs={{1,2},{3,4},{5,6},{9,10},{11,12},{13,14},{17,18},{19,20},{21,22},{... | collective-permute-start | bytes 1179656 | tf_op jit(solution)/shard_map/ppermute | solution.py:55
  12.3 7.4 %collective-permute-start.3 = (bf16[256,768]{1,0:T(8,128)(2,1)S(1)}, bf16[256,768]{1,0:T(8,128)(2,1)S(1)}, u32[]{:S(2)}, u32[]{:S(2)}) collective-permute-start(bf16[256,768]{1,0:T(8,128)(2,1)S(1)} %get-tuple-element.27), channel_id=1, source_target_pairs={{7,4},{15,12},{23,20},{31,28}} | collective-permute-start | bytes 1179656 | tf_op jit(solution)/shard_map/ppermute | solution.py:71
  18.1 9.9 %collective-permute-start.6 = (bf16[3,2,128,384]{3,2,1,0:T(8,128)(2,1)S(1)}, bf16[3,2,128,384]{3,2,1,0:T(8,128)(2,1)S(1)}, u32[]{:S(2)}, u32[]{:S(2)}) collective-permute-start(bf16[3,2,128,384]{3,2,1,0:T(8,128)(2,1)S(1)} %step.1.refs_1_), channel_id=1, source_target_pairs={{0,4},{1,3},{2,6},{3,1},{4,0},{5,7},{6,2},{7,5},{8,12},{9,11},{10,... | collective-permute-start | bytes 1769480 | tf_op jit(solution)/shard_map/ppermute | solution.py:50
  21.3 8.9 %collective-permute-start.8 = (f32[6,8,256]{2,1,0:T(8,128)S(1)}, f32[6,8,256]{2,1,0:T(8,128)S(1)}, u32[]{:S(2)}, u32[]{:S(2)}) collective-permute-start(f32[6,8,256]{2,1,0:T(8,128)S(1)} %get-tuple-element.28.refs_2_.refs_1_), channel_id=1, source_target_pairs={{0,1},{1,0},{2,3},{3,2},{4,5},{5,4},{6,7},{7,6},{8,9},{9,8},{10,11... | collective-permute-start | bytes 147464 | tf_op jit(solution)/shard_map/ppermute | solution.py:50
  25.2 17.2 %collective-permute-start.10 = (bf16[256,768]{1,0:T(8,128)(2,1)S(1)}, bf16[256,768]{1,0:T(8,128)(2,1)S(1)}, u32[]{:S(2)}, u32[]{:S(2)}) collective-permute-start(bf16[256,768]{1,0:T(8,128)(2,1)S(1)} %get-tuple-element.35), channel_id=1, source_target_pairs={{2,1},{4,3},{6,5},{10,9},{12,11},{14,13},{18,17},{20,19},{22,21},{... | collective-permute-start | bytes 1179656 | tf_op jit(solution)/shard_map/ppermute | solution.py:55
  25.9 12.7 %collective-permute-start.12 = (bf16[256,768]{1,0:T(8,128)(2,1)S(1)}, bf16[256,768]{1,0:T(8,128)(2,1)S(1)}, u32[]{:S(2)}, u32[]{:S(2)}) collective-permute-start(bf16[256,768]{1,0:T(8,128)(2,1)S(1)} %get-tuple-element.39), channel_id=1, source_target_pairs={{2,1},{4,0},{6,5},{10,9},{12,8},{14,13},{18,17},{20,16},{22,21},{2... | collective-permute-start | bytes 1179656 | tf_op jit(solution)/shard_map/ppermute | solution.py:66
  28.4 6.4 %collective-permute-start.7 = (bf16[2,2,128,384]{3,2,1,0:T(8,128)(2,1)S(1)}, bf16[2,2,128,384]{3,2,1,0:T(8,128)(2,1)S(1)}, u32[]{:S(2)}, u32[]{:S(2)}) collective-permute-start(bf16[2,2,128,384]{3,2,1,0:T(8,128)(2,1)S(1)} %get-tuple-element.30.refs_7_), channel_id=1, source_target_pairs={{0,1},{1,0},{2,3},{3,2},{4,5},{5,4},{6,7},{7,6},{8,9},{9,8},{10,11... | collective-permute-start | bytes 1179656 | tf_op jit(solution)/shard_map/ppermute | solution.py:50
  32.2 12.2 %collective-permute-start.9 = (bf16[3,2,128,384]{3,2,1,0:T(8,128)(2,1)S(1)}, bf16[3,2,128,384]{3,2,1,0:T(8,128)(2,1)S(1)}, u32[]{:S(2)}, u32[]{:S(2)}) collective-permute-start(bf16[3,2,128,384]{3,2,1,0:T(8,128)(2,1)S(1)} %get-tuple-element.31.refs_6_), channel_id=1, source_target_pairs={{0,4},{1,3},{2,6},{3,1},{4,0},{5,7},{6,2},{7,5},{8,12},{9,11},{10,... | collective-permute-start | bytes 1769480 | tf_op jit(solution)/shard_map/ppermute | solution.py:50
  37.3 11.8 %collective-permute-start.11 = (f32[6,8,256]{2,1,0:T(8,128)S(1)}, f32[6,8,256]{2,1,0:T(8,128)S(1)}, u32[]{:S(2)}, u32[]{:S(2)}) collective-permute-start(f32[6,8,256]{2,1,0:T(8,128)S(1)} %get-tuple-element.32.refs_1_), channel_id=1, source_target_pairs={{1,0},{2,1},{3,2},{4,3},{5,4},{6,5},{7,6},{9,8},{10,9},{11,10},{12... | collective-permute-start | bytes 147464 | tf_op jit(solution)/shard_map/ppermute | solution.py:708
  38.6 10.5 %collective-permute-start.13 = (bf16[256,768]{1,0:T(8,128)(2,1)S(1)}, bf16[256,768]{1,0:T(8,128)(2,1)S(1)}, u32[]{:S(2)}, u32[]{:S(2)}) collective-permute-start(bf16[256,768]{1,0:T(8,128)(2,1)S(1)} %pass_on.1), channel_id=1, source_target_pairs={{0,3},{8,11},{16,19},{24,27}} | collective-permute-start | bytes 1179656 | tf_op jit(solution)/shard_map/ppermute | solution.py:71
  44.5 9.9 %collective-permute-start.14 = (bf16[3,2,128,384]{3,2,1,0:T(8,128)(2,1)S(1)}, bf16[3,2,128,384]{3,2,1,0:T(8,128)(2,1)S(1)}, u32[]{:S(2)}, u32[]{:S(2)}) collective-permute-start(bf16[3,2,128,384]{3,2,1,0:T(8,128)(2,1)S(1)} %get-tuple-element.36.refs_10_), channel_id=1, source_target_pairs={{0,2},{1,5},{2,0},{3,7},{4,6},{5,1},{6,4},{7,3},{8,10},{9,13},{10,... | collective-permute-start | bytes 1769480 | tf_op jit(solution)/shard_map/ppermute | solution.py:50
  54.7 1.8 %collective-permute-start.15 = (bf16[2,2,128,384]{3,2,1,0:T(8,128)(2,1)S(1)}, bf16[2,2,128,384]{3,2,1,0:T(8,128)(2,1)S(1)}, u32[]{:S(2)}, u32[]{:S(2)}) collective-permute-start(bf16[2,2,128,384]{3,2,1,0:T(8,128)(2,1)S(1)} %owned_pair.1.refs_3_), channel_id=1, source_target_pairs={{0,1},{1,0},{2,3},{3,2},{4,5},{5,4},{6,7},{7,6},{8,9},{9,8},{10,11... | collective-permute-start | bytes 1179656 | tf_op jit(solution)/shard_map/ppermute | solution.py:50
